TPU v7x, 32 devices: a whole 2x2x4 slice. The times are simulated.
32 devices in a mesh: groups: 2 (over x), band: 16 (over z, y, core).
Axes of the slice: x: 2, y: 2, z: 4, core: 2. Of those that a mesh axis runs over, the one named last changes fastest.
Arguments:
- node_latent: bfloat16 [10240, 512], P(('groups', 'band')), parts along dimension 0, may hold values from -6 to 6
- edge_latent: bfloat16 [32, 11, 128, 512], P(('groups', 'band')), parts along dimension 0, may hold values from -6 to 6
- recv_slot: int32 [32, 11, 128], P(('groups', 'band')), parts along dimension 0, may hold values from 0 to 319
- send_slot: int32 [32, 11, 128], P(('groups', 'band')), parts along dimension 0, may hold values from 0 to 319
- edge_count: int32 [32, 11], P(('groups', 'band')), parts along dimension 0, may hold values from 42 to 128, as said below
- edge_first: bfloat16 [1536, 512], replicated, may hold values from -0.15625 to 0.15625
- edge_second: bfloat16 [512, 512], replicated, may hold values from -0.25 to 0.25
- node_first: bfloat16 [1024, 512], replicated, may hold values from -0.1875 to 0.1875
- node_second: bfloat16 [512, 512], replicated, may hold values from -0.25 to 0.25
- node_cotan: bfloat16 [10240, 512], P(('groups', 'band')), parts along dimension 0, may hold values from -6 to 6
- edge_cotan: bfloat16 [32, 11, 128, 512], P(('groups', 'band')), parts along dimension 0, may hold values from -6 to 6
Outputs:
- node_new: bfloat16 [10240, 512], P(('groups', 'band')), parts along dimension 0
- edge_new: bfloat16 [32, 11, 128, 512], P(('groups', 'band')), parts along dimension 0
- grad_nodes: bfloat16 [10240, 512], P(('groups', 'band')), parts along dimension 0
- grad_edges: bfloat16 [32, 11, 128, 512], P(('groups', 'band')), parts along dimension 0
- grad_edge_first: bfloat16 [3072, 512], P('groups'), parts along dimension 0
- grad_edge_second: bfloat16 [1024, 512], P('groups'), parts along dimension 0
- grad_node_first: bfloat16 [2048, 512], P('groups'), parts along dimension 0
- grad_node_second: bfloat16 [1024, 512], P('groups'), parts along dimension 0
There are 2 independent parts, one for each index of `groups`. A program takes and returns all parts, laid end to end along the dimension named above; an argument that names none is the same for every part. Nothing has to cross between parts.
Inputs may be any that keep to these rules, and one draw needn't show every extreme that they name: Slots from edge_count on are padding; every edge set is full (128 live slots) on some band. `recv_slot`: indices within the receiver band. `send_slot`: indices within the sender band, the band o_k below the receiver round the loop.
All inputs are finite; a program needn't handle non-finite values.
Results may differ from a plain program's by a relative error of at most 0.0085.
Values may be sent and summed in bfloat16 or wider, within the bound.
No kernel may reach another device: no remote copies, remote signals or barrier semaphores. Data moves between devices by JAX's collectives and lax.ppermute only.
A program may use at most 128 MiB of HBM per device.

v0:
```python
import jax
import jax.numpy as jnp
from jax import lax
from jax.sharding import PartitionSpec as P

band_offsets = (0, 1, -1, 2, -2, 4, -4, 8, -8, 16, -16)
norm_eps = 1e-05


def passed_along(block, axis, distance):
    devices = range(lax.axis_size(axis))
    route = [((i - distance) % len(devices), i) for i in devices]
    return lax.ppermute(block, axis, route)


def swish_act(inputs):
    return inputs * jax.nn.sigmoid(inputs)


def swish_slope(inputs):
    squashed = jax.nn.sigmoid(inputs)
    return squashed * (1.0 + inputs * (1.0 - squashed))


def layer_norm(inputs):
    average = jnp.mean(inputs, axis=-1, keepdims=True)
    centred = inputs - average
    inverse = lax.rsqrt(jnp.mean(centred * centred, axis=-1, keepdims=True) + norm_eps)
    return (centred * inverse, inverse)


def norm_back(normed, inverse, upstream):
    return inverse * (
        upstream
        - jnp.mean(upstream, axis=-1, keepdims=True)
        - normed * jnp.mean(upstream * normed, axis=-1, keepdims=True)
    )


def one_hot_rows(slot_ids, node_count):
    return (slot_ids[..., None] == jnp.arange(node_count, dtype=jnp.int32)).astype(jnp.bfloat16)


def edge_proj(row_block, weight):
    return jnp.einsum("gcd,de->gce", row_block, weight, preferred_element_type=jnp.float32)


def edge_back(row_block, weight):
    return jnp.einsum("gce,de->gcd", row_block, weight, preferred_element_type=jnp.float32)


def edge_outer(left_side, right_side):
    return jnp.einsum("gcd,gce->de", left_side, right_side, preferred_element_type=jnp.float32)


def pick_rows(hot_table, node_block):
    return jnp.einsum(
        "gcn,nd->gcd", hot_table, node_block, preferred_element_type=jnp.float32
    ).astype(jnp.bfloat16)


def spread_rows(hot_table, row_block):
    return jnp.einsum(
        "gcn,gcd->nd", hot_table.astype(jnp.float32), row_block, precision=lax.Precision.HIGHEST
    )


def plain_dot(left_side, right_side):
    return jnp.dot(left_side, right_side, preferred_element_type=jnp.float32)


def dot_right_t(left_side, right_side):
    return lax.dot_general(
        left_side, right_side, (((1,), (1,)), ((), ())), preferred_element_type=jnp.float32
    )


def dot_left_t(left_side, right_side):
    return lax.dot_general(
        left_side, right_side, (((0,), (0,)), ((), ())), preferred_element_type=jnp.float32
    )


def local(
    node_latent,
    edge_latent,
    recv_slot,
    send_slot,
    edge_count,
    edge_first,
    edge_second,
    node_first,
    node_second,
    node_cotan,
    edge_cotan,
):
    band_total = lax.axis_size("band")
    width = node_latent.shape[1]
    node_rows = node_latent.shape[0]
    capacity = edge_latent.shape[2]
    w_edge = edge_first[:width]
    w_send = edge_first[width : 2 * width]
    w_recv = edge_first[2 * width :]
    edge_local = edge_latent[0]
    cotan_local = edge_cotan[0]
    recv_table = one_hot_rows(recv_slot[0], node_rows)
    live = (jnp.arange(capacity, dtype=jnp.int32)[None, :] < edge_count[0][:, None]).astype(
        jnp.float32
    )[:, :, None]
    receiver_x = pick_rows(recv_table, node_latent)
    slot_blocks = []
    for set_index, offset in enumerate(band_offsets):
        back_by = -offset % band_total
        slot_ids = send_slot[0, set_index]
        if back_by != 0:
            slot_ids = passed_along(slot_ids, "band", back_by)
        slot_blocks.append(slot_ids)
    send_table = one_hot_rows(jnp.stack(slot_blocks), node_rows)
    sender_x = pick_rows(send_table, node_latent)
    own_terms = edge_proj(sender_x, w_send).astype(jnp.bfloat16)
    term_blocks = []
    for set_index, offset in enumerate(band_offsets):
        forward_by = offset % band_total
        term_block = own_terms[set_index]
        if forward_by != 0:
            term_block = passed_along(term_block, "band", forward_by)
        term_blocks.append(term_block)
    sender_term = jnp.stack(term_blocks)
    pre_edge = (
        edge_proj(edge_local, w_edge)
        + sender_term.astype(jnp.float32)
        + edge_proj(receiver_x, w_recv)
    )
    act_edge = swish_act(pre_edge).astype(jnp.bfloat16)
    out_edge = edge_proj(act_edge, edge_second)
    normed_edge, inverse_edge = layer_norm(out_edge)
    message_f = live * normed_edge
    message = message_f.astype(jnp.bfloat16)
    edge_new = (edge_local.astype(jnp.float32) + message_f).astype(jnp.bfloat16)
    gathered = jnp.einsum(
        "gcn,gcd->nd", recv_table, message, preferred_element_type=jnp.float32
    ).astype(jnp.bfloat16)
    pre_node = plain_dot(node_latent, node_first[:width]) + plain_dot(gathered, node_first[width:])
    act_node = swish_act(pre_node).astype(jnp.bfloat16)
    out_node = plain_dot(act_node, node_second)
    normed_node, inverse_node = layer_norm(out_node)
    node_new = (node_latent.astype(jnp.float32) + normed_node).astype(jnp.bfloat16)
    grad_out_node = norm_back(normed_node, inverse_node, node_cotan.astype(jnp.float32)).astype(
        jnp.bfloat16
    )
    grad_node_second = dot_left_t(act_node, grad_out_node)
    grad_pre_node = (dot_right_t(grad_out_node, node_second) * swish_slope(pre_node)).astype(
        jnp.bfloat16
    )
    grad_node_first = jnp.concatenate(
        [dot_left_t(node_latent, grad_pre_node), dot_left_t(gathered, grad_pre_node)], axis=0
    )
    grad_gathered = dot_right_t(grad_pre_node, node_first[width:]).astype(jnp.bfloat16)
    grad_nodes = node_cotan.astype(jnp.float32) + dot_right_t(grad_pre_node, node_first[:width])
    grad_at_slots = jnp.einsum(
        "gcn,nd->gcd", recv_table, grad_gathered, preferred_element_type=jnp.float32
    )
    grad_message = live * (cotan_local.astype(jnp.float32) + grad_at_slots)
    grad_out_edge = norm_back(normed_edge, inverse_edge, grad_message).astype(jnp.bfloat16)
    grad_edge_second = edge_outer(act_edge, grad_out_edge)
    grad_pre_edge = (edge_back(grad_out_edge, edge_second) * swish_slope(pre_edge)).astype(
        jnp.bfloat16
    )
    grad_w_edge = edge_outer(edge_local, grad_pre_edge)
    grad_w_recv = edge_outer(receiver_x, grad_pre_edge)
    grad_edges = (cotan_local.astype(jnp.float32) + edge_back(grad_pre_edge, w_edge)).astype(
        jnp.bfloat16
    )
    grad_nodes = grad_nodes + spread_rows(recv_table, edge_back(grad_pre_edge, w_recv))
    grad_blocks = []
    for set_index, offset in enumerate(band_offsets):
        back_by = -offset % band_total
        grad_block = grad_pre_edge[set_index]
        if back_by != 0:
            grad_block = passed_along(grad_block, "band", back_by)
        grad_blocks.append(grad_block)
    grad_sent = jnp.stack(grad_blocks)
    grad_w_send = edge_outer(sender_x, grad_sent)
    grad_nodes = grad_nodes + spread_rows(send_table, edge_back(grad_sent, w_send))
    grad_edge_first = jnp.concatenate([grad_w_edge, grad_w_send, grad_w_recv], axis=0)
    grad_edge_first, grad_edge_second, grad_node_first, grad_node_second = lax.psum(
        (grad_edge_first, grad_edge_second, grad_node_first, grad_node_second), "band"
    )
    return (
        node_new,
        edge_new[None],
        grad_nodes.astype(jnp.bfloat16),
        grad_edges[None],
        grad_edge_first.astype(jnp.bfloat16),
        grad_edge_second.astype(jnp.bfloat16),
        grad_node_first.astype(jnp.bfloat16),
        grad_node_second.astype(jnp.bfloat16),
    )


def solution(mesh):
    return jax.shard_map(
        local,
        mesh=mesh,
        in_specs=(
            P(("groups", "band"), None),
            P(("groups", "band"), None, None, None),
            P(("groups", "band"), None, None),
            P(("groups", "band"), None, None),
            P(("groups", "band"), None),
            P(),
            P(),
            P(),
            P(),
            P(("groups", "band"), None),
            P(("groups", "band"), None, None, None),
        ),
        out_specs=(
            P(("groups", "band"), None),
            P(("groups", "band"), None, None, None),
            P(("groups", "band"), None),
            P(("groups", "band"), None, None, None),
            P("groups", None),
            P("groups", None),
            P("groups", None),
            P("groups", None),
        ),
        check_vma=False,
    )
```

profile of v0, /device:TPU:0, one launch (start us, length us, event | category | flops | bytes accessed | tf_op | source)
XLA Modules:
  0.0 284.2 jit_solution(12913193940058787875)
XLA Ops:
  0.6 0.8 slice_bitcast_fusion.16
  1.5 5.5 %collective-permute-start = (s32[128]{0:T(128)S(1)}, s32[128]{0:T(128)S(1)}, u32[]{:S(2)}, u32[]{:S(2)}) collective-permute-start(s32[128]{0:T(128)S(1)} %get-tuple-element.46), channel_id=1, source_target_pairs={{1,0},{2,1},{3,2},{4,3},{5,4},{6,5},{7,6},{8,7},{9,8},{10,9},{11,1... | collective-permute-start | bytes 1544 | tf_op jit(solution)/shard_map/ppermute | solution.py:13
  7.0 1.1 collective-permute-start.2
  8.1 1.0 collective-permute-start.3
  10.2 1.9 fusion.7
  12.1 2.4 fusion.47
  14.6 1.6 collective-permute-start.5
  16.2 2.9 %collective-permute-start.7 = (s32[128]{0:T(128)S(1)}, s32[128]{0:T(128)S(1)}, u32[]{:S(2)}, u32[]{:S(2)}) collective-permute-start(s32[128]{0:T(128)S(1)} %get-tuple-element.39), channel_id=1, source_target_pairs={{8,0},{9,1},{10,2},{11,3},{12,4},{13,5},{14,6},{15,7},{0,8},{1,9},... | collective-permute-start | bytes 1544 | tf_op jit(solution)/shard_map/ppermute | solution.py:13
  19.2 1.2 fusion.64
  20.9 2.1 fusion.8
  23.0 0.9 convolution_convert_fusion
  24.2 1.0 collective-permute-start.8
  25.3 6.3 %collective-permute-start.9 = (bf16[128,512]{1,0:T(8,128)(2,1)S(1)}, bf16[128,512]{1,0:T(8,128)(2,1)S(1)}, u32[]{:S(2)}, u32[]{:S(2)}) collective-permute-start(bf16[128,512]{1,0:T(8,128)(2,1)S(1)} %get-tuple-element.33), channel_id=1, source_target_pairs={{1,0},{2,1},{3,2},{4,3},{5,4},{6,5},{7,6},{8,7},{9,8},{10,9},{11,1... | collective-permute-start | bytes 393224 | tf_op jit(solution)/shard_map/ppermute | solution.py:13
  31.6 4.7 %collective-permute-start.11 = (bf16[128,512]{1,0:T(8,128)(2,1)S(1)}, bf16[128,512]{1,0:T(8,128)(2,1)S(1)}, u32[]{:S(2)}, u32[]{:S(2)}) collective-permute-start(bf16[128,512]{1,0:T(8,128)(2,1)S(1)} %get-tuple-element.31), channel_id=1, source_target_pairs={{2,0},{3,1},{4,2},{5,3},{6,4},{7,5},{8,6},{9,7},{10,8},{11,9},{12,... | collective-permute-start | bytes 393224 | tf_op jit(solution)/shard_map/ppermute | solution.py:13
  36.3 3.8 %collective-permute-start.13 = (bf16[128,512]{1,0:T(8,128)(2,1)S(1)}, bf16[128,512]{1,0:T(8,128)(2,1)S(1)}, u32[]{:S(2)}, u32[]{:S(2)}) collective-permute-start(bf16[128,512]{1,0:T(8,128)(2,1)S(1)} %get-tuple-element.29), channel_id=1, source_target_pairs={{4,0},{5,1},{6,2},{7,3},{8,4},{9,5},{10,6},{11,7},{12,8},{13,9},{1... | collective-permute-start | bytes 393224 | tf_op jit(solution)/shard_map/ppermute | solution.py:13
  40.4 2.9 %collective-permute-start.15 = (bf16[128,512]{1,0:T(8,128)(2,1)S(1)}, bf16[128,512]{1,0:T(8,128)(2,1)S(1)}, u32[]{:S(2)}, u32[]{:S(2)}) collective-permute-start(bf16[128,512]{1,0:T(8,128)(2,1)S(1)} %get-tuple-element.27), channel_id=1, source_target_pairs={{8,0},{9,1},{10,2},{11,3},{12,4},{13,5},{14,6},{15,7},{0,8},{1,9},... | collective-permute-start | bytes 393224 | tf_op jit(solution)/shard_map/ppermute | solution.py:13
  43.3 1.0 collective-permute-done.12
  44.9 8.9 %collective-permute-done.14 = bf16[128,512]{1,0:T(8,128)(2,1)S(1)} collective-permute-done((bf16[128,512]{1,0:T(8,128)(2,1)S(1)}, bf16[128,512]{1,0:T(8,128)(2,1)S(1)}, u32[]{:S(2)}, u32[]{:S(2)}) %collective-permute-start.14) | collective-permute-done | bytes 131104 | tf_op jit(solution)/shard_map/ppermute | solution.py:13
  53.8 1.4 collective-permute-done.15
  55.2 1.0 add_add_fusion
  56.2 1.1 fusion.72
  58.4 0.9 fusion.30
  60.1 0.8 copy-done.29
  62.5 1.0 fusion.40
  64.2 1.2 fusion.29
  65.4 5.1 %fusion.71 = (f32[11,128]{1,0:T(8,128)S(1)}, f32[11,128]{1,0:T(8,128)S(1)}, f32[11,128,512]{2,1,0:T(8,128)}) fusion(f32[11,128]{1,0:T(8,128)S(1)} %add_rsqrt_fusion, f32[11,128,512]{2,1,0:T(8,128)S(1)} %get-tuple-element.50, f32[11,128]{1,0:T(8,128)S(1)} %broadcast_multiply_fusion.2, bf16[320,512]{1,0:T(8,128)(2,1)} %fusion.29, ...), kind=kOutput, calls=%fused_computation.156 | convolution fusion | flops 635524352 | bytes 8094720 | tf_op jit(solution)/shard_map/gcn,nd->gcd/dot_general | solution.py:160
  70.4 4.0 %multiply_convert_fusion.1 = (bf16[11,128,512]{2,1,0:T(8,128)(2,1)S(1)}, bf16[1,11,128,512]{3,2,1,0:T(8,128)(2,1)}) fusion(f32[11,128,512]{2,1,0:T(8,128)} %get-tuple-element.53, f32[11,128,512]{2,1,0:T(8,128)S(1)} %get-tuple-element.50, f32[11,128]{1,0:T(8,128)S(1)} %broadcast_multiply_fusion, f32[11,128]{1,0:T(8,128)S(1)} %broadcast_multiply_fusion.1, ...), kind=kLoop, calls=%fused_computation.6 | loop fusion | flops 7929856 | bytes 10120704 | tf_op jit(solution)/shard_map/convert_element_type | solution.py:164
  74.4 1.6 multiply_convert_fusion
  76.0 0.9 fusion.45
  77.1 1.2 copy-done.28
  78.3 2.1 fusion.9
  80.4 1.0 convolution_bitcast_fusion.2
  81.7 1.0 fusion.20
  82.8 2.0 convolution_bitcast_fusion.1
  86.3 1.5 fusion.69
  87.8 2.0 fusion.24
  90.8 1.7 collective-permute-start.18
  92.9 2.3 collective-permute-start.20
  95.7 2.4 collective-permute-done.17
  98.1 3.0 %collective-permute-start.23 = (bf16[128,512]{1,0:T(8,128)(2,1)S(1)}, bf16[128,512]{1,0:T(8,128)(2,1)S(1)}, u32[]{:S(2)}, u32[]{:S(2)}) collective-permute-start(bf16[128,512]{1,0:T(8,128)(2,1)S(1)} %get-tuple-element.18), channel_id=1, source_target_pairs={{8,0},{9,1},{10,2},{11,3},{12,4},{13,5},{14,6},{15,7},{0,8},{1,9},... | collective-permute-start | bytes 393224 | tf_op jit(solution)/shard_map/ppermute | solution.py:13
  101.1 2.8 collective-permute-done.21
  104.0 8.7 %collective-permute-done.22 = bf16[128,512]{1,0:T(8,128)(2,1)S(1)} collective-permute-done((bf16[128,512]{1,0:T(8,128)(2,1)S(1)}, bf16[128,512]{1,0:T(8,128)(2,1)S(1)}, u32[]{:S(2)}, u32[]{:S(2)}) %collective-permute-start.22) | collective-permute-done | bytes 131104 | tf_op jit(solution)/shard_map/ppermute | solution.py:13
  112.7 2.2 collective-permute-done.23
  115.0 0.9 fusion.49
  116.3 1.0 convolution_bitcast_fusion.3
  117.3 1.9 pad_maximum_fusion
  119.3 2.8 fusion.28
  122.0 162.2 %all-reduce.2 = (bf16[1536,512]{1,0:T(8,128)(2,1)}, bf16[512,512]{1,0:T(8,128)(2,1)}, bf16[1024,512]{1,0:T(8,128)(2,1)}, bf16[512,512]{1,0:T(8,128)(2,1)}) all-reduce(f32[1536,512]{1,0:T(8,128)} %pad_maximum_fusion, f32[512,512]{1,0:T(8,128)} %convolution_bitcast_fusion.1, ...), channel_id=1, replica_groups=mesh['groups'=2,'band'=16] {'band'}, use_global_device_ids=true, to_apply=%region_8.0 | all-reduce | flops 1835008 | bytes 11010048 | tf_op jit(solution)/shard_map/psum | solution.py:186
  (125 shorter events, 11.2 us)
Async XLA Ops:
  0.6 55.6 %copy-start = (bf16[512,512]{1,0:T(8,128)(2,1)S(1)}, bf16[512,512]{1,0:T(8,128)(2,1)}, u32[]{:S(2)}) copy-start(bf16[512,512]{1,0:T(8,128)(2,1)} %param.17) | copy-start | bytes 1572868
  1.5 13.1 %collective-permute-start = (s32[128]{0:T(128)S(1)}, s32[128]{0:T(128)S(1)}, u32[]{:S(2)}, u32[]{:S(2)}) collective-permute-start(s32[128]{0:T(128)S(1)} %get-tuple-element.46), channel_id=1, source_target_pairs={{1,0},{2,1},{3,2},{4,3},{5,4},{6,5},{7,6},{8,7},{9,8},{10,9},{11,1... | collective-permute-start | bytes 1544 | tf_op jit(solution)/shard_map/ppermute | solution.py:13
  7.0 9.2 %collective-permute-start.1 = (s32[128]{0:T(128)S(1)}, s32[128]{0:T(128)S(1)}, u32[]{:S(2)}, u32[]{:S(2)}) collective-permute-start(s32[128]{0:T(128)S(1)} %get-tuple-element.45), channel_id=1, source_target_pairs={{15,0},{0,1},{1,2},{2,3},{3,4},{4,5},{5,6},{6,7},{7,8},{8,9},{9,10... | collective-permute-start | bytes 1544 | tf_op jit(solution)/shard_map/ppermute | solution.py:13
  7.0 9.3 %collective-permute-start.2 = (s32[128]{0:T(128)S(1)}, s32[128]{0:T(128)S(1)}, u32[]{:S(2)}, u32[]{:S(2)}) collective-permute-start(s32[128]{0:T(128)S(1)} %get-tuple-element.44), channel_id=1, source_target_pairs={{2,0},{3,1},{4,2},{5,3},{6,4},{7,5},{8,6},{9,7},{10,8},{11,9},{12,... | collective-permute-start | bytes 1544 | tf_op jit(solution)/shard_map/ppermute | solution.py:13
  8.1 12.3 %collective-permute-start.3 = (s32[128]{0:T(128)S(1)}, s32[128]{0:T(128)S(1)}, u32[]{:S(2)}, u32[]{:S(2)}) collective-permute-start(s32[128]{0:T(128)S(1)} %get-tuple-element.43), channel_id=1, source_target_pairs={{14,0},{15,1},{0,2},{1,3},{2,4},{3,5},{4,6},{5,7},{6,8},{7,9},{8,1... | collective-permute-start | bytes 1544 | tf_op jit(solution)/shard_map/ppermute | solution.py:13
  9.0 11.3 %collective-permute-start.4 = (s32[128]{0:T(128)S(1)}, s32[128]{0:T(128)S(1)}, u32[]{:S(2)}, u32[]{:S(2)}) collective-permute-start(s32[128]{0:T(128)S(1)} %get-tuple-element.42), channel_id=1, source_target_pairs={{4,0},{5,1},{6,2},{7,3},{8,4},{9,5},{10,6},{11,7},{12,8},{13,9},{1... | collective-permute-start | bytes 1544 | tf_op jit(solution)/shard_map/ppermute | solution.py:13
  12.1 2.5 copy-start.3
  12.1 7.1 %copy-start.8 = (bf16[320,512]{1,0:T(8,128)(2,1)S(1)}, bf16[320,512]{1,0:T(8,128)(2,1)}, u32[]{:S(2)}) copy-start(bf16[320,512]{1,0:T(8,128)(2,1)} %param.11) | copy-start | bytes 983044
  12.1 7.1 %copy-start.16 = (bf16[1024,512]{1,0:T(8,128)(2,1)S(1)}, bf16[1024,512]{1,0:T(8,128)(2,1)}, u32[]{:S(2)}) copy-start(bf16[1024,512]{1,0:T(8,128)(2,1)} %param.18) | copy-start | bytes 3145732
  14.6 5.7 %collective-permute-start.5 = (s32[128]{0:T(128)S(1)}, s32[128]{0:T(128)S(1)}, u32[]{:S(2)}, u32[]{:S(2)}) collective-permute-start(s32[128]{0:T(128)S(1)} %get-tuple-element.41), channel_id=1, source_target_pairs={{12,0},{13,1},{14,2},{15,3},{0,4},{1,5},{2,6},{3,7},{4,8},{5,9},{6... | collective-permute-start | bytes 1544 | tf_op jit(solution)/shard_map/ppermute | solution.py:13
  16.2 4.4 %collective-permute-start.6 = (s32[128]{0:T(128)S(1)}, s32[128]{0:T(128)S(1)}, u32[]{:S(2)}, u32[]{:S(2)}) collective-permute-start(s32[128]{0:T(128)S(1)} %get-tuple-element.40), channel_id=1, source_target_pairs={{8,0},{9,1},{10,2},{11,3},{12,4},{13,5},{14,6},{15,7},{0,8},{1,9},... | collective-permute-start | bytes 1544 | tf_op jit(solution)/shard_map/ppermute | solution.py:13
  16.2 4.6 %collective-permute-start.7 = (s32[128]{0:T(128)S(1)}, s32[128]{0:T(128)S(1)}, u32[]{:S(2)}, u32[]{:S(2)}) collective-permute-start(s32[128]{0:T(128)S(1)} %get-tuple-element.39), channel_id=1, source_target_pairs={{8,0},{9,1},{10,2},{11,3},{12,4},{13,5},{14,6},{15,7},{0,8},{1,9},... | collective-permute-start | bytes 1544 | tf_op jit(solution)/shard_map/ppermute | solution.py:13
  20.9 2.1 copy-start.13
  24.2 31.0 %copy-start.1 = (bf16[1,11,128,512]{3,2,1,0:T(8,128)(2,1)S(1)}, bf16[1,11,128,512]{3,2,1,0:T(8,128)(2,1)}, u32[]{:S(2)}) copy-start(bf16[1,11,128,512]{3,2,1,0:T(8,128)(2,1)} %param.12) | copy-start | bytes 4325380
  24.2 12.1 %collective-permute-start.8 = (bf16[128,512]{1,0:T(8,128)(2,1)S(1)}, bf16[128,512]{1,0:T(8,128)(2,1)S(1)}, u32[]{:S(2)}, u32[]{:S(2)}) collective-permute-start(bf16[128,512]{1,0:T(8,128)(2,1)S(1)} %get-tuple-element.34), channel_id=1, source_target_pairs={{15,0},{0,1},{1,2},{2,3},{3,4},{4,5},{5,6},{6,7},{7,8},{8,9},{9,10... | collective-permute-start | bytes 393224 | tf_op jit(solution)/shard_map/ppermute | solution.py:13
  25.3 14.9 %collective-permute-start.9 = (bf16[128,512]{1,0:T(8,128)(2,1)S(1)}, bf16[128,512]{1,0:T(8,128)(2,1)S(1)}, u32[]{:S(2)}, u32[]{:S(2)}) collective-permute-start(bf16[128,512]{1,0:T(8,128)(2,1)S(1)} %get-tuple-element.33), channel_id=1, source_target_pairs={{1,0},{2,1},{3,2},{4,3},{5,4},{6,5},{7,6},{8,7},{9,8},{10,9},{11,1... | collective-permute-start | bytes 393224 | tf_op jit(solution)/shard_map/ppermute | solution.py:13
  31.6 8.8 %collective-permute-start.10 = (bf16[128,512]{1,0:T(8,128)(2,1)S(1)}, bf16[128,512]{1,0:T(8,128)(2,1)S(1)}, u32[]{:S(2)}, u32[]{:S(2)}) collective-permute-start(bf16[128,512]{1,0:T(8,128)(2,1)S(1)} %get-tuple-element.32), channel_id=1, source_target_pairs={{14,0},{15,1},{0,2},{1,3},{2,4},{3,5},{4,6},{5,7},{6,8},{7,9},{8,1... | collective-permute-start | bytes 393224 | tf_op jit(solution)/shard_map/ppermute | solution.py:13
  31.6 11.7 %collective-permute-start.11 = (bf16[128,512]{1,0:T(8,128)(2,1)S(1)}, bf16[128,512]{1,0:T(8,128)(2,1)S(1)}, u32[]{:S(2)}, u32[]{:S(2)}) collective-permute-start(bf16[128,512]{1,0:T(8,128)(2,1)S(1)} %get-tuple-element.31), channel_id=1, source_target_pairs={{2,0},{3,1},{4,2},{5,3},{6,4},{7,5},{8,6},{9,7},{10,8},{11,9},{12,... | collective-permute-start | bytes 393224 | tf_op jit(solution)/shard_map/ppermute | solution.py:13
  36.3 8.0 %collective-permute-start.12 = (bf16[128,512]{1,0:T(8,128)(2,1)S(1)}, bf16[128,512]{1,0:T(8,128)(2,1)S(1)}, u32[]{:S(2)}, u32[]{:S(2)}) collective-permute-start(bf16[128,512]{1,0:T(8,128)(2,1)S(1)} %get-tuple-element.30), channel_id=1, source_target_pairs={{12,0},{13,1},{14,2},{15,3},{0,4},{1,5},{2,6},{3,7},{4,8},{5,9},{6... | collective-permute-start | bytes 393224 | tf_op jit(solution)/shard_map/ppermute | solution.py:13
  36.3 8.6 %collective-permute-start.13 = (bf16[128,512]{1,0:T(8,128)(2,1)S(1)}, bf16[128,512]{1,0:T(8,128)(2,1)S(1)}, u32[]{:S(2)}, u32[]{:S(2)}) collective-permute-start(bf16[128,512]{1,0:T(8,128)(2,1)S(1)} %get-tuple-element.29), channel_id=1, source_target_pairs={{4,0},{5,1},{6,2},{7,3},{8,4},{9,5},{10,6},{11,7},{12,8},{13,9},{1... | collective-permute-start | bytes 393224 | tf_op jit(solution)/shard_map/ppermute | solution.py:13
  40.2 13.6 %collective-permute-start.14 = (bf16[128,512]{1,0:T(8,128)(2,1)S(1)}, bf16[128,512]{1,0:T(8,128)(2,1)S(1)}, u32[]{:S(2)}, u32[]{:S(2)}) collective-permute-start(bf16[128,512]{1,0:T(8,128)(2,1)S(1)} %get-tuple-element.28), channel_id=1, source_target_pairs={{8,0},{9,1},{10,2},{11,3},{12,4},{13,5},{14,6},{15,7},{0,8},{1,9},... | collective-permute-start | bytes 393224 | tf_op jit(solution)/shard_map/ppermute | solution.py:13
  40.4 14.8 %collective-permute-start.15 = (bf16[128,512]{1,0:T(8,128)(2,1)S(1)}, bf16[128,512]{1,0:T(8,128)(2,1)S(1)}, u32[]{:S(2)}, u32[]{:S(2)}) collective-permute-start(bf16[128,512]{1,0:T(8,128)(2,1)S(1)} %get-tuple-element.27), channel_id=1, source_target_pairs={{8,0},{9,1},{10,2},{11,3},{12,4},{13,5},{14,6},{15,7},{0,8},{1,9},... | collective-permute-start | bytes 393224 | tf_op jit(solution)/shard_map/ppermute | solution.py:13
  56.2 1.6 copy-start.11
  58.4 1.4 copy-start.17
  59.8 1.6 copy-start.21
  59.8 1.2 copy-start.29
  60.9 2.5 copy-start.23
  60.9 1.2 copy-start.6
  70.4 4.0 %copy-start.12 = (f32[11,128,512]{2,1,0:T(8,128)S(1)}, f32[11,128,512]{2,1,0:T(8,128)}, u32[]{:S(2)}) copy-start(f32[11,128,512]{2,1,0:T(8,128)} %copy-done.11) | copy-start | bytes 8650756
  74.4 1.6 copy-start.14
  76.9 1.4 copy-start.28
  78.3 2.1 copy-start.4
  80.4 1.4 copy-start.2
  82.7 2.1 copy-start.5
  82.8 2.0 copy-start.22
  84.8 1.5 copy-start.24
  84.8 1.5 copy-start.26
  87.8 2.1 copy-start.7
  87.8 2.1 copy-start.18
  90.3 5.1 %collective-permute-start.16 = (bf16[128,512]{1,0:T(8,128)(2,1)S(1)}, bf16[128,512]{1,0:T(8,128)(2,1)S(1)}, u32[]{:S(2)}, u32[]{:S(2)}) collective-permute-start(bf16[128,512]{1,0:T(8,128)(2,1)S(1)} %get-tuple-element.25), channel_id=1, source_target_pairs={{1,0},{2,1},{3,2},{4,3},{5,4},{6,5},{7,6},{8,7},{9,8},{10,9},{11,1... | collective-permute-start | bytes 393224 | tf_op jit(solution)/shard_map/ppermute | solution.py:13
  90.8 7.3 %collective-permute-start.17 = (bf16[128,512]{1,0:T(8,128)(2,1)S(1)}, bf16[128,512]{1,0:T(8,128)(2,1)S(1)}, u32[]{:S(2)}, u32[]{:S(2)}) collective-permute-start(bf16[128,512]{1,0:T(8,128)(2,1)S(1)} %get-tuple-element.24), channel_id=1, source_target_pairs={{15,0},{0,1},{1,2},{2,3},{3,4},{4,5},{5,6},{6,7},{7,8},{8,9},{9,10... | collective-permute-start | bytes 393224 | tf_op jit(solution)/shard_map/ppermute | solution.py:13
  90.8 7.2 %collective-permute-start.18 = (bf16[128,512]{1,0:T(8,128)(2,1)S(1)}, bf16[128,512]{1,0:T(8,128)(2,1)S(1)}, u32[]{:S(2)}, u32[]{:S(2)}) collective-permute-start(bf16[128,512]{1,0:T(8,128)(2,1)S(1)} %get-tuple-element.23), channel_id=1, source_target_pairs={{2,0},{3,1},{4,2},{5,3},{6,4},{7,5},{8,6},{9,7},{10,8},{11,9},{12,... | collective-permute-start | bytes 393224 | tf_op jit(solution)/shard_map/ppermute | solution.py:13
  92.6 8.5 %collective-permute-start.19 = (bf16[128,512]{1,0:T(8,128)(2,1)S(1)}, bf16[128,512]{1,0:T(8,128)(2,1)S(1)}, u32[]{:S(2)}, u32[]{:S(2)}) collective-permute-start(bf16[128,512]{1,0:T(8,128)(2,1)S(1)} %get-tuple-element.22), channel_id=1, source_target_pairs={{14,0},{15,1},{0,2},{1,3},{2,4},{3,5},{4,6},{5,7},{6,8},{7,9},{8,1... | collective-permute-start | bytes 393224 | tf_op jit(solution)/shard_map/ppermute | solution.py:13
  92.9 8.2 %collective-permute-start.20 = (bf16[128,512]{1,0:T(8,128)(2,1)S(1)}, bf16[128,512]{1,0:T(8,128)(2,1)S(1)}, u32[]{:S(2)}, u32[]{:S(2)}) collective-permute-start(bf16[128,512]{1,0:T(8,128)(2,1)S(1)} %get-tuple-element.21), channel_id=1, source_target_pairs={{4,0},{5,1},{6,2},{7,3},{8,4},{9,5},{10,6},{11,7},{12,8},{13,9},{1... | collective-permute-start | bytes 393224 | tf_op jit(solution)/shard_map/ppermute | solution.py:13
  95.4 8.6 %collective-permute-start.21 = (bf16[128,512]{1,0:T(8,128)(2,1)S(1)}, bf16[128,512]{1,0:T(8,128)(2,1)S(1)}, u32[]{:S(2)}, u32[]{:S(2)}) collective-permute-start(bf16[128,512]{1,0:T(8,128)(2,1)S(1)} %get-tuple-element.20), channel_id=1, source_target_pairs={{12,0},{13,1},{14,2},{15,3},{0,4},{1,5},{2,6},{3,7},{4,8},{5,9},{6... | collective-permute-start | bytes 393224 | tf_op jit(solution)/shard_map/ppermute | solution.py:13
  98.1 14.6 %collective-permute-start.22 = (bf16[128,512]{1,0:T(8,128)(2,1)S(1)}, bf16[128,512]{1,0:T(8,128)(2,1)S(1)}, u32[]{:S(2)}, u32[]{:S(2)}) collective-permute-start(bf16[128,512]{1,0:T(8,128)(2,1)S(1)} %get-tuple-element.19), channel_id=1, source_target_pairs={{8,0},{9,1},{10,2},{11,3},{12,4},{13,5},{14,6},{15,7},{0,8},{1,9},... | collective-permute-start | bytes 393224 | tf_op jit(solution)/shard_map/ppermute | solution.py:13
  98.1 16.8 %collective-permute-start.23 = (bf16[128,512]{1,0:T(8,128)(2,1)S(1)}, bf16[128,512]{1,0:T(8,128)(2,1)S(1)}, u32[]{:S(2)}, u32[]{:S(2)}) collective-permute-start(bf16[128,512]{1,0:T(8,128)(2,1)S(1)} %get-tuple-element.18), channel_id=1, source_target_pairs={{8,0},{9,1},{10,2},{11,3},{12,4},{13,5},{14,6},{15,7},{0,8},{1,9},... | collective-permute-start | bytes 393224 | tf_op jit(solution)/shard_map/ppermute | solution.py:13
  115.0 1.4 copy-start.20
  (6 other events, 6.1 us)
where the time goes:
time: 286 us; the launch traced here: 284 us
  blocking collectives  162 us (57%)
  starting transfers between devices  39.5 us (14%)
  matrix products  36.7 us (13%)
  waiting for transfers between devices  28.6 us (10%)
  other arithmetic  8.28 us (3%)
  local copies, waits for them, and re-layouts  7.78 us (3%)
    psum x1, blocking collectives, local(): lax.psum((grad_edge_first, grad_edge_second, grad_node_first, grad_node_s...  162 us
    ppermute x24, starting transfers between devices, passed_along(): return lax.ppermute(block, axis, route)  39.5 us
    ppermute x24, waiting for transfers between devices, passed_along(): return lax.ppermute(block, axis, route)  28.6 us
    unnamed x77, local copies, waits for them, and re-layouts  6.61 us
  transfers between devices with their start and end apart: 24, of which 11 were waited for; matrix products, arithmetic and copies ran while one was open for 2% of the time, Pallas kernels for 0%

commit v1 on v0

v1 whole, which is shorter than its diff:
```python
import jax
import jax.numpy as jnp
from jax import lax
from jax.sharding import PartitionSpec as P

band_offsets = (0, 1, -1, 2, -2, 4, -4, 8, -8, 16, -16)
norm_eps = 1e-05


def passed_along(block, axis, distance):
    devices = range(lax.axis_size(axis))
    route = [((i - distance) % len(devices), i) for i in devices]
    return lax.ppermute(block, axis, route)


def swish_slope(inputs):
    squashed = jax.nn.sigmoid(inputs)
    return squashed * (1.0 + inputs * (1.0 - squashed))


def layer_norm(inputs):
    average = jnp.mean(inputs, axis=-1, keepdims=True)
    centred = inputs - average
    inverse = lax.rsqrt(jnp.mean(centred * centred, axis=-1, keepdims=True) + norm_eps)
    return (centred * inverse, inverse)


def norm_back(normed, inverse, upstream):
    return inverse * (
        upstream
        - jnp.mean(upstream, axis=-1, keepdims=True)
        - normed * jnp.mean(upstream * normed, axis=-1, keepdims=True)
    )


def one_hot(slot_ids, node_count):
    return (slot_ids[:, None] == jnp.arange(node_count, dtype=jnp.int32)).astype(jnp.bfloat16)


def dot(left_side, right_side):
    return jnp.dot(left_side, right_side, preferred_element_type=jnp.float32)


def dot_rt(left_side, right_side):
    return lax.dot_general(
        left_side, right_side, (((1,), (1,)), ((), ())), preferred_element_type=jnp.float32
    )


def dot_lt(left_side, right_side):
    return lax.dot_general(
        left_side, right_side, (((0,), (0,)), ((), ())), preferred_element_type=jnp.float32
    )


def local(
    node_latent,
    edge_latent,
    recv_slot,
    send_slot,
    edge_count,
    edge_first,
    edge_second,
    node_first,
    node_second,
    node_cotan,
    edge_cotan,
):
    bf16 = jnp.bfloat16
    f32 = jnp.float32
    bands = lax.axis_size("band")
    me = lax.axis_index("band")
    nodes, width = node_latent.shape
    sets, cap = edge_latent.shape[1:3]
    by_distance = {}
    for k, offset in enumerate(band_offsets):
        by_distance.setdefault(offset % bands, []).append(k)
    order = sorted(by_distance, key=lambda d: -min(d, bands - d))

    w_edge = edge_first[:width]
    w_send = edge_first[width : 2 * width]
    w_recv = edge_first[2 * width :]
    edges = edge_latent[0].reshape(sets * cap, width)
    cotan = edge_cotan[0].reshape(sets * cap, width)
    recv_hot = one_hot(recv_slot[0].reshape(-1), nodes)
    live = (jnp.arange(cap, dtype=jnp.int32)[None, :] < edge_count[0][:, None]).astype(f32)
    live = live.reshape(sets * cap, 1)

    all_ids = lax.all_gather(send_slot[0], "band")
    send_hot = {}
    rows = [None] * sets
    for d in order:
        ids = lax.dynamic_index_in_dim(all_ids, (me + d) % bands, 0, keepdims=False)
        ids = jnp.concatenate([ids[k] for k in by_distance[d]])
        send_hot[d] = one_hot(ids, nodes)
        picked = dot(send_hot[d], node_latent).astype(bf16)
        if d:
            picked = passed_along(picked, "band", d)
        for i, k in enumerate(by_distance[d]):
            rows[k] = picked[i * cap : (i + 1) * cap]
    sender_x = jnp.concatenate(rows)
    receiver_x = dot(recv_hot, node_latent).astype(bf16)

    pre_edge = dot(edges, w_edge) + dot(sender_x, w_send) + dot(receiver_x, w_recv)
    squashed = jax.nn.sigmoid(pre_edge)
    act_edge = (pre_edge * squashed).astype(bf16)
    out_edge = dot(act_edge, edge_second)
    normed_edge, inverse_edge = layer_norm(out_edge)
    message_f = live * normed_edge
    message = message_f.astype(bf16)
    edge_new = (edges.astype(f32) + message_f).astype(bf16)
    gathered = dot_lt(recv_hot, message).astype(bf16)

    pre_node = dot(node_latent, node_first[:width]) + dot(gathered, node_first[width:])
    act_node = (pre_node * jax.nn.sigmoid(pre_node)).astype(bf16)
    normed_node, inverse_node = layer_norm(dot(act_node, node_second))
    node_new = (node_latent.astype(f32) + normed_node).astype(bf16)
    grad_out_node = norm_back(normed_node, inverse_node, node_cotan.astype(f32)).astype(bf16)
    grad_pre_node = (dot_rt(grad_out_node, node_second) * swish_slope(pre_node)).astype(bf16)
    grad_gathered = dot_rt(grad_pre_node, node_first[width:]).astype(bf16)

    grad_message = live * (cotan.astype(f32) + dot(recv_hot, grad_gathered))
    grad_out_edge = norm_back(normed_edge, inverse_edge, grad_message).astype(bf16)
    grad_pre_edge = (dot_rt(grad_out_edge, edge_second) * swish_slope(pre_edge)).astype(bf16)

    arrived = {}
    for d in order:
        block = jnp.concatenate([grad_pre_edge[k * cap : (k + 1) * cap] for k in by_distance[d]])
        arrived[d] = passed_along(block, "band", -d) if d else block

    recv_sum = dot_lt(recv_hot, grad_pre_edge).astype(bf16)
    weight_grads = jnp.concatenate(
        [
            dot_lt(edges, grad_pre_edge),
            dot_lt(sender_x, grad_pre_edge),
            dot_lt(node_latent, recv_sum),
            dot_lt(act_edge, grad_out_edge),
            dot_lt(node_latent, grad_pre_node),
            dot_lt(gathered, grad_pre_node),
            dot_lt(act_node, grad_out_node),
        ]
    ).astype(bf16)
    share = lax.psum_scatter(weight_grads, "band", scatter_dimension=0, tiled=True)
    weight_grads = lax.all_gather(share, "band", axis=0, tiled=True)

    grad_edges = (cotan.astype(f32) + dot_rt(grad_pre_edge, w_edge)).astype(bf16)
    send_sum = dot_lt(
        jnp.concatenate([send_hot[d] for d in order]),
        jnp.concatenate([arrived[d] for d in order]),
    ).astype(bf16)
    grad_nodes = (
        node_cotan.astype(f32)
        + dot_rt(grad_pre_node, node_first[:width])
        + dot_rt(recv_sum, w_recv)
        + dot_rt(send_sum, w_send)
    )
    first = 3 * width
    return (
        node_new,
        edge_new.reshape(edge_latent.shape),
        grad_nodes.astype(bf16),
        grad_edges.reshape(edge_latent.shape),
        weight_grads[:first],
        weight_grads[first : first + width],
        weight_grads[first + width : first + 3 * width],
        weight_grads[first + 3 * width :],
    )


def solution(mesh):
    return jax.shard_map(
        local,
        mesh=mesh,
        in_specs=(
            P(("groups", "band"), None),
            P(("groups", "band"), None, None, None),
            P(("groups", "band"), None, None),
            P(("groups", "band"), None, None),
            P(("groups", "band"), None),
            P(),
            P(),
            P(),
            P(),
            P(("groups", "band"), None),
            P(("groups", "band"), None, None, None),
        ),
        out_specs=(
            P(("groups", "band"), None),
            P(("groups", "band"), None, None, None),
            P(("groups", "band"), None),
            P(("groups", "band"), None, None, None),
            P("groups", None),
            P("groups", None),
            P("groups", None),
            P("groups", None),
        ),
        check_vma=False,
    )
```

time: 286 us -> 255 us (0.89)
  blocking collectives: 162 us -> 23.4 us
  waiting for transfers between devices: 28.6 us -> 101 us
  matrix products: 36.7 us -> 58.6 us
  local copies, waits for them, and re-layouts: 7.78 us -> 27.7 us
  starting transfers between devices: 39.5 us -> 22 us
  between operations: 1.19 us -> 14.5 us
    psum x1 -> x0, blocking collectives: 162 us -> none  [local(): lax.psum((grad_edge_first, grad_edge_second, grad_node_first, grad_node_s...]
    reduce_scatter x0 -> x1, waiting for transfers between devices: none -> 69.9 us  [local(): lax.psum_scatter(weight_grads, 'band', scatter_dimension=0, tiled=True)]
    all_gather x0 -> x1, blocking collectives: none -> 23.4 us  [local(): all_ids = lax.all_gather(send_slot[0], 'band')]
    dot_general x26 -> x31, matrix products: 36.7 us -> 58.6 us  [the longest x16 33.4 us: dot(): return jnp.dot(left_side, right_side, preferred_element_type=jnp.float32)]
    ppermute x24 -> x14, starting transfers between devices: 39.5 us -> 21.9 us  [passed_along(): return lax.ppermute(block, axis, route)]
    all_gather x0 -> x1, waiting for transfers between devices: none -> 17.4 us  [local(): weight_grads = lax.all_gather(share, 'band', axis=0, tiled=True)]
    ppermute x24 -> x14, waiting for transfers between devices: 28.6 us -> 13.5 us  [passed_along(): return lax.ppermute(block, axis, route)]
    unnamed x77 -> x67, local copies, waits for them, and re-layouts: 6.61 us -> 16.7 us
  transfers between devices with their start and end apart: 24 -> 16, of which waited for: 11 -> 6; matrix products, arithmetic and copies ran while one was open for 2% -> 15% of each run, Pallas kernels for 0% -> 0%
where the time goes in v1:
time: 255 us
  waiting for transfers between devices  101 us (40%)
  matrix products  58.6 us (23%)
  local copies, waits for them, and re-layouts  27.7 us (11%)
  blocking collectives  23.4 us (9%)
  starting transfers between devices  22 us (9%)
  between operations  14.5 us (6%)
  other arithmetic  7.42 us (3%)
    reduce_scatter x1, waiting for transfers between devices, local(): lax.psum_scatter(weight_grads, 'band', scatter_dimension=0, tiled=True)  69.9 us
    dot_general x16, matrix products, dot(): return jnp.dot(left_side, right_side, preferred_element_type=jnp.float32)  33.4 us
    all_gather x1, blocking collectives, local(): all_ids = lax.all_gather(send_slot[0], 'band')  23.4 us
    ppermute x14, starting transfers between devices, passed_along(): return lax.ppermute(block, axis, route)  21.9 us
    all_gather x1, waiting for transfers between devices, local(): weight_grads = lax.all_gather(share, 'band', axis=0, tiled=True)  17.4 us
    unnamed x67, local copies, waits for them, and re-layouts  16.7 us
    dot_general x9, matrix products, dot_lt(): lax.dot_general(left_side, right_side, (((0,), (0,)), ((), ())), preferre...  13.7 us
    ppermute x14, waiting for transfers between devices, passed_along(): return lax.ppermute(block, axis, route)  13.5 us
  transfers between devices with their start and end apart: 16, of which 6 were waited for; matrix products, arithmetic and copies ran while one was open for 15% of the time, Pallas kernels for 0%

profile of v1, /device:TPU:0, one launch (start us, length us, event | category | flops | bytes accessed | tf_op | source)
XLA Modules:
  0.0 254.5 jit_solution(12926257708762984948)
XLA Ops:
  8.1 23.4 %all_gather.6 = s32[16,11,128]{2,1,0:T(8,128)S(1)} all-gather(s32[1,11,128]{2,1,0:T(8,128)S(1)} %copy.20), channel_id=1, replica_groups=mesh['groups'=2,'band'=16] {'band'}, dimensions={0}, use_global_device_ids=true | all-gather | bytes 95744 | tf_op jit(solution)/shard_map/all_gather | solution.py:89
  31.5 1.9 convolution_convert_fusion.17
  33.8 1.9 convolution_convert_fusion.16
  35.7 4.1 %collective-permute-start.1 = (bf16[128,512]{1,0:T(8,128)(2,1)}, bf16[128,512]{1,0:T(8,128)(2,1)}, u32[]{:S(2)}, u32[]{:S(2)}) collective-permute-start(bf16[128,512]{1,0:T(8,128)(2,1)} %convolution_convert_fusion.16), channel_id=1, source_target_pairs={{1,0},{2,1},{3,2},{4,3},{5,4},{6,5},{7,6},{8,7},{9,8},{10,9},{11,1... | collective-permute-start | bytes 393224 | tf_op jit(solution)/shard_map/ppermute | solution.py:13
  39.8 1.9 convolution_convert_fusion.15
  41.7 0.9 convolution_convert_fusion.14
  42.6 4.7 %collective-permute-start.3 = (bf16[128,512]{1,0:T(8,128)(2,1)}, bf16[128,512]{1,0:T(8,128)(2,1)}, u32[]{:S(2)}, u32[]{:S(2)}) collective-permute-start(bf16[128,512]{1,0:T(8,128)(2,1)} %convolution_convert_fusion.14), channel_id=1, source_target_pairs={{2,0},{3,1},{4,2},{5,3},{6,4},{7,5},{8,6},{9,7},{10,8},{11,9},{12,... | collective-permute-start | bytes 393224 | tf_op jit(solution)/shard_map/ppermute | solution.py:13
  47.3 0.9 convolution_convert_fusion.13
  50.3 1.1 convolution_convert_fusion.11
  51.7 3.5 %fusion.40 = f32[1408,512]{1,0:T(8,128)} fusion(bf16[1408,512]{1,0:T(8,128)(2,1)S(1)} %bitcast.80, bf16[1536,512]{1,0:T(8,128)(2,1)} %param.16), kind=kOutput, calls=%fused_computation.84 | convolution fusion | flops 738197504 | bytes 4849664 | tf_op jit(solution)/shard_map/dot_general | solution.py:41
  55.4 4.0 %collective-permute-start.5 = (bf16[128,512]{1,0:T(8,128)(2,1)}, bf16[128,512]{1,0:T(8,128)(2,1)S(1)}, u32[]{:S(2)}, u32[]{:S(2)}) collective-permute-start(bf16[128,512]{1,0:T(8,128)(2,1)} %convolution_convert_fusion.12), channel_id=1, source_target_pairs={{4,0},{5,1},{6,2},{7,3},{8,4},{9,5},{10,6},{11,7},{12,8},{13,9},{1... | collective-permute-start | bytes 393224 | tf_op jit(solution)/shard_map/ppermute | solution.py:13
  59.4 1.6 constant_dynamic-update-slice_fusion.6
  61.0 1.6 constant_dynamic-update-slice_fusion.5
  62.6 1.6 constant_dynamic-update-slice_fusion.4
  64.1 1.6 constant_dynamic-update-slice_fusion.3
  67.0 2.1 collective-permute-done.6
  70.6 4.9 %convolution_add_fusion.1 = f32[1408,512]{1,0:T(8,128)} fusion(f32[1408,512]{1,0:T(8,128)} %fusion.40, bf16[1408,512]{1,0:T(8,128)(2,1)} %slice_dynamic-update-slice_fusion.1, bf16[1536,512]{1,0:T(8,128)(2,1)} %param.16), kind=kOutput, calls=%fused_computation.5 | convolution fusion | flops 738918400 | bytes 7733248 | tf_op jit(solution)/shard_map/dot_general | solution.py:41
  75.5 5.3 %convolution_add_fusion = f32[1408,512]{1,0:T(8,128)} fusion(f32[1408,512]{1,0:T(8,128)} %convolution_add_fusion.1, bf16[320,512]{1,0:T(8,128)(2,1)S(1)} %copy-done.1, s32[1408]{0:T(1024)S(1)} %bitcast.83, bf16[1536,512]{1,0:T(8,128)(2,1)} %param.16), kind=kOutput, calls=%fused_computation.4 | convolution fusion | flops 1201463296 | bytes 6624768 | tf_op jit(solution)/shard_map/dot_general | solution.py:41
  80.7 2.9 %fusion.78 = (f32[1408]{0:T(1024)S(1)}, f32[1408,512]{1,0:T(8,128)S(1)}) fusion(bf16[512,512]{1,0:T(8,128)(2,1)S(1)} %copy-done, f32[1408,512]{1,0:T(8,128)} %convolution_add_fusion), kind=kOutput, calls=%fused_computation.168 | convolution fusion | flops 742521472 | bytes 6297088 | tf_op jit(solution)/shard_map/dot_general | solution.py:41
  84.2 1.7 fusion.20
  88.3 1.0 convert_reduce_fusion
  89.4 1.3 fusion.18
  90.7 5.8 %fusion.75 = (f32[1408]{0:T(1024)S(1)}, f32[1408]{0:T(1024)S(1)}, f32[1408,512]{1,0:T(8,128)}) fusion(f32[1408]{0:T(1024)S(1)} %add_rsqrt_fusion, f32[1408,512]{1,0:T(8,128)} %copy-done.2, f32[1408]{0:T(1024)S(1)} %broadcast_multiply_fusion.2, bf16[320,512]{1,0:T(8,128)(2,1)} %fusion.18, bf16[1024,512]{1,0:T(8,128)(2,1)} %param.18, s32[1408]{0:T(1024)S(1)} %bitcast.85, ...), kind=kOutput, calls=%fused_computation.165 | convolution fusion | flops 635524352 | bytes 8094720 | tf_op jit(solution)/shard_map/dot_general | solution.py:41
  96.5 4.5 %multiply_convert_fusion = (bf16[1408,512]{1,0:T(8,128)(2,1)S(1)}, bf16[1408,512]{1,0:T(8,128)(2,1)}) fusion(f32[1408,512]{1,0:T(8,128)} %get-tuple-element.38, f32[1408,512]{1,0:T(8,128)} %copy-done.2, f32[1408]{0:T(1024)S(1)} %broadcast_multiply_fusion, f32[1408]{0:T(1024)S(1)} %broadcast_multiply_fusion.1, f32[1408]{0:T(1024)S(1)} %add_rsqrt_fusion, ...), kind=kLoop, calls=%fused_computation.9 | loop fusion | flops 7929856 | bytes 10120704 | tf_op jit(solution)/shard_map/convert_element_type | solution.py:123
  101.0 1.6 fusion.1
  102.6 1.8 fusion.13
  104.5 1.1 fusion.21
  105.8 1.8 fusion.8
  107.7 1.3 fusion.15
  108.9 1.9 fusion.9
  110.8 1.3 fusion.17
  112.1 1.3 fusion.10
  113.4 1.5 fusion.11
  115.0 69.9 %reduce-scatter.2.cloned.1.call-done = bf16[224,512]{1,0:T(8,128)(2,1)} async-done(((bf16[3584,512]{1,0:T(8,128)(2,1)}), bf16[224,512]{1,0:T(8,128)(2,1)}) %reduce-scatter.2.cloned.1.call-update) | async-done | bytes 229392 | tf_op jit(solution)/shard_map/reduce_scatter | solution.py:143
  185.8 1.2 concatenate.35
  187.0 1.3 collective-permute-start.7
  188.4 1.3 fusion.77
  189.6 2.1 collective-permute-start.8
  191.7 4.8 %collective-permute-start.10 = (bf16[128,512]{1,0:T(8,128)(2,1)S(1)}, bf16[128,512]{1,0:T(8,128)(2,1)S(1)}, u32[]{:S(2)}, u32[]{:S(2)}) collective-permute-start(bf16[128,512]{1,0:T(8,128)(2,1)S(1)} %get-tuple-element.19), channel_id=1, source_target_pairs={{2,0},{3,1},{4,2},{5,3},{6,4},{7,5},{8,6},{9,7},{10,8},{11,9},{12,... | collective-permute-start | bytes 393224 | tf_op jit(solution)/shard_map/ppermute | solution.py:13
  196.5 1.3 convolution_add_fusion.4
  197.9 3.5 %fusion.2 = bf16[1408,512]{1,0:T(8,128)(2,1)} fusion(bf16[1408,512]{1,0:T(8,128)(2,1)S(1)} %copy-done.10, bf16[1408,512]{1,0:T(8,128)(2,1)} %bitcast.89, bf16[1536,512]{1,0:T(8,128)(2,1)S(1)} %copy-done.8), kind=kOutput, calls=%fused_computation.7 | convolution fusion | flops 740360192 | bytes 4849664 | tf_op jit(solution)/shard_map/dot_general | solution.py:45
  201.7 7.6 %collective-permute-done.7 = bf16[256,512]{1,0:T(8,128)(2,1)S(1)} collective-permute-done((bf16[256,512]{1,0:T(8,128)(2,1)S(1)}, bf16[256,512]{1,0:T(8,128)(2,1)S(1)}, u32[]{:S(2)}, u32[]{:S(2)}) %collective-permute-start.7) | collective-permute-done | bytes 262176 | tf_op jit(solution)/shard_map/ppermute | solution.py:13
  214.0 3.7 %collective-permute-done.13 = bf16[128,512]{1,0:T(8,128)(2,1)S(1)} collective-permute-done((bf16[128,512]{1,0:T(8,128)(2,1)S(1)}, bf16[128,512]{1,0:T(8,128)(2,1)S(1)}, u32[]{:S(2)}, u32[]{:S(2)}) %collective-permute-start.13) | collective-permute-done | bytes 131104 | tf_op jit(solution)/shard_map/ppermute | solution.py:13
  219.7 3.4 %fusion.19 = bf16[320,512]{1,0:T(8,128)(2,1)} fusion(f32[320,512]{1,0:T(8,128)S(1)} %convolution_add_fusion.3, pred[1408,320]{1,0:T(8,128)(4,1)} %copy-done.20, bf16[1408,512]{1,0:T(8,128)(2,1)} %slice_dynamic-update-slice_fusion, bf16[1536,512]{1,0:T(8,128)(2,1)S(1)} %copy-done.8), kind=kOutput, calls=%fused_computation.47 | convolution fusion | flops 629637120 | bytes 3399680 | tf_op jit(solution)/shard_map/dot_general | solution.py:45
  223.1 17.4 %all-gather.2.cloned.1.call-done = bf16[3584,512]{1,0:T(8,128)(2,1)} async-done(((bf16[224,512]{1,0:T(8,128)(2,1)}), bf16[3584,512]{1,0:T(8,128)(2,1)}) %all-gather.2.cloned.1.call-update) | async-done | bytes 3670032 | tf_op jit(solution)/shard_map/all_gather | solution.py:144
  240.5 2.7 %slice.153 = bf16[1536,512]{1,0:T(8,128)(2,1)} slice(bf16[3584,512]{1,0:T(8,128)(2,1)} %all-gather.2.cloned.1.call-done), slice={[0:1536], [0:512]} | slice | bytes 3145728 | tf_op jit(solution)/shard_map/slice | solution.py:163
  243.2 2.2 fusion.76
  245.4 2.3 slice.155
  (116 shorter events, 17.7 us)
Async XLA Ops:
  7.2 73.6 %copy-start = (bf16[512,512]{1,0:T(8,128)(2,1)S(1)}, bf16[512,512]{1,0:T(8,128)(2,1)}, u32[]{:S(2)}) copy-start(bf16[512,512]{1,0:T(8,128)(2,1)} %param.17) | copy-start | bytes 1572868
  7.2 34.5 %copy-start.1 = (bf16[320,512]{1,0:T(8,128)(2,1)S(1)}, bf16[320,512]{1,0:T(8,128)(2,1)}, u32[]{:S(2)}) copy-start(bf16[320,512]{1,0:T(8,128)(2,1)} %param.11) | copy-start | bytes 983044
  7.2 177.6 %reduce-scatter.2.cloned.1.call-start = ((), (), s32[]{:S(2)}) async-start(), calls=%async_computation.1 | async-start | bytes 3899392 | tf_op jit(solution)/shard_map/reduce_scatter | solution.py:143
  33.4 21.9 %collective-permute-start = (bf16[128,512]{1,0:T(8,128)(2,1)}, bf16[128,512]{1,0:T(8,128)(2,1)}, u32[]{:S(2)}, u32[]{:S(2)}) collective-permute-start(bf16[128,512]{1,0:T(8,128)(2,1)} %convolution_convert_fusion.17), channel_id=1, source_target_pairs={{15,0},{0,1},{1,2},{2,3},{3,4},{4,5},{5,6},{6,7},{7,8},{8,9},{9,10... | collective-permute-start | bytes 393224 | tf_op jit(solution)/shard_map/ppermute | solution.py:13
  35.7 25.3 %collective-permute-start.1 = (bf16[128,512]{1,0:T(8,128)(2,1)}, bf16[128,512]{1,0:T(8,128)(2,1)}, u32[]{:S(2)}, u32[]{:S(2)}) collective-permute-start(bf16[128,512]{1,0:T(8,128)(2,1)} %convolution_convert_fusion.16), channel_id=1, source_target_pairs={{1,0},{2,1},{3,2},{4,3},{5,4},{6,5},{7,6},{8,7},{9,8},{10,9},{11,1... | collective-permute-start | bytes 393224 | tf_op jit(solution)/shard_map/ppermute | solution.py:13
  41.7 9.7 %copy-start.4 = (bf16[1024,512]{1,0:T(8,128)(2,1)S(1)}, bf16[1024,512]{1,0:T(8,128)(2,1)}, u32[]{:S(2)}) copy-start(bf16[1024,512]{1,0:T(8,128)(2,1)} %param.18) | copy-start | bytes 3145732
  41.7 20.9 %collective-permute-start.2 = (bf16[128,512]{1,0:T(8,128)(2,1)}, bf16[128,512]{1,0:T(8,128)(2,1)}, u32[]{:S(2)}, u32[]{:S(2)}) collective-permute-start(bf16[128,512]{1,0:T(8,128)(2,1)} %convolution_convert_fusion.15), channel_id=1, source_target_pairs={{14,0},{15,1},{0,2},{1,3},{2,4},{3,5},{4,6},{5,7},{6,8},{7,9},{8,1... | collective-permute-start | bytes 393224 | tf_op jit(solution)/shard_map/ppermute | solution.py:13
  42.6 21.5 %collective-permute-start.3 = (bf16[128,512]{1,0:T(8,128)(2,1)}, bf16[128,512]{1,0:T(8,128)(2,1)}, u32[]{:S(2)}, u32[]{:S(2)}) collective-permute-start(bf16[128,512]{1,0:T(8,128)(2,1)} %convolution_convert_fusion.14), channel_id=1, source_target_pairs={{2,0},{3,1},{4,2},{5,3},{6,4},{7,5},{8,6},{9,7},{10,8},{11,9},{12,... | collective-permute-start | bytes 393224 | tf_op jit(solution)/shard_map/ppermute | solution.py:13
  48.3 17.4 %collective-permute-start.4 = (bf16[128,512]{1,0:T(8,128)(2,1)}, bf16[128,512]{1,0:T(8,128)(2,1)S(1)}, u32[]{:S(2)}, u32[]{:S(2)}) collective-permute-start(bf16[128,512]{1,0:T(8,128)(2,1)} %convolution_convert_fusion.13), channel_id=1, source_target_pairs={{12,0},{13,1},{14,2},{15,3},{0,4},{1,5},{2,6},{3,7},{4,8},{5,9},{6... | collective-permute-start | bytes 393224 | tf_op jit(solution)/shard_map/ppermute | solution.py:13
  48.7 3.0 %copy-start.3 = (bf16[1,11,128,512]{3,2,1,0:T(8,128)(2,1)S(1)}, bf16[1,11,128,512]{3,2,1,0:T(8,128)(2,1)}, u32[]{:S(2)}) copy-start(bf16[1,11,128,512]{3,2,1,0:T(8,128)(2,1)} %param.12) | copy-start | bytes 4325380
  51.7 3.6 %copy-start.22 = (s32[1,11]{1,0:T(1,128)S(1)}, s32[1,11]{1,0:T(1,128)}, u32[]{:S(2)}) copy-start(s32[1,11]{1,0:T(1,128)} %param.15) | copy-start | bytes 136
  51.7 3.6 %copy-start.21 = (s32[1,11,128]{2,0,1:T(1,128)S(1)}, s32[1,11,128]{2,0,1:T(1,128)}, u32[]{:S(2)}) copy-start(s32[1,11,128]{2,0,1:T(1,128)} %param.13) | copy-start | bytes 16900
  55.4 11.0 %collective-permute-start.5 = (bf16[128,512]{1,0:T(8,128)(2,1)}, bf16[128,512]{1,0:T(8,128)(2,1)S(1)}, u32[]{:S(2)}, u32[]{:S(2)}) collective-permute-start(bf16[128,512]{1,0:T(8,128)(2,1)} %convolution_convert_fusion.12), channel_id=1, source_target_pairs={{4,0},{5,1},{6,2},{7,3},{8,4},{9,5},{10,6},{11,7},{12,8},{13,9},{1... | collective-permute-start | bytes 393224 | tf_op jit(solution)/shard_map/ppermute | solution.py:13
  61.0 8.2 %collective-permute-start.6 = (bf16[256,512]{1,0:T(8,128)(2,1)}, bf16[256,512]{1,0:T(8,128)(2,1)S(1)}, u32[]{:S(2)}, u32[]{:S(2)}) collective-permute-start(bf16[256,512]{1,0:T(8,128)(2,1)} %convolution_convert_fusion.11), channel_id=1, source_target_pairs={{8,0},{9,1},{10,2},{11,3},{12,4},{13,5},{14,6},{15,7},{0,8},{1,9},... | collective-permute-start | bytes 786440 | tf_op jit(solution)/shard_map/ppermute | solution.py:13
  83.6 2.4 copy-start.2
  84.2 1.8 copy-start.5
  86.0 1.6 copy-start.18
  86.0 1.2 copy-start.23
  87.2 2.2 copy-start.13
  87.2 1.2 copy-start.11
  96.5 4.5 %copy-start.24 = (f32[1408,512]{1,0:T(8,128)S(1)}, f32[1408,512]{1,0:T(8,128)}, u32[]{:S(2)}) copy-start(f32[1408,512]{1,0:T(8,128)} %convolution_add_fusion) | copy-start | bytes 8650756
  102.6 3.0 %copy-start.9 = (bf16[1408,512]{1,0:T(8,128)(2,1)}, bf16[1408,512]{1,0:T(8,128)(2,1)S(1)}, u32[]{:S(2)}) copy-start(bf16[1408,512]{1,0:T(8,128)(2,1)S(1)} %fusion.1) | copy-start | bytes 4325380
  104.5 1.4 copy-start.7
  105.8 1.8 copy-start.16
  108.9 1.9 copy-start.15
  108.9 3.2 %copy-start.19 = (bf16[320,512]{1,0:T(8,128)(2,1)S(1)}, bf16[320,512]{1,0:T(8,128)(2,1)}, u32[]{:S(2)}) copy-start(bf16[320,512]{1,0:T(8,128)(2,1)} %copy-done.18) | copy-start | bytes 983044
  110.8 2.6 %copy-start.14 = (f32[320,512]{1,0:T(8,128)S(1)}, f32[320,512]{1,0:T(8,128)}, u32[]{:S(2)}) copy-start(f32[320,512]{1,0:T(8,128)} %copy-done.13) | copy-start | bytes 1966084
  114.9 81.6 %copy-start.6 = (bf16[1024,512]{1,0:T(8,128)(2,1)S(1)}, bf16[1024,512]{1,0:T(8,128)(2,1)}, u32[]{:S(2)}) copy-start(bf16[1024,512]{1,0:T(8,128)(2,1)} %param.18) | copy-start | bytes 3145732
  114.9 81.6 %copy-start.12 = (bf16[320,512]{1,0:T(8,128)(2,1)S(1)}, bf16[320,512]{1,0:T(8,128)(2,1)}, u32[]{:S(2)}) copy-start(bf16[320,512]{1,0:T(8,128)(2,1)} %param.20) | copy-start | bytes 983044
  114.9 125.6 %all-gather.2.cloned.1.call-start = ((), (), s32[]{:S(2)}) async-start(), calls=%async_computation.2 | async-start | bytes 3899392 | tf_op jit(solution)/shard_map/all_gather | solution.py:144
  185.8 1.2 copy-start.20
  187.0 10.9 %copy-start.8 = (bf16[1536,512]{1,0:T(8,128)(2,1)S(1)}, bf16[1536,512]{1,0:T(8,128)(2,1)}, u32[]{:S(2)}) copy-start(bf16[1536,512]{1,0:T(8,128)(2,1)} %param.16) | copy-start | bytes 4718596
  187.0 10.9 %copy-start.10 = (bf16[1408,512]{1,0:T(8,128)(2,1)S(1)}, bf16[1408,512]{1,0:T(8,128)(2,1)}, u32[]{:S(2)}) copy-start(bf16[1408,512]{1,0:T(8,128)(2,1)} %copy-done.9) | copy-start | bytes 4325380
  187.0 22.3 %collective-permute-start.7 = (bf16[256,512]{1,0:T(8,128)(2,1)S(1)}, bf16[256,512]{1,0:T(8,128)(2,1)S(1)}, u32[]{:S(2)}, u32[]{:S(2)}) collective-permute-start(bf16[256,512]{1,0:T(8,128)(2,1)S(1)} %concatenate.35), channel_id=1, source_target_pairs={{8,0},{9,1},{10,2},{11,3},{12,4},{13,5},{14,6},{15,7},{0,8},{1,9},... | collective-permute-start | bytes 786440 | tf_op jit(solution)/shard_map/ppermute | solution.py:13
  189.6 20.8 %collective-permute-start.8 = (bf16[128,512]{1,0:T(8,128)(2,1)S(1)}, bf16[128,512]{1,0:T(8,128)(2,1)S(1)}, u32[]{:S(2)}, u32[]{:S(2)}) collective-permute-start(bf16[128,512]{1,0:T(8,128)(2,1)S(1)} %get-tuple-element.21), channel_id=1, source_target_pairs={{4,0},{5,1},{6,2},{7,3},{8,4},{9,5},{10,6},{11,7},{12,8},{13,9},{1... | collective-permute-start | bytes 393224 | tf_op jit(solution)/shard_map/ppermute | solution.py:13
  191.7 19.5 %collective-permute-start.9 = (bf16[128,512]{1,0:T(8,128)(2,1)S(1)}, bf16[128,512]{1,0:T(8,128)(2,1)S(1)}, u32[]{:S(2)}, u32[]{:S(2)}) collective-permute-start(bf16[128,512]{1,0:T(8,128)(2,1)S(1)} %get-tuple-element.20), channel_id=1, source_target_pairs={{12,0},{13,1},{14,2},{15,3},{0,4},{1,5},{2,6},{3,7},{4,8},{5,9},{6... | collective-permute-start | bytes 393224 | tf_op jit(solution)/shard_map/ppermute | solution.py:13
  191.7 20.2 %collective-permute-start.10 = (bf16[128,512]{1,0:T(8,128)(2,1)S(1)}, bf16[128,512]{1,0:T(8,128)(2,1)S(1)}, u32[]{:S(2)}, u32[]{:S(2)}) collective-permute-start(bf16[128,512]{1,0:T(8,128)(2,1)S(1)} %get-tuple-element.19), channel_id=1, source_target_pairs={{2,0},{3,1},{4,2},{5,3},{6,4},{7,5},{8,6},{9,7},{10,8},{11,9},{12,... | collective-permute-start | bytes 393224 | tf_op jit(solution)/shard_map/ppermute | solution.py:13
  196.5 16.1 %collective-permute-start.11 = (bf16[128,512]{1,0:T(8,128)(2,1)S(1)}, bf16[128,512]{1,0:T(8,128)(2,1)S(1)}, u32[]{:S(2)}, u32[]{:S(2)}) collective-permute-start(bf16[128,512]{1,0:T(8,128)(2,1)S(1)} %get-tuple-element.18), channel_id=1, source_target_pairs={{14,0},{15,1},{0,2},{1,3},{2,4},{3,5},{4,6},{5,7},{6,8},{7,9},{8,1... | collective-permute-start | bytes 393224 | tf_op jit(solution)/shard_map/ppermute | solution.py:13
  197.9 3.5 %copy-start.17 = (bf16[320,512]{1,0:T(8,128)(2,1)S(1)}, bf16[320,512]{1,0:T(8,128)(2,1)}, u32[]{:S(2)}) copy-start(bf16[320,512]{1,0:T(8,128)(2,1)} %copy-done.16) | copy-start | bytes 983044
  209.3 4.0 %collective-permute-start.12 = (bf16[128,512]{1,0:T(8,128)(2,1)S(1)}, bf16[128,512]{1,0:T(8,128)(2,1)S(1)}, u32[]{:S(2)}, u32[]{:S(2)}) collective-permute-start(bf16[128,512]{1,0:T(8,128)(2,1)S(1)} %get-tuple-element.17), channel_id=1, source_target_pairs={{1,0},{2,1},{3,2},{4,3},{5,4},{6,5},{7,6},{8,7},{9,8},{10,9},{11,1... | collective-permute-start | bytes 393224 | tf_op jit(solution)/shard_map/ppermute | solution.py:13
  210.4 7.3 %collective-permute-start.13 = (bf16[128,512]{1,0:T(8,128)(2,1)S(1)}, bf16[128,512]{1,0:T(8,128)(2,1)S(1)}, u32[]{:S(2)}, u32[]{:S(2)}) collective-permute-start(bf16[128,512]{1,0:T(8,128)(2,1)S(1)} %get-tuple-element.16), channel_id=1, source_target_pairs={{15,0},{0,1},{1,2},{2,3},{3,4},{4,5},{5,6},{6,7},{7,8},{8,9},{9,10... | collective-permute-start | bytes 393224 | tf_op jit(solution)/shard_map/ppermute | solution.py:13
Sparse Core Ops, SparseCore 0:
  115.0 69.7 reduce-scatter.1
  187.4 53.1 all-gather.1

commit v2 on v1

v2 whole, which is shorter than its diff:
```python
import functools

import jax
import jax.numpy as jnp
from jax import lax
from jax.experimental import pallas as pl
from jax.experimental.pallas import tpu as pltpu
from jax.sharding import PartitionSpec as P

band_offsets = (0, 1, -1, 2, -2, 4, -4, 8, -8, 16, -16)
norm_eps = 1e-05
near_sets = 7
id_rows = 16
bf16 = jnp.bfloat16
f32 = jnp.float32
params = pltpu.CompilerParams(vmem_limit_bytes=48 * 1024 * 1024)


def passed_along(block, axis, distance):
    devices = range(lax.axis_size(axis))
    route = [((i - distance) % len(devices), i) for i in devices]
    return lax.ppermute(block, axis, route)


def swapped(block, axis):
    return lax.ppermute(block, axis, [(i, i ^ 1) for i in range(lax.axis_size(axis))])


def layer_norm(inputs):
    average = jnp.mean(inputs, axis=-1, keepdims=True)
    centred = inputs - average
    inverse = lax.rsqrt(jnp.mean(centred * centred, axis=-1, keepdims=True) + norm_eps)
    return (centred * inverse, inverse)


def norm_back(normed, inverse, upstream):
    return inverse * (
        upstream
        - jnp.mean(upstream, axis=-1, keepdims=True)
        - normed * jnp.mean(upstream * normed, axis=-1, keepdims=True)
    )


def slope_of(inputs, squashed):
    return squashed * (1.0 + inputs * (1.0 - squashed))


def dot(left_side, right_side):
    return jnp.dot(left_side, right_side, preferred_element_type=f32)


def dot_rt(left_side, right_side):
    return lax.dot_general(
        left_side, right_side, (((1,), (1,)), ((), ())), preferred_element_type=f32
    )


def dot_lt(left_side, right_side):
    return lax.dot_general(
        left_side, right_side, (((0,), (0,)), ((), ())), preferred_element_type=f32
    )


def pick_table(ids, nodes):
    cap = ids.shape[1]
    down = jnp.transpose(jnp.broadcast_to(ids, (cap, cap)))
    parts = []
    for first in range(0, nodes, cap):
        wide = min(cap, nodes - first)
        lanes = lax.broadcasted_iota(jnp.int32, (cap, wide), 1) + first
        parts.append(jnp.where(down[:, :wide] == lanes, 1.0, 0.0).astype(bf16))
    return jnp.concatenate(parts, axis=1)


def sum_table(ids, nodes):
    down = lax.broadcasted_iota(jnp.int32, (nodes, ids.shape[1]), 0)
    return jnp.where(down == ids, 1.0, 0.0).astype(bf16)


def live_rows(count, cap):
    return (lax.broadcasted_iota(jnp.int32, (cap, 128), 0) < count).astype(f32)


def call(body, outs, scratch, *args, smem=()):
    spaces = [
        pl.BlockSpec(memory_space=pltpu.SMEM if i in smem else pltpu.VMEM) for i in range(len(args))
    ]
    return pl.pallas_call(
        body,
        out_shape=[jax.ShapeDtypeStruct(shape, kind) for shape, kind in outs],
        in_specs=spaces,
        out_specs=[pl.BlockSpec(memory_space=pltpu.VMEM)] * len(outs),
        scratch_shapes=[pltpu.VMEM(shape, kind) for shape, kind in scratch],
        compiler_params=params,
    )(*args)


def pick_kernel(count, *refs):
    node_ref, id_refs, out_refs = refs[0], refs[1 : 1 + count], refs[1 + count :]
    nodes = node_ref.shape[0]
    for id_ref, out_ref in zip(id_refs, out_refs):
        cap = id_ref.shape[1]
        for i in range(id_ref.shape[0]):
            hot = pick_table(id_ref[i : i + 1, :], nodes)
            out_ref[i * cap : (i + 1) * cap, :] = dot(hot, node_ref[...]).astype(bf16)


def forward_rows(rows, x_ref, w1_ref, w2_ref, live_ref, pre_ref, normed_ref, inv_ref, msg_ref):
    pre = dot(x_ref[rows, :], w1_ref[...])
    pre_ref[rows, :] = pre
    act = (pre * jax.nn.sigmoid(pre)).astype(bf16)
    normed, inverse = layer_norm(dot(act, w2_ref[...]))
    normed_ref[rows, :] = normed
    inv_ref[rows, :] = jnp.broadcast_to(inverse, (inverse.shape[0], 128))
    msg_ref[rows, :] = (live_ref[rows, :1] * normed).astype(bf16)
    return act


def near_kernel(plan, *refs):
    sets, sources, count = plan
    (edge_ref, recv_ref, send_ref, count_ref, w1_ref, w2_ref) = refs[:6]
    node_refs = refs[6 : 6 + count]
    (sx_ref, pre_ref, normed_ref, inv_ref, live_ref, sum_ref, x_ref, msg_ref, hot_ref) = refs[6 + count :]
    nodes, width = node_refs[0].shape
    cap = recv_ref.shape[1]
    for i, k in enumerate(sets):
        rows = slice(i * cap, (i + 1) * cap)
        x_ref[rows, :width] = edge_ref[k]
        picked = dot(pick_table(send_ref[k : k + 1, :], nodes), node_refs[sources[i]][...])
        sx_ref[rows, :] = picked.astype(bf16)
        x_ref[rows, width : 2 * width] = picked.astype(bf16)
        picked = dot(pick_table(recv_ref[k : k + 1, :], nodes), node_refs[0][...])
        x_ref[rows, 2 * width :] = picked.astype(bf16)
        live_ref[rows, :] = live_rows(count_ref[0, k], cap)
        hot_ref[:, rows] = sum_table(recv_ref[k : k + 1, :], nodes)
    half = len(sets) * cap // 2

    def step(j, carry):
        rows = pl.ds(pl.multiple_of(j * half, 16), half)
        forward_rows(rows, x_ref, w1_ref, w2_ref, live_ref, pre_ref, normed_ref, inv_ref, msg_ref)
        return carry

    lax.fori_loop(0, 2, step, 0)
    sum_ref[...] = dot(hot_ref[...], msg_ref[...])


def far_kernel(plan, *refs):
    sets, pieces = plan
    count = len(pieces)
    (
        edge_ref,
        cotan_ref,
        recv_ref,
        count_ref,
        w1_ref,
        w2_ref,
        node_ref,
        ncot_ref,
        sum_ref,
        n1_ref,
        n2_ref,
    ) = refs[:11]
    sx_refs = refs[11 : 11 + count]
    gpe_refs = refs[11 + count : 11 + 2 * count]
    (
        act_ref,
        goe_ref,
        new_ref,
        node_new_ref,
        gathered_ref,
        gpn_ref,
        act_node_ref,
        gon_ref,
        gg_ref,
        x_ref,
        live_ref,
        pre_ref,
        normed_ref,
        inv_ref,
        msg_ref,
        hot_ref,
        pick_ref,
        cot_ref,
    ) = refs[11 + 2 * count :]
    nodes, width = node_ref.shape
    cap = recv_ref.shape[1]
    total = len(sets) * cap
    first = 0
    for sx_ref in sx_refs:
        x_ref[first : first + sx_ref.shape[0], width : 2 * width] = sx_ref[...]
        first += sx_ref.shape[0]
    for i, k in enumerate(sets):
        rows = slice(i * cap, (i + 1) * cap)
        x_ref[rows, :width] = edge_ref[k]
        cot_ref[rows, :] = cotan_ref[k]
        hot = pick_table(recv_ref[k : k + 1, :], nodes)
        pick_ref[rows, :] = hot
        x_ref[rows, 2 * width :] = dot(hot, node_ref[...]).astype(bf16)
        live_ref[rows, :] = live_rows(count_ref[0, k], cap)
        hot_ref[:, rows] = sum_table(recv_ref[k : k + 1, :], nodes)
    half = total // 2

    def ahead(j, carry):
        rows = pl.ds(pl.multiple_of(j * half, 16), half)
        act = forward_rows(
            rows, x_ref, w1_ref, w2_ref, live_ref, pre_ref, normed_ref, inv_ref, msg_ref
        )
        act_ref[rows, :] = act
        message = live_ref[rows, :1] * normed_ref[rows, :]
        new_ref[rows, :] = (x_ref[rows, :width].astype(f32) + message).astype(bf16)
        return carry

    lax.fori_loop(0, 2, ahead, 0)
    gathered = (sum_ref[...] + dot(hot_ref[...], msg_ref[...])).astype(bf16)
    gathered_ref[...] = gathered

    pre = dot(node_ref[...], n1_ref[:width, :]) + dot(gathered, n1_ref[width:, :])
    squashed = jax.nn.sigmoid(pre)
    act_node = (pre * squashed).astype(bf16)
    act_node_ref[...] = act_node
    normed, inverse = layer_norm(dot(act_node, n2_ref[...]))
    node_new_ref[...] = (node_ref[...].astype(f32) + normed).astype(bf16)
    gon = norm_back(normed, inverse, ncot_ref[...].astype(f32)).astype(bf16)
    gon_ref[...] = gon
    gpn = (dot_rt(gon, n2_ref[...]) * slope_of(pre, squashed)).astype(bf16)
    gpn_ref[...] = gpn
    gg_ref[...] = dot_rt(gpn, n1_ref[width:, :]).astype(bf16)

    first = 0
    for gpe_ref in gpe_refs:
        size = gpe_ref.shape[0]
        rows = slice(first, first + size)
        upstream = cot_ref[rows, :].astype(f32) + dot(pick_ref[rows, :], gg_ref[...])
        upstream = live_ref[rows, :1] * upstream
        goe = norm_back(normed_ref[rows, :], inv_ref[rows, :1], upstream).astype(bf16)
        goe_ref[rows, :] = goe
        pre = pre_ref[rows, :]
        slope = slope_of(pre, jax.nn.sigmoid(pre))
        gpe_ref[...] = (dot_rt(goe, w2_ref[...]) * slope).astype(bf16)
        first += size


def back_kernel(plan, *refs):
    near, far, local_count, near_count, far_count = plan
    (
        edge_ref,
        cotan_ref,
        recv_ref,
        send_ref,
        core_ref,
        w1_ref,
        w2_ref,
        wx_ref,
        live_ref,
        pre_ref,
        normed_ref,
        inv_ref,
        sx_ref,
        act_far_ref,
        goe_far_ref,
        new_far_ref,
        node_ref,
        ncot_ref,
        gathered_ref,
        gpn_ref,
        act_node_ref,
        gon_ref,
        gg_ref,
    ) = refs[:23]
    sx_far = refs[23 : 23 + far_count]
    gpe_far = refs[23 + far_count : 23 + 2 * far_count]
    outs = refs[23 + 2 * far_count :]
    new_ref, gedge_ref, base_ref, keep_ref, send_out_ref, gpe_local_ref = outs[:6]
    gpe_out = outs[6 : 6 + near_count]
    xe_ref, sxs_ref, acts_ref, goes_ref, gpes_ref, pick_ref, hot_ref, block_ref = outs[6 + near_count :]
    nodes, width = node_ref.shape
    cap = recv_ref.shape[1]
    near_rows = len(near) * cap
    order = near + far
    for i, k in enumerate(order):
        rows = slice(i * cap, (i + 1) * cap)
        xe_ref[rows, :] = edge_ref[k]
        hot_ref[:, rows] = sum_table(recv_ref[k : k + 1, :], nodes)
        if i < len(near):
            pick_ref[rows, :] = pick_table(recv_ref[k : k + 1, :], nodes)
    half = near_rows // 2
    for j in range(2):
        rows = slice(j * half, (j + 1) * half)
        cot = jnp.concatenate([cotan_ref[k] for k in near]).astype(f32)[rows, :]
        upstream = live_ref[rows, :1] * (cot + dot(pick_ref[rows, :], gg_ref[...]))
        goe = norm_back(normed_ref[rows, :], inv_ref[rows, :1], upstream).astype(bf16)
        goes_ref[rows, :] = goe
        pre = pre_ref[rows, :]
        squashed = jax.nn.sigmoid(pre)
        acts_ref[rows, :] = (pre * squashed).astype(bf16)
        gpes_ref[rows, :] = (dot_rt(goe, w2_ref[...]) * slope_of(pre, squashed)).astype(bf16)
    gpe_local_ref[...] = gpes_ref[: local_count * cap, :]
    for j, out_ref in enumerate(gpe_out):
        i = local_count + j
        out_ref[:cap, :] = gpes_ref[i * cap : (i + 1) * cap, :]
        ids = send_ref[near[i] : near[i] + 1, :]
        high, low = ids // 16, ids % 16
        blank = jnp.zeros((1, width - 2 * cap), f32)
        coded = jnp.concatenate([high.astype(f32), low.astype(f32), blank], axis=1)
        out_ref[cap:, :] = jnp.broadcast_to(coded, (id_rows, width)).astype(bf16)
    acts_ref[near_rows:, :] = act_far_ref[...]
    goes_ref[near_rows:, :] = goe_far_ref[...]
    sxs_ref[:near_rows, :] = sx_ref[...]
    first = near_rows
    for one_x, one_g in zip(sx_far, gpe_far):
        rows = slice(first, first + one_x.shape[0])
        sxs_ref[rows, :] = one_x[...]
        gpes_ref[rows, :] = one_g[...]
        first += one_x.shape[0]

    core = core_ref[0]
    half_rows = width // 2

    def put(index, left_side, right_side):
        block_ref[...] = dot_lt(left_side, right_side)
        mine = pl.ds(pl.multiple_of(core * half_rows, half_rows), half_rows)
        other = pl.ds(pl.multiple_of((1 - core) * half_rows, half_rows), half_rows)
        keep_ref[index] = block_ref[mine, :].astype(bf16)
        send_out_ref[index] = block_ref[other, :].astype(bf16)

    recv_sum = dot(hot_ref[...], gpes_ref[...]).astype(bf16)
    put(0, xe_ref[...], gpes_ref[...])
    put(1, sxs_ref[...], gpes_ref[...])
    put(2, node_ref[...], recv_sum)
    put(3, acts_ref[...], goes_ref[...])
    put(4, node_ref[...], gpn_ref[...])
    put(5, gathered_ref[...], gpn_ref[...])
    put(6, act_node_ref[...], gon_ref[...])

    base_ref[...] = (
        ncot_ref[...].astype(f32)
        + dot_rt(gpn_ref[...], wx_ref[...])
        + dot_rt(recv_sum, w1_ref[2 * width :, :])
    )
    for i, k in enumerate(order):
        rows = slice(i * cap, (i + 1) * cap)
        grad = cotan_ref[k].astype(f32) + dot_rt(gpes_ref[rows, :], w1_ref[:width, :])
        gedge_ref[k] = grad.astype(bf16)
        if i < len(near):
            message = live_ref[rows, :1] * normed_ref[rows, :]
            new_ref[k] = (edge_ref[k].astype(f32) + message).astype(bf16)
        else:
            new_ref[k] = new_far_ref[(i - len(near)) * cap : (i - len(near) + 1) * cap, :]


def final_kernel(plan, *refs):
    local_sets, near_count, far_count = plan
    base_ref, ws_ref, send_ref, gpe_local_ref = refs[:4]
    near_refs = refs[4 : 4 + near_count]
    far_refs = refs[4 + near_count : 4 + near_count + far_count]
    id_refs = refs[4 + near_count + far_count : 4 + near_count + 2 * far_count]
    out_ref, hot_ref, rows_ref = refs[4 + near_count + 2 * far_count :]
    nodes = base_ref.shape[0]
    cap = send_ref.shape[1]
    at = 0
    for k in local_sets:
        hot_ref[:, at : at + cap] = sum_table(send_ref[k : k + 1, :], nodes)
        at += cap
    rows_ref[:at, :] = gpe_local_ref[...]
    for near_ref in near_refs:
        coded = near_ref[cap : cap + 8, :].astype(f32)
        ids = (coded[:1, :cap] * 16.0 + coded[:1, cap : 2 * cap]).astype(jnp.int32)
        hot_ref[:, at : at + cap] = sum_table(ids, nodes)
        rows_ref[at : at + cap, :] = near_ref[:cap, :]
        at += cap
    for far_ref, id_ref in zip(far_refs, id_refs):
        rows_ref[at : at + far_ref.shape[0], :] = far_ref[...]
        for i in range(id_ref.shape[0]):
            hot_ref[:, at : at + cap] = sum_table(id_ref[i : i + 1, :], nodes)
            at += cap
    send_sum = dot(hot_ref[...], rows_ref[...]).astype(bf16)
    out_ref[...] = (base_ref[...] + dot_rt(send_sum, ws_ref[...])).astype(bf16)


def join_kernel(core_ref, mine_ref, other_ref, e1_ref, e2_ref, n1_ref, n2_ref):
    core = core_ref[0]
    half_rows = mine_ref.shape[1]
    places = [(e1_ref, 0), (e1_ref, 1), (e1_ref, 2), (e2_ref, 0), (n1_ref, 0), (n1_ref, 1), (n2_ref, 0)]
    for index, (out_ref, block) in enumerate(places):
        first = 2 * block * half_rows
        at = pl.multiple_of(first + core * half_rows, half_rows)
        out_ref[pl.ds(at, half_rows), :] = mine_ref[index]
        at = pl.multiple_of(first + (1 - core) * half_rows, half_rows)
        out_ref[pl.ds(at, half_rows), :] = other_ref[index]


def local(
    node_latent,
    edge_latent,
    recv_slot,
    send_slot,
    edge_count,
    edge_first,
    edge_second,
    node_first,
    node_second,
    node_cotan,
    edge_cotan,
):
    bands = lax.axis_size("band")
    nodes, width = node_latent.shape
    sets, cap = edge_latent.shape[1:3]
    edges, cotan = edge_latent[0], edge_cotan[0]
    recv_ids, send_ids = recv_slot[0], send_slot[0]
    core = (lax.axis_index("band") % 2).reshape(1)

    def reach(d):
        return min(d, bands - d)

    ordered = sorted(range(sets), key=lambda k: (reach(band_offsets[k] % bands), band_offsets[k] % bands))
    near, far = tuple(ordered[:near_sets]), tuple(ordered[near_sets:])
    near_steps = [band_offsets[k] % bands for k in near]
    far_steps = sorted({band_offsets[k] % bands for k in far}, key=lambda d: -reach(d))
    pieces = tuple(tuple(k for k in far if band_offsets[k] % bands == d) for d in far_steps)
    far = sum(pieces, ())
    local_count = sum(d == 0 for d in near_steps)
    local_sets = near[:local_count]
    near_count = len(near) - local_count
    sources = tuple(max(0, i + 1 - local_count) for i in range(len(near)))

    far_ids = [
        passed_along(send_ids[piece[0] : piece[-1] + 1], "band", -d)
        for piece, d in zip(pieces, far_steps)
    ]
    node_blocks = [node_latent] + [passed_along(node_latent, "band", d) for d in near_steps[local_count:]]
    picked = call(
        functools.partial(pick_kernel, len(far_ids)),
        [((len(piece) * cap, width), bf16) for piece in pieces],
        [],
        node_latent,
        *far_ids,
    )
    sx_far = [passed_along(block, "band", d) for block, d in zip(picked, far_steps)]

    near_rows, far_rows = len(near) * cap, len(far) * cap
    sx, pre, normed, inverse, live, part_sum = call(
        functools.partial(near_kernel, (near, sources, len(node_blocks))),
        [
            ((near_rows, width), bf16),
            ((near_rows, width), f32),
            ((near_rows, width), f32),
            ((near_rows, 128), f32),
            ((near_rows, 128), f32),
            ((nodes, width), f32),
        ],
        [
            ((near_rows, 3 * width), bf16),
            ((near_rows, width), bf16),
            ((nodes, near_rows), bf16),
        ],
        edges,
        recv_ids,
        send_ids,
        edge_count,
        edge_first,
        edge_second,
        *node_blocks,
        smem=(3,),
    )

    outs = call(
        functools.partial(far_kernel, (far, pieces)),
        [((len(piece) * cap, width), bf16) for piece in pieces]
        + [((far_rows, width), bf16)] * 3
        + [((nodes, width), bf16)] * 6,
        [
            ((far_rows, 3 * width), bf16),
            ((far_rows, 128), f32),
            ((far_rows, width), f32),
            ((far_rows, width), f32),
            ((far_rows, 128), f32),
            ((far_rows, width), bf16),
            ((nodes, far_rows), bf16),
            ((far_rows, nodes), bf16),
            ((far_rows, width), bf16),
        ],
        edges,
        cotan,
        recv_ids,
        edge_count,
        edge_first,
        edge_second,
        node_latent,
        node_cotan,
        part_sum,
        node_first,
        node_second,
        *sx_far,
        smem=(3,),
    )
    gpe_far, outs = outs[: len(pieces)], outs[len(pieces) :]
    act_far, goe_far, new_far, node_new, gathered, gpn, act_node, gon, gg = outs
    back_far = [passed_along(block, "band", -d) for block, d in zip(gpe_far, far_steps)]

    outs = call(
        functools.partial(back_kernel, (near, far, local_count, near_count, len(pieces))),
        [
            ((sets, cap, width), bf16),
            ((sets, cap, width), bf16),
            ((nodes, width), f32),
            ((7, width // 2, width), bf16),
            ((7, width // 2, width), bf16),
            ((local_count * cap, width), bf16),
        ]
        + [((cap + id_rows, width), bf16)] * near_count,
        [
            ((sets * cap, width), bf16),
            ((sets * cap, width), bf16),
            ((sets * cap, width), bf16),
            ((sets * cap, width), bf16),
            ((sets * cap, width), bf16),
            ((near_rows, nodes), bf16),
            ((nodes, sets * cap), bf16),
            ((width, width), f32),
        ],
        edges,
        cotan,
        recv_ids,
        send_ids,
        core,
        edge_first,
        edge_second,
        node_first[:width],
        live,
        pre,
        normed,
        inverse,
        sx,
        act_far,
        goe_far,
        new_far,
        node_latent,
        node_cotan,
        gathered,
        gpn,
        act_node,
        gon,
        gg,
        *sx_far,
        *gpe_far,
        smem=(4,),
    )
    edge_new, grad_edges, base, keep, sent, gpe_local = outs[:6]
    back_near = [
        passed_along(block, "band", -d) for block, d in zip(outs[6:], near_steps[local_count:])
    ]
    arrived = swapped(sent, "band")
    share = (keep.astype(f32) + arrived.astype(f32)).astype(bf16)
    chips = [[i for i in range(bands) if i % 2 == c] for c in range(2)]
    total = lax.psum((share[:3], share[3:]), "band", axis_index_groups=chips)
    total = jnp.concatenate(total)
    other = swapped(total, "band")

    (grad_nodes,) = call(
        functools.partial(final_kernel, (local_sets, near_count, len(pieces))),
        [((nodes, width), bf16)],
        [((nodes, sets * cap), bf16), ((sets * cap, width), bf16)],
        base,
        edge_first[width : 2 * width],
        send_ids,
        gpe_local,
        *back_near,
        *back_far,
        *far_ids,
    )
    grad_e1, grad_e2, grad_n1, grad_n2 = call(
        join_kernel,
        [
            ((3 * width, width), bf16),
            ((width, width), bf16),
            ((2 * width, width), bf16),
            ((width, width), bf16),
        ],
        [],
        core,
        total,
        other,
        smem=(0,),
    )
    return (
        node_new,
        edge_new[None],
        grad_nodes,
        grad_edges[None],
        grad_e1,
        grad_e2,
        grad_n1,
        grad_n2,
    )


def solution(mesh):
    return jax.shard_map(
        local,
        mesh=mesh,
        in_specs=(
            P(("groups", "band"), None),
            P(("groups", "band"), None, None, None),
            P(("groups", "band"), None, None),
            P(("groups", "band"), None, None),
            P(("groups", "band"), None),
            P(),
            P(),
            P(),
            P(),
            P(("groups", "band"), None),
            P(("groups", "band"), None, None, None),
        ),
        out_specs=(
            P(("groups", "band"), None),
            P(("groups", "band"), None, None, None),
            P(("groups", "band"), None),
            P(("groups", "band"), None, None, None),
            P("groups", None),
            P("groups", None),
            P("groups", None),
            P("groups", None),
        ),
        check_vma=False,
    )
```

time: 255 us -> 225 us (0.88); the launches traced: 255 us -> 221 us
  matrix products: 58.6 us -> 0 us
  Pallas kernels: 0 us -> 36.3 us
  waiting for transfers between devices: 101 us -> 126 us
  blocking collectives: 23.4 us -> 0 us
  local copies, waits for them, and re-layouts: 27.7 us -> 17 us
  other arithmetic: 7.42 us -> 1.93 us
  starting transfers between devices: 22 us -> 25.7 us
    psum x0 -> x1, waiting for transfers between devices: none -> 93.6 us  [local(): total = lax.psum((share[:3], share[3:]), 'band', axis_index_groups=chips)]
    reduce_scatter x1 -> x0, waiting for transfers between devices: 69.9 us -> none  [local(): lax.psum_scatter(weight_grads, 'band', scatter_dimension=0, tiled=True)]
    dot_general x31 -> x0, matrix products: 58.6 us -> none  [the longest x16 33.4 us: dot(): return jnp.dot(left_side, right_side, preferred_element_type=jnp.float32)]
    pallas_call x0 -> x6, Pallas kernels: none -> 36.3 us  [call(): pl.pallas_call(body, out_shape=[jax.ShapeDtypeStruct(shape, kind) for sha...]
    all_gather x1 -> x0, blocking collectives: 23.4 us -> none  [local(): all_ids = lax.all_gather(send_slot[0], 'band')]
    all_gather x1 -> x0, waiting for transfers between devices: 17.4 us -> none  [local(): weight_grads = lax.all_gather(share, 'band', axis=0, tiled=True)]
    ppermute x14 -> x17, waiting for transfers between devices: 13.5 us -> 28 us  [passed_along(): return lax.ppermute(block, axis, route)]
    unnamed x67 -> x35, local copies, waits for them, and re-layouts: 16.7 us -> 10.7 us
  transfers between devices with their start and end apart: 16 -> 20, of which waited for: 6 -> 10; matrix products, arithmetic and copies ran while one was open for 15% -> 3% of each run, Pallas kernels for 0% -> 4%
where the time goes in v2:
time: 225 us; the launch traced here: 221 us
  waiting for transfers between devices  126 us (56%)
  Pallas kernels  36.3 us (16%)
  starting transfers between devices  25.7 us (11%)
  local copies, waits for them, and re-layouts  17 us (8%)
  between operations  14.2 us (6%)
    psum x1, waiting for transfers between devices, local(): total = lax.psum((share[:3], share[3:]), 'band', axis_index_groups=chips)  93.6 us
    pallas_call x6, Pallas kernels, call(): pl.pallas_call(body, out_shape=[jax.ShapeDtypeStruct(shape, kind) for sha...  36.3 us
    ppermute x17, waiting for transfers between devices, passed_along(): return lax.ppermute(block, axis, route)  28 us
    ppermute x17, starting transfers between devices, passed_along(): return lax.ppermute(block, axis, route)  25.6 us
    unnamed x35, local copies, waits for them, and re-layouts  10.7 us
  transfers between devices with their start and end apart: 20, of which 10 were waited for; matrix products, arithmetic and copies ran while one was open for 3% of the time, Pallas kernels for 4%

profile of v2, /device:TPU:0, one launch (start us, length us, event | category | flops | bytes accessed | tf_op | source)
XLA Modules:
  0.0 220.8 jit_solution(7574824641520158811)
XLA Ops:
  7.2 0.5 collective-permute-start
  7.7 5.1 %collective-permute-start.1 = (bf16[320,512]{1,0:T(8,128)(2,1)}, bf16[320,512]{1,0:T(8,128)(2,1)S(1)}, u32[]{:S(2)}, u32[]{:S(2)}) collective-permute-start(bf16[320,512]{1,0:T(8,128)(2,1)} %refs_16_.1), channel_id=1, source_target_pairs={{1,0},{2,1},{3,2},{4,3},{5,4},{6,5},{7,6},{8,7},{9,8},{10,9},{11,1... | collective-permute-start | bytes 983048 | tf_op jit(solution)/shard_map/ppermute | solution.py:22
  12.8 4.7 %collective-permute-start.3 = (bf16[320,512]{1,0:T(8,128)(2,1)}, bf16[320,512]{1,0:T(8,128)(2,1)S(1)}, u32[]{:S(2)}, u32[]{:S(2)}) collective-permute-start(bf16[320,512]{1,0:T(8,128)(2,1)} %refs_16_.1), channel_id=1, source_target_pairs={{2,0},{3,1},{4,2},{5,3},{6,4},{7,5},{8,6},{9,7},{10,8},{11,9},{12,... | collective-permute-start | bytes 983048 | tf_op jit(solution)/shard_map/ppermute | solution.py:22
  17.5 0.7 slice_bitcast_fusion
  18.2 0.4 collective-permute-start.5
  18.6 6.7 %collective-permute-done.5.refs_2_.refs_12_ = s32[1,128]{1,0:T(1,128)S(1)} collective-permute-done((s32[1,128]{1,0:T(1,128)S(1)}, s32[1,128]{1,0:T(1,128)S(1)}, u32[]{:S(2)}, u32[]{:S(2)}) %collective-permute-start.5) | collective-permute-done | bytes 544 | tf_op jit(solution)/shard_map/ppermute | solution.py:22
  25.3 1.6 collective-permute-start.6
  26.8 0.7 slice.30
  27.5 3.1 %collective-permute-done.6.refs_3_.refs_13_ = s32[1,128]{1,0:T(1,128)S(1)} collective-permute-done((s32[1,128]{1,0:T(1,128)S(1)}, s32[1,128]{1,0:T(1,128)S(1)}, u32[]{:S(2)}, u32[]{:S(2)}) %collective-permute-start.6) | collective-permute-done | bytes 544 | tf_op jit(solution)/shard_map/ppermute | solution.py:22
  30.6 0.8 collective-permute-start.4
  31.4 3.7 %collective-permute-done.4.refs_1_.refs_11_ = s32[2,128]{1,0:T(2,128)S(1)} collective-permute-done((s32[2,128]{1,0:T(2,128)S(1)}, s32[2,128]{1,0:T(2,128)S(1)}, u32[]{:S(2)}, u32[]{:S(2)}) %collective-permute-start.4) | collective-permute-done | bytes 1056 | tf_op jit(solution)/shard_map/ppermute | solution.py:22
  35.1 1.0 copy-done.1
  36.0 1.1 shard_map.171
  37.1 0.8 collective-permute-start.7
  37.9 1.7 collective-permute-start.8
  39.6 2.2 collective-permute-start.9
  41.7 0.7 copy.25
  42.4 0.7 copy.26
  43.1 1.9 slice.36.refs_7_
  45.0 1.0 copy-done.2
  46.0 1.0 copy-done.4
  47.0 0.7 copy-done.14
  47.7 7.0 %shard_map.170 = (bf16[896,512]{1,0:T(8,128)(2,1)S(1)}, f32[896,512]{1,0:T(8,128)}, f32[896,512]{1,0:T(8,128)}, f32[896,128]{1,0:T(8,128)S(1)}, f32[896,128]{1,0:T(8,128)S(1)}, /*index=5*/f32[320,512]{1,0:T(8,128)S(1)}) custom-call(bf16[11,128,512]{2,1,0:T(8,128)(2,1)S(1)} %bitcast.20, s32[11,128]{1,0:T(8,128)S(1)} %bitcast.24, s32[11,128]{1,0:T(8,128)S(1)} %bitcast.21, ...), custom_call_target="tpu_custom_call" | custom-call | tf_op jit(solution)/shard_map/pallas_call | solution.py:88
  54.7 0.9 copy-done.7
  55.6 0.8 copy-done.8
  56.5 9.5 %shard_map.172 = (bf16[256,512]{1,0:T(8,128)(2,1)S(1)}, bf16[128,512]{1,0:T(8,128)(2,1)S(1)}, bf16[128,512]{1,0:T(8,128)(2,1)S(1)}, bf16[512,512]{1,0:T(8,128)(2...) custom-call(bf16[11,128,512]{2,1,0:T(8,128)(2,1)} %bitcast.18, ...), custom_call_target="tpu_custom_call" | custom-call | tf_op jit(solution)/shard_map/pallas_call | solution.py:88
  66.0 0.8 copy-done.11
  66.8 0.8 copy-done.12
  67.6 0.8 copy-done.13
  68.4 15.0 %shard_map.173 = (bf16[11,128,512]{2,1,0:T(8,128)(2,1)}, bf16[11,128,512]{2,1,0:T(8,128)(2,1)}, f32[320,512]{1,0:T(8,128)}, bf16[7,256,512]{2,1,0:T(8,128)(2,1)}...) custom-call(bf16[11,128,512]{2,1,0:T(8,128)(2,1)} %bitcast.19, ...), custom_call_target="tpu_custom_call" | custom-call | tf_op jit(solution)/shard_map/pallas_call | solution.py:88
  83.5 4.0 %collective-permute-done.17 = bf16[7,256,512]{2,1,0:T(8,128)(2,1)S(1)} collective-permute-done((bf16[7,256,512]{2,1,0:T(8,128)(2,1)}, bf16[7,256,512]{2,1,0:T(8,128)(2,1)S(1)}, u32[]{:S(2)}, u32[]{:S(2)}) %collective-permute-start.17) | collective-permute-done | bytes 1835040 | tf_op jit(solution)/shard_map/ppermute | solution.py:26
  87.5 1.9 add_convert_fusion
  89.4 0.9 slice.40
  90.3 1.0 slice.41
  91.4 93.6 %all-reduce.3.cloned.1.call-done = (bf16[3,256,512]{2,1,0:T(8,128)(2,1)}, bf16[4,256,512]{2,1,0:T(8,128)(2,1)}) async-done(((bf16[3,256,512]{2,1,0:T(8,128)(2,1)}, bf16[4,256,512]{2,1,0:T(8,128)(2,1)}), (bf16[3,256,512]{2,1,0:T(8,128)(2,1)}, bf16[4,256,512]{2,1,0:T(8,128)(2,1)})) %all-reduce.3.cloned.1.call-update) | async-done | bytes 1835024 | tf_op jit(solution)/shard_map/psum | solution.py:555
  185.0 1.3 constant_dynamic-update-slice_fusion.1
  186.6 2.8 %collective-permute-start.10 = (bf16[144,512]{1,0:T(8,128)(2,1)S(1)}, bf16[144,512]{1,0:T(8,128)(2,1)S(1)}, u32[]{:S(2)}, u32[]{:S(2)}) collective-permute-start(bf16[144,512]{1,0:T(8,128)(2,1)S(1)} %get-tuple-element.67), channel_id=1, source_target_pairs={{1,0},{2,1},{3,2},{4,3},{5,4},{6,5},{7,6},{8,7},{9,8},{10,9},{11,1... | collective-permute-start | bytes 442376 | tf_op jit(solution)/shard_map/ppermute | solution.py:22
  189.4 1.7 collective-permute-start.15
  191.5 1.1 collective-permute-start.14
  192.5 4.4 %collective-permute-done.15.refs_9_ = bf16[128,512]{1,0:T(8,128)(2,1)S(1)} collective-permute-done((bf16[128,512]{1,0:T(8,128)(2,1)S(1)}, bf16[128,512]{1,0:T(8,128)(2,1)S(1)}, u32[]{:S(2)}, u32[]{:S(2)}) %collective-permute-start.15) | collective-permute-done | bytes 131104 | tf_op jit(solution)/shard_map/ppermute | solution.py:22
  197.0 4.1 %collective-permute-done.16.refs_10_ = bf16[128,512]{1,0:T(8,128)(2,1)S(1)} collective-permute-done((bf16[128,512]{1,0:T(8,128)(2,1)S(1)}, bf16[128,512]{1,0:T(8,128)(2,1)S(1)}, u32[]{:S(2)}, u32[]{:S(2)}) %collective-permute-start.16) | collective-permute-done | bytes 131104 | tf_op jit(solution)/shard_map/ppermute | solution.py:22
  201.1 2.0 collective-permute-start.13
  203.1 1.1 slice.37.refs_1_
  204.2 0.8 collective-permute-done.11.refs_5_
  205.0 1.5 collective-permute-done.12.refs_6_
  206.6 3.6 %collective-permute-done.13.refs_7_ = bf16[144,512]{1,0:T(8,128)(2,1)S(1)} collective-permute-done((bf16[144,512]{1,0:T(8,128)(2,1)S(1)}, bf16[144,512]{1,0:T(8,128)(2,1)S(1)}, u32[]{:S(2)}, u32[]{:S(2)}) %collective-permute-start.13) | collective-permute-done | bytes 147488 | tf_op jit(solution)/shard_map/ppermute | solution.py:22
  210.2 1.7 shard_map.174
  211.9 2.1 shard_map.175
  (42 shorter events, 0.8 us)
Async XLA Ops:
  7.2 37.8 %copy-start = (bf16[1,11,128,512]{3,2,1,0:T(8,128)(2,1)S(1)}, bf16[1,11,128,512]{3,2,1,0:T(8,128)(2,1)}, u32[]{:S(2)}) copy-start(bf16[1,11,128,512]{3,2,1,0:T(8,128)(2,1)} %param.12) | copy-start | bytes 4325380
  7.2 177.8 %all-reduce.3.cloned.1.call-start = ((), (), s32[]{:S(2)}) async-start(), calls=%async_computation | async-start | bytes 3670016 | tf_op jit(solution)/shard_map/psum | solution.py:555
  7.2 30.7 %collective-permute-start = (bf16[320,512]{1,0:T(8,128)(2,1)}, bf16[320,512]{1,0:T(8,128)(2,1)S(1)}, u32[]{:S(2)}, u32[]{:S(2)}) collective-permute-start(bf16[320,512]{1,0:T(8,128)(2,1)} %refs_16_.1), channel_id=1, source_target_pairs={{15,0},{0,1},{1,2},{2,3},{3,4},{4,5},{5,6},{6,7},{7,8},{8,9},{9,10... | collective-permute-start | bytes 983048 | tf_op jit(solution)/shard_map/ppermute | solution.py:22
  7.7 31.9 %collective-permute-start.1 = (bf16[320,512]{1,0:T(8,128)(2,1)}, bf16[320,512]{1,0:T(8,128)(2,1)S(1)}, u32[]{:S(2)}, u32[]{:S(2)}) collective-permute-start(bf16[320,512]{1,0:T(8,128)(2,1)} %refs_16_.1), channel_id=1, source_target_pairs={{1,0},{2,1},{3,2},{4,3},{5,4},{6,5},{7,6},{8,7},{9,8},{10,9},{11,1... | collective-permute-start | bytes 983048 | tf_op jit(solution)/shard_map/ppermute | solution.py:22
  12.8 32.2 %collective-permute-start.2 = (bf16[320,512]{1,0:T(8,128)(2,1)}, bf16[320,512]{1,0:T(8,128)(2,1)S(1)}, u32[]{:S(2)}, u32[]{:S(2)}) collective-permute-start(bf16[320,512]{1,0:T(8,128)(2,1)} %refs_16_.1), channel_id=1, source_target_pairs={{14,0},{15,1},{0,2},{1,3},{2,4},{3,5},{4,6},{5,7},{6,8},{7,9},{8,1... | collective-permute-start | bytes 983048 | tf_op jit(solution)/shard_map/ppermute | solution.py:22
  12.8 32.2 %collective-permute-start.3 = (bf16[320,512]{1,0:T(8,128)(2,1)}, bf16[320,512]{1,0:T(8,128)(2,1)S(1)}, u32[]{:S(2)}, u32[]{:S(2)}) collective-permute-start(bf16[320,512]{1,0:T(8,128)(2,1)} %refs_16_.1), channel_id=1, source_target_pairs={{2,0},{3,1},{4,2},{5,3},{6,4},{7,5},{8,6},{9,7},{10,8},{11,9},{12,... | collective-permute-start | bytes 983048 | tf_op jit(solution)/shard_map/ppermute | solution.py:22
  18.2 7.1 %collective-permute-start.5 = (s32[1,128]{1,0:T(1,128)S(1)}, s32[1,128]{1,0:T(1,128)S(1)}, u32[]{:S(2)}, u32[]{:S(2)}) collective-permute-start(s32[1,128]{1,0:T(1,128)S(1)} %get-tuple-element.81), channel_id=1, source_target_pairs={{4,0},{5,1},{6,2},{7,3},{8,4},{9,5},{10,6},{11,7},{12,8},{13,9},{1... | collective-permute-start | bytes 1544 | tf_op jit(solution)/shard_map/ppermute | solution.py:22
  25.3 5.3 %collective-permute-start.6 = (s32[1,128]{1,0:T(1,128)S(1)}, s32[1,128]{1,0:T(1,128)S(1)}, u32[]{:S(2)}, u32[]{:S(2)}) collective-permute-start(s32[1,128]{1,0:T(1,128)S(1)} %get-tuple-element.80), channel_id=1, source_target_pairs={{12,0},{13,1},{14,2},{15,3},{0,4},{1,5},{2,6},{3,7},{4,8},{5,9},{6... | collective-permute-start | bytes 1544 | tf_op jit(solution)/shard_map/ppermute | solution.py:22
  30.6 4.5 %collective-permute-start.4 = (s32[2,128]{1,0:T(2,128)S(1)}, s32[2,128]{1,0:T(2,128)S(1)}, u32[]{:S(2)}, u32[]{:S(2)}) collective-permute-start(s32[2,128]{1,0:T(2,128)S(1)} %bitcast.29), channel_id=1, source_target_pairs={{8,0},{9,1},{10,2},{11,3},{12,4},{13,5},{14,6},{15,7},{0,8},{1,9},... | collective-permute-start | bytes 3080 | tf_op jit(solution)/shard_map/ppermute | solution.py:22
  35.1 1.0 copy-start.1
  37.1 19.3 %collective-permute-start.7 = (bf16[256,512]{1,0:T(8,128)(2,1)}, bf16[256,512]{1,0:T(8,128)(2,1)S(1)}, u32[]{:S(2)}, u32[]{:S(2)}) collective-permute-start(bf16[256,512]{1,0:T(8,128)(2,1)} %get-tuple-element.44), channel_id=1, source_target_pairs={{8,0},{9,1},{10,2},{11,3},{12,4},{13,5},{14,6},{15,7},{0,8},{1,9},... | collective-permute-start | bytes 786440 | tf_op jit(solution)/shard_map/ppermute | solution.py:22
  37.9 18.5 %collective-permute-start.8 = (bf16[128,512]{1,0:T(8,128)(2,1)}, bf16[128,512]{1,0:T(8,128)(2,1)S(1)}, u32[]{:S(2)}, u32[]{:S(2)}) collective-permute-start(bf16[128,512]{1,0:T(8,128)(2,1)} %get-tuple-element.45), channel_id=1, source_target_pairs={{12,0},{13,1},{14,2},{15,3},{0,4},{1,5},{2,6},{3,7},{4,8},{5,9},{6... | collective-permute-start | bytes 393224 | tf_op jit(solution)/shard_map/ppermute | solution.py:22
  39.6 16.9 %collective-permute-start.9 = (bf16[128,512]{1,0:T(8,128)(2,1)S(1)}, bf16[128,512]{1,0:T(8,128)(2,1)S(1)}, u32[]{:S(2)}, u32[]{:S(2)}) collective-permute-start(bf16[128,512]{1,0:T(8,128)(2,1)S(1)} %get-tuple-element.46), channel_id=1, source_target_pairs={{4,0},{5,1},{6,2},{7,3},{8,4},{9,5},{10,6},{11,7},{12,8},{13,9},{1... | collective-permute-start | bytes 393224 | tf_op jit(solution)/shard_map/ppermute | solution.py:22
  45.0 1.0 copy-start.2
  46.0 1.0 copy-start.4
  47.0 0.7 copy-start.14
  47.7 8.8 %copy-start.3 = (bf16[320,512]{1,0:T(8,128)(2,1)S(1)}, bf16[320,512]{1,0:T(8,128)(2,1)}, u32[]{:S(2)}) copy-start(bf16[320,512]{1,0:T(8,128)(2,1)} %refs_16_.1) | copy-start | bytes 983044
  47.7 8.8 %copy-start.5 = (bf16[512,512]{1,0:T(8,128)(2,1)S(1)}, bf16[512,512]{1,0:T(8,128)(2,1)}, u32[]{:S(2)}) copy-start(bf16[512,512]{1,0:T(8,128)(2,1)} %refs_6_.5) | copy-start | bytes 1572868
  47.7 8.8 %copy-start.6 = (bf16[320,512]{1,0:T(8,128)(2,1)S(1)}, bf16[320,512]{1,0:T(8,128)(2,1)}, u32[]{:S(2)}) copy-start(bf16[320,512]{1,0:T(8,128)(2,1)} %refs_17_.1) | copy-start | bytes 983044
  47.7 8.8 %copy-start.10 = (bf16[512,512]{1,0:T(8,128)(2,1)S(1)}, bf16[512,512]{1,0:T(8,128)(2,1)}, u32[]{:S(2)}) copy-start(bf16[512,512]{1,0:T(8,128)(2,1)} %refs_10_.1) | copy-start | bytes 1572868
  54.7 0.9 copy-start.7
  55.6 0.8 copy-start.8
  66.0 0.8 copy-start.11
  66.8 0.8 copy-start.12
  67.6 0.8 copy-start.13
  83.5 4.0 %collective-permute-start.17 = (bf16[7,256,512]{2,1,0:T(8,128)(2,1)}, bf16[7,256,512]{2,1,0:T(8,128)(2,1)S(1)}, u32[]{:S(2)}, u32[]{:S(2)}) collective-permute-start(bf16[7,256,512]{2,1,0:T(8,128)(2,1)} %get-tuple-element.73), channel_id=1, source_target_pairs={{0,1},{1,0},{2,3},{3,2},{4,5},{5,4},{6,7},{7,6},{8,9},{9,8},{10,11... | collective-permute-start | bytes 5505032 | tf_op jit(solution)/shard_map/ppermute | solution.py:26
  185.0 1.5 copy-start.15
  186.3 23.9 %copy-start.9 = (f32[320,512]{1,0:T(8,128)S(1)}, f32[320,512]{1,0:T(8,128)}, u32[]{:S(2)}) copy-start(f32[320,512]{1,0:T(8,128)} %get-tuple-element.65.refs_0_) | copy-start | bytes 1966084
  186.5 25.3 %collective-permute-start.18 = (bf16[7,256,512]{2,1,0:T(8,128)(2,1)S(1)}, bf16[7,256,512]{2,1,0:T(8,128)(2,1)S(1)}, u32[]{:S(2)}, u32[]{:S(2)}) collective-permute-start(bf16[7,256,512]{2,1,0:T(8,128)(2,1)S(1)} %constant_dynamic-update-slice_fusion.mine_ref), channel_id=1, source_target_pairs={{0,1},{1,0},{2,3},{3,2},{4,5},{5,4},{6,7},{7,6},{8,9},{9,8},{10,11... | collective-permute-start | bytes 5505032 | tf_op jit(solution)/shard_map/ppermute | solution.py:26
  186.6 14.5 %collective-permute-start.10 = (bf16[144,512]{1,0:T(8,128)(2,1)S(1)}, bf16[144,512]{1,0:T(8,128)(2,1)S(1)}, u32[]{:S(2)}, u32[]{:S(2)}) collective-permute-start(bf16[144,512]{1,0:T(8,128)(2,1)S(1)} %get-tuple-element.67), channel_id=1, source_target_pairs={{1,0},{2,1},{3,2},{4,3},{5,4},{6,5},{7,6},{8,7},{9,8},{10,9},{11,1... | collective-permute-start | bytes 442376 | tf_op jit(solution)/shard_map/ppermute | solution.py:22
  189.4 7.5 %collective-permute-start.15 = (bf16[128,512]{1,0:T(8,128)(2,1)S(1)}, bf16[128,512]{1,0:T(8,128)(2,1)S(1)}, u32[]{:S(2)}, u32[]{:S(2)}) collective-permute-start(bf16[128,512]{1,0:T(8,128)(2,1)S(1)} %get-tuple-element.62.refs_27_), channel_id=1, source_target_pairs={{4,0},{5,1},{6,2},{7,3},{8,4},{9,5},{10,6},{11,7},{12,8},{13,9},{1... | collective-permute-start | bytes 393224 | tf_op jit(solution)/shard_map/ppermute | solution.py:22
  191.1 10.0 %collective-permute-start.16 = (bf16[128,512]{1,0:T(8,128)(2,1)S(1)}, bf16[128,512]{1,0:T(8,128)(2,1)S(1)}, u32[]{:S(2)}, u32[]{:S(2)}) collective-permute-start(bf16[128,512]{1,0:T(8,128)(2,1)S(1)} %get-tuple-element.63.refs_28_), channel_id=1, source_target_pairs={{12,0},{13,1},{14,2},{15,3},{0,4},{1,5},{2,6},{3,7},{4,8},{5,9},{6... | collective-permute-start | bytes 393224 | tf_op jit(solution)/shard_map/ppermute | solution.py:22
  191.5 18.7 %collective-permute-start.14 = (bf16[256,512]{1,0:T(8,128)(2,1)S(1)}, bf16[256,512]{1,0:T(8,128)(2,1)S(1)}, u32[]{:S(2)}, u32[]{:S(2)}) collective-permute-start(bf16[256,512]{1,0:T(8,128)(2,1)S(1)} %get-tuple-element.61.refs_26_), channel_id=1, source_target_pairs={{8,0},{9,1},{10,2},{11,3},{12,4},{13,5},{14,6},{15,7},{0,8},{1,9},... | collective-permute-start | bytes 786440 | tf_op jit(solution)/shard_map/ppermute | solution.py:22
  197.0 8.0 %collective-permute-start.11 = (bf16[144,512]{1,0:T(8,128)(2,1)S(1)}, bf16[144,512]{1,0:T(8,128)(2,1)S(1)}, u32[]{:S(2)}, u32[]{:S(2)}) collective-permute-start(bf16[144,512]{1,0:T(8,128)(2,1)S(1)} %get-tuple-element.68), channel_id=1, source_target_pairs={{15,0},{0,1},{1,2},{2,3},{3,4},{4,5},{5,6},{6,7},{7,8},{8,9},{9,10... | collective-permute-start | bytes 442376 | tf_op jit(solution)/shard_map/ppermute | solution.py:22
  201.1 5.5 %collective-permute-start.12 = (bf16[144,512]{1,0:T(8,128)(2,1)S(1)}, bf16[144,512]{1,0:T(8,128)(2,1)S(1)}, u32[]{:S(2)}, u32[]{:S(2)}) collective-permute-start(bf16[144,512]{1,0:T(8,128)(2,1)S(1)} %get-tuple-element.69), channel_id=1, source_target_pairs={{2,0},{3,1},{4,2},{5,3},{6,4},{7,5},{8,6},{9,7},{10,8},{11,9},{12,... | collective-permute-start | bytes 442376 | tf_op jit(solution)/shard_map/ppermute | solution.py:22
  201.1 9.1 %collective-permute-start.13 = (bf16[144,512]{1,0:T(8,128)(2,1)S(1)}, bf16[144,512]{1,0:T(8,128)(2,1)S(1)}, u32[]{:S(2)}, u32[]{:S(2)}) collective-permute-start(bf16[144,512]{1,0:T(8,128)(2,1)S(1)} %get-tuple-element.70), channel_id=1, source_target_pairs={{14,0},{15,1},{0,2},{1,3},{2,4},{3,5},{4,6},{5,7},{6,8},{7,9},{8,1... | collective-permute-start | bytes 442376 | tf_op jit(solution)/shard_map/ppermute | solution.py:22
Sparse Core Ops, SparseCore 0:
  91.5 93.4 all-reduce.2

commit v3 on v2

v3 whole, which is shorter than its diff:
```python
import functools

import jax
import jax.numpy as jnp
from jax import lax
from jax.experimental import pallas as pl
from jax.experimental.pallas import tpu as pltpu
from jax.sharding import PartitionSpec as P

band_offsets = (0, 1, -1, 2, -2, 4, -4, 8, -8, 16, -16)
norm_eps = 1e-05
near_sets = 7
bf16 = jnp.bfloat16
f32 = jnp.float32
params = pltpu.CompilerParams(vmem_limit_bytes=48 * 1024 * 1024)


def passed_along(block, axis, distance):
    devices = range(lax.axis_size(axis))
    route = [((i - distance) % len(devices), i) for i in devices]
    return lax.ppermute(block, axis, route)


def layer_norm(inputs):
    average = jnp.mean(inputs, axis=-1, keepdims=True)
    centred = inputs - average
    inverse = lax.rsqrt(jnp.mean(centred * centred, axis=-1, keepdims=True) + norm_eps)
    return (centred * inverse, inverse)


def norm_back(normed, inverse, upstream):
    return inverse * (
        upstream
        - jnp.mean(upstream, axis=-1, keepdims=True)
        - normed * jnp.mean(upstream * normed, axis=-1, keepdims=True)
    )


def slope_of(inputs, squashed):
    return squashed * (1.0 + inputs * (1.0 - squashed))


def dot(left_side, right_side):
    return jnp.dot(left_side, right_side, preferred_element_type=f32)


def dot_rt(left_side, right_side):
    return lax.dot_general(
        left_side, right_side, (((1,), (1,)), ((), ())), preferred_element_type=f32
    )


def dot_lt(left_side, right_side):
    return lax.dot_general(
        left_side, right_side, (((0,), (0,)), ((), ())), preferred_element_type=f32
    )


def pick_table(ids, nodes):
    cap = ids.shape[1]
    down = jnp.transpose(jnp.broadcast_to(ids, (cap, cap)))
    parts = []
    for first in range(0, nodes, cap):
        wide = min(cap, nodes - first)
        lanes = lax.broadcasted_iota(jnp.int32, (cap, wide), 1) + first
        parts.append(jnp.where(down[:, :wide] == lanes, 1.0, 0.0).astype(bf16))
    return jnp.concatenate(parts, axis=1)


def sum_table(ids, nodes):
    down = lax.broadcasted_iota(jnp.int32, (nodes, ids.shape[1]), 0)
    return jnp.where(down == ids, 1.0, 0.0).astype(bf16)


def live_rows(count, cap):
    return (lax.broadcasted_iota(jnp.int32, (cap, 128), 0) < count).astype(f32)


def call(body, outs, scratch, *args, smem=()):
    spaces = [
        pl.BlockSpec(memory_space=pltpu.SMEM if i in smem else pltpu.VMEM) for i in range(len(args))
    ]
    return pl.pallas_call(
        body,
        out_shape=[jax.ShapeDtypeStruct(shape, kind) for shape, kind in outs],
        in_specs=spaces,
        out_specs=[pl.BlockSpec(memory_space=pltpu.VMEM)] * len(outs),
        scratch_shapes=[pltpu.VMEM(shape, kind) for shape, kind in scratch],
        compiler_params=params,
    )(*args)


def pick_kernel(plan, *refs):
    node_ref = refs[0]
    nodes = node_ref.shape[0]
    for id_ref, out_ref, sets in zip(refs[1 : 1 + len(plan)], refs[1 + len(plan) :], plan):
        cap = id_ref.shape[2]
        for i, k in enumerate(sets):
            hot = pick_table(id_ref[k], nodes)
            out_ref[i * cap : (i + 1) * cap, :] = dot(hot, node_ref[...]).astype(bf16)


def forward_rows(rows, x_ref, w1_ref, w2_ref, live_ref, pre_ref, normed_ref, inv_ref, msg_ref):
    pre = dot(x_ref[rows, :], w1_ref[...])
    pre_ref[rows, :] = pre
    act = (pre * jax.nn.sigmoid(pre)).astype(bf16)
    normed, inverse = layer_norm(dot(act, w2_ref[...]))
    normed_ref[rows, :] = normed
    inv_ref[rows, :] = jnp.broadcast_to(inverse, (inverse.shape[0], 128))
    msg_ref[rows, :] = (live_ref[rows, :1] * normed).astype(bf16)
    return act


def near_kernel(plan, *refs):
    sets, local_count = plan
    (edge_ref, recv_ref, send_ref, count_ref, w1_ref, w2_ref, node_ref) = refs[:7]
    remote = len(sets) - local_count
    in_refs = refs[7 : 7 + remote]
    (
        sx_ref,
        act_ref,
        pre_ref,
        normed_ref,
        inv_ref,
        live_ref,
        sum_ref,
        x_ref,
        msg_ref,
        hot_ref,
    ) = refs[7 + remote :]
    nodes, width = node_ref.shape
    cap = recv_ref.shape[2]
    for i, k in enumerate(sets):
        rows = slice(i * cap, (i + 1) * cap)
        x_ref[rows, :width] = edge_ref[k]
        if i < local_count:
            picked = dot(pick_table(send_ref[k], nodes), node_ref[...]).astype(bf16)
            sx_ref[rows, :] = picked
        else:
            picked = in_refs[i - local_count][...]
        x_ref[rows, width : 2 * width] = picked
        picked = dot(pick_table(recv_ref[k], nodes), node_ref[...])
        x_ref[rows, 2 * width :] = picked.astype(bf16)
        live_ref[rows, :] = live_rows(count_ref[0, k], cap)
        hot_ref[:, rows] = sum_table(recv_ref[k], nodes)
    half = len(sets) * cap // 2

    def step(j, carry):
        rows = pl.ds(pl.multiple_of(j * half, 16), half)
        act_ref[rows, :] = forward_rows(
            rows, x_ref, w1_ref, w2_ref, live_ref, pre_ref, normed_ref, inv_ref, msg_ref
        )
        return carry

    lax.fori_loop(0, 2, step, 0)
    sum_ref[...] = dot(hot_ref[...], msg_ref[...])


def far_kernel(plan, *refs):
    sets, pieces = plan
    count = len(pieces)
    (
        edge_ref,
        cotan_ref,
        recv_ref,
        count_ref,
        w1_ref,
        w2_ref,
        node_ref,
        ncot_ref,
        sum_ref,
        n1_ref,
        n2_ref,
    ) = refs[:11]
    sx_refs = refs[11 : 11 + count]
    gpe_refs = refs[11 + count : 11 + 2 * count]
    (
        act_ref,
        goe_ref,
        new_ref,
        node_new_ref,
        gathered_ref,
        gpn_ref,
        act_node_ref,
        gon_ref,
        gg_ref,
        x_ref,
        live_ref,
        pre_ref,
        normed_ref,
        inv_ref,
        msg_ref,
        hot_ref,
        pick_ref,
        cot_ref,
    ) = refs[11 + 2 * count :]
    nodes, width = node_ref.shape
    cap = recv_ref.shape[2]
    total = len(sets) * cap
    first = 0
    for sx_ref in sx_refs:
        x_ref[first : first + sx_ref.shape[0], width : 2 * width] = sx_ref[...]
        first += sx_ref.shape[0]
    for i, k in enumerate(sets):
        rows = slice(i * cap, (i + 1) * cap)
        x_ref[rows, :width] = edge_ref[k]
        cot_ref[rows, :] = cotan_ref[k]
        hot = pick_table(recv_ref[k], nodes)
        pick_ref[rows, :] = hot
        x_ref[rows, 2 * width :] = dot(hot, node_ref[...]).astype(bf16)
        live_ref[rows, :] = live_rows(count_ref[0, k], cap)
        hot_ref[:, rows] = sum_table(recv_ref[k], nodes)
    half = total // 2

    def ahead(j, carry):
        rows = pl.ds(pl.multiple_of(j * half, 16), half)
        act = forward_rows(
            rows, x_ref, w1_ref, w2_ref, live_ref, pre_ref, normed_ref, inv_ref, msg_ref
        )
        act_ref[rows, :] = act
        message = live_ref[rows, :1] * normed_ref[rows, :]
        new_ref[rows, :] = (x_ref[rows, :width].astype(f32) + message).astype(bf16)
        return carry

    lax.fori_loop(0, 2, ahead, 0)
    gathered = (sum_ref[...] + dot(hot_ref[...], msg_ref[...])).astype(bf16)
    gathered_ref[...] = gathered

    pre = dot(node_ref[...], n1_ref[:width, :]) + dot(gathered, n1_ref[width:, :])
    squashed = jax.nn.sigmoid(pre)
    act_node = (pre * squashed).astype(bf16)
    act_node_ref[...] = act_node
    normed, inverse = layer_norm(dot(act_node, n2_ref[...]))
    node_new_ref[...] = (node_ref[...].astype(f32) + normed).astype(bf16)
    gon = norm_back(normed, inverse, ncot_ref[...].astype(f32)).astype(bf16)
    gon_ref[...] = gon
    gpn = (dot_rt(gon, n2_ref[...]) * slope_of(pre, squashed)).astype(bf16)
    gpn_ref[...] = gpn
    gg_ref[...] = dot_rt(gpn, n1_ref[width:, :]).astype(bf16)

    first = 0
    for gpe_ref in gpe_refs:
        size = gpe_ref.shape[0]
        rows = slice(first, first + size)
        upstream = cot_ref[rows, :].astype(f32) + dot(pick_ref[rows, :], gg_ref[...])
        upstream = live_ref[rows, :1] * upstream
        goe = norm_back(normed_ref[rows, :], inv_ref[rows, :1], upstream).astype(bf16)
        goe_ref[rows, :] = goe
        pre = pre_ref[rows, :]
        slope = slope_of(pre, jax.nn.sigmoid(pre))
        gpe_ref[...] = (dot_rt(goe, w2_ref[...]) * slope).astype(bf16)
        first += size


def back_kernel(plan, *refs):
    near, local_count = plan
    (
        cotan_ref,
        recv_ref,
        me_ref,
        w2_ref,
        live_ref,
        pre_ref,
        normed_ref,
        inv_ref,
        node_ref,
        gathered_ref,
        gpn_ref,
        act_node_ref,
        gon_ref,
        gg_ref,
        keep_ref,
        sent_ref,
        goe_ref,
        local_ref,
    ) = refs[:18]
    gpe_refs, (gpe_ref, pick_ref, block_ref) = refs[18:-3], refs[-3:]
    nodes, width = node_ref.shape
    cap = recv_ref.shape[2]
    for i, k in enumerate(near):
        pick_ref[i * cap : (i + 1) * cap, :] = pick_table(recv_ref[k], nodes)
    half = len(near) * cap // 2
    for j in range(2):
        rows = slice(j * half, (j + 1) * half)
        cot = jnp.concatenate([cotan_ref[k] for k in near])[rows, :].astype(f32)
        upstream = live_ref[rows, :1] * (cot + dot(pick_ref[rows, :], gg_ref[...]))
        goe = norm_back(normed_ref[rows, :], inv_ref[rows, :1], upstream).astype(bf16)
        goe_ref[rows, :] = goe
        pre = pre_ref[rows, :]
        slope = slope_of(pre, jax.nn.sigmoid(pre))
        gpe_ref[rows, :] = (dot_rt(goe, w2_ref[...]) * slope).astype(bf16)
    local_ref[...] = gpe_ref[: local_count * cap, :]
    for j, out_ref in enumerate(gpe_refs):
        i = local_count + j
        out_ref[...] = gpe_ref[i * cap : (i + 1) * cap, :]
    put = functools.partial(put_block, me_ref, block_ref, keep_ref, sent_ref)
    put(0, node_ref[...], gpn_ref[...])
    put(1, gathered_ref[...], gpn_ref[...])
    put(2, act_node_ref[...], gon_ref[...])


def put_block(me_ref, block_ref, keep_ref, sent_ref, index, left_side, right_side):
    core = lax.rem(me_ref[0], 2)
    half = block_ref.shape[0] // 2
    block_ref[...] = dot_lt(left_side, right_side)
    keep_ref[index] = block_ref[pl.ds(pl.multiple_of(core * half, half), half), :]
    other = block_ref[pl.ds(pl.multiple_of((1 - core) * half, half), half), :]
    sent_ref[index] = other.astype(bf16)


def stack_into(out_ref, refs):
    first = 0
    for ref in refs:
        out_ref[first : first + ref.shape[0], :] = ref[...]
        first += ref.shape[0]


def weight_kernel(plan, *refs):
    order, sx_count, gpe_count, act_count = plan
    edge_ref, recv_ref, me_ref, node_ref = refs[:4]
    refs = refs[4:]
    sx_refs, refs = refs[:sx_count], refs[sx_count:]
    gpe_refs, refs = refs[:gpe_count], refs[gpe_count:]
    act_refs, refs = refs[:act_count], refs[act_count:]
    goe_refs, refs = refs[:act_count], refs[act_count:]
    keep_ref, sent_ref, rsum_ref, x_ref, sx_ref, gpe_ref, act_ref, goe_ref, hot_ref, block_ref = refs
    nodes = node_ref.shape[0]
    cap = recv_ref.shape[2]
    for i, k in enumerate(order):
        rows = slice(i * cap, (i + 1) * cap)
        x_ref[rows, :] = edge_ref[k]
        hot_ref[:, rows] = sum_table(recv_ref[k], nodes)
    stack_into(sx_ref, sx_refs)
    stack_into(gpe_ref, gpe_refs)
    stack_into(act_ref, act_refs)
    stack_into(goe_ref, goe_refs)
    recv_sum = dot(hot_ref[...], gpe_ref[...]).astype(bf16)
    rsum_ref[...] = recv_sum
    put = functools.partial(put_block, me_ref, block_ref, keep_ref, sent_ref)
    put(0, x_ref[...], gpe_ref[...])
    put(1, sx_ref[...], gpe_ref[...])
    put(2, node_ref[...], recv_sum)
    put(3, act_ref[...], goe_ref[...])


def edge_kernel(plan, *refs):
    near, far, gpe_count = plan
    (edge_ref, cotan_ref, w1_ref, wn_ref, live_ref, normed_ref, new_far_ref, ncot_ref, gpn_ref, rsum_ref) = refs[:10]
    gpe_refs = refs[10 : 10 + gpe_count]
    new_ref, gedge_ref, base_ref, gpe_ref = refs[10 + gpe_count :]
    width = w1_ref.shape[1]
    cap = edge_ref.shape[1]
    stack_into(gpe_ref, gpe_refs)
    base_ref[...] = (
        ncot_ref[...].astype(f32)
        + dot_rt(gpn_ref[...], wn_ref[:width, :])
        + dot_rt(rsum_ref[...], w1_ref[2 * width :, :])
    )
    for i, k in enumerate(near + far):
        rows = slice(i * cap, (i + 1) * cap)
        grad = cotan_ref[k].astype(f32) + dot_rt(gpe_ref[rows, :], w1_ref[:width, :])
        gedge_ref[k] = grad.astype(bf16)
        if i < len(near):
            message = live_ref[rows, :1] * normed_ref[rows, :]
            new_ref[k] = (edge_ref[k].astype(f32) + message).astype(bf16)
        else:
            first = (i - len(near)) * cap
            new_ref[k] = new_far_ref[first : first + cap, :]


def final_kernel(plan, *refs):
    base_ref, w1_ref = refs[:2]
    id_refs = refs[2 : 2 + len(plan)]
    row_refs = refs[2 + len(plan) : 2 + 2 * len(plan)]
    out_ref, hot_ref, rows_ref = refs[2 + 2 * len(plan) :]
    nodes, width = base_ref.shape
    cap = id_refs[0].shape[2]
    at = 0
    for id_ref, sets in zip(id_refs, plan):
        for k in sets:
            hot_ref[:, at : at + cap] = sum_table(id_ref[k], nodes)
            at += cap
    stack_into(rows_ref, row_refs)
    send_sum = dot(hot_ref[...], rows_ref[...]).astype(bf16)
    grad = base_ref[...] + dot_rt(send_sum, w1_ref[width : 2 * width, :])
    out_ref[...] = grad.astype(bf16)


def place(me_ref, stride, members):
    return lax.rem(lax.div(me_ref[0], stride), members)


def add_kernel(plan, *refs):
    came, stride, members = plan
    me_ref, keep_ref = refs[:2]
    arr_refs, out_refs = refs[2 : 2 + came], refs[2 + came :]
    size = keep_ref.shape[1] // members
    here = place(me_ref, stride, members)
    for j, out_ref in enumerate(out_refs):
        at = lax.rem(here + j, members) * size
        rows = pl.ds(pl.multiple_of(at, size), size)
        piece = keep_ref[:, rows, :]
        for arr_ref in arr_refs:
            piece += arr_ref[:, rows, :].astype(f32)
        out_ref[...] = piece.astype(out_ref.dtype)


def gather_kernel(plan, *refs):
    stride, members = plan
    me_ref, piece_refs, out_ref = refs[0], refs[1:-1], refs[-1]
    size = piece_refs[0].shape[1]
    here = place(me_ref, stride, members)
    for j, piece_ref in enumerate(piece_refs):
        at = lax.rem(here + members - j, members) * size
        out_ref[:, pl.ds(pl.multiple_of(at, size), size), :] = piece_ref[...]


def join_kernel(plan, *refs):
    members, blocks = plan
    me_ref = refs[0]
    piece_refs, other_refs = refs[1 : 1 + members], refs[1 + members : 1 + 2 * members]
    out_refs = refs[1 + 2 * members :]
    size = piece_refs[0].shape[1]
    core = lax.rem(me_ref[0], 2)
    here = place(me_ref, 2, members)
    for index, (which, block) in enumerate(blocks):
        first = 2 * block * members * size
        for side, side_refs in ((core, piece_refs), (1 - core, other_refs)):
            for j, piece_ref in enumerate(side_refs):
                at = first + (side * members + lax.rem(here + members - j, members)) * size
                rows = pl.ds(pl.multiple_of(at, size), size)
                out_refs[which][rows, :] = piece_ref[index]


def in_group(block, axis, stride, members, step):
    route = []
    for i in range(lax.axis_size(axis)):
        at = (i // stride) % members
        route.append((i, i + ((at + step) % members - at) * stride))
    return lax.ppermute(block, axis, route)


def split_of(bands):
    chips = bands // 2
    first = 1
    while first * first * 4 <= chips:
        first *= 2
    return first, chips // first


def reduce_over_chips(me, keep, sent):
    bands = lax.axis_size("band")
    first, second = split_of(bands)
    count, rows, width = keep.shape
    arrived = [in_group(sent, "band", 1, 2, 1)]
    for stride, members in ((2, first), (2 * first, second)):
        rows //= members
        outs = call(
            functools.partial(add_kernel, (len(arrived), stride, members)),
            [((count, rows, width), f32)] + [((count, rows, width), bf16)] * (members - 1),
            [],
            me,
            keep,
            *arrived,
            smem=(0,),
        )
        keep = outs[0]
        arrived = [
            in_group(out, "band", stride, members, j + 1) for j, out in enumerate(outs[1:])
        ]
    (piece,) = call(
        functools.partial(add_kernel, (len(arrived), 1, 1)),
        [((count, rows, width), bf16)],
        [],
        me,
        keep,
        *arrived,
        smem=(0,),
    )
    return piece


def gather_over_chips(me, piece, blocks, shapes):
    bands = lax.axis_size("band")
    first, second = split_of(bands)
    count, rows, width = piece.shape
    pieces = [piece] + [
        in_group(piece, "band", 2 * first, second, j) for j in range(1, second)
    ]
    (mine,) = call(
        functools.partial(gather_kernel, (2 * first, second)),
        [((count, rows * second, width), bf16)],
        [],
        me,
        *pieces,
        smem=(0,),
    )
    pieces = [mine] + [in_group(mine, "band", 2, first, j) for j in range(1, first)]
    others = [in_group(one, "band", 1, 2, 1) for one in pieces]
    return call(
        functools.partial(join_kernel, (first, blocks)),
        [(shape, bf16) for shape in shapes],
        [],
        me,
        *pieces,
        *others,
        smem=(0,),
    )


def reduce_whole(keep, sent):
    bands = lax.axis_size("band")
    chips = [[i for i in range(bands) if i % 2 == c] for c in range(2)]
    total = keep + in_group(sent, "band", 1, 2, 1).astype(f32)
    total = lax.psum(total.astype(bf16), "band", axis_index_groups=chips)
    other = in_group(total, "band", 1, 2, 1)
    core = lax.axis_index("band") % 2
    low, high = jnp.where(core == 0, total, other), jnp.where(core == 0, other, total)
    return jnp.concatenate([low, high], axis=1)


def local(
    node_latent,
    edge_latent,
    recv_slot,
    send_slot,
    edge_count,
    edge_first,
    edge_second,
    node_first,
    node_second,
    node_cotan,
    edge_cotan,
):
    bands = lax.axis_size("band")
    nodes, width = node_latent.shape
    sets, cap = edge_latent.shape[1:3]
    edges, cotan = edge_latent[0], edge_cotan[0]
    recv_ids, send_ids = recv_slot.reshape(sets, 1, cap), send_slot.reshape(sets, 1, cap)
    me = lax.axis_index("band").astype(jnp.int32).reshape(1)

    def step_of(k):
        return band_offsets[k] % bands

    def reach(k):
        return min(step_of(k), bands - step_of(k))

    ordered = sorted(range(sets), key=lambda k: (reach(k), step_of(k)))
    near, far = tuple(ordered[:near_sets]), tuple(ordered[near_sets:])
    local_count = sum(step_of(k) == 0 for k in near)
    near_steps = [step_of(k) for k in near[local_count:]]
    far_steps = list(dict.fromkeys(step_of(k) for k in far))
    steps = near_steps + far_steps
    near_plan = tuple((k,) for k in near[local_count:])
    far_plan = tuple(tuple(k for k in far if step_of(k) == d) for d in far_steps)
    far = sum(far_plan, ())

    ids = [passed_along(send_ids, "band", -d) for d in steps]
    picked = call(
        functools.partial(pick_kernel, near_plan + far_plan),
        [((len(piece) * cap, width), bf16) for piece in near_plan + far_plan],
        [],
        node_latent,
        *ids,
    )
    sx = [passed_along(block, "band", d) for block, d in zip(picked, steps)]
    sx_near, sx_far = sx[: len(near_plan)], sx[len(near_plan) :]

    local_rows, near_rows, far_rows = local_count * cap, len(near) * cap, len(far) * cap
    sx_local, act_near, pre, normed, inverse, live, part_sum = call(
        functools.partial(near_kernel, (near, local_count)),
        [
            ((local_rows, width), bf16),
            ((near_rows, width), bf16),
            ((near_rows, width), f32),
            ((near_rows, width), f32),
            ((near_rows, 128), f32),
            ((near_rows, 128), f32),
            ((nodes, width), f32),
        ],
        [
            ((near_rows, 3 * width), bf16),
            ((near_rows, width), bf16),
            ((nodes, near_rows), bf16),
        ],
        edges,
        recv_ids,
        send_ids,
        edge_count,
        edge_first,
        edge_second,
        node_latent,
        *sx_near,
        smem=(3,),
    )

    outs = call(
        functools.partial(far_kernel, (far, far_plan)),
        [((len(piece) * cap, width), bf16) for piece in far_plan]
        + [((far_rows, width), bf16)] * 3
        + [((nodes, width), bf16)] * 6,
        [
            ((far_rows, 3 * width), bf16),
            ((far_rows, 128), f32),
            ((far_rows, width), f32),
            ((far_rows, width), f32),
            ((far_rows, 128), f32),
            ((far_rows, width), bf16),
            ((nodes, far_rows), bf16),
            ((far_rows, nodes), bf16),
            ((far_rows, width), bf16),
        ],
        edges,
        cotan,
        recv_ids,
        edge_count,
        edge_first,
        edge_second,
        node_latent,
        node_cotan,
        part_sum,
        node_first,
        node_second,
        *sx_far,
        smem=(3,),
    )
    gpe_far, outs = list(outs[: len(far_plan)]), outs[len(far_plan) :]
    act_far, goe_far, new_far, node_new, gathered, gpn, act_node, gon, gg = outs
    back_far = [passed_along(block, "band", -d) for block, d in zip(gpe_far, far_steps)]

    half = (width // 2, width)
    outs = call(
        functools.partial(back_kernel, (near, local_count)),
        [
            ((3, *half), f32),
            ((3, *half), bf16),
            ((near_rows, width), bf16),
            ((local_rows, width), bf16),
        ]
        + [((cap, width), bf16)] * len(near_steps),
        [((near_rows, width), bf16), ((near_rows, nodes), bf16), ((width, width), f32)],
        cotan,
        recv_ids,
        me,
        edge_second,
        live,
        pre,
        normed,
        inverse,
        node_latent,
        gathered,
        gpn,
        act_node,
        gon,
        gg,
        smem=(2,),
    )
    keep_node, sent_node, goe_near, gpe_local = outs[:4]
    gpe_near = list(outs[4:])
    back_near = [passed_along(block, "band", -d) for block, d in zip(gpe_near, near_steps)]

    order = near + far
    gpe = [gpe_local] + gpe_near + gpe_far
    sx_all = [sx_local] + sx_near + sx_far
    total = sets * cap
    keep_edge, sent_edge, recv_sum = call(
        functools.partial(weight_kernel, (order, len(sx_all), len(gpe), 2)),
        [((4, *half), f32), ((4, *half), bf16), ((nodes, width), bf16)],
        [((total, width), bf16)] * 5 + [((nodes, total), bf16), ((width, width), f32)],
        edges,
        recv_ids,
        me,
        node_latent,
        *sx_all,
        *gpe,
        act_near,
        act_far,
        goe_near,
        goe_far,
        smem=(2,),
    )

    first, second = split_of(bands)
    if width // 2 % (16 * first * second) == 0:
        piece_node = reduce_over_chips(me, keep_node, sent_node)
        piece_edge = reduce_over_chips(me, keep_edge, sent_edge)
        grad_n1, grad_n2 = gather_over_chips(
            me, piece_node, ((0, 0), (0, 1), (1, 0)), [(2 * width, width), (width, width)]
        )
        grad_e1, grad_e2 = gather_over_chips(
            me, piece_edge, ((0, 0), (0, 1), (0, 2), (1, 0)), [(3 * width, width), (width, width)]
        )
    else:
        whole = reduce_whole(keep_node, sent_node)
        grad_n1, grad_n2 = whole[:2].reshape(2 * width, width), whole[2]
        whole = reduce_whole(keep_edge, sent_edge)
        grad_e1, grad_e2 = whole[:3].reshape(3 * width, width), whole[3]

    edge_new, grad_edges, base = call(
        functools.partial(edge_kernel, (near, far, len(gpe))),
        [((sets, cap, width), bf16), ((sets, cap, width), bf16), ((nodes, width), f32)],
        [((total, width), bf16)],
        edges,
        cotan,
        edge_first,
        node_first,
        live,
        normed,
        new_far,
        node_cotan,
        gpn,
        recv_sum,
        *gpe,
    )
    (grad_nodes,) = call(
        functools.partial(final_kernel, (near[:local_count],) + near_plan + far_plan),
        [((nodes, width), bf16)],
        [((nodes, total), bf16), ((total, width), bf16)],
        base,
        edge_first,
        send_ids,
        *ids,
        gpe_local,
        *back_near,
        *back_far,
    )
    return (
        node_new,
        edge_new[None],
        grad_nodes,
        grad_edges[None],
        grad_e1,
        grad_e2,
        grad_n1,
        grad_n2,
    )


def solution(mesh):
    return jax.shard_map(
        local,
        mesh=mesh,
        in_specs=(
            P(("groups", "band"), None),
            P(("groups", "band"), None, None, None),
            P(("groups", "band"), None, None),
            P(("groups", "band"), None, None),
            P(("groups", "band"), None),
            P(),
            P(),
            P(),
            P(),
            P(("groups", "band"), None),
            P(("groups", "band"), None, None, None),
        ),
        out_specs=(
            P(("groups", "band"), None),
            P(("groups", "band"), None, None, None),
            P(("groups", "band"), None),
            P(("groups", "band"), None, None, None),
            P("groups", None),
            P("groups", None),
            P("groups", None),
            P("groups", None),
        ),
        check_vma=False,
    )
```

time: 225 us -> 192 us (0.85); the launches traced: 221 us -> 191 us
  waiting for transfers between devices: 126 us -> 66.2 us
  starting transfers between devices: 25.7 us -> 70.8 us
  between operations: 14.2 us -> 0.81 us
  Pallas kernels: 36.3 us -> 42.5 us
  local copies, waits for them, and re-layouts: 17 us -> 10.9 us
    psum x1 -> x0, waiting for transfers between devices: 93.6 us -> none  [local(): total = lax.psum((share[:3], share[3:]), 'band', axis_index_groups=chips)]
    ppermute x2 -> x22, waiting for transfers between devices: 3.99 us -> 39.3 us  [in_group(): return lax.ppermute(block, axis, route)]
    ppermute x2 -> x22, starting transfers between devices: 0.12 us -> 33.6 us  [in_group(): return lax.ppermute(block, axis, route)]
    ppermute x17 -> x21, starting transfers between devices: 25.6 us -> 37.1 us  [passed_along(): return lax.ppermute(block, axis, route)]
    slice x6 -> x0, local copies, waits for them, and re-layouts: 6.26 us -> none  [the longest x2 1.97 us: local(): total = lax.psum((share[:3], share[3:]), 'band', axis_index_groups=chips)]
    pallas_call x6 -> x17, Pallas kernels: 36.3 us -> 42.5 us  [call(): pl.pallas_call(body, out_shape=[jax.ShapeDtypeStruct(shape, kind) for sha...]
    ppermute x17 -> x21, waiting for transfers between devices: 28 us -> 26.9 us  [passed_along(): return lax.ppermute(block, axis, route)]
    unnamed x35 -> x34, local copies, waits for them, and re-layouts: 10.7 us -> 10.9 us
  transfers between devices with their start and end apart: 20 -> 43, of which waited for: 10 -> 20; matrix products, arithmetic and copies ran while one was open for 3% -> 0% of each run, Pallas kernels for 4% -> 9%
where the time goes in v3:
time: 192 us; the launch traced here: 191 us
  starting transfers between devices  70.8 us (37%)
  waiting for transfers between devices  66.2 us (34%)
  Pallas kernels  42.5 us (22%)
  local copies, waits for them, and re-layouts  10.9 us (6%)
    pallas_call x17, Pallas kernels, call(): pl.pallas_call(body, out_shape=[jax.ShapeDtypeStruct(shape, kind) for sha...  42.5 us
    ppermute x22, waiting for transfers between devices, in_group(): return lax.ppermute(block, axis, route)  39.3 us
    ppermute x21, starting transfers between devices, passed_along(): return lax.ppermute(block, axis, route)  37.1 us
    ppermute x22, starting transfers between devices, in_group(): return lax.ppermute(block, axis, route)  33.6 us
    ppermute x21, waiting for transfers between devices, passed_along(): return lax.ppermute(block, axis, route)  26.9 us
    unnamed x34, local copies, waits for them, and re-layouts  10.9 us
  transfers between devices with their start and end apart: 43, of which 20 were waited for; matrix products, arithmetic and copies ran while one was open for 0% of the time, Pallas kernels for 9%

profile of v3, /device:TPU:0, one launch (start us, length us, event | category | flops | bytes accessed | tf_op | source)
XLA Modules:
  0.0 191.2 jit_solution(8776304541468565472)
XLA Ops:
  0.6 5.5 %collective-permute-start = (s32[11,1,128]{2,1,0:T(1,128)}, s32[11,1,128]{2,1,0:T(1,128)S(1)}, u32[]{:S(2)}, u32[]{:S(2)}) collective-permute-start(s32[11,1,128]{2,1,0:T(1,128)} %bitcast.15), channel_id=1, source_target_pairs={{1,0},{2,1},{3,2},{4,3},{5,4},{6,5},{7,6},{8,7},{9,8},{10,9},{11,1... | collective-permute-start | bytes 16904 | tf_op jit(solution)/shard_map/ppermute | solution.py:21
  8.6 1.6 collective-permute-start.5
  10.2 1.9 collective-permute-done.1.refs_2_.refs_4_
  12.1 1.6 collective-permute-done.3.refs_4_.refs_6_
  14.2 2.6 %collective-permute-done.6.refs_7_.refs_9_ = s32[11,1,128]{2,1,0:T(1,128)S(1)} collective-permute-done((s32[11,1,128]{2,1,0:T(1,128)}, s32[11,1,128]{2,1,0:T(1,128)S(1)}, u32[]{:S(2)}, u32[]{:S(2)}) %collective-permute-start.6) | collective-permute-done | bytes 5664 | tf_op jit(solution)/shard_map/ppermute | solution.py:21
  18.5 3.7 %collective-permute-start.10 = (bf16[128,512]{1,0:T(8,128)(2,1)S(1)}, bf16[128,512]{1,0:T(8,128)(2,1)S(1)}, u32[]{:S(2)}, u32[]{:S(2)}) collective-permute-start(bf16[128,512]{1,0:T(8,128)(2,1)S(1)} %get-tuple-element.67), channel_id=1, source_target_pairs={{2,0},{3,1},{4,2},{5,3},{6,4},{7,5},{8,6},{9,7},{10,8},{11,9},{12,... | collective-permute-start | bytes 393224 | tf_op jit(solution)/shard_map/ppermute | solution.py:21
  23.5 3.2 %collective-permute-start.8 = (bf16[128,512]{1,0:T(8,128)(2,1)S(1)}, bf16[128,512]{1,0:T(8,128)(2,1)S(1)}, u32[]{:S(2)}, u32[]{:S(2)}) collective-permute-start(bf16[128,512]{1,0:T(8,128)(2,1)S(1)} %get-tuple-element.65), channel_id=1, source_target_pairs={{1,0},{2,1},{3,2},{4,3},{5,4},{6,5},{7,6},{8,7},{9,8},{10,9},{11,1... | collective-permute-start | bytes 393224 | tf_op jit(solution)/shard_map/ppermute | solution.py:21
  26.7 3.3 %collective-permute-done.7.refs_7_.refs_5_ = bf16[128,512]{1,0:T(8,128)(2,1)S(1)} collective-permute-done((bf16[128,512]{1,0:T(8,128)(2,1)S(1)}, bf16[128,512]{1,0:T(8,128)(2,1)S(1)}, u32[]{:S(2)}, u32[]{:S(2)}) %collective-permute-start.7) | collective-permute-done | bytes 131104 | tf_op jit(solution)/shard_map/ppermute | solution.py:21
  30.6 3.6 %collective-permute-done.8.refs_8_.refs_6_ = bf16[128,512]{1,0:T(8,128)(2,1)S(1)} collective-permute-done((bf16[128,512]{1,0:T(8,128)(2,1)S(1)}, bf16[128,512]{1,0:T(8,128)(2,1)S(1)}, u32[]{:S(2)}, u32[]{:S(2)}) %collective-permute-start.8) | collective-permute-done | bytes 131104 | tf_op jit(solution)/shard_map/ppermute | solution.py:21
  34.2 1.8 collective-permute-done.9.refs_9_.refs_7_
  36.0 1.4 copy-done.1
  41.4 6.9 %shard_map.171 = (bf16[384,512]{1,0:T(8,128)(2,1)S(1)}, bf16[896,512]{1,0:T(8,128)(2,1)S(1)}, f32[896,512]{1,0:T(8,128)}, f32[896,512]{1,0:T(8,128)}, f32[896,12...) custom-call(bf16[11,128,512]{2,1,0:T(8,128)(2,1)S(1)} %bitcast.10, s32[11,1,128]{2,1,0:T(1,128)S(1)} %bitcast.11, ...), custom_call_target="tpu_custom_call" | custom-call | tf_op jit(solution)/shard_map/pallas_call | solution.py:83
  49.2 8.8 %shard_map.172 = (bf16[128,512]{1,0:T(8,128)(2,1)S(1)}, bf16[128,512]{1,0:T(8,128)(2,1)S(1)}, bf16[256,512]{1,0:T(8,128)(2,1)S(1)}, bf16[512,512]{1,0:T(8,128)(2...) custom-call(bf16[11,128,512]{2,1,0:T(8,128)(2,1)} %bitcast.7, ...), custom_call_target="tpu_custom_call" | custom-call | tf_op jit(solution)/shard_map/pallas_call | solution.py:83
  58.0 7.0 %shard_map.173 = (f32[3,256,512]{2,1,0:T(8,128)}, bf16[3,256,512]{2,1,0:T(8,128)(2,1)S(1)}, bf16[896,512]{1,0:T(8,128)(2,1)S(1)}, bf16[384,512]{1,0:T(8,128)(2,1...) custom-call(bf16[11,128,512]{2,1,0:T(8,128)(2,1)} %bitcast.25, ...), custom_call_target="tpu_custom_call" | custom-call | tf_op jit(solution)/shard_map/pallas_call | solution.py:83
  65.9 7.2 %shard_map.174 = (f32[4,256,512]{2,1,0:T(8,128)}, bf16[4,256,512]{2,1,0:T(8,128)(2,1)}, bf16[320,512]{1,0:T(8,128)(2,1)S(1)}) custom-call(bf16[11,128,512]{2,1,0:T(8,128)(2,1)} %bitcast.8, s32[11,1,128]{2,1,0:T(1,128)S(1)} %bitcast.14, s32[1]{0:T(128)} %bitcast.4.refs_2_.refs_0_, bf16[320,512]{1,0:T(8,128)(2,1)S(1)} %copy-done.3, ...), custom_call_target="tpu_custom_call" | custom-call | tf_op jit(solution)/shard_map/pallas_call | solution.py:83
  73.6 3.5 %collective-permute-done.21.refs_2_ = bf16[4,256,512]{2,1,0:T(8,128)(2,1)S(1)} collective-permute-done((bf16[4,256,512]{2,1,0:T(8,128)(2,1)}, bf16[4,256,512]{2,1,0:T(8,128)(2,1)S(1)}, u32[]{:S(2)}, u32[]{:S(2)}) %collective-permute-start.21) | collective-permute-done | bytes 1048608 | tf_op jit(solution)/shard_map/ppermute | solution.py:440
  77.1 1.6 copy-done.7
  81.2 12.5 %collective-permute-done.22.refs_2_ = bf16[4,128,512]{2,1,0:T(8,128)(2,1)S(1)} collective-permute-done((bf16[4,128,512]{2,1,0:T(8,128)(2,1)S(1)}, bf16[4,128,512]{2,1,0:T(8,128)(2,1)S(1)}, u32[]{:S(2)}, u32[]{:S(2)}) %collective-permute-start.22) | collective-permute-done | bytes 524320 | tf_op jit(solution)/shard_map/ppermute | solution.py:440
  93.8 6.2 %collective-permute-start.23 = (bf16[4,32,512]{2,1,0:T(8,128)(2,1)S(1)}, bf16[4,32,512]{2,1,0:T(8,128)(2,1)S(1)}, u32[]{:S(2)}, u32[]{:S(2)}) collective-permute-start(bf16[4,32,512]{2,1,0:T(8,128)(2,1)S(1)} %get-tuple-element.105), channel_id=1, source_target_pairs={{0,4},{1,5},{2,6},{3,7},{4,8},{5,9},{6,10},{7,11},{8,12},{9,13},{1... | collective-permute-start | bytes 393224 | tf_op jit(solution)/shard_map/ppermute | solution.py:440
  100.0 1.3 collective-permute-start.24
  101.3 2.8 %collective-permute-start.25 = (bf16[4,32,512]{2,1,0:T(8,128)(2,1)S(1)}, bf16[4,32,512]{2,1,0:T(8,128)(2,1)S(1)}, u32[]{:S(2)}, u32[]{:S(2)}) collective-permute-start(bf16[4,32,512]{2,1,0:T(8,128)(2,1)S(1)} %get-tuple-element.107), channel_id=1, source_target_pairs={{0,12},{1,13},{2,14},{3,15},{4,0},{5,1},{6,2},{7,3},{8,4},{9,5},{1... | collective-permute-start | bytes 393224 | tf_op jit(solution)/shard_map/ppermute | solution.py:440
  104.1 5.1 %collective-permute-done.24.refs_3_ = bf16[4,32,512]{2,1,0:T(8,128)(2,1)S(1)} collective-permute-done((bf16[4,32,512]{2,1,0:T(8,128)(2,1)S(1)}, bf16[4,32,512]{2,1,0:T(8,128)(2,1)S(1)}, u32[]{:S(2)}, u32[]{:S(2)}) %collective-permute-start.24) | collective-permute-done | bytes 131104 | tf_op jit(solution)/shard_map/ppermute | solution.py:440
  109.3 3.6 %collective-permute-start.26 = (bf16[4,32,512]{2,1,0:T(8,128)(2,1)S(1)}, bf16[4,32,512]{2,1,0:T(8,128)(2,1)S(1)}, u32[]{:S(2)}, u32[]{:S(2)}) collective-permute-start(bf16[4,32,512]{2,1,0:T(8,128)(2,1)S(1)} %shard_map.179.refs_1_), channel_id=1, source_target_pairs={{0,4},{1,5},{2,6},{3,7},{4,8},{5,9},{6,10},{7,11},{8,12},{9,13},{1... | collective-permute-start | bytes 393224 | tf_op jit(solution)/shard_map/ppermute | solution.py:440
  112.9 3.4 %collective-permute-start.27 = (bf16[4,32,512]{2,1,0:T(8,128)(2,1)S(1)}, bf16[4,32,512]{2,1,0:T(8,128)(2,1)S(1)}, u32[]{:S(2)}, u32[]{:S(2)}) collective-permute-start(bf16[4,32,512]{2,1,0:T(8,128)(2,1)S(1)} %shard_map.179.refs_1_), channel_id=1, source_target_pairs={{0,8},{1,9},{2,10},{3,11},{4,12},{5,13},{6,14},{7,15},{8,0},{9,1},... | collective-permute-start | bytes 393224 | tf_op jit(solution)/shard_map/ppermute | solution.py:440
  116.2 3.5 %collective-permute-done.26.refs_2_ = bf16[4,32,512]{2,1,0:T(8,128)(2,1)S(1)} collective-permute-done((bf16[4,32,512]{2,1,0:T(8,128)(2,1)S(1)}, bf16[4,32,512]{2,1,0:T(8,128)(2,1)S(1)}, u32[]{:S(2)}, u32[]{:S(2)}) %collective-permute-start.26) | collective-permute-done | bytes 131104 | tf_op jit(solution)/shard_map/ppermute | solution.py:440
  119.7 3.5 %collective-permute-done.27.refs_3_ = bf16[4,32,512]{2,1,0:T(8,128)(2,1)S(1)} collective-permute-done((bf16[4,32,512]{2,1,0:T(8,128)(2,1)S(1)}, bf16[4,32,512]{2,1,0:T(8,128)(2,1)S(1)}, u32[]{:S(2)}, u32[]{:S(2)}) %collective-permute-start.27) | collective-permute-done | bytes 131104 | tf_op jit(solution)/shard_map/ppermute | solution.py:440
  123.5 2.6 %collective-permute-start.34 = (bf16[3,32,512]{2,1,0:T(8,128)(2,1)S(1)}, bf16[3,32,512]{2,1,0:T(8,128)(2,1)S(1)}, u32[]{:S(2)}, u32[]{:S(2)}) collective-permute-start(bf16[3,32,512]{2,1,0:T(8,128)(2,1)S(1)} %get-tuple-element.115), channel_id=1, source_target_pairs={{0,4},{1,5},{2,6},{3,7},{4,8},{5,9},{6,10},{7,11},{8,12},{9,13},{1... | collective-permute-start | bytes 294920 | tf_op jit(solution)/shard_map/ppermute | solution.py:440
  126.1 1.5 collective-permute-start.35
  128.6 2.4 %collective-permute-done.34.refs_2_ = bf16[3,32,512]{2,1,0:T(8,128)(2,1)S(1)} collective-permute-done((bf16[3,32,512]{2,1,0:T(8,128)(2,1)S(1)}, bf16[3,32,512]{2,1,0:T(8,128)(2,1)S(1)}, u32[]{:S(2)}, u32[]{:S(2)}) %collective-permute-start.34) | collective-permute-done | bytes 98336 | tf_op jit(solution)/shard_map/ppermute | solution.py:440
  131.0 3.0 %collective-permute-done.35.refs_3_ = bf16[3,32,512]{2,1,0:T(8,128)(2,1)S(1)} collective-permute-done((bf16[3,32,512]{2,1,0:T(8,128)(2,1)S(1)}, bf16[3,32,512]{2,1,0:T(8,128)(2,1)S(1)}, u32[]{:S(2)}, u32[]{:S(2)}) %collective-permute-start.35) | collective-permute-done | bytes 98336 | tf_op jit(solution)/shard_map/ppermute | solution.py:440
  134.0 2.5 %collective-permute-start.37 = (bf16[3,32,512]{2,1,0:T(8,128)(2,1)S(1)}, bf16[3,32,512]{2,1,0:T(8,128)(2,1)S(1)}, u32[]{:S(2)}, u32[]{:S(2)}) collective-permute-start(bf16[3,32,512]{2,1,0:T(8,128)(2,1)S(1)} %shard_map.184.refs_1_), channel_id=1, source_target_pairs={{0,4},{1,5},{2,6},{3,7},{4,8},{5,9},{6,10},{7,11},{8,12},{9,13},{1... | collective-permute-start | bytes 294920 | tf_op jit(solution)/shard_map/ppermute | solution.py:440
  136.5 1.3 collective-permute-start.38
  138.9 2.7 %collective-permute-done.37.refs_2_ = bf16[3,32,512]{2,1,0:T(8,128)(2,1)S(1)} collective-permute-done((bf16[3,32,512]{2,1,0:T(8,128)(2,1)S(1)}, bf16[3,32,512]{2,1,0:T(8,128)(2,1)S(1)}, u32[]{:S(2)}, u32[]{:S(2)}) %collective-permute-start.37) | collective-permute-done | bytes 98336 | tf_op jit(solution)/shard_map/ppermute | solution.py:440
  141.6 3.2 %collective-permute-done.38.refs_3_ = bf16[3,32,512]{2,1,0:T(8,128)(2,1)S(1)} collective-permute-done((bf16[3,32,512]{2,1,0:T(8,128)(2,1)S(1)}, bf16[3,32,512]{2,1,0:T(8,128)(2,1)S(1)}, u32[]{:S(2)}, u32[]{:S(2)}) %collective-permute-start.38) | collective-permute-done | bytes 98336 | tf_op jit(solution)/shard_map/ppermute | solution.py:440
  144.8 1.6 collective-permute-start.40
  146.4 1.9 collective-permute-start.14
  148.3 1.8 collective-permute-start.16
  150.8 8.8 %collective-permute-start.17 = (bf16[128,512]{1,0:T(8,128)(2,1)S(1)}, bf16[128,512]{1,0:T(8,128)(2,1)S(1)}, u32[]{:S(2)}, u32[]{:S(2)}) collective-permute-start(bf16[128,512]{1,0:T(8,128)(2,1)S(1)} %get-tuple-element.88.refs_16_.refs_14_), channel_id=1, source_target_pairs={{14,0},{15,1},{0,2},{1,3},{2,4},{3,5},{4,6},{5,7},{6,8},{7,9},{8,1... | collective-permute-start | bytes 393224 | tf_op jit(solution)/shard_map/ppermute | solution.py:21
  159.6 2.7 %collective-permute-start.18 = (bf16[128,512]{1,0:T(8,128)(2,1)S(1)}, bf16[128,512]{1,0:T(8,128)(2,1)S(1)}, u32[]{:S(2)}, u32[]{:S(2)}) collective-permute-start(bf16[128,512]{1,0:T(8,128)(2,1)S(1)} %get-tuple-element.89.refs_17_.refs_15_), channel_id=1, source_target_pairs={{4,0},{5,1},{6,2},{7,3},{8,4},{9,5},{10,6},{11,7},{12,8},{13,9},{1... | collective-permute-start | bytes 393224 | tf_op jit(solution)/shard_map/ppermute | solution.py:21
  162.8 1.9 collective-permute-done.17.refs_14_
  164.7 1.4 collective-permute-start.19
  166.0 2.6 %collective-permute-start.41 = (bf16[3,128,512]{2,1,0:T(8,128)(2,1)S(1)}, bf16[3,128,512]{2,1,0:T(8,128)(2,1)S(1)}, u32[]{:S(2)}, u32[]{:S(2)}) collective-permute-start(bf16[3,128,512]{2,1,0:T(8,128)(2,1)S(1)} %shard_map.185.refs_1_), channel_id=1, source_target_pairs={{0,1},{1,0},{2,3},{3,2},{4,5},{5,4},{6,7},{7,6},{8,9},{9,8},{10,11... | collective-permute-start | bytes 1179656 | tf_op jit(solution)/shard_map/ppermute | solution.py:440
  168.7 3.3 %collective-permute-done.19.refs_16_ = bf16[128,512]{1,0:T(8,128)(2,1)S(1)} collective-permute-done((bf16[128,512]{1,0:T(8,128)(2,1)S(1)}, bf16[128,512]{1,0:T(8,128)(2,1)S(1)}, u32[]{:S(2)}, u32[]{:S(2)}) %collective-permute-start.19) | collective-permute-done | bytes 131104 | tf_op jit(solution)/shard_map/ppermute | solution.py:21
  172.0 2.3 %collective-permute-start.20 = (bf16[256,512]{1,0:T(8,128)(2,1)S(1)}, bf16[256,512]{1,0:T(8,128)(2,1)S(1)}, u32[]{:S(2)}, u32[]{:S(2)}) collective-permute-start(bf16[256,512]{1,0:T(8,128)(2,1)S(1)} %get-tuple-element.91.refs_19_.refs_17_), channel_id=1, source_target_pairs={{8,0},{9,1},{10,2},{11,3},{12,4},{13,5},{14,6},{15,7},{0,8},{1,9},... | collective-permute-start | bytes 786440 | tf_op jit(solution)/shard_map/ppermute | solution.py:21
  174.3 6.9 %shard_map.175 = (bf16[11,128,512]{2,1,0:T(8,128)(2,1)}, bf16[11,128,512]{2,1,0:T(8,128)(2,1)}, f32[320,512]{1,0:T(8,128)S(1)}) custom-call(bf16[11,128,512]{2,1,0:T(8,128)(2,1)} %bitcast.9, bf16[11,128,512]{2,1,0:T(8,128)(2,1)} %bitcast.26, bf16[1536,512]{1,0:T(8,128)(2,1)} %refs_1_.1, bf16[1024,512]{1,0:T(8,128)(2,1)S(1)} %copy-done.6, ...), custom_call_target="tpu_custom_call" | custom-call | tf_op jit(solution)/shard_map/pallas_call | solution.py:83
  181.1 5.7 %collective-permute-done.20.refs_17_ = bf16[256,512]{1,0:T(8,128)(2,1)S(1)} collective-permute-done((bf16[256,512]{1,0:T(8,128)(2,1)S(1)}, bf16[256,512]{1,0:T(8,128)(2,1)S(1)}, u32[]{:S(2)}, u32[]{:S(2)}) %collective-permute-start.20) | collective-permute-done | bytes 262176 | tf_op jit(solution)/shard_map/ppermute | solution.py:21
  186.8 1.6 shard_map.176
  189.8 1.5 shard_map.181
  (89 shorter events, 20.5 us)
Async XLA Ops:
  0.6 8.0 %collective-permute-start = (s32[11,1,128]{2,1,0:T(1,128)}, s32[11,1,128]{2,1,0:T(1,128)S(1)}, u32[]{:S(2)}, u32[]{:S(2)}) collective-permute-start(s32[11,1,128]{2,1,0:T(1,128)} %bitcast.15), channel_id=1, source_target_pairs={{1,0},{2,1},{3,2},{4,3},{5,4},{6,5},{7,6},{8,7},{9,8},{10,9},{11,1... | collective-permute-start | bytes 16904 | tf_op jit(solution)/shard_map/ppermute | solution.py:21
  6.1 6.0 %collective-permute-start.1 = (s32[11,1,128]{2,1,0:T(1,128)}, s32[11,1,128]{2,1,0:T(1,128)S(1)}, u32[]{:S(2)}, u32[]{:S(2)}) collective-permute-start(s32[11,1,128]{2,1,0:T(1,128)} %bitcast.16), channel_id=1, source_target_pairs={{15,0},{0,1},{1,2},{2,3},{3,4},{4,5},{5,6},{6,7},{7,8},{8,9},{9,10... | collective-permute-start | bytes 16904 | tf_op jit(solution)/shard_map/ppermute | solution.py:21
  6.1 6.0 %collective-permute-start.2 = (s32[11,1,128]{2,1,0:T(1,128)}, s32[11,1,128]{2,1,0:T(1,128)S(1)}, u32[]{:S(2)}, u32[]{:S(2)}) collective-permute-start(s32[11,1,128]{2,1,0:T(1,128)} %bitcast.17), channel_id=1, source_target_pairs={{2,0},{3,1},{4,2},{5,3},{6,4},{7,5},{8,6},{9,7},{10,8},{11,9},{12,... | collective-permute-start | bytes 16904 | tf_op jit(solution)/shard_map/ppermute | solution.py:21
  7.2 6.5 %collective-permute-start.3 = (s32[11,1,128]{2,1,0:T(1,128)}, s32[11,1,128]{2,1,0:T(1,128)S(1)}, u32[]{:S(2)}, u32[]{:S(2)}) collective-permute-start(s32[11,1,128]{2,1,0:T(1,128)} %bitcast.18), channel_id=1, source_target_pairs={{14,0},{15,1},{0,2},{1,3},{2,4},{3,5},{4,6},{5,7},{6,8},{7,9},{8,1... | collective-permute-start | bytes 16904 | tf_op jit(solution)/shard_map/ppermute | solution.py:21
  8.2 5.6 %collective-permute-start.4 = (s32[11,1,128]{2,1,0:T(1,128)}, s32[11,1,128]{2,1,0:T(1,128)S(1)}, u32[]{:S(2)}, u32[]{:S(2)}) collective-permute-start(s32[11,1,128]{2,1,0:T(1,128)} %bitcast.19), channel_id=1, source_target_pairs={{4,0},{5,1},{6,2},{7,3},{8,4},{9,5},{10,6},{11,7},{12,8},{13,9},{1... | collective-permute-start | bytes 16904 | tf_op jit(solution)/shard_map/ppermute | solution.py:21
  8.6 5.6 %collective-permute-start.5 = (s32[11,1,128]{2,1,0:T(1,128)}, s32[11,1,128]{2,1,0:T(1,128)S(1)}, u32[]{:S(2)}, u32[]{:S(2)}) collective-permute-start(s32[11,1,128]{2,1,0:T(1,128)} %bitcast.20), channel_id=1, source_target_pairs={{12,0},{13,1},{14,2},{15,3},{0,4},{1,5},{2,6},{3,7},{4,8},{5,9},{6... | collective-permute-start | bytes 16904 | tf_op jit(solution)/shard_map/ppermute | solution.py:21
  12.1 4.7 %collective-permute-start.6 = (s32[11,1,128]{2,1,0:T(1,128)}, s32[11,1,128]{2,1,0:T(1,128)S(1)}, u32[]{:S(2)}, u32[]{:S(2)}) collective-permute-start(s32[11,1,128]{2,1,0:T(1,128)} %bitcast.21), channel_id=1, source_target_pairs={{8,0},{9,1},{10,2},{11,3},{12,4},{13,5},{14,6},{15,7},{0,8},{1,9},... | collective-permute-start | bytes 16904 | tf_op jit(solution)/shard_map/ppermute | solution.py:21
  18.5 8.2 %collective-permute-start.10 = (bf16[128,512]{1,0:T(8,128)(2,1)S(1)}, bf16[128,512]{1,0:T(8,128)(2,1)S(1)}, u32[]{:S(2)}, u32[]{:S(2)}) collective-permute-start(bf16[128,512]{1,0:T(8,128)(2,1)S(1)} %get-tuple-element.67), channel_id=1, source_target_pairs={{2,0},{3,1},{4,2},{5,3},{6,4},{7,5},{8,6},{9,7},{10,8},{11,9},{12,... | collective-permute-start | bytes 393224 | tf_op jit(solution)/shard_map/ppermute | solution.py:21
  22.3 7.8 %collective-permute-start.7 = (bf16[128,512]{1,0:T(8,128)(2,1)S(1)}, bf16[128,512]{1,0:T(8,128)(2,1)S(1)}, u32[]{:S(2)}, u32[]{:S(2)}) collective-permute-start(bf16[128,512]{1,0:T(8,128)(2,1)S(1)} %get-tuple-element.64), channel_id=1, source_target_pairs={{15,0},{0,1},{1,2},{2,3},{3,4},{4,5},{5,6},{6,7},{7,8},{8,9},{9,10... | collective-permute-start | bytes 393224 | tf_op jit(solution)/shard_map/ppermute | solution.py:21
  23.5 25.7 %collective-permute-start.13 = (bf16[256,512]{1,0:T(8,128)(2,1)S(1)}, bf16[256,512]{1,0:T(8,128)(2,1)S(1)}, u32[]{:S(2)}, u32[]{:S(2)}) collective-permute-start(bf16[256,512]{1,0:T(8,128)(2,1)S(1)} %get-tuple-element.71), channel_id=1, source_target_pairs={{8,0},{9,1},{10,2},{11,3},{12,4},{13,5},{14,6},{15,7},{0,8},{1,9},... | collective-permute-start | bytes 786440 | tf_op jit(solution)/shard_map/ppermute | solution.py:21
  23.5 10.7 %collective-permute-start.8 = (bf16[128,512]{1,0:T(8,128)(2,1)S(1)}, bf16[128,512]{1,0:T(8,128)(2,1)S(1)}, u32[]{:S(2)}, u32[]{:S(2)}) collective-permute-start(bf16[128,512]{1,0:T(8,128)(2,1)S(1)} %get-tuple-element.65), channel_id=1, source_target_pairs={{1,0},{2,1},{3,2},{4,3},{5,4},{6,5},{7,6},{8,7},{9,8},{10,9},{11,1... | collective-permute-start | bytes 393224 | tf_op jit(solution)/shard_map/ppermute | solution.py:21
  26.7 9.3 %collective-permute-start.9 = (bf16[128,512]{1,0:T(8,128)(2,1)S(1)}, bf16[128,512]{1,0:T(8,128)(2,1)S(1)}, u32[]{:S(2)}, u32[]{:S(2)}) collective-permute-start(bf16[128,512]{1,0:T(8,128)(2,1)S(1)} %get-tuple-element.66), channel_id=1, source_target_pairs={{14,0},{15,1},{0,2},{1,3},{2,4},{3,5},{4,6},{5,7},{6,8},{7,9},{8,1... | collective-permute-start | bytes 393224 | tf_op jit(solution)/shard_map/ppermute | solution.py:21
  26.7 22.4 %collective-permute-start.11 = (bf16[128,512]{1,0:T(8,128)(2,1)S(1)}, bf16[128,512]{1,0:T(8,128)(2,1)S(1)}, u32[]{:S(2)}, u32[]{:S(2)}) collective-permute-start(bf16[128,512]{1,0:T(8,128)(2,1)S(1)} %get-tuple-element.69), channel_id=1, source_target_pairs={{12,0},{13,1},{14,2},{15,3},{0,4},{1,5},{2,6},{3,7},{4,8},{5,9},{6... | collective-permute-start | bytes 393224 | tf_op jit(solution)/shard_map/ppermute | solution.py:21
  30.0 19.1 %collective-permute-start.12 = (bf16[128,512]{1,0:T(8,128)(2,1)S(1)}, bf16[128,512]{1,0:T(8,128)(2,1)S(1)}, u32[]{:S(2)}, u32[]{:S(2)}) collective-permute-start(bf16[128,512]{1,0:T(8,128)(2,1)S(1)} %get-tuple-element.70), channel_id=1, source_target_pairs={{4,0},{5,1},{6,2},{7,3},{8,4},{9,5},{10,6},{11,7},{12,8},{13,9},{1... | collective-permute-start | bytes 393224 | tf_op jit(solution)/shard_map/ppermute | solution.py:21
  41.4 7.7 %copy-start.9 = (bf16[320,512]{1,0:T(8,128)(2,1)S(1)}, bf16[320,512]{1,0:T(8,128)(2,1)}, u32[]{:S(2)}) copy-start(bf16[320,512]{1,0:T(8,128)(2,1)} %refs_7_.3) | copy-start | bytes 983044
  41.4 7.7 %copy-start.12 = (bf16[512,512]{1,0:T(8,128)(2,1)S(1)}, bf16[512,512]{1,0:T(8,128)(2,1)}, u32[]{:S(2)}) copy-start(bf16[512,512]{1,0:T(8,128)(2,1)} %refs_10_.1) | copy-start | bytes 1572868
  73.1 4.0 %collective-permute-start.21 = (bf16[4,256,512]{2,1,0:T(8,128)(2,1)}, bf16[4,256,512]{2,1,0:T(8,128)(2,1)S(1)}, u32[]{:S(2)}, u32[]{:S(2)}) collective-permute-start(bf16[4,256,512]{2,1,0:T(8,128)(2,1)} %get-tuple-element.101), channel_id=1, source_target_pairs={{0,1},{1,0},{2,3},{3,2},{4,5},{5,4},{6,7},{7,6},{8,9},{9,8},{10,11... | collective-permute-start | bytes 3145736 | tf_op jit(solution)/shard_map/ppermute | solution.py:440
  73.1 5.8 %collective-permute-start.32 = (bf16[3,256,512]{2,1,0:T(8,128)(2,1)S(1)}, bf16[3,256,512]{2,1,0:T(8,128)(2,1)S(1)}, u32[]{:S(2)}, u32[]{:S(2)}) collective-permute-start(bf16[3,256,512]{2,1,0:T(8,128)(2,1)S(1)} %get-tuple-element.111), channel_id=1, source_target_pairs={{0,1},{1,0},{2,3},{3,2},{4,5},{5,4},{6,7},{7,6},{8,9},{9,8},{10,11... | collective-permute-start | bytes 2359304 | tf_op jit(solution)/shard_map/ppermute | solution.py:440
  78.8 14.8 %collective-permute-start.22 = (bf16[4,128,512]{2,1,0:T(8,128)(2,1)S(1)}, bf16[4,128,512]{2,1,0:T(8,128)(2,1)S(1)}, u32[]{:S(2)}, u32[]{:S(2)}) collective-permute-start(bf16[4,128,512]{2,1,0:T(8,128)(2,1)S(1)} %get-tuple-element.103), channel_id=1, source_target_pairs={{0,2},{1,3},{2,0},{3,1},{4,6},{5,7},{6,4},{7,5},{8,10},{9,11},{10,... | collective-permute-start | bytes 1572872 | tf_op jit(solution)/shard_map/ppermute | solution.py:440
  80.2 43.2 %collective-permute-start.33 = (bf16[3,128,512]{2,1,0:T(8,128)(2,1)S(1)}, bf16[3,128,512]{2,1,0:T(8,128)(2,1)S(1)}, u32[]{:S(2)}, u32[]{:S(2)}) collective-permute-start(bf16[3,128,512]{2,1,0:T(8,128)(2,1)S(1)} %get-tuple-element.113), channel_id=1, source_target_pairs={{0,2},{1,3},{2,0},{3,1},{4,6},{5,7},{6,4},{7,5},{8,10},{9,11},{10,... | collective-permute-start | bytes 1179656 | tf_op jit(solution)/shard_map/ppermute | solution.py:440
  93.8 10.4 %collective-permute-start.23 = (bf16[4,32,512]{2,1,0:T(8,128)(2,1)S(1)}, bf16[4,32,512]{2,1,0:T(8,128)(2,1)S(1)}, u32[]{:S(2)}, u32[]{:S(2)}) collective-permute-start(bf16[4,32,512]{2,1,0:T(8,128)(2,1)S(1)} %get-tuple-element.105), channel_id=1, source_target_pairs={{0,4},{1,5},{2,6},{3,7},{4,8},{5,9},{6,10},{7,11},{8,12},{9,13},{1... | collective-permute-start | bytes 393224 | tf_op jit(solution)/shard_map/ppermute | solution.py:440
  100.0 9.2 %collective-permute-start.24 = (bf16[4,32,512]{2,1,0:T(8,128)(2,1)S(1)}, bf16[4,32,512]{2,1,0:T(8,128)(2,1)S(1)}, u32[]{:S(2)}, u32[]{:S(2)}) collective-permute-start(bf16[4,32,512]{2,1,0:T(8,128)(2,1)S(1)} %get-tuple-element.106), channel_id=1, source_target_pairs={{0,8},{1,9},{2,10},{3,11},{4,12},{5,13},{6,14},{7,15},{8,0},{9,1},... | collective-permute-start | bytes 393224 | tf_op jit(solution)/shard_map/ppermute | solution.py:440
  101.3 7.9 %collective-permute-start.25 = (bf16[4,32,512]{2,1,0:T(8,128)(2,1)S(1)}, bf16[4,32,512]{2,1,0:T(8,128)(2,1)S(1)}, u32[]{:S(2)}, u32[]{:S(2)}) collective-permute-start(bf16[4,32,512]{2,1,0:T(8,128)(2,1)S(1)} %get-tuple-element.107), channel_id=1, source_target_pairs={{0,12},{1,13},{2,14},{3,15},{4,0},{5,1},{6,2},{7,3},{8,4},{9,5},{1... | collective-permute-start | bytes 393224 | tf_op jit(solution)/shard_map/ppermute | solution.py:440
  109.3 65.0 %copy-start.6 = (bf16[1024,512]{1,0:T(8,128)(2,1)S(1)}, bf16[1024,512]{1,0:T(8,128)(2,1)}, u32[]{:S(2)}) copy-start(bf16[1024,512]{1,0:T(8,128)(2,1)} %refs_3_.9) | copy-start | bytes 3145732
  109.3 10.4 %collective-permute-start.26 = (bf16[4,32,512]{2,1,0:T(8,128)(2,1)S(1)}, bf16[4,32,512]{2,1,0:T(8,128)(2,1)S(1)}, u32[]{:S(2)}, u32[]{:S(2)}) collective-permute-start(bf16[4,32,512]{2,1,0:T(8,128)(2,1)S(1)} %shard_map.179.refs_1_), channel_id=1, source_target_pairs={{0,4},{1,5},{2,6},{3,7},{4,8},{5,9},{6,10},{7,11},{8,12},{9,13},{1... | collective-permute-start | bytes 393224 | tf_op jit(solution)/shard_map/ppermute | solution.py:440
  112.9 10.4 %collective-permute-start.27 = (bf16[4,32,512]{2,1,0:T(8,128)(2,1)S(1)}, bf16[4,32,512]{2,1,0:T(8,128)(2,1)S(1)}, u32[]{:S(2)}, u32[]{:S(2)}) collective-permute-start(bf16[4,32,512]{2,1,0:T(8,128)(2,1)S(1)} %shard_map.179.refs_1_), channel_id=1, source_target_pairs={{0,8},{1,9},{2,10},{3,11},{4,12},{5,13},{6,14},{7,15},{8,0},{9,1},... | collective-permute-start | bytes 393224 | tf_op jit(solution)/shard_map/ppermute | solution.py:440
  116.2 7.0 %collective-permute-start.28 = (bf16[4,32,512]{2,1,0:T(8,128)(2,1)S(1)}, bf16[4,32,512]{2,1,0:T(8,128)(2,1)S(1)}, u32[]{:S(2)}, u32[]{:S(2)}) collective-permute-start(bf16[4,32,512]{2,1,0:T(8,128)(2,1)S(1)} %shard_map.179.refs_1_), channel_id=1, source_target_pairs={{0,12},{1,13},{2,14},{3,15},{4,0},{5,1},{6,2},{7,3},{8,4},{9,5},{1... | collective-permute-start | bytes 393224 | tf_op jit(solution)/shard_map/ppermute | solution.py:440
  123.3 39.0 %collective-permute-start.29 = (bf16[4,128,512]{2,1,0:T(8,128)(2,1)S(1)}, bf16[4,128,512]{2,1,0:T(8,128)(2,1)S(1)}, u32[]{:S(2)}, u32[]{:S(2)}) collective-permute-start(bf16[4,128,512]{2,1,0:T(8,128)(2,1)S(1)} %shard_map.180.refs_1_), channel_id=1, source_target_pairs={{0,2},{1,3},{2,0},{3,1},{4,6},{5,7},{6,4},{7,5},{8,10},{9,11},{10,... | collective-permute-start | bytes 1572872 | tf_op jit(solution)/shard_map/ppermute | solution.py:440
  123.5 7.4 %collective-permute-start.34 = (bf16[3,32,512]{2,1,0:T(8,128)(2,1)S(1)}, bf16[3,32,512]{2,1,0:T(8,128)(2,1)S(1)}, u32[]{:S(2)}, u32[]{:S(2)}) collective-permute-start(bf16[3,32,512]{2,1,0:T(8,128)(2,1)S(1)} %get-tuple-element.115), channel_id=1, source_target_pairs={{0,4},{1,5},{2,6},{3,7},{4,8},{5,9},{6,10},{7,11},{8,12},{9,13},{1... | collective-permute-start | bytes 294920 | tf_op jit(solution)/shard_map/ppermute | solution.py:440
  126.1 7.8 %collective-permute-start.35 = (bf16[3,32,512]{2,1,0:T(8,128)(2,1)S(1)}, bf16[3,32,512]{2,1,0:T(8,128)(2,1)S(1)}, u32[]{:S(2)}, u32[]{:S(2)}) collective-permute-start(bf16[3,32,512]{2,1,0:T(8,128)(2,1)S(1)} %get-tuple-element.116), channel_id=1, source_target_pairs={{0,8},{1,9},{2,10},{3,11},{4,12},{5,13},{6,14},{7,15},{8,0},{9,1},... | collective-permute-start | bytes 294920 | tf_op jit(solution)/shard_map/ppermute | solution.py:440
  127.6 6.3 %collective-permute-start.36 = (bf16[3,32,512]{2,1,0:T(8,128)(2,1)S(1)}, bf16[3,32,512]{2,1,0:T(8,128)(2,1)S(1)}, u32[]{:S(2)}, u32[]{:S(2)}) collective-permute-start(bf16[3,32,512]{2,1,0:T(8,128)(2,1)S(1)} %get-tuple-element.117), channel_id=1, source_target_pairs={{0,12},{1,13},{2,14},{3,15},{4,0},{5,1},{6,2},{7,3},{8,4},{9,5},{1... | collective-permute-start | bytes 294920 | tf_op jit(solution)/shard_map/ppermute | solution.py:440
  134.0 7.6 %collective-permute-start.37 = (bf16[3,32,512]{2,1,0:T(8,128)(2,1)S(1)}, bf16[3,32,512]{2,1,0:T(8,128)(2,1)S(1)}, u32[]{:S(2)}, u32[]{:S(2)}) collective-permute-start(bf16[3,32,512]{2,1,0:T(8,128)(2,1)S(1)} %shard_map.184.refs_1_), channel_id=1, source_target_pairs={{0,4},{1,5},{2,6},{3,7},{4,8},{5,9},{6,10},{7,11},{8,12},{9,13},{1... | collective-permute-start | bytes 294920 | tf_op jit(solution)/shard_map/ppermute | solution.py:440
  136.5 8.3 %collective-permute-start.38 = (bf16[3,32,512]{2,1,0:T(8,128)(2,1)S(1)}, bf16[3,32,512]{2,1,0:T(8,128)(2,1)S(1)}, u32[]{:S(2)}, u32[]{:S(2)}) collective-permute-start(bf16[3,32,512]{2,1,0:T(8,128)(2,1)S(1)} %shard_map.184.refs_1_), channel_id=1, source_target_pairs={{0,8},{1,9},{2,10},{3,11},{4,12},{5,13},{6,14},{7,15},{8,0},{9,1},... | collective-permute-start | bytes 294920 | tf_op jit(solution)/shard_map/ppermute | solution.py:440
  137.8 7.0 %collective-permute-start.39 = (bf16[3,32,512]{2,1,0:T(8,128)(2,1)S(1)}, bf16[3,32,512]{2,1,0:T(8,128)(2,1)S(1)}, u32[]{:S(2)}, u32[]{:S(2)}) collective-permute-start(bf16[3,32,512]{2,1,0:T(8,128)(2,1)S(1)} %shard_map.184.refs_1_), channel_id=1, source_target_pairs={{0,12},{1,13},{2,14},{3,15},{4,0},{5,1},{6,2},{7,3},{8,4},{9,5},{1... | collective-permute-start | bytes 294920 | tf_op jit(solution)/shard_map/ppermute | solution.py:440
  144.8 23.8 %collective-permute-start.40 = (bf16[3,128,512]{2,1,0:T(8,128)(2,1)S(1)}, bf16[3,128,512]{2,1,0:T(8,128)(2,1)S(1)}, u32[]{:S(2)}, u32[]{:S(2)}) collective-permute-start(bf16[3,128,512]{2,1,0:T(8,128)(2,1)S(1)} %shard_map.185.refs_1_), channel_id=1, source_target_pairs={{0,2},{1,3},{2,0},{3,1},{4,6},{5,7},{6,4},{7,5},{8,10},{9,11},{10,... | collective-permute-start | bytes 1179656 | tf_op jit(solution)/shard_map/ppermute | solution.py:440
  146.4 4.4 %collective-permute-start.14 = (bf16[128,512]{1,0:T(8,128)(2,1)S(1)}, bf16[128,512]{1,0:T(8,128)(2,1)S(1)}, u32[]{:S(2)}, u32[]{:S(2)}) collective-permute-start(bf16[128,512]{1,0:T(8,128)(2,1)S(1)} %get-tuple-element.85.refs_13_.refs_11_), channel_id=1, source_target_pairs={{1,0},{2,1},{3,2},{4,3},{5,4},{6,5},{7,6},{8,7},{9,8},{10,9},{11,1... | collective-permute-start | bytes 393224 | tf_op jit(solution)/shard_map/ppermute | solution.py:21
  148.3 11.3 %collective-permute-start.15 = (bf16[128,512]{1,0:T(8,128)(2,1)S(1)}, bf16[128,512]{1,0:T(8,128)(2,1)S(1)}, u32[]{:S(2)}, u32[]{:S(2)}) collective-permute-start(bf16[128,512]{1,0:T(8,128)(2,1)S(1)} %get-tuple-element.86.refs_14_.refs_12_), channel_id=1, source_target_pairs={{15,0},{0,1},{1,2},{2,3},{3,4},{4,5},{5,6},{6,7},{7,8},{8,9},{9,10... | collective-permute-start | bytes 393224 | tf_op jit(solution)/shard_map/ppermute | solution.py:21
  148.3 14.0 %collective-permute-start.16 = (bf16[128,512]{1,0:T(8,128)(2,1)S(1)}, bf16[128,512]{1,0:T(8,128)(2,1)S(1)}, u32[]{:S(2)}, u32[]{:S(2)}) collective-permute-start(bf16[128,512]{1,0:T(8,128)(2,1)S(1)} %get-tuple-element.87.refs_15_.refs_13_), channel_id=1, source_target_pairs={{2,0},{3,1},{4,2},{5,3},{6,4},{7,5},{8,6},{9,7},{10,8},{11,9},{12,... | collective-permute-start | bytes 393224 | tf_op jit(solution)/shard_map/ppermute | solution.py:21
  150.8 13.8 %collective-permute-start.17 = (bf16[128,512]{1,0:T(8,128)(2,1)S(1)}, bf16[128,512]{1,0:T(8,128)(2,1)S(1)}, u32[]{:S(2)}, u32[]{:S(2)}) collective-permute-start(bf16[128,512]{1,0:T(8,128)(2,1)S(1)} %get-tuple-element.88.refs_16_.refs_14_), channel_id=1, source_target_pairs={{14,0},{15,1},{0,2},{1,3},{2,4},{3,5},{4,6},{5,7},{6,8},{7,9},{8,1... | collective-permute-start | bytes 393224 | tf_op jit(solution)/shard_map/ppermute | solution.py:21
  159.6 6.4 %collective-permute-start.18 = (bf16[128,512]{1,0:T(8,128)(2,1)S(1)}, bf16[128,512]{1,0:T(8,128)(2,1)S(1)}, u32[]{:S(2)}, u32[]{:S(2)}) collective-permute-start(bf16[128,512]{1,0:T(8,128)(2,1)S(1)} %get-tuple-element.89.refs_17_.refs_15_), channel_id=1, source_target_pairs={{4,0},{5,1},{6,2},{7,3},{8,4},{9,5},{10,6},{11,7},{12,8},{13,9},{1... | collective-permute-start | bytes 393224 | tf_op jit(solution)/shard_map/ppermute | solution.py:21
  162.3 27.5 %collective-permute-start.30 = (bf16[4,128,512]{2,1,0:T(8,128)(2,1)S(1)}, bf16[4,128,512]{2,1,0:T(8,128)(2,1)S(1)}, u32[]{:S(2)}, u32[]{:S(2)}) collective-permute-start(bf16[4,128,512]{2,1,0:T(8,128)(2,1)S(1)} %shard_map.180.refs_1_), channel_id=1, source_target_pairs={{0,1},{1,0},{2,3},{3,2},{4,5},{5,4},{6,7},{7,6},{8,9},{9,8},{10,11... | collective-permute-start | bytes 1572872 | tf_op jit(solution)/shard_map/ppermute | solution.py:440
  162.3 27.5 %collective-permute-start.31 = (bf16[4,128,512]{2,1,0:T(8,128)(2,1)S(1)}, bf16[4,128,512]{2,1,0:T(8,128)(2,1)S(1)}, u32[]{:S(2)}, u32[]{:S(2)}) collective-permute-start(bf16[4,128,512]{2,1,0:T(8,128)(2,1)S(1)} %collective-permute-done.29.refs_2_), channel_id=1, source_target_pairs={{0,1},{1,0},{2,3},{3,2},{4,5},{5,4},{6,7},{7,6},{8,9},{9,8},{10,11... | collective-permute-start | bytes 1572872 | tf_op jit(solution)/shard_map/ppermute | solution.py:440
  164.7 7.3 %collective-permute-start.19 = (bf16[128,512]{1,0:T(8,128)(2,1)S(1)}, bf16[128,512]{1,0:T(8,128)(2,1)S(1)}, u32[]{:S(2)}, u32[]{:S(2)}) collective-permute-start(bf16[128,512]{1,0:T(8,128)(2,1)S(1)} %get-tuple-element.90.refs_18_.refs_16_), channel_id=1, source_target_pairs={{12,0},{13,1},{14,2},{15,3},{0,4},{1,5},{2,6},{3,7},{4,8},{5,9},{6... | collective-permute-start | bytes 393224 | tf_op jit(solution)/shard_map/ppermute | solution.py:21
  166.0 22.5 %collective-permute-start.41 = (bf16[3,128,512]{2,1,0:T(8,128)(2,1)S(1)}, bf16[3,128,512]{2,1,0:T(8,128)(2,1)S(1)}, u32[]{:S(2)}, u32[]{:S(2)}) collective-permute-start(bf16[3,128,512]{2,1,0:T(8,128)(2,1)S(1)} %shard_map.185.refs_1_), channel_id=1, source_target_pairs={{0,1},{1,0},{2,3},{3,2},{4,5},{5,4},{6,7},{7,6},{8,9},{9,8},{10,11... | collective-permute-start | bytes 1179656 | tf_op jit(solution)/shard_map/ppermute | solution.py:440
  168.6 19.9 %collective-permute-start.42 = (bf16[3,128,512]{2,1,0:T(8,128)(2,1)S(1)}, bf16[3,128,512]{2,1,0:T(8,128)(2,1)S(1)}, u32[]{:S(2)}, u32[]{:S(2)}) collective-permute-start(bf16[3,128,512]{2,1,0:T(8,128)(2,1)S(1)} %collective-permute-done.40.refs_2_), channel_id=1, source_target_pairs={{0,1},{1,0},{2,3},{3,2},{4,5},{5,4},{6,7},{7,6},{8,9},{9,8},{10,11... | collective-permute-start | bytes 1179656 | tf_op jit(solution)/shard_map/ppermute | solution.py:440
  172.0 14.9 %collective-permute-start.20 = (bf16[256,512]{1,0:T(8,128)(2,1)S(1)}, bf16[256,512]{1,0:T(8,128)(2,1)S(1)}, u32[]{:S(2)}, u32[]{:S(2)}) collective-permute-start(bf16[256,512]{1,0:T(8,128)(2,1)S(1)} %get-tuple-element.91.refs_19_.refs_17_), channel_id=1, source_target_pairs={{8,0},{9,1},{10,2},{11,3},{12,4},{13,5},{14,6},{15,7},{0,8},{1,9},... | collective-permute-start | bytes 786440 | tf_op jit(solution)/shard_map/ppermute | solution.py:21
  174.3 12.6 %copy-start = (bf16[1536,512]{1,0:T(8,128)(2,1)S(1)}, bf16[1536,512]{1,0:T(8,128)(2,1)}, u32[]{:S(2)}) copy-start(bf16[1536,512]{1,0:T(8,128)(2,1)} %refs_1_.1) | copy-start | bytes 4718596
  174.3 12.6 %copy-start.15 = (s32[1,11,128]{2,0,1:T(1,128)S(1)}, s32[1,11,128]{2,0,1:T(1,128)}, u32[]{:S(2)}) copy-start(s32[1,11,128]{2,0,1:T(1,128)} %param.14) | copy-start | bytes 16900
  (12 other events, 18.9 us)

commit v4 on v3

--- a/solution.py
+++ b/solution.py
@@ -12,7 +12,7 @@
 near_sets = 7
 bf16 = jnp.bfloat16
 f32 = jnp.float32
-params = pltpu.CompilerParams(vmem_limit_bytes=48 * 1024 * 1024)
+small, large = 24 * 1024 * 1024, 24 * 1024 * 1024
 
 
 def passed_along(block, axis, distance):
@@ -76,18 +76,24 @@
     return (lax.broadcasted_iota(jnp.int32, (cap, 128), 0) < count).astype(f32)
 
 
-def call(body, outs, scratch, *args, smem=()):
+def call(body, outs, scratch, *args, smem=(), after=(), vmem=small):
     spaces = [
         pl.BlockSpec(memory_space=pltpu.SMEM if i in smem else pltpu.VMEM) for i in range(len(args))
     ]
+    spaces += [pl.BlockSpec(memory_space=pl.ANY)] * len(after)
+
+    def kernel(*refs):
+        body(*refs[: len(args)], *refs[len(args) + len(after) :])
+
     return pl.pallas_call(
-        body,
+        kernel,
         out_shape=[jax.ShapeDtypeStruct(shape, kind) for shape, kind in outs],
         in_specs=spaces,
         out_specs=[pl.BlockSpec(memory_space=pltpu.VMEM)] * len(outs),
         scratch_shapes=[pltpu.VMEM(shape, kind) for shape, kind in scratch],
-        compiler_params=params,
-    )(*args)
+        compiler_params=pltpu.CompilerParams(vmem_limit_bytes=vmem),
+        cost_estimate=pl.CostEstimate(flops=1, bytes_accessed=1, transcendentals=0),
+    )(*args, *after)
 
 
 def pick_kernel(plan, *refs):
@@ -257,25 +263,17 @@
     (
         cotan_ref,
         recv_ref,
-        me_ref,
         w2_ref,
         live_ref,
         pre_ref,
         normed_ref,
         inv_ref,
-        node_ref,
-        gathered_ref,
-        gpn_ref,
-        act_node_ref,
-        gon_ref,
         gg_ref,
-        keep_ref,
-        sent_ref,
         goe_ref,
         local_ref,
-    ) = refs[:18]
-    gpe_refs, (gpe_ref, pick_ref, block_ref) = refs[18:-3], refs[-3:]
-    nodes, width = node_ref.shape
+    ) = refs[:10]
+    gpe_refs, (gpe_ref, pick_ref) = refs[10:-2], refs[-2:]
+    nodes = gg_ref.shape[0]
     cap = recv_ref.shape[2]
     for i, k in enumerate(near):
         pick_ref[i * cap : (i + 1) * cap, :] = pick_table(recv_ref[k], nodes)
@@ -293,6 +291,9 @@
     for j, out_ref in enumerate(gpe_refs):
         i = local_count + j
         out_ref[...] = gpe_ref[i * cap : (i + 1) * cap, :]
+
+
+def node_weight_kernel(me_ref, node_ref, gathered_ref, gpn_ref, act_node_ref, gon_ref, keep_ref, sent_ref, block_ref):
     put = functools.partial(put_block, me_ref, block_ref, keep_ref, sent_ref)
     put(0, node_ref[...], gpn_ref[...])
     put(1, gathered_ref[...], gpn_ref[...])
@@ -448,63 +449,60 @@
     return first, chips // first
 
 
-def reduce_over_chips(me, keep, sent):
-    bands = lax.axis_size("band")
-    first, second = split_of(bands)
+def add_stage(me, keep, arrived, stride, members, kind, after):
     count, rows, width = keep.shape
-    arrived = [in_group(sent, "band", 1, 2, 1)]
-    for stride, members in ((2, first), (2 * first, second)):
-        rows //= members
-        outs = call(
-            functools.partial(add_kernel, (len(arrived), stride, members)),
-            [((count, rows, width), f32)] + [((count, rows, width), bf16)] * (members - 1),
-            [],
-            me,
-            keep,
-            *arrived,
-            smem=(0,),
-        )
-        keep = outs[0]
-        arrived = [
-            in_group(out, "band", stride, members, j + 1) for j, out in enumerate(outs[1:])
-        ]
-    (piece,) = call(
-        functools.partial(add_kernel, (len(arrived), 1, 1)),
-        [((count, rows, width), bf16)],
+    shape = (count, rows // members, width)
+    outs = call(
+        functools.partial(add_kernel, (len(arrived), stride, members)),
+        [(shape, kind)] + [(shape, bf16)] * (members - 1),
         [],
         me,
         keep,
         *arrived,
         smem=(0,),
-    )
-    return piece
-
-
-def gather_over_chips(me, piece, blocks, shapes):
-    bands = lax.axis_size("band")
-    first, second = split_of(bands)
+        after=after,
+    )
+    return outs[0], [in_group(out, "band", stride, members, j + 1) for j, out in enumerate(outs[1:])]
+
+
+def held_until(array, after):
+    return pl.pallas_call(
+        lambda *refs: None,
+        out_shape=jax.ShapeDtypeStruct(array.shape, array.dtype),
+        in_specs=[pl.BlockSpec(memory_space=pl.ANY)] * (1 + len(after)),
+        out_specs=pl.BlockSpec(memory_space=pl.ANY),
+        input_output_aliases={0: 0},
+        cost_estimate=pl.CostEstimate(flops=1, bytes_accessed=1, transcendentals=0),
+    )(array, *after)
+
+
+def gather_stage(me, piece, stride, members, after):
     count, rows, width = piece.shape
-    pieces = [piece] + [
-        in_group(piece, "band", 2 * first, second, j) for j in range(1, second)
-    ]
+    pieces = [piece] + [in_group(piece, "band", stride, members, j) for j in range(1, members)]
     (mine,) = call(
-        functools.partial(gather_kernel, (2 * first, second)),
-        [((count, rows * second, width), bf16)],
+        functools.partial(gather_kernel, (stride, members)),
+        [((count, rows * members, width), bf16)],
         [],
         me,
         *pieces,
         smem=(0,),
-    )
-    pieces = [mine] + [in_group(mine, "band", 2, first, j) for j in range(1, first)]
+        after=after,
+    )
+    return mine
+
+
+def join_stage(me, mine, members, blocks, shapes, after):
+    pieces = [mine] + [in_group(mine, "band", 2, members, j) for j in range(1, members)]
     others = [in_group(one, "band", 1, 2, 1) for one in pieces]
     return call(
-        functools.partial(join_kernel, (first, blocks)),
+        functools.partial(join_kernel, (members, blocks)),
         [(shape, bf16) for shape in shapes],
         [],
         me,
         *pieces,
         *others,
         smem=(0,),
+        after=after,
     )
 
 
@@ -592,6 +590,7 @@
         node_latent,
         *sx_near,
         smem=(3,),
+        vmem=large,
     )
 
     outs = call(
@@ -623,6 +622,7 @@
         node_second,
         *sx_far,
         smem=(3,),
+        vmem=large,
     )
     gpe_far, outs = list(outs[: len(far_plan)]), outs[len(far_plan) :]
     act_far, goe_far, new_far, node_new, gathered, gpn, act_node, gon, gg = outs
@@ -631,32 +631,20 @@
     half = (width // 2, width)
     outs = call(
         functools.partial(back_kernel, (near, local_count)),
-        [
-            ((3, *half), f32),
-            ((3, *half), bf16),
-            ((near_rows, width), bf16),
-            ((local_rows, width), bf16),
-        ]
+        [((near_rows, width), bf16), ((local_rows, width), bf16)]
         + [((cap, width), bf16)] * len(near_steps),
-        [((near_rows, width), bf16), ((near_rows, nodes), bf16), ((width, width), f32)],
+        [((near_rows, width), bf16), ((near_rows, nodes), bf16)],
         cotan,
         recv_ids,
-        me,
         edge_second,
         live,
         pre,
         normed,
         inverse,
-        node_latent,
-        gathered,
-        gpn,
-        act_node,
-        gon,
         gg,
-        smem=(2,),
-    )
-    keep_node, sent_node, goe_near, gpe_local = outs[:4]
-    gpe_near = list(outs[4:])
+    )
+    goe_near, gpe_local = outs[:2]
+    gpe_near = list(outs[2:])
     back_near = [passed_along(block, "band", -d) for block, d in zip(gpe_near, near_steps)]
 
     order = near + far
@@ -678,52 +666,90 @@
         goe_near,
         goe_far,
         smem=(2,),
-    )
+        vmem=large,
+    )
+
+    def edge_outputs(after):
+        return call(
+            functools.partial(edge_kernel, (near, far, len(gpe))),
+            [((sets, cap, width), bf16), ((sets, cap, width), bf16), ((nodes, width), f32)],
+            [((total, width), bf16)],
+            edges,
+            cotan,
+            edge_first,
+            node_first,
+            live,
+            normed,
+            new_far,
+            node_cotan,
+            gpn,
+            recv_sum,
+            *gpe,
+            after=after,
+            vmem=large,
+        )
+
+    def node_output(base, after):
+        (grad_nodes,) = call(
+            functools.partial(final_kernel, (near[:local_count],) + near_plan + far_plan),
+            [((nodes, width), bf16)],
+            [((nodes, total), bf16), ((total, width), bf16)],
+            base,
+            edge_first,
+            send_ids,
+            *ids,
+            gpe_local,
+            *back_near,
+            *back_far,
+            after=after,
+            vmem=large,
+        )
+        return grad_nodes
+
+    def node_weights(after):
+        return call(
+            node_weight_kernel,
+            [((3, *half), f32), ((3, *half), bf16)],
+            [((width, width), f32)],
+            me,
+            node_latent,
+            gathered,
+            gpn,
+            act_node,
+            gon,
+            smem=(0,),
+            after=after,
+        )
 
     first, second = split_of(bands)
+    node_blocks, node_shapes = ((0, 0), (0, 1), (1, 0)), [(2 * width, width), (width, width)]
+    edge_blocks = ((0, 0), (0, 1), (0, 2), (1, 0))
+    edge_shapes = [(3 * width, width), (width, width)]
     if width // 2 % (16 * first * second) == 0:
-        piece_node = reduce_over_chips(me, keep_node, sent_node)
-        piece_edge = reduce_over_chips(me, keep_edge, sent_edge)
-        grad_n1, grad_n2 = gather_over_chips(
-            me, piece_node, ((0, 0), (0, 1), (1, 0)), [(2 * width, width), (width, width)]
-        )
-        grad_e1, grad_e2 = gather_over_chips(
-            me, piece_edge, ((0, 0), (0, 1), (0, 2), (1, 0)), [(3 * width, width), (width, width)]
-        )
+        along_y, along_z = (2, first), (2 * first, second)
+        sent_edge = held_until(sent_edge, back_far)
+        came_edge = [in_group(sent_edge, "band", 1, 2, 1)]
+        keep_node, sent_node = node_weights([sent_edge])
+        came_node = [in_group(sent_node, "band", 1, 2, 1)]
+        keep_edge, came_edge = add_stage(me, keep_edge, came_edge, *along_y, f32, [keep_node])
+        keep_node, came_node = add_stage(me, keep_node, came_node, *along_y, f32, [keep_edge])
+        edge_new, grad_edges, base = edge_outputs([keep_node])
+        keep_edge, came_edge = add_stage(me, keep_edge, came_edge, *along_z, f32, [base])
+        grad_nodes = node_output(base, [keep_edge])
+        keep_node, came_node = add_stage(me, keep_node, came_node, *along_z, f32, [grad_nodes])
+        piece_edge, _ = add_stage(me, keep_edge, came_edge, 1, 1, bf16, [keep_node])
+        piece_node, _ = add_stage(me, keep_node, came_node, 1, 1, bf16, [piece_edge])
+        mine_edge = gather_stage(me, piece_edge, *along_z, [piece_node])
+        mine_node = gather_stage(me, piece_node, *along_z, [mine_edge])
+        grad_e1, grad_e2 = join_stage(me, mine_edge, first, edge_blocks, edge_shapes, [mine_node])
+        grad_n1, grad_n2 = join_stage(me, mine_node, first, node_blocks, node_shapes, [grad_e2])
     else:
-        whole = reduce_whole(keep_node, sent_node)
+        whole = reduce_whole(*node_weights([]))
         grad_n1, grad_n2 = whole[:2].reshape(2 * width, width), whole[2]
         whole = reduce_whole(keep_edge, sent_edge)
         grad_e1, grad_e2 = whole[:3].reshape(3 * width, width), whole[3]
-
-    edge_new, grad_edges, base = call(
-        functools.partial(edge_kernel, (near, far, len(gpe))),
-        [((sets, cap, width), bf16), ((sets, cap, width), bf16), ((nodes, width), f32)],
-        [((total, width), bf16)],
-        edges,
-        cotan,
-        edge_first,
-        node_first,
-        live,
-        normed,
-        new_far,
-        node_cotan,
-        gpn,
-        recv_sum,
-        *gpe,
-    )
-    (grad_nodes,) = call(
-        functools.partial(final_kernel, (near[:local_count],) + near_plan + far_plan),
-        [((nodes, width), bf16)],
-        [((nodes, total), bf16), ((total, width), bf16)],
-        base,
-        edge_first,
-        send_ids,
-        *ids,
-        gpe_local,
-        *back_near,
-        *back_far,
-    )
+        edge_new, grad_edges, base = edge_outputs([])
+        grad_nodes = node_output(base, [])
     return (
         node_new,
         edge_new[None],

time: 192 us -> 190 us (0.990)
  local copies, waits for them, and re-layouts: 10.9 us -> 38.1 us
  starting transfers between devices: 70.8 us -> 58.9 us
  Pallas kernels: 42.5 us -> 32.6 us
  waiting for transfers between devices: 66.2 us -> 58.3 us
    unnamed x34 -> x166, local copies, waits for them, and re-layouts: 10.9 us -> 38.1 us
    pallas_call x17 -> x19, Pallas kernels: 42.5 us -> 32.6 us  [the longest x18 32.6 us: call(): pl.pallas_call(kernel, out_shape=[jax.ShapeDtypeStruct(shape, kind) for s...]
    ppermute x21, waiting for transfers between devices: 26.9 us -> 17 us  [passed_along(): return lax.ppermute(block, axis, route)]
    ppermute x22, starting transfers between devices: 33.6 us -> 24.3 us  [in_group(): return lax.ppermute(block, axis, route)]
    ppermute x21, starting transfers between devices: 37.1 us -> 34.7 us  [passed_along(): return lax.ppermute(block, axis, route)]
    ppermute x22, waiting for transfers between devices: 39.3 us -> 41.2 us  [in_group(): return lax.ppermute(block, axis, route)]
  transfers between devices with their start and end apart: 43 -> 43, of which waited for: 20 -> 18; matrix products, arithmetic and copies ran while one was open for 0% -> 0% of each run, Pallas kernels for 9% -> 12%
where the time goes in v4:
time: 190 us; the launch traced here: 189 us
  starting transfers between devices  58.9 us (31%)
  waiting for transfers between devices  58.3 us (31%)
  local copies, waits for them, and re-layouts  38.1 us (20%)
  Pallas kernels  32.6 us (17%)
    ppermute x22, waiting for transfers between devices, in_group(): return lax.ppermute(block, axis, route)  41.2 us
    unnamed x166, local copies, waits for them, and re-layouts  38.1 us
    ppermute x21, starting transfers between devices, passed_along(): return lax.ppermute(block, axis, route)  34.7 us
    pallas_call x18, Pallas kernels, call(): pl.pallas_call(kernel, out_shape=[jax.ShapeDtypeStruct(shape, kind) for s...  32.6 us
    ppermute x22, starting transfers between devices, in_group(): return lax.ppermute(block, axis, route)  24.3 us
    ppermute x21, waiting for transfers between devices, passed_along(): return lax.ppermute(block, axis, route)  17 us
  transfers between devices with their start and end apart: 43, of which 18 were waited for; matrix products, arithmetic and copies ran while one was open for 0% of the time, Pallas kernels for 12%

profile of v4, /device:TPU:0, one launch (start us, length us, event | category | flops | bytes accessed | tf_op | source)
XLA Modules:
  0.0 189.3 jit_solution(8282404374044915274)
XLA Ops:
  0.6 5.5 %collective-permute-start = (s32[11,1,128]{2,1,0:T(1,128)}, s32[11,1,128]{2,1,0:T(1,128)S(1)}, u32[]{:S(2)}, u32[]{:S(2)}) collective-permute-start(s32[11,1,128]{2,1,0:T(1,128)} %bitcast.18), channel_id=1, source_target_pairs={{1,0},{2,1},{3,2},{4,3},{5,4},{6,5},{7,6},{8,7},{9,8},{10,9},{11,1... | collective-permute-start | bytes 16904 | tf_op jit(solution)/shard_map/ppermute | solution.py:21
  8.6 1.6 collective-permute-start.5
  10.2 1.9 %collective-permute-done.1.refs_2_.refs_4_ = s32[11,1,128]{2,1,0:T(1,128)S(1)} collective-permute-done((s32[11,1,128]{2,1,0:T(1,128)}, s32[11,1,128]{2,1,0:T(1,128)S(1)}, u32[]{:S(2)}, u32[]{:S(2)}) %collective-permute-start.1) | collective-permute-done | bytes 5664 | tf_op jit(solution)/shard_map/ppermute | solution.py:21
  12.1 1.6 collective-permute-done.3.refs_4_.refs_6_
  14.2 2.6 %collective-permute-done.6.refs_7_.refs_9_ = s32[11,1,128]{2,1,0:T(1,128)S(1)} collective-permute-done((s32[11,1,128]{2,1,0:T(1,128)}, s32[11,1,128]{2,1,0:T(1,128)S(1)}, u32[]{:S(2)}, u32[]{:S(2)}) %collective-permute-start.6) | collective-permute-done | bytes 5664 | tf_op jit(solution)/shard_map/ppermute | solution.py:21
  18.5 3.7 %collective-permute-start.10 = (bf16[128,512]{1,0:T(8,128)(2,1)S(1)}, bf16[128,512]{1,0:T(8,128)(2,1)S(1)}, u32[]{:S(2)}, u32[]{:S(2)}) collective-permute-start(bf16[128,512]{1,0:T(8,128)(2,1)S(1)} %get-tuple-element.67), channel_id=1, source_target_pairs={{2,0},{3,1},{4,2},{5,3},{6,4},{7,5},{8,6},{9,7},{10,8},{11,9},{12,... | collective-permute-start | bytes 393224 | tf_op jit(solution)/shard_map/ppermute | solution.py:21
  23.5 3.2 %collective-permute-start.8 = (bf16[128,512]{1,0:T(8,128)(2,1)S(1)}, bf16[128,512]{1,0:T(8,128)(2,1)S(1)}, u32[]{:S(2)}, u32[]{:S(2)}) collective-permute-start(bf16[128,512]{1,0:T(8,128)(2,1)S(1)} %get-tuple-element.65), channel_id=1, source_target_pairs={{1,0},{2,1},{3,2},{4,3},{5,4},{6,5},{7,6},{8,7},{9,8},{10,9},{11,1... | collective-permute-start | bytes 393224 | tf_op jit(solution)/shard_map/ppermute | solution.py:21
  26.8 3.2 %collective-permute-done.7.refs_7_.refs_5_ = bf16[128,512]{1,0:T(8,128)(2,1)S(1)} collective-permute-done((bf16[128,512]{1,0:T(8,128)(2,1)S(1)}, bf16[128,512]{1,0:T(8,128)(2,1)S(1)}, u32[]{:S(2)}, u32[]{:S(2)}) %collective-permute-start.7) | collective-permute-done | bytes 131104 | tf_op jit(solution)/shard_map/ppermute | solution.py:21
  30.6 3.6 %collective-permute-done.8.refs_8_.refs_6_ = bf16[128,512]{1,0:T(8,128)(2,1)S(1)} collective-permute-done((bf16[128,512]{1,0:T(8,128)(2,1)S(1)}, bf16[128,512]{1,0:T(8,128)(2,1)S(1)}, u32[]{:S(2)}, u32[]{:S(2)}) %collective-permute-start.8) | collective-permute-done | bytes 131104 | tf_op jit(solution)/shard_map/ppermute | solution.py:21
  34.2 1.8 collective-permute-done.9.refs_9_.refs_7_
  36.0 1.5 copy-done
  37.5 1.4 copy-done.2
  41.9 4.8 %shard_map.171 = (bf16[384,512]{1,0:T(8,128)(2,1)S(1)}, bf16[896,512]{1,0:T(8,128)(2,1)S(1)}, f32[896,512]{1,0:T(8,128)S(1)}, f32[896,512]{1,0:T(8,128)S(1)}, f3...) custom-call(bf16[11,128,512]{2,1,0:T(8,128)(2,1)S(1)} %bitcast.7, ...), custom_call_target="tpu_custom_call" | custom-call | flops 1 | bytes 1 | tf_op jit(solution)/shard_map/pallas_call | solution.py:88
  46.8 1.3 copy-done.9
  48.1 1.2 copy-done.23
  51.9 1.5 copy-done.17
  53.4 7.2 %shard_map.172 = (bf16[128,512]{1,0:T(8,128)(2,1)}, bf16[128,512]{1,0:T(8,128)(2,1)}, bf16[256,512]{1,0:T(8,128)(2,1)}, bf16[512,512]{1,0:T(8,128)(2,1)S(1)}, bf...) custom-call(bf16[11,128,512]{2,1,0:T(8,128)(2,1)S(1)} %bitcast.8, ...), custom_call_target="tpu_custom_call" | custom-call | flops 1 | bytes 1 | tf_op jit(solution)/shard_map/pallas_call | solution.py:88
  66.6 7.2 %collective-permute-start.16 = (bf16[256,512]{1,0:T(8,128)(2,1)}, bf16[256,512]{1,0:T(8,128)(2,1)}, u32[]{:S(2)}, u32[]{:S(2)}) collective-permute-start(bf16[256,512]{1,0:T(8,128)(2,1)} %get-tuple-element.88.refs_19_.refs_17_), channel_id=1, source_target_pairs={{8,0},{9,1},{10,2},{11,3},{12,4},{13,5},{14,6},{15,7},{0,8},{1,9},... | collective-permute-start | bytes 786440 | tf_op jit(solution)/shard_map/ppermute | solution.py:21
  73.9 2.0 %collective-permute-start.15 = (bf16[128,512]{1,0:T(8,128)(2,1)}, bf16[128,512]{1,0:T(8,128)(2,1)}, u32[]{:S(2)}, u32[]{:S(2)}) collective-permute-start(bf16[128,512]{1,0:T(8,128)(2,1)} %get-tuple-element.87.refs_18_.refs_16_), channel_id=1, source_target_pairs={{12,0},{13,1},{14,2},{15,3},{0,4},{1,5},{2,6},{3,7},{4,8},{5,9},{6... | collective-permute-start | bytes 393224 | tf_op jit(solution)/shard_map/ppermute | solution.py:21
  75.9 1.4 copy-done.5
  77.3 1.5 copy-done.10
  79.8 1.5 copy-done.24
  84.4 2.2 %shard_map.173 = (bf16[896,512]{1,0:T(8,128)(2,1)S(1)}, bf16[384,512]{1,0:T(8,128)(2,1)S(1)}, bf16[128,512]{1,0:T(8,128)(2,1)S(1)}, bf16[128,512]{1,0:T(8,128)(2...) custom-call(bf16[11,128,512]{2,1,0:T(8,128)(2,1)S(1)} %bitcast.12, s32[11,1,128]{2,1,0:T(1,128)S(1)} %bitcast.16, ...), custom_call_target="tpu_custom_call" | custom-call | flops 1 | bytes 1 | tf_op jit(solution)/shard_map/pallas_call | solution.py:88
  86.8 5.1 %shard_map.174 = (f32[4,256,512]{2,1,0:T(8,128)S(1)}, bf16[4,256,512]{2,1,0:T(8,128)(2,1)S(1)}, bf16[320,512]{1,0:T(8,128)(2,1)S(1)}) custom-call(bf16[11,128,512]{2,1,0:T(8,128)(2,1)S(1)} %bitcast.9, s32[11,1,128]{2,1,0:T(1,128)S(1)} %bitcast.17, s32[1]{0:T(128)} %bitcast.4.refs_2_.refs_0_, bf16[320,512]{1,0:T(8,128)(2,1)S(1)} %copy-done.8, ...), custom_call_target="tpu_custom_call" | custom-call | flops 1 | bytes 1 | tf_op jit(solution)/shard_map/pallas_call | solution.py:88
  92.9 1.3 copy-done.21
  100.2 1.3 shard_map.176
  105.2 2.8 %collective-permute-start.19 = (bf16[128,512]{1,0:T(8,128)(2,1)S(1)}, bf16[128,512]{1,0:T(8,128)(2,1)S(1)}, u32[]{:S(2)}, u32[]{:S(2)}) collective-permute-start(bf16[128,512]{1,0:T(8,128)(2,1)S(1)} %copy-done.43), channel_id=1, source_target_pairs={{1,0},{2,1},{3,2},{4,3},{5,4},{6,5},{7,6},{8,7},{9,8},{10,9},{11,1... | collective-permute-start | bytes 393224 | tf_op jit(solution)/shard_map/ppermute | solution.py:21
  108.0 1.7 collective-permute-start.21
  109.7 10.0 %collective-permute-done.23.refs_2_ = bf16[4,128,512]{2,1,0:T(8,128)(2,1)S(1)} collective-permute-done((bf16[4,128,512]{2,1,0:T(8,128)(2,1)S(1)}, bf16[4,128,512]{2,1,0:T(8,128)(2,1)S(1)}, u32[]{:S(2)}, u32[]{:S(2)}) %collective-permute-start.23) | collective-permute-done | bytes 524320 | tf_op jit(solution)/shard_map/ppermute | solution.py:441
  119.8 2.5 %collective-permute-start.22 = (bf16[128,512]{1,0:T(8,128)(2,1)S(1)}, bf16[128,512]{1,0:T(8,128)(2,1)S(1)}, u32[]{:S(2)}, u32[]{:S(2)}) collective-permute-start(bf16[128,512]{1,0:T(8,128)(2,1)S(1)} %get-tuple-element.85.refs_16_.refs_14_), channel_id=1, source_target_pairs={{14,0},{15,1},{0,2},{1,3},{2,4},{3,5},{4,6},{5,7},{6,8},{7,9},{8,1... | collective-permute-start | bytes 393224 | tf_op jit(solution)/shard_map/ppermute | solution.py:21
  122.3 5.0 %shard_map.179 = (bf16[11,128,512]{2,1,0:T(8,128)(2,1)}, bf16[11,128,512]{2,1,0:T(8,128)(2,1)}, f32[320,512]{1,0:T(8,128)S(1)}) custom-call(bf16[11,128,512]{2,1,0:T(8,128)(2,1)S(1)} %bitcast.10, bf16[11,128,512]{2,1,0:T(8,128)(2,1)S(1)} %bitcast.13, bf16[1536,512]{1,0:T(8,128)(2,1)S(1)} %copy-done.1, bf16[1024,512]{1,0:T(8,128)(2,1)S(1)} %copy-done.18, ...), custom_call_target="tpu_custom_call" | custom-call | flops 1 | bytes 1 | tf_op jit(solution)/shard_map/pallas_call | solution.py:88
  127.5 4.1 %collective-permute-start.25 = (bf16[4,32,512]{2,1,0:T(8,128)(2,1)S(1)}, bf16[4,32,512]{2,1,0:T(8,128)(2,1)S(1)}, u32[]{:S(2)}, u32[]{:S(2)}) collective-permute-start(bf16[4,32,512]{2,1,0:T(8,128)(2,1)S(1)} %get-tuple-element.109), channel_id=1, source_target_pairs={{0,8},{1,9},{2,10},{3,11},{4,12},{5,13},{6,14},{7,15},{8,0},{9,1},... | collective-permute-start | bytes 393224 | tf_op jit(solution)/shard_map/ppermute | solution.py:441
  131.6 1.8 collective-permute-done.21.refs_13_
  133.4 2.7 %collective-permute-start.26 = (bf16[4,32,512]{2,1,0:T(8,128)(2,1)S(1)}, bf16[4,32,512]{2,1,0:T(8,128)(2,1)S(1)}, u32[]{:S(2)}, u32[]{:S(2)}) collective-permute-start(bf16[4,32,512]{2,1,0:T(8,128)(2,1)S(1)} %get-tuple-element.110), channel_id=1, source_target_pairs={{0,12},{1,13},{2,14},{3,15},{4,0},{5,1},{6,2},{7,3},{8,4},{9,5},{1... | collective-permute-start | bytes 393224 | tf_op jit(solution)/shard_map/ppermute | solution.py:441
  136.1 2.7 %shard_map.181.refs_3_ = bf16[320,512]{1,0:T(8,128)(2,1)} custom-call(f32[320,512]{1,0:T(8,128)S(1)} %get-tuple-element.104.refs_3_.refs_0_, bf16[1536,512]{1,0:T(8,128)(2,1)S(1)} %copy-done.1, s32[11,1,128]{2,1,0:T(1,128)S(1)} %bitcast.26, s32[11,1,128]{2,1,0:T(1,128)S(1)} %collective-permute-done.refs_1_.refs_3_, ...), custom_call_target="tpu_custom_call" | custom-call | flops 1 | bytes 1 | tf_op jit(solution)/shard_map/pallas_call | solution.py:88
  141.0 1.6 collective-permute-done.26.refs_4_
  142.7 2.8 %collective-permute-start.28 = (bf16[4,32,512]{2,1,0:T(8,128)(2,1)S(1)}, bf16[4,32,512]{2,1,0:T(8,128)(2,1)S(1)}, u32[]{:S(2)}, u32[]{:S(2)}) collective-permute-start(bf16[4,32,512]{2,1,0:T(8,128)(2,1)S(1)} %shard_map.183.refs_5_.refs_1_), channel_id=1, source_target_pairs={{0,4},{1,5},{2,6},{3,7},{4,8},{5,9},{6,10},{7,11},{8,12},{9,13},{1... | collective-permute-start | bytes 393224 | tf_op jit(solution)/shard_map/ppermute | solution.py:441
  145.5 2.4 %collective-permute-start.30 = (bf16[4,32,512]{2,1,0:T(8,128)(2,1)S(1)}, bf16[4,32,512]{2,1,0:T(8,128)(2,1)S(1)}, u32[]{:S(2)}, u32[]{:S(2)}) collective-permute-start(bf16[4,32,512]{2,1,0:T(8,128)(2,1)S(1)} %shard_map.183.refs_5_.refs_1_), channel_id=1, source_target_pairs={{0,12},{1,13},{2,14},{3,15},{4,0},{5,1},{6,2},{7,3},{8,4},{9,5},{1... | collective-permute-start | bytes 393224 | tf_op jit(solution)/shard_map/ppermute | solution.py:441
  148.6 1.3 collective-permute-start.33
  149.9 13.0 %collective-permute-done.32.refs_3_ = bf16[3,32,512]{2,1,0:T(8,128)(2,1)S(1)} collective-permute-done((bf16[3,32,512]{2,1,0:T(8,128)(2,1)S(1)}, bf16[3,32,512]{2,1,0:T(8,128)(2,1)S(1)}, u32[]{:S(2)}, u32[]{:S(2)}) %collective-permute-start.32) | collective-permute-done | bytes 98336 | tf_op jit(solution)/shard_map/ppermute | solution.py:441
  163.1 2.6 %collective-permute-start.37 = (bf16[3,32,512]{2,1,0:T(8,128)(2,1)S(1)}, bf16[3,32,512]{2,1,0:T(8,128)(2,1)S(1)}, u32[]{:S(2)}, u32[]{:S(2)}) collective-permute-start(bf16[3,32,512]{2,1,0:T(8,128)(2,1)S(1)} %shard_map.184.refs_5_.refs_1_), channel_id=1, source_target_pairs={{0,4},{1,5},{2,6},{3,7},{4,8},{5,9},{6,10},{7,11},{8,12},{9,13},{1... | collective-permute-start | bytes 294920 | tf_op jit(solution)/shard_map/ppermute | solution.py:441
  165.7 1.5 collective-permute-start.38
  168.1 2.3 %collective-permute-done.37.refs_2_ = bf16[3,32,512]{2,1,0:T(8,128)(2,1)S(1)} collective-permute-done((bf16[3,32,512]{2,1,0:T(8,128)(2,1)S(1)}, bf16[3,32,512]{2,1,0:T(8,128)(2,1)S(1)}, u32[]{:S(2)}, u32[]{:S(2)}) %collective-permute-start.37) | collective-permute-done | bytes 98336 | tf_op jit(solution)/shard_map/ppermute | solution.py:441
  170.5 3.4 %collective-permute-done.38.refs_3_ = bf16[3,32,512]{2,1,0:T(8,128)(2,1)S(1)} collective-permute-done((bf16[3,32,512]{2,1,0:T(8,128)(2,1)S(1)}, bf16[3,32,512]{2,1,0:T(8,128)(2,1)S(1)}, u32[]{:S(2)}, u32[]{:S(2)}) %collective-permute-start.38) | collective-permute-done | bytes 98336 | tf_op jit(solution)/shard_map/ppermute | solution.py:441
  173.9 1.9 %collective-permute-start.40 = (bf16[3,128,512]{2,1,0:T(8,128)(2,1)S(1)}, bf16[3,128,512]{2,1,0:T(8,128)(2,1)S(1)}, u32[]{:S(2)}, u32[]{:S(2)}) collective-permute-start(bf16[3,128,512]{2,1,0:T(8,128)(2,1)S(1)} %shard_map.186.refs_5_.refs_1_), channel_id=1, source_target_pairs={{0,2},{1,3},{2,0},{3,1},{4,6},{5,7},{6,4},{7,5},{8,10},{9,11},{10,... | collective-permute-start | bytes 1179656 | tf_op jit(solution)/shard_map/ppermute | solution.py:441
  177.5 7.7 %collective-permute-done.40.refs_2_ = bf16[3,128,512]{2,1,0:T(8,128)(2,1)S(1)} collective-permute-done((bf16[3,128,512]{2,1,0:T(8,128)(2,1)S(1)}, bf16[3,128,512]{2,1,0:T(8,128)(2,1)S(1)}, u32[]{:S(2)}, u32[]{:S(2)}) %collective-permute-start.40) | collective-permute-done | bytes 393248 | tf_op jit(solution)/shard_map/ppermute | solution.py:441
  185.3 1.5 shard_map.187
  188.0 1.3 shard_map.188
  (223 shorter events, 39.9 us)
Async XLA Ops:
  0.6 8.0 %collective-permute-start = (s32[11,1,128]{2,1,0:T(1,128)}, s32[11,1,128]{2,1,0:T(1,128)S(1)}, u32[]{:S(2)}, u32[]{:S(2)}) collective-permute-start(s32[11,1,128]{2,1,0:T(1,128)} %bitcast.18), channel_id=1, source_target_pairs={{1,0},{2,1},{3,2},{4,3},{5,4},{6,5},{7,6},{8,7},{9,8},{10,9},{11,1... | collective-permute-start | bytes 16904 | tf_op jit(solution)/shard_map/ppermute | solution.py:21
  6.1 6.0 %collective-permute-start.1 = (s32[11,1,128]{2,1,0:T(1,128)}, s32[11,1,128]{2,1,0:T(1,128)S(1)}, u32[]{:S(2)}, u32[]{:S(2)}) collective-permute-start(s32[11,1,128]{2,1,0:T(1,128)} %bitcast.19), channel_id=1, source_target_pairs={{15,0},{0,1},{1,2},{2,3},{3,4},{4,5},{5,6},{6,7},{7,8},{8,9},{9,10... | collective-permute-start | bytes 16904 | tf_op jit(solution)/shard_map/ppermute | solution.py:21
  6.1 6.0 %collective-permute-start.2 = (s32[11,1,128]{2,1,0:T(1,128)}, s32[11,1,128]{2,1,0:T(1,128)S(1)}, u32[]{:S(2)}, u32[]{:S(2)}) collective-permute-start(s32[11,1,128]{2,1,0:T(1,128)} %bitcast.20), channel_id=1, source_target_pairs={{2,0},{3,1},{4,2},{5,3},{6,4},{7,5},{8,6},{9,7},{10,8},{11,9},{12,... | collective-permute-start | bytes 16904 | tf_op jit(solution)/shard_map/ppermute | solution.py:21
  7.2 6.5 %collective-permute-start.3 = (s32[11,1,128]{2,1,0:T(1,128)}, s32[11,1,128]{2,1,0:T(1,128)S(1)}, u32[]{:S(2)}, u32[]{:S(2)}) collective-permute-start(s32[11,1,128]{2,1,0:T(1,128)} %bitcast.21), channel_id=1, source_target_pairs={{14,0},{15,1},{0,2},{1,3},{2,4},{3,5},{4,6},{5,7},{6,8},{7,9},{8,1... | collective-permute-start | bytes 16904 | tf_op jit(solution)/shard_map/ppermute | solution.py:21
  8.2 5.6 %collective-permute-start.4 = (s32[11,1,128]{2,1,0:T(1,128)}, s32[11,1,128]{2,1,0:T(1,128)S(1)}, u32[]{:S(2)}, u32[]{:S(2)}) collective-permute-start(s32[11,1,128]{2,1,0:T(1,128)} %bitcast.22), channel_id=1, source_target_pairs={{4,0},{5,1},{6,2},{7,3},{8,4},{9,5},{10,6},{11,7},{12,8},{13,9},{1... | collective-permute-start | bytes 16904 | tf_op jit(solution)/shard_map/ppermute | solution.py:21
  8.6 5.6 %collective-permute-start.5 = (s32[11,1,128]{2,1,0:T(1,128)}, s32[11,1,128]{2,1,0:T(1,128)S(1)}, u32[]{:S(2)}, u32[]{:S(2)}) collective-permute-start(s32[11,1,128]{2,1,0:T(1,128)} %bitcast.23), channel_id=1, source_target_pairs={{12,0},{13,1},{14,2},{15,3},{0,4},{1,5},{2,6},{3,7},{4,8},{5,9},{6... | collective-permute-start | bytes 16904 | tf_op jit(solution)/shard_map/ppermute | solution.py:21
  12.1 4.7 %collective-permute-start.6 = (s32[11,1,128]{2,1,0:T(1,128)}, s32[11,1,128]{2,1,0:T(1,128)S(1)}, u32[]{:S(2)}, u32[]{:S(2)}) collective-permute-start(s32[11,1,128]{2,1,0:T(1,128)} %bitcast.24), channel_id=1, source_target_pairs={{8,0},{9,1},{10,2},{11,3},{12,4},{13,5},{14,6},{15,7},{0,8},{1,9},... | collective-permute-start | bytes 16904 | tf_op jit(solution)/shard_map/ppermute | solution.py:21
  18.5 8.2 %collective-permute-start.10 = (bf16[128,512]{1,0:T(8,128)(2,1)S(1)}, bf16[128,512]{1,0:T(8,128)(2,1)S(1)}, u32[]{:S(2)}, u32[]{:S(2)}) collective-permute-start(bf16[128,512]{1,0:T(8,128)(2,1)S(1)} %get-tuple-element.67), channel_id=1, source_target_pairs={{2,0},{3,1},{4,2},{5,3},{6,4},{7,5},{8,6},{9,7},{10,8},{11,9},{12,... | collective-permute-start | bytes 393224 | tf_op jit(solution)/shard_map/ppermute | solution.py:21
  22.3 7.8 %collective-permute-start.7 = (bf16[128,512]{1,0:T(8,128)(2,1)S(1)}, bf16[128,512]{1,0:T(8,128)(2,1)S(1)}, u32[]{:S(2)}, u32[]{:S(2)}) collective-permute-start(bf16[128,512]{1,0:T(8,128)(2,1)S(1)} %get-tuple-element.64), channel_id=1, source_target_pairs={{15,0},{0,1},{1,2},{2,3},{3,4},{4,5},{5,6},{6,7},{7,8},{8,9},{9,10... | collective-permute-start | bytes 393224 | tf_op jit(solution)/shard_map/ppermute | solution.py:21
  23.5 28.3 %collective-permute-start.13 = (bf16[256,512]{1,0:T(8,128)(2,1)S(1)}, bf16[256,512]{1,0:T(8,128)(2,1)S(1)}, u32[]{:S(2)}, u32[]{:S(2)}) collective-permute-start(bf16[256,512]{1,0:T(8,128)(2,1)S(1)} %get-tuple-element.71), channel_id=1, source_target_pairs={{8,0},{9,1},{10,2},{11,3},{12,4},{13,5},{14,6},{15,7},{0,8},{1,9},... | collective-permute-start | bytes 786440 | tf_op jit(solution)/shard_map/ppermute | solution.py:21
  23.5 10.7 %collective-permute-start.8 = (bf16[128,512]{1,0:T(8,128)(2,1)S(1)}, bf16[128,512]{1,0:T(8,128)(2,1)S(1)}, u32[]{:S(2)}, u32[]{:S(2)}) collective-permute-start(bf16[128,512]{1,0:T(8,128)(2,1)S(1)} %get-tuple-element.65), channel_id=1, source_target_pairs={{1,0},{2,1},{3,2},{4,3},{5,4},{6,5},{7,6},{8,7},{9,8},{10,9},{11,1... | collective-permute-start | bytes 393224 | tf_op jit(solution)/shard_map/ppermute | solution.py:21
  26.7 9.3 %collective-permute-start.9 = (bf16[128,512]{1,0:T(8,128)(2,1)S(1)}, bf16[128,512]{1,0:T(8,128)(2,1)S(1)}, u32[]{:S(2)}, u32[]{:S(2)}) collective-permute-start(bf16[128,512]{1,0:T(8,128)(2,1)S(1)} %get-tuple-element.66), channel_id=1, source_target_pairs={{14,0},{15,1},{0,2},{1,3},{2,4},{3,5},{4,6},{5,7},{6,8},{7,9},{8,1... | collective-permute-start | bytes 393224 | tf_op jit(solution)/shard_map/ppermute | solution.py:21
  26.7 25.0 %collective-permute-start.11 = (bf16[128,512]{1,0:T(8,128)(2,1)S(1)}, bf16[128,512]{1,0:T(8,128)(2,1)S(1)}, u32[]{:S(2)}, u32[]{:S(2)}) collective-permute-start(bf16[128,512]{1,0:T(8,128)(2,1)S(1)} %get-tuple-element.69), channel_id=1, source_target_pairs={{12,0},{13,1},{14,2},{15,3},{0,4},{1,5},{2,6},{3,7},{4,8},{5,9},{6... | collective-permute-start | bytes 393224 | tf_op jit(solution)/shard_map/ppermute | solution.py:21
  30.0 21.7 %collective-permute-start.12 = (bf16[128,512]{1,0:T(8,128)(2,1)S(1)}, bf16[128,512]{1,0:T(8,128)(2,1)S(1)}, u32[]{:S(2)}, u32[]{:S(2)}) collective-permute-start(bf16[128,512]{1,0:T(8,128)(2,1)S(1)} %get-tuple-element.70), channel_id=1, source_target_pairs={{4,0},{5,1},{6,2},{7,3},{8,4},{9,5},{10,6},{11,7},{12,8},{13,9},{1... | collective-permute-start | bytes 393224 | tf_op jit(solution)/shard_map/ppermute | solution.py:21
  53.4 22.5 %copy-start.79 = (s32[1,11,128]{2,0,1:T(1,128)S(1)}, s32[1,11,128]{2,0,1:T(1,128)}, u32[]{:S(2)}) copy-start(s32[1,11,128]{2,0,1:T(1,128)} %param.13) | copy-start | bytes 16900
  66.6 28.4 %collective-permute-start.16 = (bf16[256,512]{1,0:T(8,128)(2,1)}, bf16[256,512]{1,0:T(8,128)(2,1)}, u32[]{:S(2)}, u32[]{:S(2)}) collective-permute-start(bf16[256,512]{1,0:T(8,128)(2,1)} %get-tuple-element.88.refs_19_.refs_17_), channel_id=1, source_target_pairs={{8,0},{9,1},{10,2},{11,3},{12,4},{13,5},{14,6},{15,7},{0,8},{1,9},... | collective-permute-start | bytes 786440 | tf_op jit(solution)/shard_map/ppermute | solution.py:21
  73.9 21.1 %collective-permute-start.14 = (bf16[128,512]{1,0:T(8,128)(2,1)}, bf16[128,512]{1,0:T(8,128)(2,1)}, u32[]{:S(2)}, u32[]{:S(2)}) collective-permute-start(bf16[128,512]{1,0:T(8,128)(2,1)} %get-tuple-element.86.refs_17_.refs_15_), channel_id=1, source_target_pairs={{4,0},{5,1},{6,2},{7,3},{8,4},{9,5},{10,6},{11,7},{12,8},{13,9},{1... | collective-permute-start | bytes 393224 | tf_op jit(solution)/shard_map/ppermute | solution.py:21
  73.9 21.1 %collective-permute-start.15 = (bf16[128,512]{1,0:T(8,128)(2,1)}, bf16[128,512]{1,0:T(8,128)(2,1)}, u32[]{:S(2)}, u32[]{:S(2)}) collective-permute-start(bf16[128,512]{1,0:T(8,128)(2,1)} %get-tuple-element.87.refs_18_.refs_16_), channel_id=1, source_target_pairs={{12,0},{13,1},{14,2},{15,3},{0,4},{1,5},{2,6},{3,7},{4,8},{5,9},{6... | collective-permute-start | bytes 393224 | tf_op jit(solution)/shard_map/ppermute | solution.py:21
  95.0 7.1 %collective-permute-start.18 = (bf16[4,256,512]{2,1,0:T(8,128)(2,1)}, bf16[4,256,512]{2,1,0:T(8,128)(2,1)S(1)}, u32[]{:S(2)}, u32[]{:S(2)}) collective-permute-start(bf16[4,256,512]{2,1,0:T(8,128)(2,1)} %shard_map.175.refs_6_), channel_id=1, source_target_pairs={{0,1},{1,0},{2,3},{3,2},{4,5},{5,4},{6,7},{7,6},{8,9},{9,8},{10,11... | collective-permute-start | bytes 3145736 | tf_op jit(solution)/shard_map/ppermute | solution.py:441
  101.5 2.5 %collective-permute-start.17 = (bf16[3,256,512]{2,1,0:T(8,128)(2,1)S(1)}, bf16[3,256,512]{2,1,0:T(8,128)(2,1)S(1)}, u32[]{:S(2)}, u32[]{:S(2)}) collective-permute-start(bf16[3,256,512]{2,1,0:T(8,128)(2,1)S(1)} %get-tuple-element.99), channel_id=1, source_target_pairs={{0,1},{1,0},{2,3},{3,2},{4,5},{5,4},{6,7},{7,6},{8,9},{9,8},{10,11... | collective-permute-start | bytes 2359304 | tf_op jit(solution)/shard_map/ppermute | solution.py:441
  102.1 20.2 %copy-start.18 = (bf16[1024,512]{1,0:T(8,128)(2,1)S(1)}, bf16[1024,512]{1,0:T(8,128)(2,1)}, u32[]{:S(2)}) copy-start(bf16[1024,512]{1,0:T(8,128)(2,1)} %refs_3_.7) | copy-start | bytes 3145732
  102.1 20.1 %copy-start.20 = (bf16[384,512]{1,0:T(8,128)(2,1)S(1)}, bf16[384,512]{1,0:T(8,128)(2,1)}, u32[]{:S(2)}) copy-start(bf16[384,512]{1,0:T(8,128)(2,1)} %copy-done.19) | copy-start | bytes 1179652
  102.1 20.1 %copy-start.27 = (f32[896,128]{1,0:T(8,128)S(1)}, f32[896,128]{1,0:T(8,128)}, u32[]{:S(2)}) copy-start(f32[896,128]{1,0:T(8,128)} %copy-done.25) | copy-start | bytes 1376260
  102.1 20.1 %copy-start.29 = (bf16[320,512]{1,0:T(8,128)(2,1)S(1)}, bf16[320,512]{1,0:T(8,128)(2,1)}, u32[]{:S(2)}) copy-start(bf16[320,512]{1,0:T(8,128)(2,1)} %refs_7_.3) | copy-start | bytes 983044
  102.4 17.3 %collective-permute-start.23 = (bf16[4,128,512]{2,1,0:T(8,128)(2,1)S(1)}, bf16[4,128,512]{2,1,0:T(8,128)(2,1)S(1)}, u32[]{:S(2)}, u32[]{:S(2)}) collective-permute-start(bf16[4,128,512]{2,1,0:T(8,128)(2,1)S(1)} %get-tuple-element.105), channel_id=1, source_target_pairs={{0,2},{1,3},{2,0},{3,1},{4,6},{5,7},{6,4},{7,5},{8,10},{9,11},{10,... | collective-permute-start | bytes 1572872 | tf_op jit(solution)/shard_map/ppermute | solution.py:441
  104.1 34.7 %collective-permute-start.27 = (bf16[3,128,512]{2,1,0:T(8,128)(2,1)S(1)}, bf16[3,128,512]{2,1,0:T(8,128)(2,1)S(1)}, u32[]{:S(2)}, u32[]{:S(2)}) collective-permute-start(bf16[3,128,512]{2,1,0:T(8,128)(2,1)S(1)} %get-tuple-element.111), channel_id=1, source_target_pairs={{0,2},{1,3},{2,0},{3,1},{4,6},{5,7},{6,4},{7,5},{8,10},{9,11},{10,... | collective-permute-start | bytes 1179656 | tf_op jit(solution)/shard_map/ppermute | solution.py:441
  105.2 22.2 %collective-permute-start.19 = (bf16[128,512]{1,0:T(8,128)(2,1)S(1)}, bf16[128,512]{1,0:T(8,128)(2,1)S(1)}, u32[]{:S(2)}, u32[]{:S(2)}) collective-permute-start(bf16[128,512]{1,0:T(8,128)(2,1)S(1)} %copy-done.43), channel_id=1, source_target_pairs={{1,0},{2,1},{3,2},{4,3},{5,4},{6,5},{7,6},{8,7},{9,8},{10,9},{11,1... | collective-permute-start | bytes 393224 | tf_op jit(solution)/shard_map/ppermute | solution.py:21
  108.0 19.5 %collective-permute-start.20 = (bf16[128,512]{1,0:T(8,128)(2,1)S(1)}, bf16[128,512]{1,0:T(8,128)(2,1)S(1)}, u32[]{:S(2)}, u32[]{:S(2)}) collective-permute-start(bf16[128,512]{1,0:T(8,128)(2,1)S(1)} %copy-done.41), channel_id=1, source_target_pairs={{15,0},{0,1},{1,2},{2,3},{3,4},{4,5},{5,6},{6,7},{7,8},{8,9},{9,10... | collective-permute-start | bytes 393224 | tf_op jit(solution)/shard_map/ppermute | solution.py:21
  108.0 25.4 %collective-permute-start.21 = (bf16[128,512]{1,0:T(8,128)(2,1)S(1)}, bf16[128,512]{1,0:T(8,128)(2,1)S(1)}, u32[]{:S(2)}, u32[]{:S(2)}) collective-permute-start(bf16[128,512]{1,0:T(8,128)(2,1)S(1)} %copy-done.39), channel_id=1, source_target_pairs={{2,0},{3,1},{4,2},{5,3},{6,4},{7,5},{8,6},{9,7},{10,8},{11,9},{12,... | collective-permute-start | bytes 393224 | tf_op jit(solution)/shard_map/ppermute | solution.py:21
  119.8 16.3 %collective-permute-start.22 = (bf16[128,512]{1,0:T(8,128)(2,1)S(1)}, bf16[128,512]{1,0:T(8,128)(2,1)S(1)}, u32[]{:S(2)}, u32[]{:S(2)}) collective-permute-start(bf16[128,512]{1,0:T(8,128)(2,1)S(1)} %get-tuple-element.85.refs_16_.refs_14_), channel_id=1, source_target_pairs={{14,0},{15,1},{0,2},{1,3},{2,4},{3,5},{4,6},{5,7},{6,8},{7,9},{8,1... | collective-permute-start | bytes 393224 | tf_op jit(solution)/shard_map/ppermute | solution.py:21
  127.4 12.5 %collective-permute-start.24 = (bf16[4,32,512]{2,1,0:T(8,128)(2,1)S(1)}, bf16[4,32,512]{2,1,0:T(8,128)(2,1)S(1)}, u32[]{:S(2)}, u32[]{:S(2)}) collective-permute-start(bf16[4,32,512]{2,1,0:T(8,128)(2,1)S(1)} %get-tuple-element.108), channel_id=1, source_target_pairs={{0,4},{1,5},{2,6},{3,7},{4,8},{5,9},{6,10},{7,11},{8,12},{9,13},{1... | collective-permute-start | bytes 393224 | tf_op jit(solution)/shard_map/ppermute | solution.py:441
  127.5 13.5 %collective-permute-start.25 = (bf16[4,32,512]{2,1,0:T(8,128)(2,1)S(1)}, bf16[4,32,512]{2,1,0:T(8,128)(2,1)S(1)}, u32[]{:S(2)}, u32[]{:S(2)}) collective-permute-start(bf16[4,32,512]{2,1,0:T(8,128)(2,1)S(1)} %get-tuple-element.109), channel_id=1, source_target_pairs={{0,8},{1,9},{2,10},{3,11},{4,12},{5,13},{6,14},{7,15},{8,0},{9,1},... | collective-permute-start | bytes 393224 | tf_op jit(solution)/shard_map/ppermute | solution.py:441
  133.4 9.2 %collective-permute-start.26 = (bf16[4,32,512]{2,1,0:T(8,128)(2,1)S(1)}, bf16[4,32,512]{2,1,0:T(8,128)(2,1)S(1)}, u32[]{:S(2)}, u32[]{:S(2)}) collective-permute-start(bf16[4,32,512]{2,1,0:T(8,128)(2,1)S(1)} %get-tuple-element.110), channel_id=1, source_target_pairs={{0,12},{1,13},{2,14},{3,15},{4,0},{5,1},{6,2},{7,3},{8,4},{9,5},{1... | collective-permute-start | bytes 393224 | tf_op jit(solution)/shard_map/ppermute | solution.py:441
  139.9 8.7 %collective-permute-start.31 = (bf16[3,32,512]{2,1,0:T(8,128)(2,1)S(1)}, bf16[3,32,512]{2,1,0:T(8,128)(2,1)S(1)}, u32[]{:S(2)}, u32[]{:S(2)}) collective-permute-start(bf16[3,32,512]{2,1,0:T(8,128)(2,1)S(1)} %get-tuple-element.113), channel_id=1, source_target_pairs={{0,4},{1,5},{2,6},{3,7},{4,8},{5,9},{6,10},{7,11},{8,12},{9,13},{1... | collective-permute-start | bytes 294920 | tf_op jit(solution)/shard_map/ppermute | solution.py:441
  142.7 20.2 %collective-permute-start.28 = (bf16[4,32,512]{2,1,0:T(8,128)(2,1)S(1)}, bf16[4,32,512]{2,1,0:T(8,128)(2,1)S(1)}, u32[]{:S(2)}, u32[]{:S(2)}) collective-permute-start(bf16[4,32,512]{2,1,0:T(8,128)(2,1)S(1)} %shard_map.183.refs_5_.refs_1_), channel_id=1, source_target_pairs={{0,4},{1,5},{2,6},{3,7},{4,8},{5,9},{6,10},{7,11},{8,12},{9,13},{1... | collective-permute-start | bytes 393224 | tf_op jit(solution)/shard_map/ppermute | solution.py:441
  145.5 17.4 %collective-permute-start.29 = (bf16[4,32,512]{2,1,0:T(8,128)(2,1)S(1)}, bf16[4,32,512]{2,1,0:T(8,128)(2,1)S(1)}, u32[]{:S(2)}, u32[]{:S(2)}) collective-permute-start(bf16[4,32,512]{2,1,0:T(8,128)(2,1)S(1)} %shard_map.183.refs_5_.refs_1_), channel_id=1, source_target_pairs={{0,8},{1,9},{2,10},{3,11},{4,12},{5,13},{6,14},{7,15},{8,0},{9,1},... | collective-permute-start | bytes 393224 | tf_op jit(solution)/shard_map/ppermute | solution.py:441
  145.5 17.4 %collective-permute-start.30 = (bf16[4,32,512]{2,1,0:T(8,128)(2,1)S(1)}, bf16[4,32,512]{2,1,0:T(8,128)(2,1)S(1)}, u32[]{:S(2)}, u32[]{:S(2)}) collective-permute-start(bf16[4,32,512]{2,1,0:T(8,128)(2,1)S(1)} %shard_map.183.refs_5_.refs_1_), channel_id=1, source_target_pairs={{0,12},{1,13},{2,14},{3,15},{4,0},{5,1},{6,2},{7,3},{8,4},{9,5},{1... | collective-permute-start | bytes 393224 | tf_op jit(solution)/shard_map/ppermute | solution.py:441
  147.9 14.9 %collective-permute-start.32 = (bf16[3,32,512]{2,1,0:T(8,128)(2,1)S(1)}, bf16[3,32,512]{2,1,0:T(8,128)(2,1)S(1)}, u32[]{:S(2)}, u32[]{:S(2)}) collective-permute-start(bf16[3,32,512]{2,1,0:T(8,128)(2,1)S(1)} %get-tuple-element.114), channel_id=1, source_target_pairs={{0,8},{1,9},{2,10},{3,11},{4,12},{5,13},{6,14},{7,15},{8,0},{9,1},... | collective-permute-start | bytes 294920 | tf_op jit(solution)/shard_map/ppermute | solution.py:441
  148.6 14.3 %collective-permute-start.33 = (bf16[3,32,512]{2,1,0:T(8,128)(2,1)S(1)}, bf16[3,32,512]{2,1,0:T(8,128)(2,1)S(1)}, u32[]{:S(2)}, u32[]{:S(2)}) collective-permute-start(bf16[3,32,512]{2,1,0:T(8,128)(2,1)S(1)} %get-tuple-element.115), channel_id=1, source_target_pairs={{0,12},{1,13},{2,14},{3,15},{4,0},{5,1},{6,2},{7,3},{8,4},{9,5},{1... | collective-permute-start | bytes 294920 | tf_op jit(solution)/shard_map/ppermute | solution.py:441
  163.0 14.0 %collective-permute-start.34 = (bf16[4,128,512]{2,1,0:T(8,128)(2,1)S(1)}, bf16[4,128,512]{2,1,0:T(8,128)(2,1)S(1)}, u32[]{:S(2)}, u32[]{:S(2)}) collective-permute-start(bf16[4,128,512]{2,1,0:T(8,128)(2,1)S(1)} %shard_map.185.refs_5_.refs_1_), channel_id=1, source_target_pairs={{0,2},{1,3},{2,0},{3,1},{4,6},{5,7},{6,4},{7,5},{8,10},{9,11},{10,... | collective-permute-start | bytes 1572872 | tf_op jit(solution)/shard_map/ppermute | solution.py:441
  163.1 7.4 %collective-permute-start.37 = (bf16[3,32,512]{2,1,0:T(8,128)(2,1)S(1)}, bf16[3,32,512]{2,1,0:T(8,128)(2,1)S(1)}, u32[]{:S(2)}, u32[]{:S(2)}) collective-permute-start(bf16[3,32,512]{2,1,0:T(8,128)(2,1)S(1)} %shard_map.184.refs_5_.refs_1_), channel_id=1, source_target_pairs={{0,4},{1,5},{2,6},{3,7},{4,8},{5,9},{6,10},{7,11},{8,12},{9,13},{1... | collective-permute-start | bytes 294920 | tf_op jit(solution)/shard_map/ppermute | solution.py:441
  165.7 8.2 %collective-permute-start.38 = (bf16[3,32,512]{2,1,0:T(8,128)(2,1)S(1)}, bf16[3,32,512]{2,1,0:T(8,128)(2,1)S(1)}, u32[]{:S(2)}, u32[]{:S(2)}) collective-permute-start(bf16[3,32,512]{2,1,0:T(8,128)(2,1)S(1)} %shard_map.184.refs_5_.refs_1_), channel_id=1, source_target_pairs={{0,8},{1,9},{2,10},{3,11},{4,12},{5,13},{6,14},{7,15},{8,0},{9,1},... | collective-permute-start | bytes 294920 | tf_op jit(solution)/shard_map/ppermute | solution.py:441
  167.2 6.7 %collective-permute-start.39 = (bf16[3,32,512]{2,1,0:T(8,128)(2,1)S(1)}, bf16[3,32,512]{2,1,0:T(8,128)(2,1)S(1)}, u32[]{:S(2)}, u32[]{:S(2)}) collective-permute-start(bf16[3,32,512]{2,1,0:T(8,128)(2,1)S(1)} %shard_map.184.refs_5_.refs_1_), channel_id=1, source_target_pairs={{0,12},{1,13},{2,14},{3,15},{4,0},{5,1},{6,2},{7,3},{8,4},{9,5},{1... | collective-permute-start | bytes 294920 | tf_op jit(solution)/shard_map/ppermute | solution.py:441
  173.9 11.3 %collective-permute-start.40 = (bf16[3,128,512]{2,1,0:T(8,128)(2,1)S(1)}, bf16[3,128,512]{2,1,0:T(8,128)(2,1)S(1)}, u32[]{:S(2)}, u32[]{:S(2)}) collective-permute-start(bf16[3,128,512]{2,1,0:T(8,128)(2,1)S(1)} %shard_map.186.refs_5_.refs_1_), channel_id=1, source_target_pairs={{0,2},{1,3},{2,0},{3,1},{4,6},{5,7},{6,4},{7,5},{8,10},{9,11},{10,... | collective-permute-start | bytes 1179656 | tf_op jit(solution)/shard_map/ppermute | solution.py:441
  175.9 9.4 %collective-permute-start.35 = (bf16[4,128,512]{2,1,0:T(8,128)(2,1)S(1)}, bf16[4,128,512]{2,1,0:T(8,128)(2,1)S(1)}, u32[]{:S(2)}, u32[]{:S(2)}) collective-permute-start(bf16[4,128,512]{2,1,0:T(8,128)(2,1)S(1)} %shard_map.185.refs_5_.refs_1_), channel_id=1, source_target_pairs={{0,1},{1,0},{2,3},{3,2},{4,5},{5,4},{6,7},{7,6},{8,9},{9,8},{10,11... | collective-permute-start | bytes 1572872 | tf_op jit(solution)/shard_map/ppermute | solution.py:441
  177.0 8.3 %collective-permute-start.36 = (bf16[4,128,512]{2,1,0:T(8,128)(2,1)S(1)}, bf16[4,128,512]{2,1,0:T(8,128)(2,1)S(1)}, u32[]{:S(2)}, u32[]{:S(2)}) collective-permute-start(bf16[4,128,512]{2,1,0:T(8,128)(2,1)S(1)} %collective-permute-done.34.refs_2_), channel_id=1, source_target_pairs={{0,1},{1,0},{2,3},{3,2},{4,5},{5,4},{6,7},{7,6},{8,9},{9,8},{10,11... | collective-permute-start | bytes 1572872 | tf_op jit(solution)/shard_map/ppermute | solution.py:441
  177.0 9.7 %collective-permute-start.41 = (bf16[3,128,512]{2,1,0:T(8,128)(2,1)S(1)}, bf16[3,128,512]{2,1,0:T(8,128)(2,1)S(1)}, u32[]{:S(2)}, u32[]{:S(2)}) collective-permute-start(bf16[3,128,512]{2,1,0:T(8,128)(2,1)S(1)} %shard_map.186.refs_5_.refs_1_), channel_id=1, source_target_pairs={{0,1},{1,0},{2,3},{3,2},{4,5},{5,4},{6,7},{7,6},{8,9},{9,8},{10,11... | collective-permute-start | bytes 1179656 | tf_op jit(solution)/shard_map/ppermute | solution.py:441
  185.2 1.7 collective-permute-start.42
  (78 other events, 356.0 us)

commit v5 on v4

--- a/solution.py
+++ b/solution.py
@@ -12,7 +12,7 @@
 near_sets = 7
 bf16 = jnp.bfloat16
 f32 = jnp.float32
-small, large = 24 * 1024 * 1024, 24 * 1024 * 1024
+vmem_limit = 24 * 1024 * 1024
 
 
 def passed_along(block, axis, distance):
@@ -76,10 +76,11 @@
     return (lax.broadcasted_iota(jnp.int32, (cap, 128), 0) < count).astype(f32)
 
 
-def call(body, outs, scratch, *args, smem=(), after=(), vmem=small):
-    spaces = [
-        pl.BlockSpec(memory_space=pltpu.SMEM if i in smem else pltpu.VMEM) for i in range(len(args))
-    ]
+def call(body, outs, scratch, *args, smem=(), after=(), last=()):
+    spaces, given = [], []
+    for i, arg in enumerate(args):
+        spaces.append(pl.BlockSpec(memory_space=pltpu.SMEM if i in smem else pltpu.VMEM))
+        given.append(arg if i in smem else pltpu.with_memory_space_constraint(arg, pltpu.VMEM))
     spaces += [pl.BlockSpec(memory_space=pl.ANY)] * len(after)
 
     def kernel(*refs):
@@ -87,13 +88,44 @@
 
     return pl.pallas_call(
         kernel,
-        out_shape=[jax.ShapeDtypeStruct(shape, kind) for shape, kind in outs],
+        out_shape=[
+            (pltpu.HBM if i in last else pltpu.VMEM)(shape, kind)
+            for i, (shape, kind) in enumerate(outs)
+        ],
         in_specs=spaces,
         out_specs=[pl.BlockSpec(memory_space=pltpu.VMEM)] * len(outs),
         scratch_shapes=[pltpu.VMEM(shape, kind) for shape, kind in scratch],
-        compiler_params=pltpu.CompilerParams(vmem_limit_bytes=vmem),
+        compiler_params=pltpu.CompilerParams(vmem_limit_bytes=vmem_limit),
         cost_estimate=pl.CostEstimate(flops=1, bytes_accessed=1, transcendentals=0),
-    )(*args, *after)
+    )(*given, *after)
+
+
+def in_hbm(array):
+    return pltpu.with_memory_space_constraint(array, pltpu.HBM)
+
+
+def load_kernel(count, *refs):
+    sems = refs[-1]
+    copies = [
+        pltpu.make_async_copy(refs[i], refs[count + i], sems.at[i]) for i in range(count)
+    ]
+    for copy in copies:
+        copy.start()
+    for copy in copies:
+        copy.wait()
+
+
+def loaded(*args):
+    count = len(args)
+    return pl.pallas_call(
+        functools.partial(load_kernel, count),
+        out_shape=[pltpu.VMEM(arg.shape, arg.dtype) for arg in args],
+        in_specs=[pl.BlockSpec(memory_space=pltpu.HBM)] * count,
+        out_specs=[pl.BlockSpec(memory_space=pltpu.VMEM)] * count,
+        scratch_shapes=[pltpu.SemaphoreType.DMA((count,))],
+        compiler_params=pltpu.CompilerParams(vmem_limit_bytes=1024 * 1024),
+        cost_estimate=pl.CostEstimate(flops=1, bytes_accessed=1, transcendentals=0),
+    )(*[in_hbm(arg) for arg in args])
 
 
 def pick_kernel(plan, *refs):
@@ -106,130 +138,140 @@
             out_ref[i * cap : (i + 1) * cap, :] = dot(hot, node_ref[...]).astype(bf16)
 
 
-def forward_rows(rows, x_ref, w1_ref, w2_ref, live_ref, pre_ref, normed_ref, inv_ref, msg_ref):
-    pre = dot(x_ref[rows, :], w1_ref[...])
-    pre_ref[rows, :] = pre
-    act = (pre * jax.nn.sigmoid(pre)).astype(bf16)
-    normed, inverse = layer_norm(dot(act, w2_ref[...]))
+def forward_rows(pre, live, w2, act_ref, slope_ref, normed_ref, inv_ref, msg_ref, rows):
+    squashed = jax.nn.sigmoid(pre)
+    slope_ref[rows, :] = slope_of(pre, squashed)
+    act = (pre * squashed).astype(bf16)
+    act_ref[rows, :] = act
+    normed, inverse = layer_norm(dot(act, w2))
     normed_ref[rows, :] = normed
     inv_ref[rows, :] = jnp.broadcast_to(inverse, (inverse.shape[0], 128))
-    msg_ref[rows, :] = (live_ref[rows, :1] * normed).astype(bf16)
-    return act
-
-
-def near_kernel(plan, *refs):
-    sets, local_count = plan
-    (edge_ref, recv_ref, send_ref, count_ref, w1_ref, w2_ref, node_ref) = refs[:7]
-    remote = len(sets) - local_count
-    in_refs = refs[7 : 7 + remote]
-    (
-        sx_ref,
-        act_ref,
-        pre_ref,
-        normed_ref,
-        inv_ref,
-        live_ref,
-        sum_ref,
-        x_ref,
-        msg_ref,
-        hot_ref,
-    ) = refs[7 + remote :]
-    nodes, width = node_ref.shape
-    cap = recv_ref.shape[2]
-    for i, k in enumerate(sets):
-        rows = slice(i * cap, (i + 1) * cap)
-        x_ref[rows, :width] = edge_ref[k]
-        if i < local_count:
-            picked = dot(pick_table(send_ref[k], nodes), node_ref[...]).astype(bf16)
-            sx_ref[rows, :] = picked
-        else:
-            picked = in_refs[i - local_count][...]
-        x_ref[rows, width : 2 * width] = picked
-        picked = dot(pick_table(recv_ref[k], nodes), node_ref[...])
-        x_ref[rows, 2 * width :] = picked.astype(bf16)
-        live_ref[rows, :] = live_rows(count_ref[0, k], cap)
-        hot_ref[:, rows] = sum_table(recv_ref[k], nodes)
-    half = len(sets) * cap // 2
-
-    def step(j, carry):
-        rows = pl.ds(pl.multiple_of(j * half, 16), half)
-        act_ref[rows, :] = forward_rows(
-            rows, x_ref, w1_ref, w2_ref, live_ref, pre_ref, normed_ref, inv_ref, msg_ref
-        )
-        return carry
-
-    lax.fori_loop(0, 2, step, 0)
-    sum_ref[...] = dot(hot_ref[...], msg_ref[...])
-
-
-def far_kernel(plan, *refs):
-    sets, pieces = plan
-    count = len(pieces)
+    msg_ref[rows, :] = (live * normed).astype(bf16)
+
+
+def backward_rows(cotan, picked, live, normed, inverse, slope, w2):
+    upstream = live * (cotan.astype(f32) + picked)
+    goe = norm_back(normed, inverse, upstream).astype(bf16)
+    return goe, (dot_rt(goe, w2) * slope).astype(bf16)
+
+
+def stack_into(out_ref, refs):
+    first = 0
+    for ref in refs:
+        out_ref[first : first + ref.shape[0], :] = ref[...]
+        first += ref.shape[0]
+
+
+def start_kernel(plan, *refs):
+    order, local_count = plan
     (
         edge_ref,
-        cotan_ref,
         recv_ref,
+        send_ref,
         count_ref,
         w1_ref,
         w2_ref,
         node_ref,
+        pick_ref,
+        hot_ref,
+        live_ref,
+        part_ref,
+        sx_ref,
+        act_ref,
+        slope_ref,
+        normed_ref,
+        inv_ref,
+        sum_ref,
+        x_ref,
+        msg_ref,
+    ) = refs
+    nodes, width = node_ref.shape
+    cap = recv_ref.shape[2]
+    split = local_count * cap
+    for i, k in enumerate(order):
+        rows = slice(i * cap, (i + 1) * cap)
+        x_ref[rows, :width] = edge_ref[k]
+        pick_ref[rows, :] = pick_table(recv_ref[k], nodes)
+        hot_ref[:, rows] = sum_table(recv_ref[k], nodes)
+        live_ref[rows, :] = live_rows(count_ref[0, k], cap)
+        if i < local_count:
+            sx_ref[rows, :] = dot(pick_table(send_ref[k], nodes), node_ref[...]).astype(bf16)
+    x_ref[:, width:] = dot(pick_ref[...], node_ref[...]).astype(bf16)
+    part = dot(x_ref[:split, :width], w1_ref[:width, :])
+    part += dot(x_ref[:split, width:], w1_ref[2 * width :, :])
+    pre = part + dot(sx_ref[...], w1_ref[width : 2 * width, :])
+    rows = slice(0, split)
+    live = live_ref[rows, :1]
+    forward_rows(pre, live, w2_ref[...], act_ref, slope_ref, normed_ref, inv_ref, msg_ref, rows)
+    sum_ref[...] = dot(hot_ref[:, :split], msg_ref[...])
+    part = dot(x_ref[split:, :width], w1_ref[:width, :])
+    part_ref[...] = part + dot(x_ref[split:, width:], w1_ref[2 * width :, :])
+
+
+def near_kernel(plan, *refs):
+    first, count = plan
+    part_ref, live_ref, hot_ref, sum_in_ref, w1_ref, w2_ref = refs[:6]
+    sx_refs = refs[6 : 6 + count]
+    act_ref, slope_ref, normed_ref, inv_ref, sum_ref, sx_ref, msg_ref = refs[6 + count :]
+    total, width = sx_ref.shape
+    stack_into(sx_ref, sx_refs)
+    for j in range(2):
+        rows = slice(j * total // 2, (j + 1) * total // 2)
+        pre = part_ref[rows, :] + dot(sx_ref[rows, :], w1_ref[width : 2 * width, :])
+        live = live_ref[first + rows.start : first + rows.stop, :1]
+        forward_rows(pre, live, w2_ref[...], act_ref, slope_ref, normed_ref, inv_ref, msg_ref, rows)
+    sum_ref[...] = sum_in_ref[...] + dot(hot_ref[:, first : first + total], msg_ref[...])
+
+
+def far_kernel(plan, *refs):
+    sets, sizes, first, part_first = plan
+    count = len(sizes)
+    (
+        cotan_ref,
+        part_ref,
+        live_ref,
+        pick_ref,
+        hot_ref,
+        sum_ref,
+        w1_ref,
+        w2_ref,
+        node_ref,
         ncot_ref,
-        sum_ref,
         n1_ref,
         n2_ref,
-    ) = refs[:11]
-    sx_refs = refs[11 : 11 + count]
-    gpe_refs = refs[11 + count : 11 + 2 * count]
+    ) = refs[:12]
+    sx_refs, refs = refs[12 : 12 + count], refs[12 + count :]
+    gpe_refs, refs = refs[:count], refs[count:]
     (
         act_ref,
         goe_ref,
-        new_ref,
-        node_new_ref,
+        normed_ref,
         gathered_ref,
         gpn_ref,
         act_node_ref,
         gon_ref,
         gg_ref,
-        x_ref,
-        live_ref,
-        pre_ref,
-        normed_ref,
+        node_new_ref,
+        sx_ref,
+        slope_ref,
         inv_ref,
         msg_ref,
-        hot_ref,
-        pick_ref,
         cot_ref,
-    ) = refs[11 + 2 * count :]
-    nodes, width = node_ref.shape
-    cap = recv_ref.shape[2]
-    total = len(sets) * cap
-    first = 0
-    for sx_ref in sx_refs:
-        x_ref[first : first + sx_ref.shape[0], width : 2 * width] = sx_ref[...]
-        first += sx_ref.shape[0]
+        gpe_ref,
+    ) = refs
+    total, width = sx_ref.shape
+    cap = cotan_ref.shape[1]
+    stack_into(sx_ref, sx_refs)
     for i, k in enumerate(sets):
-        rows = slice(i * cap, (i + 1) * cap)
-        x_ref[rows, :width] = edge_ref[k]
-        cot_ref[rows, :] = cotan_ref[k]
-        hot = pick_table(recv_ref[k], nodes)
-        pick_ref[rows, :] = hot
-        x_ref[rows, 2 * width :] = dot(hot, node_ref[...]).astype(bf16)
-        live_ref[rows, :] = live_rows(count_ref[0, k], cap)
-        hot_ref[:, rows] = sum_table(recv_ref[k], nodes)
-    half = total // 2
-
-    def ahead(j, carry):
-        rows = pl.ds(pl.multiple_of(j * half, 16), half)
-        act = forward_rows(
-            rows, x_ref, w1_ref, w2_ref, live_ref, pre_ref, normed_ref, inv_ref, msg_ref
-        )
-        act_ref[rows, :] = act
-        message = live_ref[rows, :1] * normed_ref[rows, :]
-        new_ref[rows, :] = (x_ref[rows, :width].astype(f32) + message).astype(bf16)
-        return carry
-
-    lax.fori_loop(0, 2, ahead, 0)
-    gathered = (sum_ref[...] + dot(hot_ref[...], msg_ref[...])).astype(bf16)
+        cot_ref[i * cap : (i + 1) * cap, :] = cotan_ref[k]
+    halves = [slice(j * total // 2, (j + 1) * total // 2) for j in range(2)]
+    for rows in halves:
+        pre = part_ref[part_first + rows.start : part_first + rows.stop, :]
+        pre = pre + dot(sx_ref[rows, :], w1_ref[width : 2 * width, :])
+        live = live_ref[first + rows.start : first + rows.stop, :1]
+        forward_rows(pre, live, w2_ref[...], act_ref, slope_ref, normed_ref, inv_ref, msg_ref, rows)
+    gathered = sum_ref[...] + dot(hot_ref[:, first : first + total], msg_ref[...])
+    gathered = gathered.astype(bf16)
     gathered_ref[...] = gathered
 
     pre = dot(node_ref[...], n1_ref[:width, :]) + dot(gathered, n1_ref[width:, :])
@@ -244,49 +286,49 @@
     gpn_ref[...] = gpn
     gg_ref[...] = dot_rt(gpn, n1_ref[width:, :]).astype(bf16)
 
+    for rows in halves:
+        whole = slice(first + rows.start, first + rows.stop)
+        goe, gpe = backward_rows(
+            cot_ref[rows, :],
+            dot(pick_ref[whole, :], gg_ref[...]),
+            live_ref[whole, :1],
+            normed_ref[rows, :],
+            inv_ref[rows, :1],
+            slope_ref[rows, :],
+            w2_ref[...],
+        )
+        goe_ref[rows, :] = goe
+        gpe_ref[rows, :] = gpe
+    at = 0
+    for out_ref, size in zip(gpe_refs, sizes):
+        out_ref[...] = gpe_ref[at : at + size, :]
+        at += size
+
+
+def back_kernel(plan, *refs):
+    sets, local_count = plan
+    cotan_ref, live_ref, pick_ref, gg_ref, w2_ref = refs[:5]
+    groups = (refs[5:8], refs[8:11])
+    goe_ref, local_ref = refs[11:13]
+    gpe_refs, (cot_ref, gpe_ref) = refs[13:-2], refs[-2:]
+    cap = cotan_ref.shape[1]
+    for i, k in enumerate(sets):
+        cot_ref[i * cap : (i + 1) * cap, :] = cotan_ref[k]
     first = 0
-    for gpe_ref in gpe_refs:
-        size = gpe_ref.shape[0]
-        rows = slice(first, first + size)
-        upstream = cot_ref[rows, :].astype(f32) + dot(pick_ref[rows, :], gg_ref[...])
-        upstream = live_ref[rows, :1] * upstream
-        goe = norm_back(normed_ref[rows, :], inv_ref[rows, :1], upstream).astype(bf16)
+    for slope_ref, normed_ref, inv_ref in groups:
+        rows = slice(first, first + slope_ref.shape[0])
+        goe, gpe = backward_rows(
+            cot_ref[rows, :],
+            dot(pick_ref[rows, :], gg_ref[...]),
+            live_ref[rows, :1],
+            normed_ref[...],
+            inv_ref[:, :1],
+            slope_ref[...],
+            w2_ref[...],
+        )
         goe_ref[rows, :] = goe
-        pre = pre_ref[rows, :]
-        slope = slope_of(pre, jax.nn.sigmoid(pre))
-        gpe_ref[...] = (dot_rt(goe, w2_ref[...]) * slope).astype(bf16)
-        first += size
-
-
-def back_kernel(plan, *refs):
-    near, local_count = plan
-    (
-        cotan_ref,
-        recv_ref,
-        w2_ref,
-        live_ref,
-        pre_ref,
-        normed_ref,
-        inv_ref,
-        gg_ref,
-        goe_ref,
-        local_ref,
-    ) = refs[:10]
-    gpe_refs, (gpe_ref, pick_ref) = refs[10:-2], refs[-2:]
-    nodes = gg_ref.shape[0]
-    cap = recv_ref.shape[2]
-    for i, k in enumerate(near):
-        pick_ref[i * cap : (i + 1) * cap, :] = pick_table(recv_ref[k], nodes)
-    half = len(near) * cap // 2
-    for j in range(2):
-        rows = slice(j * half, (j + 1) * half)
-        cot = jnp.concatenate([cotan_ref[k] for k in near])[rows, :].astype(f32)
-        upstream = live_ref[rows, :1] * (cot + dot(pick_ref[rows, :], gg_ref[...]))
-        goe = norm_back(normed_ref[rows, :], inv_ref[rows, :1], upstream).astype(bf16)
-        goe_ref[rows, :] = goe
-        pre = pre_ref[rows, :]
-        slope = slope_of(pre, jax.nn.sigmoid(pre))
-        gpe_ref[rows, :] = (dot_rt(goe, w2_ref[...]) * slope).astype(bf16)
+        gpe_ref[rows, :] = gpe
+        first = rows.stop
     local_ref[...] = gpe_ref[: local_count * cap, :]
     for j, out_ref in enumerate(gpe_refs):
         i = local_count + j
@@ -309,28 +351,18 @@
     sent_ref[index] = other.astype(bf16)
 
 
-def stack_into(out_ref, refs):
-    first = 0
-    for ref in refs:
-        out_ref[first : first + ref.shape[0], :] = ref[...]
-        first += ref.shape[0]
-
-
 def weight_kernel(plan, *refs):
-    order, sx_count, gpe_count, act_count = plan
-    edge_ref, recv_ref, me_ref, node_ref = refs[:4]
+    order, sx_count, gpe_count, act_count, goe_count = plan
+    edge_ref, hot_ref, me_ref, node_ref = refs[:4]
     refs = refs[4:]
     sx_refs, refs = refs[:sx_count], refs[sx_count:]
     gpe_refs, refs = refs[:gpe_count], refs[gpe_count:]
     act_refs, refs = refs[:act_count], refs[act_count:]
-    goe_refs, refs = refs[:act_count], refs[act_count:]
-    keep_ref, sent_ref, rsum_ref, x_ref, sx_ref, gpe_ref, act_ref, goe_ref, hot_ref, block_ref = refs
-    nodes = node_ref.shape[0]
-    cap = recv_ref.shape[2]
+    goe_refs, refs = refs[:goe_count], refs[goe_count:]
+    keep_ref, sent_ref, rsum_ref, x_ref, sx_ref, gpe_ref, act_ref, goe_ref, block_ref = refs
+    cap = edge_ref.shape[1]
     for i, k in enumerate(order):
-        rows = slice(i * cap, (i + 1) * cap)
-        x_ref[rows, :] = edge_ref[k]
-        hot_ref[:, rows] = sum_table(recv_ref[k], nodes)
+        x_ref[i * cap : (i + 1) * cap, :] = edge_ref[k]
     stack_into(sx_ref, sx_refs)
     stack_into(gpe_ref, gpe_refs)
     stack_into(act_ref, act_refs)
@@ -344,29 +376,32 @@
     put(3, act_ref[...], goe_ref[...])
 
 
+def base_kernel(ncot_ref, gpn_ref, rsum_ref, w1_ref, n1_ref, base_ref):
+    width = w1_ref.shape[1]
+    base_ref[...] = (
+        ncot_ref[...].astype(f32)
+        + dot_rt(gpn_ref[...], n1_ref[:width, :])
+        + dot_rt(rsum_ref[...], w1_ref[2 * width :, :])
+    )
+
+
 def edge_kernel(plan, *refs):
-    near, far, gpe_count = plan
-    (edge_ref, cotan_ref, w1_ref, wn_ref, live_ref, normed_ref, new_far_ref, ncot_ref, gpn_ref, rsum_ref) = refs[:10]
-    gpe_refs = refs[10 : 10 + gpe_count]
-    new_ref, gedge_ref, base_ref, gpe_ref = refs[10 + gpe_count :]
+    order, normed_count, gpe_count = plan
+    edge_ref, cotan_ref, w1_ref, live_ref = refs[:4]
+    refs = refs[4:]
+    normed_refs, refs = refs[:normed_count], refs[normed_count:]
+    gpe_refs, refs = refs[:gpe_count], refs[gpe_count:]
+    new_ref, gedge_ref, gpe_ref = refs
     width = w1_ref.shape[1]
     cap = edge_ref.shape[1]
     stack_into(gpe_ref, gpe_refs)
-    base_ref[...] = (
-        ncot_ref[...].astype(f32)
-        + dot_rt(gpn_ref[...], wn_ref[:width, :])
-        + dot_rt(rsum_ref[...], w1_ref[2 * width :, :])
-    )
-    for i, k in enumerate(near + far):
+    places = [(ref, at) for ref in normed_refs for at in range(0, ref.shape[0], cap)]
+    for i, (k, (normed_ref, at)) in enumerate(zip(order, places)):
         rows = slice(i * cap, (i + 1) * cap)
         grad = cotan_ref[k].astype(f32) + dot_rt(gpe_ref[rows, :], w1_ref[:width, :])
         gedge_ref[k] = grad.astype(bf16)
-        if i < len(near):
-            message = live_ref[rows, :1] * normed_ref[rows, :]
-            new_ref[k] = (edge_ref[k].astype(f32) + message).astype(bf16)
-        else:
-            first = (i - len(near)) * cap
-            new_ref[k] = new_far_ref[first : first + cap, :]
+        message = live_ref[rows, :1] * normed_ref[at : at + cap, :]
+        new_ref[k] = (edge_ref[k].astype(f32) + message).astype(bf16)
 
 
 def final_kernel(plan, *refs):
@@ -468,12 +503,14 @@
 def held_until(array, after):
     return pl.pallas_call(
         lambda *refs: None,
-        out_shape=jax.ShapeDtypeStruct(array.shape, array.dtype),
-        in_specs=[pl.BlockSpec(memory_space=pl.ANY)] * (1 + len(after)),
-        out_specs=pl.BlockSpec(memory_space=pl.ANY),
+        out_shape=pltpu.VMEM(array.shape, array.dtype),
+        in_specs=[pl.BlockSpec(memory_space=pltpu.VMEM)]
+        + [pl.BlockSpec(memory_space=pl.ANY)] * len(after),
+        out_specs=pl.BlockSpec(memory_space=pltpu.VMEM),
         input_output_aliases={0: 0},
+        compiler_params=pltpu.CompilerParams(vmem_limit_bytes=1024 * 1024),
         cost_estimate=pl.CostEstimate(flops=1, bytes_accessed=1, transcendentals=0),
-    )(array, *after)
+    )(pltpu.with_memory_space_constraint(array, pltpu.VMEM), *after)
 
 
 def gather_stage(me, piece, stride, members, after):
@@ -503,6 +540,7 @@
         *others,
         smem=(0,),
         after=after,
+        last=range(len(shapes)),
     )
 
 
@@ -533,8 +571,7 @@
     bands = lax.axis_size("band")
     nodes, width = node_latent.shape
     sets, cap = edge_latent.shape[1:3]
-    edges, cotan = edge_latent[0], edge_cotan[0]
-    recv_ids, send_ids = recv_slot.reshape(sets, 1, cap), send_slot.reshape(sets, 1, cap)
+    send_ids = send_slot.reshape(sets, 1, cap)
     me = lax.axis_index("band").astype(jnp.int32).reshape(1)
 
     def step_of(k):
@@ -553,7 +590,32 @@
     far_plan = tuple(tuple(k for k in far if step_of(k) == d) for d in far_steps)
     far = sum(far_plan, ())
 
+    order = near + far
+
     ids = [passed_along(send_ids, "band", -d) for d in steps]
+    (
+        node_latent,
+        send_ids,
+        recv_ids,
+        edges,
+        edge_first,
+        edge_second,
+        node_first,
+        node_second,
+        node_cotan,
+        cotan,
+    ) = loaded(
+        node_latent,
+        send_ids,
+        recv_slot.reshape(sets, 1, cap),
+        edge_latent[0],
+        edge_first,
+        edge_second,
+        node_first,
+        node_second,
+        node_cotan,
+        edge_cotan[0],
+    )
     picked = call(
         functools.partial(pick_kernel, near_plan + far_plan),
         [((len(piece) * cap, width), bf16) for piece in near_plan + far_plan],
@@ -564,132 +626,155 @@
     sx = [passed_along(block, "band", d) for block, d in zip(picked, steps)]
     sx_near, sx_far = sx[: len(near_plan)], sx[len(near_plan) :]
 
-    local_rows, near_rows, far_rows = local_count * cap, len(near) * cap, len(far) * cap
-    sx_local, act_near, pre, normed, inverse, live, part_sum = call(
-        functools.partial(near_kernel, (near, local_count)),
+    local_rows, near_rows, far_rows = local_count * cap, len(near_plan) * cap, len(far) * cap
+    total = sets * cap
+
+    def forward_outs(rows):
+        return [
+            ((rows, width), bf16),
+            ((rows, width), f32),
+            ((rows, width), f32),
+            ((rows, 128), f32),
+            ((nodes, width), f32),
+        ]
+
+    pick, hot, live, part, sx_local, act_local, slope_local, normed_local, inv_local, node_sum = call(
+        functools.partial(start_kernel, (order, local_count)),
         [
+            ((total, nodes), bf16),
+            ((nodes, total), bf16),
+            ((total, 128), f32),
+            ((near_rows + far_rows, width), f32),
             ((local_rows, width), bf16),
-            ((near_rows, width), bf16),
-            ((near_rows, width), f32),
-            ((near_rows, width), f32),
-            ((near_rows, 128), f32),
-            ((near_rows, 128), f32),
-            ((nodes, width), f32),
-        ],
-        [
-            ((near_rows, 3 * width), bf16),
-            ((near_rows, width), bf16),
-            ((nodes, near_rows), bf16),
-        ],
+        ]
+        + forward_outs(local_rows),
+        [((total, 2 * width), bf16), ((local_rows, width), bf16)],
         edges,
         recv_ids,
         send_ids,
-        edge_count,
+        in_hbm(edge_count),
         edge_first,
         edge_second,
         node_latent,
+        smem=(3,),
+        after=[picked[0]],
+    )
+    act_near, slope_near, normed_near, inv_near, node_sum = call(
+        functools.partial(near_kernel, (local_rows, len(near_plan))),
+        forward_outs(near_rows),
+        [((near_rows, width), bf16), ((near_rows, width), bf16)],
+        part,
+        live,
+        hot,
+        node_sum,
+        edge_first,
+        edge_second,
         *sx_near,
-        smem=(3,),
-        vmem=large,
-    )
-
+    )
+    sizes = [len(piece) * cap for piece in far_plan]
     outs = call(
-        functools.partial(far_kernel, (far, far_plan)),
-        [((len(piece) * cap, width), bf16) for piece in far_plan]
-        + [((far_rows, width), bf16)] * 3
+        functools.partial(far_kernel, (far, sizes, local_rows + near_rows, near_rows)),
+        [((size, width), bf16) for size in sizes]
+        + [((far_rows, width), bf16), ((far_rows, width), bf16), ((far_rows, width), f32)]
         + [((nodes, width), bf16)] * 6,
         [
-            ((far_rows, 3 * width), bf16),
-            ((far_rows, 128), f32),
-            ((far_rows, width), f32),
+            ((far_rows, width), bf16),
             ((far_rows, width), f32),
             ((far_rows, 128), f32),
             ((far_rows, width), bf16),
-            ((nodes, far_rows), bf16),
-            ((far_rows, nodes), bf16),
+            ((far_rows, width), bf16),
             ((far_rows, width), bf16),
         ],
-        edges,
         cotan,
-        recv_ids,
-        edge_count,
+        part,
+        live,
+        pick,
+        hot,
+        node_sum,
         edge_first,
         edge_second,
         node_latent,
         node_cotan,
-        part_sum,
         node_first,
         node_second,
         *sx_far,
-        smem=(3,),
-        vmem=large,
+        last=(len(sizes) + 8,),
     )
     gpe_far, outs = list(outs[: len(far_plan)]), outs[len(far_plan) :]
-    act_far, goe_far, new_far, node_new, gathered, gpn, act_node, gon, gg = outs
+    act_far, goe_far, normed_far, gathered, gpn, act_node, gon, gg, node_new = outs
     back_far = [passed_along(block, "band", -d) for block, d in zip(gpe_far, far_steps)]
 
     half = (width // 2, width)
     outs = call(
         functools.partial(back_kernel, (near, local_count)),
-        [((near_rows, width), bf16), ((local_rows, width), bf16)]
+        [((local_rows + near_rows, width), bf16), ((local_rows, width), bf16)]
         + [((cap, width), bf16)] * len(near_steps),
-        [((near_rows, width), bf16), ((near_rows, nodes), bf16)],
+        [((local_rows + near_rows, width), bf16)] * 2,
         cotan,
-        recv_ids,
+        live,
+        pick,
+        gg,
         edge_second,
-        live,
-        pre,
-        normed,
-        inverse,
-        gg,
+        slope_local,
+        normed_local,
+        inv_local,
+        slope_near,
+        normed_near,
+        inv_near,
     )
     goe_near, gpe_local = outs[:2]
     gpe_near = list(outs[2:])
     back_near = [passed_along(block, "band", -d) for block, d in zip(gpe_near, near_steps)]
 
-    order = near + far
     gpe = [gpe_local] + gpe_near + gpe_far
     sx_all = [sx_local] + sx_near + sx_far
-    total = sets * cap
     keep_edge, sent_edge, recv_sum = call(
-        functools.partial(weight_kernel, (order, len(sx_all), len(gpe), 2)),
+        functools.partial(weight_kernel, (order, len(sx_all), len(gpe), 3, 2)),
         [((4, *half), f32), ((4, *half), bf16), ((nodes, width), bf16)],
-        [((total, width), bf16)] * 5 + [((nodes, total), bf16), ((width, width), f32)],
+        [((total, width), bf16)] * 5 + [((width, width), f32)],
         edges,
-        recv_ids,
+        hot,
         me,
         node_latent,
         *sx_all,
         *gpe,
+        act_local,
         act_near,
         act_far,
         goe_near,
         goe_far,
         smem=(2,),
-        vmem=large,
     )
 
     def edge_outputs(after):
         return call(
-            functools.partial(edge_kernel, (near, far, len(gpe))),
-            [((sets, cap, width), bf16), ((sets, cap, width), bf16), ((nodes, width), f32)],
+            functools.partial(edge_kernel, (order, 3, len(gpe))),
+            [((sets, cap, width), bf16), ((sets, cap, width), bf16)],
             [((total, width), bf16)],
             edges,
             cotan,
             edge_first,
-            node_first,
             live,
-            normed,
-            new_far,
+            normed_local,
+            normed_near,
+            normed_far,
+            *gpe,
+            after=after,
+            last=(0, 1),
+        )
+
+    def node_output(after):
+        (base,) = call(
+            base_kernel,
+            [((nodes, width), f32)],
+            [],
             node_cotan,
             gpn,
             recv_sum,
-            *gpe,
+            edge_first,
+            node_first,
             after=after,
-            vmem=large,
         )
-
-    def node_output(base, after):
         (grad_nodes,) = call(
             functools.partial(final_kernel, (near[:local_count],) + near_plan + far_plan),
             [((nodes, width), bf16)],
@@ -701,8 +786,7 @@
             gpe_local,
             *back_near,
             *back_far,
-            after=after,
-            vmem=large,
+            last=(0,),
         )
         return grad_nodes
 
@@ -733,23 +817,23 @@
         came_node = [in_group(sent_node, "band", 1, 2, 1)]
         keep_edge, came_edge = add_stage(me, keep_edge, came_edge, *along_y, f32, [keep_node])
         keep_node, came_node = add_stage(me, keep_node, came_node, *along_y, f32, [keep_edge])
-        edge_new, grad_edges, base = edge_outputs([keep_node])
-        keep_edge, came_edge = add_stage(me, keep_edge, came_edge, *along_z, f32, [base])
-        grad_nodes = node_output(base, [keep_edge])
-        keep_node, came_node = add_stage(me, keep_node, came_node, *along_z, f32, [grad_nodes])
+        edge_new, grad_edges = edge_outputs([keep_node])
+        keep_edge, came_edge = add_stage(me, keep_edge, came_edge, *along_z, f32, [in_hbm(edge_new)])
+        grad_nodes = node_output([keep_edge])
+        keep_node, came_node = add_stage(me, keep_node, came_node, *along_z, f32, [in_hbm(grad_nodes)])
         piece_edge, _ = add_stage(me, keep_edge, came_edge, 1, 1, bf16, [keep_node])
         piece_node, _ = add_stage(me, keep_node, came_node, 1, 1, bf16, [piece_edge])
         mine_edge = gather_stage(me, piece_edge, *along_z, [piece_node])
         mine_node = gather_stage(me, piece_node, *along_z, [mine_edge])
         grad_e1, grad_e2 = join_stage(me, mine_edge, first, edge_blocks, edge_shapes, [mine_node])
-        grad_n1, grad_n2 = join_stage(me, mine_node, first, node_blocks, node_shapes, [grad_e2])
+        grad_n1, grad_n2 = join_stage(me, mine_node, first, node_blocks, node_shapes, [in_hbm(grad_e2)])
     else:
         whole = reduce_whole(*node_weights([]))
         grad_n1, grad_n2 = whole[:2].reshape(2 * width, width), whole[2]
         whole = reduce_whole(keep_edge, sent_edge)
         grad_e1, grad_e2 = whole[:3].reshape(3 * width, width), whole[3]
-        edge_new, grad_edges, base = edge_outputs([])
-        grad_nodes = node_output(base, [])
+        edge_new, grad_edges = edge_outputs([])
+        grad_nodes = node_output([])
     return (
         node_new,
         edge_new[None],

time: 190 us -> 171 us (0.900)
  local copies, waits for them, and re-layouts: 38.1 us -> 23.7 us
  waiting for transfers between devices: 58.3 us -> 51.8 us
    unnamed x166 -> x156, local copies, waits for them, and re-layouts: 38.1 us -> 23.7 us
    ppermute x21, waiting for transfers between devices: 17 us -> 12.4 us  [passed_along(): return lax.ppermute(block, axis, route)]
    pallas_call x19 -> x22, Pallas kernels: 32.6 us -> 34.5 us  [the longest x20 31.2 us: call(): pl.pallas_call(kernel, out_shape=[(pltpu.HBM if i in last else pltpu.VMEM...]
  transfers between devices with their start and end apart: 43 -> 43, of which waited for: 18 -> 16; matrix products, arithmetic and copies ran while one was open for 0% -> 0% of each run, Pallas kernels for 12% -> 16%
where the time goes in v5:
time: 171 us
  starting transfers between devices  59.1 us (35%)
  waiting for transfers between devices  51.8 us (30%)
  Pallas kernels  34.5 us (20%)
  local copies, waits for them, and re-layouts  23.7 us (14%)
    ppermute x22, waiting for transfers between devices, in_group(): return lax.ppermute(block, axis, route)  39.4 us
    ppermute x21, starting transfers between devices, passed_along(): return lax.ppermute(block, axis, route)  33.5 us
    pallas_call x20, Pallas kernels, call(): pl.pallas_call(kernel, out_shape=[(pltpu.HBM if i in last else pltpu.VMEM...  31.2 us
    ppermute x22, starting transfers between devices, in_group(): return lax.ppermute(block, axis, route)  25.6 us
    unnamed x156, local copies, waits for them, and re-layouts  23.7 us
    ppermute x21, waiting for transfers between devices, passed_along(): return lax.ppermute(block, axis, route)  12.4 us
  transfers between devices with their start and end apart: 43, of which 16 were waited for; matrix products, arithmetic and copies ran while one was open for 0% of the time, Pallas kernels for 16%

profile of v5, /device:TPU:0, one launch (start us, length us, event | category | flops | bytes accessed | tf_op | source)
XLA Modules:
  0.0 170.7 jit_solution(5211382888297743421)
XLA Ops:
  0.6 5.5 %collective-permute-start = (s32[11,1,128]{2,1,0:T(1,128)}, s32[11,1,128]{2,1,0:T(1,128)S(1)}, u32[]{:S(2)}, u32[]{:S(2)}) collective-permute-start(s32[11,1,128]{2,1,0:T(1,128)} %bitcast.11), channel_id=1, source_target_pairs={{1,0},{2,1},{3,2},{4,3},{5,4},{6,5},{7,6},{8,7},{9,8},{10,9},{11,1... | collective-permute-start | bytes 16904 | tf_op jit(solution)/shard_map/ppermute | solution.py:21
  6.1 1.1 collective-permute-start.2
  8.6 1.6 collective-permute-start.5
  10.2 1.9 %collective-permute-done.1.refs_2_.refs_4_ = s32[11,1,128]{2,1,0:T(1,128)S(1)} collective-permute-done((s32[11,1,128]{2,1,0:T(1,128)}, s32[11,1,128]{2,1,0:T(1,128)S(1)}, u32[]{:S(2)}, u32[]{:S(2)}) %collective-permute-start.1) | collective-permute-done | bytes 5664 | tf_op jit(solution)/shard_map/ppermute | solution.py:21
  12.1 3.2 %shard_map.170 = (bf16[320,512]{1,0:T(8,128)(2,1)S(1)}, s32[11,1,128]{2,1,0:T(1,128)S(1)}, s32[11,1,128]{2,1,0:T(1,128)S(1)}, bf16[11,128,512]{2,1,0:T(8,128)(2,...) custom-call(bf16[320,512]{1,0:T(8,128)(2,1)} %refs_0_.1, ...), custom_call_target="tpu_custom_call" | custom-call | flops 1 | bytes 1 | tf_op jit(solution)/shard_map/pallas_call | solution.py:120
  15.4 1.4 collective-permute-done.6.refs_7_.refs_9_
  20.5 5.2 %collective-permute-start.10 = (bf16[128,512]{1,0:T(8,128)(2,1)S(1)}, bf16[128,512]{1,0:T(8,128)(2,1)S(1)}, u32[]{:S(2)}, u32[]{:S(2)}) collective-permute-start(bf16[128,512]{1,0:T(8,128)(2,1)S(1)} %get-tuple-element.96), channel_id=1, source_target_pairs={{2,0},{3,1},{4,2},{5,3},{6,4},{7,5},{8,6},{9,7},{10,8},{11,9},{12,... | collective-permute-start | bytes 393224 | tf_op jit(solution)/shard_map/ppermute | solution.py:21
  25.7 1.7 collective-permute-start.13
  28.5 1.2 collective-permute-done.10.refs_9_.refs_8_
  29.6 2.7 %collective-permute-start.12 = (bf16[128,512]{1,0:T(8,128)(2,1)S(1)}, bf16[128,512]{1,0:T(8,128)(2,1)S(1)}, u32[]{:S(2)}, u32[]{:S(2)}) collective-permute-start(bf16[128,512]{1,0:T(8,128)(2,1)S(1)} %get-tuple-element.102), channel_id=1, source_target_pairs={{4,0},{5,1},{6,2},{7,3},{8,4},{9,5},{10,6},{11,7},{12,8},{13,9},{1... | collective-permute-start | bytes 393224 | tf_op jit(solution)/shard_map/ppermute | solution.py:21
  32.3 4.5 %shard_map.172 = (bf16[1408,320]{1,0:T(8,128)(2,1)S(1)}, bf16[320,1408]{1,0:T(8,128)(2,1)S(1)}, f32[1408,128]{1,0:T(8,128)S(1)}, f32[1024,512]{1,0:T(8,128)S(1)}...) custom-call(bf16[11,128,512]{2,1,0:T(8,128)(2,1)S(1)} %get-tuple-ele, ...), custom_call_target="tpu_custom_call" | custom-call | flops 1 | bytes 1 | tf_op jit(solution)/shard_map/pallas_call | solution.py:89
  38.7 1.6 shard_map.173
  41.0 5.2 %collective-permute-done.12.refs_13_.refs_10_ = bf16[128,512]{1,0:T(8,128)(2,1)S(1)} collective-permute-done((bf16[128,512]{1,0:T(8,128)(2,1)S(1)}, bf16[128,512]{1,0:T(8,128)(2,1)S(1)}, u32[]{:S(2)}, u32[]{:S(2)}) %collective-permute-start.12) | collective-permute-done | bytes 131104 | tf_op jit(solution)/shard_map/ppermute | solution.py:21
  46.3 4.7 %shard_map.174 = (bf16[128,512]{1,0:T(8,128)(2,1)}, bf16[128,512]{1,0:T(8,128)(2,1)}, bf16[256,512]{1,0:T(8,128)(2,1)}, bf16[512,512]{1,0:T(8,128)(2,1)S(1)}, bf...) custom-call(bf16[11,128,512]{2,1,0:T(8,128)(2,1)S(1)} %get-tuple-ele, ...), custom_call_target="tpu_custom_call" | custom-call | flops 1 | bytes 1 | tf_op jit(solution)/shard_map/pallas_call | solution.py:89
  57.2 3.5 %collective-permute-start.16 = (bf16[256,512]{1,0:T(8,128)(2,1)}, bf16[256,512]{1,0:T(8,128)(2,1)}, u32[]{:S(2)}, u32[]{:S(2)}) collective-permute-start(bf16[256,512]{1,0:T(8,128)(2,1)} %get-tuple-element.120.refs_19_.refs_14_), channel_id=1, source_target_pairs={{8,0},{9,1},{10,2},{11,3},{12,4},{13,5},{14,6},{15,7},{0,8},{1,9},... | collective-permute-start | bytes 786440 | tf_op jit(solution)/shard_map/ppermute | solution.py:21
  60.8 2.3 %collective-permute-start.14 = (bf16[128,512]{1,0:T(8,128)(2,1)}, bf16[128,512]{1,0:T(8,128)(2,1)}, u32[]{:S(2)}, u32[]{:S(2)}) collective-permute-start(bf16[128,512]{1,0:T(8,128)(2,1)} %get-tuple-element.118.refs_17_.refs_12_), channel_id=1, source_target_pairs={{4,0},{5,1},{6,2},{7,3},{8,4},{9,5},{10,6},{11,7},{12,8},{13,9},{1... | collective-permute-start | bytes 393224 | tf_op jit(solution)/shard_map/ppermute | solution.py:21
  63.0 1.4 copy-done.1
  64.4 1.1 copy-done.4
  65.5 1.2 copy-done.11
  66.7 1.2 copy-done.15
  68.0 1.1 copy-done.18
  69.1 1.2 copy-done.29
  70.3 1.1 copy-done.31
  74.4 2.1 %shard_map.175 = (bf16[896,512]{1,0:T(8,128)(2,1)S(1)}, bf16[384,512]{1,0:T(8,128)(2,1)S(1)}, bf16[128,512]{1,0:T(8,128)(2,1)S(1)}, bf16[128,512]{1,0:T(8,128)(2...) custom-call(bf16[11,128,512]{2,1,0:T(8,128)(2,1)S(1)} %copy-done.1, f32[1408,128]{1,0:T(8,128)S(1)} %copy-done.4, ...), custom_call_target="tpu_custom_call" | custom-call | flops 1 | bytes 1 | tf_op jit(solution)/shard_map/pallas_call | solution.py:89
  76.6 5.0 %shard_map.176 = (f32[4,256,512]{2,1,0:T(8,128)S(1)}, bf16[4,256,512]{2,1,0:T(8,128)(2,1)S(1)}, bf16[320,512]{1,0:T(8,128)(2,1)S(1)}) custom-call(bf16[11,128,512]{2,1,0:T(8,128)(2,1)S(1)} %get-tuple-element.82.refs_0_, bf16[320,1408]{1,0:T(8,128)(2,1)S(1)} %copy-done.9, s32[1]{0:T(128)} %bitcast.4.refs_2_.refs_0_, bf16[320,512]{1,0:T(8,128)(2,1)S(1)} %copy-done.7, ...), custom_call_target="tpu_custom_call" | custom-call | flops 1 | bytes 1 | tf_op jit(solution)/shard_map/pallas_call | solution.py:89
  82.9 1.3 shard_map.178
  87.5 4.0 %collective-permute-start.20 = (bf16[128,512]{1,0:T(8,128)(2,1)S(1)}, bf16[128,512]{1,0:T(8,128)(2,1)S(1)}, u32[]{:S(2)}, u32[]{:S(2)}) collective-permute-start(bf16[128,512]{1,0:T(8,128)(2,1)S(1)} %get-tuple-element.114.refs_13_.refs_8_), channel_id=1, source_target_pairs={{1,0},{2,1},{3,2},{4,3},{5,4},{6,5},{7,6},{8,7},{9,8},{10,9},{11,1... | collective-permute-start | bytes 393224 | tf_op jit(solution)/shard_map/ppermute | solution.py:21
  92.6 9.5 %collective-permute-done.19.refs_2_ = bf16[4,128,512]{2,1,0:T(8,128)(2,1)S(1)} collective-permute-done((bf16[4,128,512]{2,1,0:T(8,128)(2,1)S(1)}, bf16[4,128,512]{2,1,0:T(8,128)(2,1)S(1)}, u32[]{:S(2)}, u32[]{:S(2)}) %collective-permute-start.19) | collective-permute-done | bytes 524320 | tf_op jit(solution)/shard_map/ppermute | solution.py:476
  102.1 2.5 %collective-permute-start.23 = (bf16[128,512]{1,0:T(8,128)(2,1)S(1)}, bf16[128,512]{1,0:T(8,128)(2,1)S(1)}, u32[]{:S(2)}, u32[]{:S(2)}) collective-permute-start(bf16[128,512]{1,0:T(8,128)(2,1)S(1)} %get-tuple-element.117.refs_16_.refs_11_), channel_id=1, source_target_pairs={{14,0},{15,1},{0,2},{1,3},{2,4},{3,5},{4,6},{5,7},{6,8},{7,9},{8,1... | collective-permute-start | bytes 393224 | tf_op jit(solution)/shard_map/ppermute | solution.py:21
  104.6 4.7 %shard_map.181 = (bf16[11,128,512]{2,1,0:T(8,128)(2,1)}, bf16[11,128,512]{2,1,0:T(8,128)(2,1)}) custom-call(bf16[11,128,512]{2,1,0:T(8,128)(2,1)S(1)} %get-tuple-element.82.refs_0_, bf16[11,128,512]{2,1,0:T(8,128)(2,1)S(1)} %copy-done.2, bf16[1536,512]{1,0:T(8,128)(2,1)S(1)} %get-tuple-element.85.refs_4_.refs_6_.refs_2_.refs_3_.refs_1_, ...), custom_call_target="tpu_custom_call" | custom-call | flops 1 | bytes 1 | tf_op jit(solution)/shard_map/pallas_call | solution.py:89
  109.6 4.1 %collective-permute-start.25 = (bf16[4,32,512]{2,1,0:T(8,128)(2,1)S(1)}, bf16[4,32,512]{2,1,0:T(8,128)(2,1)S(1)}, u32[]{:S(2)}, u32[]{:S(2)}) collective-permute-start(bf16[4,32,512]{2,1,0:T(8,128)(2,1)S(1)} %get-tuple-element.143), channel_id=1, source_target_pairs={{0,8},{1,9},{2,10},{3,11},{4,12},{5,13},{6,14},{7,15},{8,0},{9,1},... | collective-permute-start | bytes 393224 | tf_op jit(solution)/shard_map/ppermute | solution.py:476
  113.6 2.1 %collective-permute-done.22.refs_13_ = bf16[128,512]{1,0:T(8,128)(2,1)S(1)} collective-permute-done((bf16[128,512]{1,0:T(8,128)(2,1)S(1)}, bf16[128,512]{1,0:T(8,128)(2,1)S(1)}, u32[]{:S(2)}, u32[]{:S(2)}) %collective-permute-start.22) | collective-permute-done | bytes 131104 | tf_op jit(solution)/shard_map/ppermute | solution.py:21
  115.8 3.8 %collective-permute-start.26 = (bf16[4,32,512]{2,1,0:T(8,128)(2,1)S(1)}, bf16[4,32,512]{2,1,0:T(8,128)(2,1)S(1)}, u32[]{:S(2)}, u32[]{:S(2)}) collective-permute-start(bf16[4,32,512]{2,1,0:T(8,128)(2,1)S(1)} %get-tuple-element.144), channel_id=1, source_target_pairs={{0,12},{1,13},{2,14},{3,15},{4,0},{5,1},{6,2},{7,3},{8,4},{9,5},{1... | collective-permute-start | bytes 393224 | tf_op jit(solution)/shard_map/ppermute | solution.py:476
  120.4 2.7 %shard_map.184.refs_3_ = bf16[320,512]{1,0:T(8,128)(2,1)} custom-call(f32[320,512]{1,0:T(8,128)S(1)} %shard_map.183.refs_0_, bf16[1536,512]{1,0:T(8,128)(2,1)S(1)} %get-tuple-element.85.refs_4_.refs_6_.refs_2_.refs_3_.refs_1_, s32[11,1,128]{2,1,0:T(1,128)S(1)} %get-tuple-element.84.refs_2_, s32[11,1,128]{2,1,0:T(1,128)S(1)} %collective-permute-done.refs_1_.refs_3_, ...), custom_call_target="tpu_custom_call" | custom-call | flops 1 | bytes 1 | tf_op jit(solution)/shard_map/pallas_call | solution.py:89
  123.2 1.1 collective-permute-done.26.refs_4_
  125.2 2.9 %collective-permute-start.29 = (bf16[4,32,512]{2,1,0:T(8,128)(2,1)S(1)}, bf16[4,32,512]{2,1,0:T(8,128)(2,1)S(1)}, u32[]{:S(2)}, u32[]{:S(2)}) collective-permute-start(bf16[4,32,512]{2,1,0:T(8,128)(2,1)S(1)} %shard_map.186.refs_5_.refs_1_), channel_id=1, source_target_pairs={{0,8},{1,9},{2,10},{3,11},{4,12},{5,13},{6,14},{7,15},{8,0},{9,1},... | collective-permute-start | bytes 393224 | tf_op jit(solution)/shard_map/ppermute | solution.py:476
  128.3 2.0 %collective-permute-start.32 = (bf16[3,32,512]{2,1,0:T(8,128)(2,1)S(1)}, bf16[3,32,512]{2,1,0:T(8,128)(2,1)S(1)}, u32[]{:S(2)}, u32[]{:S(2)}) collective-permute-start(bf16[3,32,512]{2,1,0:T(8,128)(2,1)S(1)} %get-tuple-element.148), channel_id=1, source_target_pairs={{0,8},{1,9},{2,10},{3,11},{4,12},{5,13},{6,14},{7,15},{8,0},{9,1},... | collective-permute-start | bytes 294920 | tf_op jit(solution)/shard_map/ppermute | solution.py:476
  130.3 2.2 %collective-permute-start.33 = (bf16[3,32,512]{2,1,0:T(8,128)(2,1)S(1)}, bf16[3,32,512]{2,1,0:T(8,128)(2,1)S(1)}, u32[]{:S(2)}, u32[]{:S(2)}) collective-permute-start(bf16[3,32,512]{2,1,0:T(8,128)(2,1)S(1)} %get-tuple-element.149), channel_id=1, source_target_pairs={{0,12},{1,13},{2,14},{3,15},{4,0},{5,1},{6,2},{7,3},{8,4},{9,5},{1... | collective-permute-start | bytes 294920 | tf_op jit(solution)/shard_map/ppermute | solution.py:476
  132.5 12.6 %collective-permute-done.32.refs_3_ = bf16[3,32,512]{2,1,0:T(8,128)(2,1)S(1)} collective-permute-done((bf16[3,32,512]{2,1,0:T(8,128)(2,1)S(1)}, bf16[3,32,512]{2,1,0:T(8,128)(2,1)S(1)}, u32[]{:S(2)}, u32[]{:S(2)}) %collective-permute-start.32) | collective-permute-done | bytes 98336 | tf_op jit(solution)/shard_map/ppermute | solution.py:476
  145.3 2.7 %collective-permute-start.37 = (bf16[3,32,512]{2,1,0:T(8,128)(2,1)S(1)}, bf16[3,32,512]{2,1,0:T(8,128)(2,1)S(1)}, u32[]{:S(2)}, u32[]{:S(2)}) collective-permute-start(bf16[3,32,512]{2,1,0:T(8,128)(2,1)S(1)} %shard_map.187.refs_5_.refs_1_), channel_id=1, source_target_pairs={{0,4},{1,5},{2,6},{3,7},{4,8},{5,9},{6,10},{7,11},{8,12},{9,13},{1... | collective-permute-start | bytes 294920 | tf_op jit(solution)/shard_map/ppermute | solution.py:476
  148.2 2.3 %collective-permute-start.39 = (bf16[3,32,512]{2,1,0:T(8,128)(2,1)S(1)}, bf16[3,32,512]{2,1,0:T(8,128)(2,1)S(1)}, u32[]{:S(2)}, u32[]{:S(2)}) collective-permute-start(bf16[3,32,512]{2,1,0:T(8,128)(2,1)S(1)} %shard_map.187.refs_5_.refs_1_), channel_id=1, source_target_pairs={{0,12},{1,13},{2,14},{3,15},{4,0},{5,1},{6,2},{7,3},{8,4},{9,5},{1... | collective-permute-start | bytes 294920 | tf_op jit(solution)/shard_map/ppermute | solution.py:476
  150.5 2.4 %collective-permute-done.37.refs_2_ = bf16[3,32,512]{2,1,0:T(8,128)(2,1)S(1)} collective-permute-done((bf16[3,32,512]{2,1,0:T(8,128)(2,1)S(1)}, bf16[3,32,512]{2,1,0:T(8,128)(2,1)S(1)}, u32[]{:S(2)}, u32[]{:S(2)}) %collective-permute-start.37) | collective-permute-done | bytes 98336 | tf_op jit(solution)/shard_map/ppermute | solution.py:476
  152.9 3.4 %collective-permute-done.38.refs_3_ = bf16[3,32,512]{2,1,0:T(8,128)(2,1)S(1)} collective-permute-done((bf16[3,32,512]{2,1,0:T(8,128)(2,1)S(1)}, bf16[3,32,512]{2,1,0:T(8,128)(2,1)S(1)}, u32[]{:S(2)}, u32[]{:S(2)}) %collective-permute-start.38) | collective-permute-done | bytes 98336 | tf_op jit(solution)/shard_map/ppermute | solution.py:476
  156.3 1.8 %collective-permute-start.40 = (bf16[3,128,512]{2,1,0:T(8,128)(2,1)S(1)}, bf16[3,128,512]{2,1,0:T(8,128)(2,1)S(1)}, u32[]{:S(2)}, u32[]{:S(2)}) collective-permute-start(bf16[3,128,512]{2,1,0:T(8,128)(2,1)S(1)} %shard_map.189.refs_5_.refs_1_), channel_id=1, source_target_pairs={{0,2},{1,3},{2,0},{3,1},{4,6},{5,7},{6,4},{7,5},{8,10},{9,11},{10,... | collective-permute-start | bytes 1179656 | tf_op jit(solution)/shard_map/ppermute | solution.py:476
  158.2 1.3 collective-permute-done.34.refs_2_
  160.0 7.7 %collective-permute-done.40.refs_2_ = bf16[3,128,512]{2,1,0:T(8,128)(2,1)S(1)} collective-permute-done((bf16[3,128,512]{2,1,0:T(8,128)(2,1)S(1)}, bf16[3,128,512]{2,1,0:T(8,128)(2,1)S(1)}, u32[]{:S(2)}, u32[]{:S(2)}) %collective-permute-start.40) | collective-permute-done | bytes 393248 | tf_op jit(solution)/shard_map/ppermute | solution.py:476
  167.7 1.5 shard_map.190
  169.4 1.3 shard_map.191
  (216 shorter events, 26.6 us)
Async XLA Ops:
  0.6 8.0 %collective-permute-start = (s32[11,1,128]{2,1,0:T(1,128)}, s32[11,1,128]{2,1,0:T(1,128)S(1)}, u32[]{:S(2)}, u32[]{:S(2)}) collective-permute-start(s32[11,1,128]{2,1,0:T(1,128)} %bitcast.11), channel_id=1, source_target_pairs={{1,0},{2,1},{3,2},{4,3},{5,4},{6,5},{7,6},{8,7},{9,8},{10,9},{11,1... | collective-permute-start | bytes 16904 | tf_op jit(solution)/shard_map/ppermute | solution.py:21
  6.1 6.0 %collective-permute-start.1 = (s32[11,1,128]{2,1,0:T(1,128)}, s32[11,1,128]{2,1,0:T(1,128)S(1)}, u32[]{:S(2)}, u32[]{:S(2)}) collective-permute-start(s32[11,1,128]{2,1,0:T(1,128)} %bitcast.12), channel_id=1, source_target_pairs={{15,0},{0,1},{1,2},{2,3},{3,4},{4,5},{5,6},{6,7},{7,8},{8,9},{9,10... | collective-permute-start | bytes 16904 | tf_op jit(solution)/shard_map/ppermute | solution.py:21
  6.1 9.2 %collective-permute-start.2 = (s32[11,1,128]{2,1,0:T(1,128)}, s32[11,1,128]{2,1,0:T(1,128)S(1)}, u32[]{:S(2)}, u32[]{:S(2)}) collective-permute-start(s32[11,1,128]{2,1,0:T(1,128)} %bitcast.13), channel_id=1, source_target_pairs={{2,0},{3,1},{4,2},{5,3},{6,4},{7,5},{8,6},{9,7},{10,8},{11,9},{12,... | collective-permute-start | bytes 16904 | tf_op jit(solution)/shard_map/ppermute | solution.py:21
  7.2 8.2 %collective-permute-start.3 = (s32[11,1,128]{2,1,0:T(1,128)}, s32[11,1,128]{2,1,0:T(1,128)S(1)}, u32[]{:S(2)}, u32[]{:S(2)}) collective-permute-start(s32[11,1,128]{2,1,0:T(1,128)} %bitcast.14), channel_id=1, source_target_pairs={{14,0},{15,1},{0,2},{1,3},{2,4},{3,5},{4,6},{5,7},{6,8},{7,9},{8,1... | collective-permute-start | bytes 16904 | tf_op jit(solution)/shard_map/ppermute | solution.py:21
  8.2 7.2 %collective-permute-start.4 = (s32[11,1,128]{2,1,0:T(1,128)}, s32[11,1,128]{2,1,0:T(1,128)S(1)}, u32[]{:S(2)}, u32[]{:S(2)}) collective-permute-start(s32[11,1,128]{2,1,0:T(1,128)} %bitcast.15), channel_id=1, source_target_pairs={{4,0},{5,1},{6,2},{7,3},{8,4},{9,5},{10,6},{11,7},{12,8},{13,9},{1... | collective-permute-start | bytes 16904 | tf_op jit(solution)/shard_map/ppermute | solution.py:21
  8.6 6.8 %collective-permute-start.5 = (s32[11,1,128]{2,1,0:T(1,128)}, s32[11,1,128]{2,1,0:T(1,128)S(1)}, u32[]{:S(2)}, u32[]{:S(2)}) collective-permute-start(s32[11,1,128]{2,1,0:T(1,128)} %bitcast.16), channel_id=1, source_target_pairs={{12,0},{13,1},{14,2},{15,3},{0,4},{1,5},{2,6},{3,7},{4,8},{5,9},{6... | collective-permute-start | bytes 16904 | tf_op jit(solution)/shard_map/ppermute | solution.py:21
  12.1 4.7 %collective-permute-start.6 = (s32[11,1,128]{2,1,0:T(1,128)}, s32[11,1,128]{2,1,0:T(1,128)S(1)}, u32[]{:S(2)}, u32[]{:S(2)}) collective-permute-start(s32[11,1,128]{2,1,0:T(1,128)} %bitcast.17), channel_id=1, source_target_pairs={{8,0},{9,1},{10,2},{11,3},{12,4},{13,5},{14,6},{15,7},{0,8},{1,9},... | collective-permute-start | bytes 16904 | tf_op jit(solution)/shard_map/ppermute | solution.py:21
  15.3 30.9 %copy-start = (bf16[11,128,512]{2,1,0:T(8,128)(2,1)}, bf16[11,128,512]{2,1,0:T(8,128)(2,1)S(1)}, u32[]{:S(2)}) copy-start(bf16[11,128,512]{2,1,0:T(8,128)(2,1)S(1)} %get-tuple-element.81.refs_0_.refs_1_) | copy-start | bytes 4325380
  15.3 30.9 %copy-start.6 = (bf16[320,512]{1,0:T(8,128)(2,1)}, bf16[320,512]{1,0:T(8,128)(2,1)S(1)}, u32[]{:S(2)}) copy-start(bf16[320,512]{1,0:T(8,128)(2,1)S(1)} %get-tuple-element.87.refs_0_.refs_6_.refs_8_.refs_3_.refs_1_) | copy-start | bytes 983044
  15.4 30.9 %copy-start.12 = (bf16[1024,512]{1,0:T(8,128)(2,1)}, bf16[1024,512]{1,0:T(8,128)(2,1)S(1)}, u32[]{:S(2)}) copy-start(bf16[1024,512]{1,0:T(8,128)(2,1)S(1)} %get-tuple-element.99.refs_10_.refs_4_) | copy-start | bytes 3145732
  15.4 30.9 %copy-start.20 = (bf16[320,512]{1,0:T(8,128)(2,1)}, bf16[320,512]{1,0:T(8,128)(2,1)S(1)}, u32[]{:S(2)}) copy-start(bf16[320,512]{1,0:T(8,128)(2,1)S(1)} %get-tuple-element.98.refs_9_.refs_0_) | copy-start | bytes 983044
  20.5 7.9 %collective-permute-start.7 = (bf16[128,512]{1,0:T(8,128)(2,1)S(1)}, bf16[128,512]{1,0:T(8,128)(2,1)S(1)}, u32[]{:S(2)}, u32[]{:S(2)}) collective-permute-start(bf16[128,512]{1,0:T(8,128)(2,1)S(1)} %get-tuple-element.88.refs_7_), channel_id=1, source_target_pairs={{15,0},{0,1},{1,2},{2,3},{3,4},{4,5},{5,6},{6,7},{7,8},{8,9},{9,10... | collective-permute-start | bytes 393224 | tf_op jit(solution)/shard_map/ppermute | solution.py:21
  20.5 9.1 %collective-permute-start.10 = (bf16[128,512]{1,0:T(8,128)(2,1)S(1)}, bf16[128,512]{1,0:T(8,128)(2,1)S(1)}, u32[]{:S(2)}, u32[]{:S(2)}) collective-permute-start(bf16[128,512]{1,0:T(8,128)(2,1)S(1)} %get-tuple-element.96), channel_id=1, source_target_pairs={{2,0},{3,1},{4,2},{5,3},{6,4},{7,5},{8,6},{9,7},{10,8},{11,9},{12,... | collective-permute-start | bytes 393224 | tf_op jit(solution)/shard_map/ppermute | solution.py:21
  25.7 20.5 %collective-permute-start.13 = (bf16[256,512]{1,0:T(8,128)(2,1)S(1)}, bf16[256,512]{1,0:T(8,128)(2,1)S(1)}, u32[]{:S(2)}, u32[]{:S(2)}) collective-permute-start(bf16[256,512]{1,0:T(8,128)(2,1)S(1)} %get-tuple-element.103), channel_id=1, source_target_pairs={{8,0},{9,1},{10,2},{11,3},{12,4},{13,5},{14,6},{15,7},{0,8},{1,9},... | collective-permute-start | bytes 786440 | tf_op jit(solution)/shard_map/ppermute | solution.py:21
  27.4 11.3 %collective-permute-start.8 = (bf16[128,512]{1,0:T(8,128)(2,1)S(1)}, bf16[128,512]{1,0:T(8,128)(2,1)S(1)}, u32[]{:S(2)}, u32[]{:S(2)}) collective-permute-start(bf16[128,512]{1,0:T(8,128)(2,1)S(1)} %get-tuple-element.94), channel_id=1, source_target_pairs={{1,0},{2,1},{3,2},{4,3},{5,4},{6,5},{7,6},{8,7},{9,8},{10,9},{11,1... | collective-permute-start | bytes 393224 | tf_op jit(solution)/shard_map/ppermute | solution.py:21
  27.6 11.1 %collective-permute-start.9 = (bf16[128,512]{1,0:T(8,128)(2,1)S(1)}, bf16[128,512]{1,0:T(8,128)(2,1)S(1)}, u32[]{:S(2)}, u32[]{:S(2)}) collective-permute-start(bf16[128,512]{1,0:T(8,128)(2,1)S(1)} %get-tuple-element.95), channel_id=1, source_target_pairs={{14,0},{15,1},{0,2},{1,3},{2,4},{3,5},{4,6},{5,7},{6,8},{7,9},{8,1... | collective-permute-start | bytes 393224 | tf_op jit(solution)/shard_map/ppermute | solution.py:21
  28.5 12.5 %collective-permute-start.11 = (bf16[128,512]{1,0:T(8,128)(2,1)S(1)}, bf16[128,512]{1,0:T(8,128)(2,1)S(1)}, u32[]{:S(2)}, u32[]{:S(2)}) collective-permute-start(bf16[128,512]{1,0:T(8,128)(2,1)S(1)} %get-tuple-element.101), channel_id=1, source_target_pairs={{12,0},{13,1},{14,2},{15,3},{0,4},{1,5},{2,6},{3,7},{4,8},{5,9},{6... | collective-permute-start | bytes 393224 | tf_op jit(solution)/shard_map/ppermute | solution.py:21
  29.6 16.6 %collective-permute-start.12 = (bf16[128,512]{1,0:T(8,128)(2,1)S(1)}, bf16[128,512]{1,0:T(8,128)(2,1)S(1)}, u32[]{:S(2)}, u32[]{:S(2)}) collective-permute-start(bf16[128,512]{1,0:T(8,128)(2,1)S(1)} %get-tuple-element.102), channel_id=1, source_target_pairs={{4,0},{5,1},{6,2},{7,3},{8,4},{9,5},{10,6},{11,7},{12,8},{13,9},{1... | collective-permute-start | bytes 393224 | tf_op jit(solution)/shard_map/ppermute | solution.py:21
  57.2 24.5 %collective-permute-start.16 = (bf16[256,512]{1,0:T(8,128)(2,1)}, bf16[256,512]{1,0:T(8,128)(2,1)}, u32[]{:S(2)}, u32[]{:S(2)}) collective-permute-start(bf16[256,512]{1,0:T(8,128)(2,1)} %get-tuple-element.120.refs_19_.refs_14_), channel_id=1, source_target_pairs={{8,0},{9,1},{10,2},{11,3},{12,4},{13,5},{14,6},{15,7},{0,8},{1,9},... | collective-permute-start | bytes 786440 | tf_op jit(solution)/shard_map/ppermute | solution.py:21
  60.8 20.9 %collective-permute-start.14 = (bf16[128,512]{1,0:T(8,128)(2,1)}, bf16[128,512]{1,0:T(8,128)(2,1)}, u32[]{:S(2)}, u32[]{:S(2)}) collective-permute-start(bf16[128,512]{1,0:T(8,128)(2,1)} %get-tuple-element.118.refs_17_.refs_12_), channel_id=1, source_target_pairs={{4,0},{5,1},{6,2},{7,3},{8,4},{9,5},{10,6},{11,7},{12,8},{13,9},{1... | collective-permute-start | bytes 393224 | tf_op jit(solution)/shard_map/ppermute | solution.py:21
  63.0 18.7 %collective-permute-start.15 = (bf16[128,512]{1,0:T(8,128)(2,1)}, bf16[128,512]{1,0:T(8,128)(2,1)}, u32[]{:S(2)}, u32[]{:S(2)}) collective-permute-start(bf16[128,512]{1,0:T(8,128)(2,1)} %get-tuple-element.119.refs_18_.refs_13_), channel_id=1, source_target_pairs={{12,0},{13,1},{14,2},{15,3},{0,4},{1,5},{2,6},{3,7},{4,8},{5,9},{6... | collective-permute-start | bytes 393224 | tf_op jit(solution)/shard_map/ppermute | solution.py:21
  81.7 2.7 %collective-permute-start.18 = (bf16[4,256,512]{2,1,0:T(8,128)(2,1)S(1)}, bf16[4,256,512]{2,1,0:T(8,128)(2,1)S(1)}, u32[]{:S(2)}, u32[]{:S(2)}) collective-permute-start(bf16[4,256,512]{2,1,0:T(8,128)(2,1)S(1)} %shard_map.177.refs_6_), channel_id=1, source_target_pairs={{0,1},{1,0},{2,3},{3,2},{4,5},{5,4},{6,7},{7,6},{8,9},{9,8},{10,11... | collective-permute-start | bytes 3145736 | tf_op jit(solution)/shard_map/ppermute | solution.py:476
  84.2 2.4 %collective-permute-start.17 = (bf16[3,256,512]{2,1,0:T(8,128)(2,1)S(1)}, bf16[3,256,512]{2,1,0:T(8,128)(2,1)S(1)}, u32[]{:S(2)}, u32[]{:S(2)}) collective-permute-start(bf16[3,256,512]{2,1,0:T(8,128)(2,1)S(1)} %get-tuple-element.133), channel_id=1, source_target_pairs={{0,1},{1,0},{2,3},{3,2},{4,5},{5,4},{6,7},{7,6},{8,9},{9,8},{10,11... | collective-permute-start | bytes 2359304 | tf_op jit(solution)/shard_map/ppermute | solution.py:476
  84.4 20.2 %copy-start.25 = (f32[512,512]{1,0:T(8,128)S(1)}, f32[512,512]{1,0:T(8,128)}, u32[]{:S(2)}) copy-start(f32[512,512]{1,0:T(8,128)} %copy-done.24) | copy-start | bytes 3145732
  84.6 17.5 %collective-permute-start.19 = (bf16[4,128,512]{2,1,0:T(8,128)(2,1)S(1)}, bf16[4,128,512]{2,1,0:T(8,128)(2,1)S(1)}, u32[]{:S(2)}, u32[]{:S(2)}) collective-permute-start(bf16[4,128,512]{2,1,0:T(8,128)(2,1)S(1)} %get-tuple-element.139), channel_id=1, source_target_pairs={{0,2},{1,3},{2,0},{3,1},{4,6},{5,7},{6,4},{7,5},{8,10},{9,11},{10,... | collective-permute-start | bytes 1572872 | tf_op jit(solution)/shard_map/ppermute | solution.py:476
  86.7 36.3 %collective-permute-start.27 = (bf16[3,128,512]{2,1,0:T(8,128)(2,1)S(1)}, bf16[3,128,512]{2,1,0:T(8,128)(2,1)S(1)}, u32[]{:S(2)}, u32[]{:S(2)}) collective-permute-start(bf16[3,128,512]{2,1,0:T(8,128)(2,1)S(1)} %get-tuple-element.145), channel_id=1, source_target_pairs={{0,2},{1,3},{2,0},{3,1},{4,6},{5,7},{6,4},{7,5},{8,10},{9,11},{10,... | collective-permute-start | bytes 1179656 | tf_op jit(solution)/shard_map/ppermute | solution.py:476
  87.5 22.0 %collective-permute-start.20 = (bf16[128,512]{1,0:T(8,128)(2,1)S(1)}, bf16[128,512]{1,0:T(8,128)(2,1)S(1)}, u32[]{:S(2)}, u32[]{:S(2)}) collective-permute-start(bf16[128,512]{1,0:T(8,128)(2,1)S(1)} %get-tuple-element.114.refs_13_.refs_8_), channel_id=1, source_target_pairs={{1,0},{2,1},{3,2},{4,3},{5,4},{6,5},{7,6},{8,7},{9,8},{10,9},{11,1... | collective-permute-start | bytes 393224 | tf_op jit(solution)/shard_map/ppermute | solution.py:21
  91.6 18.0 %collective-permute-start.21 = (bf16[128,512]{1,0:T(8,128)(2,1)S(1)}, bf16[128,512]{1,0:T(8,128)(2,1)S(1)}, u32[]{:S(2)}, u32[]{:S(2)}) collective-permute-start(bf16[128,512]{1,0:T(8,128)(2,1)S(1)} %get-tuple-element.115.refs_14_.refs_9_), channel_id=1, source_target_pairs={{15,0},{0,1},{1,2},{2,3},{3,4},{4,5},{5,6},{6,7},{7,8},{8,9},{9,10... | collective-permute-start | bytes 393224 | tf_op jit(solution)/shard_map/ppermute | solution.py:21
  91.6 24.2 %collective-permute-start.22 = (bf16[128,512]{1,0:T(8,128)(2,1)S(1)}, bf16[128,512]{1,0:T(8,128)(2,1)S(1)}, u32[]{:S(2)}, u32[]{:S(2)}) collective-permute-start(bf16[128,512]{1,0:T(8,128)(2,1)S(1)} %get-tuple-element.116.refs_15_.refs_10_), channel_id=1, source_target_pairs={{2,0},{3,1},{4,2},{5,3},{6,4},{7,5},{8,6},{9,7},{10,8},{11,9},{12,... | collective-permute-start | bytes 393224 | tf_op jit(solution)/shard_map/ppermute | solution.py:21
  102.1 18.0 %collective-permute-start.23 = (bf16[128,512]{1,0:T(8,128)(2,1)S(1)}, bf16[128,512]{1,0:T(8,128)(2,1)S(1)}, u32[]{:S(2)}, u32[]{:S(2)}) collective-permute-start(bf16[128,512]{1,0:T(8,128)(2,1)S(1)} %get-tuple-element.117.refs_16_.refs_11_), channel_id=1, source_target_pairs={{14,0},{15,1},{0,2},{1,3},{2,4},{3,5},{4,6},{5,7},{6,8},{7,9},{8,1... | collective-permute-start | bytes 393224 | tf_op jit(solution)/shard_map/ppermute | solution.py:21
  109.5 13.7 %collective-permute-start.24 = (bf16[4,32,512]{2,1,0:T(8,128)(2,1)S(1)}, bf16[4,32,512]{2,1,0:T(8,128)(2,1)S(1)}, u32[]{:S(2)}, u32[]{:S(2)}) collective-permute-start(bf16[4,32,512]{2,1,0:T(8,128)(2,1)S(1)} %get-tuple-element.142), channel_id=1, source_target_pairs={{0,4},{1,5},{2,6},{3,7},{4,8},{5,9},{6,10},{7,11},{8,12},{9,13},{1... | collective-permute-start | bytes 393224 | tf_op jit(solution)/shard_map/ppermute | solution.py:476
  109.6 13.7 %collective-permute-start.25 = (bf16[4,32,512]{2,1,0:T(8,128)(2,1)S(1)}, bf16[4,32,512]{2,1,0:T(8,128)(2,1)S(1)}, u32[]{:S(2)}, u32[]{:S(2)}) collective-permute-start(bf16[4,32,512]{2,1,0:T(8,128)(2,1)S(1)} %get-tuple-element.143), channel_id=1, source_target_pairs={{0,8},{1,9},{2,10},{3,11},{4,12},{5,13},{6,14},{7,15},{8,0},{9,1},... | collective-permute-start | bytes 393224 | tf_op jit(solution)/shard_map/ppermute | solution.py:476
  115.8 8.5 %collective-permute-start.26 = (bf16[4,32,512]{2,1,0:T(8,128)(2,1)S(1)}, bf16[4,32,512]{2,1,0:T(8,128)(2,1)S(1)}, u32[]{:S(2)}, u32[]{:S(2)}) collective-permute-start(bf16[4,32,512]{2,1,0:T(8,128)(2,1)S(1)} %get-tuple-element.144), channel_id=1, source_target_pairs={{0,12},{1,13},{2,14},{3,15},{4,0},{5,1},{6,2},{7,3},{8,4},{9,5},{1... | collective-permute-start | bytes 393224 | tf_op jit(solution)/shard_map/ppermute | solution.py:476
  123.2 7.1 %collective-permute-start.31 = (bf16[3,32,512]{2,1,0:T(8,128)(2,1)S(1)}, bf16[3,32,512]{2,1,0:T(8,128)(2,1)S(1)}, u32[]{:S(2)}, u32[]{:S(2)}) collective-permute-start(bf16[3,32,512]{2,1,0:T(8,128)(2,1)S(1)} %get-tuple-element.147), channel_id=1, source_target_pairs={{0,4},{1,5},{2,6},{3,7},{4,8},{5,9},{6,10},{7,11},{8,12},{9,13},{1... | collective-permute-start | bytes 294920 | tf_op jit(solution)/shard_map/ppermute | solution.py:476
  124.4 20.8 %collective-permute-start.28 = (bf16[4,32,512]{2,1,0:T(8,128)(2,1)S(1)}, bf16[4,32,512]{2,1,0:T(8,128)(2,1)S(1)}, u32[]{:S(2)}, u32[]{:S(2)}) collective-permute-start(bf16[4,32,512]{2,1,0:T(8,128)(2,1)S(1)} %shard_map.186.refs_5_.refs_1_), channel_id=1, source_target_pairs={{0,4},{1,5},{2,6},{3,7},{4,8},{5,9},{6,10},{7,11},{8,12},{9,13},{1... | collective-permute-start | bytes 393224 | tf_op jit(solution)/shard_map/ppermute | solution.py:476
  125.2 20.0 %collective-permute-start.29 = (bf16[4,32,512]{2,1,0:T(8,128)(2,1)S(1)}, bf16[4,32,512]{2,1,0:T(8,128)(2,1)S(1)}, u32[]{:S(2)}, u32[]{:S(2)}) collective-permute-start(bf16[4,32,512]{2,1,0:T(8,128)(2,1)S(1)} %shard_map.186.refs_5_.refs_1_), channel_id=1, source_target_pairs={{0,8},{1,9},{2,10},{3,11},{4,12},{5,13},{6,14},{7,15},{8,0},{9,1},... | collective-permute-start | bytes 393224 | tf_op jit(solution)/shard_map/ppermute | solution.py:476
  128.1 17.1 %collective-permute-start.30 = (bf16[4,32,512]{2,1,0:T(8,128)(2,1)S(1)}, bf16[4,32,512]{2,1,0:T(8,128)(2,1)S(1)}, u32[]{:S(2)}, u32[]{:S(2)}) collective-permute-start(bf16[4,32,512]{2,1,0:T(8,128)(2,1)S(1)} %shard_map.186.refs_5_.refs_1_), channel_id=1, source_target_pairs={{0,12},{1,13},{2,14},{3,15},{4,0},{5,1},{6,2},{7,3},{8,4},{9,5},{1... | collective-permute-start | bytes 393224 | tf_op jit(solution)/shard_map/ppermute | solution.py:476
  128.3 16.8 %collective-permute-start.32 = (bf16[3,32,512]{2,1,0:T(8,128)(2,1)S(1)}, bf16[3,32,512]{2,1,0:T(8,128)(2,1)S(1)}, u32[]{:S(2)}, u32[]{:S(2)}) collective-permute-start(bf16[3,32,512]{2,1,0:T(8,128)(2,1)S(1)} %get-tuple-element.148), channel_id=1, source_target_pairs={{0,8},{1,9},{2,10},{3,11},{4,12},{5,13},{6,14},{7,15},{8,0},{9,1},... | collective-permute-start | bytes 294920 | tf_op jit(solution)/shard_map/ppermute | solution.py:476
  130.3 14.8 %collective-permute-start.33 = (bf16[3,32,512]{2,1,0:T(8,128)(2,1)S(1)}, bf16[3,32,512]{2,1,0:T(8,128)(2,1)S(1)}, u32[]{:S(2)}, u32[]{:S(2)}) collective-permute-start(bf16[3,32,512]{2,1,0:T(8,128)(2,1)S(1)} %get-tuple-element.149), channel_id=1, source_target_pairs={{0,12},{1,13},{2,14},{3,15},{4,0},{5,1},{6,2},{7,3},{8,4},{9,5},{1... | collective-permute-start | bytes 294920 | tf_op jit(solution)/shard_map/ppermute | solution.py:476
  145.2 14.3 %collective-permute-start.34 = (bf16[4,128,512]{2,1,0:T(8,128)(2,1)S(1)}, bf16[4,128,512]{2,1,0:T(8,128)(2,1)S(1)}, u32[]{:S(2)}, u32[]{:S(2)}) collective-permute-start(bf16[4,128,512]{2,1,0:T(8,128)(2,1)S(1)} %shard_map.188.refs_5_.refs_1_), channel_id=1, source_target_pairs={{0,2},{1,3},{2,0},{3,1},{4,6},{5,7},{6,4},{7,5},{8,10},{9,11},{10,... | collective-permute-start | bytes 1572872 | tf_op jit(solution)/shard_map/ppermute | solution.py:476
  145.3 7.6 %collective-permute-start.37 = (bf16[3,32,512]{2,1,0:T(8,128)(2,1)S(1)}, bf16[3,32,512]{2,1,0:T(8,128)(2,1)S(1)}, u32[]{:S(2)}, u32[]{:S(2)}) collective-permute-start(bf16[3,32,512]{2,1,0:T(8,128)(2,1)S(1)} %shard_map.187.refs_5_.refs_1_), channel_id=1, source_target_pairs={{0,4},{1,5},{2,6},{3,7},{4,8},{5,9},{6,10},{7,11},{8,12},{9,13},{1... | collective-permute-start | bytes 294920 | tf_op jit(solution)/shard_map/ppermute | solution.py:476
  148.0 8.3 %collective-permute-start.38 = (bf16[3,32,512]{2,1,0:T(8,128)(2,1)S(1)}, bf16[3,32,512]{2,1,0:T(8,128)(2,1)S(1)}, u32[]{:S(2)}, u32[]{:S(2)}) collective-permute-start(bf16[3,32,512]{2,1,0:T(8,128)(2,1)S(1)} %shard_map.187.refs_5_.refs_1_), channel_id=1, source_target_pairs={{0,8},{1,9},{2,10},{3,11},{4,12},{5,13},{6,14},{7,15},{8,0},{9,1},... | collective-permute-start | bytes 294920 | tf_op jit(solution)/shard_map/ppermute | solution.py:476
  148.2 8.1 %collective-permute-start.39 = (bf16[3,32,512]{2,1,0:T(8,128)(2,1)S(1)}, bf16[3,32,512]{2,1,0:T(8,128)(2,1)S(1)}, u32[]{:S(2)}, u32[]{:S(2)}) collective-permute-start(bf16[3,32,512]{2,1,0:T(8,128)(2,1)S(1)} %shard_map.187.refs_5_.refs_1_), channel_id=1, source_target_pairs={{0,12},{1,13},{2,14},{3,15},{4,0},{5,1},{6,2},{7,3},{8,4},{9,5},{1... | collective-permute-start | bytes 294920 | tf_op jit(solution)/shard_map/ppermute | solution.py:476
  156.3 11.3 %collective-permute-start.40 = (bf16[3,128,512]{2,1,0:T(8,128)(2,1)S(1)}, bf16[3,128,512]{2,1,0:T(8,128)(2,1)S(1)}, u32[]{:S(2)}, u32[]{:S(2)}) collective-permute-start(bf16[3,128,512]{2,1,0:T(8,128)(2,1)S(1)} %shard_map.189.refs_5_.refs_1_), channel_id=1, source_target_pairs={{0,2},{1,3},{2,0},{3,1},{4,6},{5,7},{6,4},{7,5},{8,10},{9,11},{10,... | collective-permute-start | bytes 1179656 | tf_op jit(solution)/shard_map/ppermute | solution.py:476
  158.2 9.5 %collective-permute-start.35 = (bf16[4,128,512]{2,1,0:T(8,128)(2,1)S(1)}, bf16[4,128,512]{2,1,0:T(8,128)(2,1)S(1)}, u32[]{:S(2)}, u32[]{:S(2)}) collective-permute-start(bf16[4,128,512]{2,1,0:T(8,128)(2,1)S(1)} %shard_map.188.refs_5_.refs_1_), channel_id=1, source_target_pairs={{0,1},{1,0},{2,3},{3,2},{4,5},{5,4},{6,7},{7,6},{8,9},{9,8},{10,11... | collective-permute-start | bytes 1572872 | tf_op jit(solution)/shard_map/ppermute | solution.py:476
  159.5 8.2 %collective-permute-start.36 = (bf16[4,128,512]{2,1,0:T(8,128)(2,1)S(1)}, bf16[4,128,512]{2,1,0:T(8,128)(2,1)S(1)}, u32[]{:S(2)}, u32[]{:S(2)}) collective-permute-start(bf16[4,128,512]{2,1,0:T(8,128)(2,1)S(1)} %collective-permute-done.34.refs_2_), channel_id=1, source_target_pairs={{0,1},{1,0},{2,3},{3,2},{4,5},{5,4},{6,7},{7,6},{8,9},{9,8},{10,11... | collective-permute-start | bytes 1572872 | tf_op jit(solution)/shard_map/ppermute | solution.py:476
  159.5 9.7 %collective-permute-start.41 = (bf16[3,128,512]{2,1,0:T(8,128)(2,1)S(1)}, bf16[3,128,512]{2,1,0:T(8,128)(2,1)S(1)}, u32[]{:S(2)}, u32[]{:S(2)}) collective-permute-start(bf16[3,128,512]{2,1,0:T(8,128)(2,1)S(1)} %shard_map.189.refs_5_.refs_1_), channel_id=1, source_target_pairs={{0,1},{1,0},{2,3},{3,2},{4,5},{5,4},{6,7},{7,6},{8,9},{9,8},{10,11... | collective-permute-start | bytes 1179656 | tf_op jit(solution)/shard_map/ppermute | solution.py:476
  167.7 1.7 %collective-permute-start.42 = (bf16[3,128,512]{2,1,0:T(8,128)(2,1)S(1)}, bf16[3,128,512]{2,1,0:T(8,128)(2,1)S(1)}, u32[]{:S(2)}, u32[]{:S(2)}) collective-permute-start(bf16[3,128,512]{2,1,0:T(8,128)(2,1)S(1)} %collective-permute-done.40.refs_2_), channel_id=1, source_target_pairs={{0,1},{1,0},{2,3},{3,2},{4,5},{5,4},{6,7},{7,6},{8,9},{9,8},{10,11... | collective-permute-start | bytes 1179656 | tf_op jit(solution)/shard_map/ppermute | solution.py:476
  (73 other events, 273.9 us)

commit v6 on v5

--- a/solution.py
+++ b/solution.py
@@ -12,7 +12,7 @@
 near_sets = 7
 bf16 = jnp.bfloat16
 f32 = jnp.float32
-vmem_limit = 24 * 1024 * 1024
+vmem_limit = 20 * 1024 * 1024
 
 
 def passed_along(block, axis, distance):
@@ -105,7 +105,7 @@
 
 
 def load_kernel(count, *refs):
-    sems = refs[-1]
+    sems, refs = refs[-1], refs[1:]
     copies = [
         pltpu.make_async_copy(refs[i], refs[count + i], sems.at[i]) for i in range(count)
     ]
@@ -115,17 +115,18 @@
         copy.wait()
 
 
-def loaded(*args):
+def loaded(me, *args):
     count = len(args)
     return pl.pallas_call(
         functools.partial(load_kernel, count),
         out_shape=[pltpu.VMEM(arg.shape, arg.dtype) for arg in args],
-        in_specs=[pl.BlockSpec(memory_space=pltpu.HBM)] * count,
+        in_specs=[pl.BlockSpec(memory_space=pltpu.SMEM)]
+        + [pl.BlockSpec(memory_space=pltpu.HBM)] * count,
         out_specs=[pl.BlockSpec(memory_space=pltpu.VMEM)] * count,
         scratch_shapes=[pltpu.SemaphoreType.DMA((count,))],
         compiler_params=pltpu.CompilerParams(vmem_limit_bytes=1024 * 1024),
         cost_estimate=pl.CostEstimate(flops=1, bytes_accessed=1, transcendentals=0),
-    )(*[in_hbm(arg) for arg in args])
+    )(me, *[in_hbm(arg) for arg in args])
 
 
 def pick_kernel(plan, *refs):
@@ -605,6 +606,7 @@
         node_cotan,
         cotan,
     ) = loaded(
+        me,
         node_latent,
         send_ids,
         recv_slot.reshape(sets, 1, cap),

time: 171 us -> 155 us (0.906)
  local copies, waits for them, and re-layouts: 23.7 us -> 0 us
  waiting for transfers between devices: 51.8 us -> 61.6 us
  Pallas kernels: 34.5 us -> 31.1 us
  starting transfers between devices: 59.1 us -> 61.7 us
    unnamed x156 -> x0, local copies, waits for them, and re-layouts: 23.7 us -> none
    ppermute x22, waiting for transfers between devices: 39.4 us -> 45.3 us  [in_group(): return lax.ppermute(block, axis, route)]
    ppermute x21, waiting for transfers between devices: 12.4 us -> 16.3 us  [passed_along(): return lax.ppermute(block, axis, route)]
    pallas_call x20, Pallas kernels: 31.2 us -> 27.9 us  [call(): pl.pallas_call(kernel, out_shape=[(pltpu.HBM if i in last else pltpu.VMEM...]
    ppermute x21, starting transfers between devices: 33.5 us -> 36.8 us  [passed_along(): return lax.ppermute(block, axis, route)]
where the time goes in v6:
time: 155 us
  starting transfers between devices  61.7 us (40%)
  waiting for transfers between devices  61.6 us (40%)
  Pallas kernels  31.1 us (20%)
    ppermute x22, waiting for transfers between devices, in_group(): return lax.ppermute(block, axis, route)  45.3 us
    ppermute x21, starting transfers between devices, passed_along(): return lax.ppermute(block, axis, route)  36.8 us
    pallas_call x20, Pallas kernels, call(): pl.pallas_call(kernel, out_shape=[(pltpu.HBM if i in last else pltpu.VMEM...  27.9 us
    ppermute x22, starting transfers between devices, in_group(): return lax.ppermute(block, axis, route)  24.9 us
    ppermute x21, waiting for transfers between devices, passed_along(): return lax.ppermute(block, axis, route)  16.3 us
    pallas_call x1, Pallas kernels, loaded(): pl.pallas_call(functools.partial(load_kernel, count), out_shape=[pltpu.VM...  3.23 us
  transfers between devices with their start and end apart: 43, of which 16 were waited for; matrix products, arithmetic and copies ran while one was open for 0% of the time, Pallas kernels for 16%

profile of v6, /device:TPU:0, one launch (start us, length us, event | category | flops | bytes accessed | tf_op | source)
XLA Modules:
  0.0 155.2 jit_solution(12812735228495943307)
XLA Ops:
  0.6 4.1 %collective-permute-start.6 = (s32[11,1,128]{2,1,0:T(1,128)}, s32[11,1,128]{2,1,0:T(1,128)S(1)}, u32[]{:S(2)}, u32[]{:S(2)}) collective-permute-start(s32[11,1,128]{2,1,0:T(1,128)} %bitcast.11), channel_id=1, source_target_pairs={{8,0},{9,1},{10,2},{11,3},{12,4},{13,5},{14,6},{15,7},{0,8},{1,9},... | collective-permute-start | bytes 16904 | tf_op jit(solution)/shard_map/ppermute | solution.py:21
  4.7 1.6 %collective-permute-start.5 = (s32[11,1,128]{2,1,0:T(1,128)}, s32[11,1,128]{2,1,0:T(1,128)S(1)}, u32[]{:S(2)}, u32[]{:S(2)}) collective-permute-start(s32[11,1,128]{2,1,0:T(1,128)} %bitcast.12), channel_id=1, source_target_pairs={{12,0},{13,1},{14,2},{15,3},{0,4},{1,5},{2,6},{3,7},{4,8},{5,9},{6... | collective-permute-start | bytes 16904 | tf_op jit(solution)/shard_map/ppermute | solution.py:21
  6.3 2.2 %collective-permute-start.4 = (s32[11,1,128]{2,1,0:T(1,128)}, s32[11,1,128]{2,1,0:T(1,128)S(1)}, u32[]{:S(2)}, u32[]{:S(2)}) collective-permute-start(s32[11,1,128]{2,1,0:T(1,128)} %bitcast.13), channel_id=1, source_target_pairs={{4,0},{5,1},{6,2},{7,3},{8,4},{9,5},{10,6},{11,7},{12,8},{13,9},{1... | collective-permute-start | bytes 16904 | tf_op jit(solution)/shard_map/ppermute | solution.py:21
  8.6 1.5 collective-permute-start.3
  10.1 3.2 %collective-permute-start.2 = (s32[11,1,128]{2,1,0:T(1,128)}, s32[11,1,128]{2,1,0:T(1,128)S(1)}, u32[]{:S(2)}, u32[]{:S(2)}) collective-permute-start(s32[11,1,128]{2,1,0:T(1,128)} %bitcast.15), channel_id=1, source_target_pairs={{2,0},{3,1},{4,2},{5,3},{6,4},{7,5},{8,6},{9,7},{10,8},{11,9},{12,... | collective-permute-start | bytes 16904 | tf_op jit(solution)/shard_map/ppermute | solution.py:21
  13.3 4.4 %collective-permute-start = (s32[11,1,128]{2,1,0:T(1,128)}, s32[11,1,128]{2,1,0:T(1,128)S(1)}, u32[]{:S(2)}, u32[]{:S(2)}) collective-permute-start(s32[11,1,128]{2,1,0:T(1,128)} %bitcast.17), channel_id=1, source_target_pairs={{1,0},{2,1},{3,2},{4,3},{5,4},{6,5},{7,6},{8,7},{9,8},{10,9},{11,1... | collective-permute-start | bytes 16904 | tf_op jit(solution)/shard_map/ppermute | solution.py:21
  17.7 3.2 %shard_map.170 = (bf16[320,512]{1,0:T(8,128)(2,1)S(1)}, s32[11,1,128]{2,1,0:T(1,128)S(1)}, s32[11,1,128]{2,1,0:T(1,128)S(1)}, bf16[11,128,512]{2,1,0:T(8,128)(2,...) custom-call(s32[1]{0:T(128)} %bitcast.refs_0_.refs_2_, ...), custom_call_target="tpu_custom_call" | custom-call | flops 1 | bytes 1 | tf_op jit(solution)/shard_map/pallas_call | solution.py:120
  21.8 2.7 %collective-permute-start.8 = (bf16[128,512]{1,0:T(8,128)(2,1)S(1)}, bf16[128,512]{1,0:T(8,128)(2,1)S(1)}, u32[]{:S(2)}, u32[]{:S(2)}) collective-permute-start(bf16[128,512]{1,0:T(8,128)(2,1)S(1)} %get-tuple-element.94), channel_id=1, source_target_pairs={{1,0},{2,1},{3,2},{4,3},{5,4},{6,5},{7,6},{8,7},{9,8},{10,9},{11,1... | collective-permute-start | bytes 393224 | tf_op jit(solution)/shard_map/ppermute | solution.py:21
  24.5 4.7 %collective-permute-start.10 = (bf16[128,512]{1,0:T(8,128)(2,1)S(1)}, bf16[128,512]{1,0:T(8,128)(2,1)S(1)}, u32[]{:S(2)}, u32[]{:S(2)}) collective-permute-start(bf16[128,512]{1,0:T(8,128)(2,1)S(1)} %get-tuple-element.96), channel_id=1, source_target_pairs={{2,0},{3,1},{4,2},{5,3},{6,4},{7,5},{8,6},{9,7},{10,8},{11,9},{12,... | collective-permute-start | bytes 393224 | tf_op jit(solution)/shard_map/ppermute | solution.py:21
  29.2 4.1 %collective-permute-done.9.refs_8_.refs_7_ = bf16[128,512]{1,0:T(8,128)(2,1)S(1)} collective-permute-done((bf16[128,512]{1,0:T(8,128)(2,1)S(1)}, bf16[128,512]{1,0:T(8,128)(2,1)S(1)}, u32[]{:S(2)}, u32[]{:S(2)}) %collective-permute-start.9) | collective-permute-done | bytes 131104 | tf_op jit(solution)/shard_map/ppermute | solution.py:21
  33.4 4.5 %shard_map.172 = (bf16[1408,320]{1,0:T(8,128)(2,1)S(1)}, bf16[320,1408]{1,0:T(8,128)(2,1)S(1)}, f32[1408,128]{1,0:T(8,128)S(1)}, f32[1024,512]{1,0:T(8,128)S(1)}...) custom-call(bf16[11,128,512]{2,1,0:T(8,128)(2,1)S(1)} %get-tuple-ele, ...), custom_call_target="tpu_custom_call" | custom-call | flops 1 | bytes 1 | tf_op jit(solution)/shard_map/pallas_call | solution.py:89
  37.9 1.6 %shard_map.173 = (bf16[512,512]{1,0:T(8,128)(2,1)S(1)}, f32[512,512]{1,0:T(8,128)S(1)}, f32[512,512]{1,0:T(8,128)S(1)}, f32[512,128]{1,0:T(8,128)S(1)}, f32[320,512]{1,0:T(8,128)S(1)}) custom-call(f32[1024,512]{1,0:T(8,128)S(1)} %get-tuple-element.89.refs_0_.refs_1_, f32[1408,128]{1,0:T(8,128)S(1)} %get-tuple-element.90.refs_1_.refs_2_.refs_3_, ...), custom_call_target="tpu_custom_call" | custom-call | flops 1 | bytes 1 | tf_op jit(solution)/shard_map/pallas_call | solution.py:89
  39.9 4.5 %shard_map.174 = (bf16[128,512]{1,0:T(8,128)(2,1)S(1)}, bf16[128,512]{1,0:T(8,128)(2,1)S(1)}, bf16[256,512]{1,0:T(8,128)(2,1)S(1)}, bf16[512,512]{1,0:T(8,128)(2...) custom-call(bf16[11,128,512]{2,1,0:T(8,128)(2,1)S(1)} %get-tuple-ele, ...), custom_call_target="tpu_custom_call" | custom-call | flops 1 | bytes 1 | tf_op jit(solution)/shard_map/pallas_call | solution.py:89
  44.5 4.6 %collective-permute-start.16 = (bf16[256,512]{1,0:T(8,128)(2,1)S(1)}, bf16[256,512]{1,0:T(8,128)(2,1)S(1)}, u32[]{:S(2)}, u32[]{:S(2)}) collective-permute-start(bf16[256,512]{1,0:T(8,128)(2,1)S(1)} %get-tuple-element.120.refs_19_.refs_14_), channel_id=1, source_target_pairs={{8,0},{9,1},{10,2},{11,3},{12,4},{13,5},{14,6},{15,7},{0,8},{1,9},... | collective-permute-start | bytes 786440 | tf_op jit(solution)/shard_map/ppermute | solution.py:21
  49.0 1.2 collective-permute-start.14
  51.0 2.1 %shard_map.175 = (bf16[896,512]{1,0:T(8,128)(2,1)S(1)}, bf16[384,512]{1,0:T(8,128)(2,1)S(1)}, bf16[128,512]{1,0:T(8,128)(2,1)S(1)}, bf16[128,512]{1,0:T(8,128)(2...) custom-call(bf16[11,128,512]{2,1,0:T(8,128)(2,1)S(1)} %get-tuple-element.81.refs_0_.refs_1_, ...), custom_call_target="tpu_custom_call" | custom-call | flops 1 | bytes 1 | tf_op jit(solution)/shard_map/pallas_call | solution.py:89
  53.1 3.9 %shard_map.176 = (f32[4,256,512]{2,1,0:T(8,128)S(1)}, bf16[4,256,512]{2,1,0:T(8,128)(2,1)S(1)}, bf16[320,512]{1,0:T(8,128)(2,1)S(1)}) custom-call(bf16[11,128,512]{2,1,0:T(8,128)(2,1)S(1)} %get-tuple-element.82.refs_0_, bf16[320,1408]{1,0:T(8,128)(2,1)S(1)} %get-tuple-element.92.refs_2_.refs_4_.refs_1_, s32[1]{0:T(128)} %bitcast.refs_0_.refs_2_, ...), custom_call_target="tpu_custom_call" | custom-call | flops 1 | bytes 1 | tf_op jit(solution)/shard_map/pallas_call | solution.py:89
  57.0 1.2 collective-permute-done.14.refs_1_.refs_15_
  58.3 4.7 %collective-permute-done.15.refs_2_.refs_16_ = bf16[128,512]{1,0:T(8,128)(2,1)S(1)} collective-permute-done((bf16[128,512]{1,0:T(8,128)(2,1)S(1)}, bf16[128,512]{1,0:T(8,128)(2,1)S(1)}, u32[]{:S(2)}, u32[]{:S(2)}) %collective-permute-start.15) | collective-permute-done | bytes 131104 | tf_op jit(solution)/shard_map/ppermute | solution.py:21
  63.0 1.1 collective-permute-done.16.refs_3_.refs_17_
  64.1 0.9 collective-permute-start.18
  64.9 1.3 shard_map.178
  66.3 0.9 collective-permute-done.18.refs_2_
  67.5 1.0 collective-permute-start.19
  68.8 1.0 collective-permute-start.27
  69.8 2.1 %collective-permute-start.20 = (bf16[128,512]{1,0:T(8,128)(2,1)S(1)}, bf16[128,512]{1,0:T(8,128)(2,1)S(1)}, u32[]{:S(2)}, u32[]{:S(2)}) collective-permute-start(bf16[128,512]{1,0:T(8,128)(2,1)S(1)} %get-tuple-element.114.refs_13_.refs_8_), channel_id=1, source_target_pairs={{1,0},{2,1},{3,2},{4,3},{5,4},{6,5},{7,6},{8,7},{9,8},{10,9},{11,1... | collective-permute-start | bytes 393224 | tf_op jit(solution)/shard_map/ppermute | solution.py:21
  71.9 1.0 collective-permute-start.22
  73.0 12.0 %collective-permute-done.19.refs_2_ = bf16[4,128,512]{2,1,0:T(8,128)(2,1)S(1)} collective-permute-done((bf16[4,128,512]{2,1,0:T(8,128)(2,1)S(1)}, bf16[4,128,512]{2,1,0:T(8,128)(2,1)S(1)}, u32[]{:S(2)}, u32[]{:S(2)}) %collective-permute-start.19) | collective-permute-done | bytes 524320 | tf_op jit(solution)/shard_map/ppermute | solution.py:477
  85.0 2.5 %collective-permute-start.23 = (bf16[128,512]{1,0:T(8,128)(2,1)S(1)}, bf16[128,512]{1,0:T(8,128)(2,1)S(1)}, u32[]{:S(2)}, u32[]{:S(2)}) collective-permute-start(bf16[128,512]{1,0:T(8,128)(2,1)S(1)} %get-tuple-element.117.refs_16_.refs_11_), channel_id=1, source_target_pairs={{14,0},{15,1},{0,2},{1,3},{2,4},{3,5},{4,6},{5,7},{6,8},{7,9},{8,1... | collective-permute-start | bytes 393224 | tf_op jit(solution)/shard_map/ppermute | solution.py:21
  87.5 3.5 %shard_map.181 = (bf16[11,128,512]{2,1,0:T(8,128)(2,1)}, bf16[11,128,512]{2,1,0:T(8,128)(2,1)}) custom-call(bf16[11,128,512]{2,1,0:T(8,128)(2,1)S(1)} %get-tuple-element.82.refs_0_, bf16[11,128,512]{2,1,0:T(8,128)(2,1)S(1)} %get-tuple-element.81.refs_0_.refs_1_, bf16[1536,512]{1,0:T(8,128)(2,1)S(1)} %get-tuple-element.85.refs_4_.refs_6_.refs_2_.refs_3_.refs_1_, ...), custom_call_target="tpu_custom_call" | custom-call | flops 1 | bytes 1 | tf_op jit(solution)/shard_map/pallas_call | solution.py:89
  91.1 2.8 %collective-permute-start.24 = (bf16[4,32,512]{2,1,0:T(8,128)(2,1)S(1)}, bf16[4,32,512]{2,1,0:T(8,128)(2,1)S(1)}, u32[]{:S(2)}, u32[]{:S(2)}) collective-permute-start(bf16[4,32,512]{2,1,0:T(8,128)(2,1)S(1)} %get-tuple-element.142), channel_id=1, source_target_pairs={{0,4},{1,5},{2,6},{3,7},{4,8},{5,9},{6,10},{7,11},{8,12},{9,13},{1... | collective-permute-start | bytes 393224 | tf_op jit(solution)/shard_map/ppermute | solution.py:477
  94.0 4.6 %collective-permute-done.22.refs_13_ = bf16[128,512]{1,0:T(8,128)(2,1)S(1)} collective-permute-done((bf16[128,512]{1,0:T(8,128)(2,1)S(1)}, bf16[128,512]{1,0:T(8,128)(2,1)S(1)}, u32[]{:S(2)}, u32[]{:S(2)}) %collective-permute-start.22) | collective-permute-done | bytes 131104 | tf_op jit(solution)/shard_map/ppermute | solution.py:21
  98.6 2.1 %collective-permute-start.26 = (bf16[4,32,512]{2,1,0:T(8,128)(2,1)S(1)}, bf16[4,32,512]{2,1,0:T(8,128)(2,1)S(1)}, u32[]{:S(2)}, u32[]{:S(2)}) collective-permute-start(bf16[4,32,512]{2,1,0:T(8,128)(2,1)S(1)} %get-tuple-element.144), channel_id=1, source_target_pairs={{0,12},{1,13},{2,14},{3,15},{4,0},{5,1},{6,2},{7,3},{8,4},{9,5},{1... | collective-permute-start | bytes 393224 | tf_op jit(solution)/shard_map/ppermute | solution.py:477
  101.3 1.6 %shard_map.184.refs_3_ = bf16[320,512]{1,0:T(8,128)(2,1)} custom-call(f32[320,512]{1,0:T(8,128)S(1)} %shard_map.183.refs_0_, bf16[1536,512]{1,0:T(8,128)(2,1)S(1)} %get-tuple-element.85.refs_4_.refs_6_.refs_2_.refs_3_.refs_1_, s32[11,1,128]{2,1,0:T(1,128)S(1)} %get-tuple-element.84.refs_2_, s32[11,1,128]{2,1,0:T(1,128)S(1)} %collective-permute-done.refs_1_.refs_3_, ...), custom_call_target="tpu_custom_call" | custom-call | flops 1 | bytes 1 | tf_op jit(solution)/shard_map/pallas_call | solution.py:89
  103.9 3.4 %collective-permute-done.26.refs_4_ = bf16[4,32,512]{2,1,0:T(8,128)(2,1)S(1)} collective-permute-done((bf16[4,32,512]{2,1,0:T(8,128)(2,1)S(1)}, bf16[4,32,512]{2,1,0:T(8,128)(2,1)S(1)}, u32[]{:S(2)}, u32[]{:S(2)}) %collective-permute-start.26) | collective-permute-done | bytes 131104 | tf_op jit(solution)/shard_map/ppermute | solution.py:477
  107.4 1.9 %collective-permute-start.30 = (bf16[4,32,512]{2,1,0:T(8,128)(2,1)S(1)}, bf16[4,32,512]{2,1,0:T(8,128)(2,1)S(1)}, u32[]{:S(2)}, u32[]{:S(2)}) collective-permute-start(bf16[4,32,512]{2,1,0:T(8,128)(2,1)S(1)} %shard_map.186.refs_5_.refs_1_), channel_id=1, source_target_pairs={{0,12},{1,13},{2,14},{3,15},{4,0},{5,1},{6,2},{7,3},{8,4},{9,5},{1... | collective-permute-start | bytes 393224 | tf_op jit(solution)/shard_map/ppermute | solution.py:477
  109.3 1.1 collective-permute-start.29
  110.5 1.8 %collective-permute-start.32 = (bf16[3,32,512]{2,1,0:T(8,128)(2,1)S(1)}, bf16[3,32,512]{2,1,0:T(8,128)(2,1)S(1)}, u32[]{:S(2)}, u32[]{:S(2)}) collective-permute-start(bf16[3,32,512]{2,1,0:T(8,128)(2,1)S(1)} %get-tuple-element.148), channel_id=1, source_target_pairs={{0,8},{1,9},{2,10},{3,11},{4,12},{5,13},{6,14},{7,15},{8,0},{9,1},... | collective-permute-start | bytes 294920 | tf_op jit(solution)/shard_map/ppermute | solution.py:477
  112.4 2.8 %collective-permute-start.33 = (bf16[3,32,512]{2,1,0:T(8,128)(2,1)S(1)}, bf16[3,32,512]{2,1,0:T(8,128)(2,1)S(1)}, u32[]{:S(2)}, u32[]{:S(2)}) collective-permute-start(bf16[3,32,512]{2,1,0:T(8,128)(2,1)S(1)} %get-tuple-element.149), channel_id=1, source_target_pairs={{0,12},{1,13},{2,14},{3,15},{4,0},{5,1},{6,2},{7,3},{8,4},{9,5},{1... | collective-permute-start | bytes 294920 | tf_op jit(solution)/shard_map/ppermute | solution.py:477
  115.1 11.0 %collective-permute-done.32.refs_3_ = bf16[3,32,512]{2,1,0:T(8,128)(2,1)S(1)} collective-permute-done((bf16[3,32,512]{2,1,0:T(8,128)(2,1)S(1)}, bf16[3,32,512]{2,1,0:T(8,128)(2,1)S(1)}, u32[]{:S(2)}, u32[]{:S(2)}) %collective-permute-start.32) | collective-permute-done | bytes 98336 | tf_op jit(solution)/shard_map/ppermute | solution.py:477
  126.3 2.7 %collective-permute-start.34 = (bf16[4,128,512]{2,1,0:T(8,128)(2,1)S(1)}, bf16[4,128,512]{2,1,0:T(8,128)(2,1)S(1)}, u32[]{:S(2)}, u32[]{:S(2)}) collective-permute-start(bf16[4,128,512]{2,1,0:T(8,128)(2,1)S(1)} %shard_map.188.refs_5_.refs_1_), channel_id=1, source_target_pairs={{0,2},{1,3},{2,0},{3,1},{4,6},{5,7},{6,4},{7,5},{8,10},{9,11},{10,... | collective-permute-start | bytes 1572872 | tf_op jit(solution)/shard_map/ppermute | solution.py:477
  128.9 3.0 %collective-permute-start.39 = (bf16[3,32,512]{2,1,0:T(8,128)(2,1)S(1)}, bf16[3,32,512]{2,1,0:T(8,128)(2,1)S(1)}, u32[]{:S(2)}, u32[]{:S(2)}) collective-permute-start(bf16[3,32,512]{2,1,0:T(8,128)(2,1)S(1)} %shard_map.187.refs_5_.refs_1_), channel_id=1, source_target_pairs={{0,12},{1,13},{2,14},{3,15},{4,0},{5,1},{6,2},{7,3},{8,4},{9,5},{1... | collective-permute-start | bytes 294920 | tf_op jit(solution)/shard_map/ppermute | solution.py:477
  132.6 2.6 %collective-permute-done.39.refs_4_ = bf16[3,32,512]{2,1,0:T(8,128)(2,1)S(1)} collective-permute-done((bf16[3,32,512]{2,1,0:T(8,128)(2,1)S(1)}, bf16[3,32,512]{2,1,0:T(8,128)(2,1)S(1)}, u32[]{:S(2)}, u32[]{:S(2)}) %collective-permute-start.39) | collective-permute-done | bytes 98336 | tf_op jit(solution)/shard_map/ppermute | solution.py:477
  135.1 6.1 %collective-permute-done.38.refs_3_ = bf16[3,32,512]{2,1,0:T(8,128)(2,1)S(1)} collective-permute-done((bf16[3,32,512]{2,1,0:T(8,128)(2,1)S(1)}, bf16[3,32,512]{2,1,0:T(8,128)(2,1)S(1)}, u32[]{:S(2)}, u32[]{:S(2)}) %collective-permute-start.38) | collective-permute-done | bytes 98336 | tf_op jit(solution)/shard_map/ppermute | solution.py:477
  141.3 1.6 %collective-permute-start.40 = (bf16[3,128,512]{2,1,0:T(8,128)(2,1)S(1)}, bf16[3,128,512]{2,1,0:T(8,128)(2,1)S(1)}, u32[]{:S(2)}, u32[]{:S(2)}) collective-permute-start(bf16[3,128,512]{2,1,0:T(8,128)(2,1)S(1)} %shard_map.189.refs_5_.refs_1_), channel_id=1, source_target_pairs={{0,2},{1,3},{2,0},{3,1},{4,6},{5,7},{6,4},{7,5},{8,10},{9,11},{10,... | collective-permute-start | bytes 1179656 | tf_op jit(solution)/shard_map/ppermute | solution.py:477
  143.4 8.9 %collective-permute-done.40.refs_2_ = bf16[3,128,512]{2,1,0:T(8,128)(2,1)S(1)} collective-permute-done((bf16[3,128,512]{2,1,0:T(8,128)(2,1)S(1)}, bf16[3,128,512]{2,1,0:T(8,128)(2,1)S(1)}, u32[]{:S(2)}, u32[]{:S(2)}) %collective-permute-start.40) | collective-permute-done | bytes 393248 | tf_op jit(solution)/shard_map/ppermute | solution.py:477
  152.3 1.5 shard_map.190
  154.0 1.3 shard_map.191
  (60 shorter events, 6.1 us)
Async XLA Ops:
  0.6 12.7 %collective-permute-start.6 = (s32[11,1,128]{2,1,0:T(1,128)}, s32[11,1,128]{2,1,0:T(1,128)S(1)}, u32[]{:S(2)}, u32[]{:S(2)}) collective-permute-start(s32[11,1,128]{2,1,0:T(1,128)} %bitcast.11), channel_id=1, source_target_pairs={{8,0},{9,1},{10,2},{11,3},{12,4},{13,5},{14,6},{15,7},{0,8},{1,9},... | collective-permute-start | bytes 16904 | tf_op jit(solution)/shard_map/ppermute | solution.py:21
  4.7 8.6 %collective-permute-start.5 = (s32[11,1,128]{2,1,0:T(1,128)}, s32[11,1,128]{2,1,0:T(1,128)S(1)}, u32[]{:S(2)}, u32[]{:S(2)}) collective-permute-start(s32[11,1,128]{2,1,0:T(1,128)} %bitcast.12), channel_id=1, source_target_pairs={{12,0},{13,1},{14,2},{15,3},{0,4},{1,5},{2,6},{3,7},{4,8},{5,9},{6... | collective-permute-start | bytes 16904 | tf_op jit(solution)/shard_map/ppermute | solution.py:21
  6.3 14.7 %collective-permute-start.4 = (s32[11,1,128]{2,1,0:T(1,128)}, s32[11,1,128]{2,1,0:T(1,128)S(1)}, u32[]{:S(2)}, u32[]{:S(2)}) collective-permute-start(s32[11,1,128]{2,1,0:T(1,128)} %bitcast.13), channel_id=1, source_target_pairs={{4,0},{5,1},{6,2},{7,3},{8,4},{9,5},{10,6},{11,7},{12,8},{13,9},{1... | collective-permute-start | bytes 16904 | tf_op jit(solution)/shard_map/ppermute | solution.py:21
  8.6 12.4 %collective-permute-start.3 = (s32[11,1,128]{2,1,0:T(1,128)}, s32[11,1,128]{2,1,0:T(1,128)S(1)}, u32[]{:S(2)}, u32[]{:S(2)}) collective-permute-start(s32[11,1,128]{2,1,0:T(1,128)} %bitcast.14), channel_id=1, source_target_pairs={{14,0},{15,1},{0,2},{1,3},{2,4},{3,5},{4,6},{5,7},{6,8},{7,9},{8,1... | collective-permute-start | bytes 16904 | tf_op jit(solution)/shard_map/ppermute | solution.py:21
  10.1 10.9 %collective-permute-start.2 = (s32[11,1,128]{2,1,0:T(1,128)}, s32[11,1,128]{2,1,0:T(1,128)S(1)}, u32[]{:S(2)}, u32[]{:S(2)}) collective-permute-start(s32[11,1,128]{2,1,0:T(1,128)} %bitcast.15), channel_id=1, source_target_pairs={{2,0},{3,1},{4,2},{5,3},{6,4},{7,5},{8,6},{9,7},{10,8},{11,9},{12,... | collective-permute-start | bytes 16904 | tf_op jit(solution)/shard_map/ppermute | solution.py:21
  13.3 7.7 %collective-permute-start.1 = (s32[11,1,128]{2,1,0:T(1,128)}, s32[11,1,128]{2,1,0:T(1,128)S(1)}, u32[]{:S(2)}, u32[]{:S(2)}) collective-permute-start(s32[11,1,128]{2,1,0:T(1,128)} %bitcast.16), channel_id=1, source_target_pairs={{15,0},{0,1},{1,2},{2,3},{3,4},{4,5},{5,6},{6,7},{7,8},{8,9},{9,10... | collective-permute-start | bytes 16904 | tf_op jit(solution)/shard_map/ppermute | solution.py:21
  13.3 7.7 %collective-permute-start = (s32[11,1,128]{2,1,0:T(1,128)}, s32[11,1,128]{2,1,0:T(1,128)S(1)}, u32[]{:S(2)}, u32[]{:S(2)}) collective-permute-start(s32[11,1,128]{2,1,0:T(1,128)} %bitcast.17), channel_id=1, source_target_pairs={{1,0},{2,1},{3,2},{4,3},{5,4},{6,5},{7,6},{8,7},{9,8},{10,9},{11,1... | collective-permute-start | bytes 16904 | tf_op jit(solution)/shard_map/ppermute | solution.py:21
  21.8 7.4 %collective-permute-start.8 = (bf16[128,512]{1,0:T(8,128)(2,1)S(1)}, bf16[128,512]{1,0:T(8,128)(2,1)S(1)}, u32[]{:S(2)}, u32[]{:S(2)}) collective-permute-start(bf16[128,512]{1,0:T(8,128)(2,1)S(1)} %get-tuple-element.94), channel_id=1, source_target_pairs={{1,0},{2,1},{3,2},{4,3},{5,4},{6,5},{7,6},{8,7},{9,8},{10,9},{11,1... | collective-permute-start | bytes 393224 | tf_op jit(solution)/shard_map/ppermute | solution.py:21
  24.5 8.9 %collective-permute-start.9 = (bf16[128,512]{1,0:T(8,128)(2,1)S(1)}, bf16[128,512]{1,0:T(8,128)(2,1)S(1)}, u32[]{:S(2)}, u32[]{:S(2)}) collective-permute-start(bf16[128,512]{1,0:T(8,128)(2,1)S(1)} %get-tuple-element.95), channel_id=1, source_target_pairs={{14,0},{15,1},{0,2},{1,3},{2,4},{3,5},{4,6},{5,7},{6,8},{7,9},{8,1... | collective-permute-start | bytes 393224 | tf_op jit(solution)/shard_map/ppermute | solution.py:21
  24.5 15.4 %collective-permute-start.13 = (bf16[256,512]{1,0:T(8,128)(2,1)S(1)}, bf16[256,512]{1,0:T(8,128)(2,1)S(1)}, u32[]{:S(2)}, u32[]{:S(2)}) collective-permute-start(bf16[256,512]{1,0:T(8,128)(2,1)S(1)} %get-tuple-element.103), channel_id=1, source_target_pairs={{8,0},{9,1},{10,2},{11,3},{12,4},{13,5},{14,6},{15,7},{0,8},{1,9},... | collective-permute-start | bytes 786440 | tf_op jit(solution)/shard_map/ppermute | solution.py:21
  24.5 13.4 %collective-permute-start.10 = (bf16[128,512]{1,0:T(8,128)(2,1)S(1)}, bf16[128,512]{1,0:T(8,128)(2,1)S(1)}, u32[]{:S(2)}, u32[]{:S(2)}) collective-permute-start(bf16[128,512]{1,0:T(8,128)(2,1)S(1)} %get-tuple-element.96), channel_id=1, source_target_pairs={{2,0},{3,1},{4,2},{5,3},{6,4},{7,5},{8,6},{9,7},{10,8},{11,9},{12,... | collective-permute-start | bytes 393224 | tf_op jit(solution)/shard_map/ppermute | solution.py:21
  29.2 8.7 %collective-permute-start.7 = (bf16[128,512]{1,0:T(8,128)(2,1)S(1)}, bf16[128,512]{1,0:T(8,128)(2,1)S(1)}, u32[]{:S(2)}, u32[]{:S(2)}) collective-permute-start(bf16[128,512]{1,0:T(8,128)(2,1)S(1)} %get-tuple-element.88.refs_7_), channel_id=1, source_target_pairs={{15,0},{0,1},{1,2},{2,3},{3,4},{4,5},{5,6},{6,7},{7,8},{8,9},{9,10... | collective-permute-start | bytes 393224 | tf_op jit(solution)/shard_map/ppermute | solution.py:21
  29.2 10.3 %collective-permute-start.11 = (bf16[128,512]{1,0:T(8,128)(2,1)S(1)}, bf16[128,512]{1,0:T(8,128)(2,1)S(1)}, u32[]{:S(2)}, u32[]{:S(2)}) collective-permute-start(bf16[128,512]{1,0:T(8,128)(2,1)S(1)} %get-tuple-element.101), channel_id=1, source_target_pairs={{12,0},{13,1},{14,2},{15,3},{0,4},{1,5},{2,6},{3,7},{4,8},{5,9},{6... | collective-permute-start | bytes 393224 | tf_op jit(solution)/shard_map/ppermute | solution.py:21
  33.4 6.6 %collective-permute-start.12 = (bf16[128,512]{1,0:T(8,128)(2,1)S(1)}, bf16[128,512]{1,0:T(8,128)(2,1)S(1)}, u32[]{:S(2)}, u32[]{:S(2)}) collective-permute-start(bf16[128,512]{1,0:T(8,128)(2,1)S(1)} %get-tuple-element.102), channel_id=1, source_target_pairs={{4,0},{5,1},{6,2},{7,3},{8,4},{9,5},{10,6},{11,7},{12,8},{13,9},{1... | collective-permute-start | bytes 393224 | tf_op jit(solution)/shard_map/ppermute | solution.py:21
  44.5 19.6 %collective-permute-start.16 = (bf16[256,512]{1,0:T(8,128)(2,1)S(1)}, bf16[256,512]{1,0:T(8,128)(2,1)S(1)}, u32[]{:S(2)}, u32[]{:S(2)}) collective-permute-start(bf16[256,512]{1,0:T(8,128)(2,1)S(1)} %get-tuple-element.120.refs_19_.refs_14_), channel_id=1, source_target_pairs={{8,0},{9,1},{10,2},{11,3},{12,4},{13,5},{14,6},{15,7},{0,8},{1,9},... | collective-permute-start | bytes 786440 | tf_op jit(solution)/shard_map/ppermute | solution.py:21
  49.0 9.2 %collective-permute-start.14 = (bf16[128,512]{1,0:T(8,128)(2,1)S(1)}, bf16[128,512]{1,0:T(8,128)(2,1)S(1)}, u32[]{:S(2)}, u32[]{:S(2)}) collective-permute-start(bf16[128,512]{1,0:T(8,128)(2,1)S(1)} %get-tuple-element.118.refs_17_.refs_12_), channel_id=1, source_target_pairs={{4,0},{5,1},{6,2},{7,3},{8,4},{9,5},{10,6},{11,7},{12,8},{13,9},{1... | collective-permute-start | bytes 393224 | tf_op jit(solution)/shard_map/ppermute | solution.py:21
  50.2 12.8 %collective-permute-start.15 = (bf16[128,512]{1,0:T(8,128)(2,1)S(1)}, bf16[128,512]{1,0:T(8,128)(2,1)S(1)}, u32[]{:S(2)}, u32[]{:S(2)}) collective-permute-start(bf16[128,512]{1,0:T(8,128)(2,1)S(1)} %get-tuple-element.119.refs_18_.refs_13_), channel_id=1, source_target_pairs={{12,0},{13,1},{14,2},{15,3},{0,4},{1,5},{2,6},{3,7},{4,8},{5,9},{6... | collective-permute-start | bytes 393224 | tf_op jit(solution)/shard_map/ppermute | solution.py:21
  64.1 3.2 %collective-permute-start.18 = (bf16[4,256,512]{2,1,0:T(8,128)(2,1)S(1)}, bf16[4,256,512]{2,1,0:T(8,128)(2,1)S(1)}, u32[]{:S(2)}, u32[]{:S(2)}) collective-permute-start(bf16[4,256,512]{2,1,0:T(8,128)(2,1)S(1)} %shard_map.177.refs_6_), channel_id=1, source_target_pairs={{0,1},{1,0},{2,3},{3,2},{4,5},{5,4},{6,7},{7,6},{8,9},{9,8},{10,11... | collective-permute-start | bytes 3145736 | tf_op jit(solution)/shard_map/ppermute | solution.py:477
  66.3 2.4 %collective-permute-start.17 = (bf16[3,256,512]{2,1,0:T(8,128)(2,1)S(1)}, bf16[3,256,512]{2,1,0:T(8,128)(2,1)S(1)}, u32[]{:S(2)}, u32[]{:S(2)}) collective-permute-start(bf16[3,256,512]{2,1,0:T(8,128)(2,1)S(1)} %get-tuple-element.133), channel_id=1, source_target_pairs={{0,1},{1,0},{2,3},{3,2},{4,5},{5,4},{6,7},{7,6},{8,9},{9,8},{10,11... | collective-permute-start | bytes 2359304 | tf_op jit(solution)/shard_map/ppermute | solution.py:477
  67.5 17.5 %collective-permute-start.19 = (bf16[4,128,512]{2,1,0:T(8,128)(2,1)S(1)}, bf16[4,128,512]{2,1,0:T(8,128)(2,1)S(1)}, u32[]{:S(2)}, u32[]{:S(2)}) collective-permute-start(bf16[4,128,512]{2,1,0:T(8,128)(2,1)S(1)} %get-tuple-element.139), channel_id=1, source_target_pairs={{0,2},{1,3},{2,0},{3,1},{4,6},{5,7},{6,4},{7,5},{8,10},{9,11},{10,... | collective-permute-start | bytes 1572872 | tf_op jit(solution)/shard_map/ppermute | solution.py:477
  68.8 34.1 %collective-permute-start.27 = (bf16[3,128,512]{2,1,0:T(8,128)(2,1)S(1)}, bf16[3,128,512]{2,1,0:T(8,128)(2,1)S(1)}, u32[]{:S(2)}, u32[]{:S(2)}) collective-permute-start(bf16[3,128,512]{2,1,0:T(8,128)(2,1)S(1)} %get-tuple-element.145), channel_id=1, source_target_pairs={{0,2},{1,3},{2,0},{3,1},{4,6},{5,7},{6,4},{7,5},{8,10},{9,11},{10,... | collective-permute-start | bytes 1179656 | tf_op jit(solution)/shard_map/ppermute | solution.py:477
  69.8 21.3 %collective-permute-start.20 = (bf16[128,512]{1,0:T(8,128)(2,1)S(1)}, bf16[128,512]{1,0:T(8,128)(2,1)S(1)}, u32[]{:S(2)}, u32[]{:S(2)}) collective-permute-start(bf16[128,512]{1,0:T(8,128)(2,1)S(1)} %get-tuple-element.114.refs_13_.refs_8_), channel_id=1, source_target_pairs={{1,0},{2,1},{3,2},{4,3},{5,4},{6,5},{7,6},{8,7},{9,8},{10,9},{11,1... | collective-permute-start | bytes 393224 | tf_op jit(solution)/shard_map/ppermute | solution.py:21
  71.9 22.0 %collective-permute-start.21 = (bf16[128,512]{1,0:T(8,128)(2,1)S(1)}, bf16[128,512]{1,0:T(8,128)(2,1)S(1)}, u32[]{:S(2)}, u32[]{:S(2)}) collective-permute-start(bf16[128,512]{1,0:T(8,128)(2,1)S(1)} %get-tuple-element.115.refs_14_.refs_9_), channel_id=1, source_target_pairs={{15,0},{0,1},{1,2},{2,3},{3,4},{4,5},{5,6},{6,7},{7,8},{8,9},{9,10... | collective-permute-start | bytes 393224 | tf_op jit(solution)/shard_map/ppermute | solution.py:21
  71.9 26.7 %collective-permute-start.22 = (bf16[128,512]{1,0:T(8,128)(2,1)S(1)}, bf16[128,512]{1,0:T(8,128)(2,1)S(1)}, u32[]{:S(2)}, u32[]{:S(2)}) collective-permute-start(bf16[128,512]{1,0:T(8,128)(2,1)S(1)} %get-tuple-element.116.refs_15_.refs_10_), channel_id=1, source_target_pairs={{2,0},{3,1},{4,2},{5,3},{6,4},{7,5},{8,6},{9,7},{10,8},{11,9},{12,... | collective-permute-start | bytes 393224 | tf_op jit(solution)/shard_map/ppermute | solution.py:21
  85.0 16.3 %collective-permute-start.23 = (bf16[128,512]{1,0:T(8,128)(2,1)S(1)}, bf16[128,512]{1,0:T(8,128)(2,1)S(1)}, u32[]{:S(2)}, u32[]{:S(2)}) collective-permute-start(bf16[128,512]{1,0:T(8,128)(2,1)S(1)} %get-tuple-element.117.refs_16_.refs_11_), channel_id=1, source_target_pairs={{14,0},{15,1},{0,2},{1,3},{2,4},{3,5},{4,6},{5,7},{6,8},{7,9},{8,1... | collective-permute-start | bytes 393224 | tf_op jit(solution)/shard_map/ppermute | solution.py:21
  91.1 12.7 %collective-permute-start.24 = (bf16[4,32,512]{2,1,0:T(8,128)(2,1)S(1)}, bf16[4,32,512]{2,1,0:T(8,128)(2,1)S(1)}, u32[]{:S(2)}, u32[]{:S(2)}) collective-permute-start(bf16[4,32,512]{2,1,0:T(8,128)(2,1)S(1)} %get-tuple-element.142), channel_id=1, source_target_pairs={{0,4},{1,5},{2,6},{3,7},{4,8},{5,9},{6,10},{7,11},{8,12},{9,13},{1... | collective-permute-start | bytes 393224 | tf_op jit(solution)/shard_map/ppermute | solution.py:477
  93.9 9.9 %collective-permute-start.25 = (bf16[4,32,512]{2,1,0:T(8,128)(2,1)S(1)}, bf16[4,32,512]{2,1,0:T(8,128)(2,1)S(1)}, u32[]{:S(2)}, u32[]{:S(2)}) collective-permute-start(bf16[4,32,512]{2,1,0:T(8,128)(2,1)S(1)} %get-tuple-element.143), channel_id=1, source_target_pairs={{0,8},{1,9},{2,10},{3,11},{4,12},{5,13},{6,14},{7,15},{8,0},{9,1},... | collective-permute-start | bytes 393224 | tf_op jit(solution)/shard_map/ppermute | solution.py:477
  98.6 8.7 %collective-permute-start.26 = (bf16[4,32,512]{2,1,0:T(8,128)(2,1)S(1)}, bf16[4,32,512]{2,1,0:T(8,128)(2,1)S(1)}, u32[]{:S(2)}, u32[]{:S(2)}) collective-permute-start(bf16[4,32,512]{2,1,0:T(8,128)(2,1)S(1)} %get-tuple-element.144), channel_id=1, source_target_pairs={{0,12},{1,13},{2,14},{3,15},{4,0},{5,1},{6,2},{7,3},{8,4},{9,5},{1... | collective-permute-start | bytes 393224 | tf_op jit(solution)/shard_map/ppermute | solution.py:477
  103.0 9.3 %collective-permute-start.31 = (bf16[3,32,512]{2,1,0:T(8,128)(2,1)S(1)}, bf16[3,32,512]{2,1,0:T(8,128)(2,1)S(1)}, u32[]{:S(2)}, u32[]{:S(2)}) collective-permute-start(bf16[3,32,512]{2,1,0:T(8,128)(2,1)S(1)} %get-tuple-element.147), channel_id=1, source_target_pairs={{0,4},{1,5},{2,6},{3,7},{4,8},{5,9},{6,10},{7,11},{8,12},{9,13},{1... | collective-permute-start | bytes 294920 | tf_op jit(solution)/shard_map/ppermute | solution.py:477
  107.4 18.8 %collective-permute-start.30 = (bf16[4,32,512]{2,1,0:T(8,128)(2,1)S(1)}, bf16[4,32,512]{2,1,0:T(8,128)(2,1)S(1)}, u32[]{:S(2)}, u32[]{:S(2)}) collective-permute-start(bf16[4,32,512]{2,1,0:T(8,128)(2,1)S(1)} %shard_map.186.refs_5_.refs_1_), channel_id=1, source_target_pairs={{0,12},{1,13},{2,14},{3,15},{4,0},{5,1},{6,2},{7,3},{8,4},{9,5},{1... | collective-permute-start | bytes 393224 | tf_op jit(solution)/shard_map/ppermute | solution.py:477
  109.3 16.9 %collective-permute-start.29 = (bf16[4,32,512]{2,1,0:T(8,128)(2,1)S(1)}, bf16[4,32,512]{2,1,0:T(8,128)(2,1)S(1)}, u32[]{:S(2)}, u32[]{:S(2)}) collective-permute-start(bf16[4,32,512]{2,1,0:T(8,128)(2,1)S(1)} %shard_map.186.refs_5_.refs_1_), channel_id=1, source_target_pairs={{0,8},{1,9},{2,10},{3,11},{4,12},{5,13},{6,14},{7,15},{8,0},{9,1},... | collective-permute-start | bytes 393224 | tf_op jit(solution)/shard_map/ppermute | solution.py:477
  110.4 15.8 %collective-permute-start.28 = (bf16[4,32,512]{2,1,0:T(8,128)(2,1)S(1)}, bf16[4,32,512]{2,1,0:T(8,128)(2,1)S(1)}, u32[]{:S(2)}, u32[]{:S(2)}) collective-permute-start(bf16[4,32,512]{2,1,0:T(8,128)(2,1)S(1)} %shard_map.186.refs_5_.refs_1_), channel_id=1, source_target_pairs={{0,4},{1,5},{2,6},{3,7},{4,8},{5,9},{6,10},{7,11},{8,12},{9,13},{1... | collective-permute-start | bytes 393224 | tf_op jit(solution)/shard_map/ppermute | solution.py:477
  110.5 15.6 %collective-permute-start.32 = (bf16[3,32,512]{2,1,0:T(8,128)(2,1)S(1)}, bf16[3,32,512]{2,1,0:T(8,128)(2,1)S(1)}, u32[]{:S(2)}, u32[]{:S(2)}) collective-permute-start(bf16[3,32,512]{2,1,0:T(8,128)(2,1)S(1)} %get-tuple-element.148), channel_id=1, source_target_pairs={{0,8},{1,9},{2,10},{3,11},{4,12},{5,13},{6,14},{7,15},{8,0},{9,1},... | collective-permute-start | bytes 294920 | tf_op jit(solution)/shard_map/ppermute | solution.py:477
  112.4 13.8 %collective-permute-start.33 = (bf16[3,32,512]{2,1,0:T(8,128)(2,1)S(1)}, bf16[3,32,512]{2,1,0:T(8,128)(2,1)S(1)}, u32[]{:S(2)}, u32[]{:S(2)}) collective-permute-start(bf16[3,32,512]{2,1,0:T(8,128)(2,1)S(1)} %get-tuple-element.149), channel_id=1, source_target_pairs={{0,12},{1,13},{2,14},{3,15},{4,0},{5,1},{6,2},{7,3},{8,4},{9,5},{1... | collective-permute-start | bytes 294920 | tf_op jit(solution)/shard_map/ppermute | solution.py:477
  126.3 16.6 %collective-permute-start.34 = (bf16[4,128,512]{2,1,0:T(8,128)(2,1)S(1)}, bf16[4,128,512]{2,1,0:T(8,128)(2,1)S(1)}, u32[]{:S(2)}, u32[]{:S(2)}) collective-permute-start(bf16[4,128,512]{2,1,0:T(8,128)(2,1)S(1)} %shard_map.188.refs_5_.refs_1_), channel_id=1, source_target_pairs={{0,2},{1,3},{2,0},{3,1},{4,6},{5,7},{6,4},{7,5},{8,10},{9,11},{10,... | collective-permute-start | bytes 1572872 | tf_op jit(solution)/shard_map/ppermute | solution.py:477
  128.9 6.2 %collective-permute-start.39 = (bf16[3,32,512]{2,1,0:T(8,128)(2,1)S(1)}, bf16[3,32,512]{2,1,0:T(8,128)(2,1)S(1)}, u32[]{:S(2)}, u32[]{:S(2)}) collective-permute-start(bf16[3,32,512]{2,1,0:T(8,128)(2,1)S(1)} %shard_map.187.refs_5_.refs_1_), channel_id=1, source_target_pairs={{0,12},{1,13},{2,14},{3,15},{4,0},{5,1},{6,2},{7,3},{8,4},{9,5},{1... | collective-permute-start | bytes 294920 | tf_op jit(solution)/shard_map/ppermute | solution.py:477
  131.9 9.3 %collective-permute-start.38 = (bf16[3,32,512]{2,1,0:T(8,128)(2,1)S(1)}, bf16[3,32,512]{2,1,0:T(8,128)(2,1)S(1)}, u32[]{:S(2)}, u32[]{:S(2)}) collective-permute-start(bf16[3,32,512]{2,1,0:T(8,128)(2,1)S(1)} %shard_map.187.refs_5_.refs_1_), channel_id=1, source_target_pairs={{0,8},{1,9},{2,10},{3,11},{4,12},{5,13},{6,14},{7,15},{8,0},{9,1},... | collective-permute-start | bytes 294920 | tf_op jit(solution)/shard_map/ppermute | solution.py:477
  132.0 9.2 %collective-permute-start.37 = (bf16[3,32,512]{2,1,0:T(8,128)(2,1)S(1)}, bf16[3,32,512]{2,1,0:T(8,128)(2,1)S(1)}, u32[]{:S(2)}, u32[]{:S(2)}) collective-permute-start(bf16[3,32,512]{2,1,0:T(8,128)(2,1)S(1)} %shard_map.187.refs_5_.refs_1_), channel_id=1, source_target_pairs={{0,4},{1,5},{2,6},{3,7},{4,8},{5,9},{6,10},{7,11},{8,12},{9,13},{1... | collective-permute-start | bytes 294920 | tf_op jit(solution)/shard_map/ppermute | solution.py:477
  141.3 11.0 %collective-permute-start.40 = (bf16[3,128,512]{2,1,0:T(8,128)(2,1)S(1)}, bf16[3,128,512]{2,1,0:T(8,128)(2,1)S(1)}, u32[]{:S(2)}, u32[]{:S(2)}) collective-permute-start(bf16[3,128,512]{2,1,0:T(8,128)(2,1)S(1)} %shard_map.189.refs_5_.refs_1_), channel_id=1, source_target_pairs={{0,2},{1,3},{2,0},{3,1},{4,6},{5,7},{6,4},{7,5},{8,10},{9,11},{10,... | collective-permute-start | bytes 1179656 | tf_op jit(solution)/shard_map/ppermute | solution.py:477
  142.9 9.4 %collective-permute-start.35 = (bf16[4,128,512]{2,1,0:T(8,128)(2,1)S(1)}, bf16[4,128,512]{2,1,0:T(8,128)(2,1)S(1)}, u32[]{:S(2)}, u32[]{:S(2)}) collective-permute-start(bf16[4,128,512]{2,1,0:T(8,128)(2,1)S(1)} %shard_map.188.refs_5_.refs_1_), channel_id=1, source_target_pairs={{0,1},{1,0},{2,3},{3,2},{4,5},{5,4},{6,7},{7,6},{8,9},{9,8},{10,11... | collective-permute-start | bytes 1572872 | tf_op jit(solution)/shard_map/ppermute | solution.py:477
  142.9 9.4 %collective-permute-start.36 = (bf16[4,128,512]{2,1,0:T(8,128)(2,1)S(1)}, bf16[4,128,512]{2,1,0:T(8,128)(2,1)S(1)}, u32[]{:S(2)}, u32[]{:S(2)}) collective-permute-start(bf16[4,128,512]{2,1,0:T(8,128)(2,1)S(1)} %collective-permute-done.34.refs_2_), channel_id=1, source_target_pairs={{0,1},{1,0},{2,3},{3,2},{4,5},{5,4},{6,7},{7,6},{8,9},{9,8},{10,11... | collective-permute-start | bytes 1572872 | tf_op jit(solution)/shard_map/ppermute | solution.py:477
  143.4 10.4 %collective-permute-start.41 = (bf16[3,128,512]{2,1,0:T(8,128)(2,1)S(1)}, bf16[3,128,512]{2,1,0:T(8,128)(2,1)S(1)}, u32[]{:S(2)}, u32[]{:S(2)}) collective-permute-start(bf16[3,128,512]{2,1,0:T(8,128)(2,1)S(1)} %shard_map.189.refs_5_.refs_1_), channel_id=1, source_target_pairs={{0,1},{1,0},{2,3},{3,2},{4,5},{5,4},{6,7},{7,6},{8,9},{9,8},{10,11... | collective-permute-start | bytes 1179656 | tf_op jit(solution)/shard_map/ppermute | solution.py:477
  152.3 1.7 %collective-permute-start.42 = (bf16[3,128,512]{2,1,0:T(8,128)(2,1)S(1)}, bf16[3,128,512]{2,1,0:T(8,128)(2,1)S(1)}, u32[]{:S(2)}, u32[]{:S(2)}) collective-permute-start(bf16[3,128,512]{2,1,0:T(8,128)(2,1)S(1)} %collective-permute-done.40.refs_2_), channel_id=1, source_target_pairs={{0,1},{1,0},{2,3},{3,2},{4,5},{5,4},{6,7},{7,6},{8,9},{9,8},{10,11... | collective-permute-start | bytes 1179656 | tf_op jit(solution)/shard_map/ppermute | solution.py:477

commit v7 on v6

--- a/solution.py
+++ b/solution.py
@@ -530,7 +530,8 @@
 
 
 def join_stage(me, mine, members, blocks, shapes, after):
-    pieces = [mine] + [in_group(mine, "band", 2, members, j) for j in range(1, members)]
+    pieces = [in_group(mine, "band", 2, members, j) for j in range(1, members)]
+    pieces = [mine] + [held_until(piece, after) if after else piece for piece in pieces]
     others = [in_group(one, "band", 1, 2, 1) for one in pieces]
     return call(
         functools.partial(join_kernel, (members, blocks)),
@@ -540,7 +541,6 @@
         *pieces,
         *others,
         smem=(0,),
-        after=after,
         last=range(len(shapes)),
     )
 
@@ -813,22 +813,24 @@
     edge_shapes = [(3 * width, width), (width, width)]
     if width // 2 % (16 * first * second) == 0:
         along_y, along_z = (2, first), (2 * first, second)
-        sent_edge = held_until(sent_edge, back_far)
+        sent_edge = held_until(sent_edge, back_far[-1:])
         came_edge = [in_group(sent_edge, "band", 1, 2, 1)]
         keep_node, sent_node = node_weights([sent_edge])
         came_node = [in_group(sent_node, "band", 1, 2, 1)]
         keep_edge, came_edge = add_stage(me, keep_edge, came_edge, *along_y, f32, [keep_node])
+        edge_new, grad_edges = edge_outputs([keep_edge])
+        keep_edge, came_edge = add_stage(
+            me, keep_edge, came_edge, *along_z, f32, [in_hbm(edge_new)] + back_near + back_far[:-1]
+        )
         keep_node, came_node = add_stage(me, keep_node, came_node, *along_y, f32, [keep_edge])
-        edge_new, grad_edges = edge_outputs([keep_node])
-        keep_edge, came_edge = add_stage(me, keep_edge, came_edge, *along_z, f32, [in_hbm(edge_new)])
-        grad_nodes = node_output([keep_edge])
-        keep_node, came_node = add_stage(me, keep_node, came_node, *along_z, f32, [in_hbm(grad_nodes)])
-        piece_edge, _ = add_stage(me, keep_edge, came_edge, 1, 1, bf16, [keep_node])
-        piece_node, _ = add_stage(me, keep_node, came_node, 1, 1, bf16, [piece_edge])
-        mine_edge = gather_stage(me, piece_edge, *along_z, [piece_node])
-        mine_node = gather_stage(me, piece_node, *along_z, [mine_edge])
-        grad_e1, grad_e2 = join_stage(me, mine_edge, first, edge_blocks, edge_shapes, [mine_node])
-        grad_n1, grad_n2 = join_stage(me, mine_node, first, node_blocks, node_shapes, [in_hbm(grad_e2)])
+        grad_nodes = node_output([keep_node])
+        piece_edge, _ = add_stage(me, keep_edge, came_edge, 1, 1, bf16, [in_hbm(grad_nodes)])
+        keep_node, came_node = add_stage(me, keep_node, came_node, *along_z, f32, [piece_edge])
+        mine_edge = gather_stage(me, piece_edge, *along_z, [keep_node])
+        piece_node, _ = add_stage(me, keep_node, came_node, 1, 1, bf16, [mine_edge])
+        grad_e1, grad_e2 = join_stage(me, mine_edge, first, edge_blocks, edge_shapes, [piece_node])
+        mine_node = gather_stage(me, piece_node, *along_z, [in_hbm(grad_e2)])
+        grad_n1, grad_n2 = join_stage(me, mine_node, first, node_blocks, node_shapes, [])
     else:
         whole = reduce_whole(*node_weights([]))
         grad_n1, grad_n2 = whole[:2].reshape(2 * width, width), whole[2]

time: 155 us -> 162 us (1.045)
  starting transfers between devices: 61.7 us -> 67.4 us
    ppermute x21, starting transfers between devices: 36.8 us -> 46.7 us  [passed_along(): return lax.ppermute(block, axis, route)]
    ppermute x22, starting transfers between devices: 24.9 us -> 20.7 us  [in_group(): return lax.ppermute(block, axis, route)]
  transfers between devices with their start and end apart: 43 -> 43, of which waited for: 16 -> 18; matrix products, arithmetic and copies ran while one was open for 0% -> 0% of each run, Pallas kernels for 16% -> 15%
where the time goes in v7:
time: 162 us
  starting transfers between devices  67.4 us (42%)
  waiting for transfers between devices  62.5 us (39%)
  Pallas kernels  31.2 us (19%)
    ppermute x21, starting transfers between devices, passed_along(): return lax.ppermute(block, axis, route)  46.7 us
    ppermute x22, waiting for transfers between devices, in_group(): return lax.ppermute(block, axis, route)  45.8 us
    pallas_call x20, Pallas kernels, call(): pl.pallas_call(kernel, out_shape=[(pltpu.HBM if i in last else pltpu.VMEM...  27.9 us
    ppermute x22, starting transfers between devices, in_group(): return lax.ppermute(block, axis, route)  20.7 us
    ppermute x21, waiting for transfers between devices, passed_along(): return lax.ppermute(block, axis, route)  16.8 us
  transfers between devices with their start and end apart: 43, of which 18 were waited for; matrix products, arithmetic and copies ran while one was open for 0% of the time, Pallas kernels for 15%

profile of v7, /device:TPU:0, one launch (start us, length us, event | category | flops | bytes accessed | tf_op | source)
XLA Modules:
  0.0 161.9 jit_solution(295540044559694968)
XLA Ops:
  0.6 4.1 %collective-permute-start.6 = (s32[11,1,128]{2,1,0:T(1,128)}, s32[11,1,128]{2,1,0:T(1,128)S(1)}, u32[]{:S(2)}, u32[]{:S(2)}) collective-permute-start(s32[11,1,128]{2,1,0:T(1,128)} %bitcast.11), channel_id=1, source_target_pairs={{8,0},{9,1},{10,2},{11,3},{12,4},{13,5},{14,6},{15,7},{0,8},{1,9},... | collective-permute-start | bytes 16904 | tf_op jit(solution)/shard_map/ppermute | solution.py:21
  4.7 1.6 collective-permute-start.5
  6.3 2.2 %collective-permute-start.4 = (s32[11,1,128]{2,1,0:T(1,128)}, s32[11,1,128]{2,1,0:T(1,128)S(1)}, u32[]{:S(2)}, u32[]{:S(2)}) collective-permute-start(s32[11,1,128]{2,1,0:T(1,128)} %bitcast.13), channel_id=1, source_target_pairs={{4,0},{5,1},{6,2},{7,3},{8,4},{9,5},{10,6},{11,7},{12,8},{13,9},{1... | collective-permute-start | bytes 16904 | tf_op jit(solution)/shard_map/ppermute | solution.py:21
  8.6 1.5 collective-permute-start.3
  10.1 3.2 %collective-permute-start.2 = (s32[11,1,128]{2,1,0:T(1,128)}, s32[11,1,128]{2,1,0:T(1,128)S(1)}, u32[]{:S(2)}, u32[]{:S(2)}) collective-permute-start(s32[11,1,128]{2,1,0:T(1,128)} %bitcast.15), channel_id=1, source_target_pairs={{2,0},{3,1},{4,2},{5,3},{6,4},{7,5},{8,6},{9,7},{10,8},{11,9},{12,... | collective-permute-start | bytes 16904 | tf_op jit(solution)/shard_map/ppermute | solution.py:21
  13.3 4.4 %collective-permute-start = (s32[11,1,128]{2,1,0:T(1,128)}, s32[11,1,128]{2,1,0:T(1,128)S(1)}, u32[]{:S(2)}, u32[]{:S(2)}) collective-permute-start(s32[11,1,128]{2,1,0:T(1,128)} %bitcast.17), channel_id=1, source_target_pairs={{1,0},{2,1},{3,2},{4,3},{5,4},{6,5},{7,6},{8,7},{9,8},{10,9},{11,1... | collective-permute-start | bytes 16904 | tf_op jit(solution)/shard_map/ppermute | solution.py:21
  17.7 3.2 %shard_map.170 = (bf16[320,512]{1,0:T(8,128)(2,1)S(1)}, s32[11,1,128]{2,1,0:T(1,128)S(1)}, s32[11,1,128]{2,1,0:T(1,128)S(1)}, bf16[11,128,512]{2,1,0:T(8,128)(2,...) custom-call(s32[1]{0:T(128)} %bitcast.refs_0_.refs_2_, ...), custom_call_target="tpu_custom_call" | custom-call | flops 1 | bytes 1 | tf_op jit(solution)/shard_map/pallas_call | solution.py:120
  21.8 2.7 %collective-permute-start.8 = (bf16[128,512]{1,0:T(8,128)(2,1)S(1)}, bf16[128,512]{1,0:T(8,128)(2,1)S(1)}, u32[]{:S(2)}, u32[]{:S(2)}) collective-permute-start(bf16[128,512]{1,0:T(8,128)(2,1)S(1)} %get-tuple-element.94), channel_id=1, source_target_pairs={{1,0},{2,1},{3,2},{4,3},{5,4},{6,5},{7,6},{8,7},{9,8},{10,9},{11,1... | collective-permute-start | bytes 393224 | tf_op jit(solution)/shard_map/ppermute | solution.py:21
  24.5 4.7 %collective-permute-start.10 = (bf16[128,512]{1,0:T(8,128)(2,1)S(1)}, bf16[128,512]{1,0:T(8,128)(2,1)S(1)}, u32[]{:S(2)}, u32[]{:S(2)}) collective-permute-start(bf16[128,512]{1,0:T(8,128)(2,1)S(1)} %get-tuple-element.96), channel_id=1, source_target_pairs={{2,0},{3,1},{4,2},{5,3},{6,4},{7,5},{8,6},{9,7},{10,8},{11,9},{12,... | collective-permute-start | bytes 393224 | tf_op jit(solution)/shard_map/ppermute | solution.py:21
  29.2 4.1 %collective-permute-done.9.refs_8_.refs_7_ = bf16[128,512]{1,0:T(8,128)(2,1)S(1)} collective-permute-done((bf16[128,512]{1,0:T(8,128)(2,1)S(1)}, bf16[128,512]{1,0:T(8,128)(2,1)S(1)}, u32[]{:S(2)}, u32[]{:S(2)}) %collective-permute-start.9) | collective-permute-done | bytes 131104 | tf_op jit(solution)/shard_map/ppermute | solution.py:21
  33.4 4.5 %shard_map.172 = (bf16[1408,320]{1,0:T(8,128)(2,1)S(1)}, bf16[320,1408]{1,0:T(8,128)(2,1)S(1)}, f32[1408,128]{1,0:T(8,128)S(1)}, f32[1024,512]{1,0:T(8,128)S(1)}...) custom-call(bf16[11,128,512]{2,1,0:T(8,128)(2,1)S(1)} %get-tuple-ele, ...), custom_call_target="tpu_custom_call" | custom-call | flops 1 | bytes 1 | tf_op jit(solution)/shard_map/pallas_call | solution.py:89
  37.9 1.6 shard_map.173
  39.9 4.5 %shard_map.174 = (bf16[128,512]{1,0:T(8,128)(2,1)S(1)}, bf16[128,512]{1,0:T(8,128)(2,1)S(1)}, bf16[256,512]{1,0:T(8,128)(2,1)S(1)}, bf16[512,512]{1,0:T(8,128)(2...) custom-call(bf16[11,128,512]{2,1,0:T(8,128)(2,1)S(1)} %get-tuple-ele, ...), custom_call_target="tpu_custom_call" | custom-call | flops 1 | bytes 1 | tf_op jit(solution)/shard_map/pallas_call | solution.py:89
  44.4 4.6 %collective-permute-start.14 = (bf16[256,512]{1,0:T(8,128)(2,1)S(1)}, bf16[256,512]{1,0:T(8,128)(2,1)S(1)}, u32[]{:S(2)}, u32[]{:S(2)}) collective-permute-start(bf16[256,512]{1,0:T(8,128)(2,1)S(1)} %get-tuple-element.120.refs_19_.refs_14_), channel_id=1, source_target_pairs={{8,0},{9,1},{10,2},{11,3},{12,4},{13,5},{14,6},{15,7},{0,8},{1,9},... | collective-permute-start | bytes 786440 | tf_op jit(solution)/shard_map/ppermute | solution.py:21
  49.0 2.1 %shard_map.175 = (bf16[896,512]{1,0:T(8,128)(2,1)S(1)}, bf16[384,512]{1,0:T(8,128)(2,1)S(1)}, bf16[128,512]{1,0:T(8,128)(2,1)S(1)}, bf16[128,512]{1,0:T(8,128)(2...) custom-call(bf16[11,128,512]{2,1,0:T(8,128)(2,1)S(1)} %get-tuple-element.81.refs_0_.refs_1_, ...), custom_call_target="tpu_custom_call" | custom-call | flops 1 | bytes 1 | tf_op jit(solution)/shard_map/pallas_call | solution.py:89
  51.0 3.9 %shard_map.176 = (f32[4,256,512]{2,1,0:T(8,128)S(1)}, bf16[4,256,512]{2,1,0:T(8,128)(2,1)S(1)}, bf16[320,512]{1,0:T(8,128)(2,1)S(1)}) custom-call(bf16[11,128,512]{2,1,0:T(8,128)(2,1)S(1)} %get-tuple-element.82.refs_0_, bf16[320,1408]{1,0:T(8,128)(2,1)S(1)} %get-tuple-element.92.refs_2_.refs_4_.refs_1_, s32[1]{0:T(128)} %bitcast.refs_0_.refs_2_, ...), custom_call_target="tpu_custom_call" | custom-call | flops 1 | bytes 1 | tf_op jit(solution)/shard_map/pallas_call | solution.py:89
  54.9 6.3 %collective-permute-done.14.refs_1_.refs_17_ = bf16[256,512]{1,0:T(8,128)(2,1)S(1)} collective-permute-done((bf16[256,512]{1,0:T(8,128)(2,1)S(1)}, bf16[256,512]{1,0:T(8,128)(2,1)S(1)}, u32[]{:S(2)}, u32[]{:S(2)}) %collective-permute-start.14) | collective-permute-done | bytes 262176 | tf_op jit(solution)/shard_map/ppermute | solution.py:21
  61.6 1.5 shard_map.178
  64.1 0.8 collective-permute-start.17
  64.9 2.4 %collective-permute-start.18 = (bf16[128,512]{1,0:T(8,128)(2,1)S(1)}, bf16[128,512]{1,0:T(8,128)(2,1)S(1)}, u32[]{:S(2)}, u32[]{:S(2)}) collective-permute-start(bf16[128,512]{1,0:T(8,128)(2,1)S(1)} %get-tuple-element.114.refs_13_.refs_8_), channel_id=1, source_target_pairs={{1,0},{2,1},{3,2},{4,3},{5,4},{6,5},{7,6},{8,7},{9,8},{10,9},{11,1... | collective-permute-start | bytes 393224 | tf_op jit(solution)/shard_map/ppermute | solution.py:21
  67.3 0.8 collective-permute-start.20
  68.2 1.7 %collective-permute-done.18.refs_4_.refs_11_ = bf16[128,512]{1,0:T(8,128)(2,1)S(1)} collective-permute-done((bf16[128,512]{1,0:T(8,128)(2,1)S(1)}, bf16[128,512]{1,0:T(8,128)(2,1)S(1)}, u32[]{:S(2)}, u32[]{:S(2)}) %collective-permute-start.18) | collective-permute-done | bytes 131104 | tf_op jit(solution)/shard_map/ppermute | solution.py:21
  69.8 12.2 %collective-permute-start.21 = (bf16[128,512]{1,0:T(8,128)(2,1)S(1)}, bf16[128,512]{1,0:T(8,128)(2,1)S(1)}, u32[]{:S(2)}, u32[]{:S(2)}) collective-permute-start(bf16[128,512]{1,0:T(8,128)(2,1)S(1)} %get-tuple-element.117.refs_16_.refs_11_), channel_id=1, source_target_pairs={{14,0},{15,1},{0,2},{1,3},{2,4},{3,5},{4,6},{5,7},{6,8},{7,9},{8,1... | collective-permute-start | bytes 393224 | tf_op jit(solution)/shard_map/ppermute | solution.py:21
  82.1 2.1 %collective-permute-start.22 = (bf16[128,512]{1,0:T(8,128)(2,1)S(1)}, bf16[128,512]{1,0:T(8,128)(2,1)S(1)}, u32[]{:S(2)}, u32[]{:S(2)}) collective-permute-start(bf16[128,512]{1,0:T(8,128)(2,1)S(1)} %get-tuple-element.118.refs_17_.refs_12_), channel_id=1, source_target_pairs={{4,0},{5,1},{6,2},{7,3},{8,4},{9,5},{10,6},{11,7},{12,8},{13,9},{1... | collective-permute-start | bytes 393224 | tf_op jit(solution)/shard_map/ppermute | solution.py:21
  84.2 3.6 %shard_map.180 = (bf16[11,128,512]{2,1,0:T(8,128)(2,1)}, bf16[11,128,512]{2,1,0:T(8,128)(2,1)}) custom-call(bf16[11,128,512]{2,1,0:T(8,128)(2,1)S(1)} %get-tuple-element.82.refs_0_, bf16[11,128,512]{2,1,0:T(8,128)(2,1)S(1)} %get-tuple-element.81.refs_0_.refs_1_, bf16[1536,512]{1,0:T(8,128)(2,1)S(1)} %get-tuple-element.85.refs_4_.refs_6_.refs_2_.refs_3_.refs_1_, ...), custom_call_target="tpu_custom_call" | custom-call | flops 1 | bytes 1 | tf_op jit(solution)/shard_map/pallas_call | solution.py:89
  87.8 4.1 %collective-permute-done.23.refs_9_.refs_16_ = bf16[128,512]{1,0:T(8,128)(2,1)S(1)} collective-permute-done((bf16[128,512]{1,0:T(8,128)(2,1)S(1)}, bf16[128,512]{1,0:T(8,128)(2,1)S(1)}, u32[]{:S(2)}, u32[]{:S(2)}) %collective-permute-start.23) | collective-permute-done | bytes 131104 | tf_op jit(solution)/shard_map/ppermute | solution.py:21
  92.2 2.7 %collective-permute-start.30 = (bf16[3,128,512]{2,1,0:T(8,128)(2,1)S(1)}, bf16[3,128,512]{2,1,0:T(8,128)(2,1)S(1)}, u32[]{:S(2)}, u32[]{:S(2)}) collective-permute-start(bf16[3,128,512]{2,1,0:T(8,128)(2,1)S(1)} %get-tuple-element.145), channel_id=1, source_target_pairs={{0,2},{1,3},{2,0},{3,1},{4,6},{5,7},{6,4},{7,5},{8,10},{9,11},{10,... | collective-permute-start | bytes 1179656 | tf_op jit(solution)/shard_map/ppermute | solution.py:477
  94.9 0.8 collective-permute-start.24
  95.7 1.2 collective-permute-start.25
  97.0 1.7 %collective-permute-start.26 = (bf16[4,32,512]{2,1,0:T(8,128)(2,1)S(1)}, bf16[4,32,512]{2,1,0:T(8,128)(2,1)S(1)}, u32[]{:S(2)}, u32[]{:S(2)}) collective-permute-start(bf16[4,32,512]{2,1,0:T(8,128)(2,1)S(1)} %get-tuple-element.144), channel_id=1, source_target_pairs={{0,12},{1,13},{2,14},{3,15},{4,0},{5,1},{6,2},{7,3},{8,4},{9,5},{1... | collective-permute-start | bytes 393224 | tf_op jit(solution)/shard_map/ppermute | solution.py:477
  99.2 1.6 %shard_map.184.refs_5_ = bf16[320,512]{1,0:T(8,128)(2,1)} custom-call(f32[320,512]{1,0:T(8,128)S(1)} %shard_map.183.refs_0_, bf16[1536,512]{1,0:T(8,128)(2,1)S(1)} %get-tuple-element.85.refs_4_.refs_6_.refs_2_.refs_3_.refs_1_, s32[11,1,128]{2,1,0:T(1,128)S(1)} %get-tuple-element.84.refs_2_, s32[11,1,128]{2,1,0:T(1,128)S(1)} %collective-permute-done.refs_1_.refs_3_, ...), custom_call_target="tpu_custom_call" | custom-call | flops 1 | bytes 1 | tf_op jit(solution)/shard_map/pallas_call | solution.py:89
  100.9 2.2 %collective-permute-done.24.refs_2_ = bf16[4,32,512]{2,1,0:T(8,128)(2,1)S(1)} collective-permute-done((bf16[4,32,512]{2,1,0:T(8,128)(2,1)S(1)}, bf16[4,32,512]{2,1,0:T(8,128)(2,1)S(1)}, u32[]{:S(2)}, u32[]{:S(2)}) %collective-permute-start.24) | collective-permute-done | bytes 131104 | tf_op jit(solution)/shard_map/ppermute | solution.py:477
  103.1 4.6 %collective-permute-done.25.refs_3_ = bf16[4,32,512]{2,1,0:T(8,128)(2,1)S(1)} collective-permute-done((bf16[4,32,512]{2,1,0:T(8,128)(2,1)S(1)}, bf16[4,32,512]{2,1,0:T(8,128)(2,1)S(1)}, u32[]{:S(2)}, u32[]{:S(2)}) %collective-permute-start.25) | collective-permute-done | bytes 131104 | tf_op jit(solution)/shard_map/ppermute | solution.py:477
  107.8 2.5 %collective-permute-start.29 = (bf16[4,32,512]{2,1,0:T(8,128)(2,1)S(1)}, bf16[4,32,512]{2,1,0:T(8,128)(2,1)S(1)}, u32[]{:S(2)}, u32[]{:S(2)}) collective-permute-start(bf16[4,32,512]{2,1,0:T(8,128)(2,1)S(1)} %shard_map.185.refs_3_.refs_1_), channel_id=1, source_target_pairs={{0,12},{1,13},{2,14},{3,15},{4,0},{5,1},{6,2},{7,3},{8,4},{9,5},{1... | collective-permute-start | bytes 393224 | tf_op jit(solution)/shard_map/ppermute | solution.py:477
  110.3 1.9 %collective-permute-start.28 = (bf16[4,32,512]{2,1,0:T(8,128)(2,1)S(1)}, bf16[4,32,512]{2,1,0:T(8,128)(2,1)S(1)}, u32[]{:S(2)}, u32[]{:S(2)}) collective-permute-start(bf16[4,32,512]{2,1,0:T(8,128)(2,1)S(1)} %shard_map.185.refs_3_.refs_1_), channel_id=1, source_target_pairs={{0,8},{1,9},{2,10},{3,11},{4,12},{5,13},{6,14},{7,15},{8,0},{9,1},... | collective-permute-start | bytes 393224 | tf_op jit(solution)/shard_map/ppermute | solution.py:477
  112.3 1.7 %collective-permute-done.29.refs_4_ = bf16[4,32,512]{2,1,0:T(8,128)(2,1)S(1)} collective-permute-done((bf16[4,32,512]{2,1,0:T(8,128)(2,1)S(1)}, bf16[4,32,512]{2,1,0:T(8,128)(2,1)S(1)}, u32[]{:S(2)}, u32[]{:S(2)}) %collective-permute-start.29) | collective-permute-done | bytes 131104 | tf_op jit(solution)/shard_map/ppermute | solution.py:477
  114.0 9.6 %collective-permute-done.28.refs_3_ = bf16[4,32,512]{2,1,0:T(8,128)(2,1)S(1)} collective-permute-done((bf16[4,32,512]{2,1,0:T(8,128)(2,1)S(1)}, bf16[4,32,512]{2,1,0:T(8,128)(2,1)S(1)}, u32[]{:S(2)}, u32[]{:S(2)}) %collective-permute-start.28) | collective-permute-done | bytes 131104 | tf_op jit(solution)/shard_map/ppermute | solution.py:477
  124.8 3.1 %collective-permute-start.34 = (bf16[3,32,512]{2,1,0:T(8,128)(2,1)S(1)}, bf16[3,32,512]{2,1,0:T(8,128)(2,1)S(1)}, u32[]{:S(2)}, u32[]{:S(2)}) collective-permute-start(bf16[3,32,512]{2,1,0:T(8,128)(2,1)S(1)} %get-tuple-element.149), channel_id=1, source_target_pairs={{0,12},{1,13},{2,14},{3,15},{4,0},{5,1},{6,2},{7,3},{8,4},{9,5},{1... | collective-permute-start | bytes 294920 | tf_op jit(solution)/shard_map/ppermute | solution.py:477
  127.9 3.5 %collective-permute-done.32.refs_2_ = bf16[3,32,512]{2,1,0:T(8,128)(2,1)S(1)} collective-permute-done((bf16[3,32,512]{2,1,0:T(8,128)(2,1)S(1)}, bf16[3,32,512]{2,1,0:T(8,128)(2,1)S(1)}, u32[]{:S(2)}, u32[]{:S(2)}) %collective-permute-start.32) | collective-permute-done | bytes 98336 | tf_op jit(solution)/shard_map/ppermute | solution.py:477
  131.4 2.2 %collective-permute-done.33.refs_3_ = bf16[3,32,512]{2,1,0:T(8,128)(2,1)S(1)} collective-permute-done((bf16[3,32,512]{2,1,0:T(8,128)(2,1)S(1)}, bf16[3,32,512]{2,1,0:T(8,128)(2,1)S(1)}, u32[]{:S(2)}, u32[]{:S(2)}) %collective-permute-start.33) | collective-permute-done | bytes 98336 | tf_op jit(solution)/shard_map/ppermute | solution.py:477
  133.7 2.8 %collective-permute-done.31.refs_0_ = bf16[4,128,512]{2,1,0:T(8,128)(2,1)S(1)} collective-permute-done((bf16[4,128,512]{2,1,0:T(8,128)(2,1)S(1)}, bf16[4,128,512]{2,1,0:T(8,128)(2,1)S(1)}, u32[]{:S(2)}, u32[]{:S(2)}) %collective-permute-start.31) | collective-permute-done | bytes 524320 | tf_op jit(solution)/shard_map/ppermute | solution.py:477
  136.5 1.7 %collective-permute-start.38 = (bf16[3,32,512]{2,1,0:T(8,128)(2,1)S(1)}, bf16[3,32,512]{2,1,0:T(8,128)(2,1)S(1)}, u32[]{:S(2)}, u32[]{:S(2)}) collective-permute-start(bf16[3,32,512]{2,1,0:T(8,128)(2,1)S(1)} %shard_map.188.refs_1_), channel_id=1, source_target_pairs={{0,8},{1,9},{2,10},{3,11},{4,12},{5,13},{6,14},{7,15},{8,0},{9,1},... | collective-permute-start | bytes 294920 | tf_op jit(solution)/shard_map/ppermute | solution.py:477
  138.2 2.0 %collective-permute-start.37 = (bf16[3,32,512]{2,1,0:T(8,128)(2,1)S(1)}, bf16[3,32,512]{2,1,0:T(8,128)(2,1)S(1)}, u32[]{:S(2)}, u32[]{:S(2)}) collective-permute-start(bf16[3,32,512]{2,1,0:T(8,128)(2,1)S(1)} %shard_map.188.refs_1_), channel_id=1, source_target_pairs={{0,4},{1,5},{2,6},{3,7},{4,8},{5,9},{6,10},{7,11},{8,12},{9,13},{1... | collective-permute-start | bytes 294920 | tf_op jit(solution)/shard_map/ppermute | solution.py:477
  140.1 1.5 shard_map.190
  141.8 6.1 %collective-permute-done.38.refs_3_ = bf16[3,32,512]{2,1,0:T(8,128)(2,1)S(1)} collective-permute-done((bf16[3,32,512]{2,1,0:T(8,128)(2,1)S(1)}, bf16[3,32,512]{2,1,0:T(8,128)(2,1)S(1)}, u32[]{:S(2)}, u32[]{:S(2)}) %collective-permute-start.38) | collective-permute-done | bytes 98336 | tf_op jit(solution)/shard_map/ppermute | solution.py:477
  148.4 10.6 %collective-permute-done.40.refs_2_ = bf16[3,128,512]{2,1,0:T(8,128)(2,1)S(1)} collective-permute-done((bf16[3,128,512]{2,1,0:T(8,128)(2,1)S(1)}, bf16[3,128,512]{2,1,0:T(8,128)(2,1)S(1)}, u32[]{:S(2)}, u32[]{:S(2)}) %collective-permute-start.40) | collective-permute-done | bytes 393248 | tf_op jit(solution)/shard_map/ppermute | solution.py:477
  159.0 1.7 %collective-permute-done.42.refs_4_ = bf16[3,128,512]{2,1,0:T(8,128)(2,1)S(1)} collective-permute-done((bf16[3,128,512]{2,1,0:T(8,128)(2,1)S(1)}, bf16[3,128,512]{2,1,0:T(8,128)(2,1)S(1)}, u32[]{:S(2)}, u32[]{:S(2)}) %collective-permute-start.42) | collective-permute-done | bytes 393248 | tf_op jit(solution)/shard_map/ppermute | solution.py:477
  160.7 1.3 shard_map.192
  (61 shorter events, 5.8 us)
Async XLA Ops:
  0.6 12.7 %collective-permute-start.6 = (s32[11,1,128]{2,1,0:T(1,128)}, s32[11,1,128]{2,1,0:T(1,128)S(1)}, u32[]{:S(2)}, u32[]{:S(2)}) collective-permute-start(s32[11,1,128]{2,1,0:T(1,128)} %bitcast.11), channel_id=1, source_target_pairs={{8,0},{9,1},{10,2},{11,3},{12,4},{13,5},{14,6},{15,7},{0,8},{1,9},... | collective-permute-start | bytes 16904 | tf_op jit(solution)/shard_map/ppermute | solution.py:21
  4.7 8.6 %collective-permute-start.5 = (s32[11,1,128]{2,1,0:T(1,128)}, s32[11,1,128]{2,1,0:T(1,128)S(1)}, u32[]{:S(2)}, u32[]{:S(2)}) collective-permute-start(s32[11,1,128]{2,1,0:T(1,128)} %bitcast.12), channel_id=1, source_target_pairs={{12,0},{13,1},{14,2},{15,3},{0,4},{1,5},{2,6},{3,7},{4,8},{5,9},{6... | collective-permute-start | bytes 16904 | tf_op jit(solution)/shard_map/ppermute | solution.py:21
  6.3 14.7 %collective-permute-start.4 = (s32[11,1,128]{2,1,0:T(1,128)}, s32[11,1,128]{2,1,0:T(1,128)S(1)}, u32[]{:S(2)}, u32[]{:S(2)}) collective-permute-start(s32[11,1,128]{2,1,0:T(1,128)} %bitcast.13), channel_id=1, source_target_pairs={{4,0},{5,1},{6,2},{7,3},{8,4},{9,5},{10,6},{11,7},{12,8},{13,9},{1... | collective-permute-start | bytes 16904 | tf_op jit(solution)/shard_map/ppermute | solution.py:21
  8.6 12.4 %collective-permute-start.3 = (s32[11,1,128]{2,1,0:T(1,128)}, s32[11,1,128]{2,1,0:T(1,128)S(1)}, u32[]{:S(2)}, u32[]{:S(2)}) collective-permute-start(s32[11,1,128]{2,1,0:T(1,128)} %bitcast.14), channel_id=1, source_target_pairs={{14,0},{15,1},{0,2},{1,3},{2,4},{3,5},{4,6},{5,7},{6,8},{7,9},{8,1... | collective-permute-start | bytes 16904 | tf_op jit(solution)/shard_map/ppermute | solution.py:21
  10.1 10.9 %collective-permute-start.2 = (s32[11,1,128]{2,1,0:T(1,128)}, s32[11,1,128]{2,1,0:T(1,128)S(1)}, u32[]{:S(2)}, u32[]{:S(2)}) collective-permute-start(s32[11,1,128]{2,1,0:T(1,128)} %bitcast.15), channel_id=1, source_target_pairs={{2,0},{3,1},{4,2},{5,3},{6,4},{7,5},{8,6},{9,7},{10,8},{11,9},{12,... | collective-permute-start | bytes 16904 | tf_op jit(solution)/shard_map/ppermute | solution.py:21
  13.3 7.7 %collective-permute-start.1 = (s32[11,1,128]{2,1,0:T(1,128)}, s32[11,1,128]{2,1,0:T(1,128)S(1)}, u32[]{:S(2)}, u32[]{:S(2)}) collective-permute-start(s32[11,1,128]{2,1,0:T(1,128)} %bitcast.16), channel_id=1, source_target_pairs={{15,0},{0,1},{1,2},{2,3},{3,4},{4,5},{5,6},{6,7},{7,8},{8,9},{9,10... | collective-permute-start | bytes 16904 | tf_op jit(solution)/shard_map/ppermute | solution.py:21
  13.3 7.7 %collective-permute-start = (s32[11,1,128]{2,1,0:T(1,128)}, s32[11,1,128]{2,1,0:T(1,128)S(1)}, u32[]{:S(2)}, u32[]{:S(2)}) collective-permute-start(s32[11,1,128]{2,1,0:T(1,128)} %bitcast.17), channel_id=1, source_target_pairs={{1,0},{2,1},{3,2},{4,3},{5,4},{6,5},{7,6},{8,7},{9,8},{10,9},{11,1... | collective-permute-start | bytes 16904 | tf_op jit(solution)/shard_map/ppermute | solution.py:21
  21.8 7.4 %collective-permute-start.8 = (bf16[128,512]{1,0:T(8,128)(2,1)S(1)}, bf16[128,512]{1,0:T(8,128)(2,1)S(1)}, u32[]{:S(2)}, u32[]{:S(2)}) collective-permute-start(bf16[128,512]{1,0:T(8,128)(2,1)S(1)} %get-tuple-element.94), channel_id=1, source_target_pairs={{1,0},{2,1},{3,2},{4,3},{5,4},{6,5},{7,6},{8,7},{9,8},{10,9},{11,1... | collective-permute-start | bytes 393224 | tf_op jit(solution)/shard_map/ppermute | solution.py:21
  24.5 8.9 %collective-permute-start.9 = (bf16[128,512]{1,0:T(8,128)(2,1)S(1)}, bf16[128,512]{1,0:T(8,128)(2,1)S(1)}, u32[]{:S(2)}, u32[]{:S(2)}) collective-permute-start(bf16[128,512]{1,0:T(8,128)(2,1)S(1)} %get-tuple-element.95), channel_id=1, source_target_pairs={{14,0},{15,1},{0,2},{1,3},{2,4},{3,5},{4,6},{5,7},{6,8},{7,9},{8,1... | collective-permute-start | bytes 393224 | tf_op jit(solution)/shard_map/ppermute | solution.py:21
  24.5 15.4 %collective-permute-start.13 = (bf16[256,512]{1,0:T(8,128)(2,1)S(1)}, bf16[256,512]{1,0:T(8,128)(2,1)S(1)}, u32[]{:S(2)}, u32[]{:S(2)}) collective-permute-start(bf16[256,512]{1,0:T(8,128)(2,1)S(1)} %get-tuple-element.103), channel_id=1, source_target_pairs={{8,0},{9,1},{10,2},{11,3},{12,4},{13,5},{14,6},{15,7},{0,8},{1,9},... | collective-permute-start | bytes 786440 | tf_op jit(solution)/shard_map/ppermute | solution.py:21
  24.5 13.4 %collective-permute-start.10 = (bf16[128,512]{1,0:T(8,128)(2,1)S(1)}, bf16[128,512]{1,0:T(8,128)(2,1)S(1)}, u32[]{:S(2)}, u32[]{:S(2)}) collective-permute-start(bf16[128,512]{1,0:T(8,128)(2,1)S(1)} %get-tuple-element.96), channel_id=1, source_target_pairs={{2,0},{3,1},{4,2},{5,3},{6,4},{7,5},{8,6},{9,7},{10,8},{11,9},{12,... | collective-permute-start | bytes 393224 | tf_op jit(solution)/shard_map/ppermute | solution.py:21
  29.2 8.7 %collective-permute-start.7 = (bf16[128,512]{1,0:T(8,128)(2,1)S(1)}, bf16[128,512]{1,0:T(8,128)(2,1)S(1)}, u32[]{:S(2)}, u32[]{:S(2)}) collective-permute-start(bf16[128,512]{1,0:T(8,128)(2,1)S(1)} %get-tuple-element.88.refs_7_), channel_id=1, source_target_pairs={{15,0},{0,1},{1,2},{2,3},{3,4},{4,5},{5,6},{6,7},{7,8},{8,9},{9,10... | collective-permute-start | bytes 393224 | tf_op jit(solution)/shard_map/ppermute | solution.py:21
  29.2 10.3 %collective-permute-start.11 = (bf16[128,512]{1,0:T(8,128)(2,1)S(1)}, bf16[128,512]{1,0:T(8,128)(2,1)S(1)}, u32[]{:S(2)}, u32[]{:S(2)}) collective-permute-start(bf16[128,512]{1,0:T(8,128)(2,1)S(1)} %get-tuple-element.101), channel_id=1, source_target_pairs={{12,0},{13,1},{14,2},{15,3},{0,4},{1,5},{2,6},{3,7},{4,8},{5,9},{6... | collective-permute-start | bytes 393224 | tf_op jit(solution)/shard_map/ppermute | solution.py:21
  33.4 6.6 %collective-permute-start.12 = (bf16[128,512]{1,0:T(8,128)(2,1)S(1)}, bf16[128,512]{1,0:T(8,128)(2,1)S(1)}, u32[]{:S(2)}, u32[]{:S(2)}) collective-permute-start(bf16[128,512]{1,0:T(8,128)(2,1)S(1)} %get-tuple-element.102), channel_id=1, source_target_pairs={{4,0},{5,1},{6,2},{7,3},{8,4},{9,5},{10,6},{11,7},{12,8},{13,9},{1... | collective-permute-start | bytes 393224 | tf_op jit(solution)/shard_map/ppermute | solution.py:21
  44.4 16.8 %collective-permute-start.14 = (bf16[256,512]{1,0:T(8,128)(2,1)S(1)}, bf16[256,512]{1,0:T(8,128)(2,1)S(1)}, u32[]{:S(2)}, u32[]{:S(2)}) collective-permute-start(bf16[256,512]{1,0:T(8,128)(2,1)S(1)} %get-tuple-element.120.refs_19_.refs_14_), channel_id=1, source_target_pairs={{8,0},{9,1},{10,2},{11,3},{12,4},{13,5},{14,6},{15,7},{0,8},{1,9},... | collective-permute-start | bytes 786440 | tf_op jit(solution)/shard_map/ppermute | solution.py:21
  61.2 2.7 %collective-permute-start.15 = (bf16[4,256,512]{2,1,0:T(8,128)(2,1)S(1)}, bf16[4,256,512]{2,1,0:T(8,128)(2,1)S(1)}, u32[]{:S(2)}, u32[]{:S(2)}) collective-permute-start(bf16[4,256,512]{2,1,0:T(8,128)(2,1)S(1)} %shard_map.177.refs_6_), channel_id=1, source_target_pairs={{0,1},{1,0},{2,3},{3,2},{4,5},{5,4},{6,7},{7,6},{8,9},{9,8},{10,11... | collective-permute-start | bytes 3145736 | tf_op jit(solution)/shard_map/ppermute | solution.py:477
  63.0 29.0 %collective-permute-start.16 = (bf16[3,256,512]{2,1,0:T(8,128)(2,1)S(1)}, bf16[3,256,512]{2,1,0:T(8,128)(2,1)S(1)}, u32[]{:S(2)}, u32[]{:S(2)}) collective-permute-start(bf16[3,256,512]{2,1,0:T(8,128)(2,1)S(1)} %get-tuple-element.137), channel_id=1, source_target_pairs={{0,1},{1,0},{2,3},{3,2},{4,5},{5,4},{6,7},{7,6},{8,9},{9,8},{10,11... | collective-permute-start | bytes 2359304 | tf_op jit(solution)/shard_map/ppermute | solution.py:477
  64.1 27.8 %collective-permute-start.17 = (bf16[4,128,512]{2,1,0:T(8,128)(2,1)S(1)}, bf16[4,128,512]{2,1,0:T(8,128)(2,1)S(1)}, u32[]{:S(2)}, u32[]{:S(2)}) collective-permute-start(bf16[4,128,512]{2,1,0:T(8,128)(2,1)S(1)} %get-tuple-element.138), channel_id=1, source_target_pairs={{0,2},{1,3},{2,0},{3,1},{4,6},{5,7},{6,4},{7,5},{8,10},{9,11},{10,... | collective-permute-start | bytes 1572872 | tf_op jit(solution)/shard_map/ppermute | solution.py:477
  64.9 4.9 %collective-permute-start.18 = (bf16[128,512]{1,0:T(8,128)(2,1)S(1)}, bf16[128,512]{1,0:T(8,128)(2,1)S(1)}, u32[]{:S(2)}, u32[]{:S(2)}) collective-permute-start(bf16[128,512]{1,0:T(8,128)(2,1)S(1)} %get-tuple-element.114.refs_13_.refs_8_), channel_id=1, source_target_pairs={{1,0},{2,1},{3,2},{4,3},{5,4},{6,5},{7,6},{8,7},{9,8},{10,9},{11,1... | collective-permute-start | bytes 393224 | tf_op jit(solution)/shard_map/ppermute | solution.py:21
  67.3 14.8 %collective-permute-start.19 = (bf16[128,512]{1,0:T(8,128)(2,1)S(1)}, bf16[128,512]{1,0:T(8,128)(2,1)S(1)}, u32[]{:S(2)}, u32[]{:S(2)}) collective-permute-start(bf16[128,512]{1,0:T(8,128)(2,1)S(1)} %get-tuple-element.115.refs_14_.refs_9_), channel_id=1, source_target_pairs={{15,0},{0,1},{1,2},{2,3},{3,4},{4,5},{5,6},{6,7},{7,8},{8,9},{9,10... | collective-permute-start | bytes 393224 | tf_op jit(solution)/shard_map/ppermute | solution.py:21
  67.3 16.8 %collective-permute-start.20 = (bf16[128,512]{1,0:T(8,128)(2,1)S(1)}, bf16[128,512]{1,0:T(8,128)(2,1)S(1)}, u32[]{:S(2)}, u32[]{:S(2)}) collective-permute-start(bf16[128,512]{1,0:T(8,128)(2,1)S(1)} %get-tuple-element.116.refs_15_.refs_10_), channel_id=1, source_target_pairs={{2,0},{3,1},{4,2},{5,3},{6,4},{7,5},{8,6},{9,7},{10,8},{11,9},{12,... | collective-permute-start | bytes 393224 | tf_op jit(solution)/shard_map/ppermute | solution.py:21
  69.8 17.9 %collective-permute-start.21 = (bf16[128,512]{1,0:T(8,128)(2,1)S(1)}, bf16[128,512]{1,0:T(8,128)(2,1)S(1)}, u32[]{:S(2)}, u32[]{:S(2)}) collective-permute-start(bf16[128,512]{1,0:T(8,128)(2,1)S(1)} %get-tuple-element.117.refs_16_.refs_11_), channel_id=1, source_target_pairs={{14,0},{15,1},{0,2},{1,3},{2,4},{3,5},{4,6},{5,7},{6,8},{7,9},{8,1... | collective-permute-start | bytes 393224 | tf_op jit(solution)/shard_map/ppermute | solution.py:21
  82.1 5.7 %collective-permute-start.22 = (bf16[128,512]{1,0:T(8,128)(2,1)S(1)}, bf16[128,512]{1,0:T(8,128)(2,1)S(1)}, u32[]{:S(2)}, u32[]{:S(2)}) collective-permute-start(bf16[128,512]{1,0:T(8,128)(2,1)S(1)} %get-tuple-element.118.refs_17_.refs_12_), channel_id=1, source_target_pairs={{4,0},{5,1},{6,2},{7,3},{8,4},{9,5},{10,6},{11,7},{12,8},{13,9},{1... | collective-permute-start | bytes 393224 | tf_op jit(solution)/shard_map/ppermute | solution.py:21
  84.2 7.7 %collective-permute-start.23 = (bf16[128,512]{1,0:T(8,128)(2,1)S(1)}, bf16[128,512]{1,0:T(8,128)(2,1)S(1)}, u32[]{:S(2)}, u32[]{:S(2)}) collective-permute-start(bf16[128,512]{1,0:T(8,128)(2,1)S(1)} %get-tuple-element.119.refs_18_.refs_13_), channel_id=1, source_target_pairs={{12,0},{13,1},{14,2},{15,3},{0,4},{1,5},{2,6},{3,7},{4,8},{5,9},{6... | collective-permute-start | bytes 393224 | tf_op jit(solution)/shard_map/ppermute | solution.py:21
  92.2 20.0 %collective-permute-start.30 = (bf16[3,128,512]{2,1,0:T(8,128)(2,1)S(1)}, bf16[3,128,512]{2,1,0:T(8,128)(2,1)S(1)}, u32[]{:S(2)}, u32[]{:S(2)}) collective-permute-start(bf16[3,128,512]{2,1,0:T(8,128)(2,1)S(1)} %get-tuple-element.145), channel_id=1, source_target_pairs={{0,2},{1,3},{2,0},{3,1},{4,6},{5,7},{6,4},{7,5},{8,10},{9,11},{10,... | collective-permute-start | bytes 1179656 | tf_op jit(solution)/shard_map/ppermute | solution.py:477
  94.9 8.2 %collective-permute-start.24 = (bf16[4,32,512]{2,1,0:T(8,128)(2,1)S(1)}, bf16[4,32,512]{2,1,0:T(8,128)(2,1)S(1)}, u32[]{:S(2)}, u32[]{:S(2)}) collective-permute-start(bf16[4,32,512]{2,1,0:T(8,128)(2,1)S(1)} %get-tuple-element.142), channel_id=1, source_target_pairs={{0,4},{1,5},{2,6},{3,7},{4,8},{5,9},{6,10},{7,11},{8,12},{9,13},{1... | collective-permute-start | bytes 393224 | tf_op jit(solution)/shard_map/ppermute | solution.py:477
  95.7 12.0 %collective-permute-start.25 = (bf16[4,32,512]{2,1,0:T(8,128)(2,1)S(1)}, bf16[4,32,512]{2,1,0:T(8,128)(2,1)S(1)}, u32[]{:S(2)}, u32[]{:S(2)}) collective-permute-start(bf16[4,32,512]{2,1,0:T(8,128)(2,1)S(1)} %get-tuple-element.143), channel_id=1, source_target_pairs={{0,8},{1,9},{2,10},{3,11},{4,12},{5,13},{6,14},{7,15},{8,0},{9,1},... | collective-permute-start | bytes 393224 | tf_op jit(solution)/shard_map/ppermute | solution.py:477
  97.0 10.7 %collective-permute-start.26 = (bf16[4,32,512]{2,1,0:T(8,128)(2,1)S(1)}, bf16[4,32,512]{2,1,0:T(8,128)(2,1)S(1)}, u32[]{:S(2)}, u32[]{:S(2)}) collective-permute-start(bf16[4,32,512]{2,1,0:T(8,128)(2,1)S(1)} %get-tuple-element.144), channel_id=1, source_target_pairs={{0,12},{1,13},{2,14},{3,15},{4,0},{5,1},{6,2},{7,3},{8,4},{9,5},{1... | collective-permute-start | bytes 393224 | tf_op jit(solution)/shard_map/ppermute | solution.py:477
  107.8 6.2 %collective-permute-start.29 = (bf16[4,32,512]{2,1,0:T(8,128)(2,1)S(1)}, bf16[4,32,512]{2,1,0:T(8,128)(2,1)S(1)}, u32[]{:S(2)}, u32[]{:S(2)}) collective-permute-start(bf16[4,32,512]{2,1,0:T(8,128)(2,1)S(1)} %shard_map.185.refs_3_.refs_1_), channel_id=1, source_target_pairs={{0,12},{1,13},{2,14},{3,15},{4,0},{5,1},{6,2},{7,3},{8,4},{9,5},{1... | collective-permute-start | bytes 393224 | tf_op jit(solution)/shard_map/ppermute | solution.py:477
  110.3 13.3 %collective-permute-start.28 = (bf16[4,32,512]{2,1,0:T(8,128)(2,1)S(1)}, bf16[4,32,512]{2,1,0:T(8,128)(2,1)S(1)}, u32[]{:S(2)}, u32[]{:S(2)}) collective-permute-start(bf16[4,32,512]{2,1,0:T(8,128)(2,1)S(1)} %shard_map.185.refs_3_.refs_1_), channel_id=1, source_target_pairs={{0,8},{1,9},{2,10},{3,11},{4,12},{5,13},{6,14},{7,15},{8,0},{9,1},... | collective-permute-start | bytes 393224 | tf_op jit(solution)/shard_map/ppermute | solution.py:477
  112.2 11.4 %collective-permute-start.27 = (bf16[4,32,512]{2,1,0:T(8,128)(2,1)S(1)}, bf16[4,32,512]{2,1,0:T(8,128)(2,1)S(1)}, u32[]{:S(2)}, u32[]{:S(2)}) collective-permute-start(bf16[4,32,512]{2,1,0:T(8,128)(2,1)S(1)} %shard_map.185.refs_3_.refs_1_), channel_id=1, source_target_pairs={{0,4},{1,5},{2,6},{3,7},{4,8},{5,9},{6,10},{7,11},{8,12},{9,13},{1... | collective-permute-start | bytes 393224 | tf_op jit(solution)/shard_map/ppermute | solution.py:477
  123.6 12.8 %collective-permute-start.31 = (bf16[4,128,512]{2,1,0:T(8,128)(2,1)S(1)}, bf16[4,128,512]{2,1,0:T(8,128)(2,1)S(1)}, u32[]{:S(2)}, u32[]{:S(2)}) collective-permute-start(bf16[4,128,512]{2,1,0:T(8,128)(2,1)S(1)} %shard_map.187.refs_5_.refs_1_), channel_id=1, source_target_pairs={{0,2},{1,3},{2,0},{3,1},{4,6},{5,7},{6,4},{7,5},{8,10},{9,11},{10,... | collective-permute-start | bytes 1572872 | tf_op jit(solution)/shard_map/ppermute | solution.py:477
  124.1 7.3 %collective-permute-start.32 = (bf16[3,32,512]{2,1,0:T(8,128)(2,1)S(1)}, bf16[3,32,512]{2,1,0:T(8,128)(2,1)S(1)}, u32[]{:S(2)}, u32[]{:S(2)}) collective-permute-start(bf16[3,32,512]{2,1,0:T(8,128)(2,1)S(1)} %get-tuple-element.147), channel_id=1, source_target_pairs={{0,4},{1,5},{2,6},{3,7},{4,8},{5,9},{6,10},{7,11},{8,12},{9,13},{1... | collective-permute-start | bytes 294920 | tf_op jit(solution)/shard_map/ppermute | solution.py:477
  124.1 9.5 %collective-permute-start.33 = (bf16[3,32,512]{2,1,0:T(8,128)(2,1)S(1)}, bf16[3,32,512]{2,1,0:T(8,128)(2,1)S(1)}, u32[]{:S(2)}, u32[]{:S(2)}) collective-permute-start(bf16[3,32,512]{2,1,0:T(8,128)(2,1)S(1)} %get-tuple-element.148), channel_id=1, source_target_pairs={{0,8},{1,9},{2,10},{3,11},{4,12},{5,13},{6,14},{7,15},{8,0},{9,1},... | collective-permute-start | bytes 294920 | tf_op jit(solution)/shard_map/ppermute | solution.py:477
  124.8 8.8 %collective-permute-start.34 = (bf16[3,32,512]{2,1,0:T(8,128)(2,1)S(1)}, bf16[3,32,512]{2,1,0:T(8,128)(2,1)S(1)}, u32[]{:S(2)}, u32[]{:S(2)}) collective-permute-start(bf16[3,32,512]{2,1,0:T(8,128)(2,1)S(1)} %get-tuple-element.149), channel_id=1, source_target_pairs={{0,12},{1,13},{2,14},{3,15},{4,0},{5,1},{6,2},{7,3},{8,4},{9,5},{1... | collective-permute-start | bytes 294920 | tf_op jit(solution)/shard_map/ppermute | solution.py:477
  127.9 12.2 %collective-permute-start.35 = (bf16[4,128,512]{2,1,0:T(8,128)(2,1)S(1)}, bf16[4,128,512]{2,1,0:T(8,128)(2,1)S(1)}, u32[]{:S(2)}, u32[]{:S(2)}) collective-permute-start(bf16[4,128,512]{2,1,0:T(8,128)(2,1)S(1)} %shard_map.187.refs_5_.refs_1_), channel_id=1, source_target_pairs={{0,1},{1,0},{2,3},{3,2},{4,5},{5,4},{6,7},{7,6},{8,9},{9,8},{10,11... | collective-permute-start | bytes 1572872 | tf_op jit(solution)/shard_map/ppermute | solution.py:477
  136.4 3.7 %collective-permute-start.36 = (bf16[4,128,512]{2,1,0:T(8,128)(2,1)S(1)}, bf16[4,128,512]{2,1,0:T(8,128)(2,1)S(1)}, u32[]{:S(2)}, u32[]{:S(2)}) collective-permute-start(bf16[4,128,512]{2,1,0:T(8,128)(2,1)S(1)} %shard_map.189.refs_2_), channel_id=1, source_target_pairs={{0,1},{1,0},{2,3},{3,2},{4,5},{5,4},{6,7},{7,6},{8,9},{9,8},{10,11... | collective-permute-start | bytes 1572872 | tf_op jit(solution)/shard_map/ppermute | solution.py:477
  136.4 5.4 %collective-permute-start.39 = (bf16[3,32,512]{2,1,0:T(8,128)(2,1)S(1)}, bf16[3,32,512]{2,1,0:T(8,128)(2,1)S(1)}, u32[]{:S(2)}, u32[]{:S(2)}) collective-permute-start(bf16[3,32,512]{2,1,0:T(8,128)(2,1)S(1)} %shard_map.188.refs_1_), channel_id=1, source_target_pairs={{0,12},{1,13},{2,14},{3,15},{4,0},{5,1},{6,2},{7,3},{8,4},{9,5},{1... | collective-permute-start | bytes 294920 | tf_op jit(solution)/shard_map/ppermute | solution.py:477
  136.5 11.4 %collective-permute-start.38 = (bf16[3,32,512]{2,1,0:T(8,128)(2,1)S(1)}, bf16[3,32,512]{2,1,0:T(8,128)(2,1)S(1)}, u32[]{:S(2)}, u32[]{:S(2)}) collective-permute-start(bf16[3,32,512]{2,1,0:T(8,128)(2,1)S(1)} %shard_map.188.refs_1_), channel_id=1, source_target_pairs={{0,8},{1,9},{2,10},{3,11},{4,12},{5,13},{6,14},{7,15},{8,0},{9,1},... | collective-permute-start | bytes 294920 | tf_op jit(solution)/shard_map/ppermute | solution.py:477
  138.2 9.7 %collective-permute-start.37 = (bf16[3,32,512]{2,1,0:T(8,128)(2,1)S(1)}, bf16[3,32,512]{2,1,0:T(8,128)(2,1)S(1)}, u32[]{:S(2)}, u32[]{:S(2)}) collective-permute-start(bf16[3,32,512]{2,1,0:T(8,128)(2,1)S(1)} %shard_map.188.refs_1_), channel_id=1, source_target_pairs={{0,4},{1,5},{2,6},{3,7},{4,8},{5,9},{6,10},{7,11},{8,12},{9,13},{1... | collective-permute-start | bytes 294920 | tf_op jit(solution)/shard_map/ppermute | solution.py:477
  147.9 11.0 %collective-permute-start.40 = (bf16[3,128,512]{2,1,0:T(8,128)(2,1)S(1)}, bf16[3,128,512]{2,1,0:T(8,128)(2,1)S(1)}, u32[]{:S(2)}, u32[]{:S(2)}) collective-permute-start(bf16[3,128,512]{2,1,0:T(8,128)(2,1)S(1)} %shard_map.191.refs_1_), channel_id=1, source_target_pairs={{0,2},{1,3},{2,0},{3,1},{4,6},{5,7},{6,4},{7,5},{8,10},{9,11},{10,... | collective-permute-start | bytes 1179656 | tf_op jit(solution)/shard_map/ppermute | solution.py:477
  148.4 10.6 %collective-permute-start.41 = (bf16[3,128,512]{2,1,0:T(8,128)(2,1)S(1)}, bf16[3,128,512]{2,1,0:T(8,128)(2,1)S(1)}, u32[]{:S(2)}, u32[]{:S(2)}) collective-permute-start(bf16[3,128,512]{2,1,0:T(8,128)(2,1)S(1)} %shard_map.191.refs_1_), channel_id=1, source_target_pairs={{0,1},{1,0},{2,3},{3,2},{4,5},{5,4},{6,7},{7,6},{8,9},{9,8},{10,11... | collective-permute-start | bytes 1179656 | tf_op jit(solution)/shard_map/ppermute | solution.py:477
  158.9 1.7 %collective-permute-start.42 = (bf16[3,128,512]{2,1,0:T(8,128)(2,1)S(1)}, bf16[3,128,512]{2,1,0:T(8,128)(2,1)S(1)}, u32[]{:S(2)}, u32[]{:S(2)}) collective-permute-start(bf16[3,128,512]{2,1,0:T(8,128)(2,1)S(1)} %collective-permute-done.40.refs_2_), channel_id=1, source_target_pairs={{0,1},{1,0},{2,3},{3,2},{4,5},{5,4},{6,7},{7,6},{8,9},{9,8},{10,11... | collective-permute-start | bytes 1179656 | tf_op jit(solution)/shard_map/ppermute | solution.py:477

commit v8 on v7

--- a/solution.py
+++ b/solution.py
@@ -129,13 +129,28 @@
     )(me, *[in_hbm(arg) for arg in args])
 
 
-def pick_kernel(plan, *refs):
-    node_ref = refs[0]
+def ask_kernel(plan, me_ref, send_ref, out_ref):
+    bands = out_ref.shape[0]
+    out_ref[...] = jnp.zeros_like(out_ref)
+    for step, sets in plan:
+        ids = [send_ref[k] for k in sets]
+        blank = out_ref.shape[2] - len(sets) * send_ref.shape[2]
+        if blank:
+            ids.append(jnp.zeros((1, blank), jnp.int32))
+        out_ref[lax.rem(me_ref[0] + bands - step, bands)] = jnp.concatenate(ids, axis=1)
+
+
+def asked(me_ref, id_ref, step, index, cap):
+    row = lax.rem(me_ref[0] + step, id_ref.shape[0])
+    return id_ref[row][:, index * cap : (index + 1) * cap]
+
+
+def pick_kernel(plan, me_ref, node_ref, id_ref, *out_refs):
     nodes = node_ref.shape[0]
-    for id_ref, out_ref, sets in zip(refs[1 : 1 + len(plan)], refs[1 + len(plan) :], plan):
-        cap = id_ref.shape[2]
-        for i, k in enumerate(sets):
-            hot = pick_table(id_ref[k], nodes)
+    for out_ref, (step, sets) in zip(out_refs, plan):
+        cap = out_ref.shape[0] // len(sets)
+        for i in range(len(sets)):
+            hot = pick_table(asked(me_ref, id_ref, step, i, cap), nodes)
             out_ref[i * cap : (i + 1) * cap, :] = dot(hot, node_ref[...]).astype(bf16)
 
 
@@ -406,17 +421,17 @@
 
 
 def final_kernel(plan, *refs):
-    base_ref, w1_ref = refs[:2]
-    id_refs = refs[2 : 2 + len(plan)]
-    row_refs = refs[2 + len(plan) : 2 + 2 * len(plan)]
-    out_ref, hot_ref, rows_ref = refs[2 + 2 * len(plan) :]
+    local_sets, remote = plan
+    me_ref, base_ref, w1_ref, send_ref, id_ref = refs[:5]
+    row_refs, (out_ref, hot_ref, rows_ref) = refs[5:-3], refs[-3:]
     nodes, width = base_ref.shape
-    cap = id_refs[0].shape[2]
-    at = 0
-    for id_ref, sets in zip(id_refs, plan):
-        for k in sets:
-            hot_ref[:, at : at + cap] = sum_table(id_ref[k], nodes)
-            at += cap
+    cap = send_ref.shape[2]
+    ids = [send_ref[k] for k in local_sets]
+    ids += [
+        asked(me_ref, id_ref, step, i, cap) for step, sets in remote for i in range(len(sets))
+    ]
+    for i, one in enumerate(ids):
+        hot_ref[:, i * cap : (i + 1) * cap] = sum_table(one, nodes)
     stack_into(rows_ref, row_refs)
     send_sum = dot(hot_ref[...], rows_ref[...]).astype(bf16)
     grad = base_ref[...] + dot_rt(send_sum, w1_ref[width : 2 * width, :])
@@ -593,7 +608,6 @@
 
     order = near + far
 
-    ids = [passed_along(send_ids, "band", -d) for d in steps]
     (
         node_latent,
         send_ids,
@@ -618,12 +632,25 @@
         node_cotan,
         edge_cotan[0],
     )
+    remote_plan = tuple(zip(steps, near_plan + far_plan))
+    widest = max(len(piece) for piece in near_plan + far_plan)
+    (ids,) = call(
+        functools.partial(ask_kernel, remote_plan),
+        [((bands, 1, widest * cap), jnp.int32)],
+        [],
+        me,
+        send_ids,
+        smem=(0,),
+    )
+    ids = lax.all_to_all(ids, "band", 0, 0, tiled=True)
     picked = call(
-        functools.partial(pick_kernel, near_plan + far_plan),
+        functools.partial(pick_kernel, remote_plan),
         [((len(piece) * cap, width), bf16) for piece in near_plan + far_plan],
         [],
+        me,
         node_latent,
-        *ids,
+        ids,
+        smem=(0,),
     )
     sx = [passed_along(block, "band", d) for block, d in zip(picked, steps)]
     sx_near, sx_far = sx[: len(near_plan)], sx[len(near_plan) :]
@@ -778,16 +805,18 @@
             after=after,
         )
         (grad_nodes,) = call(
-            functools.partial(final_kernel, (near[:local_count],) + near_plan + far_plan),
+            functools.partial(final_kernel, (near[:local_count], remote_plan)),
             [((nodes, width), bf16)],
             [((nodes, total), bf16), ((total, width), bf16)],
+            me,
             base,
             edge_first,
             send_ids,
-            *ids,
+            ids,
             gpe_local,
             *back_near,
             *back_far,
+            smem=(0,),
             last=(0,),
         )
         return grad_nodes
@@ -815,12 +844,12 @@
         along_y, along_z = (2, first), (2 * first, second)
         sent_edge = held_until(sent_edge, back_far[-1:])
         came_edge = [in_group(sent_edge, "band", 1, 2, 1)]
-        keep_node, sent_node = node_weights([sent_edge])
+        keep_edge, came_edge = add_stage(me, keep_edge, came_edge, *along_y, f32, back_near)
+        edge_new, grad_edges = edge_outputs([keep_edge])
+        keep_node, sent_node = node_weights([in_hbm(edge_new)])
         came_node = [in_group(sent_node, "band", 1, 2, 1)]
-        keep_edge, came_edge = add_stage(me, keep_edge, came_edge, *along_y, f32, [keep_node])
-        edge_new, grad_edges = edge_outputs([keep_edge])
         keep_edge, came_edge = add_stage(
-            me, keep_edge, came_edge, *along_z, f32, [in_hbm(edge_new)] + back_near + back_far[:-1]
+            me, keep_edge, came_edge, *along_z, f32, [keep_node] + back_far[:-1]
         )
         keep_node, came_node = add_stage(me, keep_node, came_node, *along_y, f32, [keep_edge])
         grad_nodes = node_output([keep_node])

time: 162 us -> 159 us (0.981)
  starting transfers between devices: 67.4 us -> 39.6 us
  blocking collectives: 0 us -> 13.7 us
  waiting for transfers between devices: 62.5 us -> 73.9 us
    ppermute x21 -> x14, starting transfers between devices: 46.7 us -> 18.5 us  [passed_along(): return lax.ppermute(block, axis, route)]
    all_to_all x0 -> x1, blocking collectives: none -> 13.7 us  [local(): ids = lax.all_to_all(ids, 'band', 0, 0, tiled=True)]
    ppermute x21 -> x14, waiting for transfers between devices: 16.8 us -> 27.3 us  [passed_along(): return lax.ppermute(block, axis, route)]
    pallas_call x20 -> x21, Pallas kernels: 27.9 us -> 27.7 us  [call(): pl.pallas_call(kernel, out_shape=[(pltpu.HBM if i in last else pltpu.VMEM...]
  transfers between devices with their start and end apart: 43 -> 36, of which waited for: 18 -> 19; matrix products, arithmetic and copies ran while one was open for 0% -> 0% of each run, Pallas kernels for 15% -> 10%
where the time goes in v8:
time: 159 us
  waiting for transfers between devices  73.9 us (46%)
  starting transfers between devices  39.6 us (25%)
  Pallas kernels  31 us (19%)
  blocking collectives  13.7 us (9%)
    ppermute x22, waiting for transfers between devices, in_group(): return lax.ppermute(block, axis, route)  46.6 us
    pallas_call x21, Pallas kernels, call(): pl.pallas_call(kernel, out_shape=[(pltpu.HBM if i in last else pltpu.VMEM...  27.7 us
    ppermute x14, waiting for transfers between devices, passed_along(): return lax.ppermute(block, axis, route)  27.3 us
    ppermute x22, starting transfers between devices, in_group(): return lax.ppermute(block, axis, route)  21 us
    ppermute x14, starting transfers between devices, passed_along(): return lax.ppermute(block, axis, route)  18.5 us
    all_to_all x1, blocking collectives, local(): ids = lax.all_to_all(ids, 'band', 0, 0, tiled=True)  13.7 us
    pallas_call x1, Pallas kernels, loaded(): pl.pallas_call(functools.partial(load_kernel, count), out_shape=[pltpu.VM...  3.24 us
  transfers between devices with their start and end apart: 36, of which 19 were waited for; matrix products, arithmetic and copies ran while one was open for 0% of the time, Pallas kernels for 10%

profile of v8, /device:TPU:0, one launch (start us, length us, event | category | flops | bytes accessed | tf_op | source)
XLA Modules:
  0.0 158.9 jit_solution(3629560865759839467)
XLA Ops:
  0.6 3.2 %shard_map.170 = (bf16[320,512]{1,0:T(8,128)(2,1)S(1)}, s32[11,1,128]{2,1,0:T(1,128)S(1)}, s32[11,1,128]{2,1,0:T(1,128)S(1)}, bf16[11,128,512]{2,1,0:T(8,128)(2,...) custom-call(s32[1]{0:T(128)} %bitcast.refs_0_.refs_2_, ...), custom_call_target="tpu_custom_call" | custom-call | flops 1 | bytes 1 | tf_op jit(solution)/shard_map/pallas_call | solution.py:120
  3.9 13.7 %all_to_all.5.refs_2_.refs_4_ = s32[16,1,256]{2,1,0:T(1,128)S(1)} all-to-all(s32[16,1,256]{2,1,0:T(1,128)S(1)} %shard_map.171), channel_id=1, replica_groups=mesh['groups'=2,'band'=16] {'band'}, dimensions={0} | all-to-all | bytes 32768 | tf_op jit(solution)/shard_map/all_to_all | solution.py:645
  18.6 1.2 collective-permute-start.2
  19.8 0.8 collective-permute-start.6
  20.6 3.3 %collective-permute-start.3 = (bf16[128,512]{1,0:T(8,128)(2,1)S(1)}, bf16[128,512]{1,0:T(8,128)(2,1)S(1)}, u32[]{:S(2)}, u32[]{:S(2)}) collective-permute-start(bf16[128,512]{1,0:T(8,128)(2,1)S(1)} %get-tuple-element.96), channel_id=1, source_target_pairs={{2,0},{3,1},{4,2},{5,3},{6,4},{7,5},{8,6},{9,7},{10,8},{11,9},{12,... | collective-permute-start | bytes 393224 | tf_op jit(solution)/shard_map/ppermute | solution.py:21
  23.9 3.9 %collective-permute-done.2.refs_8_.refs_7_ = bf16[128,512]{1,0:T(8,128)(2,1)S(1)} collective-permute-done((bf16[128,512]{1,0:T(8,128)(2,1)S(1)}, bf16[128,512]{1,0:T(8,128)(2,1)S(1)}, u32[]{:S(2)}, u32[]{:S(2)}) %collective-permute-start.2) | collective-permute-done | bytes 131104 | tf_op jit(solution)/shard_map/ppermute | solution.py:21
  27.8 4.5 %shard_map.173 = (bf16[1408,320]{1,0:T(8,128)(2,1)S(1)}, bf16[320,1408]{1,0:T(8,128)(2,1)S(1)}, f32[1408,128]{1,0:T(8,128)S(1)}, f32[1024,512]{1,0:T(8,128)S(1)}...) custom-call(bf16[11,128,512]{2,1,0:T(8,128)(2,1)S(1)} %get-tuple-ele, ...), custom_call_target="tpu_custom_call" | custom-call | flops 1 | bytes 1 | tf_op jit(solution)/shard_map/pallas_call | solution.py:89
  32.3 2.7 %collective-permute-done.refs_6_.refs_5_ = bf16[128,512]{1,0:T(8,128)(2,1)S(1)} collective-permute-done((bf16[128,512]{1,0:T(8,128)(2,1)S(1)}, bf16[128,512]{1,0:T(8,128)(2,1)S(1)}, u32[]{:S(2)}, u32[]{:S(2)}) %collective-permute-start) | collective-permute-done | bytes 131104 | tf_op jit(solution)/shard_map/ppermute | solution.py:21
  35.0 1.6 shard_map.174
  36.6 2.8 %collective-permute-done.5.refs_13_.refs_10_ = bf16[128,512]{1,0:T(8,128)(2,1)S(1)} collective-permute-done((bf16[128,512]{1,0:T(8,128)(2,1)S(1)}, bf16[128,512]{1,0:T(8,128)(2,1)S(1)}, u32[]{:S(2)}, u32[]{:S(2)}) %collective-permute-start.5) | collective-permute-done | bytes 131104 | tf_op jit(solution)/shard_map/ppermute | solution.py:21
  39.4 4.5 %shard_map.175 = (bf16[128,512]{1,0:T(8,128)(2,1)S(1)}, bf16[128,512]{1,0:T(8,128)(2,1)S(1)}, bf16[256,512]{1,0:T(8,128)(2,1)S(1)}, bf16[512,512]{1,0:T(8,128)(2...) custom-call(bf16[11,128,512]{2,1,0:T(8,128)(2,1)S(1)} %get-tuple-ele, ...), custom_call_target="tpu_custom_call" | custom-call | flops 1 | bytes 1 | tf_op jit(solution)/shard_map/pallas_call | solution.py:89
  43.8 4.7 %collective-permute-start.7 = (bf16[256,512]{1,0:T(8,128)(2,1)S(1)}, bf16[256,512]{1,0:T(8,128)(2,1)S(1)}, u32[]{:S(2)}, u32[]{:S(2)}) collective-permute-start(bf16[256,512]{1,0:T(8,128)(2,1)S(1)} %get-tuple-element.120.refs_19_.refs_14_), channel_id=1, source_target_pairs={{8,0},{9,1},{10,2},{11,3},{12,4},{13,5},{14,6},{15,7},{0,8},{1,9},... | collective-permute-start | bytes 786440 | tf_op jit(solution)/shard_map/ppermute | solution.py:21
  48.5 2.1 %shard_map.176 = (bf16[896,512]{1,0:T(8,128)(2,1)S(1)}, bf16[384,512]{1,0:T(8,128)(2,1)S(1)}, bf16[128,512]{1,0:T(8,128)(2,1)S(1)}, bf16[128,512]{1,0:T(8,128)(2...) custom-call(bf16[11,128,512]{2,1,0:T(8,128)(2,1)S(1)} %get-tuple-element.81.refs_0_.refs_1_, ...), custom_call_target="tpu_custom_call" | custom-call | flops 1 | bytes 1 | tf_op jit(solution)/shard_map/pallas_call | solution.py:89
  50.6 3.9 %shard_map.177 = (f32[4,256,512]{2,1,0:T(8,128)S(1)}, bf16[4,256,512]{2,1,0:T(8,128)(2,1)S(1)}, bf16[320,512]{1,0:T(8,128)(2,1)S(1)}) custom-call(bf16[11,128,512]{2,1,0:T(8,128)(2,1)S(1)} %get-tuple-element.82.refs_0_, bf16[320,1408]{1,0:T(8,128)(2,1)S(1)} %get-tuple-element.92.refs_2_.refs_4_.refs_1_, s32[1]{0:T(128)} %bitcast.refs_0_.refs_2_, ...), custom_call_target="tpu_custom_call" | custom-call | flops 1 | bytes 1 | tf_op jit(solution)/shard_map/pallas_call | solution.py:89
  54.5 4.7 %collective-permute-done.7.refs_1_.refs_12_ = bf16[256,512]{1,0:T(8,128)(2,1)S(1)} collective-permute-done((bf16[256,512]{1,0:T(8,128)(2,1)S(1)}, bf16[256,512]{1,0:T(8,128)(2,1)S(1)}, u32[]{:S(2)}, u32[]{:S(2)}) %collective-permute-start.7) | collective-permute-done | bytes 262176 | tf_op jit(solution)/shard_map/ppermute | solution.py:21
  59.2 4.3 %collective-permute-start.9 = (bf16[128,512]{1,0:T(8,128)(2,1)S(1)}, bf16[128,512]{1,0:T(8,128)(2,1)S(1)}, u32[]{:S(2)}, u32[]{:S(2)}) collective-permute-start(bf16[128,512]{1,0:T(8,128)(2,1)S(1)} %get-tuple-element.114.refs_13_.refs_8_), channel_id=1, source_target_pairs={{1,0},{2,1},{3,2},{4,3},{5,4},{6,5},{7,6},{8,7},{9,8},{10,9},{11,1... | collective-permute-start | bytes 393224 | tf_op jit(solution)/shard_map/ppermute | solution.py:21
  63.8 1.6 %collective-permute-start.12 = (bf16[128,512]{1,0:T(8,128)(2,1)S(1)}, bf16[128,512]{1,0:T(8,128)(2,1)S(1)}, u32[]{:S(2)}, u32[]{:S(2)}) collective-permute-start(bf16[128,512]{1,0:T(8,128)(2,1)S(1)} %get-tuple-element.117.refs_16_.refs_11_), channel_id=1, source_target_pairs={{14,0},{15,1},{0,2},{1,3},{2,4},{3,5},{4,6},{5,7},{6,8},{7,9},{8,1... | collective-permute-start | bytes 393224 | tf_op jit(solution)/shard_map/ppermute | solution.py:21
  66.0 5.1 %collective-permute-done.10.refs_4_.refs_7_ = bf16[128,512]{1,0:T(8,128)(2,1)S(1)} collective-permute-done((bf16[128,512]{1,0:T(8,128)(2,1)S(1)}, bf16[128,512]{1,0:T(8,128)(2,1)S(1)}, u32[]{:S(2)}, u32[]{:S(2)}) %collective-permute-start.10) | collective-permute-done | bytes 131104 | tf_op jit(solution)/shard_map/ppermute | solution.py:21
  71.1 1.3 collective-permute-done.11.refs_5_.refs_8_
  72.6 3.5 %shard_map.180 = (bf16[11,128,512]{2,1,0:T(8,128)(2,1)}, bf16[11,128,512]{2,1,0:T(8,128)(2,1)}) custom-call(bf16[11,128,512]{2,1,0:T(8,128)(2,1)S(1)} %get-tuple-element.82.refs_0_, bf16[11,128,512]{2,1,0:T(8,128)(2,1)S(1)} %get-tuple-element.81.refs_0_.refs_1_, bf16[1536,512]{1,0:T(8,128)(2,1)S(1)} %get-tuple-element.85.refs_4_.refs_6_.refs_2_.refs_3_, ...), custom_call_target="tpu_custom_call" | custom-call | flops 1 | bytes 1 | tf_op jit(solution)/shard_map/pallas_call | solution.py:89
  76.1 1.3 shard_map.181
  77.4 2.2 %collective-permute-start.13 = (bf16[3,256,512]{2,1,0:T(8,128)(2,1)S(1)}, bf16[3,256,512]{2,1,0:T(8,128)(2,1)S(1)}, u32[]{:S(2)}, u32[]{:S(2)}) collective-permute-start(bf16[3,256,512]{2,1,0:T(8,128)(2,1)S(1)} %get-tuple-element.137), channel_id=1, source_target_pairs={{0,1},{1,0},{2,3},{3,2},{4,5},{5,4},{6,7},{7,6},{8,9},{9,8},{10,11... | collective-permute-start | bytes 2359304 | tf_op jit(solution)/shard_map/ppermute | solution.py:492
  79.6 1.3 collective-permute-start.15
  80.9 0.8 collective-permute-start.16
  81.6 6.3 %collective-permute-done.15.refs_4_.refs_10_ = bf16[128,512]{1,0:T(8,128)(2,1)S(1)} collective-permute-done((bf16[128,512]{1,0:T(8,128)(2,1)S(1)}, bf16[128,512]{1,0:T(8,128)(2,1)S(1)}, u32[]{:S(2)}, u32[]{:S(2)}) %collective-permute-start.15) | collective-permute-done | bytes 131104 | tf_op jit(solution)/shard_map/ppermute | solution.py:21
  87.9 5.5 %collective-permute-done.14.refs_2_ = bf16[4,128,512]{2,1,0:T(8,128)(2,1)S(1)} collective-permute-done((bf16[4,128,512]{2,1,0:T(8,128)(2,1)S(1)}, bf16[4,128,512]{2,1,0:T(8,128)(2,1)S(1)}, u32[]{:S(2)}, u32[]{:S(2)}) %collective-permute-start.14) | collective-permute-done | bytes 524320 | tf_op jit(solution)/shard_map/ppermute | solution.py:492
  94.2 1.5 collective-permute-start.18
  95.7 2.3 %collective-permute-start.19 = (bf16[4,32,512]{2,1,0:T(8,128)(2,1)S(1)}, bf16[4,32,512]{2,1,0:T(8,128)(2,1)S(1)}, u32[]{:S(2)}, u32[]{:S(2)}) collective-permute-start(bf16[4,32,512]{2,1,0:T(8,128)(2,1)S(1)} %get-tuple-element.144), channel_id=1, source_target_pairs={{0,12},{1,13},{2,14},{3,15},{4,0},{5,1},{6,2},{7,3},{8,4},{9,5},{1... | collective-permute-start | bytes 393224 | tf_op jit(solution)/shard_map/ppermute | solution.py:492
  98.5 1.6 %shard_map.185.refs_5_ = bf16[320,512]{1,0:T(8,128)(2,1)} custom-call(s32[1]{0:T(128)} %bitcast.refs_0_.refs_2_, f32[320,512]{1,0:T(8,128)S(1)} %shard_map.184.refs_1_, bf16[1536,512]{1,0:T(8,128)(2,1)S(1)} %get-tuple-element.85.refs_4_.refs_6_.refs_2_.refs_3_, s32[11,1,128]{2,1,0:T(1,128)S(1)} %get-tuple-element.84.refs_1_.refs_2_.refs_3_, ...), custom_call_target="tpu_custom_call" | custom-call | flops 1 | bytes 1 | tf_op jit(solution)/shard_map/pallas_call | solution.py:89
  100.2 2.3 %collective-permute-done.17.refs_2_ = bf16[4,32,512]{2,1,0:T(8,128)(2,1)S(1)} collective-permute-done((bf16[4,32,512]{2,1,0:T(8,128)(2,1)S(1)}, bf16[4,32,512]{2,1,0:T(8,128)(2,1)S(1)}, u32[]{:S(2)}, u32[]{:S(2)}) %collective-permute-start.17) | collective-permute-done | bytes 131104 | tf_op jit(solution)/shard_map/ppermute | solution.py:492
  102.5 4.0 %collective-permute-done.18.refs_3_ = bf16[4,32,512]{2,1,0:T(8,128)(2,1)S(1)} collective-permute-done((bf16[4,32,512]{2,1,0:T(8,128)(2,1)S(1)}, bf16[4,32,512]{2,1,0:T(8,128)(2,1)S(1)}, u32[]{:S(2)}, u32[]{:S(2)}) %collective-permute-start.18) | collective-permute-done | bytes 131104 | tf_op jit(solution)/shard_map/ppermute | solution.py:492
  106.5 2.0 %collective-permute-start.22 = (bf16[4,32,512]{2,1,0:T(8,128)(2,1)S(1)}, bf16[4,32,512]{2,1,0:T(8,128)(2,1)S(1)}, u32[]{:S(2)}, u32[]{:S(2)}) collective-permute-start(bf16[4,32,512]{2,1,0:T(8,128)(2,1)S(1)} %shard_map.186.refs_3_.refs_1_), channel_id=1, source_target_pairs={{0,12},{1,13},{2,14},{3,15},{4,0},{5,1},{6,2},{7,3},{8,4},{9,5},{1... | collective-permute-start | bytes 393224 | tf_op jit(solution)/shard_map/ppermute | solution.py:492
  108.5 1.8 %collective-permute-start.21 = (bf16[4,32,512]{2,1,0:T(8,128)(2,1)S(1)}, bf16[4,32,512]{2,1,0:T(8,128)(2,1)S(1)}, u32[]{:S(2)}, u32[]{:S(2)}) collective-permute-start(bf16[4,32,512]{2,1,0:T(8,128)(2,1)S(1)} %shard_map.186.refs_3_.refs_1_), channel_id=1, source_target_pairs={{0,8},{1,9},{2,10},{3,11},{4,12},{5,13},{6,14},{7,15},{8,0},{9,1},... | collective-permute-start | bytes 393224 | tf_op jit(solution)/shard_map/ppermute | solution.py:492
  110.4 1.9 %collective-permute-done.22.refs_4_ = bf16[4,32,512]{2,1,0:T(8,128)(2,1)S(1)} collective-permute-done((bf16[4,32,512]{2,1,0:T(8,128)(2,1)S(1)}, bf16[4,32,512]{2,1,0:T(8,128)(2,1)S(1)}, u32[]{:S(2)}, u32[]{:S(2)}) %collective-permute-start.22) | collective-permute-done | bytes 131104 | tf_op jit(solution)/shard_map/ppermute | solution.py:492
  112.3 8.8 %collective-permute-done.21.refs_3_ = bf16[4,32,512]{2,1,0:T(8,128)(2,1)S(1)} collective-permute-done((bf16[4,32,512]{2,1,0:T(8,128)(2,1)S(1)}, bf16[4,32,512]{2,1,0:T(8,128)(2,1)S(1)}, u32[]{:S(2)}, u32[]{:S(2)}) %collective-permute-start.21) | collective-permute-done | bytes 131104 | tf_op jit(solution)/shard_map/ppermute | solution.py:492
  121.2 1.5 collective-permute-start.24
  123.5 3.1 %collective-permute-start.27 = (bf16[3,32,512]{2,1,0:T(8,128)(2,1)S(1)}, bf16[3,32,512]{2,1,0:T(8,128)(2,1)S(1)}, u32[]{:S(2)}, u32[]{:S(2)}) collective-permute-start(bf16[3,32,512]{2,1,0:T(8,128)(2,1)S(1)} %get-tuple-element.149), channel_id=1, source_target_pairs={{0,12},{1,13},{2,14},{3,15},{4,0},{5,1},{6,2},{7,3},{8,4},{9,5},{1... | collective-permute-start | bytes 294920 | tf_op jit(solution)/shard_map/ppermute | solution.py:492
  126.6 3.0 %collective-permute-done.25.refs_2_ = bf16[3,32,512]{2,1,0:T(8,128)(2,1)S(1)} collective-permute-done((bf16[3,32,512]{2,1,0:T(8,128)(2,1)S(1)}, bf16[3,32,512]{2,1,0:T(8,128)(2,1)S(1)}, u32[]{:S(2)}, u32[]{:S(2)}) %collective-permute-start.25) | collective-permute-done | bytes 98336 | tf_op jit(solution)/shard_map/ppermute | solution.py:492
  129.6 2.0 %collective-permute-done.26.refs_3_ = bf16[3,32,512]{2,1,0:T(8,128)(2,1)S(1)} collective-permute-done((bf16[3,32,512]{2,1,0:T(8,128)(2,1)S(1)}, bf16[3,32,512]{2,1,0:T(8,128)(2,1)S(1)}, u32[]{:S(2)}, u32[]{:S(2)}) %collective-permute-start.26) | collective-permute-done | bytes 98336 | tf_op jit(solution)/shard_map/ppermute | solution.py:492
  131.7 1.7 %collective-permute-done.24.refs_0_ = bf16[4,128,512]{2,1,0:T(8,128)(2,1)S(1)} collective-permute-done((bf16[4,128,512]{2,1,0:T(8,128)(2,1)S(1)}, bf16[4,128,512]{2,1,0:T(8,128)(2,1)S(1)}, u32[]{:S(2)}, u32[]{:S(2)}) %collective-permute-start.24) | collective-permute-done | bytes 524320 | tf_op jit(solution)/shard_map/ppermute | solution.py:492
  133.5 1.4 collective-permute-start.32
  135.4 2.0 %collective-permute-start.30 = (bf16[3,32,512]{2,1,0:T(8,128)(2,1)S(1)}, bf16[3,32,512]{2,1,0:T(8,128)(2,1)S(1)}, u32[]{:S(2)}, u32[]{:S(2)}) collective-permute-start(bf16[3,32,512]{2,1,0:T(8,128)(2,1)S(1)} %shard_map.189.refs_1_), channel_id=1, source_target_pairs={{0,4},{1,5},{2,6},{3,7},{4,8},{5,9},{6,10},{7,11},{8,12},{9,13},{1... | collective-permute-start | bytes 294920 | tf_op jit(solution)/shard_map/ppermute | solution.py:492
  137.4 1.5 shard_map.191
  138.9 6.3 %collective-permute-done.31.refs_3_ = bf16[3,32,512]{2,1,0:T(8,128)(2,1)S(1)} collective-permute-done((bf16[3,32,512]{2,1,0:T(8,128)(2,1)S(1)}, bf16[3,32,512]{2,1,0:T(8,128)(2,1)S(1)}, u32[]{:S(2)}, u32[]{:S(2)}) %collective-permute-start.31) | collective-permute-done | bytes 98336 | tf_op jit(solution)/shard_map/ppermute | solution.py:492
  145.2 1.6 collective-permute-start.33
  146.8 9.2 %collective-permute-done.33.refs_2_ = bf16[3,128,512]{2,1,0:T(8,128)(2,1)S(1)} collective-permute-done((bf16[3,128,512]{2,1,0:T(8,128)(2,1)S(1)}, bf16[3,128,512]{2,1,0:T(8,128)(2,1)S(1)}, u32[]{:S(2)}, u32[]{:S(2)}) %collective-permute-start.33) | collective-permute-done | bytes 393248 | tf_op jit(solution)/shard_map/ppermute | solution.py:492
  156.0 1.7 %collective-permute-done.35.refs_4_ = bf16[3,128,512]{2,1,0:T(8,128)(2,1)S(1)} collective-permute-done((bf16[3,128,512]{2,1,0:T(8,128)(2,1)S(1)}, bf16[3,128,512]{2,1,0:T(8,128)(2,1)S(1)}, u32[]{:S(2)}, u32[]{:S(2)}) %collective-permute-start.35) | collective-permute-done | bytes 393248 | tf_op jit(solution)/shard_map/ppermute | solution.py:492
  157.7 1.3 shard_map.193
  (49 shorter events, 4.9 us)
Async XLA Ops:
  18.4 5.5 %collective-permute-start.1 = (bf16[128,512]{1,0:T(8,128)(2,1)S(1)}, bf16[128,512]{1,0:T(8,128)(2,1)S(1)}, u32[]{:S(2)}, u32[]{:S(2)}) collective-permute-start(bf16[128,512]{1,0:T(8,128)(2,1)S(1)} %get-tuple-element.94), channel_id=1, source_target_pairs={{1,0},{2,1},{3,2},{4,3},{5,4},{6,5},{7,6},{8,7},{9,8},{10,9},{11,1... | collective-permute-start | bytes 393224 | tf_op jit(solution)/shard_map/ppermute | solution.py:21
  18.6 9.1 %collective-permute-start.2 = (bf16[128,512]{1,0:T(8,128)(2,1)S(1)}, bf16[128,512]{1,0:T(8,128)(2,1)S(1)}, u32[]{:S(2)}, u32[]{:S(2)}) collective-permute-start(bf16[128,512]{1,0:T(8,128)(2,1)S(1)} %get-tuple-element.95), channel_id=1, source_target_pairs={{14,0},{15,1},{0,2},{1,3},{2,4},{3,5},{4,6},{5,7},{6,8},{7,9},{8,1... | collective-permute-start | bytes 393224 | tf_op jit(solution)/shard_map/ppermute | solution.py:21
  19.8 19.6 %collective-permute-start.6 = (bf16[256,512]{1,0:T(8,128)(2,1)S(1)}, bf16[256,512]{1,0:T(8,128)(2,1)S(1)}, u32[]{:S(2)}, u32[]{:S(2)}) collective-permute-start(bf16[256,512]{1,0:T(8,128)(2,1)S(1)} %get-tuple-element.103), channel_id=1, source_target_pairs={{8,0},{9,1},{10,2},{11,3},{12,4},{13,5},{14,6},{15,7},{0,8},{1,9},... | collective-permute-start | bytes 786440 | tf_op jit(solution)/shard_map/ppermute | solution.py:21
  20.6 11.6 %collective-permute-start.3 = (bf16[128,512]{1,0:T(8,128)(2,1)S(1)}, bf16[128,512]{1,0:T(8,128)(2,1)S(1)}, u32[]{:S(2)}, u32[]{:S(2)}) collective-permute-start(bf16[128,512]{1,0:T(8,128)(2,1)S(1)} %get-tuple-element.96), channel_id=1, source_target_pairs={{2,0},{3,1},{4,2},{5,3},{6,4},{7,5},{8,6},{9,7},{10,8},{11,9},{12,... | collective-permute-start | bytes 393224 | tf_op jit(solution)/shard_map/ppermute | solution.py:21
  23.9 11.1 %collective-permute-start = (bf16[128,512]{1,0:T(8,128)(2,1)S(1)}, bf16[128,512]{1,0:T(8,128)(2,1)S(1)}, u32[]{:S(2)}, u32[]{:S(2)}) collective-permute-start(bf16[128,512]{1,0:T(8,128)(2,1)S(1)} %get-tuple-element.88.refs_7_), channel_id=1, source_target_pairs={{15,0},{0,1},{1,2},{2,3},{3,4},{4,5},{5,6},{6,7},{7,8},{8,9},{9,10... | collective-permute-start | bytes 393224 | tf_op jit(solution)/shard_map/ppermute | solution.py:21
  23.9 12.7 %collective-permute-start.4 = (bf16[128,512]{1,0:T(8,128)(2,1)S(1)}, bf16[128,512]{1,0:T(8,128)(2,1)S(1)}, u32[]{:S(2)}, u32[]{:S(2)}) collective-permute-start(bf16[128,512]{1,0:T(8,128)(2,1)S(1)} %get-tuple-element.101), channel_id=1, source_target_pairs={{12,0},{13,1},{14,2},{15,3},{0,4},{1,5},{2,6},{3,7},{4,8},{5,9},{6... | collective-permute-start | bytes 393224 | tf_op jit(solution)/shard_map/ppermute | solution.py:21
  27.8 11.6 %collective-permute-start.5 = (bf16[128,512]{1,0:T(8,128)(2,1)S(1)}, bf16[128,512]{1,0:T(8,128)(2,1)S(1)}, u32[]{:S(2)}, u32[]{:S(2)}) collective-permute-start(bf16[128,512]{1,0:T(8,128)(2,1)S(1)} %get-tuple-element.102), channel_id=1, source_target_pairs={{4,0},{5,1},{6,2},{7,3},{8,4},{9,5},{10,6},{11,7},{12,8},{13,9},{1... | collective-permute-start | bytes 393224 | tf_op jit(solution)/shard_map/ppermute | solution.py:21
  43.8 15.3 %collective-permute-start.7 = (bf16[256,512]{1,0:T(8,128)(2,1)S(1)}, bf16[256,512]{1,0:T(8,128)(2,1)S(1)}, u32[]{:S(2)}, u32[]{:S(2)}) collective-permute-start(bf16[256,512]{1,0:T(8,128)(2,1)S(1)} %get-tuple-element.120.refs_19_.refs_14_), channel_id=1, source_target_pairs={{8,0},{9,1},{10,2},{11,3},{12,4},{13,5},{14,6},{15,7},{0,8},{1,9},... | collective-permute-start | bytes 786440 | tf_op jit(solution)/shard_map/ppermute | solution.py:21
  59.2 13.3 %collective-permute-start.8 = (bf16[4,256,512]{2,1,0:T(8,128)(2,1)S(1)}, bf16[4,256,512]{2,1,0:T(8,128)(2,1)S(1)}, u32[]{:S(2)}, u32[]{:S(2)}) collective-permute-start(bf16[4,256,512]{2,1,0:T(8,128)(2,1)S(1)} %shard_map.178), channel_id=1, source_target_pairs={{0,1},{1,0},{2,3},{3,2},{4,5},{5,4},{6,7},{7,6},{8,9},{9,8},{10,11... | collective-permute-start | bytes 3145736 | tf_op jit(solution)/shard_map/ppermute | solution.py:492
  59.2 6.8 %collective-permute-start.9 = (bf16[128,512]{1,0:T(8,128)(2,1)S(1)}, bf16[128,512]{1,0:T(8,128)(2,1)S(1)}, u32[]{:S(2)}, u32[]{:S(2)}) collective-permute-start(bf16[128,512]{1,0:T(8,128)(2,1)S(1)} %get-tuple-element.114.refs_13_.refs_8_), channel_id=1, source_target_pairs={{1,0},{2,1},{3,2},{4,3},{5,4},{6,5},{7,6},{8,7},{9,8},{10,9},{11,1... | collective-permute-start | bytes 393224 | tf_op jit(solution)/shard_map/ppermute | solution.py:21
  63.4 7.6 %collective-permute-start.10 = (bf16[128,512]{1,0:T(8,128)(2,1)S(1)}, bf16[128,512]{1,0:T(8,128)(2,1)S(1)}, u32[]{:S(2)}, u32[]{:S(2)}) collective-permute-start(bf16[128,512]{1,0:T(8,128)(2,1)S(1)} %get-tuple-element.115.refs_14_.refs_9_), channel_id=1, source_target_pairs={{15,0},{0,1},{1,2},{2,3},{3,4},{4,5},{5,6},{6,7},{7,8},{8,9},{9,10... | collective-permute-start | bytes 393224 | tf_op jit(solution)/shard_map/ppermute | solution.py:21
  63.4 9.0 %collective-permute-start.11 = (bf16[128,512]{1,0:T(8,128)(2,1)S(1)}, bf16[128,512]{1,0:T(8,128)(2,1)S(1)}, u32[]{:S(2)}, u32[]{:S(2)}) collective-permute-start(bf16[128,512]{1,0:T(8,128)(2,1)S(1)} %get-tuple-element.116.refs_15_.refs_10_), channel_id=1, source_target_pairs={{2,0},{3,1},{4,2},{5,3},{6,4},{7,5},{8,6},{9,7},{10,8},{11,9},{12,... | collective-permute-start | bytes 393224 | tf_op jit(solution)/shard_map/ppermute | solution.py:21
  63.8 8.6 %collective-permute-start.12 = (bf16[128,512]{1,0:T(8,128)(2,1)S(1)}, bf16[128,512]{1,0:T(8,128)(2,1)S(1)}, u32[]{:S(2)}, u32[]{:S(2)}) collective-permute-start(bf16[128,512]{1,0:T(8,128)(2,1)S(1)} %get-tuple-element.117.refs_16_.refs_11_), channel_id=1, source_target_pairs={{14,0},{15,1},{0,2},{1,3},{2,4},{3,5},{4,6},{5,7},{6,8},{7,9},{8,1... | collective-permute-start | bytes 393224 | tf_op jit(solution)/shard_map/ppermute | solution.py:21
  77.4 16.2 %collective-permute-start.13 = (bf16[3,256,512]{2,1,0:T(8,128)(2,1)S(1)}, bf16[3,256,512]{2,1,0:T(8,128)(2,1)S(1)}, u32[]{:S(2)}, u32[]{:S(2)}) collective-permute-start(bf16[3,256,512]{2,1,0:T(8,128)(2,1)S(1)} %get-tuple-element.137), channel_id=1, source_target_pairs={{0,1},{1,0},{2,3},{3,2},{4,5},{5,4},{6,7},{7,6},{8,9},{9,8},{10,11... | collective-permute-start | bytes 2359304 | tf_op jit(solution)/shard_map/ppermute | solution.py:492
  79.6 13.9 %collective-permute-start.14 = (bf16[4,128,512]{2,1,0:T(8,128)(2,1)S(1)}, bf16[4,128,512]{2,1,0:T(8,128)(2,1)S(1)}, u32[]{:S(2)}, u32[]{:S(2)}) collective-permute-start(bf16[4,128,512]{2,1,0:T(8,128)(2,1)S(1)} %get-tuple-element.138), channel_id=1, source_target_pairs={{0,2},{1,3},{2,0},{3,1},{4,6},{5,7},{6,4},{7,5},{8,10},{9,11},{10,... | collective-permute-start | bytes 1572872 | tf_op jit(solution)/shard_map/ppermute | solution.py:492
  79.6 8.4 %collective-permute-start.15 = (bf16[128,512]{1,0:T(8,128)(2,1)S(1)}, bf16[128,512]{1,0:T(8,128)(2,1)S(1)}, u32[]{:S(2)}, u32[]{:S(2)}) collective-permute-start(bf16[128,512]{1,0:T(8,128)(2,1)S(1)} %get-tuple-element.118.refs_17_.refs_12_), channel_id=1, source_target_pairs={{4,0},{5,1},{6,2},{7,3},{8,4},{9,5},{10,6},{11,7},{12,8},{13,9},{1... | collective-permute-start | bytes 393224 | tf_op jit(solution)/shard_map/ppermute | solution.py:21
  80.9 7.1 %collective-permute-start.16 = (bf16[128,512]{1,0:T(8,128)(2,1)S(1)}, bf16[128,512]{1,0:T(8,128)(2,1)S(1)}, u32[]{:S(2)}, u32[]{:S(2)}) collective-permute-start(bf16[128,512]{1,0:T(8,128)(2,1)S(1)} %get-tuple-element.119.refs_18_.refs_13_), channel_id=1, source_target_pairs={{12,0},{13,1},{14,2},{15,3},{0,4},{1,5},{2,6},{3,7},{4,8},{5,9},{6... | collective-permute-start | bytes 393224 | tf_op jit(solution)/shard_map/ppermute | solution.py:21
  93.8 16.5 %collective-permute-start.23 = (bf16[3,128,512]{2,1,0:T(8,128)(2,1)S(1)}, bf16[3,128,512]{2,1,0:T(8,128)(2,1)S(1)}, u32[]{:S(2)}, u32[]{:S(2)}) collective-permute-start(bf16[3,128,512]{2,1,0:T(8,128)(2,1)S(1)} %get-tuple-element.145), channel_id=1, source_target_pairs={{0,2},{1,3},{2,0},{3,1},{4,6},{5,7},{6,4},{7,5},{8,10},{9,11},{10,... | collective-permute-start | bytes 1179656 | tf_op jit(solution)/shard_map/ppermute | solution.py:492
  94.2 8.3 %collective-permute-start.17 = (bf16[4,32,512]{2,1,0:T(8,128)(2,1)S(1)}, bf16[4,32,512]{2,1,0:T(8,128)(2,1)S(1)}, u32[]{:S(2)}, u32[]{:S(2)}) collective-permute-start(bf16[4,32,512]{2,1,0:T(8,128)(2,1)S(1)} %get-tuple-element.142), channel_id=1, source_target_pairs={{0,4},{1,5},{2,6},{3,7},{4,8},{5,9},{6,10},{7,11},{8,12},{9,13},{1... | collective-permute-start | bytes 393224 | tf_op jit(solution)/shard_map/ppermute | solution.py:492
  94.2 12.3 %collective-permute-start.18 = (bf16[4,32,512]{2,1,0:T(8,128)(2,1)S(1)}, bf16[4,32,512]{2,1,0:T(8,128)(2,1)S(1)}, u32[]{:S(2)}, u32[]{:S(2)}) collective-permute-start(bf16[4,32,512]{2,1,0:T(8,128)(2,1)S(1)} %get-tuple-element.143), channel_id=1, source_target_pairs={{0,8},{1,9},{2,10},{3,11},{4,12},{5,13},{6,14},{7,15},{8,0},{9,1},... | collective-permute-start | bytes 393224 | tf_op jit(solution)/shard_map/ppermute | solution.py:492
  95.7 10.7 %collective-permute-start.19 = (bf16[4,32,512]{2,1,0:T(8,128)(2,1)S(1)}, bf16[4,32,512]{2,1,0:T(8,128)(2,1)S(1)}, u32[]{:S(2)}, u32[]{:S(2)}) collective-permute-start(bf16[4,32,512]{2,1,0:T(8,128)(2,1)S(1)} %get-tuple-element.144), channel_id=1, source_target_pairs={{0,12},{1,13},{2,14},{3,15},{4,0},{5,1},{6,2},{7,3},{8,4},{9,5},{1... | collective-permute-start | bytes 393224 | tf_op jit(solution)/shard_map/ppermute | solution.py:492
  106.5 5.8 %collective-permute-start.22 = (bf16[4,32,512]{2,1,0:T(8,128)(2,1)S(1)}, bf16[4,32,512]{2,1,0:T(8,128)(2,1)S(1)}, u32[]{:S(2)}, u32[]{:S(2)}) collective-permute-start(bf16[4,32,512]{2,1,0:T(8,128)(2,1)S(1)} %shard_map.186.refs_3_.refs_1_), channel_id=1, source_target_pairs={{0,12},{1,13},{2,14},{3,15},{4,0},{5,1},{6,2},{7,3},{8,4},{9,5},{1... | collective-permute-start | bytes 393224 | tf_op jit(solution)/shard_map/ppermute | solution.py:492
  108.5 12.7 %collective-permute-start.21 = (bf16[4,32,512]{2,1,0:T(8,128)(2,1)S(1)}, bf16[4,32,512]{2,1,0:T(8,128)(2,1)S(1)}, u32[]{:S(2)}, u32[]{:S(2)}) collective-permute-start(bf16[4,32,512]{2,1,0:T(8,128)(2,1)S(1)} %shard_map.186.refs_3_.refs_1_), channel_id=1, source_target_pairs={{0,8},{1,9},{2,10},{3,11},{4,12},{5,13},{6,14},{7,15},{8,0},{9,1},... | collective-permute-start | bytes 393224 | tf_op jit(solution)/shard_map/ppermute | solution.py:492
  110.3 10.9 %collective-permute-start.20 = (bf16[4,32,512]{2,1,0:T(8,128)(2,1)S(1)}, bf16[4,32,512]{2,1,0:T(8,128)(2,1)S(1)}, u32[]{:S(2)}, u32[]{:S(2)}) collective-permute-start(bf16[4,32,512]{2,1,0:T(8,128)(2,1)S(1)} %shard_map.186.refs_3_.refs_1_), channel_id=1, source_target_pairs={{0,4},{1,5},{2,6},{3,7},{4,8},{5,9},{6,10},{7,11},{8,12},{9,13},{1... | collective-permute-start | bytes 393224 | tf_op jit(solution)/shard_map/ppermute | solution.py:492
  121.2 12.2 %collective-permute-start.24 = (bf16[4,128,512]{2,1,0:T(8,128)(2,1)S(1)}, bf16[4,128,512]{2,1,0:T(8,128)(2,1)S(1)}, u32[]{:S(2)}, u32[]{:S(2)}) collective-permute-start(bf16[4,128,512]{2,1,0:T(8,128)(2,1)S(1)} %shard_map.188.refs_5_.refs_1_), channel_id=1, source_target_pairs={{0,2},{1,3},{2,0},{3,1},{4,6},{5,7},{6,4},{7,5},{8,10},{9,11},{10,... | collective-permute-start | bytes 1572872 | tf_op jit(solution)/shard_map/ppermute | solution.py:492
  122.8 6.9 %collective-permute-start.25 = (bf16[3,32,512]{2,1,0:T(8,128)(2,1)S(1)}, bf16[3,32,512]{2,1,0:T(8,128)(2,1)S(1)}, u32[]{:S(2)}, u32[]{:S(2)}) collective-permute-start(bf16[3,32,512]{2,1,0:T(8,128)(2,1)S(1)} %get-tuple-element.147), channel_id=1, source_target_pairs={{0,4},{1,5},{2,6},{3,7},{4,8},{5,9},{6,10},{7,11},{8,12},{9,13},{1... | collective-permute-start | bytes 294920 | tf_op jit(solution)/shard_map/ppermute | solution.py:492
  122.8 8.9 %collective-permute-start.26 = (bf16[3,32,512]{2,1,0:T(8,128)(2,1)S(1)}, bf16[3,32,512]{2,1,0:T(8,128)(2,1)S(1)}, u32[]{:S(2)}, u32[]{:S(2)}) collective-permute-start(bf16[3,32,512]{2,1,0:T(8,128)(2,1)S(1)} %get-tuple-element.148), channel_id=1, source_target_pairs={{0,8},{1,9},{2,10},{3,11},{4,12},{5,13},{6,14},{7,15},{8,0},{9,1},... | collective-permute-start | bytes 294920 | tf_op jit(solution)/shard_map/ppermute | solution.py:492
  123.5 8.2 %collective-permute-start.27 = (bf16[3,32,512]{2,1,0:T(8,128)(2,1)S(1)}, bf16[3,32,512]{2,1,0:T(8,128)(2,1)S(1)}, u32[]{:S(2)}, u32[]{:S(2)}) collective-permute-start(bf16[3,32,512]{2,1,0:T(8,128)(2,1)S(1)} %get-tuple-element.149), channel_id=1, source_target_pairs={{0,12},{1,13},{2,14},{3,15},{4,0},{5,1},{6,2},{7,3},{8,4},{9,5},{1... | collective-permute-start | bytes 294920 | tf_op jit(solution)/shard_map/ppermute | solution.py:492
  126.6 10.8 %collective-permute-start.28 = (bf16[4,128,512]{2,1,0:T(8,128)(2,1)S(1)}, bf16[4,128,512]{2,1,0:T(8,128)(2,1)S(1)}, u32[]{:S(2)}, u32[]{:S(2)}) collective-permute-start(bf16[4,128,512]{2,1,0:T(8,128)(2,1)S(1)} %shard_map.188.refs_5_.refs_1_), channel_id=1, source_target_pairs={{0,1},{1,0},{2,3},{3,2},{4,5},{5,4},{6,7},{7,6},{8,9},{9,8},{10,11... | collective-permute-start | bytes 1572872 | tf_op jit(solution)/shard_map/ppermute | solution.py:492
  133.4 4.0 %collective-permute-start.29 = (bf16[4,128,512]{2,1,0:T(8,128)(2,1)S(1)}, bf16[4,128,512]{2,1,0:T(8,128)(2,1)S(1)}, u32[]{:S(2)}, u32[]{:S(2)}) collective-permute-start(bf16[4,128,512]{2,1,0:T(8,128)(2,1)S(1)} %shard_map.190.refs_2_), channel_id=1, source_target_pairs={{0,1},{1,0},{2,3},{3,2},{4,5},{5,4},{6,7},{7,6},{8,9},{9,8},{10,11... | collective-permute-start | bytes 1572872 | tf_op jit(solution)/shard_map/ppermute | solution.py:492
  133.5 5.4 %collective-permute-start.32 = (bf16[3,32,512]{2,1,0:T(8,128)(2,1)S(1)}, bf16[3,32,512]{2,1,0:T(8,128)(2,1)S(1)}, u32[]{:S(2)}, u32[]{:S(2)}) collective-permute-start(bf16[3,32,512]{2,1,0:T(8,128)(2,1)S(1)} %shard_map.189.refs_1_), channel_id=1, source_target_pairs={{0,12},{1,13},{2,14},{3,15},{4,0},{5,1},{6,2},{7,3},{8,4},{9,5},{1... | collective-permute-start | bytes 294920 | tf_op jit(solution)/shard_map/ppermute | solution.py:492
  134.9 10.3 %collective-permute-start.31 = (bf16[3,32,512]{2,1,0:T(8,128)(2,1)S(1)}, bf16[3,32,512]{2,1,0:T(8,128)(2,1)S(1)}, u32[]{:S(2)}, u32[]{:S(2)}) collective-permute-start(bf16[3,32,512]{2,1,0:T(8,128)(2,1)S(1)} %shard_map.189.refs_1_), channel_id=1, source_target_pairs={{0,8},{1,9},{2,10},{3,11},{4,12},{5,13},{6,14},{7,15},{8,0},{9,1},... | collective-permute-start | bytes 294920 | tf_op jit(solution)/shard_map/ppermute | solution.py:492
  135.4 9.7 %collective-permute-start.30 = (bf16[3,32,512]{2,1,0:T(8,128)(2,1)S(1)}, bf16[3,32,512]{2,1,0:T(8,128)(2,1)S(1)}, u32[]{:S(2)}, u32[]{:S(2)}) collective-permute-start(bf16[3,32,512]{2,1,0:T(8,128)(2,1)S(1)} %shard_map.189.refs_1_), channel_id=1, source_target_pairs={{0,4},{1,5},{2,6},{3,7},{4,8},{5,9},{6,10},{7,11},{8,12},{9,13},{1... | collective-permute-start | bytes 294920 | tf_op jit(solution)/shard_map/ppermute | solution.py:492
  145.2 10.8 %collective-permute-start.33 = (bf16[3,128,512]{2,1,0:T(8,128)(2,1)S(1)}, bf16[3,128,512]{2,1,0:T(8,128)(2,1)S(1)}, u32[]{:S(2)}, u32[]{:S(2)}) collective-permute-start(bf16[3,128,512]{2,1,0:T(8,128)(2,1)S(1)} %shard_map.192.refs_1_), channel_id=1, source_target_pairs={{0,2},{1,3},{2,0},{3,1},{4,6},{5,7},{6,4},{7,5},{8,10},{9,11},{10,... | collective-permute-start | bytes 1179656 | tf_op jit(solution)/shard_map/ppermute | solution.py:492
  146.8 9.2 %collective-permute-start.34 = (bf16[3,128,512]{2,1,0:T(8,128)(2,1)S(1)}, bf16[3,128,512]{2,1,0:T(8,128)(2,1)S(1)}, u32[]{:S(2)}, u32[]{:S(2)}) collective-permute-start(bf16[3,128,512]{2,1,0:T(8,128)(2,1)S(1)} %shard_map.192.refs_1_), channel_id=1, source_target_pairs={{0,1},{1,0},{2,3},{3,2},{4,5},{5,4},{6,7},{7,6},{8,9},{9,8},{10,11... | collective-permute-start | bytes 1179656 | tf_op jit(solution)/shard_map/ppermute | solution.py:492
  156.0 1.7 %collective-permute-start.35 = (bf16[3,128,512]{2,1,0:T(8,128)(2,1)S(1)}, bf16[3,128,512]{2,1,0:T(8,128)(2,1)S(1)}, u32[]{:S(2)}, u32[]{:S(2)}) collective-permute-start(bf16[3,128,512]{2,1,0:T(8,128)(2,1)S(1)} %collective-permute-done.33.refs_2_), channel_id=1, source_target_pairs={{0,1},{1,0},{2,3},{3,2},{4,5},{5,4},{6,7},{7,6},{8,9},{9,8},{10,11... | collective-permute-start | bytes 1179656 | tf_op jit(solution)/shard_map/ppermute | solution.py:492

commit v9 on v8

--- a/solution.py
+++ b/solution.py
@@ -544,9 +544,9 @@
     return mine
 
 
-def join_stage(me, mine, members, blocks, shapes, after):
+def join_stage(me, mine, members, blocks, shapes, swap_after, after):
     pieces = [in_group(mine, "band", 2, members, j) for j in range(1, members)]
-    pieces = [mine] + [held_until(piece, after) if after else piece for piece in pieces]
+    pieces = [mine] + [held_until(piece, swap_after) if swap_after else piece for piece in pieces]
     others = [in_group(one, "band", 1, 2, 1) for one in pieces]
     return call(
         functools.partial(join_kernel, (members, blocks)),
@@ -556,6 +556,7 @@
         *pieces,
         *others,
         smem=(0,),
+        after=after,
         last=range(len(shapes)),
     )
 
@@ -842,24 +843,26 @@
     edge_shapes = [(3 * width, width), (width, width)]
     if width // 2 % (16 * first * second) == 0:
         along_y, along_z = (2, first), (2 * first, second)
-        sent_edge = held_until(sent_edge, back_far[-1:])
+        keep_node, sent_node = node_weights([])
+        came_node = [in_group(sent_node, "band", 1, 2, 1)]
+        keep_node, came_node = add_stage(me, keep_node, came_node, *along_y, f32, [])
+        sent_edge = held_until(sent_edge, back_far + came_node)
         came_edge = [in_group(sent_edge, "band", 1, 2, 1)]
-        keep_edge, came_edge = add_stage(me, keep_edge, came_edge, *along_y, f32, back_near)
+        keep_node, came_node = add_stage(me, keep_node, came_node, *along_z, f32, [sent_edge])
+        keep_edge, came_edge = add_stage(me, keep_edge, came_edge, *along_y, f32, [keep_node])
         edge_new, grad_edges = edge_outputs([keep_edge])
-        keep_node, sent_node = node_weights([in_hbm(edge_new)])
-        came_node = [in_group(sent_node, "band", 1, 2, 1)]
-        keep_edge, came_edge = add_stage(
-            me, keep_edge, came_edge, *along_z, f32, [keep_node] + back_far[:-1]
+        piece_node, _ = add_stage(me, keep_node, came_node, 1, 1, bf16, [in_hbm(edge_new)])
+        keep_edge, came_edge = add_stage(me, keep_edge, came_edge, *along_z, f32, [piece_node])
+        mine_node = gather_stage(me, piece_node, *along_z, [keep_edge])
+        piece_edge, _ = add_stage(me, keep_edge, came_edge, 1, 1, bf16, [mine_node])
+        grad_n1, grad_n2 = join_stage(
+            me, mine_node, first, node_blocks, node_shapes, [piece_edge], []
         )
-        keep_node, came_node = add_stage(me, keep_node, came_node, *along_y, f32, [keep_edge])
-        grad_nodes = node_output([keep_node])
-        piece_edge, _ = add_stage(me, keep_edge, came_edge, 1, 1, bf16, [in_hbm(grad_nodes)])
-        keep_node, came_node = add_stage(me, keep_node, came_node, *along_z, f32, [piece_edge])
-        mine_edge = gather_stage(me, piece_edge, *along_z, [keep_node])
-        piece_node, _ = add_stage(me, keep_node, came_node, 1, 1, bf16, [mine_edge])
-        grad_e1, grad_e2 = join_stage(me, mine_edge, first, edge_blocks, edge_shapes, [piece_node])
-        mine_node = gather_stage(me, piece_node, *along_z, [in_hbm(grad_e2)])
-        grad_n1, grad_n2 = join_stage(me, mine_node, first, node_blocks, node_shapes, [])
+        mine_edge = gather_stage(me, piece_edge, *along_z, [in_hbm(grad_n2)])
+        grad_nodes = node_output([mine_edge])
+        grad_e1, grad_e2 = join_stage(
+            me, mine_edge, first, edge_blocks, edge_shapes, [in_hbm(grad_nodes)], []
+        )
     else:
         whole = reduce_whole(*node_weights([]))
         grad_n1, grad_n2 = whole[:2].reshape(2 * width, width), whole[2]

time: 159 us -> 155 us (0.975)
  waiting for transfers between devices: 73.9 us -> 56.4 us
  starting transfers between devices: 39.6 us -> 53.3 us
    ppermute x22, starting transfers between devices: 21 us -> 41.4 us  [in_group(): return lax.ppermute(block, axis, route)]
    ppermute x22, waiting for transfers between devices: 46.6 us -> 36.8 us  [in_group(): return lax.ppermute(block, axis, route)]
    ppermute x14, waiting for transfers between devices: 27.3 us -> 19.6 us  [passed_along(): return lax.ppermute(block, axis, route)]
    ppermute x14, starting transfers between devices: 18.5 us -> 11.9 us  [passed_along(): return lax.ppermute(block, axis, route)]
  transfers between devices with their start and end apart: 36 -> 36, of which waited for: 19 -> 17; matrix products, arithmetic and copies ran while one was open for 0% -> 0% of each run, Pallas kernels for 10% -> 12%
where the time goes in v9:
time: 155 us
  waiting for transfers between devices  56.4 us (36%)
  starting transfers between devices  53.3 us (34%)
  Pallas kernels  30.9 us (20%)
  blocking collectives  13.7 us (9%)
    ppermute x22, starting transfers between devices, in_group(): return lax.ppermute(block, axis, route)  41.4 us
    ppermute x22, waiting for transfers between devices, in_group(): return lax.ppermute(block, axis, route)  36.8 us
    pallas_call x21, Pallas kernels, call(): pl.pallas_call(kernel, out_shape=[(pltpu.HBM if i in last else pltpu.VMEM...  27.7 us
    ppermute x14, waiting for transfers between devices, passed_along(): return lax.ppermute(block, axis, route)  19.6 us
    all_to_all x1, blocking collectives, local(): ids = lax.all_to_all(ids, 'band', 0, 0, tiled=True)  13.7 us
    ppermute x14, starting transfers between devices, passed_along(): return lax.ppermute(block, axis, route)  11.9 us
    pallas_call x1, Pallas kernels, loaded(): pl.pallas_call(functools.partial(load_kernel, count), out_shape=[pltpu.VM...  3.24 us
  transfers between devices with their start and end apart: 36, of which 17 were waited for; matrix products, arithmetic and copies ran while one was open for 0% of the time, Pallas kernels for 12%

profile of v9, /device:TPU:0, one launch (start us, length us, event | category | flops | bytes accessed | tf_op | source)
XLA Modules:
  0.0 155.2 jit_solution(2615139260675420866)
XLA Ops:
  0.6 3.2 %shard_map.170 = (bf16[320,512]{1,0:T(8,128)(2,1)S(1)}, s32[11,1,128]{2,1,0:T(1,128)S(1)}, s32[11,1,128]{2,1,0:T(1,128)S(1)}, bf16[11,128,512]{2,1,0:T(8,128)(2,...) custom-call(s32[1]{0:T(128)} %bitcast.refs_0_.refs_2_, ...), custom_call_target="tpu_custom_call" | custom-call | flops 1 | bytes 1 | tf_op jit(solution)/shard_map/pallas_call | solution.py:120
  3.9 13.7 %all_to_all.5.refs_2_.refs_4_ = s32[16,1,256]{2,1,0:T(1,128)S(1)} all-to-all(s32[16,1,256]{2,1,0:T(1,128)S(1)} %shard_map.171), channel_id=1, replica_groups=mesh['groups'=2,'band'=16] {'band'}, dimensions={0} | all-to-all | bytes 32768 | tf_op jit(solution)/shard_map/all_to_all | solution.py:646
  17.6 0.8 shard_map.172
  18.6 1.2 collective-permute-start.2
  19.8 0.8 collective-permute-start.6
  20.6 3.3 %collective-permute-start.3 = (bf16[128,512]{1,0:T(8,128)(2,1)S(1)}, bf16[128,512]{1,0:T(8,128)(2,1)S(1)}, u32[]{:S(2)}, u32[]{:S(2)}) collective-permute-start(bf16[128,512]{1,0:T(8,128)(2,1)S(1)} %get-tuple-element.96), channel_id=1, source_target_pairs={{2,0},{3,1},{4,2},{5,3},{6,4},{7,5},{8,6},{9,7},{10,8},{11,9},{12,... | collective-permute-start | bytes 393224 | tf_op jit(solution)/shard_map/ppermute | solution.py:21
  23.9 3.8 %collective-permute-done.2.refs_8_.refs_7_ = bf16[128,512]{1,0:T(8,128)(2,1)S(1)} collective-permute-done((bf16[128,512]{1,0:T(8,128)(2,1)S(1)}, bf16[128,512]{1,0:T(8,128)(2,1)S(1)}, u32[]{:S(2)}, u32[]{:S(2)}) %collective-permute-start.2) | collective-permute-done | bytes 131104 | tf_op jit(solution)/shard_map/ppermute | solution.py:21
  27.8 4.5 %shard_map.173 = (bf16[1408,320]{1,0:T(8,128)(2,1)S(1)}, bf16[320,1408]{1,0:T(8,128)(2,1)S(1)}, f32[1408,128]{1,0:T(8,128)S(1)}, f32[1024,512]{1,0:T(8,128)S(1)}...) custom-call(bf16[11,128,512]{2,1,0:T(8,128)(2,1)S(1)} %get-tuple-ele, ...), custom_call_target="tpu_custom_call" | custom-call | flops 1 | bytes 1 | tf_op jit(solution)/shard_map/pallas_call | solution.py:89
  32.3 2.7 %collective-permute-done.refs_6_.refs_5_ = bf16[128,512]{1,0:T(8,128)(2,1)S(1)} collective-permute-done((bf16[128,512]{1,0:T(8,128)(2,1)S(1)}, bf16[128,512]{1,0:T(8,128)(2,1)S(1)}, u32[]{:S(2)}, u32[]{:S(2)}) %collective-permute-start) | collective-permute-done | bytes 131104 | tf_op jit(solution)/shard_map/ppermute | solution.py:21
  35.0 1.6 %shard_map.174 = (bf16[512,512]{1,0:T(8,128)(2,1)S(1)}, f32[512,512]{1,0:T(8,128)S(1)}, f32[512,512]{1,0:T(8,128)S(1)}, f32[512,128]{1,0:T(8,128)S(1)}, f32[320,512]{1,0:T(8,128)S(1)}) custom-call(f32[1024,512]{1,0:T(8,128)S(1)} %get-tuple-element.89.refs_0_.refs_1_, f32[1408,128]{1,0:T(8,128)S(1)} %get-tuple-element.90.refs_1_.refs_2_.refs_3_, ...), custom_call_target="tpu_custom_call" | custom-call | flops 1 | bytes 1 | tf_op jit(solution)/shard_map/pallas_call | solution.py:89
  36.6 2.8 %collective-permute-done.5.refs_13_.refs_10_ = bf16[128,512]{1,0:T(8,128)(2,1)S(1)} collective-permute-done((bf16[128,512]{1,0:T(8,128)(2,1)S(1)}, bf16[128,512]{1,0:T(8,128)(2,1)S(1)}, u32[]{:S(2)}, u32[]{:S(2)}) %collective-permute-start.5) | collective-permute-done | bytes 131104 | tf_op jit(solution)/shard_map/ppermute | solution.py:21
  39.4 4.5 %shard_map.175 = (bf16[128,512]{1,0:T(8,128)(2,1)S(1)}, bf16[128,512]{1,0:T(8,128)(2,1)S(1)}, bf16[256,512]{1,0:T(8,128)(2,1)S(1)}, bf16[512,512]{1,0:T(8,128)(2...) custom-call(bf16[11,128,512]{2,1,0:T(8,128)(2,1)S(1)} %get-tuple-ele, ...), custom_call_target="tpu_custom_call" | custom-call | flops 1 | bytes 1 | tf_op jit(solution)/shard_map/pallas_call | solution.py:89
  43.8 1.3 shard_map.178
  45.2 2.3 %collective-permute-done.10.refs_2_ = bf16[3,256,512]{2,1,0:T(8,128)(2,1)S(1)} collective-permute-done((bf16[3,256,512]{2,1,0:T(8,128)(2,1)S(1)}, bf16[3,256,512]{2,1,0:T(8,128)(2,1)S(1)}, u32[]{:S(2)}, u32[]{:S(2)}) %collective-permute-start.10) | collective-permute-done | bytes 786464 | tf_op jit(solution)/shard_map/ppermute | solution.py:492
  47.7 5.0 %collective-permute-start.11 = (bf16[3,128,512]{2,1,0:T(8,128)(2,1)S(1)}, bf16[3,128,512]{2,1,0:T(8,128)(2,1)S(1)}, u32[]{:S(2)}, u32[]{:S(2)}) collective-permute-start(bf16[3,128,512]{2,1,0:T(8,128)(2,1)S(1)} %get-tuple-element.135), channel_id=1, source_target_pairs={{0,2},{1,3},{2,0},{3,1},{4,6},{5,7},{6,4},{7,5},{8,10},{9,11},{10,... | collective-permute-start | bytes 1179656 | tf_op jit(solution)/shard_map/ppermute | solution.py:492
  53.1 3.4 %collective-permute-start.7 = (bf16[128,512]{1,0:T(8,128)(2,1)S(1)}, bf16[128,512]{1,0:T(8,128)(2,1)S(1)}, u32[]{:S(2)}, u32[]{:S(2)}) collective-permute-start(bf16[128,512]{1,0:T(8,128)(2,1)S(1)} %get-tuple-element.118.refs_17_.refs_12_), channel_id=1, source_target_pairs={{4,0},{5,1},{6,2},{7,3},{8,4},{9,5},{10,6},{11,7},{12,8},{13,9},{1... | collective-permute-start | bytes 393224 | tf_op jit(solution)/shard_map/ppermute | solution.py:21
  56.5 2.1 %shard_map.176 = (bf16[896,512]{1,0:T(8,128)(2,1)S(1)}, bf16[384,512]{1,0:T(8,128)(2,1)S(1)}, bf16[128,512]{1,0:T(8,128)(2,1)S(1)}, bf16[128,512]{1,0:T(8,128)(2...) custom-call(bf16[11,128,512]{2,1,0:T(8,128)(2,1)S(1)} %get-tuple-element.81.refs_0_.refs_1_, ...), custom_call_target="tpu_custom_call" | custom-call | flops 1 | bytes 1 | tf_op jit(solution)/shard_map/pallas_call | solution.py:89
  58.6 3.9 %shard_map.177 = (f32[4,256,512]{2,1,0:T(8,128)S(1)}, bf16[4,256,512]{2,1,0:T(8,128)(2,1)S(1)}, bf16[320,512]{1,0:T(8,128)(2,1)S(1)}) custom-call(bf16[11,128,512]{2,1,0:T(8,128)(2,1)S(1)} %get-tuple-element.82.refs_0_, bf16[320,1408]{1,0:T(8,128)(2,1)S(1)} %get-tuple-element.92.refs_2_.refs_4_.refs_1_, s32[1]{0:T(128)} %bitcast.refs_0_.refs_2_, ...), custom_call_target="tpu_custom_call" | custom-call | flops 1 | bytes 1 | tf_op jit(solution)/shard_map/pallas_call | solution.py:89
  62.6 5.7 %collective-permute-done.8.refs_2_.refs_11_ = bf16[128,512]{1,0:T(8,128)(2,1)S(1)} collective-permute-done((bf16[128,512]{1,0:T(8,128)(2,1)S(1)}, bf16[128,512]{1,0:T(8,128)(2,1)S(1)}, u32[]{:S(2)}, u32[]{:S(2)}) %collective-permute-start.8) | collective-permute-done | bytes 131104 | tf_op jit(solution)/shard_map/ppermute | solution.py:21
  68.3 2.8 %collective-permute-done.9.refs_3_.refs_12_ = bf16[256,512]{1,0:T(8,128)(2,1)S(1)} collective-permute-done((bf16[256,512]{1,0:T(8,128)(2,1)S(1)}, bf16[256,512]{1,0:T(8,128)(2,1)S(1)}, u32[]{:S(2)}, u32[]{:S(2)}) %collective-permute-start.9) | collective-permute-done | bytes 262176 | tf_op jit(solution)/shard_map/ppermute | solution.py:21
  71.1 2.6 %collective-permute-done.12.refs_2_ = bf16[4,256,512]{2,1,0:T(8,128)(2,1)S(1)} collective-permute-done((bf16[4,256,512]{2,1,0:T(8,128)(2,1)S(1)}, bf16[4,256,512]{2,1,0:T(8,128)(2,1)S(1)}, u32[]{:S(2)}, u32[]{:S(2)}) %collective-permute-start.12) | collective-permute-done | bytes 1048608 | tf_op jit(solution)/shard_map/ppermute | solution.py:492
  74.2 2.7 %collective-permute-start.14 = (bf16[3,32,512]{2,1,0:T(8,128)(2,1)S(1)}, bf16[3,32,512]{2,1,0:T(8,128)(2,1)S(1)}, u32[]{:S(2)}, u32[]{:S(2)}) collective-permute-start(bf16[3,32,512]{2,1,0:T(8,128)(2,1)S(1)} %get-tuple-element.142), channel_id=1, source_target_pairs={{0,4},{1,5},{2,6},{3,7},{4,8},{5,9},{6,10},{7,11},{8,12},{9,13},{1... | collective-permute-start | bytes 294920 | tf_op jit(solution)/shard_map/ppermute | solution.py:492
  76.8 2.6 %collective-permute-start.16 = (bf16[3,32,512]{2,1,0:T(8,128)(2,1)S(1)}, bf16[3,32,512]{2,1,0:T(8,128)(2,1)S(1)}, u32[]{:S(2)}, u32[]{:S(2)}) collective-permute-start(bf16[3,32,512]{2,1,0:T(8,128)(2,1)S(1)} %get-tuple-element.144), channel_id=1, source_target_pairs={{0,12},{1,13},{2,14},{3,15},{4,0},{5,1},{6,2},{7,3},{8,4},{9,5},{1... | collective-permute-start | bytes 294920 | tf_op jit(solution)/shard_map/ppermute | solution.py:492
  79.5 3.5 %shard_map.183 = (bf16[11,128,512]{2,1,0:T(8,128)(2,1)}, bf16[11,128,512]{2,1,0:T(8,128)(2,1)}) custom-call(bf16[11,128,512]{2,1,0:T(8,128)(2,1)S(1)} %get-tuple-element.82.refs_0_, bf16[11,128,512]{2,1,0:T(8,128)(2,1)S(1)} %get-tuple-element.81.refs_0_.refs_1_, bf16[1536,512]{1,0:T(8,128)(2,1)S(1)} %get-tuple-element.85.refs_4_.refs_6_.refs_2_.refs_3_, ...), custom_call_target="tpu_custom_call" | custom-call | flops 1 | bytes 1 | tf_op jit(solution)/shard_map/pallas_call | solution.py:89
  83.0 2.0 %collective-permute-done.15.refs_3_ = bf16[3,32,512]{2,1,0:T(8,128)(2,1)S(1)} collective-permute-done((bf16[3,32,512]{2,1,0:T(8,128)(2,1)S(1)}, bf16[3,32,512]{2,1,0:T(8,128)(2,1)S(1)}, u32[]{:S(2)}, u32[]{:S(2)}) %collective-permute-start.15) | collective-permute-done | bytes 98336 | tf_op jit(solution)/shard_map/ppermute | solution.py:492
  85.1 3.4 %collective-permute-start.22 = (bf16[3,32,512]{2,1,0:T(8,128)(2,1)S(1)}, bf16[3,32,512]{2,1,0:T(8,128)(2,1)S(1)}, u32[]{:S(2)}, u32[]{:S(2)}) collective-permute-start(bf16[3,32,512]{2,1,0:T(8,128)(2,1)S(1)} %shard_map.184.refs_3_.refs_1_), channel_id=1, source_target_pairs={{0,12},{1,13},{2,14},{3,15},{4,0},{5,1},{6,2},{7,3},{8,4},{9,5},{1... | collective-permute-start | bytes 294920 | tf_op jit(solution)/shard_map/ppermute | solution.py:492
  88.5 0.7 collective-permute-start.21
  89.3 2.3 %collective-permute-done.22.refs_4_ = bf16[3,32,512]{2,1,0:T(8,128)(2,1)S(1)} collective-permute-done((bf16[3,32,512]{2,1,0:T(8,128)(2,1)S(1)}, bf16[3,32,512]{2,1,0:T(8,128)(2,1)S(1)}, u32[]{:S(2)}, u32[]{:S(2)}) %collective-permute-start.22) | collective-permute-done | bytes 98336 | tf_op jit(solution)/shard_map/ppermute | solution.py:492
  91.6 6.6 %collective-permute-done.21.refs_3_ = bf16[3,32,512]{2,1,0:T(8,128)(2,1)S(1)} collective-permute-done((bf16[3,32,512]{2,1,0:T(8,128)(2,1)S(1)}, bf16[3,32,512]{2,1,0:T(8,128)(2,1)S(1)}, u32[]{:S(2)}, u32[]{:S(2)}) %collective-permute-start.21) | collective-permute-done | bytes 98336 | tf_op jit(solution)/shard_map/ppermute | solution.py:492
  98.2 1.7 %collective-permute-start.26 = (bf16[3,128,512]{2,1,0:T(8,128)(2,1)S(1)}, bf16[3,128,512]{2,1,0:T(8,128)(2,1)S(1)}, u32[]{:S(2)}, u32[]{:S(2)}) collective-permute-start(bf16[3,128,512]{2,1,0:T(8,128)(2,1)S(1)} %shard_map.186.refs_5_.refs_1_), channel_id=1, source_target_pairs={{0,2},{1,3},{2,0},{3,1},{4,6},{5,7},{6,4},{7,5},{8,10},{9,11},{10,... | collective-permute-start | bytes 1179656 | tf_op jit(solution)/shard_map/ppermute | solution.py:492
  100.0 1.1 collective-permute-start.18
  101.0 2.8 %collective-permute-start.19 = (bf16[4,32,512]{2,1,0:T(8,128)(2,1)S(1)}, bf16[4,32,512]{2,1,0:T(8,128)(2,1)S(1)}, u32[]{:S(2)}, u32[]{:S(2)}) collective-permute-start(bf16[4,32,512]{2,1,0:T(8,128)(2,1)S(1)} %get-tuple-element.148), channel_id=1, source_target_pairs={{0,12},{1,13},{2,14},{3,15},{4,0},{5,1},{6,2},{7,3},{8,4},{9,5},{1... | collective-permute-start | bytes 393224 | tf_op jit(solution)/shard_map/ppermute | solution.py:492
  103.8 4.5 %collective-permute-done.17.refs_2_ = bf16[4,32,512]{2,1,0:T(8,128)(2,1)S(1)} collective-permute-done((bf16[4,32,512]{2,1,0:T(8,128)(2,1)S(1)}, bf16[4,32,512]{2,1,0:T(8,128)(2,1)S(1)}, u32[]{:S(2)}, u32[]{:S(2)}) %collective-permute-start.17) | collective-permute-done | bytes 131104 | tf_op jit(solution)/shard_map/ppermute | solution.py:492
  108.3 3.6 %collective-permute-done.18.refs_3_ = bf16[4,32,512]{2,1,0:T(8,128)(2,1)S(1)} collective-permute-done((bf16[4,32,512]{2,1,0:T(8,128)(2,1)S(1)}, bf16[4,32,512]{2,1,0:T(8,128)(2,1)S(1)}, u32[]{:S(2)}, u32[]{:S(2)}) %collective-permute-start.18) | collective-permute-done | bytes 131104 | tf_op jit(solution)/shard_map/ppermute | solution.py:492
  112.0 2.9 %collective-permute-start.25 = (bf16[4,32,512]{2,1,0:T(8,128)(2,1)S(1)}, bf16[4,32,512]{2,1,0:T(8,128)(2,1)S(1)}, u32[]{:S(2)}, u32[]{:S(2)}) collective-permute-start(bf16[4,32,512]{2,1,0:T(8,128)(2,1)S(1)} %shard_map.187.refs_1_), channel_id=1, source_target_pairs={{0,12},{1,13},{2,14},{3,15},{4,0},{5,1},{6,2},{7,3},{8,4},{9,5},{1... | collective-permute-start | bytes 393224 | tf_op jit(solution)/shard_map/ppermute | solution.py:492
  115.0 0.9 collective-permute-start.24
  115.9 1.3 shard_map.189
  117.1 1.7 %collective-permute-done.25.refs_4_ = bf16[4,32,512]{2,1,0:T(8,128)(2,1)S(1)} collective-permute-done((bf16[4,32,512]{2,1,0:T(8,128)(2,1)S(1)}, bf16[4,32,512]{2,1,0:T(8,128)(2,1)S(1)}, u32[]{:S(2)}, u32[]{:S(2)}) %collective-permute-start.25) | collective-permute-done | bytes 131104 | tf_op jit(solution)/shard_map/ppermute | solution.py:492
  118.9 9.2 %collective-permute-done.24.refs_3_ = bf16[4,32,512]{2,1,0:T(8,128)(2,1)S(1)} collective-permute-done((bf16[4,32,512]{2,1,0:T(8,128)(2,1)S(1)}, bf16[4,32,512]{2,1,0:T(8,128)(2,1)S(1)}, u32[]{:S(2)}, u32[]{:S(2)}) %collective-permute-start.24) | collective-permute-done | bytes 131104 | tf_op jit(solution)/shard_map/ppermute | solution.py:492
  128.7 0.5 collective-permute-start.30
  129.2 0.9 collective-permute-start.31
  130.0 1.1 collective-permute-start.32
  131.2 0.5 shard_map.191.refs_1_
  131.7 16.8 %collective-permute-start.34 = (bf16[4,128,512]{2,1,0:T(8,128)(2,1)S(1)}, bf16[4,128,512]{2,1,0:T(8,128)(2,1)S(1)}, u32[]{:S(2)}, u32[]{:S(2)}) collective-permute-start(bf16[4,128,512]{2,1,0:T(8,128)(2,1)S(1)} %shard_map.190.refs_5_.refs_1_), channel_id=1, source_target_pairs={{0,1},{1,0},{2,3},{3,2},{4,5},{5,4},{6,7},{7,6},{8,9},{9,8},{10,11... | collective-permute-start | bytes 1572872 | tf_op jit(solution)/shard_map/ppermute | solution.py:492
  148.6 1.6 %collective-permute-done.31.refs_8_ = bf16[128,512]{1,0:T(8,128)(2,1)S(1)} collective-permute-done((bf16[128,512]{1,0:T(8,128)(2,1)S(1)}, bf16[128,512]{1,0:T(8,128)(2,1)S(1)}, u32[]{:S(2)}, u32[]{:S(2)}) %collective-permute-start.31) | collective-permute-done | bytes 131104 | tf_op jit(solution)/shard_map/ppermute | solution.py:21
  150.2 1.6 %shard_map.192.refs_1_ = bf16[320,512]{1,0:T(8,128)(2,1)} custom-call(s32[1]{0:T(128)} %bitcast.refs_0_.refs_2_, f32[320,512]{1,0:T(8,128)S(1)} %shard_map.191.refs_1_, bf16[1536,512]{1,0:T(8,128)(2,1)S(1)} %get-tuple-element.85.refs_4_.refs_6_.refs_2_.refs_3_, s32[11,1,128]{2,1,0:T(1,128)S(1)} %get-tuple-element.84.refs_1_.refs_2_.refs_3_, ...), custom_call_target="tpu_custom_call" | custom-call | flops 1 | bytes 1 | tf_op jit(solution)/shard_map/pallas_call | solution.py:89
  151.8 1.9 %collective-permute-done.35.refs_4_ = bf16[4,128,512]{2,1,0:T(8,128)(2,1)S(1)} collective-permute-done((bf16[4,128,512]{2,1,0:T(8,128)(2,1)S(1)}, bf16[4,128,512]{2,1,0:T(8,128)(2,1)S(1)}, u32[]{:S(2)}, u32[]{:S(2)}) %collective-permute-start.35) | collective-permute-done | bytes 524320 | tf_op jit(solution)/shard_map/ppermute | solution.py:492
  153.7 1.5 shard_map.194
  (50 shorter events, 2.6 us)
Async XLA Ops:
  18.4 5.5 %collective-permute-start.1 = (bf16[128,512]{1,0:T(8,128)(2,1)S(1)}, bf16[128,512]{1,0:T(8,128)(2,1)S(1)}, u32[]{:S(2)}, u32[]{:S(2)}) collective-permute-start(bf16[128,512]{1,0:T(8,128)(2,1)S(1)} %get-tuple-element.94), channel_id=1, source_target_pairs={{1,0},{2,1},{3,2},{4,3},{5,4},{6,5},{7,6},{8,7},{9,8},{10,9},{11,1... | collective-permute-start | bytes 393224 | tf_op jit(solution)/shard_map/ppermute | solution.py:21
  18.6 9.1 %collective-permute-start.2 = (bf16[128,512]{1,0:T(8,128)(2,1)S(1)}, bf16[128,512]{1,0:T(8,128)(2,1)S(1)}, u32[]{:S(2)}, u32[]{:S(2)}) collective-permute-start(bf16[128,512]{1,0:T(8,128)(2,1)S(1)} %get-tuple-element.95), channel_id=1, source_target_pairs={{14,0},{15,1},{0,2},{1,3},{2,4},{3,5},{4,6},{5,7},{6,8},{7,9},{8,1... | collective-permute-start | bytes 393224 | tf_op jit(solution)/shard_map/ppermute | solution.py:21
  19.8 19.6 %collective-permute-start.6 = (bf16[256,512]{1,0:T(8,128)(2,1)S(1)}, bf16[256,512]{1,0:T(8,128)(2,1)S(1)}, u32[]{:S(2)}, u32[]{:S(2)}) collective-permute-start(bf16[256,512]{1,0:T(8,128)(2,1)S(1)} %get-tuple-element.103), channel_id=1, source_target_pairs={{8,0},{9,1},{10,2},{11,3},{12,4},{13,5},{14,6},{15,7},{0,8},{1,9},... | collective-permute-start | bytes 786440 | tf_op jit(solution)/shard_map/ppermute | solution.py:21
  20.6 11.6 %collective-permute-start.3 = (bf16[128,512]{1,0:T(8,128)(2,1)S(1)}, bf16[128,512]{1,0:T(8,128)(2,1)S(1)}, u32[]{:S(2)}, u32[]{:S(2)}) collective-permute-start(bf16[128,512]{1,0:T(8,128)(2,1)S(1)} %get-tuple-element.96), channel_id=1, source_target_pairs={{2,0},{3,1},{4,2},{5,3},{6,4},{7,5},{8,6},{9,7},{10,8},{11,9},{12,... | collective-permute-start | bytes 393224 | tf_op jit(solution)/shard_map/ppermute | solution.py:21
  23.9 11.1 %collective-permute-start = (bf16[128,512]{1,0:T(8,128)(2,1)S(1)}, bf16[128,512]{1,0:T(8,128)(2,1)S(1)}, u32[]{:S(2)}, u32[]{:S(2)}) collective-permute-start(bf16[128,512]{1,0:T(8,128)(2,1)S(1)} %get-tuple-element.88.refs_7_), channel_id=1, source_target_pairs={{15,0},{0,1},{1,2},{2,3},{3,4},{4,5},{5,6},{6,7},{7,8},{8,9},{9,10... | collective-permute-start | bytes 393224 | tf_op jit(solution)/shard_map/ppermute | solution.py:21
  23.9 12.7 %collective-permute-start.4 = (bf16[128,512]{1,0:T(8,128)(2,1)S(1)}, bf16[128,512]{1,0:T(8,128)(2,1)S(1)}, u32[]{:S(2)}, u32[]{:S(2)}) collective-permute-start(bf16[128,512]{1,0:T(8,128)(2,1)S(1)} %get-tuple-element.101), channel_id=1, source_target_pairs={{12,0},{13,1},{14,2},{15,3},{0,4},{1,5},{2,6},{3,7},{4,8},{5,9},{6... | collective-permute-start | bytes 393224 | tf_op jit(solution)/shard_map/ppermute | solution.py:21
  27.8 11.6 %collective-permute-start.5 = (bf16[128,512]{1,0:T(8,128)(2,1)S(1)}, bf16[128,512]{1,0:T(8,128)(2,1)S(1)}, u32[]{:S(2)}, u32[]{:S(2)}) collective-permute-start(bf16[128,512]{1,0:T(8,128)(2,1)S(1)} %get-tuple-element.102), channel_id=1, source_target_pairs={{4,0},{5,1},{6,2},{7,3},{8,4},{9,5},{10,6},{11,7},{12,8},{13,9},{1... | collective-permute-start | bytes 393224 | tf_op jit(solution)/shard_map/ppermute | solution.py:21
  45.2 2.4 %collective-permute-start.10 = (bf16[3,256,512]{2,1,0:T(8,128)(2,1)S(1)}, bf16[3,256,512]{2,1,0:T(8,128)(2,1)S(1)}, u32[]{:S(2)}, u32[]{:S(2)}) collective-permute-start(bf16[3,256,512]{2,1,0:T(8,128)(2,1)S(1)} %get-tuple-element.134), channel_id=1, source_target_pairs={{0,1},{1,0},{2,3},{3,2},{4,5},{5,4},{6,7},{7,6},{8,9},{9,8},{10,11... | collective-permute-start | bytes 2359304 | tf_op jit(solution)/shard_map/ppermute | solution.py:492
  47.7 23.4 %collective-permute-start.11 = (bf16[3,128,512]{2,1,0:T(8,128)(2,1)S(1)}, bf16[3,128,512]{2,1,0:T(8,128)(2,1)S(1)}, u32[]{:S(2)}, u32[]{:S(2)}) collective-permute-start(bf16[3,128,512]{2,1,0:T(8,128)(2,1)S(1)} %get-tuple-element.135), channel_id=1, source_target_pairs={{0,2},{1,3},{2,0},{3,1},{4,6},{5,7},{6,4},{7,5},{8,10},{9,11},{10,... | collective-permute-start | bytes 1179656 | tf_op jit(solution)/shard_map/ppermute | solution.py:492
  52.7 18.4 %collective-permute-start.9 = (bf16[256,512]{1,0:T(8,128)(2,1)S(1)}, bf16[256,512]{1,0:T(8,128)(2,1)S(1)}, u32[]{:S(2)}, u32[]{:S(2)}) collective-permute-start(bf16[256,512]{1,0:T(8,128)(2,1)S(1)} %get-tuple-element.120.refs_19_.refs_14_), channel_id=1, source_target_pairs={{8,0},{9,1},{10,2},{11,3},{12,4},{13,5},{14,6},{15,7},{0,8},{1,9},... | collective-permute-start | bytes 786440 | tf_op jit(solution)/shard_map/ppermute | solution.py:21
  53.1 9.5 %collective-permute-start.7 = (bf16[128,512]{1,0:T(8,128)(2,1)S(1)}, bf16[128,512]{1,0:T(8,128)(2,1)S(1)}, u32[]{:S(2)}, u32[]{:S(2)}) collective-permute-start(bf16[128,512]{1,0:T(8,128)(2,1)S(1)} %get-tuple-element.118.refs_17_.refs_12_), channel_id=1, source_target_pairs={{4,0},{5,1},{6,2},{7,3},{8,4},{9,5},{10,6},{11,7},{12,8},{13,9},{1... | collective-permute-start | bytes 393224 | tf_op jit(solution)/shard_map/ppermute | solution.py:21
  56.5 11.8 %collective-permute-start.8 = (bf16[128,512]{1,0:T(8,128)(2,1)S(1)}, bf16[128,512]{1,0:T(8,128)(2,1)S(1)}, u32[]{:S(2)}, u32[]{:S(2)}) collective-permute-start(bf16[128,512]{1,0:T(8,128)(2,1)S(1)} %get-tuple-element.119.refs_18_.refs_13_), channel_id=1, source_target_pairs={{12,0},{13,1},{14,2},{15,3},{0,4},{1,5},{2,6},{3,7},{4,8},{5,9},{6... | collective-permute-start | bytes 393224 | tf_op jit(solution)/shard_map/ppermute | solution.py:21
  71.1 2.7 %collective-permute-start.12 = (bf16[4,256,512]{2,1,0:T(8,128)(2,1)S(1)}, bf16[4,256,512]{2,1,0:T(8,128)(2,1)S(1)}, u32[]{:S(2)}, u32[]{:S(2)}) collective-permute-start(bf16[4,256,512]{2,1,0:T(8,128)(2,1)S(1)} %shard_map.180.refs_3_), channel_id=1, source_target_pairs={{0,1},{1,0},{2,3},{3,2},{4,5},{5,4},{6,7},{7,6},{8,9},{9,8},{10,11... | collective-permute-start | bytes 3145736 | tf_op jit(solution)/shard_map/ppermute | solution.py:492
  73.9 15.2 %collective-permute-start.13 = (bf16[4,128,512]{2,1,0:T(8,128)(2,1)S(1)}, bf16[4,128,512]{2,1,0:T(8,128)(2,1)S(1)}, u32[]{:S(2)}, u32[]{:S(2)}) collective-permute-start(bf16[4,128,512]{2,1,0:T(8,128)(2,1)S(1)} %get-tuple-element.141), channel_id=1, source_target_pairs={{0,2},{1,3},{2,0},{3,1},{4,6},{5,7},{6,4},{7,5},{8,10},{9,11},{10,... | collective-permute-start | bytes 1572872 | tf_op jit(solution)/shard_map/ppermute | solution.py:492
  74.2 8.8 %collective-permute-start.14 = (bf16[3,32,512]{2,1,0:T(8,128)(2,1)S(1)}, bf16[3,32,512]{2,1,0:T(8,128)(2,1)S(1)}, u32[]{:S(2)}, u32[]{:S(2)}) collective-permute-start(bf16[3,32,512]{2,1,0:T(8,128)(2,1)S(1)} %get-tuple-element.142), channel_id=1, source_target_pairs={{0,4},{1,5},{2,6},{3,7},{4,8},{5,9},{6,10},{7,11},{8,12},{9,13},{1... | collective-permute-start | bytes 294920 | tf_op jit(solution)/shard_map/ppermute | solution.py:492
  76.8 8.2 %collective-permute-start.15 = (bf16[3,32,512]{2,1,0:T(8,128)(2,1)S(1)}, bf16[3,32,512]{2,1,0:T(8,128)(2,1)S(1)}, u32[]{:S(2)}, u32[]{:S(2)}) collective-permute-start(bf16[3,32,512]{2,1,0:T(8,128)(2,1)S(1)} %get-tuple-element.143), channel_id=1, source_target_pairs={{0,8},{1,9},{2,10},{3,11},{4,12},{5,13},{6,14},{7,15},{8,0},{9,1},... | collective-permute-start | bytes 294920 | tf_op jit(solution)/shard_map/ppermute | solution.py:492
  76.8 8.2 %collective-permute-start.16 = (bf16[3,32,512]{2,1,0:T(8,128)(2,1)S(1)}, bf16[3,32,512]{2,1,0:T(8,128)(2,1)S(1)}, u32[]{:S(2)}, u32[]{:S(2)}) collective-permute-start(bf16[3,32,512]{2,1,0:T(8,128)(2,1)S(1)} %get-tuple-element.144), channel_id=1, source_target_pairs={{0,12},{1,13},{2,14},{3,15},{4,0},{5,1},{6,2},{7,3},{8,4},{9,5},{1... | collective-permute-start | bytes 294920 | tf_op jit(solution)/shard_map/ppermute | solution.py:492
  85.1 6.5 %collective-permute-start.22 = (bf16[3,32,512]{2,1,0:T(8,128)(2,1)S(1)}, bf16[3,32,512]{2,1,0:T(8,128)(2,1)S(1)}, u32[]{:S(2)}, u32[]{:S(2)}) collective-permute-start(bf16[3,32,512]{2,1,0:T(8,128)(2,1)S(1)} %shard_map.184.refs_3_.refs_1_), channel_id=1, source_target_pairs={{0,12},{1,13},{2,14},{3,15},{4,0},{5,1},{6,2},{7,3},{8,4},{9,5},{1... | collective-permute-start | bytes 294920 | tf_op jit(solution)/shard_map/ppermute | solution.py:492
  88.5 9.7 %collective-permute-start.21 = (bf16[3,32,512]{2,1,0:T(8,128)(2,1)S(1)}, bf16[3,32,512]{2,1,0:T(8,128)(2,1)S(1)}, u32[]{:S(2)}, u32[]{:S(2)}) collective-permute-start(bf16[3,32,512]{2,1,0:T(8,128)(2,1)S(1)} %shard_map.184.refs_3_.refs_1_), channel_id=1, source_target_pairs={{0,8},{1,9},{2,10},{3,11},{4,12},{5,13},{6,14},{7,15},{8,0},{9,1},... | collective-permute-start | bytes 294920 | tf_op jit(solution)/shard_map/ppermute | solution.py:492
  89.2 9.0 %collective-permute-start.20 = (bf16[3,32,512]{2,1,0:T(8,128)(2,1)S(1)}, bf16[3,32,512]{2,1,0:T(8,128)(2,1)S(1)}, u32[]{:S(2)}, u32[]{:S(2)}) collective-permute-start(bf16[3,32,512]{2,1,0:T(8,128)(2,1)S(1)} %shard_map.184.refs_3_.refs_1_), channel_id=1, source_target_pairs={{0,4},{1,5},{2,6},{3,7},{4,8},{5,9},{6,10},{7,11},{8,12},{9,13},{1... | collective-permute-start | bytes 294920 | tf_op jit(solution)/shard_map/ppermute | solution.py:492
  98.2 13.7 %collective-permute-start.26 = (bf16[3,128,512]{2,1,0:T(8,128)(2,1)S(1)}, bf16[3,128,512]{2,1,0:T(8,128)(2,1)S(1)}, u32[]{:S(2)}, u32[]{:S(2)}) collective-permute-start(bf16[3,128,512]{2,1,0:T(8,128)(2,1)S(1)} %shard_map.186.refs_5_.refs_1_), channel_id=1, source_target_pairs={{0,2},{1,3},{2,0},{3,1},{4,6},{5,7},{6,4},{7,5},{8,10},{9,11},{10,... | collective-permute-start | bytes 1179656 | tf_op jit(solution)/shard_map/ppermute | solution.py:492
  100.0 8.3 %collective-permute-start.17 = (bf16[4,32,512]{2,1,0:T(8,128)(2,1)S(1)}, bf16[4,32,512]{2,1,0:T(8,128)(2,1)S(1)}, u32[]{:S(2)}, u32[]{:S(2)}) collective-permute-start(bf16[4,32,512]{2,1,0:T(8,128)(2,1)S(1)} %get-tuple-element.146), channel_id=1, source_target_pairs={{0,4},{1,5},{2,6},{3,7},{4,8},{5,9},{6,10},{7,11},{8,12},{9,13},{1... | collective-permute-start | bytes 393224 | tf_op jit(solution)/shard_map/ppermute | solution.py:492
  100.0 11.9 %collective-permute-start.18 = (bf16[4,32,512]{2,1,0:T(8,128)(2,1)S(1)}, bf16[4,32,512]{2,1,0:T(8,128)(2,1)S(1)}, u32[]{:S(2)}, u32[]{:S(2)}) collective-permute-start(bf16[4,32,512]{2,1,0:T(8,128)(2,1)S(1)} %get-tuple-element.147), channel_id=1, source_target_pairs={{0,8},{1,9},{2,10},{3,11},{4,12},{5,13},{6,14},{7,15},{8,0},{9,1},... | collective-permute-start | bytes 393224 | tf_op jit(solution)/shard_map/ppermute | solution.py:492
  101.0 10.9 %collective-permute-start.19 = (bf16[4,32,512]{2,1,0:T(8,128)(2,1)S(1)}, bf16[4,32,512]{2,1,0:T(8,128)(2,1)S(1)}, u32[]{:S(2)}, u32[]{:S(2)}) collective-permute-start(bf16[4,32,512]{2,1,0:T(8,128)(2,1)S(1)} %get-tuple-element.148), channel_id=1, source_target_pairs={{0,12},{1,13},{2,14},{3,15},{4,0},{5,1},{6,2},{7,3},{8,4},{9,5},{1... | collective-permute-start | bytes 393224 | tf_op jit(solution)/shard_map/ppermute | solution.py:492
  103.8 12.1 %collective-permute-start.27 = (bf16[3,128,512]{2,1,0:T(8,128)(2,1)S(1)}, bf16[3,128,512]{2,1,0:T(8,128)(2,1)S(1)}, u32[]{:S(2)}, u32[]{:S(2)}) collective-permute-start(bf16[3,128,512]{2,1,0:T(8,128)(2,1)S(1)} %shard_map.186.refs_5_.refs_1_), channel_id=1, source_target_pairs={{0,1},{1,0},{2,3},{3,2},{4,5},{5,4},{6,7},{7,6},{8,9},{9,8},{10,11... | collective-permute-start | bytes 1179656 | tf_op jit(solution)/shard_map/ppermute | solution.py:492
  112.0 3.9 %collective-permute-start.28 = (bf16[3,128,512]{2,1,0:T(8,128)(2,1)S(1)}, bf16[3,128,512]{2,1,0:T(8,128)(2,1)S(1)}, u32[]{:S(2)}, u32[]{:S(2)}) collective-permute-start(bf16[3,128,512]{2,1,0:T(8,128)(2,1)S(1)} %shard_map.188.refs_2_), channel_id=1, source_target_pairs={{0,1},{1,0},{2,3},{3,2},{4,5},{5,4},{6,7},{7,6},{8,9},{9,8},{10,11... | collective-permute-start | bytes 1179656 | tf_op jit(solution)/shard_map/ppermute | solution.py:492
  112.0 6.8 %collective-permute-start.25 = (bf16[4,32,512]{2,1,0:T(8,128)(2,1)S(1)}, bf16[4,32,512]{2,1,0:T(8,128)(2,1)S(1)}, u32[]{:S(2)}, u32[]{:S(2)}) collective-permute-start(bf16[4,32,512]{2,1,0:T(8,128)(2,1)S(1)} %shard_map.187.refs_1_), channel_id=1, source_target_pairs={{0,12},{1,13},{2,14},{3,15},{4,0},{5,1},{6,2},{7,3},{8,4},{9,5},{1... | collective-permute-start | bytes 393224 | tf_op jit(solution)/shard_map/ppermute | solution.py:492
  115.0 13.1 %collective-permute-start.24 = (bf16[4,32,512]{2,1,0:T(8,128)(2,1)S(1)}, bf16[4,32,512]{2,1,0:T(8,128)(2,1)S(1)}, u32[]{:S(2)}, u32[]{:S(2)}) collective-permute-start(bf16[4,32,512]{2,1,0:T(8,128)(2,1)S(1)} %shard_map.187.refs_1_), channel_id=1, source_target_pairs={{0,8},{1,9},{2,10},{3,11},{4,12},{5,13},{6,14},{7,15},{8,0},{9,1},... | collective-permute-start | bytes 393224 | tf_op jit(solution)/shard_map/ppermute | solution.py:492
  115.9 12.2 %collective-permute-start.23 = (bf16[4,32,512]{2,1,0:T(8,128)(2,1)S(1)}, bf16[4,32,512]{2,1,0:T(8,128)(2,1)S(1)}, u32[]{:S(2)}, u32[]{:S(2)}) collective-permute-start(bf16[4,32,512]{2,1,0:T(8,128)(2,1)S(1)} %shard_map.187.refs_1_), channel_id=1, source_target_pairs={{0,4},{1,5},{2,6},{3,7},{4,8},{5,9},{6,10},{7,11},{8,12},{9,13},{1... | collective-permute-start | bytes 393224 | tf_op jit(solution)/shard_map/ppermute | solution.py:492
  128.2 23.6 %collective-permute-start.33 = (bf16[4,128,512]{2,1,0:T(8,128)(2,1)S(1)}, bf16[4,128,512]{2,1,0:T(8,128)(2,1)S(1)}, u32[]{:S(2)}, u32[]{:S(2)}) collective-permute-start(bf16[4,128,512]{2,1,0:T(8,128)(2,1)S(1)} %shard_map.190.refs_5_.refs_1_), channel_id=1, source_target_pairs={{0,2},{1,3},{2,0},{3,1},{4,6},{5,7},{6,4},{7,5},{8,10},{9,11},{10,... | collective-permute-start | bytes 1572872 | tf_op jit(solution)/shard_map/ppermute | solution.py:492
  128.7 3.1 %collective-permute-start.29 = (bf16[128,512]{1,0:T(8,128)(2,1)S(1)}, bf16[128,512]{1,0:T(8,128)(2,1)S(1)}, u32[]{:S(2)}, u32[]{:S(2)}) collective-permute-start(bf16[128,512]{1,0:T(8,128)(2,1)S(1)} %get-tuple-element.114.refs_13_.refs_8_), channel_id=1, source_target_pairs={{1,0},{2,1},{3,2},{4,3},{5,4},{6,5},{7,6},{8,7},{9,8},{10,9},{11,1... | collective-permute-start | bytes 393224 | tf_op jit(solution)/shard_map/ppermute | solution.py:21
  128.7 19.9 %collective-permute-start.30 = (bf16[128,512]{1,0:T(8,128)(2,1)S(1)}, bf16[128,512]{1,0:T(8,128)(2,1)S(1)}, u32[]{:S(2)}, u32[]{:S(2)}) collective-permute-start(bf16[128,512]{1,0:T(8,128)(2,1)S(1)} %get-tuple-element.115.refs_14_.refs_9_), channel_id=1, source_target_pairs={{15,0},{0,1},{1,2},{2,3},{3,4},{4,5},{5,6},{6,7},{7,8},{8,9},{9,10... | collective-permute-start | bytes 393224 | tf_op jit(solution)/shard_map/ppermute | solution.py:21
  129.2 21.0 %collective-permute-start.31 = (bf16[128,512]{1,0:T(8,128)(2,1)S(1)}, bf16[128,512]{1,0:T(8,128)(2,1)S(1)}, u32[]{:S(2)}, u32[]{:S(2)}) collective-permute-start(bf16[128,512]{1,0:T(8,128)(2,1)S(1)} %get-tuple-element.116.refs_15_.refs_10_), channel_id=1, source_target_pairs={{2,0},{3,1},{4,2},{5,3},{6,4},{7,5},{8,6},{9,7},{10,8},{11,9},{12,... | collective-permute-start | bytes 393224 | tf_op jit(solution)/shard_map/ppermute | solution.py:21
  130.0 20.1 %collective-permute-start.32 = (bf16[128,512]{1,0:T(8,128)(2,1)S(1)}, bf16[128,512]{1,0:T(8,128)(2,1)S(1)}, u32[]{:S(2)}, u32[]{:S(2)}) collective-permute-start(bf16[128,512]{1,0:T(8,128)(2,1)S(1)} %get-tuple-element.117.refs_16_.refs_11_), channel_id=1, source_target_pairs={{14,0},{15,1},{0,2},{1,3},{2,4},{3,5},{4,6},{5,7},{6,8},{7,9},{8,1... | collective-permute-start | bytes 393224 | tf_op jit(solution)/shard_map/ppermute | solution.py:21
  131.7 20.1 %collective-permute-start.34 = (bf16[4,128,512]{2,1,0:T(8,128)(2,1)S(1)}, bf16[4,128,512]{2,1,0:T(8,128)(2,1)S(1)}, u32[]{:S(2)}, u32[]{:S(2)}) collective-permute-start(bf16[4,128,512]{2,1,0:T(8,128)(2,1)S(1)} %shard_map.190.refs_5_.refs_1_), channel_id=1, source_target_pairs={{0,1},{1,0},{2,3},{3,2},{4,5},{5,4},{6,7},{7,6},{8,9},{9,8},{10,11... | collective-permute-start | bytes 1572872 | tf_op jit(solution)/shard_map/ppermute | solution.py:492
  151.8 1.9 %collective-permute-start.35 = (bf16[4,128,512]{2,1,0:T(8,128)(2,1)S(1)}, bf16[4,128,512]{2,1,0:T(8,128)(2,1)S(1)}, u32[]{:S(2)}, u32[]{:S(2)}) collective-permute-start(bf16[4,128,512]{2,1,0:T(8,128)(2,1)S(1)} %shard_map.193.refs_2_), channel_id=1, source_target_pairs={{0,1},{1,0},{2,3},{3,2},{4,5},{5,4},{6,7},{7,6},{8,9},{9,8},{10,11... | collective-permute-start | bytes 1572872 | tf_op jit(solution)/shard_map/ppermute | solution.py:492

commit v10 on v9

--- a/solution.py
+++ b/solution.py
@@ -351,31 +351,48 @@
         out_ref[...] = gpe_ref[i * cap : (i + 1) * cap, :]
 
 
-def node_weight_kernel(me_ref, node_ref, gathered_ref, gpn_ref, act_node_ref, gon_ref, keep_ref, sent_ref, block_ref):
-    put = functools.partial(put_block, me_ref, block_ref, keep_ref, sent_ref)
-    put(0, node_ref[...], gpn_ref[...])
-    put(1, gathered_ref[...], gpn_ref[...])
-    put(2, act_node_ref[...], gon_ref[...])
-
-
-def put_block(me_ref, block_ref, keep_ref, sent_ref, index, left_side, right_side):
+def deal_out(plan, me_ref, grad_ref, keep_ref, sent_ref):
     core = lax.rem(me_ref[0], 2)
-    half = block_ref.shape[0] // 2
-    block_ref[...] = dot_lt(left_side, right_side)
-    keep_ref[index] = block_ref[pl.ds(pl.multiple_of(core * half, half), half), :]
-    other = block_ref[pl.ds(pl.multiple_of((1 - core) * half, half), half), :]
-    sent_ref[index] = other.astype(bf16)
+    outer, inner = keep_ref.shape[:2]
+    for i in range(outer):
+        for j in range(inner):
+            pair = (i * inner + j) * 2
+            at = 0
+            for first, rows in plan:
+                for side, out_ref in ((core, keep_ref), (1 - core, sent_ref)):
+                    start = pl.multiple_of(first + (pair + side) * rows, rows)
+                    piece = grad_ref[pl.ds(start, rows), :]
+                    out_ref[i, j, at : at + rows, :] = piece.astype(out_ref.dtype)
+                at += rows
+
+
+def node_weight_kernel(plan, *refs):
+    me_ref, node_ref, gathered_ref, gpn_ref, act_node_ref, gon_ref = refs[:6]
+    *deal_refs, grad_ref = refs[6:] if plan else (refs[6],)
+    width = node_ref.shape[1]
+    grad_ref[:width, :] = dot_lt(node_ref[...], gpn_ref[...])
+    grad_ref[width : 2 * width, :] = dot_lt(gathered_ref[...], gpn_ref[...])
+    grad_ref[2 * width :, :] = dot_lt(act_node_ref[...], gon_ref[...])
+    if plan:
+        deal_out(plan, me_ref, grad_ref, *deal_refs)
 
 
 def weight_kernel(plan, *refs):
-    order, sx_count, gpe_count, act_count, goe_count = plan
+    order, counts, cuts = plan
     edge_ref, hot_ref, me_ref, node_ref = refs[:4]
     refs = refs[4:]
-    sx_refs, refs = refs[:sx_count], refs[sx_count:]
-    gpe_refs, refs = refs[:gpe_count], refs[gpe_count:]
-    act_refs, refs = refs[:act_count], refs[act_count:]
-    goe_refs, refs = refs[:goe_count], refs[goe_count:]
-    keep_ref, sent_ref, rsum_ref, x_ref, sx_ref, gpe_ref, act_ref, goe_ref, block_ref = refs
+    groups = []
+    for count in counts:
+        groups.append(refs[:count])
+        refs = refs[count:]
+    sx_refs, gpe_refs, act_refs, goe_refs = groups
+    rsum_ref, refs = refs[0], refs[1:]
+    if cuts:
+        deal_refs, refs = refs[:2], refs[2:]
+        x_ref, sx_ref, gpe_ref, act_ref, goe_ref, grad_ref = refs
+    else:
+        grad_ref, x_ref, sx_ref, gpe_ref, act_ref, goe_ref = refs
+    width = node_ref.shape[1]
     cap = edge_ref.shape[1]
     for i, k in enumerate(order):
         x_ref[i * cap : (i + 1) * cap, :] = edge_ref[k]
@@ -385,11 +402,12 @@
     stack_into(goe_ref, goe_refs)
     recv_sum = dot(hot_ref[...], gpe_ref[...]).astype(bf16)
     rsum_ref[...] = recv_sum
-    put = functools.partial(put_block, me_ref, block_ref, keep_ref, sent_ref)
-    put(0, x_ref[...], gpe_ref[...])
-    put(1, sx_ref[...], gpe_ref[...])
-    put(2, node_ref[...], recv_sum)
-    put(3, act_ref[...], goe_ref[...])
+    grad_ref[:width, :] = dot_lt(x_ref[...], gpe_ref[...])
+    grad_ref[width : 2 * width, :] = dot_lt(sx_ref[...], gpe_ref[...])
+    grad_ref[2 * width : 3 * width, :] = dot_lt(node_ref[...], recv_sum)
+    grad_ref[3 * width :, :] = dot_lt(act_ref[...], goe_ref[...])
+    if cuts:
+        deal_out(cuts, me_ref, grad_ref, *deal_refs)
 
 
 def base_kernel(ncot_ref, gpn_ref, rsum_ref, w1_ref, n1_ref, base_ref):
@@ -443,45 +461,45 @@
 
 
 def add_kernel(plan, *refs):
-    came, stride, members = plan
+    came, stride, members, axis = plan
     me_ref, keep_ref = refs[:2]
     arr_refs, out_refs = refs[2 : 2 + came], refs[2 + came :]
-    size = keep_ref.shape[1] // members
     here = place(me_ref, stride, members)
     for j, out_ref in enumerate(out_refs):
-        at = lax.rem(here + j, members) * size
-        rows = pl.ds(pl.multiple_of(at, size), size)
-        piece = keep_ref[:, rows, :]
+        at = lax.rem(here + j, members)
+        index = (slice(None), at) if axis else (at,)
+        piece = keep_ref[index]
         for arr_ref in arr_refs:
-            piece += arr_ref[:, rows, :].astype(f32)
+            piece += arr_ref[index].astype(f32)
         out_ref[...] = piece.astype(out_ref.dtype)
 
 
-def gather_kernel(plan, *refs):
-    stride, members = plan
-    me_ref, piece_refs, out_ref = refs[0], refs[1:-1], refs[-1]
-    size = piece_refs[0].shape[1]
-    here = place(me_ref, stride, members)
-    for j, piece_ref in enumerate(piece_refs):
-        at = lax.rem(here + members - j, members) * size
-        out_ref[:, pl.ds(pl.multiple_of(at, size), size), :] = piece_ref[...]
-
-
-def join_kernel(plan, *refs):
-    members, blocks = plan
-    me_ref = refs[0]
-    piece_refs, other_refs = refs[1 : 1 + members], refs[1 + members : 1 + 2 * members]
-    out_refs = refs[1 + 2 * members :]
-    size = piece_refs[0].shape[1]
-    core = lax.rem(me_ref[0], 2)
-    here = place(me_ref, 2, members)
-    for index, (which, block) in enumerate(blocks):
-        first = 2 * block * members * size
-        for side, side_refs in ((core, piece_refs), (1 - core, other_refs)):
-            for j, piece_ref in enumerate(side_refs):
-                at = first + (side * members + lax.rem(here + members - j, members)) * size
-                rows = pl.ds(pl.multiple_of(at, size), size)
-                out_refs[which][rows, :] = piece_ref[index]
+def last_kernel(counts, *refs):
+    refs, out_ref = refs[:-1], refs[-1]
+    at = 0
+    for count in counts:
+        keep_ref, arr_refs, refs = refs[0], refs[1:count], refs[count:]
+        piece = keep_ref[...]
+        for arr_ref in arr_refs:
+            piece += arr_ref[...].astype(f32)
+        out_ref[at : at + keep_ref.shape[0], :] = piece.astype(bf16)
+        at += keep_ref.shape[0]
+
+
+def sort_kernel(plan, in_ref, *refs):
+    bands, sizes = plan
+    out_refs, sems = refs[:-1], refs[-1]
+    copies = []
+    for band in range(bands):
+        at = band * sum(sizes)
+        for size, out_ref in zip(sizes, out_refs):
+            source, target = in_ref.at[pl.ds(at, size)], out_ref.at[pl.ds(band * size, size)]
+            copies.append(pltpu.make_async_copy(source, target, sems.at[len(copies)]))
+            at += size
+    for copy in copies:
+        copy.start()
+    for copy in copies:
+        copy.wait()
 
 
 def in_group(block, axis, stride, members, step):
@@ -500,12 +518,11 @@
     return first, chips // first
 
 
-def add_stage(me, keep, arrived, stride, members, kind, after):
-    count, rows, width = keep.shape
-    shape = (count, rows // members, width)
+def add_stage(me, keep, arrived, stride, members, axis, after):
+    shape = keep.shape[:axis] + keep.shape[axis + 1 :]
     outs = call(
-        functools.partial(add_kernel, (len(arrived), stride, members)),
-        [(shape, kind)] + [(shape, bf16)] * (members - 1),
+        functools.partial(add_kernel, (len(arrived), stride, members, axis)),
+        [(shape, f32)] + [(shape, bf16)] * (members - 1),
         [],
         me,
         keep,
@@ -514,6 +531,38 @@
         after=after,
     )
     return outs[0], [in_group(out, "band", stride, members, j + 1) for j, out in enumerate(outs[1:])]
+
+
+def last_sum(*chunks):
+    rows, width = sum(keep.shape[0] for keep, _ in chunks), chunks[0][0].shape[1]
+    (piece,) = call(
+        functools.partial(last_kernel, [1 + len(arrived) for _, arrived in chunks]),
+        [((rows, width), bf16)],
+        [],
+        *[array for keep, arrived in chunks for array in [keep, *arrived]],
+    )
+    return piece
+
+
+def gathered_from_all(piece, sizes, after):
+    width = piece.shape[1]
+    bands = lax.axis_size("band")
+    whole = lax.all_gather(piece, "band", axis=0, tiled=True)
+    count = bands * len(sizes)
+
+    def kernel(in_ref, *refs):
+        sort_kernel((bands, sizes), in_ref, *refs[len(after) :])
+
+    return pl.pallas_call(
+        kernel,
+        out_shape=[pltpu.HBM((bands * size, width), bf16) for size in sizes],
+        in_specs=[pl.BlockSpec(memory_space=pltpu.HBM)]
+        + [pl.BlockSpec(memory_space=pl.ANY)] * len(after),
+        out_specs=[pl.BlockSpec(memory_space=pltpu.HBM)] * len(sizes),
+        scratch_shapes=[pltpu.SemaphoreType.DMA((count,))],
+        compiler_params=pltpu.CompilerParams(vmem_limit_bytes=1024 * 1024),
+        cost_estimate=pl.CostEstimate(flops=1, bytes_accessed=1, transcendentals=0),
+    )(in_hbm(whole), *after)
 
 
 def held_until(array, after):
@@ -527,49 +576,6 @@
         compiler_params=pltpu.CompilerParams(vmem_limit_bytes=1024 * 1024),
         cost_estimate=pl.CostEstimate(flops=1, bytes_accessed=1, transcendentals=0),
     )(pltpu.with_memory_space_constraint(array, pltpu.VMEM), *after)
-
-
-def gather_stage(me, piece, stride, members, after):
-    count, rows, width = piece.shape
-    pieces = [piece] + [in_group(piece, "band", stride, members, j) for j in range(1, members)]
-    (mine,) = call(
-        functools.partial(gather_kernel, (stride, members)),
-        [((count, rows * members, width), bf16)],
-        [],
-        me,
-        *pieces,
-        smem=(0,),
-        after=after,
-    )
-    return mine
-
-
-def join_stage(me, mine, members, blocks, shapes, swap_after, after):
-    pieces = [in_group(mine, "band", 2, members, j) for j in range(1, members)]
-    pieces = [mine] + [held_until(piece, swap_after) if swap_after else piece for piece in pieces]
-    others = [in_group(one, "band", 1, 2, 1) for one in pieces]
-    return call(
-        functools.partial(join_kernel, (members, blocks)),
-        [(shape, bf16) for shape in shapes],
-        [],
-        me,
-        *pieces,
-        *others,
-        smem=(0,),
-        after=after,
-        last=range(len(shapes)),
-    )
-
-
-def reduce_whole(keep, sent):
-    bands = lax.axis_size("band")
-    chips = [[i for i in range(bands) if i % 2 == c] for c in range(2)]
-    total = keep + in_group(sent, "band", 1, 2, 1).astype(f32)
-    total = lax.psum(total.astype(bf16), "band", axis_index_groups=chips)
-    other = in_group(total, "band", 1, 2, 1)
-    core = lax.axis_index("band") % 2
-    low, high = jnp.where(core == 0, total, other), jnp.where(core == 0, other, total)
-    return jnp.concatenate([low, high], axis=1)
 
 
 def local(
@@ -609,6 +615,7 @@
 
     order = near + far
 
+    given_cotan, given_first = node_cotan, node_first
     (
         node_latent,
         send_ids,
@@ -734,7 +741,17 @@
     act_far, goe_far, normed_far, gathered, gpn, act_node, gon, gg, node_new = outs
     back_far = [passed_along(block, "band", -d) for block, d in zip(gpe_far, far_steps)]
 
-    half = (width // 2, width)
+    first, second = split_of(bands)
+    cut = width % (32 * bands) == 0
+    edge_sizes, node_sizes = (3 * width // bands, width // bands), (2 * width // bands, width // bands)
+    edge_cuts, node_cuts = ((0, edge_sizes[0]), (3 * width, edge_sizes[1])), ((0, node_sizes[0]), (2 * width, node_sizes[1]))
+
+    def weight_outs(sizes, rows):
+        if cut:
+            shape = (second, first, sum(sizes), width)
+            return [(shape, f32), (shape, bf16)]
+        return [((rows, width), f32)]
+
     outs = call(
         functools.partial(back_kernel, (near, local_count)),
         [((local_rows + near_rows, width), bf16), ((local_rows, width), bf16)]
@@ -758,10 +775,12 @@
 
     gpe = [gpe_local] + gpe_near + gpe_far
     sx_all = [sx_local] + sx_near + sx_far
-    keep_edge, sent_edge, recv_sum = call(
-        functools.partial(weight_kernel, (order, len(sx_all), len(gpe), 3, 2)),
-        [((4, *half), f32), ((4, *half), bf16), ((nodes, width), bf16)],
-        [((total, width), bf16)] * 5 + [((width, width), f32)],
+    recv_sum, *edge_weights = call(
+        functools.partial(
+            weight_kernel, (order, (len(sx_all), len(gpe), 3, 2), edge_cuts if cut else ())
+        ),
+        [((nodes, width), bf16)] + weight_outs(edge_sizes, 4 * width),
+        [((total, width), bf16)] * 5 + [((4 * width, width), f32)] * cut,
         edges,
         hot,
         me,
@@ -798,11 +817,11 @@
             base_kernel,
             [((nodes, width), f32)],
             [],
-            node_cotan,
+            given_cotan,
             gpn,
             recv_sum,
             edge_first,
-            node_first,
+            given_first,
             after=after,
         )
         (grad_nodes,) = call(
@@ -822,52 +841,40 @@
         )
         return grad_nodes
 
-    def node_weights(after):
-        return call(
-            node_weight_kernel,
-            [((3, *half), f32), ((3, *half), bf16)],
-            [((width, width), f32)],
-            me,
-            node_latent,
-            gathered,
-            gpn,
-            act_node,
-            gon,
-            smem=(0,),
-            after=after,
-        )
-
-    first, second = split_of(bands)
-    node_blocks, node_shapes = ((0, 0), (0, 1), (1, 0)), [(2 * width, width), (width, width)]
-    edge_blocks = ((0, 0), (0, 1), (0, 2), (1, 0))
-    edge_shapes = [(3 * width, width), (width, width)]
-    if width // 2 % (16 * first * second) == 0:
-        along_y, along_z = (2, first), (2 * first, second)
-        keep_node, sent_node = node_weights([])
+    node_weights = call(
+        functools.partial(node_weight_kernel, node_cuts if cut else ()),
+        weight_outs(node_sizes, 3 * width),
+        [((3 * width, width), f32)] * cut,
+        me,
+        node_latent,
+        gathered,
+        gpn,
+        act_node,
+        gon,
+        smem=(0,),
+    )
+    if cut:
+        along_y, along_z = (2, first, 1), (2 * first, second, 0)
+        keep_node, sent_node = node_weights
+        keep_edge, sent_edge = edge_weights
         came_node = [in_group(sent_node, "band", 1, 2, 1)]
-        keep_node, came_node = add_stage(me, keep_node, came_node, *along_y, f32, [])
+        keep_node, came_node = add_stage(me, keep_node, came_node, *along_y, [])
         sent_edge = held_until(sent_edge, back_far + came_node)
         came_edge = [in_group(sent_edge, "band", 1, 2, 1)]
-        keep_node, came_node = add_stage(me, keep_node, came_node, *along_z, f32, [sent_edge])
-        keep_edge, came_edge = add_stage(me, keep_edge, came_edge, *along_y, f32, [keep_node])
+        keep_node, came_node = add_stage(me, keep_node, came_node, *along_z, [sent_edge])
+        keep_edge, came_edge = add_stage(me, keep_edge, came_edge, *along_y, [keep_node])
         edge_new, grad_edges = edge_outputs([keep_edge])
-        piece_node, _ = add_stage(me, keep_node, came_node, 1, 1, bf16, [in_hbm(edge_new)])
-        keep_edge, came_edge = add_stage(me, keep_edge, came_edge, *along_z, f32, [piece_node])
-        mine_node = gather_stage(me, piece_node, *along_z, [keep_edge])
-        piece_edge, _ = add_stage(me, keep_edge, came_edge, 1, 1, bf16, [mine_node])
-        grad_n1, grad_n2 = join_stage(
-            me, mine_node, first, node_blocks, node_shapes, [piece_edge], []
-        )
-        mine_edge = gather_stage(me, piece_edge, *along_z, [in_hbm(grad_n2)])
-        grad_nodes = node_output([mine_edge])
-        grad_e1, grad_e2 = join_stage(
-            me, mine_edge, first, edge_blocks, edge_shapes, [in_hbm(grad_nodes)], []
+        keep_edge, came_edge = add_stage(me, keep_edge, came_edge, *along_z, [in_hbm(edge_new)] + came_node)
+        piece = last_sum((keep_edge, came_edge), (keep_node, came_node))
+        grad_nodes = node_output([piece])
+        grad_e1, grad_e2, grad_n1, grad_n2 = gathered_from_all(
+            piece, edge_sizes + node_sizes, [in_hbm(grad_nodes)]
         )
     else:
-        whole = reduce_whole(*node_weights([]))
-        grad_n1, grad_n2 = whole[:2].reshape(2 * width, width), whole[2]
-        whole = reduce_whole(keep_edge, sent_edge)
-        grad_e1, grad_e2 = whole[:3].reshape(3 * width, width), whole[3]
+        whole = lax.psum(node_weights[0], "band").astype(bf16)
+        grad_n1, grad_n2 = whole[: 2 * width], whole[2 * width :]
+        whole = lax.psum(edge_weights[0], "band").astype(bf16)
+        grad_e1, grad_e2 = whole[: 3 * width], whole[3 * width :]
         edge_new, grad_edges = edge_outputs([])
         grad_nodes = node_output([])
     return (

time: 155 us -> 277 us (1.79)
  Pallas kernels: 30.9 us -> 142 us
  starting transfers between devices: 53.3 us -> 29.5 us
  waiting for transfers between devices: 56.4 us -> 75 us
  between operations: 0.84 us -> 14.3 us
    pallas_call x0 -> x1, Pallas kernels: none -> 113 us  [gathered_from_all(): pl.pallas_call(kernel, out_shape=[pltpu.HBM((bands * size, width), bf16)...]
    all_gather x0 -> x1, waiting for transfers between devices: none -> 35.1 us  [gathered_from_all(): whole = lax.all_gather(piece, 'band', axis=0, tiled=True)]
    ppermute x22 -> x10, starting transfers between devices: 41.4 us -> 15.7 us  [in_group(): return lax.ppermute(block, axis, route)]
    ppermute x22 -> x10, waiting for transfers between devices: 36.8 us -> 16.3 us  [in_group(): return lax.ppermute(block, axis, route)]
    ppermute x14, waiting for transfers between devices: 19.6 us -> 23.6 us  [passed_along(): return lax.ppermute(block, axis, route)]
    pallas_call x21 -> x16, Pallas kernels: 27.7 us -> 25.5 us  [call(): pl.pallas_call(kernel, out_shape=[(pltpu.HBM if i in last else pltpu.VMEM...]
  transfers between devices with their start and end apart: 36 -> 25, of which waited for: 17 -> 16; matrix products, arithmetic and copies ran while one was open for 0% -> 0% of each run, Pallas kernels for 12% -> 6%
where the time goes in v10:
time: 277 us
  Pallas kernels  142 us (51%)
  waiting for transfers between devices  75 us (27%)
  starting transfers between devices  29.5 us (11%)
  between operations  14.3 us (5%)
  blocking collectives  13.7 us (5%)
    pallas_call x1, Pallas kernels, gathered_from_all(): pl.pallas_call(kernel, out_shape=[pltpu.HBM((bands * size, width), bf16)...  113 us
    all_gather x1, waiting for transfers between devices, gathered_from_all(): whole = lax.all_gather(piece, 'band', axis=0, tiled=True)  35.1 us
    pallas_call x16, Pallas kernels, call(): pl.pallas_call(kernel, out_shape=[(pltpu.HBM if i in last else pltpu.VMEM...  25.5 us
    ppermute x14, waiting for transfers between devices, passed_along(): return lax.ppermute(block, axis, route)  23.6 us
    ppermute x10, waiting for transfers between devices, in_group(): return lax.ppermute(block, axis, route)  16.3 us
    ppermute x10, starting transfers between devices, in_group(): return lax.ppermute(block, axis, route)  15.7 us
    ppermute x14, starting transfers between devices, passed_along(): return lax.ppermute(block, axis, route)  13.8 us
    all_to_all x1, blocking collectives, local(): ids = lax.all_to_all(ids, 'band', 0, 0, tiled=True)  13.7 us
  transfers between devices with their start and end apart: 25, of which 16 were waited for; matrix products, arithmetic and copies ran while one was open for 0% of the time, Pallas kernels for 6%

profile of v10, /device:TPU:0, one launch (start us, length us, event | category | flops | bytes accessed | tf_op | source)
XLA Modules:
  0.0 276.6 jit_solution(7653056903073249325)
XLA Ops:
  7.2 3.2 %shard_map.170 = (bf16[320,512]{1,0:T(8,128)(2,1)S(1)}, s32[11,1,128]{2,1,0:T(1,128)S(1)}, s32[11,1,128]{2,1,0:T(1,128)S(1)}, bf16[11,128,512]{2,1,0:T(8,128)(2,...) custom-call(s32[1]{0:T(128)} %bitcast.refs_0_.refs_2_, ...), custom_call_target="tpu_custom_call" | custom-call | flops 1 | bytes 1 | tf_op jit(solution)/shard_map/pallas_call | solution.py:120
  10.5 13.7 %all_to_all.5.refs_2_.refs_4_ = s32[16,1,256]{2,1,0:T(1,128)S(1)} all-to-all(s32[16,1,256]{2,1,0:T(1,128)S(1)} %shard_map.171), channel_id=1, replica_groups=mesh['groups'=2,'band'=16] {'band'}, dimensions={0} | all-to-all | bytes 32768 | tf_op jit(solution)/shard_map/all_to_all | solution.py:653
  24.2 0.8 shard_map.172
  24.9 0.3 collective-permute-start.1
  25.2 1.2 collective-permute-start.2
  26.4 0.8 collective-permute-start.6
  27.2 3.3 %collective-permute-start.3 = (bf16[128,512]{1,0:T(8,128)(2,1)S(1)}, bf16[128,512]{1,0:T(8,128)(2,1)S(1)}, u32[]{:S(2)}, u32[]{:S(2)}) collective-permute-start(bf16[128,512]{1,0:T(8,128)(2,1)S(1)} %get-tuple-element.96), channel_id=1, source_target_pairs={{2,0},{3,1},{4,2},{5,3},{6,4},{7,5},{8,6},{9,7},{10,8},{11,9},{12,... | collective-permute-start | bytes 393224 | tf_op jit(solution)/shard_map/ppermute | solution.py:21
  30.5 3.8 %collective-permute-done.2.refs_8_.refs_7_ = bf16[128,512]{1,0:T(8,128)(2,1)S(1)} collective-permute-done((bf16[128,512]{1,0:T(8,128)(2,1)S(1)}, bf16[128,512]{1,0:T(8,128)(2,1)S(1)}, u32[]{:S(2)}, u32[]{:S(2)}) %collective-permute-start.2) | collective-permute-done | bytes 131104 | tf_op jit(solution)/shard_map/ppermute | solution.py:21
  34.3 4.5 %shard_map.173 = (bf16[1408,320]{1,0:T(8,128)(2,1)S(1)}, bf16[320,1408]{1,0:T(8,128)(2,1)S(1)}, f32[1408,128]{1,0:T(8,128)S(1)}, f32[1024,512]{1,0:T(8,128)S(1)}...) custom-call(bf16[11,128,512]{2,1,0:T(8,128)(2,1)S(1)} %get-tuple-ele, ...), custom_call_target="tpu_custom_call" | custom-call | flops 1 | bytes 1 | tf_op jit(solution)/shard_map/pallas_call | solution.py:89
  38.9 2.7 collective-permute-done.refs_6_.refs_5_
  41.6 1.5 shard_map.174
  43.2 2.8 %collective-permute-done.5.refs_13_.refs_10_ = bf16[128,512]{1,0:T(8,128)(2,1)S(1)} collective-permute-done((bf16[128,512]{1,0:T(8,128)(2,1)S(1)}, bf16[128,512]{1,0:T(8,128)(2,1)S(1)}, u32[]{:S(2)}, u32[]{:S(2)}) %collective-permute-start.5) | collective-permute-done | bytes 131104 | tf_op jit(solution)/shard_map/ppermute | solution.py:21
  46.0 4.5 %shard_map.175 = (bf16[128,512]{1,0:T(8,128)(2,1)S(1)}, bf16[128,512]{1,0:T(8,128)(2,1)S(1)}, bf16[256,512]{1,0:T(8,128)(2,1)S(1)}, bf16[512,512]{1,0:T(8,128)(2...) custom-call(bf16[11,128,512]{2,1,0:T(8,128)(2,1)S(1)} %get-tuple-ele, ...), custom_call_target="tpu_custom_call" | custom-call | flops 1 | bytes 1 | tf_op jit(solution)/shard_map/pallas_call | solution.py:89
  50.4 1.3 shard_map.178
  51.8 2.3 collective-permute-done.10.refs_2_
  54.2 5.0 %collective-permute-start.11 = (bf16[4,96,512]{2,1,0:T(8,128)(2,1)S(1)}, bf16[4,96,512]{2,1,0:T(8,128)(2,1)S(1)}, u32[]{:S(2)}, u32[]{:S(2)}) collective-permute-start(bf16[4,96,512]{2,1,0:T(8,128)(2,1)S(1)} %get-tuple-element.135), channel_id=1, source_target_pairs={{0,2},{1,3},{2,0},{3,1},{4,6},{5,7},{6,4},{7,5},{8,10},{9,11},{10,... | collective-permute-start | bytes 1179656 | tf_op jit(solution)/shard_map/ppermute | solution.py:510
  59.2 0.4 collective-permute-start.9
  59.6 3.4 %collective-permute-start.7 = (bf16[128,512]{1,0:T(8,128)(2,1)S(1)}, bf16[128,512]{1,0:T(8,128)(2,1)S(1)}, u32[]{:S(2)}, u32[]{:S(2)}) collective-permute-start(bf16[128,512]{1,0:T(8,128)(2,1)S(1)} %get-tuple-element.118.refs_17_.refs_12_), channel_id=1, source_target_pairs={{4,0},{5,1},{6,2},{7,3},{8,4},{9,5},{10,6},{11,7},{12,8},{13,9},{1... | collective-permute-start | bytes 393224 | tf_op jit(solution)/shard_map/ppermute | solution.py:21
  63.0 2.1 shard_map.176
  65.1 3.9 %shard_map.177 = (bf16[320,512]{1,0:T(8,128)(2,1)S(1)}, f32[4,2,128,512]{3,2,1,0:T(8,128)S(1)}, bf16[4,2,128,512]{3,2,1,0:T(8,128)(2,1)S(1)}) custom-call(bf16[11,128,512]{2,1,0:T(8,128)(2,1)S(1)} %get-tuple-element.82.refs_0_, bf16[320,1408]{1,0:T(8,128)(2,1)S(1)} %get-tuple-element.92.refs_2_.refs_4_.refs_1_, s32[1]{0:T(128)} %bitcast.refs_0_.refs_2_, ...), custom_call_target="tpu_custom_call" | custom-call | flops 1 | bytes 1 | tf_op jit(solution)/shard_map/pallas_call | solution.py:89
  69.0 0.2 collective-permute-done.7.refs_1_.refs_10_
  69.1 5.7 %collective-permute-done.8.refs_2_.refs_11_ = bf16[128,512]{1,0:T(8,128)(2,1)S(1)} collective-permute-done((bf16[128,512]{1,0:T(8,128)(2,1)S(1)}, bf16[128,512]{1,0:T(8,128)(2,1)S(1)}, u32[]{:S(2)}, u32[]{:S(2)}) %collective-permute-start.8) | collective-permute-done | bytes 131104 | tf_op jit(solution)/shard_map/ppermute | solution.py:21
  74.8 2.8 %collective-permute-done.9.refs_3_.refs_12_ = bf16[256,512]{1,0:T(8,128)(2,1)S(1)} collective-permute-done((bf16[256,512]{1,0:T(8,128)(2,1)S(1)}, bf16[256,512]{1,0:T(8,128)(2,1)S(1)}, u32[]{:S(2)}, u32[]{:S(2)}) %collective-permute-start.9) | collective-permute-done | bytes 262176 | tf_op jit(solution)/shard_map/ppermute | solution.py:21
  77.7 0.6 copy-done.2
  78.3 2.0 collective-permute-done.12.refs_2_
  80.2 0.2 shard_map.182
  80.4 0.2 collective-permute-start.13
  80.6 2.7 collective-permute-start.14
  83.3 2.6 collective-permute-start.16
  85.9 3.5 %shard_map.183 = (bf16[11,128,512]{2,1,0:T(8,128)(2,1)}, bf16[11,128,512]{2,1,0:T(8,128)(2,1)}) custom-call(bf16[11,128,512]{2,1,0:T(8,128)(2,1)S(1)} %get-tuple-element.82.refs_0_, bf16[11,128,512]{2,1,0:T(8,128)(2,1)S(1)} %get-tuple-element.81.refs_0_.refs_1_, bf16[1536,512]{1,0:T(8,128)(2,1)S(1)} %get-tuple-element.85.refs_4_.refs_6_.refs_2_.refs_3_, ...), custom_call_target="tpu_custom_call" | custom-call | flops 1 | bytes 1 | tf_op jit(solution)/shard_map/pallas_call | solution.py:89
  89.5 2.0 collective-permute-done.15.refs_5_.refs_6_
  91.5 3.0 %collective-permute-done.13.refs_2_ = bf16[4,128,512]{2,1,0:T(8,128)(2,1)S(1)} collective-permute-done((bf16[4,128,512]{2,1,0:T(8,128)(2,1)S(1)}, bf16[4,128,512]{2,1,0:T(8,128)(2,1)S(1)}, u32[]{:S(2)}, u32[]{:S(2)}) %collective-permute-start.13) | collective-permute-done | bytes 524320 | tf_op jit(solution)/shard_map/ppermute | solution.py:510
  94.5 2.5 collective-permute-start.17
  97.1 2.6 collective-permute-start.19
  99.7 3.2 %collective-permute-done.17.refs_1_ = bf16[128,512]{1,0:T(8,128)(2,1)S(1)} collective-permute-done((bf16[128,512]{1,0:T(8,128)(2,1)S(1)}, bf16[128,512]{1,0:T(8,128)(2,1)S(1)}, u32[]{:S(2)}, u32[]{:S(2)}) %collective-permute-start.17) | collective-permute-done | bytes 131104 | tf_op jit(solution)/shard_map/ppermute | solution.py:510
  102.9 3.9 %collective-permute-done.18.refs_2_ = bf16[128,512]{1,0:T(8,128)(2,1)S(1)} collective-permute-done((bf16[128,512]{1,0:T(8,128)(2,1)S(1)}, bf16[128,512]{1,0:T(8,128)(2,1)S(1)}, u32[]{:S(2)}, u32[]{:S(2)}) %collective-permute-start.18) | collective-permute-done | bytes 131104 | tf_op jit(solution)/shard_map/ppermute | solution.py:510
  106.8 0.8 shard_map.185.refs_5_
  107.6 1.9 collective-permute-start.20
  109.6 2.4 collective-permute-start.22
  112.0 1.0 copy-done.1
  113.0 1.0 copy-done.12
  114.0 0.5 shard_map.186.refs_1_
  114.5 2.5 collective-permute-done.21.refs_7_
  117.0 0.3 collective-permute-done.22.refs_8_
  117.2 2.9 %collective-permute-done.23.refs_9_ = bf16[128,512]{1,0:T(8,128)(2,1)S(1)} collective-permute-done((bf16[128,512]{1,0:T(8,128)(2,1)S(1)}, bf16[128,512]{1,0:T(8,128)(2,1)S(1)}, u32[]{:S(2)}, u32[]{:S(2)}) %collective-permute-start.23) | collective-permute-done | bytes 131104 | tf_op jit(solution)/shard_map/ppermute | solution.py:21
  120.1 1.6 shard_map.187.refs_0_
  121.8 35.1 %all-gather.2.cloned.1.call-done.in_ref = bf16[3584,512]{1,0:T(8,128)(2,1)} async-done(((bf16[224,512]{1,0:T(8,128)(2,1)}), bf16[3584,512]{1,0:T(8,128)(2,1)}) %all-gather.2.cloned.1.call-update) | async-done | bytes 3670032 | tf_op jit(solution)/shard_map/all_gather | solution.py:550
  156.9 112.8 %shard_map.188 = (bf16[1536,512]{1,0:T(8,128)(2,1)}, bf16[512,512]{1,0:T(8,128)(2,1)}, bf16[1024,512]{1,0:T(8,128)(2,1)}, bf16[512,512]{1,0:T(8,128)(2,1)}) custom-call(bf16[3584,512]{1,0:T(8,128)(2,1)} %all-gather.2.cloned.1.call-done.in_ref, bf16[320,512]{1,0:T(8,128)(2,1)} %shard_map.187.refs_0_), custom_call_target="tpu_custom_call" | custom-call | flops 1 | bytes 1 | tf_op jit(solution)/shard_map/pallas_call | solution.py:556
  (49 shorter events, 0.5 us)
Async XLA Ops:
  7.2 149.7 %all-gather.2.cloned.1.call-start = ((), (), s32[]{:S(2)}) async-start(), calls=%async_computation.1 | async-start | bytes 3899392 | tf_op jit(solution)/shard_map/all_gather | solution.py:550
  24.9 5.5 %collective-permute-start.1 = (bf16[128,512]{1,0:T(8,128)(2,1)S(1)}, bf16[128,512]{1,0:T(8,128)(2,1)S(1)}, u32[]{:S(2)}, u32[]{:S(2)}) collective-permute-start(bf16[128,512]{1,0:T(8,128)(2,1)S(1)} %get-tuple-element.94), channel_id=1, source_target_pairs={{1,0},{2,1},{3,2},{4,3},{5,4},{6,5},{7,6},{8,7},{9,8},{10,9},{11,1... | collective-permute-start | bytes 393224 | tf_op jit(solution)/shard_map/ppermute | solution.py:21
  25.2 9.1 %collective-permute-start.2 = (bf16[128,512]{1,0:T(8,128)(2,1)S(1)}, bf16[128,512]{1,0:T(8,128)(2,1)S(1)}, u32[]{:S(2)}, u32[]{:S(2)}) collective-permute-start(bf16[128,512]{1,0:T(8,128)(2,1)S(1)} %get-tuple-element.95), channel_id=1, source_target_pairs={{14,0},{15,1},{0,2},{1,3},{2,4},{3,5},{4,6},{5,7},{6,8},{7,9},{8,1... | collective-permute-start | bytes 393224 | tf_op jit(solution)/shard_map/ppermute | solution.py:21
  26.4 19.6 %collective-permute-start.6 = (bf16[256,512]{1,0:T(8,128)(2,1)S(1)}, bf16[256,512]{1,0:T(8,128)(2,1)S(1)}, u32[]{:S(2)}, u32[]{:S(2)}) collective-permute-start(bf16[256,512]{1,0:T(8,128)(2,1)S(1)} %get-tuple-element.103), channel_id=1, source_target_pairs={{8,0},{9,1},{10,2},{11,3},{12,4},{13,5},{14,6},{15,7},{0,8},{1,9},... | collective-permute-start | bytes 786440 | tf_op jit(solution)/shard_map/ppermute | solution.py:21
  27.2 11.6 %collective-permute-start.3 = (bf16[128,512]{1,0:T(8,128)(2,1)S(1)}, bf16[128,512]{1,0:T(8,128)(2,1)S(1)}, u32[]{:S(2)}, u32[]{:S(2)}) collective-permute-start(bf16[128,512]{1,0:T(8,128)(2,1)S(1)} %get-tuple-element.96), channel_id=1, source_target_pairs={{2,0},{3,1},{4,2},{5,3},{6,4},{7,5},{8,6},{9,7},{10,8},{11,9},{12,... | collective-permute-start | bytes 393224 | tf_op jit(solution)/shard_map/ppermute | solution.py:21
  30.5 11.1 %collective-permute-start = (bf16[128,512]{1,0:T(8,128)(2,1)S(1)}, bf16[128,512]{1,0:T(8,128)(2,1)S(1)}, u32[]{:S(2)}, u32[]{:S(2)}) collective-permute-start(bf16[128,512]{1,0:T(8,128)(2,1)S(1)} %get-tuple-element.88.refs_7_), channel_id=1, source_target_pairs={{15,0},{0,1},{1,2},{2,3},{3,4},{4,5},{5,6},{6,7},{7,8},{8,9},{9,10... | collective-permute-start | bytes 393224 | tf_op jit(solution)/shard_map/ppermute | solution.py:21
  30.5 12.7 %collective-permute-start.4 = (bf16[128,512]{1,0:T(8,128)(2,1)S(1)}, bf16[128,512]{1,0:T(8,128)(2,1)S(1)}, u32[]{:S(2)}, u32[]{:S(2)}) collective-permute-start(bf16[128,512]{1,0:T(8,128)(2,1)S(1)} %get-tuple-element.101), channel_id=1, source_target_pairs={{12,0},{13,1},{14,2},{15,3},{0,4},{1,5},{2,6},{3,7},{4,8},{5,9},{6... | collective-permute-start | bytes 393224 | tf_op jit(solution)/shard_map/ppermute | solution.py:21
  34.3 11.6 %collective-permute-start.5 = (bf16[128,512]{1,0:T(8,128)(2,1)S(1)}, bf16[128,512]{1,0:T(8,128)(2,1)S(1)}, u32[]{:S(2)}, u32[]{:S(2)}) collective-permute-start(bf16[128,512]{1,0:T(8,128)(2,1)S(1)} %get-tuple-element.102), channel_id=1, source_target_pairs={{4,0},{5,1},{6,2},{7,3},{8,4},{9,5},{10,6},{11,7},{12,8},{13,9},{1... | collective-permute-start | bytes 393224 | tf_op jit(solution)/shard_map/ppermute | solution.py:21
  51.7 2.4 collective-permute-start.10
  54.2 23.4 %collective-permute-start.11 = (bf16[4,96,512]{2,1,0:T(8,128)(2,1)S(1)}, bf16[4,96,512]{2,1,0:T(8,128)(2,1)S(1)}, u32[]{:S(2)}, u32[]{:S(2)}) collective-permute-start(bf16[4,96,512]{2,1,0:T(8,128)(2,1)S(1)} %get-tuple-element.135), channel_id=1, source_target_pairs={{0,2},{1,3},{2,0},{3,1},{4,6},{5,7},{6,4},{7,5},{8,10},{9,11},{10,... | collective-permute-start | bytes 1179656 | tf_op jit(solution)/shard_map/ppermute | solution.py:510
  59.2 18.4 %collective-permute-start.9 = (bf16[256,512]{1,0:T(8,128)(2,1)S(1)}, bf16[256,512]{1,0:T(8,128)(2,1)S(1)}, u32[]{:S(2)}, u32[]{:S(2)}) collective-permute-start(bf16[256,512]{1,0:T(8,128)(2,1)S(1)} %get-tuple-element.120.refs_19_.refs_14_), channel_id=1, source_target_pairs={{8,0},{9,1},{10,2},{11,3},{12,4},{13,5},{14,6},{15,7},{0,8},{1,9},... | collective-permute-start | bytes 786440 | tf_op jit(solution)/shard_map/ppermute | solution.py:21
  59.6 9.5 %collective-permute-start.7 = (bf16[128,512]{1,0:T(8,128)(2,1)S(1)}, bf16[128,512]{1,0:T(8,128)(2,1)S(1)}, u32[]{:S(2)}, u32[]{:S(2)}) collective-permute-start(bf16[128,512]{1,0:T(8,128)(2,1)S(1)} %get-tuple-element.118.refs_17_.refs_12_), channel_id=1, source_target_pairs={{4,0},{5,1},{6,2},{7,3},{8,4},{9,5},{10,6},{11,7},{12,8},{13,9},{1... | collective-permute-start | bytes 393224 | tf_op jit(solution)/shard_map/ppermute | solution.py:21
  63.0 11.8 %collective-permute-start.8 = (bf16[128,512]{1,0:T(8,128)(2,1)S(1)}, bf16[128,512]{1,0:T(8,128)(2,1)S(1)}, u32[]{:S(2)}, u32[]{:S(2)}) collective-permute-start(bf16[128,512]{1,0:T(8,128)(2,1)S(1)} %get-tuple-element.119.refs_18_.refs_13_), channel_id=1, source_target_pairs={{12,0},{13,1},{14,2},{15,3},{0,4},{1,5},{2,6},{3,7},{4,8},{5,9},{6... | collective-permute-start | bytes 393224 | tf_op jit(solution)/shard_map/ppermute | solution.py:21
  65.1 20.9 %copy-start.4 = (bf16[128,512]{1,0:T(8,128)(2,1)}, bf16[128,512]{1,0:T(8,128)(2,1)S(1)}, u32[]{:S(2)}) copy-start(bf16[128,512]{1,0:T(8,128)(2,1)S(1)} %get-tuple-element.116.refs_15_.refs_10_) | copy-start | bytes 393220
  65.1 20.9 %copy-start.5 = (bf16[128,512]{1,0:T(8,128)(2,1)}, bf16[128,512]{1,0:T(8,128)(2,1)S(1)}, u32[]{:S(2)}) copy-start(bf16[128,512]{1,0:T(8,128)(2,1)S(1)} %get-tuple-element.115.refs_14_.refs_9_) | copy-start | bytes 393220
  65.1 20.9 %copy-start.6 = (bf16[128,512]{1,0:T(8,128)(2,1)}, bf16[128,512]{1,0:T(8,128)(2,1)S(1)}, u32[]{:S(2)}) copy-start(bf16[128,512]{1,0:T(8,128)(2,1)S(1)} %get-tuple-element.114.refs_13_.refs_8_) | copy-start | bytes 393220
  69.0 8.7 %copy-start.11 = (bf16[320,512]{1,0:T(8,128)(2,1)}, bf16[320,512]{1,0:T(8,128)(2,1)S(1)}, u32[]{:S(2)}) copy-start(bf16[320,512]{1,0:T(8,128)(2,1)S(1)} %get-tuple-element.140.refs_2_) | copy-start | bytes 983044
  69.1 8.6 %copy-start.7 = (bf16[128,512]{1,0:T(8,128)(2,1)}, bf16[128,512]{1,0:T(8,128)(2,1)S(1)}, u32[]{:S(2)}) copy-start(bf16[128,512]{1,0:T(8,128)(2,1)S(1)} %collective-permute-done.7.refs_1_.refs_10_) | copy-start | bytes 393220
  74.8 2.9 %copy-start.9 = (bf16[128,512]{1,0:T(8,128)(2,1)}, bf16[128,512]{1,0:T(8,128)(2,1)S(1)}, u32[]{:S(2)}) copy-start(bf16[128,512]{1,0:T(8,128)(2,1)S(1)} %collective-permute-done.8.refs_2_.refs_11_) | copy-start | bytes 393220
  77.6 0.7 copy-start.2
  77.6 2.7 collective-permute-start.12
  80.4 14.0 %collective-permute-start.13 = (bf16[4,128,512]{2,1,0:T(8,128)(2,1)S(1)}, bf16[4,128,512]{2,1,0:T(8,128)(2,1)S(1)}, u32[]{:S(2)}, u32[]{:S(2)}) collective-permute-start(bf16[4,128,512]{2,1,0:T(8,128)(2,1)S(1)} %get-tuple-element.141), channel_id=1, source_target_pairs={{0,2},{1,3},{2,0},{3,1},{4,6},{5,7},{6,4},{7,5},{8,10},{9,11},{10,... | collective-permute-start | bytes 1572872 | tf_op jit(solution)/shard_map/ppermute | solution.py:510
  80.6 8.8 %collective-permute-start.14 = (bf16[96,512]{1,0:T(8,128)(2,1)S(1)}, bf16[96,512]{1,0:T(8,128)(2,1)S(1)}, u32[]{:S(2)}, u32[]{:S(2)}) collective-permute-start(bf16[96,512]{1,0:T(8,128)(2,1)S(1)} %get-tuple-element.142), channel_id=1, source_target_pairs={{0,4},{1,5},{2,6},{3,7},{4,8},{5,9},{6,10},{7,11},{8,12},{9,13},{1... | collective-permute-start | bytes 294920 | tf_op jit(solution)/shard_map/ppermute | solution.py:510
  83.3 8.2 %collective-permute-start.15 = (bf16[96,512]{1,0:T(8,128)(2,1)S(1)}, bf16[96,512]{1,0:T(8,128)(2,1)S(1)}, u32[]{:S(2)}, u32[]{:S(2)}) collective-permute-start(bf16[96,512]{1,0:T(8,128)(2,1)S(1)} %get-tuple-element.143), channel_id=1, source_target_pairs={{0,8},{1,9},{2,10},{3,11},{4,12},{5,13},{6,14},{7,15},{8,0},{9,1},... | collective-permute-start | bytes 294920 | tf_op jit(solution)/shard_map/ppermute | solution.py:510
  83.3 8.2 %collective-permute-start.16 = (bf16[96,512]{1,0:T(8,128)(2,1)S(1)}, bf16[96,512]{1,0:T(8,128)(2,1)S(1)}, u32[]{:S(2)}, u32[]{:S(2)}) collective-permute-start(bf16[96,512]{1,0:T(8,128)(2,1)S(1)} %get-tuple-element.144), channel_id=1, source_target_pairs={{0,12},{1,13},{2,14},{3,15},{4,0},{5,1},{6,2},{7,3},{8,4},{9,5},{1... | collective-permute-start | bytes 294920 | tf_op jit(solution)/shard_map/ppermute | solution.py:510
  94.5 17.5 %copy-start = (bf16[1024,512]{1,0:T(8,128)(2,1)S(1)}, bf16[1024,512]{1,0:T(8,128)(2,1)}, u32[]{:S(2)}) copy-start(bf16[1024,512]{1,0:T(8,128)(2,1)} %refs_4_.1) | copy-start | bytes 3145732
  94.5 8.4 %collective-permute-start.17 = (bf16[128,512]{1,0:T(8,128)(2,1)S(1)}, bf16[128,512]{1,0:T(8,128)(2,1)S(1)}, u32[]{:S(2)}, u32[]{:S(2)}) collective-permute-start(bf16[128,512]{1,0:T(8,128)(2,1)S(1)} %get-tuple-element.146), channel_id=1, source_target_pairs={{0,4},{1,5},{2,6},{3,7},{4,8},{5,9},{6,10},{7,11},{8,12},{9,13},{1... | collective-permute-start | bytes 393224 | tf_op jit(solution)/shard_map/ppermute | solution.py:510
  97.1 9.8 %collective-permute-start.18 = (bf16[128,512]{1,0:T(8,128)(2,1)S(1)}, bf16[128,512]{1,0:T(8,128)(2,1)S(1)}, u32[]{:S(2)}, u32[]{:S(2)}) collective-permute-start(bf16[128,512]{1,0:T(8,128)(2,1)S(1)} %get-tuple-element.147), channel_id=1, source_target_pairs={{0,8},{1,9},{2,10},{3,11},{4,12},{5,13},{6,14},{7,15},{8,0},{9,1},... | collective-permute-start | bytes 393224 | tf_op jit(solution)/shard_map/ppermute | solution.py:510
  97.1 9.8 %collective-permute-start.19 = (bf16[128,512]{1,0:T(8,128)(2,1)S(1)}, bf16[128,512]{1,0:T(8,128)(2,1)S(1)}, u32[]{:S(2)}, u32[]{:S(2)}) collective-permute-start(bf16[128,512]{1,0:T(8,128)(2,1)S(1)} %get-tuple-element.148), channel_id=1, source_target_pairs={{0,12},{1,13},{2,14},{3,15},{4,0},{5,1},{6,2},{7,3},{8,4},{9,5},{1... | collective-permute-start | bytes 393224 | tf_op jit(solution)/shard_map/ppermute | solution.py:510
  107.6 6.9 %collective-permute-start.20 = (bf16[128,512]{1,0:T(8,128)(2,1)}, bf16[128,512]{1,0:T(8,128)(2,1)S(1)}, u32[]{:S(2)}, u32[]{:S(2)}) collective-permute-start(bf16[128,512]{1,0:T(8,128)(2,1)} %copy-done.6), channel_id=1, source_target_pairs={{1,0},{2,1},{3,2},{4,3},{5,4},{6,5},{7,6},{8,7},{9,8},{10,9},{11,1... | collective-permute-start | bytes 393224 | tf_op jit(solution)/shard_map/ppermute | solution.py:21
  109.6 7.4 %collective-permute-start.21 = (bf16[128,512]{1,0:T(8,128)(2,1)}, bf16[128,512]{1,0:T(8,128)(2,1)S(1)}, u32[]{:S(2)}, u32[]{:S(2)}) collective-permute-start(bf16[128,512]{1,0:T(8,128)(2,1)} %copy-done.5), channel_id=1, source_target_pairs={{15,0},{0,1},{1,2},{2,3},{3,4},{4,5},{5,6},{6,7},{7,8},{8,9},{9,10... | collective-permute-start | bytes 393224 | tf_op jit(solution)/shard_map/ppermute | solution.py:21
  109.6 7.7 %collective-permute-start.22 = (bf16[128,512]{1,0:T(8,128)(2,1)}, bf16[128,512]{1,0:T(8,128)(2,1)S(1)}, u32[]{:S(2)}, u32[]{:S(2)}) collective-permute-start(bf16[128,512]{1,0:T(8,128)(2,1)} %copy-done.4), channel_id=1, source_target_pairs={{2,0},{3,1},{4,2},{5,3},{6,4},{7,5},{8,6},{9,7},{10,8},{11,9},{12,... | collective-permute-start | bytes 393224 | tf_op jit(solution)/shard_map/ppermute | solution.py:21
  112.0 8.1 %collective-permute-start.23 = (bf16[128,512]{1,0:T(8,128)(2,1)S(1)}, bf16[128,512]{1,0:T(8,128)(2,1)S(1)}, u32[]{:S(2)}, u32[]{:S(2)}) collective-permute-start(bf16[128,512]{1,0:T(8,128)(2,1)S(1)} %get-tuple-element.117.refs_16_.refs_11_), channel_id=1, source_target_pairs={{14,0},{15,1},{0,2},{1,3},{2,4},{3,5},{4,6},{5,7},{6,8},{7,9},{8,1... | collective-permute-start | bytes 393224 | tf_op jit(solution)/shard_map/ppermute | solution.py:21
  112.0 1.0 copy-start.1
  113.0 1.0 copy-start.12
  114.0 6.2 %copy-start.3 = (bf16[256,512]{1,0:T(8,128)(2,1)S(1)}, bf16[256,512]{1,0:T(8,128)(2,1)}, u32[]{:S(2)}) copy-start(bf16[256,512]{1,0:T(8,128)(2,1)} %copy-done.2) | copy-start | bytes 786436
  114.0 6.2 %copy-start.8 = (bf16[128,512]{1,0:T(8,128)(2,1)S(1)}, bf16[128,512]{1,0:T(8,128)(2,1)}, u32[]{:S(2)}) copy-start(bf16[128,512]{1,0:T(8,128)(2,1)} %copy-done.7) | copy-start | bytes 393220
  114.0 6.2 %copy-start.10 = (bf16[128,512]{1,0:T(8,128)(2,1)S(1)}, bf16[128,512]{1,0:T(8,128)(2,1)}, u32[]{:S(2)}) copy-start(bf16[128,512]{1,0:T(8,128)(2,1)} %copy-done.9) | copy-start | bytes 393220
Sparse Core Ops, SparseCore 0:
  107.7 49.0 all-gather.1

commit v11 on v10

--- a/solution.py
+++ b/solution.py
@@ -533,13 +533,14 @@
     return outs[0], [in_group(out, "band", stride, members, j + 1) for j, out in enumerate(outs[1:])]
 
 
-def last_sum(*chunks):
-    rows, width = sum(keep.shape[0] for keep, _ in chunks), chunks[0][0].shape[1]
+def last_sum(keep, arrived, after):
     (piece,) = call(
-        functools.partial(last_kernel, [1 + len(arrived) for _, arrived in chunks]),
-        [((rows, width), bf16)],
+        functools.partial(last_kernel, [1 + len(arrived)]),
+        [(keep.shape, bf16)],
         [],
-        *[array for keep, arrived in chunks for array in [keep, *arrived]],
+        keep,
+        *arrived,
+        after=after,
     )
     return piece
 
@@ -558,9 +559,9 @@
         out_shape=[pltpu.HBM((bands * size, width), bf16) for size in sizes],
         in_specs=[pl.BlockSpec(memory_space=pltpu.HBM)]
         + [pl.BlockSpec(memory_space=pl.ANY)] * len(after),
-        out_specs=[pl.BlockSpec(memory_space=pltpu.HBM)] * len(sizes),
+        out_specs=[pl.BlockSpec(memory_space=pltpu.VMEM)] * len(sizes),
         scratch_shapes=[pltpu.SemaphoreType.DMA((count,))],
-        compiler_params=pltpu.CompilerParams(vmem_limit_bytes=1024 * 1024),
+        compiler_params=pltpu.CompilerParams(vmem_limit_bytes=8 * 1024 * 1024),
         cost_estimate=pl.CostEstimate(flops=1, bytes_accessed=1, transcendentals=0),
     )(in_hbm(whole), *after)
 
@@ -864,12 +865,12 @@
         keep_node, came_node = add_stage(me, keep_node, came_node, *along_z, [sent_edge])
         keep_edge, came_edge = add_stage(me, keep_edge, came_edge, *along_y, [keep_node])
         edge_new, grad_edges = edge_outputs([keep_edge])
-        keep_edge, came_edge = add_stage(me, keep_edge, came_edge, *along_z, [in_hbm(edge_new)] + came_node)
-        piece = last_sum((keep_edge, came_edge), (keep_node, came_node))
-        grad_nodes = node_output([piece])
-        grad_e1, grad_e2, grad_n1, grad_n2 = gathered_from_all(
-            piece, edge_sizes + node_sizes, [in_hbm(grad_nodes)]
-        )
+        piece_node = last_sum(keep_node, came_node, [in_hbm(edge_new)] + came_edge)
+        keep_edge, came_edge = add_stage(me, keep_edge, came_edge, *along_z, [piece_node])
+        piece_edge = last_sum(keep_edge, came_edge, [])
+        grad_nodes = node_output([piece_edge])
+        grad_n1, grad_n2 = gathered_from_all(piece_node, node_sizes, [in_hbm(grad_nodes)])
+        grad_e1, grad_e2 = gathered_from_all(piece_edge, edge_sizes, [in_hbm(grad_n2)])
     else:
         whole = lax.psum(node_weights[0], "band").astype(bf16)
         grad_n1, grad_n2 = whole[: 2 * width], whole[2 * width :]

time: 277 us -> 191 us (0.69)
  Pallas kernels: 142 us -> 34.7 us
  waiting for transfers between devices: 75 us -> 90.4 us
  local copies, waits for them, and re-layouts: 2.56 us -> 6.29 us
    pallas_call x1 -> x2, Pallas kernels: 113 us -> 6 us  [gathered_from_all(): pl.pallas_call(kernel, out_shape=[pltpu.HBM((bands * size, width), bf16)...]
    all_gather x1 -> x2, waiting for transfers between devices: 35.1 us -> 51.7 us  [gathered_from_all(): whole = lax.all_gather(piece, 'band', axis=0, tiled=True)]
    unnamed x26 -> x40, local copies, waits for them, and re-layouts: 2.56 us -> 6.29 us
    pallas_call x16 -> x17, Pallas kernels: 25.5 us -> 25.5 us  [call(): pl.pallas_call(kernel, out_shape=[(pltpu.HBM if i in last else pltpu.VMEM...]
  transfers between devices with their start and end apart: 25 -> 26, of which waited for: 16 -> 15; matrix products, arithmetic and copies ran while one was open for 0% -> 0% of each run, Pallas kernels for 6% -> 11%
where the time goes in v11:
time: 191 us; the launch traced here: 190 us
  waiting for transfers between devices  90.4 us (47%)
  Pallas kernels  34.7 us (18%)
  starting transfers between devices  30.5 us (16%)
  between operations  14.4 us (8%)
  blocking collectives  13.7 us (7%)
  local copies, waits for them, and re-layouts  6.29 us (3%)
    all_gather x2, waiting for transfers between devices, gathered_from_all(): whole = lax.all_gather(piece, 'band', axis=0, tiled=True)  51.7 us
    pallas_call x17, Pallas kernels, call(): pl.pallas_call(kernel, out_shape=[(pltpu.HBM if i in last else pltpu.VMEM...  25.5 us
    ppermute x14, waiting for transfers between devices, passed_along(): return lax.ppermute(block, axis, route)  21.2 us
    ppermute x10, waiting for transfers between devices, in_group(): return lax.ppermute(block, axis, route)  17.5 us
    ppermute x10, starting transfers between devices, in_group(): return lax.ppermute(block, axis, route)  15.7 us
    ppermute x14, starting transfers between devices, passed_along(): return lax.ppermute(block, axis, route)  14.7 us
    all_to_all x1, blocking collectives, local(): ids = lax.all_to_all(ids, 'band', 0, 0, tiled=True)  13.7 us
    unnamed x40, local copies, waits for them, and re-layouts  6.29 us
  transfers between devices with their start and end apart: 26, of which 15 were waited for; matrix products, arithmetic and copies ran while one was open for 0% of the time, Pallas kernels for 11%

profile of v11, /device:TPU:0, one launch (start us, length us, event | category | flops | bytes accessed | tf_op | source)
XLA Modules:
  0.0 190.0 jit_solution(9137094467743735565)
XLA Ops:
  7.2 3.2 %shard_map.170 = (bf16[320,512]{1,0:T(8,128)(2,1)S(1)}, s32[11,1,128]{2,1,0:T(1,128)S(1)}, s32[11,1,128]{2,1,0:T(1,128)S(1)}, bf16[11,128,512]{2,1,0:T(8,128)(2,...) custom-call(s32[1]{0:T(128)} %bitcast.refs_0_.refs_2_, ...), custom_call_target="tpu_custom_call" | custom-call | flops 1 | bytes 1 | tf_op jit(solution)/shard_map/pallas_call | solution.py:120
  10.5 13.7 %all_to_all.5.refs_2_.refs_4_ = s32[16,1,256]{2,1,0:T(1,128)S(1)} all-to-all(s32[16,1,256]{2,1,0:T(1,128)S(1)} %shard_map.171), channel_id=1, replica_groups=mesh['groups'=2,'band'=16] {'band'}, dimensions={0} | all-to-all | bytes 32768 | tf_op jit(solution)/shard_map/all_to_all | solution.py:654
  24.2 0.8 shard_map.172
  25.2 1.2 collective-permute-start.2
  26.4 0.8 collective-permute-start.6
  27.2 3.3 %collective-permute-start.3 = (bf16[128,512]{1,0:T(8,128)(2,1)S(1)}, bf16[128,512]{1,0:T(8,128)(2,1)S(1)}, u32[]{:S(2)}, u32[]{:S(2)}) collective-permute-start(bf16[128,512]{1,0:T(8,128)(2,1)S(1)} %get-tuple-element.96), channel_id=1, source_target_pairs={{2,0},{3,1},{4,2},{5,3},{6,4},{7,5},{8,6},{9,7},{10,8},{11,9},{12,... | collective-permute-start | bytes 393224 | tf_op jit(solution)/shard_map/ppermute | solution.py:21
  30.5 3.9 %collective-permute-done.2.refs_8_.refs_7_ = bf16[128,512]{1,0:T(8,128)(2,1)S(1)} collective-permute-done((bf16[128,512]{1,0:T(8,128)(2,1)S(1)}, bf16[128,512]{1,0:T(8,128)(2,1)S(1)}, u32[]{:S(2)}, u32[]{:S(2)}) %collective-permute-start.2) | collective-permute-done | bytes 131104 | tf_op jit(solution)/shard_map/ppermute | solution.py:21
  34.4 4.5 %shard_map.173 = (bf16[1408,320]{1,0:T(8,128)(2,1)S(1)}, bf16[320,1408]{1,0:T(8,128)(2,1)S(1)}, f32[1408,128]{1,0:T(8,128)S(1)}, f32[1024,512]{1,0:T(8,128)S(1)}...) custom-call(bf16[11,128,512]{2,1,0:T(8,128)(2,1)S(1)} %get-tuple-ele, ...), custom_call_target="tpu_custom_call" | custom-call | flops 1 | bytes 1 | tf_op jit(solution)/shard_map/pallas_call | solution.py:89
  38.9 2.7 %collective-permute-done.refs_6_.refs_5_ = bf16[128,512]{1,0:T(8,128)(2,1)S(1)} collective-permute-done((bf16[128,512]{1,0:T(8,128)(2,1)S(1)}, bf16[128,512]{1,0:T(8,128)(2,1)S(1)}, u32[]{:S(2)}, u32[]{:S(2)}) %collective-permute-start) | collective-permute-done | bytes 131104 | tf_op jit(solution)/shard_map/ppermute | solution.py:21
  41.6 1.6 shard_map.174
  43.2 2.8 %collective-permute-done.5.refs_13_.refs_10_ = bf16[128,512]{1,0:T(8,128)(2,1)S(1)} collective-permute-done((bf16[128,512]{1,0:T(8,128)(2,1)S(1)}, bf16[128,512]{1,0:T(8,128)(2,1)S(1)}, u32[]{:S(2)}, u32[]{:S(2)}) %collective-permute-start.5) | collective-permute-done | bytes 131104 | tf_op jit(solution)/shard_map/ppermute | solution.py:21
  46.0 4.5 %shard_map.175 = (bf16[128,512]{1,0:T(8,128)(2,1)S(1)}, bf16[128,512]{1,0:T(8,128)(2,1)S(1)}, bf16[256,512]{1,0:T(8,128)(2,1)S(1)}, bf16[512,512]{1,0:T(8,128)(2...) custom-call(bf16[11,128,512]{2,1,0:T(8,128)(2,1)S(1)} %get-tuple-ele, ...), custom_call_target="tpu_custom_call" | custom-call | flops 1 | bytes 1 | tf_op jit(solution)/shard_map/pallas_call | solution.py:89
  50.4 1.3 shard_map.178
  51.8 2.3 %collective-permute-done.10.refs_2_ = bf16[4,2,96,512]{3,2,1,0:T(8,128)(2,1)S(1)} collective-permute-done((bf16[4,2,96,512]{3,2,1,0:T(8,128)(2,1)S(1)}, bf16[4,2,96,512]{3,2,1,0:T(8,128)(2,1)S(1)}, u32[]{:S(2)}, u32[]{:S(2)}) %collective-permute-start.10) | collective-permute-done | bytes 786464 | tf_op jit(solution)/shard_map/ppermute | solution.py:510
  54.2 5.0 %collective-permute-start.11 = (bf16[4,96,512]{2,1,0:T(8,128)(2,1)S(1)}, bf16[4,96,512]{2,1,0:T(8,128)(2,1)S(1)}, u32[]{:S(2)}, u32[]{:S(2)}) collective-permute-start(bf16[4,96,512]{2,1,0:T(8,128)(2,1)S(1)} %get-tuple-element.135), channel_id=1, source_target_pairs={{0,2},{1,3},{2,0},{3,1},{4,6},{5,7},{6,4},{7,5},{8,10},{9,11},{10,... | collective-permute-start | bytes 1179656 | tf_op jit(solution)/shard_map/ppermute | solution.py:510
  59.2 0.4 collective-permute-start.9
  59.6 3.4 %collective-permute-start.7 = (bf16[128,512]{1,0:T(8,128)(2,1)S(1)}, bf16[128,512]{1,0:T(8,128)(2,1)S(1)}, u32[]{:S(2)}, u32[]{:S(2)}) collective-permute-start(bf16[128,512]{1,0:T(8,128)(2,1)S(1)} %get-tuple-element.118.refs_17_.refs_12_), channel_id=1, source_target_pairs={{4,0},{5,1},{6,2},{7,3},{8,4},{9,5},{10,6},{11,7},{12,8},{13,9},{1... | collective-permute-start | bytes 393224 | tf_op jit(solution)/shard_map/ppermute | solution.py:21
  63.0 2.1 %shard_map.176 = (bf16[896,512]{1,0:T(8,128)(2,1)S(1)}, bf16[384,512]{1,0:T(8,128)(2,1)S(1)}, bf16[128,512]{1,0:T(8,128)(2,1)S(1)}, bf16[128,512]{1,0:T(8,128)(2...) custom-call(bf16[11,128,512]{2,1,0:T(8,128)(2,1)S(1)} %get-tuple-element.81.refs_0_.refs_1_, ...), custom_call_target="tpu_custom_call" | custom-call | flops 1 | bytes 1 | tf_op jit(solution)/shard_map/pallas_call | solution.py:89
  65.1 3.9 %shard_map.177 = (bf16[320,512]{1,0:T(8,128)(2,1)S(1)}, f32[4,2,128,512]{3,2,1,0:T(8,128)S(1)}, bf16[4,2,128,512]{3,2,1,0:T(8,128)(2,1)S(1)}) custom-call(bf16[11,128,512]{2,1,0:T(8,128)(2,1)S(1)} %get-tuple-element.82.refs_0_, bf16[320,1408]{1,0:T(8,128)(2,1)S(1)} %get-tuple-element.92.refs_2_.refs_4_.refs_1_, s32[1]{0:T(128)} %bitcast.refs_0_.refs_2_, ...), custom_call_target="tpu_custom_call" | custom-call | flops 1 | bytes 1 | tf_op jit(solution)/shard_map/pallas_call | solution.py:89
  69.2 5.6 %collective-permute-done.8.refs_2_.refs_11_ = bf16[128,512]{1,0:T(8,128)(2,1)S(1)} collective-permute-done((bf16[128,512]{1,0:T(8,128)(2,1)S(1)}, bf16[128,512]{1,0:T(8,128)(2,1)S(1)}, u32[]{:S(2)}, u32[]{:S(2)}) %collective-permute-start.8) | collective-permute-done | bytes 131104 | tf_op jit(solution)/shard_map/ppermute | solution.py:21
  74.8 2.8 %collective-permute-done.9.refs_3_.refs_12_ = bf16[256,512]{1,0:T(8,128)(2,1)S(1)} collective-permute-done((bf16[256,512]{1,0:T(8,128)(2,1)S(1)}, bf16[256,512]{1,0:T(8,128)(2,1)S(1)}, u32[]{:S(2)}, u32[]{:S(2)}) %collective-permute-start.9) | collective-permute-done | bytes 262176 | tf_op jit(solution)/shard_map/ppermute | solution.py:21
  77.7 0.6 copy-done.4
  78.3 2.0 %collective-permute-done.12.refs_2_ = bf16[4,2,128,512]{3,2,1,0:T(8,128)(2,1)S(1)} collective-permute-done((bf16[4,2,128,512]{3,2,1,0:T(8,128)(2,1)S(1)}, bf16[4,2,128,512]{3,2,1,0:T(8,128)(2,1)S(1)}, u32[]{:S(2)}, u32[]{:S(2)}) %collective-permute-start.12) | collective-permute-done | bytes 1048608 | tf_op jit(solution)/shard_map/ppermute | solution.py:510
  80.7 2.7 %collective-permute-start.14 = (bf16[96,512]{1,0:T(8,128)(2,1)S(1)}, bf16[96,512]{1,0:T(8,128)(2,1)S(1)}, u32[]{:S(2)}, u32[]{:S(2)}) collective-permute-start(bf16[96,512]{1,0:T(8,128)(2,1)S(1)} %get-tuple-element.142), channel_id=1, source_target_pairs={{0,4},{1,5},{2,6},{3,7},{4,8},{5,9},{6,10},{7,11},{8,12},{9,13},{1... | collective-permute-start | bytes 294920 | tf_op jit(solution)/shard_map/ppermute | solution.py:510
  83.3 2.6 %collective-permute-start.16 = (bf16[96,512]{1,0:T(8,128)(2,1)S(1)}, bf16[96,512]{1,0:T(8,128)(2,1)S(1)}, u32[]{:S(2)}, u32[]{:S(2)}) collective-permute-start(bf16[96,512]{1,0:T(8,128)(2,1)S(1)} %get-tuple-element.144), channel_id=1, source_target_pairs={{0,12},{1,13},{2,14},{3,15},{4,0},{5,1},{6,2},{7,3},{8,4},{9,5},{1... | collective-permute-start | bytes 294920 | tf_op jit(solution)/shard_map/ppermute | solution.py:510
  86.0 3.5 %shard_map.183 = (bf16[11,128,512]{2,1,0:T(8,128)(2,1)}, bf16[11,128,512]{2,1,0:T(8,128)(2,1)}) custom-call(bf16[11,128,512]{2,1,0:T(8,128)(2,1)S(1)} %get-tuple-element.82.refs_0_, bf16[11,128,512]{2,1,0:T(8,128)(2,1)S(1)} %get-tuple-element.81.refs_0_.refs_1_, bf16[1536,512]{1,0:T(8,128)(2,1)S(1)} %get-tuple-element.85.refs_4_.refs_6_.refs_2_.refs_3_, ...), custom_call_target="tpu_custom_call" | custom-call | flops 1 | bytes 1 | tf_op jit(solution)/shard_map/pallas_call | solution.py:89
  89.5 2.0 %collective-permute-done.15.refs_2_ = bf16[96,512]{1,0:T(8,128)(2,1)S(1)} collective-permute-done((bf16[96,512]{1,0:T(8,128)(2,1)S(1)}, bf16[96,512]{1,0:T(8,128)(2,1)S(1)}, u32[]{:S(2)}, u32[]{:S(2)}) %collective-permute-start.15) | collective-permute-done | bytes 98336 | tf_op jit(solution)/shard_map/ppermute | solution.py:510
  91.5 3.0 %collective-permute-done.13.refs_5_.refs_2_ = bf16[4,128,512]{2,1,0:T(8,128)(2,1)S(1)} collective-permute-done((bf16[4,128,512]{2,1,0:T(8,128)(2,1)S(1)}, bf16[4,128,512]{2,1,0:T(8,128)(2,1)S(1)}, u32[]{:S(2)}, u32[]{:S(2)}) %collective-permute-start.13) | collective-permute-done | bytes 524320 | tf_op jit(solution)/shard_map/ppermute | solution.py:510
  94.5 0.6 copy-done.6
  95.2 0.9 copy-done.7
  96.2 2.5 %collective-permute-start.17 = (bf16[128,512]{1,0:T(8,128)(2,1)S(1)}, bf16[128,512]{1,0:T(8,128)(2,1)S(1)}, u32[]{:S(2)}, u32[]{:S(2)}) collective-permute-start(bf16[128,512]{1,0:T(8,128)(2,1)S(1)} %get-tuple-element.146), channel_id=1, source_target_pairs={{0,4},{1,5},{2,6},{3,7},{4,8},{5,9},{6,10},{7,11},{8,12},{9,13},{1... | collective-permute-start | bytes 393224 | tf_op jit(solution)/shard_map/ppermute | solution.py:510
  98.8 2.6 %collective-permute-start.19 = (bf16[128,512]{1,0:T(8,128)(2,1)S(1)}, bf16[128,512]{1,0:T(8,128)(2,1)S(1)}, u32[]{:S(2)}, u32[]{:S(2)}) collective-permute-start(bf16[128,512]{1,0:T(8,128)(2,1)S(1)} %get-tuple-element.148), channel_id=1, source_target_pairs={{0,12},{1,13},{2,14},{3,15},{4,0},{5,1},{6,2},{7,3},{8,4},{9,5},{1... | collective-permute-start | bytes 393224 | tf_op jit(solution)/shard_map/ppermute | solution.py:510
  101.4 3.2 %collective-permute-done.17.refs_1_ = bf16[128,512]{1,0:T(8,128)(2,1)S(1)} collective-permute-done((bf16[128,512]{1,0:T(8,128)(2,1)S(1)}, bf16[128,512]{1,0:T(8,128)(2,1)S(1)}, u32[]{:S(2)}, u32[]{:S(2)}) %collective-permute-start.17) | collective-permute-done | bytes 131104 | tf_op jit(solution)/shard_map/ppermute | solution.py:510
  104.6 5.0 %collective-permute-done.18.refs_2_ = bf16[128,512]{1,0:T(8,128)(2,1)S(1)} collective-permute-done((bf16[128,512]{1,0:T(8,128)(2,1)S(1)}, bf16[128,512]{1,0:T(8,128)(2,1)S(1)}, u32[]{:S(2)}, u32[]{:S(2)}) %collective-permute-start.18) | collective-permute-done | bytes 131104 | tf_op jit(solution)/shard_map/ppermute | solution.py:510
  109.6 0.7 shard_map.186.refs_5_
  110.4 0.5 collective-permute-start.21
  110.9 4.8 %collective-permute-start.22 = (bf16[128,512]{1,0:T(8,128)(2,1)}, bf16[128,512]{1,0:T(8,128)(2,1)S(1)}, u32[]{:S(2)}, u32[]{:S(2)}) collective-permute-start(bf16[128,512]{1,0:T(8,128)(2,1)} %copy-done.9), channel_id=1, source_target_pairs={{2,0},{3,1},{4,2},{5,3},{6,4},{7,5},{8,6},{9,7},{10,8},{11,9},{12,... | collective-permute-start | bytes 393224 | tf_op jit(solution)/shard_map/ppermute | solution.py:21
  115.7 1.2 copy-done
  117.0 1.0 copy-done.2
  117.9 1.0 copy-done.3
  118.9 1.0 copy-done.17
  119.9 0.5 shard_map.187.refs_1_
  120.5 3.3 %collective-permute-done.23.refs_9_ = bf16[128,512]{1,0:T(8,128)(2,1)S(1)} collective-permute-done((bf16[128,512]{1,0:T(8,128)(2,1)}, bf16[128,512]{1,0:T(8,128)(2,1)S(1)}, u32[]{:S(2)}, u32[]{:S(2)}) %collective-permute-start.23) | collective-permute-done | bytes 131104 | tf_op jit(solution)/shard_map/ppermute | solution.py:21
  123.8 1.7 shard_map.188.refs_0_
  125.5 11.5 %all-gather.5.cloned.1.call-done.in_ref = bf16[1536,512]{1,0:T(8,128)(2,1)} async-done(((bf16[96,512]{1,0:T(8,128)(2,1)}), bf16[1536,512]{1,0:T(8,128)(2,1)}) %all-gather.5.cloned.1.call-update) | async-done | bytes 1572880 | tf_op jit(solution)/shard_map/all_gather | solution.py:551
  137.0 2.8 %shard_map.189 = (bf16[1024,512]{1,0:T(8,128)(2,1)}, bf16[512,512]{1,0:T(8,128)(2,1)}) custom-call(bf16[1536,512]{1,0:T(8,128)(2,1)} %all-gather.5.cloned.1.call-done.in_ref, bf16[320,512]{1,0:T(8,128)(2,1)} %shard_map.188.refs_0_), custom_call_target="tpu_custom_call" | custom-call | flops 1 | bytes 1 | tf_op jit(solution)/shard_map/pallas_call | solution.py:557
  139.8 40.2 %all-gather.3.cloned.1.call-done.in_ref = bf16[2048,512]{1,0:T(8,128)(2,1)} async-done(((bf16[128,512]{1,0:T(8,128)(2,1)}), bf16[2048,512]{1,0:T(8,128)(2,1)}) %all-gather.3.cloned.1.call-update) | async-done | bytes 2097168 | tf_op jit(solution)/shard_map/all_gather | solution.py:551
  180.0 3.2 %shard_map.190 = (bf16[1536,512]{1,0:T(8,128)(2,1)}, bf16[512,512]{1,0:T(8,128)(2,1)}) custom-call(bf16[2048,512]{1,0:T(8,128)(2,1)} %all-gather.3.cloned.1.call-done.in_ref, bf16[512,512]{1,0:T(8,128)(2,1)} %get-tuple-element.80.refs_0_), custom_call_target="tpu_custom_call" | custom-call | flops 1 | bytes 1 | tf_op jit(solution)/shard_map/pallas_call | solution.py:557
  (68 shorter events, 1.6 us)
Async XLA Ops:
  7.2 129.8 %all-gather.5.cloned.1.call-start = ((), (), s32[]{:S(2)}) async-start(), calls=%async_computation.2 | async-start | bytes 1671168 | tf_op jit(solution)/shard_map/all_gather | solution.py:551
  10.5 28.4 %copy-start.18 = (s32[11,1,128]{2,1,0:T(1,128)}, s32[11,1,128]{2,1,0:T(1,128)S(1)}, u32[]{:S(2)}) copy-start(s32[11,1,128]{2,1,0:T(1,128)S(1)} %get-tuple-element.84.refs_1_.refs_2_.refs_3_) | copy-start | bytes 16900
  25.0 5.5 %collective-permute-start.1 = (bf16[128,512]{1,0:T(8,128)(2,1)S(1)}, bf16[128,512]{1,0:T(8,128)(2,1)S(1)}, u32[]{:S(2)}, u32[]{:S(2)}) collective-permute-start(bf16[128,512]{1,0:T(8,128)(2,1)S(1)} %get-tuple-element.94), channel_id=1, source_target_pairs={{1,0},{2,1},{3,2},{4,3},{5,4},{6,5},{7,6},{8,7},{9,8},{10,9},{11,1... | collective-permute-start | bytes 393224 | tf_op jit(solution)/shard_map/ppermute | solution.py:21
  25.2 9.1 %collective-permute-start.2 = (bf16[128,512]{1,0:T(8,128)(2,1)S(1)}, bf16[128,512]{1,0:T(8,128)(2,1)S(1)}, u32[]{:S(2)}, u32[]{:S(2)}) collective-permute-start(bf16[128,512]{1,0:T(8,128)(2,1)S(1)} %get-tuple-element.95), channel_id=1, source_target_pairs={{14,0},{15,1},{0,2},{1,3},{2,4},{3,5},{4,6},{5,7},{6,8},{7,9},{8,1... | collective-permute-start | bytes 393224 | tf_op jit(solution)/shard_map/ppermute | solution.py:21
  26.4 19.6 %collective-permute-start.6 = (bf16[256,512]{1,0:T(8,128)(2,1)S(1)}, bf16[256,512]{1,0:T(8,128)(2,1)S(1)}, u32[]{:S(2)}, u32[]{:S(2)}) collective-permute-start(bf16[256,512]{1,0:T(8,128)(2,1)S(1)} %get-tuple-element.103), channel_id=1, source_target_pairs={{8,0},{9,1},{10,2},{11,3},{12,4},{13,5},{14,6},{15,7},{0,8},{1,9},... | collective-permute-start | bytes 786440 | tf_op jit(solution)/shard_map/ppermute | solution.py:21
  27.2 11.7 %collective-permute-start.3 = (bf16[128,512]{1,0:T(8,128)(2,1)S(1)}, bf16[128,512]{1,0:T(8,128)(2,1)S(1)}, u32[]{:S(2)}, u32[]{:S(2)}) collective-permute-start(bf16[128,512]{1,0:T(8,128)(2,1)S(1)} %get-tuple-element.96), channel_id=1, source_target_pairs={{2,0},{3,1},{4,2},{5,3},{6,4},{7,5},{8,6},{9,7},{10,8},{11,9},{12,... | collective-permute-start | bytes 393224 | tf_op jit(solution)/shard_map/ppermute | solution.py:21
  30.5 11.1 %collective-permute-start = (bf16[128,512]{1,0:T(8,128)(2,1)S(1)}, bf16[128,512]{1,0:T(8,128)(2,1)S(1)}, u32[]{:S(2)}, u32[]{:S(2)}) collective-permute-start(bf16[128,512]{1,0:T(8,128)(2,1)S(1)} %get-tuple-element.88.refs_7_), channel_id=1, source_target_pairs={{15,0},{0,1},{1,2},{2,3},{3,4},{4,5},{5,6},{6,7},{7,8},{8,9},{9,10... | collective-permute-start | bytes 393224 | tf_op jit(solution)/shard_map/ppermute | solution.py:21
  30.5 12.7 %collective-permute-start.4 = (bf16[128,512]{1,0:T(8,128)(2,1)S(1)}, bf16[128,512]{1,0:T(8,128)(2,1)S(1)}, u32[]{:S(2)}, u32[]{:S(2)}) collective-permute-start(bf16[128,512]{1,0:T(8,128)(2,1)S(1)} %get-tuple-element.101), channel_id=1, source_target_pairs={{12,0},{13,1},{14,2},{15,3},{0,4},{1,5},{2,6},{3,7},{4,8},{5,9},{6... | collective-permute-start | bytes 393224 | tf_op jit(solution)/shard_map/ppermute | solution.py:21
  34.4 11.6 %collective-permute-start.5 = (bf16[128,512]{1,0:T(8,128)(2,1)S(1)}, bf16[128,512]{1,0:T(8,128)(2,1)S(1)}, u32[]{:S(2)}, u32[]{:S(2)}) collective-permute-start(bf16[128,512]{1,0:T(8,128)(2,1)S(1)} %get-tuple-element.102), channel_id=1, source_target_pairs={{4,0},{5,1},{6,2},{7,3},{8,4},{9,5},{10,6},{11,7},{12,8},{13,9},{1... | collective-permute-start | bytes 393224 | tf_op jit(solution)/shard_map/ppermute | solution.py:21
  50.4 3.8 %copy-start.1 = (bf16[320,512]{1,0:T(8,128)(2,1)}, bf16[320,512]{1,0:T(8,128)(2,1)S(1)}, u32[]{:S(2)}) copy-start(bf16[320,512]{1,0:T(8,128)(2,1)S(1)} %get-tuple-element.130.refs_3_.refs_1_) | copy-start | bytes 983044
  51.7 2.4 %collective-permute-start.10 = (bf16[4,2,96,512]{3,2,1,0:T(8,128)(2,1)S(1)}, bf16[4,2,96,512]{3,2,1,0:T(8,128)(2,1)S(1)}, u32[]{:S(2)}, u32[]{:S(2)}) collective-permute-start(bf16[4,2,96,512]{3,2,1,0:T(8,128)(2,1)S(1)} %get-tuple-element.134), channel_id=1, source_target_pairs={{0,1},{1,0},{2,3},{3,2},{4,5},{5,4},{6,7},{7,6},{8,9},{9,8},{10,11... | collective-permute-start | bytes 2359304 | tf_op jit(solution)/shard_map/ppermute | solution.py:510
  54.2 23.4 %collective-permute-start.11 = (bf16[4,96,512]{2,1,0:T(8,128)(2,1)S(1)}, bf16[4,96,512]{2,1,0:T(8,128)(2,1)S(1)}, u32[]{:S(2)}, u32[]{:S(2)}) collective-permute-start(bf16[4,96,512]{2,1,0:T(8,128)(2,1)S(1)} %get-tuple-element.135), channel_id=1, source_target_pairs={{0,2},{1,3},{2,0},{3,1},{4,6},{5,7},{6,4},{7,5},{8,10},{9,11},{10,... | collective-permute-start | bytes 1179656 | tf_op jit(solution)/shard_map/ppermute | solution.py:510
  59.2 18.4 %collective-permute-start.9 = (bf16[256,512]{1,0:T(8,128)(2,1)S(1)}, bf16[256,512]{1,0:T(8,128)(2,1)S(1)}, u32[]{:S(2)}, u32[]{:S(2)}) collective-permute-start(bf16[256,512]{1,0:T(8,128)(2,1)S(1)} %get-tuple-element.120.refs_19_.refs_14_), channel_id=1, source_target_pairs={{8,0},{9,1},{10,2},{11,3},{12,4},{13,5},{14,6},{15,7},{0,8},{1,9},... | collective-permute-start | bytes 786440 | tf_op jit(solution)/shard_map/ppermute | solution.py:21
  59.6 9.5 %collective-permute-start.7 = (bf16[128,512]{1,0:T(8,128)(2,1)S(1)}, bf16[128,512]{1,0:T(8,128)(2,1)S(1)}, u32[]{:S(2)}, u32[]{:S(2)}) collective-permute-start(bf16[128,512]{1,0:T(8,128)(2,1)S(1)} %get-tuple-element.118.refs_17_.refs_12_), channel_id=1, source_target_pairs={{4,0},{5,1},{6,2},{7,3},{8,4},{9,5},{10,6},{11,7},{12,8},{13,9},{1... | collective-permute-start | bytes 393224 | tf_op jit(solution)/shard_map/ppermute | solution.py:21
  63.0 11.8 %collective-permute-start.8 = (bf16[128,512]{1,0:T(8,128)(2,1)S(1)}, bf16[128,512]{1,0:T(8,128)(2,1)S(1)}, u32[]{:S(2)}, u32[]{:S(2)}) collective-permute-start(bf16[128,512]{1,0:T(8,128)(2,1)S(1)} %get-tuple-element.119.refs_18_.refs_13_), channel_id=1, source_target_pairs={{12,0},{13,1},{14,2},{15,3},{0,4},{1,5},{2,6},{3,7},{4,8},{5,9},{6... | collective-permute-start | bytes 393224 | tf_op jit(solution)/shard_map/ppermute | solution.py:21
  65.1 20.9 %copy-start.8 = (bf16[128,512]{1,0:T(8,128)(2,1)}, bf16[128,512]{1,0:T(8,128)(2,1)S(1)}, u32[]{:S(2)}) copy-start(bf16[128,512]{1,0:T(8,128)(2,1)S(1)} %get-tuple-element.117.refs_16_.refs_11_) | copy-start | bytes 393220
  65.1 20.9 %copy-start.9 = (bf16[128,512]{1,0:T(8,128)(2,1)}, bf16[128,512]{1,0:T(8,128)(2,1)S(1)}, u32[]{:S(2)}) copy-start(bf16[128,512]{1,0:T(8,128)(2,1)S(1)} %get-tuple-element.116.refs_15_.refs_10_) | copy-start | bytes 393220
  65.1 20.8 %copy-start.10 = (bf16[128,512]{1,0:T(8,128)(2,1)}, bf16[128,512]{1,0:T(8,128)(2,1)S(1)}, u32[]{:S(2)}) copy-start(bf16[128,512]{1,0:T(8,128)(2,1)S(1)} %get-tuple-element.115.refs_14_.refs_9_) | copy-start | bytes 393220
  65.1 20.8 %copy-start.11 = (bf16[128,512]{1,0:T(8,128)(2,1)}, bf16[128,512]{1,0:T(8,128)(2,1)S(1)}, u32[]{:S(2)}) copy-start(bf16[128,512]{1,0:T(8,128)(2,1)S(1)} %get-tuple-element.114.refs_13_.refs_8_) | copy-start | bytes 393220
  69.0 8.7 %copy-start.16 = (bf16[320,512]{1,0:T(8,128)(2,1)}, bf16[320,512]{1,0:T(8,128)(2,1)S(1)}, u32[]{:S(2)}) copy-start(bf16[320,512]{1,0:T(8,128)(2,1)S(1)} %get-tuple-element.140.refs_2_) | copy-start | bytes 983044
  69.2 8.5 %copy-start.12 = (bf16[128,512]{1,0:T(8,128)(2,1)}, bf16[128,512]{1,0:T(8,128)(2,1)S(1)}, u32[]{:S(2)}) copy-start(bf16[128,512]{1,0:T(8,128)(2,1)S(1)} %collective-permute-done.7.refs_1_.refs_10_) | copy-start | bytes 393220
  74.8 2.9 %copy-start.14 = (bf16[128,512]{1,0:T(8,128)(2,1)}, bf16[128,512]{1,0:T(8,128)(2,1)S(1)}, u32[]{:S(2)}) copy-start(bf16[128,512]{1,0:T(8,128)(2,1)S(1)} %collective-permute-done.8.refs_2_.refs_11_) | copy-start | bytes 393220
  77.6 0.7 copy-start.4
  77.6 2.7 %collective-permute-start.12 = (bf16[4,2,128,512]{3,2,1,0:T(8,128)(2,1)S(1)}, bf16[4,2,128,512]{3,2,1,0:T(8,128)(2,1)S(1)}, u32[]{:S(2)}, u32[]{:S(2)}) collective-permute-start(bf16[4,2,128,512]{3,2,1,0:T(8,128)(2,1)S(1)} %shard_map.180.refs_3_), channel_id=1, source_target_pairs={{0,1},{1,0},{2,3},{3,2},{4,5},{5,4},{6,7},{7,6},{8,9},{9,8},{10,11... | collective-permute-start | bytes 3145736 | tf_op jit(solution)/shard_map/ppermute | solution.py:510
  80.4 14.0 %collective-permute-start.13 = (bf16[4,128,512]{2,1,0:T(8,128)(2,1)S(1)}, bf16[4,128,512]{2,1,0:T(8,128)(2,1)S(1)}, u32[]{:S(2)}, u32[]{:S(2)}) collective-permute-start(bf16[4,128,512]{2,1,0:T(8,128)(2,1)S(1)} %get-tuple-element.141), channel_id=1, source_target_pairs={{0,2},{1,3},{2,0},{3,1},{4,6},{5,7},{6,4},{7,5},{8,10},{9,11},{10,... | collective-permute-start | bytes 1572872 | tf_op jit(solution)/shard_map/ppermute | solution.py:510
  80.7 8.8 %collective-permute-start.14 = (bf16[96,512]{1,0:T(8,128)(2,1)S(1)}, bf16[96,512]{1,0:T(8,128)(2,1)S(1)}, u32[]{:S(2)}, u32[]{:S(2)}) collective-permute-start(bf16[96,512]{1,0:T(8,128)(2,1)S(1)} %get-tuple-element.142), channel_id=1, source_target_pairs={{0,4},{1,5},{2,6},{3,7},{4,8},{5,9},{6,10},{7,11},{8,12},{9,13},{1... | collective-permute-start | bytes 294920 | tf_op jit(solution)/shard_map/ppermute | solution.py:510
  83.3 8.2 %collective-permute-start.15 = (bf16[96,512]{1,0:T(8,128)(2,1)S(1)}, bf16[96,512]{1,0:T(8,128)(2,1)S(1)}, u32[]{:S(2)}, u32[]{:S(2)}) collective-permute-start(bf16[96,512]{1,0:T(8,128)(2,1)S(1)} %get-tuple-element.143), channel_id=1, source_target_pairs={{0,8},{1,9},{2,10},{3,11},{4,12},{5,13},{6,14},{7,15},{8,0},{9,1},... | collective-permute-start | bytes 294920 | tf_op jit(solution)/shard_map/ppermute | solution.py:510
  83.3 8.2 %collective-permute-start.16 = (bf16[96,512]{1,0:T(8,128)(2,1)S(1)}, bf16[96,512]{1,0:T(8,128)(2,1)S(1)}, u32[]{:S(2)}, u32[]{:S(2)}) collective-permute-start(bf16[96,512]{1,0:T(8,128)(2,1)S(1)} %get-tuple-element.144), channel_id=1, source_target_pairs={{0,12},{1,13},{2,14},{3,15},{4,0},{5,1},{6,2},{7,3},{8,4},{9,5},{1... | collective-permute-start | bytes 294920 | tf_op jit(solution)/shard_map/ppermute | solution.py:510
  94.5 0.6 copy-start.6
  95.2 84.8 %all-gather.3.cloned.1.call-start = ((), (), s32[]{:S(2)}) async-start(), calls=%async_computation.1 | async-start | bytes 2228224 | tf_op jit(solution)/shard_map/all_gather | solution.py:551
  95.2 0.9 copy-start.7
  96.2 8.4 %collective-permute-start.17 = (bf16[128,512]{1,0:T(8,128)(2,1)S(1)}, bf16[128,512]{1,0:T(8,128)(2,1)S(1)}, u32[]{:S(2)}, u32[]{:S(2)}) collective-permute-start(bf16[128,512]{1,0:T(8,128)(2,1)S(1)} %get-tuple-element.146), channel_id=1, source_target_pairs={{0,4},{1,5},{2,6},{3,7},{4,8},{5,9},{6,10},{7,11},{8,12},{9,13},{1... | collective-permute-start | bytes 393224 | tf_op jit(solution)/shard_map/ppermute | solution.py:510
  98.8 10.8 %collective-permute-start.18 = (bf16[128,512]{1,0:T(8,128)(2,1)S(1)}, bf16[128,512]{1,0:T(8,128)(2,1)S(1)}, u32[]{:S(2)}, u32[]{:S(2)}) collective-permute-start(bf16[128,512]{1,0:T(8,128)(2,1)S(1)} %get-tuple-element.147), channel_id=1, source_target_pairs={{0,8},{1,9},{2,10},{3,11},{4,12},{5,13},{6,14},{7,15},{8,0},{9,1},... | collective-permute-start | bytes 393224 | tf_op jit(solution)/shard_map/ppermute | solution.py:510
  98.8 10.8 %collective-permute-start.19 = (bf16[128,512]{1,0:T(8,128)(2,1)S(1)}, bf16[128,512]{1,0:T(8,128)(2,1)S(1)}, u32[]{:S(2)}, u32[]{:S(2)}) collective-permute-start(bf16[128,512]{1,0:T(8,128)(2,1)S(1)} %get-tuple-element.148), channel_id=1, source_target_pairs={{0,12},{1,13},{2,14},{3,15},{4,0},{5,1},{6,2},{7,3},{8,4},{9,5},{1... | collective-permute-start | bytes 393224 | tf_op jit(solution)/shard_map/ppermute | solution.py:510
  110.3 10.1 %collective-permute-start.20 = (bf16[128,512]{1,0:T(8,128)(2,1)}, bf16[128,512]{1,0:T(8,128)(2,1)S(1)}, u32[]{:S(2)}, u32[]{:S(2)}) collective-permute-start(bf16[128,512]{1,0:T(8,128)(2,1)} %copy-done.11), channel_id=1, source_target_pairs={{1,0},{2,1},{3,2},{4,3},{5,4},{6,5},{7,6},{8,7},{9,8},{10,9},{11,1... | collective-permute-start | bytes 393224 | tf_op jit(solution)/shard_map/ppermute | solution.py:21
  110.4 10.1 %collective-permute-start.21 = (bf16[128,512]{1,0:T(8,128)(2,1)}, bf16[128,512]{1,0:T(8,128)(2,1)S(1)}, u32[]{:S(2)}, u32[]{:S(2)}) collective-permute-start(bf16[128,512]{1,0:T(8,128)(2,1)} %copy-done.10), channel_id=1, source_target_pairs={{15,0},{0,1},{1,2},{2,3},{3,4},{4,5},{5,6},{6,7},{7,8},{8,9},{9,10... | collective-permute-start | bytes 393224 | tf_op jit(solution)/shard_map/ppermute | solution.py:21
  110.9 9.6 %collective-permute-start.22 = (bf16[128,512]{1,0:T(8,128)(2,1)}, bf16[128,512]{1,0:T(8,128)(2,1)S(1)}, u32[]{:S(2)}, u32[]{:S(2)}) collective-permute-start(bf16[128,512]{1,0:T(8,128)(2,1)} %copy-done.9), channel_id=1, source_target_pairs={{2,0},{3,1},{4,2},{5,3},{6,4},{7,5},{8,6},{9,7},{10,8},{11,9},{12,... | collective-permute-start | bytes 393224 | tf_op jit(solution)/shard_map/ppermute | solution.py:21
  115.7 8.0 %collective-permute-start.23 = (bf16[128,512]{1,0:T(8,128)(2,1)}, bf16[128,512]{1,0:T(8,128)(2,1)S(1)}, u32[]{:S(2)}, u32[]{:S(2)}) collective-permute-start(bf16[128,512]{1,0:T(8,128)(2,1)} %copy-done.8), channel_id=1, source_target_pairs={{14,0},{15,1},{0,2},{1,3},{2,4},{3,5},{4,6},{5,7},{6,8},{7,9},{8,1... | collective-permute-start | bytes 393224 | tf_op jit(solution)/shard_map/ppermute | solution.py:21
  115.7 1.2 copy-start
  117.0 1.0 copy-start.2
  117.9 1.0 copy-start.3
  118.9 1.0 copy-start.17
  119.9 3.9 %copy-start.5 = (bf16[256,512]{1,0:T(8,128)(2,1)S(1)}, bf16[256,512]{1,0:T(8,128)(2,1)}, u32[]{:S(2)}) copy-start(bf16[256,512]{1,0:T(8,128)(2,1)} %copy-done.4) | copy-start | bytes 786436
  119.9 3.9 %copy-start.13 = (bf16[128,512]{1,0:T(8,128)(2,1)S(1)}, bf16[128,512]{1,0:T(8,128)(2,1)}, u32[]{:S(2)}) copy-start(bf16[128,512]{1,0:T(8,128)(2,1)} %copy-done.12) | copy-start | bytes 393220
  119.9 3.9 %copy-start.15 = (bf16[128,512]{1,0:T(8,128)(2,1)S(1)}, bf16[128,512]{1,0:T(8,128)(2,1)}, u32[]{:S(2)}) copy-start(bf16[128,512]{1,0:T(8,128)(2,1)} %copy-done.14) | copy-start | bytes 393220
  119.9 3.9 %copy-start.19 = (s32[11,1,128]{2,1,0:T(1,128)S(1)}, s32[11,1,128]{2,1,0:T(1,128)}, u32[]{:S(2)}) copy-start(s32[11,1,128]{2,1,0:T(1,128)} %copy-done.18) | copy-start | bytes 16900
Sparse Core Ops, SparseCore 0:
  95.3 41.6 all-gather.4
  139.7 40.2 all-gather.2

commit v12 on v9

--- a/solution.py
+++ b/solution.py
@@ -492,15 +492,7 @@
     return lax.ppermute(block, axis, route)
 
 
-def split_of(bands):
-    chips = bands // 2
-    first = 1
-    while first * first * 4 <= chips:
-        first *= 2
-    return first, chips // first
-
-
-def add_stage(me, keep, arrived, stride, members, kind, after):
+def add_stage(me, keep, arrived, stride, after, members=2, kind=f32):
     count, rows, width = keep.shape
     shape = (count, rows // members, width)
     outs = call(
@@ -529,9 +521,9 @@
     )(pltpu.with_memory_space_constraint(array, pltpu.VMEM), *after)
 
 
-def gather_stage(me, piece, stride, members, after):
+def gather_stage(me, piece, came, stride, after):
     count, rows, width = piece.shape
-    pieces = [piece] + [in_group(piece, "band", stride, members, j) for j in range(1, members)]
+    members, pieces = 2, [piece, came]
     (mine,) = call(
         functools.partial(gather_kernel, (stride, members)),
         [((count, rows * members, width), bf16)],
@@ -837,31 +829,37 @@
             after=after,
         )
 
-    first, second = split_of(bands)
+    first = 2
     node_blocks, node_shapes = ((0, 0), (0, 1), (1, 0)), [(2 * width, width), (width, width)]
     edge_blocks = ((0, 0), (0, 1), (0, 2), (1, 0))
     edge_shapes = [(3 * width, width), (width, width)]
-    if width // 2 % (16 * first * second) == 0:
-        along_y, along_z = (2, first), (2 * first, second)
+    if bands == 16 and width % 512 == 0:
+        def over(block, stride):
+            return in_group(block, "band", stride, 2, 1)
+
         keep_node, sent_node = node_weights([])
-        came_node = [in_group(sent_node, "band", 1, 2, 1)]
-        keep_node, came_node = add_stage(me, keep_node, came_node, *along_y, f32, [])
+        keep_node, came_node = add_stage(me, keep_node, [over(sent_node, 1)], 2, [])
         sent_edge = held_until(sent_edge, back_far + came_node)
-        came_edge = [in_group(sent_edge, "band", 1, 2, 1)]
-        keep_node, came_node = add_stage(me, keep_node, came_node, *along_z, f32, [sent_edge])
-        keep_edge, came_edge = add_stage(me, keep_edge, came_edge, *along_y, f32, [keep_node])
+        came_edge = [over(sent_edge, 1)]
+        keep_node, came_node = add_stage(me, keep_node, came_node, 4, [sent_edge])
+        keep_edge, came_edge = add_stage(me, keep_edge, came_edge, 2, [keep_node])
         edge_new, grad_edges = edge_outputs([keep_edge])
-        piece_node, _ = add_stage(me, keep_node, came_node, 1, 1, bf16, [in_hbm(edge_new)])
-        keep_edge, came_edge = add_stage(me, keep_edge, came_edge, *along_z, f32, [piece_node])
-        mine_node = gather_stage(me, piece_node, *along_z, [keep_edge])
-        piece_edge, _ = add_stage(me, keep_edge, came_edge, 1, 1, bf16, [mine_node])
+        keep_node, came_node = add_stage(me, keep_node, came_node, 8, [in_hbm(edge_new)])
+        piece_node, _ = add_stage(me, keep_node, came_node, 1, [], 1, bf16)
+        keep_edge, came_edge = add_stage(me, keep_edge, came_edge, 4, [piece_node])
+        piece_node = gather_stage(me, piece_node, over(piece_node, 8), 8, [keep_edge])
+        keep_edge, came_edge = add_stage(me, keep_edge, came_edge, 8, [piece_node])
+        piece_node = gather_stage(me, piece_node, over(piece_node, 4), 4, [keep_edge])
+        piece_edge, _ = add_stage(me, keep_edge, came_edge, 1, [piece_node], 1, bf16)
+        some, rest = back_near[: len(back_near) // 2], back_near[len(back_near) // 2 :]
+        piece_edge = gather_stage(me, piece_edge, over(piece_edge, 8), 8, some)
         grad_n1, grad_n2 = join_stage(
-            me, mine_node, first, node_blocks, node_shapes, [piece_edge], []
+            me, piece_node, first, node_blocks, node_shapes, [], [piece_edge]
         )
-        mine_edge = gather_stage(me, piece_edge, *along_z, [in_hbm(grad_n2)])
-        grad_nodes = node_output([mine_edge])
+        piece_edge = gather_stage(me, piece_edge, over(piece_edge, 4), 4, rest + [in_hbm(grad_n2)])
+        grad_nodes = node_output([piece_edge])
         grad_e1, grad_e2 = join_stage(
-            me, mine_edge, first, edge_blocks, edge_shapes, [in_hbm(grad_nodes)], []
+            me, piece_edge, first, edge_blocks, edge_shapes, [in_hbm(grad_nodes)], []
         )
     else:
         whole = reduce_whole(*node_weights([]))

time: 155 us -> 153 us (0.987)
  starting transfers between devices: 53.3 us -> 27.5 us
  waiting for transfers between devices: 56.4 us -> 79.8 us
    ppermute x22 -> x18, starting transfers between devices: 41.4 us -> 15 us  [in_group(): return lax.ppermute(block, axis, route)]
    ppermute x22 -> x18, waiting for transfers between devices: 36.8 us -> 53.7 us  [in_group(): return lax.ppermute(block, axis, route)]
    ppermute x14, waiting for transfers between devices: 19.6 us -> 26.1 us  [passed_along(): return lax.ppermute(block, axis, route)]
    pallas_call x21 -> x25, Pallas kernels: 27.7 us -> 27.8 us  [call(): pl.pallas_call(kernel, out_shape=[(pltpu.HBM if i in last else pltpu.VMEM...]
  transfers between devices with their start and end apart: 36 -> 32, of which waited for: 17 -> 19; matrix products, arithmetic and copies ran while one was open for 0% -> 0% of each run, Pallas kernels for 12% -> 13%
where the time goes in v12:
time: 153 us
  waiting for transfers between devices  79.8 us (52%)
  Pallas kernels  31.1 us (20%)
  starting transfers between devices  27.5 us (18%)
  blocking collectives  13.7 us (9%)
    ppermute x18, waiting for transfers between devices, in_group(): return lax.ppermute(block, axis, route)  53.7 us
    pallas_call x25, Pallas kernels, call(): pl.pallas_call(kernel, out_shape=[(pltpu.HBM if i in last else pltpu.VMEM...  27.8 us
    ppermute x14, waiting for transfers between devices, passed_along(): return lax.ppermute(block, axis, route)  26.1 us
    ppermute x18, starting transfers between devices, in_group(): return lax.ppermute(block, axis, route)  15 us
    all_to_all x1, blocking collectives, local(): ids = lax.all_to_all(ids, 'band', 0, 0, tiled=True)  13.7 us
    ppermute x14, starting transfers between devices, passed_along(): return lax.ppermute(block, axis, route)  12.5 us
    pallas_call x1, Pallas kernels, loaded(): pl.pallas_call(functools.partial(load_kernel, count), out_shape=[pltpu.VM...  3.24 us
  transfers between devices with their start and end apart: 32, of which 19 were waited for; matrix products, arithmetic and copies ran while one was open for 0% of the time, Pallas kernels for 13%

profile of v12, /device:TPU:0, one launch (start us, length us, event | category | flops | bytes accessed | tf_op | source)
XLA Modules:
  0.0 152.9 jit_solution(16323454672289580730)
XLA Ops:
  0.6 3.2 %shard_map.170 = (bf16[320,512]{1,0:T(8,128)(2,1)S(1)}, s32[11,1,128]{2,1,0:T(1,128)S(1)}, s32[11,1,128]{2,1,0:T(1,128)S(1)}, bf16[11,128,512]{2,1,0:T(8,128)(2,...) custom-call(s32[1]{0:T(128)} %bitcast.refs_0_.refs_2_, ...), custom_call_target="tpu_custom_call" | custom-call | flops 1 | bytes 1 | tf_op jit(solution)/shard_map/pallas_call | solution.py:120
  3.9 13.7 %all_to_all.5.refs_2_.refs_4_ = s32[16,1,256]{2,1,0:T(1,128)S(1)} all-to-all(s32[16,1,256]{2,1,0:T(1,128)S(1)} %shard_map.171), channel_id=1, replica_groups=mesh['groups'=2,'band'=16] {'band'}, dimensions={0} | all-to-all | bytes 32768 | tf_op jit(solution)/shard_map/all_to_all | solution.py:638
  17.6 0.8 shard_map.172
  18.4 0.3 collective-permute-start.1
  18.6 1.2 collective-permute-start.2
  19.8 0.8 collective-permute-start.6
  20.6 3.3 %collective-permute-start.3 = (bf16[128,512]{1,0:T(8,128)(2,1)S(1)}, bf16[128,512]{1,0:T(8,128)(2,1)S(1)}, u32[]{:S(2)}, u32[]{:S(2)}) collective-permute-start(bf16[128,512]{1,0:T(8,128)(2,1)S(1)} %get-tuple-element.96), channel_id=1, source_target_pairs={{2,0},{3,1},{4,2},{5,3},{6,4},{7,5},{8,6},{9,7},{10,8},{11,9},{12,... | collective-permute-start | bytes 393224 | tf_op jit(solution)/shard_map/ppermute | solution.py:21
  23.9 3.8 %collective-permute-done.2.refs_8_.refs_7_ = bf16[128,512]{1,0:T(8,128)(2,1)S(1)} collective-permute-done((bf16[128,512]{1,0:T(8,128)(2,1)S(1)}, bf16[128,512]{1,0:T(8,128)(2,1)S(1)}, u32[]{:S(2)}, u32[]{:S(2)}) %collective-permute-start.2) | collective-permute-done | bytes 131104 | tf_op jit(solution)/shard_map/ppermute | solution.py:21
  27.8 4.5 %shard_map.173 = (bf16[1408,320]{1,0:T(8,128)(2,1)S(1)}, bf16[320,1408]{1,0:T(8,128)(2,1)S(1)}, f32[1408,128]{1,0:T(8,128)S(1)}, f32[1024,512]{1,0:T(8,128)S(1)}...) custom-call(bf16[11,128,512]{2,1,0:T(8,128)(2,1)S(1)} %get-tuple-ele, ...), custom_call_target="tpu_custom_call" | custom-call | flops 1 | bytes 1 | tf_op jit(solution)/shard_map/pallas_call | solution.py:89
  32.3 2.7 %collective-permute-done.refs_6_.refs_5_ = bf16[128,512]{1,0:T(8,128)(2,1)S(1)} collective-permute-done((bf16[128,512]{1,0:T(8,128)(2,1)S(1)}, bf16[128,512]{1,0:T(8,128)(2,1)S(1)}, u32[]{:S(2)}, u32[]{:S(2)}) %collective-permute-start) | collective-permute-done | bytes 131104 | tf_op jit(solution)/shard_map/ppermute | solution.py:21
  35.0 1.6 %shard_map.174 = (bf16[512,512]{1,0:T(8,128)(2,1)S(1)}, f32[512,512]{1,0:T(8,128)S(1)}, f32[512,512]{1,0:T(8,128)S(1)}, f32[512,128]{1,0:T(8,128)S(1)}, f32[320,512]{1,0:T(8,128)S(1)}) custom-call(f32[1024,512]{1,0:T(8,128)S(1)} %get-tuple-element.89.refs_0_.refs_1_, f32[1408,128]{1,0:T(8,128)S(1)} %get-tuple-element.90.refs_1_.refs_2_.refs_3_, ...), custom_call_target="tpu_custom_call" | custom-call | flops 1 | bytes 1 | tf_op jit(solution)/shard_map/pallas_call | solution.py:89
  36.6 2.8 %collective-permute-done.5.refs_13_.refs_10_ = bf16[128,512]{1,0:T(8,128)(2,1)S(1)} collective-permute-done((bf16[128,512]{1,0:T(8,128)(2,1)S(1)}, bf16[128,512]{1,0:T(8,128)(2,1)S(1)}, u32[]{:S(2)}, u32[]{:S(2)}) %collective-permute-start.5) | collective-permute-done | bytes 131104 | tf_op jit(solution)/shard_map/ppermute | solution.py:21
  39.4 4.5 %shard_map.175 = (bf16[128,512]{1,0:T(8,128)(2,1)S(1)}, bf16[128,512]{1,0:T(8,128)(2,1)S(1)}, bf16[256,512]{1,0:T(8,128)(2,1)S(1)}, bf16[512,512]{1,0:T(8,128)(2...) custom-call(bf16[11,128,512]{2,1,0:T(8,128)(2,1)S(1)} %get-tuple-ele, ...), custom_call_target="tpu_custom_call" | custom-call | flops 1 | bytes 1 | tf_op jit(solution)/shard_map/pallas_call | solution.py:89
  43.8 1.3 shard_map.178
  45.2 2.3 %collective-permute-done.10.refs_2_ = bf16[3,256,512]{2,1,0:T(8,128)(2,1)S(1)} collective-permute-done((bf16[3,256,512]{2,1,0:T(8,128)(2,1)S(1)}, bf16[3,256,512]{2,1,0:T(8,128)(2,1)S(1)}, u32[]{:S(2)}, u32[]{:S(2)}) %collective-permute-start.10) | collective-permute-done | bytes 786464 | tf_op jit(solution)/shard_map/ppermute | solution.py:492
  47.7 5.0 %collective-permute-start.11 = (bf16[3,128,512]{2,1,0:T(8,128)(2,1)S(1)}, bf16[3,128,512]{2,1,0:T(8,128)(2,1)S(1)}, u32[]{:S(2)}, u32[]{:S(2)}) collective-permute-start(bf16[3,128,512]{2,1,0:T(8,128)(2,1)S(1)} %get-tuple-element.135), channel_id=1, source_target_pairs={{0,2},{1,3},{2,0},{3,1},{4,6},{5,7},{6,4},{7,5},{8,10},{9,11},{10,... | collective-permute-start | bytes 1179656 | tf_op jit(solution)/shard_map/ppermute | solution.py:492
  52.7 0.4 collective-permute-start.9
  53.1 3.4 %collective-permute-start.7 = (bf16[128,512]{1,0:T(8,128)(2,1)S(1)}, bf16[128,512]{1,0:T(8,128)(2,1)S(1)}, u32[]{:S(2)}, u32[]{:S(2)}) collective-permute-start(bf16[128,512]{1,0:T(8,128)(2,1)S(1)} %get-tuple-element.118.refs_17_.refs_12_), channel_id=1, source_target_pairs={{4,0},{5,1},{6,2},{7,3},{8,4},{9,5},{10,6},{11,7},{12,8},{13,9},{1... | collective-permute-start | bytes 393224 | tf_op jit(solution)/shard_map/ppermute | solution.py:21
  56.5 2.1 %shard_map.176 = (bf16[896,512]{1,0:T(8,128)(2,1)S(1)}, bf16[384,512]{1,0:T(8,128)(2,1)S(1)}, bf16[128,512]{1,0:T(8,128)(2,1)S(1)}, bf16[128,512]{1,0:T(8,128)(2...) custom-call(bf16[11,128,512]{2,1,0:T(8,128)(2,1)S(1)} %get-tuple-element.81.refs_0_.refs_1_, ...), custom_call_target="tpu_custom_call" | custom-call | flops 1 | bytes 1 | tf_op jit(solution)/shard_map/pallas_call | solution.py:89
  58.6 3.9 %shard_map.177 = (f32[4,256,512]{2,1,0:T(8,128)S(1)}, bf16[4,256,512]{2,1,0:T(8,128)(2,1)S(1)}, bf16[320,512]{1,0:T(8,128)(2,1)S(1)}) custom-call(bf16[11,128,512]{2,1,0:T(8,128)(2,1)S(1)} %get-tuple-element.82.refs_0_, bf16[320,1408]{1,0:T(8,128)(2,1)S(1)} %get-tuple-element.92.refs_2_.refs_4_.refs_1_, s32[1]{0:T(128)} %bitcast.refs_0_.refs_2_, ...), custom_call_target="tpu_custom_call" | custom-call | flops 1 | bytes 1 | tf_op jit(solution)/shard_map/pallas_call | solution.py:89
  62.6 5.7 %collective-permute-done.8.refs_2_.refs_11_ = bf16[128,512]{1,0:T(8,128)(2,1)S(1)} collective-permute-done((bf16[128,512]{1,0:T(8,128)(2,1)S(1)}, bf16[128,512]{1,0:T(8,128)(2,1)S(1)}, u32[]{:S(2)}, u32[]{:S(2)}) %collective-permute-start.8) | collective-permute-done | bytes 131104 | tf_op jit(solution)/shard_map/ppermute | solution.py:21
  68.3 2.8 %collective-permute-done.9.refs_3_.refs_12_ = bf16[256,512]{1,0:T(8,128)(2,1)S(1)} collective-permute-done((bf16[256,512]{1,0:T(8,128)(2,1)S(1)}, bf16[256,512]{1,0:T(8,128)(2,1)S(1)}, u32[]{:S(2)}, u32[]{:S(2)}) %collective-permute-start.9) | collective-permute-done | bytes 262176 | tf_op jit(solution)/shard_map/ppermute | solution.py:21
  71.1 2.6 %collective-permute-done.12.refs_2_ = bf16[4,256,512]{2,1,0:T(8,128)(2,1)S(1)} collective-permute-done((bf16[4,256,512]{2,1,0:T(8,128)(2,1)S(1)}, bf16[4,256,512]{2,1,0:T(8,128)(2,1)S(1)}, u32[]{:S(2)}, u32[]{:S(2)}) %collective-permute-start.12) | collective-permute-done | bytes 1048608 | tf_op jit(solution)/shard_map/ppermute | solution.py:492
  74.2 2.7 %collective-permute-start.14 = (bf16[3,64,512]{2,1,0:T(8,128)(2,1)S(1)}, bf16[3,64,512]{2,1,0:T(8,128)(2,1)S(1)}, u32[]{:S(2)}, u32[]{:S(2)}) collective-permute-start(bf16[3,64,512]{2,1,0:T(8,128)(2,1)S(1)} %get-tuple-element.142), channel_id=1, source_target_pairs={{0,4},{1,5},{2,6},{3,7},{4,0},{5,1},{6,2},{7,3},{8,12},{9,13},{10,... | collective-permute-start | bytes 589832 | tf_op jit(solution)/shard_map/ppermute | solution.py:492
  76.8 3.5 %shard_map.183 = (bf16[11,128,512]{2,1,0:T(8,128)(2,1)}, bf16[11,128,512]{2,1,0:T(8,128)(2,1)}) custom-call(bf16[11,128,512]{2,1,0:T(8,128)(2,1)S(1)} %get-tuple-element.82.refs_0_, bf16[11,128,512]{2,1,0:T(8,128)(2,1)S(1)} %get-tuple-element.81.refs_0_.refs_1_, bf16[1536,512]{1,0:T(8,128)(2,1)S(1)} %get-tuple-element.85.refs_4_.refs_6_.refs_2_.refs_3_, ...), custom_call_target="tpu_custom_call" | custom-call | flops 1 | bytes 1 | tf_op jit(solution)/shard_map/pallas_call | solution.py:89
  80.4 1.4 collective-permute-done.14.refs_2_
  81.8 1.5 collective-permute-start.15
  83.3 5.6 %collective-permute-done.15.refs_2_ = bf16[3,32,512]{2,1,0:T(8,128)(2,1)S(1)} collective-permute-done((bf16[3,32,512]{2,1,0:T(8,128)(2,1)S(1)}, bf16[3,32,512]{2,1,0:T(8,128)(2,1)S(1)}, u32[]{:S(2)}, u32[]{:S(2)}) %collective-permute-start.15) | collective-permute-done | bytes 98336 | tf_op jit(solution)/shard_map/ppermute | solution.py:492
  89.1 1.7 %collective-permute-start.16 = (bf16[4,64,512]{2,1,0:T(8,128)(2,1)S(1)}, bf16[4,64,512]{2,1,0:T(8,128)(2,1)S(1)}, u32[]{:S(2)}, u32[]{:S(2)}) collective-permute-start(bf16[4,64,512]{2,1,0:T(8,128)(2,1)S(1)} %get-tuple-element.146), channel_id=1, source_target_pairs={{0,4},{1,5},{2,6},{3,7},{4,0},{5,1},{6,2},{7,3},{8,12},{9,13},{10,... | collective-permute-start | bytes 786440 | tf_op jit(solution)/shard_map/ppermute | solution.py:492
  90.8 4.7 %collective-permute-done.17.refs_2_ = bf16[3,32,512]{2,1,0:T(8,128)(2,1)S(1)} collective-permute-done((bf16[3,32,512]{2,1,0:T(8,128)(2,1)S(1)}, bf16[3,32,512]{2,1,0:T(8,128)(2,1)S(1)}, u32[]{:S(2)}, u32[]{:S(2)}) %collective-permute-start.17) | collective-permute-done | bytes 98336 | tf_op jit(solution)/shard_map/ppermute | solution.py:492
  95.6 0.4 collective-permute-start.19
  96.0 3.4 %collective-permute-done.16.refs_2_ = bf16[4,64,512]{2,1,0:T(8,128)(2,1)S(1)} collective-permute-done((bf16[4,64,512]{2,1,0:T(8,128)(2,1)S(1)}, bf16[4,64,512]{2,1,0:T(8,128)(2,1)S(1)}, u32[]{:S(2)}, u32[]{:S(2)}) %collective-permute-start.16) | collective-permute-done | bytes 262176 | tf_op jit(solution)/shard_map/ppermute | solution.py:492
  99.5 3.2 %collective-permute-done.19.refs_2_ = bf16[3,64,512]{2,1,0:T(8,128)(2,1)S(1)} collective-permute-done((bf16[3,64,512]{2,1,0:T(8,128)(2,1)S(1)}, bf16[3,64,512]{2,1,0:T(8,128)(2,1)S(1)}, u32[]{:S(2)}, u32[]{:S(2)}) %collective-permute-start.19) | collective-permute-done | bytes 196640 | tf_op jit(solution)/shard_map/ppermute | solution.py:492
  102.7 0.8 collective-permute-start.26
  103.5 1.6 %collective-permute-start.18 = (bf16[4,32,512]{2,1,0:T(8,128)(2,1)S(1)}, bf16[4,32,512]{2,1,0:T(8,128)(2,1)S(1)}, u32[]{:S(2)}, u32[]{:S(2)}) collective-permute-start(bf16[4,32,512]{2,1,0:T(8,128)(2,1)S(1)} %get-tuple-element.148), channel_id=1, source_target_pairs={{0,8},{1,9},{2,10},{3,11},{4,12},{5,13},{6,14},{7,15},{8,0},{9,1},... | collective-permute-start | bytes 393224 | tf_op jit(solution)/shard_map/ppermute | solution.py:492
  105.1 0.3 collective-permute-start.21
  105.6 8.7 %collective-permute-done.26.refs_2_ = bf16[3,128,512]{2,1,0:T(8,128)(2,1)S(1)} collective-permute-done((bf16[3,128,512]{2,1,0:T(8,128)(2,1)S(1)}, bf16[3,128,512]{2,1,0:T(8,128)(2,1)S(1)}, u32[]{:S(2)}, u32[]{:S(2)}) %collective-permute-start.26) | collective-permute-done | bytes 393248 | tf_op jit(solution)/shard_map/ppermute | solution.py:492
  114.5 9.6 %collective-permute-done.20.refs_2_ = bf16[4,32,512]{2,1,0:T(8,128)(2,1)S(1)} collective-permute-done((bf16[4,32,512]{2,1,0:T(8,128)(2,1)S(1)}, bf16[4,32,512]{2,1,0:T(8,128)(2,1)S(1)}, u32[]{:S(2)}, u32[]{:S(2)}) %collective-permute-start.20) | collective-permute-done | bytes 131104 | tf_op jit(solution)/shard_map/ppermute | solution.py:492
  124.1 2.6 %collective-permute-start.24 = (bf16[128,512]{1,0:T(8,128)(2,1)S(1)}, bf16[128,512]{1,0:T(8,128)(2,1)S(1)}, u32[]{:S(2)}, u32[]{:S(2)}) collective-permute-start(bf16[128,512]{1,0:T(8,128)(2,1)S(1)} %get-tuple-element.116.refs_15_.refs_10_), channel_id=1, source_target_pairs={{2,0},{3,1},{4,2},{5,3},{6,4},{7,5},{8,6},{9,7},{10,8},{11,9},{12,... | collective-permute-start | bytes 393224 | tf_op jit(solution)/shard_map/ppermute | solution.py:21
  126.8 1.3 shard_map.192
  128.0 4.9 %collective-permute-done.24.refs_3_.refs_8_ = bf16[128,512]{1,0:T(8,128)(2,1)S(1)} collective-permute-done((bf16[128,512]{1,0:T(8,128)(2,1)S(1)}, bf16[128,512]{1,0:T(8,128)(2,1)S(1)}, u32[]{:S(2)}, u32[]{:S(2)}) %collective-permute-start.24) | collective-permute-done | bytes 131104 | tf_op jit(solution)/shard_map/ppermute | solution.py:21
  132.9 3.2 %collective-permute-done.25.refs_4_.refs_9_ = bf16[128,512]{1,0:T(8,128)(2,1)S(1)} collective-permute-done((bf16[128,512]{1,0:T(8,128)(2,1)S(1)}, bf16[128,512]{1,0:T(8,128)(2,1)S(1)}, u32[]{:S(2)}, u32[]{:S(2)}) %collective-permute-start.25) | collective-permute-done | bytes 131104 | tf_op jit(solution)/shard_map/ppermute | solution.py:21
  136.2 0.7 collective-permute-start.29
  136.9 0.5 shard_map.194.refs_1_
  137.6 1.6 %shard_map.195.refs_1_ = bf16[320,512]{1,0:T(8,128)(2,1)} custom-call(s32[1]{0:T(128)} %bitcast.refs_0_.refs_2_, f32[320,512]{1,0:T(8,128)S(1)} %shard_map.194.refs_1_, bf16[1536,512]{1,0:T(8,128)(2,1)S(1)} %get-tuple-element.85.refs_4_.refs_6_.refs_2_.refs_3_, s32[11,1,128]{2,1,0:T(1,128)S(1)} %get-tuple-element.84.refs_1_.refs_2_.refs_3_, ...), custom_call_target="tpu_custom_call" | custom-call | flops 1 | bytes 1 | tf_op jit(solution)/shard_map/pallas_call | solution.py:89
  139.2 10.3 %collective-permute-done.29.refs_0_ = bf16[4,128,512]{2,1,0:T(8,128)(2,1)S(1)} collective-permute-done((bf16[4,128,512]{2,1,0:T(8,128)(2,1)S(1)}, bf16[4,128,512]{2,1,0:T(8,128)(2,1)S(1)}, u32[]{:S(2)}, u32[]{:S(2)}) %collective-permute-start.29) | collective-permute-done | bytes 524320 | tf_op jit(solution)/shard_map/ppermute | solution.py:492
  149.6 1.9 %collective-permute-done.31.refs_4_ = bf16[4,128,512]{2,1,0:T(8,128)(2,1)S(1)} collective-permute-done((bf16[4,128,512]{2,1,0:T(8,128)(2,1)S(1)}, bf16[4,128,512]{2,1,0:T(8,128)(2,1)S(1)}, u32[]{:S(2)}, u32[]{:S(2)}) %collective-permute-start.31) | collective-permute-done | bytes 524320 | tf_op jit(solution)/shard_map/ppermute | solution.py:492
  151.5 1.5 shard_map.197
  (45 shorter events, 1.9 us)
Async XLA Ops:
  18.4 5.5 %collective-permute-start.1 = (bf16[128,512]{1,0:T(8,128)(2,1)S(1)}, bf16[128,512]{1,0:T(8,128)(2,1)S(1)}, u32[]{:S(2)}, u32[]{:S(2)}) collective-permute-start(bf16[128,512]{1,0:T(8,128)(2,1)S(1)} %get-tuple-element.94), channel_id=1, source_target_pairs={{1,0},{2,1},{3,2},{4,3},{5,4},{6,5},{7,6},{8,7},{9,8},{10,9},{11,1... | collective-permute-start | bytes 393224 | tf_op jit(solution)/shard_map/ppermute | solution.py:21
  18.6 9.1 %collective-permute-start.2 = (bf16[128,512]{1,0:T(8,128)(2,1)S(1)}, bf16[128,512]{1,0:T(8,128)(2,1)S(1)}, u32[]{:S(2)}, u32[]{:S(2)}) collective-permute-start(bf16[128,512]{1,0:T(8,128)(2,1)S(1)} %get-tuple-element.95), channel_id=1, source_target_pairs={{14,0},{15,1},{0,2},{1,3},{2,4},{3,5},{4,6},{5,7},{6,8},{7,9},{8,1... | collective-permute-start | bytes 393224 | tf_op jit(solution)/shard_map/ppermute | solution.py:21
  19.8 19.6 %collective-permute-start.6 = (bf16[256,512]{1,0:T(8,128)(2,1)S(1)}, bf16[256,512]{1,0:T(8,128)(2,1)S(1)}, u32[]{:S(2)}, u32[]{:S(2)}) collective-permute-start(bf16[256,512]{1,0:T(8,128)(2,1)S(1)} %get-tuple-element.103), channel_id=1, source_target_pairs={{8,0},{9,1},{10,2},{11,3},{12,4},{13,5},{14,6},{15,7},{0,8},{1,9},... | collective-permute-start | bytes 786440 | tf_op jit(solution)/shard_map/ppermute | solution.py:21
  20.6 11.6 %collective-permute-start.3 = (bf16[128,512]{1,0:T(8,128)(2,1)S(1)}, bf16[128,512]{1,0:T(8,128)(2,1)S(1)}, u32[]{:S(2)}, u32[]{:S(2)}) collective-permute-start(bf16[128,512]{1,0:T(8,128)(2,1)S(1)} %get-tuple-element.96), channel_id=1, source_target_pairs={{2,0},{3,1},{4,2},{5,3},{6,4},{7,5},{8,6},{9,7},{10,8},{11,9},{12,... | collective-permute-start | bytes 393224 | tf_op jit(solution)/shard_map/ppermute | solution.py:21
  23.9 11.1 %collective-permute-start = (bf16[128,512]{1,0:T(8,128)(2,1)S(1)}, bf16[128,512]{1,0:T(8,128)(2,1)S(1)}, u32[]{:S(2)}, u32[]{:S(2)}) collective-permute-start(bf16[128,512]{1,0:T(8,128)(2,1)S(1)} %get-tuple-element.88.refs_7_), channel_id=1, source_target_pairs={{15,0},{0,1},{1,2},{2,3},{3,4},{4,5},{5,6},{6,7},{7,8},{8,9},{9,10... | collective-permute-start | bytes 393224 | tf_op jit(solution)/shard_map/ppermute | solution.py:21
  23.9 12.7 %collective-permute-start.4 = (bf16[128,512]{1,0:T(8,128)(2,1)S(1)}, bf16[128,512]{1,0:T(8,128)(2,1)S(1)}, u32[]{:S(2)}, u32[]{:S(2)}) collective-permute-start(bf16[128,512]{1,0:T(8,128)(2,1)S(1)} %get-tuple-element.101), channel_id=1, source_target_pairs={{12,0},{13,1},{14,2},{15,3},{0,4},{1,5},{2,6},{3,7},{4,8},{5,9},{6... | collective-permute-start | bytes 393224 | tf_op jit(solution)/shard_map/ppermute | solution.py:21
  27.8 11.6 %collective-permute-start.5 = (bf16[128,512]{1,0:T(8,128)(2,1)S(1)}, bf16[128,512]{1,0:T(8,128)(2,1)S(1)}, u32[]{:S(2)}, u32[]{:S(2)}) collective-permute-start(bf16[128,512]{1,0:T(8,128)(2,1)S(1)} %get-tuple-element.102), channel_id=1, source_target_pairs={{4,0},{5,1},{6,2},{7,3},{8,4},{9,5},{10,6},{11,7},{12,8},{13,9},{1... | collective-permute-start | bytes 393224 | tf_op jit(solution)/shard_map/ppermute | solution.py:21
  45.2 2.4 %collective-permute-start.10 = (bf16[3,256,512]{2,1,0:T(8,128)(2,1)S(1)}, bf16[3,256,512]{2,1,0:T(8,128)(2,1)S(1)}, u32[]{:S(2)}, u32[]{:S(2)}) collective-permute-start(bf16[3,256,512]{2,1,0:T(8,128)(2,1)S(1)} %get-tuple-element.134), channel_id=1, source_target_pairs={{0,1},{1,0},{2,3},{3,2},{4,5},{5,4},{6,7},{7,6},{8,9},{9,8},{10,11... | collective-permute-start | bytes 2359304 | tf_op jit(solution)/shard_map/ppermute | solution.py:492
  47.7 23.4 %collective-permute-start.11 = (bf16[3,128,512]{2,1,0:T(8,128)(2,1)S(1)}, bf16[3,128,512]{2,1,0:T(8,128)(2,1)S(1)}, u32[]{:S(2)}, u32[]{:S(2)}) collective-permute-start(bf16[3,128,512]{2,1,0:T(8,128)(2,1)S(1)} %get-tuple-element.135), channel_id=1, source_target_pairs={{0,2},{1,3},{2,0},{3,1},{4,6},{5,7},{6,4},{7,5},{8,10},{9,11},{10,... | collective-permute-start | bytes 1179656 | tf_op jit(solution)/shard_map/ppermute | solution.py:492
  52.7 18.4 %collective-permute-start.9 = (bf16[256,512]{1,0:T(8,128)(2,1)S(1)}, bf16[256,512]{1,0:T(8,128)(2,1)S(1)}, u32[]{:S(2)}, u32[]{:S(2)}) collective-permute-start(bf16[256,512]{1,0:T(8,128)(2,1)S(1)} %get-tuple-element.120.refs_19_.refs_14_), channel_id=1, source_target_pairs={{8,0},{9,1},{10,2},{11,3},{12,4},{13,5},{14,6},{15,7},{0,8},{1,9},... | collective-permute-start | bytes 786440 | tf_op jit(solution)/shard_map/ppermute | solution.py:21
  53.1 9.5 %collective-permute-start.7 = (bf16[128,512]{1,0:T(8,128)(2,1)S(1)}, bf16[128,512]{1,0:T(8,128)(2,1)S(1)}, u32[]{:S(2)}, u32[]{:S(2)}) collective-permute-start(bf16[128,512]{1,0:T(8,128)(2,1)S(1)} %get-tuple-element.118.refs_17_.refs_12_), channel_id=1, source_target_pairs={{4,0},{5,1},{6,2},{7,3},{8,4},{9,5},{10,6},{11,7},{12,8},{13,9},{1... | collective-permute-start | bytes 393224 | tf_op jit(solution)/shard_map/ppermute | solution.py:21
  56.5 11.8 %collective-permute-start.8 = (bf16[128,512]{1,0:T(8,128)(2,1)S(1)}, bf16[128,512]{1,0:T(8,128)(2,1)S(1)}, u32[]{:S(2)}, u32[]{:S(2)}) collective-permute-start(bf16[128,512]{1,0:T(8,128)(2,1)S(1)} %get-tuple-element.119.refs_18_.refs_13_), channel_id=1, source_target_pairs={{12,0},{13,1},{14,2},{15,3},{0,4},{1,5},{2,6},{3,7},{4,8},{5,9},{6... | collective-permute-start | bytes 393224 | tf_op jit(solution)/shard_map/ppermute | solution.py:21
  71.1 2.7 %collective-permute-start.12 = (bf16[4,256,512]{2,1,0:T(8,128)(2,1)S(1)}, bf16[4,256,512]{2,1,0:T(8,128)(2,1)S(1)}, u32[]{:S(2)}, u32[]{:S(2)}) collective-permute-start(bf16[4,256,512]{2,1,0:T(8,128)(2,1)S(1)} %shard_map.180.refs_3_), channel_id=1, source_target_pairs={{0,1},{1,0},{2,3},{3,2},{4,5},{5,4},{6,7},{7,6},{8,9},{9,8},{10,11... | collective-permute-start | bytes 3145736 | tf_op jit(solution)/shard_map/ppermute | solution.py:492
  73.9 15.1 %collective-permute-start.13 = (bf16[4,128,512]{2,1,0:T(8,128)(2,1)S(1)}, bf16[4,128,512]{2,1,0:T(8,128)(2,1)S(1)}, u32[]{:S(2)}, u32[]{:S(2)}) collective-permute-start(bf16[4,128,512]{2,1,0:T(8,128)(2,1)S(1)} %get-tuple-element.141), channel_id=1, source_target_pairs={{0,2},{1,3},{2,0},{3,1},{4,6},{5,7},{6,4},{7,5},{8,10},{9,11},{10,... | collective-permute-start | bytes 1572872 | tf_op jit(solution)/shard_map/ppermute | solution.py:492
  74.2 7.6 %collective-permute-start.14 = (bf16[3,64,512]{2,1,0:T(8,128)(2,1)S(1)}, bf16[3,64,512]{2,1,0:T(8,128)(2,1)S(1)}, u32[]{:S(2)}, u32[]{:S(2)}) collective-permute-start(bf16[3,64,512]{2,1,0:T(8,128)(2,1)S(1)} %get-tuple-element.142), channel_id=1, source_target_pairs={{0,4},{1,5},{2,6},{3,7},{4,0},{5,1},{6,2},{7,3},{8,12},{9,13},{10,... | collective-permute-start | bytes 589832 | tf_op jit(solution)/shard_map/ppermute | solution.py:492
  81.8 7.1 %collective-permute-start.15 = (bf16[3,32,512]{2,1,0:T(8,128)(2,1)S(1)}, bf16[3,32,512]{2,1,0:T(8,128)(2,1)S(1)}, u32[]{:S(2)}, u32[]{:S(2)}) collective-permute-start(bf16[3,32,512]{2,1,0:T(8,128)(2,1)S(1)} %get-tuple-element.144), channel_id=1, source_target_pairs={{0,8},{1,9},{2,10},{3,11},{4,12},{5,13},{6,14},{7,15},{8,0},{9,1},... | collective-permute-start | bytes 294920 | tf_op jit(solution)/shard_map/ppermute | solution.py:492
  88.9 6.7 %collective-permute-start.17 = (bf16[3,32,512]{2,1,0:T(8,128)(2,1)S(1)}, bf16[3,32,512]{2,1,0:T(8,128)(2,1)S(1)}, u32[]{:S(2)}, u32[]{:S(2)}) collective-permute-start(bf16[3,32,512]{2,1,0:T(8,128)(2,1)S(1)} %shard_map.185.refs_3_.refs_1_), channel_id=1, source_target_pairs={{0,8},{1,9},{2,10},{3,11},{4,12},{5,13},{6,14},{7,15},{8,0},{9,1},... | collective-permute-start | bytes 294920 | tf_op jit(solution)/shard_map/ppermute | solution.py:492
  89.1 10.4 %collective-permute-start.16 = (bf16[4,64,512]{2,1,0:T(8,128)(2,1)S(1)}, bf16[4,64,512]{2,1,0:T(8,128)(2,1)S(1)}, u32[]{:S(2)}, u32[]{:S(2)}) collective-permute-start(bf16[4,64,512]{2,1,0:T(8,128)(2,1)S(1)} %get-tuple-element.146), channel_id=1, source_target_pairs={{0,4},{1,5},{2,6},{3,7},{4,0},{5,1},{6,2},{7,3},{8,12},{9,13},{10,... | collective-permute-start | bytes 786440 | tf_op jit(solution)/shard_map/ppermute | solution.py:492
  95.6 7.1 %collective-permute-start.19 = (bf16[3,64,512]{2,1,0:T(8,128)(2,1)S(1)}, bf16[3,64,512]{2,1,0:T(8,128)(2,1)S(1)}, u32[]{:S(2)}, u32[]{:S(2)}) collective-permute-start(bf16[3,64,512]{2,1,0:T(8,128)(2,1)S(1)} %shard_map.187.refs_3_.refs_1_), channel_id=1, source_target_pairs={{0,4},{1,5},{2,6},{3,7},{4,0},{5,1},{6,2},{7,3},{8,12},{9,13},{10,... | collective-permute-start | bytes 589832 | tf_op jit(solution)/shard_map/ppermute | solution.py:492
  102.7 11.6 %collective-permute-start.26 = (bf16[3,128,512]{2,1,0:T(8,128)(2,1)S(1)}, bf16[3,128,512]{2,1,0:T(8,128)(2,1)S(1)}, u32[]{:S(2)}, u32[]{:S(2)}) collective-permute-start(bf16[3,128,512]{2,1,0:T(8,128)(2,1)S(1)} %shard_map.189.refs_3_.refs_1_), channel_id=1, source_target_pairs={{0,2},{1,3},{2,0},{3,1},{4,6},{5,7},{6,4},{7,5},{8,10},{9,11},{10,... | collective-permute-start | bytes 1179656 | tf_op jit(solution)/shard_map/ppermute | solution.py:492
  103.5 10.8 %collective-permute-start.18 = (bf16[4,32,512]{2,1,0:T(8,128)(2,1)S(1)}, bf16[4,32,512]{2,1,0:T(8,128)(2,1)S(1)}, u32[]{:S(2)}, u32[]{:S(2)}) collective-permute-start(bf16[4,32,512]{2,1,0:T(8,128)(2,1)S(1)} %get-tuple-element.148), channel_id=1, source_target_pairs={{0,8},{1,9},{2,10},{3,11},{4,12},{5,13},{6,14},{7,15},{8,0},{9,1},... | collective-permute-start | bytes 393224 | tf_op jit(solution)/shard_map/ppermute | solution.py:492
  105.1 9.4 %collective-permute-start.21 = (bf16[128,512]{1,0:T(8,128)(2,1)S(1)}, bf16[128,512]{1,0:T(8,128)(2,1)S(1)}, u32[]{:S(2)}, u32[]{:S(2)}) collective-permute-start(bf16[128,512]{1,0:T(8,128)(2,1)S(1)} %get-tuple-element.114.refs_13_.refs_8_), channel_id=1, source_target_pairs={{1,0},{2,1},{3,2},{4,3},{5,4},{6,5},{7,6},{8,7},{9,8},{10,9},{11,1... | collective-permute-start | bytes 393224 | tf_op jit(solution)/shard_map/ppermute | solution.py:21
  105.4 9.1 %collective-permute-start.22 = (bf16[128,512]{1,0:T(8,128)(2,1)S(1)}, bf16[128,512]{1,0:T(8,128)(2,1)S(1)}, u32[]{:S(2)}, u32[]{:S(2)}) collective-permute-start(bf16[128,512]{1,0:T(8,128)(2,1)S(1)} %get-tuple-element.115.refs_14_.refs_9_), channel_id=1, source_target_pairs={{15,0},{0,1},{1,2},{2,3},{3,4},{4,5},{5,6},{6,7},{7,8},{8,9},{9,10... | collective-permute-start | bytes 393224 | tf_op jit(solution)/shard_map/ppermute | solution.py:21
  105.6 21.2 %collective-permute-start.27 = (bf16[3,128,512]{2,1,0:T(8,128)(2,1)S(1)}, bf16[3,128,512]{2,1,0:T(8,128)(2,1)S(1)}, u32[]{:S(2)}, u32[]{:S(2)}) collective-permute-start(bf16[3,128,512]{2,1,0:T(8,128)(2,1)S(1)} %shard_map.189.refs_3_.refs_1_), channel_id=1, source_target_pairs={{0,1},{1,0},{2,3},{3,2},{4,5},{5,4},{6,7},{7,6},{8,9},{9,8},{10,11... | collective-permute-start | bytes 1179656 | tf_op jit(solution)/shard_map/ppermute | solution.py:492
  114.3 12.5 %collective-permute-start.28 = (bf16[3,128,512]{2,1,0:T(8,128)(2,1)S(1)}, bf16[3,128,512]{2,1,0:T(8,128)(2,1)S(1)}, u32[]{:S(2)}, u32[]{:S(2)}) collective-permute-start(bf16[3,128,512]{2,1,0:T(8,128)(2,1)S(1)} %collective-permute-done.26.refs_2_), channel_id=1, source_target_pairs={{0,1},{1,0},{2,3},{3,2},{4,5},{5,4},{6,7},{7,6},{8,9},{9,8},{10,11... | collective-permute-start | bytes 1179656 | tf_op jit(solution)/shard_map/ppermute | solution.py:492
  114.4 9.7 %collective-permute-start.20 = (bf16[4,32,512]{2,1,0:T(8,128)(2,1)S(1)}, bf16[4,32,512]{2,1,0:T(8,128)(2,1)S(1)}, u32[]{:S(2)}, u32[]{:S(2)}) collective-permute-start(bf16[4,32,512]{2,1,0:T(8,128)(2,1)S(1)} %shard_map.190.refs_1_), channel_id=1, source_target_pairs={{0,8},{1,9},{2,10},{3,11},{4,12},{5,13},{6,14},{7,15},{8,0},{9,1},... | collective-permute-start | bytes 393224 | tf_op jit(solution)/shard_map/ppermute | solution.py:492
  124.1 12.1 %collective-permute-start.23 = (bf16[4,64,512]{2,1,0:T(8,128)(2,1)S(1)}, bf16[4,64,512]{2,1,0:T(8,128)(2,1)S(1)}, u32[]{:S(2)}, u32[]{:S(2)}) collective-permute-start(bf16[4,64,512]{2,1,0:T(8,128)(2,1)S(1)} %shard_map.191.refs_5_.refs_1_), channel_id=1, source_target_pairs={{0,4},{1,5},{2,6},{3,7},{4,0},{5,1},{6,2},{7,3},{8,12},{9,13},{10,... | collective-permute-start | bytes 786440 | tf_op jit(solution)/shard_map/ppermute | solution.py:492
  124.1 8.8 %collective-permute-start.24 = (bf16[128,512]{1,0:T(8,128)(2,1)S(1)}, bf16[128,512]{1,0:T(8,128)(2,1)S(1)}, u32[]{:S(2)}, u32[]{:S(2)}) collective-permute-start(bf16[128,512]{1,0:T(8,128)(2,1)S(1)} %get-tuple-element.116.refs_15_.refs_10_), channel_id=1, source_target_pairs={{2,0},{3,1},{4,2},{5,3},{6,4},{7,5},{8,6},{9,7},{10,8},{11,9},{12,... | collective-permute-start | bytes 393224 | tf_op jit(solution)/shard_map/ppermute | solution.py:21
  126.8 9.4 %collective-permute-start.25 = (bf16[128,512]{1,0:T(8,128)(2,1)S(1)}, bf16[128,512]{1,0:T(8,128)(2,1)S(1)}, u32[]{:S(2)}, u32[]{:S(2)}) collective-permute-start(bf16[128,512]{1,0:T(8,128)(2,1)S(1)} %get-tuple-element.117.refs_16_.refs_11_), channel_id=1, source_target_pairs={{14,0},{15,1},{0,2},{1,3},{2,4},{3,5},{4,6},{5,7},{6,8},{7,9},{8,1... | collective-permute-start | bytes 393224 | tf_op jit(solution)/shard_map/ppermute | solution.py:21
  136.2 13.3 %collective-permute-start.29 = (bf16[4,128,512]{2,1,0:T(8,128)(2,1)S(1)}, bf16[4,128,512]{2,1,0:T(8,128)(2,1)S(1)}, u32[]{:S(2)}, u32[]{:S(2)}) collective-permute-start(bf16[4,128,512]{2,1,0:T(8,128)(2,1)S(1)} %shard_map.193.refs_5_.refs_1_), channel_id=1, source_target_pairs={{0,2},{1,3},{2,0},{3,1},{4,6},{5,7},{6,4},{7,5},{8,10},{9,11},{10,... | collective-permute-start | bytes 1572872 | tf_op jit(solution)/shard_map/ppermute | solution.py:492
  137.5 12.1 %collective-permute-start.30 = (bf16[4,128,512]{2,1,0:T(8,128)(2,1)S(1)}, bf16[4,128,512]{2,1,0:T(8,128)(2,1)S(1)}, u32[]{:S(2)}, u32[]{:S(2)}) collective-permute-start(bf16[4,128,512]{2,1,0:T(8,128)(2,1)S(1)} %shard_map.193.refs_5_.refs_1_), channel_id=1, source_target_pairs={{0,1},{1,0},{2,3},{3,2},{4,5},{5,4},{6,7},{7,6},{8,9},{9,8},{10,11... | collective-permute-start | bytes 1572872 | tf_op jit(solution)/shard_map/ppermute | solution.py:492
  149.5 1.9 %collective-permute-start.31 = (bf16[4,128,512]{2,1,0:T(8,128)(2,1)S(1)}, bf16[4,128,512]{2,1,0:T(8,128)(2,1)S(1)}, u32[]{:S(2)}, u32[]{:S(2)}) collective-permute-start(bf16[4,128,512]{2,1,0:T(8,128)(2,1)S(1)} %shard_map.196.refs_2_), channel_id=1, source_target_pairs={{0,1},{1,0},{2,3},{3,2},{4,5},{5,4},{6,7},{7,6},{8,9},{9,8},{10,11... | collective-permute-start | bytes 1572872 | tf_op jit(solution)/shard_map/ppermute | solution.py:492

commit v13 on v12

--- a/solution.py
+++ b/solution.py
@@ -10,6 +10,7 @@
 band_offsets = (0, 1, -1, 2, -2, 4, -4, 8, -8, 16, -16)
 norm_eps = 1e-05
 near_sets = 7
+edge_work = 20_000_000_000
 bf16 = jnp.bfloat16
 f32 = jnp.float32
 vmem_limit = 20 * 1024 * 1024
@@ -76,7 +77,7 @@
     return (lax.broadcasted_iota(jnp.int32, (cap, 128), 0) < count).astype(f32)
 
 
-def call(body, outs, scratch, *args, smem=(), after=(), last=()):
+def call(body, outs, scratch, *args, smem=(), after=(), last=(), work=1):
     spaces, given = [], []
     for i, arg in enumerate(args):
         spaces.append(pl.BlockSpec(memory_space=pltpu.SMEM if i in smem else pltpu.VMEM))
@@ -96,7 +97,7 @@
         out_specs=[pl.BlockSpec(memory_space=pltpu.VMEM)] * len(outs),
         scratch_shapes=[pltpu.VMEM(shape, kind) for shape, kind in scratch],
         compiler_params=pltpu.CompilerParams(vmem_limit_bytes=vmem_limit),
-        cost_estimate=pl.CostEstimate(flops=1, bytes_accessed=1, transcendentals=0),
+        cost_estimate=pl.CostEstimate(flops=work, bytes_accessed=1, transcendentals=0),
     )(*given, *after)
 
 
@@ -783,6 +784,7 @@
             *gpe,
             after=after,
             last=(0, 1),
+            work=edge_work,
         )
 
     def node_output(after):
@@ -839,28 +841,25 @@
 
         keep_node, sent_node = node_weights([])
         keep_node, came_node = add_stage(me, keep_node, [over(sent_node, 1)], 2, [])
-        sent_edge = held_until(sent_edge, back_far + came_node)
+        sent_edge = held_until(sent_edge, back_far + [keep_node])
         came_edge = [over(sent_edge, 1)]
-        keep_node, came_node = add_stage(me, keep_node, came_node, 4, [sent_edge])
+        edge_new, grad_edges = edge_outputs([sent_edge])
+        keep_node, came_node = add_stage(me, keep_node, came_node, 4, [in_hbm(edge_new)])
         keep_edge, came_edge = add_stage(me, keep_edge, came_edge, 2, [keep_node])
-        edge_new, grad_edges = edge_outputs([keep_edge])
-        keep_node, came_node = add_stage(me, keep_node, came_node, 8, [in_hbm(edge_new)])
+        keep_node, came_node = add_stage(me, keep_node, came_node, 8, [keep_edge])
         piece_node, _ = add_stage(me, keep_node, came_node, 1, [], 1, bf16)
         keep_edge, came_edge = add_stage(me, keep_edge, came_edge, 4, [piece_node])
         piece_node = gather_stage(me, piece_node, over(piece_node, 8), 8, [keep_edge])
         keep_edge, came_edge = add_stage(me, keep_edge, came_edge, 8, [piece_node])
-        piece_node = gather_stage(me, piece_node, over(piece_node, 4), 4, [keep_edge])
-        piece_edge, _ = add_stage(me, keep_edge, came_edge, 1, [piece_node], 1, bf16)
-        some, rest = back_near[: len(back_near) // 2], back_near[len(back_near) // 2 :]
-        piece_edge = gather_stage(me, piece_edge, over(piece_edge, 8), 8, some)
+        piece_edge, _ = add_stage(me, keep_edge, came_edge, 1, back_near, 1, bf16)
+        piece_node = gather_stage(me, piece_node, over(piece_node, 4), 4, [piece_edge])
+        grad_nodes = node_output([piece_node])
+        piece_edge = gather_stage(me, piece_edge, over(piece_edge, 8), 8, [in_hbm(grad_nodes)])
         grad_n1, grad_n2 = join_stage(
             me, piece_node, first, node_blocks, node_shapes, [], [piece_edge]
         )
-        piece_edge = gather_stage(me, piece_edge, over(piece_edge, 4), 4, rest + [in_hbm(grad_n2)])
-        grad_nodes = node_output([piece_edge])
-        grad_e1, grad_e2 = join_stage(
-            me, piece_edge, first, edge_blocks, edge_shapes, [in_hbm(grad_nodes)], []
-        )
+        piece_edge = gather_stage(me, piece_edge, over(piece_edge, 4), 4, [in_hbm(grad_n2)])
+        grad_e1, grad_e2 = join_stage(me, piece_edge, first, edge_blocks, edge_shapes, [], [])
     else:
         whole = reduce_whole(*node_weights([]))
         grad_n1, grad_n2 = whole[:2].reshape(2 * width, width), whole[2]

time: 153 us -> 153 us (level)
  waiting for transfers between devices: 79.8 us -> 71.5 us
  starting transfers between devices: 27.5 us -> 35.4 us
    ppermute x18, waiting for transfers between devices: 53.7 us -> 47.7 us  [in_group(): return lax.ppermute(block, axis, route)]
    ppermute x14, starting transfers between devices: 12.5 us -> 16.7 us  [passed_along(): return lax.ppermute(block, axis, route)]
    ppermute x18, starting transfers between devices: 15 us -> 18.7 us  [in_group(): return lax.ppermute(block, axis, route)]
    ppermute x14, waiting for transfers between devices: 26.1 us -> 23.7 us  [passed_along(): return lax.ppermute(block, axis, route)]
  transfers between devices with their start and end apart: 32 -> 32, of which waited for: 19 -> 16; matrix products, arithmetic and copies ran while one was open for 0% -> 0% of each run, Pallas kernels for 13% -> 13%
where the time goes in v13:
time: 153 us; the launch traced here: 152 us
  waiting for transfers between devices  71.5 us (47%)
  starting transfers between devices  35.4 us (23%)
  Pallas kernels  31 us (20%)
  blocking collectives  13.7 us (9%)
    ppermute x18, waiting for transfers between devices, in_group(): return lax.ppermute(block, axis, route)  47.7 us
    pallas_call x25, Pallas kernels, call(): pl.pallas_call(kernel, out_shape=[(pltpu.HBM if i in last else pltpu.VMEM...  27.8 us
    ppermute x14, waiting for transfers between devices, passed_along(): return lax.ppermute(block, axis, route)  23.7 us
    ppermute x18, starting transfers between devices, in_group(): return lax.ppermute(block, axis, route)  18.7 us
    ppermute x14, starting transfers between devices, passed_along(): return lax.ppermute(block, axis, route)  16.7 us
    all_to_all x1, blocking collectives, local(): ids = lax.all_to_all(ids, 'band', 0, 0, tiled=True)  13.7 us
    pallas_call x1, Pallas kernels, loaded(): pl.pallas_call(functools.partial(load_kernel, count), out_shape=[pltpu.VM...  3.24 us
  transfers between devices with their start and end apart: 32, of which 16 were waited for; matrix products, arithmetic and copies ran while one was open for 0% of the time, Pallas kernels for 13%

profile of v13, /device:TPU:0, one launch (start us, length us, event | category | flops | bytes accessed | tf_op | source)
XLA Modules:
  0.0 152.5 jit_solution(17757880598804549413)
XLA Ops:
  0.6 3.2 %shard_map.170 = (bf16[320,512]{1,0:T(8,128)(2,1)S(1)}, s32[11,1,128]{2,1,0:T(1,128)S(1)}, s32[11,1,128]{2,1,0:T(1,128)S(1)}, bf16[11,128,512]{2,1,0:T(8,128)(2,...) custom-call(s32[1]{0:T(128)} %bitcast.refs_0_.refs_2_, ...), custom_call_target="tpu_custom_call" | custom-call | flops 1 | bytes 1 | tf_op jit(solution)/shard_map/pallas_call | solution.py:121
  3.9 13.7 %all_to_all.5.refs_2_.refs_4_ = s32[16,1,256]{2,1,0:T(1,128)S(1)} all-to-all(s32[16,1,256]{2,1,0:T(1,128)S(1)} %shard_map.171), channel_id=1, replica_groups=mesh['groups'=2,'band'=16] {'band'}, dimensions={0} | all-to-all | bytes 32768 | tf_op jit(solution)/shard_map/all_to_all | solution.py:639
  17.6 0.8 shard_map.172
  18.4 0.3 collective-permute-start.1
  18.6 1.2 collective-permute-start.2
  19.8 0.8 collective-permute-start.6
  20.6 3.3 %collective-permute-start.3 = (bf16[128,512]{1,0:T(8,128)(2,1)S(1)}, bf16[128,512]{1,0:T(8,128)(2,1)S(1)}, u32[]{:S(2)}, u32[]{:S(2)}) collective-permute-start(bf16[128,512]{1,0:T(8,128)(2,1)S(1)} %get-tuple-element.96), channel_id=1, source_target_pairs={{2,0},{3,1},{4,2},{5,3},{6,4},{7,5},{8,6},{9,7},{10,8},{11,9},{12,... | collective-permute-start | bytes 393224 | tf_op jit(solution)/shard_map/ppermute | solution.py:22
  23.9 3.8 %collective-permute-done.2.refs_8_.refs_7_ = bf16[128,512]{1,0:T(8,128)(2,1)S(1)} collective-permute-done((bf16[128,512]{1,0:T(8,128)(2,1)S(1)}, bf16[128,512]{1,0:T(8,128)(2,1)S(1)}, u32[]{:S(2)}, u32[]{:S(2)}) %collective-permute-start.2) | collective-permute-done | bytes 131104 | tf_op jit(solution)/shard_map/ppermute | solution.py:22
  27.8 4.5 %shard_map.173 = (bf16[1408,320]{1,0:T(8,128)(2,1)S(1)}, bf16[320,1408]{1,0:T(8,128)(2,1)S(1)}, f32[1408,128]{1,0:T(8,128)S(1)}, f32[1024,512]{1,0:T(8,128)S(1)}...) custom-call(bf16[11,128,512]{2,1,0:T(8,128)(2,1)S(1)} %get-tuple-ele, ...), custom_call_target="tpu_custom_call" | custom-call | flops 1 | bytes 1 | tf_op jit(solution)/shard_map/pallas_call | solution.py:90
  32.3 2.7 %collective-permute-done.refs_6_.refs_5_ = bf16[128,512]{1,0:T(8,128)(2,1)S(1)} collective-permute-done((bf16[128,512]{1,0:T(8,128)(2,1)S(1)}, bf16[128,512]{1,0:T(8,128)(2,1)S(1)}, u32[]{:S(2)}, u32[]{:S(2)}) %collective-permute-start) | collective-permute-done | bytes 131104 | tf_op jit(solution)/shard_map/ppermute | solution.py:22
  35.0 1.6 %shard_map.174 = (bf16[512,512]{1,0:T(8,128)(2,1)S(1)}, f32[512,512]{1,0:T(8,128)S(1)}, f32[512,512]{1,0:T(8,128)S(1)}, f32[512,128]{1,0:T(8,128)S(1)}, f32[320,512]{1,0:T(8,128)S(1)}) custom-call(f32[1024,512]{1,0:T(8,128)S(1)} %get-tuple-element.89.refs_0_.refs_1_, f32[1408,128]{1,0:T(8,128)S(1)} %get-tuple-element.90.refs_1_.refs_2_.refs_3_, ...), custom_call_target="tpu_custom_call" | custom-call | flops 1 | bytes 1 | tf_op jit(solution)/shard_map/pallas_call | solution.py:90
  36.6 2.8 %collective-permute-done.5.refs_13_.refs_10_ = bf16[128,512]{1,0:T(8,128)(2,1)S(1)} collective-permute-done((bf16[128,512]{1,0:T(8,128)(2,1)S(1)}, bf16[128,512]{1,0:T(8,128)(2,1)S(1)}, u32[]{:S(2)}, u32[]{:S(2)}) %collective-permute-start.5) | collective-permute-done | bytes 131104 | tf_op jit(solution)/shard_map/ppermute | solution.py:22
  39.4 4.5 %shard_map.175 = (bf16[128,512]{1,0:T(8,128)(2,1)S(1)}, bf16[128,512]{1,0:T(8,128)(2,1)S(1)}, bf16[256,512]{1,0:T(8,128)(2,1)S(1)}, bf16[512,512]{1,0:T(8,128)(2...) custom-call(bf16[11,128,512]{2,1,0:T(8,128)(2,1)S(1)} %get-tuple-ele, ...), custom_call_target="tpu_custom_call" | custom-call | flops 1 | bytes 1 | tf_op jit(solution)/shard_map/pallas_call | solution.py:90
  43.9 1.3 shard_map.178
  45.3 4.7 %collective-permute-start.9 = (bf16[256,512]{1,0:T(8,128)(2,1)S(1)}, bf16[256,512]{1,0:T(8,128)(2,1)S(1)}, u32[]{:S(2)}, u32[]{:S(2)}) collective-permute-start(bf16[256,512]{1,0:T(8,128)(2,1)S(1)} %get-tuple-element.120.refs_19_.refs_14_), channel_id=1, source_target_pairs={{8,0},{9,1},{10,2},{11,3},{12,4},{13,5},{14,6},{15,7},{0,8},{1,9},... | collective-permute-start | bytes 786440 | tf_op jit(solution)/shard_map/ppermute | solution.py:22
  50.0 1.7 %collective-permute-start.7 = (bf16[128,512]{1,0:T(8,128)(2,1)S(1)}, bf16[128,512]{1,0:T(8,128)(2,1)S(1)}, u32[]{:S(2)}, u32[]{:S(2)}) collective-permute-start(bf16[128,512]{1,0:T(8,128)(2,1)S(1)} %get-tuple-element.118.refs_17_.refs_12_), channel_id=1, source_target_pairs={{4,0},{5,1},{6,2},{7,3},{8,4},{9,5},{10,6},{11,7},{12,8},{13,9},{1... | collective-permute-start | bytes 393224 | tf_op jit(solution)/shard_map/ppermute | solution.py:22
  51.7 0.4 collective-permute-start.8
  52.0 2.1 %shard_map.176 = (bf16[896,512]{1,0:T(8,128)(2,1)S(1)}, bf16[384,512]{1,0:T(8,128)(2,1)S(1)}, bf16[128,512]{1,0:T(8,128)(2,1)S(1)}, bf16[128,512]{1,0:T(8,128)(2...) custom-call(bf16[11,128,512]{2,1,0:T(8,128)(2,1)S(1)} %get-tuple-element.81.refs_0_.refs_1_, ...), custom_call_target="tpu_custom_call" | custom-call | flops 1 | bytes 1 | tf_op jit(solution)/shard_map/pallas_call | solution.py:90
  54.1 3.9 %shard_map.177 = (f32[4,256,512]{2,1,0:T(8,128)S(1)}, bf16[4,256,512]{2,1,0:T(8,128)(2,1)S(1)}, bf16[320,512]{1,0:T(8,128)(2,1)S(1)}) custom-call(bf16[11,128,512]{2,1,0:T(8,128)(2,1)S(1)} %get-tuple-element.82.refs_0_, bf16[320,1408]{1,0:T(8,128)(2,1)S(1)} %get-tuple-element.92.refs_2_.refs_4_.refs_1_, s32[1]{0:T(128)} %bitcast.refs_0_.refs_2_, ...), custom_call_target="tpu_custom_call" | custom-call | flops 1 | bytes 1 | tf_op jit(solution)/shard_map/pallas_call | solution.py:90
  58.1 2.1 %collective-permute-start.11 = (bf16[3,128,512]{2,1,0:T(8,128)(2,1)S(1)}, bf16[3,128,512]{2,1,0:T(8,128)(2,1)S(1)}, u32[]{:S(2)}, u32[]{:S(2)}) collective-permute-start(bf16[3,128,512]{2,1,0:T(8,128)(2,1)S(1)} %get-tuple-element.137), channel_id=1, source_target_pairs={{0,2},{1,3},{2,0},{3,1},{4,6},{5,7},{6,4},{7,5},{8,10},{9,11},{10,... | collective-permute-start | bytes 1179656 | tf_op jit(solution)/shard_map/ppermute | solution.py:493
  60.3 3.8 %collective-permute-done.8.refs_2_.refs_11_ = bf16[128,512]{1,0:T(8,128)(2,1)S(1)} collective-permute-done((bf16[128,512]{1,0:T(8,128)(2,1)S(1)}, bf16[128,512]{1,0:T(8,128)(2,1)S(1)}, u32[]{:S(2)}, u32[]{:S(2)}) %collective-permute-start.8) | collective-permute-done | bytes 131104 | tf_op jit(solution)/shard_map/ppermute | solution.py:22
  64.0 1.5 %collective-permute-done.9.refs_3_.refs_12_ = bf16[256,512]{1,0:T(8,128)(2,1)S(1)} collective-permute-done((bf16[256,512]{1,0:T(8,128)(2,1)S(1)}, bf16[256,512]{1,0:T(8,128)(2,1)S(1)}, u32[]{:S(2)}, u32[]{:S(2)}) %collective-permute-start.9) | collective-permute-done | bytes 262176 | tf_op jit(solution)/shard_map/ppermute | solution.py:22
  65.6 3.5 %shard_map.181 = (bf16[11,128,512]{2,1,0:T(8,128)(2,1)}, bf16[11,128,512]{2,1,0:T(8,128)(2,1)}) custom-call(bf16[11,128,512]{2,1,0:T(8,128)(2,1)S(1)} %get-tuple-element.82.refs_0_, bf16[11,128,512]{2,1,0:T(8,128)(2,1)S(1)} %get-tuple-element.81.refs_0_.refs_1_, bf16[1536,512]{1,0:T(8,128)(2,1)S(1)} %get-tuple-element.85.refs_4_.refs_6_.refs_2_.refs_3_, ...), custom_call_target="tpu_custom_call" | custom-call | flops 20000000000 | bytes 1 | tf_op jit(solution)/shard_map/pallas_call | solution.py:90
  69.1 0.3 collective-permute-done.11.refs_2_
  69.5 0.2 shard_map.183
  69.7 2.9 %collective-permute-start.16 = (bf16[4,128,512]{2,1,0:T(8,128)(2,1)S(1)}, bf16[4,128,512]{2,1,0:T(8,128)(2,1)S(1)}, u32[]{:S(2)}, u32[]{:S(2)}) collective-permute-start(bf16[4,128,512]{2,1,0:T(8,128)(2,1)S(1)} %get-tuple-element.144), channel_id=1, source_target_pairs={{0,2},{1,3},{2,0},{3,1},{4,6},{5,7},{6,4},{7,5},{8,10},{9,11},{10,... | collective-permute-start | bytes 1572872 | tf_op jit(solution)/shard_map/ppermute | solution.py:493
  72.6 3.0 %collective-permute-start.12 = (bf16[3,64,512]{2,1,0:T(8,128)(2,1)S(1)}, bf16[3,64,512]{2,1,0:T(8,128)(2,1)S(1)}, u32[]{:S(2)}, u32[]{:S(2)}) collective-permute-start(bf16[3,64,512]{2,1,0:T(8,128)(2,1)S(1)} %get-tuple-element.139), channel_id=1, source_target_pairs={{0,4},{1,5},{2,6},{3,7},{4,0},{5,1},{6,2},{7,3},{8,12},{9,13},{10,... | collective-permute-start | bytes 589832 | tf_op jit(solution)/shard_map/ppermute | solution.py:493
  75.6 5.3 %collective-permute-done.12.refs_2_ = bf16[3,64,512]{2,1,0:T(8,128)(2,1)S(1)} collective-permute-done((bf16[3,64,512]{2,1,0:T(8,128)(2,1)S(1)}, bf16[3,64,512]{2,1,0:T(8,128)(2,1)S(1)}, u32[]{:S(2)}, u32[]{:S(2)}) %collective-permute-start.12) | collective-permute-done | bytes 196640 | tf_op jit(solution)/shard_map/ppermute | solution.py:493
  80.9 1.4 collective-permute-start.14
  82.3 6.0 %collective-permute-done.14.refs_2_ = bf16[3,32,512]{2,1,0:T(8,128)(2,1)S(1)} collective-permute-done((bf16[3,32,512]{2,1,0:T(8,128)(2,1)S(1)}, bf16[3,32,512]{2,1,0:T(8,128)(2,1)S(1)}, u32[]{:S(2)}, u32[]{:S(2)}) %collective-permute-start.14) | collective-permute-done | bytes 98336 | tf_op jit(solution)/shard_map/ppermute | solution.py:493
  88.6 1.7 %collective-permute-start.15 = (bf16[3,32,512]{2,1,0:T(8,128)(2,1)S(1)}, bf16[3,32,512]{2,1,0:T(8,128)(2,1)S(1)}, u32[]{:S(2)}, u32[]{:S(2)}) collective-permute-start(bf16[3,32,512]{2,1,0:T(8,128)(2,1)S(1)} %shard_map.185.refs_3_.refs_1_), channel_id=1, source_target_pairs={{0,8},{1,9},{2,10},{3,11},{4,12},{5,13},{6,14},{7,15},{8,0},{9,1},... | collective-permute-start | bytes 294920 | tf_op jit(solution)/shard_map/ppermute | solution.py:493
  90.3 0.7 collective-permute-start.20
  91.0 5.1 %collective-permute-done.15.refs_2_ = bf16[3,32,512]{2,1,0:T(8,128)(2,1)S(1)} collective-permute-done((bf16[3,32,512]{2,1,0:T(8,128)(2,1)S(1)}, bf16[3,32,512]{2,1,0:T(8,128)(2,1)S(1)}, u32[]{:S(2)}, u32[]{:S(2)}) %collective-permute-start.15) | collective-permute-done | bytes 98336 | tf_op jit(solution)/shard_map/ppermute | solution.py:493
  96.1 2.2 %collective-permute-start.17 = (bf16[3,64,512]{2,1,0:T(8,128)(2,1)S(1)}, bf16[3,64,512]{2,1,0:T(8,128)(2,1)S(1)}, u32[]{:S(2)}, u32[]{:S(2)}) collective-permute-start(bf16[3,64,512]{2,1,0:T(8,128)(2,1)S(1)} %shard_map.187.refs_3_.refs_1_), channel_id=1, source_target_pairs={{0,4},{1,5},{2,6},{3,7},{4,0},{5,1},{6,2},{7,3},{8,12},{9,13},{10,... | collective-permute-start | bytes 589832 | tf_op jit(solution)/shard_map/ppermute | solution.py:493
  98.3 3.7 %collective-permute-start.22 = (bf16[128,512]{1,0:T(8,128)(2,1)S(1)}, bf16[128,512]{1,0:T(8,128)(2,1)S(1)}, u32[]{:S(2)}, u32[]{:S(2)}) collective-permute-start(bf16[128,512]{1,0:T(8,128)(2,1)S(1)} %get-tuple-element.116.refs_15_.refs_10_), channel_id=1, source_target_pairs={{2,0},{3,1},{4,2},{5,3},{6,4},{7,5},{8,6},{9,7},{10,8},{11,9},{12,... | collective-permute-start | bytes 393224 | tf_op jit(solution)/shard_map/ppermute | solution.py:22
  102.1 4.6 %collective-permute-done.21.refs_4_.refs_7_ = bf16[128,512]{1,0:T(8,128)(2,1)S(1)} collective-permute-done((bf16[128,512]{1,0:T(8,128)(2,1)S(1)}, bf16[128,512]{1,0:T(8,128)(2,1)S(1)}, u32[]{:S(2)}, u32[]{:S(2)}) %collective-permute-start.21) | collective-permute-done | bytes 131104 | tf_op jit(solution)/shard_map/ppermute | solution.py:22
  106.7 4.4 %collective-permute-done.23.refs_6_.refs_9_ = bf16[128,512]{1,0:T(8,128)(2,1)S(1)} collective-permute-done((bf16[128,512]{1,0:T(8,128)(2,1)S(1)}, bf16[128,512]{1,0:T(8,128)(2,1)S(1)}, u32[]{:S(2)}, u32[]{:S(2)}) %collective-permute-start.23) | collective-permute-done | bytes 131104 | tf_op jit(solution)/shard_map/ppermute | solution.py:22
  111.2 0.9 collective-permute-done.19.refs_2_
  112.2 3.3 %collective-permute-start.26 = (bf16[3,128,512]{2,1,0:T(8,128)(2,1)S(1)}, bf16[3,128,512]{2,1,0:T(8,128)(2,1)S(1)}, u32[]{:S(2)}, u32[]{:S(2)}) collective-permute-start(bf16[3,128,512]{2,1,0:T(8,128)(2,1)S(1)} %shard_map.190.refs_5_.refs_1_), channel_id=1, source_target_pairs={{0,2},{1,3},{2,0},{3,1},{4,6},{5,7},{6,4},{7,5},{8,10},{9,11},{10,... | collective-permute-start | bytes 1179656 | tf_op jit(solution)/shard_map/ppermute | solution.py:493
  115.5 8.9 %collective-permute-done.26.refs_2_ = bf16[3,128,512]{2,1,0:T(8,128)(2,1)S(1)} collective-permute-done((bf16[3,128,512]{2,1,0:T(8,128)(2,1)S(1)}, bf16[3,128,512]{2,1,0:T(8,128)(2,1)S(1)}, u32[]{:S(2)}, u32[]{:S(2)}) %collective-permute-start.26) | collective-permute-done | bytes 393248 | tf_op jit(solution)/shard_map/ppermute | solution.py:493
  124.4 0.5 shard_map.191.refs_1_
  125.0 1.6 %shard_map.192.refs_3_ = bf16[320,512]{1,0:T(8,128)(2,1)} custom-call(s32[1]{0:T(128)} %bitcast.refs_0_.refs_2_, f32[320,512]{1,0:T(8,128)S(1)} %shard_map.191.refs_1_, bf16[1536,512]{1,0:T(8,128)(2,1)S(1)} %get-tuple-element.85.refs_4_.refs_6_.refs_2_.refs_3_, s32[11,1,128]{2,1,0:T(1,128)S(1)} %get-tuple-element.84.refs_1_.refs_2_.refs_3_, ...), custom_call_target="tpu_custom_call" | custom-call | flops 1 | bytes 1 | tf_op jit(solution)/shard_map/pallas_call | solution.py:90
  126.8 1.3 shard_map.194
  128.0 7.4 %collective-permute-done.25.refs_2_ = bf16[4,64,512]{2,1,0:T(8,128)(2,1)S(1)} collective-permute-done((bf16[4,64,512]{2,1,0:T(8,128)(2,1)S(1)}, bf16[4,64,512]{2,1,0:T(8,128)(2,1)S(1)}, u32[]{:S(2)}, u32[]{:S(2)}) %collective-permute-start.25) | collective-permute-done | bytes 262176 | tf_op jit(solution)/shard_map/ppermute | solution.py:493
  135.5 1.8 %collective-permute-start.29 = (bf16[4,128,512]{2,1,0:T(8,128)(2,1)S(1)}, bf16[4,128,512]{2,1,0:T(8,128)(2,1)S(1)}, u32[]{:S(2)}, u32[]{:S(2)}) collective-permute-start(bf16[4,128,512]{2,1,0:T(8,128)(2,1)S(1)} %shard_map.195.refs_1_), channel_id=1, source_target_pairs={{0,2},{1,3},{2,0},{3,1},{4,6},{5,7},{6,4},{7,5},{8,10},{9,11},{10,... | collective-permute-start | bytes 1572872 | tf_op jit(solution)/shard_map/ppermute | solution.py:493
  137.3 11.8 %collective-permute-done.29.refs_2_ = bf16[4,128,512]{2,1,0:T(8,128)(2,1)S(1)} collective-permute-done((bf16[4,128,512]{2,1,0:T(8,128)(2,1)S(1)}, bf16[4,128,512]{2,1,0:T(8,128)(2,1)S(1)}, u32[]{:S(2)}, u32[]{:S(2)}) %collective-permute-start.29) | collective-permute-done | bytes 524320 | tf_op jit(solution)/shard_map/ppermute | solution.py:493
  149.1 1.9 %collective-permute-done.31.refs_4_ = bf16[4,128,512]{2,1,0:T(8,128)(2,1)S(1)} collective-permute-done((bf16[4,128,512]{2,1,0:T(8,128)(2,1)S(1)}, bf16[4,128,512]{2,1,0:T(8,128)(2,1)S(1)}, u32[]{:S(2)}, u32[]{:S(2)}) %collective-permute-start.31) | collective-permute-done | bytes 524320 | tf_op jit(solution)/shard_map/ppermute | solution.py:493
  151.0 1.5 shard_map.196
  (44 shorter events, 1.0 us)
Async XLA Ops:
  18.4 5.5 %collective-permute-start.1 = (bf16[128,512]{1,0:T(8,128)(2,1)S(1)}, bf16[128,512]{1,0:T(8,128)(2,1)S(1)}, u32[]{:S(2)}, u32[]{:S(2)}) collective-permute-start(bf16[128,512]{1,0:T(8,128)(2,1)S(1)} %get-tuple-element.94), channel_id=1, source_target_pairs={{1,0},{2,1},{3,2},{4,3},{5,4},{6,5},{7,6},{8,7},{9,8},{10,9},{11,1... | collective-permute-start | bytes 393224 | tf_op jit(solution)/shard_map/ppermute | solution.py:22
  18.6 9.1 %collective-permute-start.2 = (bf16[128,512]{1,0:T(8,128)(2,1)S(1)}, bf16[128,512]{1,0:T(8,128)(2,1)S(1)}, u32[]{:S(2)}, u32[]{:S(2)}) collective-permute-start(bf16[128,512]{1,0:T(8,128)(2,1)S(1)} %get-tuple-element.95), channel_id=1, source_target_pairs={{14,0},{15,1},{0,2},{1,3},{2,4},{3,5},{4,6},{5,7},{6,8},{7,9},{8,1... | collective-permute-start | bytes 393224 | tf_op jit(solution)/shard_map/ppermute | solution.py:22
  19.8 19.6 %collective-permute-start.6 = (bf16[256,512]{1,0:T(8,128)(2,1)S(1)}, bf16[256,512]{1,0:T(8,128)(2,1)S(1)}, u32[]{:S(2)}, u32[]{:S(2)}) collective-permute-start(bf16[256,512]{1,0:T(8,128)(2,1)S(1)} %get-tuple-element.103), channel_id=1, source_target_pairs={{8,0},{9,1},{10,2},{11,3},{12,4},{13,5},{14,6},{15,7},{0,8},{1,9},... | collective-permute-start | bytes 786440 | tf_op jit(solution)/shard_map/ppermute | solution.py:22
  20.6 11.6 %collective-permute-start.3 = (bf16[128,512]{1,0:T(8,128)(2,1)S(1)}, bf16[128,512]{1,0:T(8,128)(2,1)S(1)}, u32[]{:S(2)}, u32[]{:S(2)}) collective-permute-start(bf16[128,512]{1,0:T(8,128)(2,1)S(1)} %get-tuple-element.96), channel_id=1, source_target_pairs={{2,0},{3,1},{4,2},{5,3},{6,4},{7,5},{8,6},{9,7},{10,8},{11,9},{12,... | collective-permute-start | bytes 393224 | tf_op jit(solution)/shard_map/ppermute | solution.py:22
  23.9 11.1 %collective-permute-start = (bf16[128,512]{1,0:T(8,128)(2,1)S(1)}, bf16[128,512]{1,0:T(8,128)(2,1)S(1)}, u32[]{:S(2)}, u32[]{:S(2)}) collective-permute-start(bf16[128,512]{1,0:T(8,128)(2,1)S(1)} %get-tuple-element.88.refs_7_), channel_id=1, source_target_pairs={{15,0},{0,1},{1,2},{2,3},{3,4},{4,5},{5,6},{6,7},{7,8},{8,9},{9,10... | collective-permute-start | bytes 393224 | tf_op jit(solution)/shard_map/ppermute | solution.py:22
  23.9 12.7 %collective-permute-start.4 = (bf16[128,512]{1,0:T(8,128)(2,1)S(1)}, bf16[128,512]{1,0:T(8,128)(2,1)S(1)}, u32[]{:S(2)}, u32[]{:S(2)}) collective-permute-start(bf16[128,512]{1,0:T(8,128)(2,1)S(1)} %get-tuple-element.101), channel_id=1, source_target_pairs={{12,0},{13,1},{14,2},{15,3},{0,4},{1,5},{2,6},{3,7},{4,8},{5,9},{6... | collective-permute-start | bytes 393224 | tf_op jit(solution)/shard_map/ppermute | solution.py:22
  27.8 11.6 %collective-permute-start.5 = (bf16[128,512]{1,0:T(8,128)(2,1)S(1)}, bf16[128,512]{1,0:T(8,128)(2,1)S(1)}, u32[]{:S(2)}, u32[]{:S(2)}) collective-permute-start(bf16[128,512]{1,0:T(8,128)(2,1)S(1)} %get-tuple-element.102), channel_id=1, source_target_pairs={{4,0},{5,1},{6,2},{7,3},{8,4},{9,5},{10,6},{11,7},{12,8},{13,9},{1... | collective-permute-start | bytes 393224 | tf_op jit(solution)/shard_map/ppermute | solution.py:22
  45.2 12.8 %collective-permute-start.10 = (bf16[3,256,512]{2,1,0:T(8,128)(2,1)S(1)}, bf16[3,256,512]{2,1,0:T(8,128)(2,1)S(1)}, u32[]{:S(2)}, u32[]{:S(2)}) collective-permute-start(bf16[3,256,512]{2,1,0:T(8,128)(2,1)S(1)} %get-tuple-element.133), channel_id=1, source_target_pairs={{0,1},{1,0},{2,3},{3,2},{4,5},{5,4},{6,7},{7,6},{8,9},{9,8},{10,11... | collective-permute-start | bytes 2359304 | tf_op jit(solution)/shard_map/ppermute | solution.py:493
  45.3 20.3 %collective-permute-start.9 = (bf16[256,512]{1,0:T(8,128)(2,1)S(1)}, bf16[256,512]{1,0:T(8,128)(2,1)S(1)}, u32[]{:S(2)}, u32[]{:S(2)}) collective-permute-start(bf16[256,512]{1,0:T(8,128)(2,1)S(1)} %get-tuple-element.120.refs_19_.refs_14_), channel_id=1, source_target_pairs={{8,0},{9,1},{10,2},{11,3},{12,4},{13,5},{14,6},{15,7},{0,8},{1,9},... | collective-permute-start | bytes 786440 | tf_op jit(solution)/shard_map/ppermute | solution.py:22
  50.0 10.2 %collective-permute-start.7 = (bf16[128,512]{1,0:T(8,128)(2,1)S(1)}, bf16[128,512]{1,0:T(8,128)(2,1)S(1)}, u32[]{:S(2)}, u32[]{:S(2)}) collective-permute-start(bf16[128,512]{1,0:T(8,128)(2,1)S(1)} %get-tuple-element.118.refs_17_.refs_12_), channel_id=1, source_target_pairs={{4,0},{5,1},{6,2},{7,3},{8,4},{9,5},{10,6},{11,7},{12,8},{13,9},{1... | collective-permute-start | bytes 393224 | tf_op jit(solution)/shard_map/ppermute | solution.py:22
  51.7 12.4 %collective-permute-start.8 = (bf16[128,512]{1,0:T(8,128)(2,1)S(1)}, bf16[128,512]{1,0:T(8,128)(2,1)S(1)}, u32[]{:S(2)}, u32[]{:S(2)}) collective-permute-start(bf16[128,512]{1,0:T(8,128)(2,1)S(1)} %get-tuple-element.119.refs_18_.refs_13_), channel_id=1, source_target_pairs={{12,0},{13,1},{14,2},{15,3},{0,4},{1,5},{2,6},{3,7},{4,8},{5,9},{6... | collective-permute-start | bytes 393224 | tf_op jit(solution)/shard_map/ppermute | solution.py:22
  58.1 11.3 %collective-permute-start.11 = (bf16[3,128,512]{2,1,0:T(8,128)(2,1)S(1)}, bf16[3,128,512]{2,1,0:T(8,128)(2,1)S(1)}, u32[]{:S(2)}, u32[]{:S(2)}) collective-permute-start(bf16[3,128,512]{2,1,0:T(8,128)(2,1)S(1)} %get-tuple-element.137), channel_id=1, source_target_pairs={{0,2},{1,3},{2,0},{3,1},{4,6},{5,7},{6,4},{7,5},{8,10},{9,11},{10,... | collective-permute-start | bytes 1179656 | tf_op jit(solution)/shard_map/ppermute | solution.py:493
  65.6 3.9 %collective-permute-start.13 = (bf16[4,256,512]{2,1,0:T(8,128)(2,1)S(1)}, bf16[4,256,512]{2,1,0:T(8,128)(2,1)S(1)}, u32[]{:S(2)}, u32[]{:S(2)}) collective-permute-start(bf16[4,256,512]{2,1,0:T(8,128)(2,1)S(1)} %shard_map.180.refs_15_), channel_id=1, source_target_pairs={{0,1},{1,0},{2,3},{3,2},{4,5},{5,4},{6,7},{7,6},{8,9},{9,8},{10,11... | collective-permute-start | bytes 3145736 | tf_op jit(solution)/shard_map/ppermute | solution.py:493
  69.7 18.7 %collective-permute-start.16 = (bf16[4,128,512]{2,1,0:T(8,128)(2,1)S(1)}, bf16[4,128,512]{2,1,0:T(8,128)(2,1)S(1)}, u32[]{:S(2)}, u32[]{:S(2)}) collective-permute-start(bf16[4,128,512]{2,1,0:T(8,128)(2,1)S(1)} %get-tuple-element.144), channel_id=1, source_target_pairs={{0,2},{1,3},{2,0},{3,1},{4,6},{5,7},{6,4},{7,5},{8,10},{9,11},{10,... | collective-permute-start | bytes 1572872 | tf_op jit(solution)/shard_map/ppermute | solution.py:493
  72.6 8.3 %collective-permute-start.12 = (bf16[3,64,512]{2,1,0:T(8,128)(2,1)S(1)}, bf16[3,64,512]{2,1,0:T(8,128)(2,1)S(1)}, u32[]{:S(2)}, u32[]{:S(2)}) collective-permute-start(bf16[3,64,512]{2,1,0:T(8,128)(2,1)S(1)} %get-tuple-element.139), channel_id=1, source_target_pairs={{0,4},{1,5},{2,6},{3,7},{4,0},{5,1},{6,2},{7,3},{8,12},{9,13},{10,... | collective-permute-start | bytes 589832 | tf_op jit(solution)/shard_map/ppermute | solution.py:493
  80.9 7.5 %collective-permute-start.14 = (bf16[3,32,512]{2,1,0:T(8,128)(2,1)S(1)}, bf16[3,32,512]{2,1,0:T(8,128)(2,1)S(1)}, u32[]{:S(2)}, u32[]{:S(2)}) collective-permute-start(bf16[3,32,512]{2,1,0:T(8,128)(2,1)S(1)} %get-tuple-element.143), channel_id=1, source_target_pairs={{0,8},{1,9},{2,10},{3,11},{4,12},{5,13},{6,14},{7,15},{8,0},{9,1},... | collective-permute-start | bytes 294920 | tf_op jit(solution)/shard_map/ppermute | solution.py:493
  88.5 13.5 %collective-permute-start.18 = (bf16[4,64,512]{2,1,0:T(8,128)(2,1)S(1)}, bf16[4,64,512]{2,1,0:T(8,128)(2,1)S(1)}, u32[]{:S(2)}, u32[]{:S(2)}) collective-permute-start(bf16[4,64,512]{2,1,0:T(8,128)(2,1)S(1)} %get-tuple-element.146), channel_id=1, source_target_pairs={{0,4},{1,5},{2,6},{3,7},{4,0},{5,1},{6,2},{7,3},{8,12},{9,13},{10,... | collective-permute-start | bytes 786440 | tf_op jit(solution)/shard_map/ppermute | solution.py:493
  88.6 7.5 %collective-permute-start.15 = (bf16[3,32,512]{2,1,0:T(8,128)(2,1)S(1)}, bf16[3,32,512]{2,1,0:T(8,128)(2,1)S(1)}, u32[]{:S(2)}, u32[]{:S(2)}) collective-permute-start(bf16[3,32,512]{2,1,0:T(8,128)(2,1)S(1)} %shard_map.185.refs_3_.refs_1_), channel_id=1, source_target_pairs={{0,8},{1,9},{2,10},{3,11},{4,12},{5,13},{6,14},{7,15},{8,0},{9,1},... | collective-permute-start | bytes 294920 | tf_op jit(solution)/shard_map/ppermute | solution.py:493
  90.3 11.8 %collective-permute-start.20 = (bf16[128,512]{1,0:T(8,128)(2,1)S(1)}, bf16[128,512]{1,0:T(8,128)(2,1)S(1)}, u32[]{:S(2)}, u32[]{:S(2)}) collective-permute-start(bf16[128,512]{1,0:T(8,128)(2,1)S(1)} %get-tuple-element.114.refs_13_.refs_8_), channel_id=1, source_target_pairs={{1,0},{2,1},{3,2},{4,3},{5,4},{6,5},{7,6},{8,7},{9,8},{10,9},{11,1... | collective-permute-start | bytes 393224 | tf_op jit(solution)/shard_map/ppermute | solution.py:22
  96.1 16.0 %collective-permute-start.17 = (bf16[3,64,512]{2,1,0:T(8,128)(2,1)S(1)}, bf16[3,64,512]{2,1,0:T(8,128)(2,1)S(1)}, u32[]{:S(2)}, u32[]{:S(2)}) collective-permute-start(bf16[3,64,512]{2,1,0:T(8,128)(2,1)S(1)} %shard_map.187.refs_3_.refs_1_), channel_id=1, source_target_pairs={{0,4},{1,5},{2,6},{3,7},{4,0},{5,1},{6,2},{7,3},{8,12},{9,13},{10,... | collective-permute-start | bytes 589832 | tf_op jit(solution)/shard_map/ppermute | solution.py:493
  98.3 8.4 %collective-permute-start.21 = (bf16[128,512]{1,0:T(8,128)(2,1)S(1)}, bf16[128,512]{1,0:T(8,128)(2,1)S(1)}, u32[]{:S(2)}, u32[]{:S(2)}) collective-permute-start(bf16[128,512]{1,0:T(8,128)(2,1)S(1)} %get-tuple-element.115.refs_14_.refs_9_), channel_id=1, source_target_pairs={{15,0},{0,1},{1,2},{2,3},{3,4},{4,5},{5,6},{6,7},{7,8},{8,9},{9,10... | collective-permute-start | bytes 393224 | tf_op jit(solution)/shard_map/ppermute | solution.py:22
  98.3 8.4 %collective-permute-start.22 = (bf16[128,512]{1,0:T(8,128)(2,1)S(1)}, bf16[128,512]{1,0:T(8,128)(2,1)S(1)}, u32[]{:S(2)}, u32[]{:S(2)}) collective-permute-start(bf16[128,512]{1,0:T(8,128)(2,1)S(1)} %get-tuple-element.116.refs_15_.refs_10_), channel_id=1, source_target_pairs={{2,0},{3,1},{4,2},{5,3},{6,4},{7,5},{8,6},{9,7},{10,8},{11,9},{12,... | collective-permute-start | bytes 393224 | tf_op jit(solution)/shard_map/ppermute | solution.py:22
  102.0 9.2 %collective-permute-start.23 = (bf16[128,512]{1,0:T(8,128)(2,1)S(1)}, bf16[128,512]{1,0:T(8,128)(2,1)S(1)}, u32[]{:S(2)}, u32[]{:S(2)}) collective-permute-start(bf16[128,512]{1,0:T(8,128)(2,1)S(1)} %get-tuple-element.117.refs_16_.refs_11_), channel_id=1, source_target_pairs={{14,0},{15,1},{0,2},{1,3},{2,4},{3,5},{4,6},{5,7},{6,8},{7,9},{8,1... | collective-permute-start | bytes 393224 | tf_op jit(solution)/shard_map/ppermute | solution.py:22
  102.1 10.0 %collective-permute-start.19 = (bf16[4,32,512]{2,1,0:T(8,128)(2,1)S(1)}, bf16[4,32,512]{2,1,0:T(8,128)(2,1)S(1)}, u32[]{:S(2)}, u32[]{:S(2)}) collective-permute-start(bf16[4,32,512]{2,1,0:T(8,128)(2,1)S(1)} %get-tuple-element.148), channel_id=1, source_target_pairs={{0,8},{1,9},{2,10},{3,11},{4,12},{5,13},{6,14},{7,15},{8,0},{9,1},... | collective-permute-start | bytes 393224 | tf_op jit(solution)/shard_map/ppermute | solution.py:493
  112.2 12.2 %collective-permute-start.26 = (bf16[3,128,512]{2,1,0:T(8,128)(2,1)S(1)}, bf16[3,128,512]{2,1,0:T(8,128)(2,1)S(1)}, u32[]{:S(2)}, u32[]{:S(2)}) collective-permute-start(bf16[3,128,512]{2,1,0:T(8,128)(2,1)S(1)} %shard_map.190.refs_5_.refs_1_), channel_id=1, source_target_pairs={{0,2},{1,3},{2,0},{3,1},{4,6},{5,7},{6,4},{7,5},{8,10},{9,11},{10,... | collective-permute-start | bytes 1179656 | tf_op jit(solution)/shard_map/ppermute | solution.py:493
  115.5 11.1 %collective-permute-start.24 = (bf16[4,32,512]{2,1,0:T(8,128)(2,1)S(1)}, bf16[4,32,512]{2,1,0:T(8,128)(2,1)S(1)}, u32[]{:S(2)}, u32[]{:S(2)}) collective-permute-start(bf16[4,32,512]{2,1,0:T(8,128)(2,1)S(1)} %shard_map.189.refs_3_.refs_1_), channel_id=1, source_target_pairs={{0,8},{1,9},{2,10},{3,11},{4,12},{5,13},{6,14},{7,15},{8,0},{9,1},... | collective-permute-start | bytes 393224 | tf_op jit(solution)/shard_map/ppermute | solution.py:493
  115.5 11.2 %collective-permute-start.27 = (bf16[3,128,512]{2,1,0:T(8,128)(2,1)S(1)}, bf16[3,128,512]{2,1,0:T(8,128)(2,1)S(1)}, u32[]{:S(2)}, u32[]{:S(2)}) collective-permute-start(bf16[3,128,512]{2,1,0:T(8,128)(2,1)S(1)} %shard_map.190.refs_5_.refs_1_), channel_id=1, source_target_pairs={{0,1},{1,0},{2,3},{3,2},{4,5},{5,4},{6,7},{7,6},{8,9},{9,8},{10,11... | collective-permute-start | bytes 1179656 | tf_op jit(solution)/shard_map/ppermute | solution.py:493
  124.4 2.3 %collective-permute-start.28 = (bf16[3,128,512]{2,1,0:T(8,128)(2,1)S(1)}, bf16[3,128,512]{2,1,0:T(8,128)(2,1)S(1)}, u32[]{:S(2)}, u32[]{:S(2)}) collective-permute-start(bf16[3,128,512]{2,1,0:T(8,128)(2,1)S(1)} %collective-permute-done.26.refs_2_), channel_id=1, source_target_pairs={{0,1},{1,0},{2,3},{3,2},{4,5},{5,4},{6,7},{7,6},{8,9},{9,8},{10,11... | collective-permute-start | bytes 1179656 | tf_op jit(solution)/shard_map/ppermute | solution.py:493
  126.7 8.8 %collective-permute-start.25 = (bf16[4,64,512]{2,1,0:T(8,128)(2,1)S(1)}, bf16[4,64,512]{2,1,0:T(8,128)(2,1)S(1)}, u32[]{:S(2)}, u32[]{:S(2)}) collective-permute-start(bf16[4,64,512]{2,1,0:T(8,128)(2,1)S(1)} %shard_map.193.refs_5_.refs_1_), channel_id=1, source_target_pairs={{0,4},{1,5},{2,6},{3,7},{4,0},{5,1},{6,2},{7,3},{8,12},{9,13},{10,... | collective-permute-start | bytes 786440 | tf_op jit(solution)/shard_map/ppermute | solution.py:493
  135.5 13.6 %collective-permute-start.29 = (bf16[4,128,512]{2,1,0:T(8,128)(2,1)S(1)}, bf16[4,128,512]{2,1,0:T(8,128)(2,1)S(1)}, u32[]{:S(2)}, u32[]{:S(2)}) collective-permute-start(bf16[4,128,512]{2,1,0:T(8,128)(2,1)S(1)} %shard_map.195.refs_1_), channel_id=1, source_target_pairs={{0,2},{1,3},{2,0},{3,1},{4,6},{5,7},{6,4},{7,5},{8,10},{9,11},{10,... | collective-permute-start | bytes 1572872 | tf_op jit(solution)/shard_map/ppermute | solution.py:493
  137.3 11.8 %collective-permute-start.30 = (bf16[4,128,512]{2,1,0:T(8,128)(2,1)S(1)}, bf16[4,128,512]{2,1,0:T(8,128)(2,1)S(1)}, u32[]{:S(2)}, u32[]{:S(2)}) collective-permute-start(bf16[4,128,512]{2,1,0:T(8,128)(2,1)S(1)} %shard_map.195.refs_1_), channel_id=1, source_target_pairs={{0,1},{1,0},{2,3},{3,2},{4,5},{5,4},{6,7},{7,6},{8,9},{9,8},{10,11... | collective-permute-start | bytes 1572872 | tf_op jit(solution)/shard_map/ppermute | solution.py:493
  149.1 1.9 %collective-permute-start.31 = (bf16[4,128,512]{2,1,0:T(8,128)(2,1)S(1)}, bf16[4,128,512]{2,1,0:T(8,128)(2,1)S(1)}, u32[]{:S(2)}, u32[]{:S(2)}) collective-permute-start(bf16[4,128,512]{2,1,0:T(8,128)(2,1)S(1)} %collective-permute-done.29.refs_2_), channel_id=1, source_target_pairs={{0,1},{1,0},{2,3},{3,2},{4,5},{5,4},{6,7},{7,6},{8,9},{9,8},{10,11... | collective-permute-start | bytes 1572872 | tf_op jit(solution)/shard_map/ppermute | solution.py:493

commit v14 on v13

--- a/solution.py
+++ b/solution.py
@@ -493,7 +493,7 @@
     return lax.ppermute(block, axis, route)
 
 
-def add_stage(me, keep, arrived, stride, after, members=2, kind=f32):
+def add_stage(me, keep, arrived, stride, after, members=2, kind=f32, work=1):
     count, rows, width = keep.shape
     shape = (count, rows // members, width)
     outs = call(
@@ -505,6 +505,7 @@
         *arrived,
         smem=(0,),
         after=after,
+        work=work,
     )
     return outs[0], [in_group(out, "band", stride, members, j + 1) for j, out in enumerate(outs[1:])]
 
@@ -537,9 +538,8 @@
     return mine
 
 
-def join_stage(me, mine, members, blocks, shapes, swap_after, after):
-    pieces = [in_group(mine, "band", 2, members, j) for j in range(1, members)]
-    pieces = [mine] + [held_until(piece, swap_after) if swap_after else piece for piece in pieces]
+def join_stage(me, piece, other, members, blocks, shapes):
+    pieces = [piece, other]
     others = [in_group(one, "band", 1, 2, 1) for one in pieces]
     return call(
         functools.partial(join_kernel, (members, blocks)),
@@ -549,7 +549,6 @@
         *pieces,
         *others,
         smem=(0,),
-        after=after,
         last=range(len(shapes)),
     )
 
@@ -847,19 +846,20 @@
         keep_node, came_node = add_stage(me, keep_node, came_node, 4, [in_hbm(edge_new)])
         keep_edge, came_edge = add_stage(me, keep_edge, came_edge, 2, [keep_node])
         keep_node, came_node = add_stage(me, keep_node, came_node, 8, [keep_edge])
-        piece_node, _ = add_stage(me, keep_node, came_node, 1, [], 1, bf16)
-        keep_edge, came_edge = add_stage(me, keep_edge, came_edge, 4, [piece_node])
+        keep_edge, came_edge = add_stage(me, keep_edge, came_edge, 4, [keep_node])
+        piece_node, _ = add_stage(me, keep_node, came_node, 1, [keep_edge], 1, bf16)
+        keep_edge, came_edge = add_stage(me, keep_edge, came_edge, 8, [piece_node])
         piece_node = gather_stage(me, piece_node, over(piece_node, 8), 8, [keep_edge])
-        keep_edge, came_edge = add_stage(me, keep_edge, came_edge, 8, [piece_node])
-        piece_edge, _ = add_stage(me, keep_edge, came_edge, 1, back_near, 1, bf16)
+        piece_edge, _ = add_stage(me, keep_edge, came_edge, 1, [], 1, bf16)
+        grad_nodes = node_output([piece_edge])
+        piece_edge = gather_stage(me, piece_edge, over(piece_edge, 8), 8, [in_hbm(grad_nodes)])
         piece_node = gather_stage(me, piece_node, over(piece_node, 4), 4, [piece_edge])
-        grad_nodes = node_output([piece_node])
-        piece_edge = gather_stage(me, piece_edge, over(piece_edge, 8), 8, [in_hbm(grad_nodes)])
-        grad_n1, grad_n2 = join_stage(
-            me, piece_node, first, node_blocks, node_shapes, [], [piece_edge]
-        )
-        piece_edge = gather_stage(me, piece_edge, over(piece_edge, 4), 4, [in_hbm(grad_n2)])
-        grad_e1, grad_e2 = join_stage(me, piece_edge, first, edge_blocks, edge_shapes, [], [])
+        other_node = over(piece_node, 2)
+        piece_edge = gather_stage(me, piece_edge, over(piece_edge, 4), 4, [other_node])
+        other_node = held_until(other_node, [piece_edge])
+        grad_n1, grad_n2 = join_stage(me, piece_node, other_node, first, node_blocks, node_shapes)
+        other_edge = held_until(over(piece_edge, 2), [in_hbm(grad_n2)])
+        grad_e1, grad_e2 = join_stage(me, piece_edge, other_edge, first, edge_blocks, edge_shapes)
     else:
         whole = reduce_whole(*node_weights([]))
         grad_n1, grad_n2 = whole[:2].reshape(2 * width, width), whole[2]

time: 153 us -> 151 us (0.987)
  waiting for transfers between devices: 71.5 us -> 66.9 us
  starting transfers between devices: 35.4 us -> 38.6 us
    ppermute x18, starting transfers between devices: 18.7 us -> 23.3 us  [in_group(): return lax.ppermute(block, axis, route)]
    ppermute x14, waiting for transfers between devices: 23.7 us -> 19.8 us  [passed_along(): return lax.ppermute(block, axis, route)]
  transfers between devices with their start and end apart: 32 -> 32, of which waited for: 16 -> 19; matrix products, arithmetic and copies ran while one was open for 0% -> 0% of each run, Pallas kernels for 13% -> 13%
where the time goes in v14:
time: 151 us
  waiting for transfers between devices  66.9 us (44%)
  starting transfers between devices  38.6 us (26%)
  Pallas kernels  31 us (21%)
  blocking collectives  13.7 us (9%)
    ppermute x18, waiting for transfers between devices, in_group(): return lax.ppermute(block, axis, route)  47 us
    pallas_call x25, Pallas kernels, call(): pl.pallas_call(kernel, out_shape=[(pltpu.HBM if i in last else pltpu.VMEM...  27.8 us
    ppermute x18, starting transfers between devices, in_group(): return lax.ppermute(block, axis, route)  23.3 us
    ppermute x14, waiting for transfers between devices, passed_along(): return lax.ppermute(block, axis, route)  19.8 us
    ppermute x14, starting transfers between devices, passed_along(): return lax.ppermute(block, axis, route)  15.3 us
    all_to_all x1, blocking collectives, local(): ids = lax.all_to_all(ids, 'band', 0, 0, tiled=True)  13.7 us
    pallas_call x1, Pallas kernels, loaded(): pl.pallas_call(functools.partial(load_kernel, count), out_shape=[pltpu.VM...  3.24 us
  transfers between devices with their start and end apart: 32, of which 19 were waited for; matrix products, arithmetic and copies ran while one was open for 0% of the time, Pallas kernels for 13%

profile of v14, /device:TPU:0, one launch (start us, length us, event | category | flops | bytes accessed | tf_op | source)
XLA Modules:
  0.0 151.0 jit_solution(5597026872906177563)
XLA Ops:
  0.6 3.2 %shard_map.170 = (bf16[320,512]{1,0:T(8,128)(2,1)S(1)}, s32[11,1,128]{2,1,0:T(1,128)S(1)}, s32[11,1,128]{2,1,0:T(1,128)S(1)}, bf16[11,128,512]{2,1,0:T(8,128)(2,...) custom-call(s32[1]{0:T(128)} %bitcast.refs_0_.refs_2_, ...), custom_call_target="tpu_custom_call" | custom-call | flops 1 | bytes 1 | tf_op jit(solution)/shard_map/pallas_call | solution.py:121
  3.9 13.7 %all_to_all.5.refs_2_.refs_4_ = s32[16,1,256]{2,1,0:T(1,128)S(1)} all-to-all(s32[16,1,256]{2,1,0:T(1,128)S(1)} %shard_map.171), channel_id=1, replica_groups=mesh['groups'=2,'band'=16] {'band'}, dimensions={0} | all-to-all | bytes 32768 | tf_op jit(solution)/shard_map/all_to_all | solution.py:638
  17.6 0.8 shard_map.172
  18.6 1.2 collective-permute-start.2
  19.8 0.8 collective-permute-start.6
  20.6 3.3 %collective-permute-start.3 = (bf16[128,512]{1,0:T(8,128)(2,1)S(1)}, bf16[128,512]{1,0:T(8,128)(2,1)S(1)}, u32[]{:S(2)}, u32[]{:S(2)}) collective-permute-start(bf16[128,512]{1,0:T(8,128)(2,1)S(1)} %get-tuple-element.96), channel_id=1, source_target_pairs={{2,0},{3,1},{4,2},{5,3},{6,4},{7,5},{8,6},{9,7},{10,8},{11,9},{12,... | collective-permute-start | bytes 393224 | tf_op jit(solution)/shard_map/ppermute | solution.py:22
  23.9 3.8 %collective-permute-done.2.refs_8_.refs_7_ = bf16[128,512]{1,0:T(8,128)(2,1)S(1)} collective-permute-done((bf16[128,512]{1,0:T(8,128)(2,1)S(1)}, bf16[128,512]{1,0:T(8,128)(2,1)S(1)}, u32[]{:S(2)}, u32[]{:S(2)}) %collective-permute-start.2) | collective-permute-done | bytes 131104 | tf_op jit(solution)/shard_map/ppermute | solution.py:22
  27.8 4.5 %shard_map.173 = (bf16[1408,320]{1,0:T(8,128)(2,1)S(1)}, bf16[320,1408]{1,0:T(8,128)(2,1)S(1)}, f32[1408,128]{1,0:T(8,128)S(1)}, f32[1024,512]{1,0:T(8,128)S(1)}...) custom-call(bf16[11,128,512]{2,1,0:T(8,128)(2,1)S(1)} %get-tuple-ele, ...), custom_call_target="tpu_custom_call" | custom-call | flops 1 | bytes 1 | tf_op jit(solution)/shard_map/pallas_call | solution.py:90
  32.3 2.7 %collective-permute-done.refs_6_.refs_5_ = bf16[128,512]{1,0:T(8,128)(2,1)S(1)} collective-permute-done((bf16[128,512]{1,0:T(8,128)(2,1)S(1)}, bf16[128,512]{1,0:T(8,128)(2,1)S(1)}, u32[]{:S(2)}, u32[]{:S(2)}) %collective-permute-start) | collective-permute-done | bytes 131104 | tf_op jit(solution)/shard_map/ppermute | solution.py:22
  35.0 1.6 %shard_map.174 = (bf16[512,512]{1,0:T(8,128)(2,1)S(1)}, f32[512,512]{1,0:T(8,128)S(1)}, f32[512,512]{1,0:T(8,128)S(1)}, f32[512,128]{1,0:T(8,128)S(1)}, f32[320,512]{1,0:T(8,128)S(1)}) custom-call(f32[1024,512]{1,0:T(8,128)S(1)} %get-tuple-element.89.refs_0_.refs_1_, f32[1408,128]{1,0:T(8,128)S(1)} %get-tuple-element.90.refs_1_.refs_2_.refs_3_, ...), custom_call_target="tpu_custom_call" | custom-call | flops 1 | bytes 1 | tf_op jit(solution)/shard_map/pallas_call | solution.py:90
  36.6 2.8 %collective-permute-done.5.refs_13_.refs_10_ = bf16[128,512]{1,0:T(8,128)(2,1)S(1)} collective-permute-done((bf16[128,512]{1,0:T(8,128)(2,1)S(1)}, bf16[128,512]{1,0:T(8,128)(2,1)S(1)}, u32[]{:S(2)}, u32[]{:S(2)}) %collective-permute-start.5) | collective-permute-done | bytes 131104 | tf_op jit(solution)/shard_map/ppermute | solution.py:22
  39.4 4.5 %shard_map.175 = (bf16[128,512]{1,0:T(8,128)(2,1)S(1)}, bf16[128,512]{1,0:T(8,128)(2,1)S(1)}, bf16[256,512]{1,0:T(8,128)(2,1)S(1)}, bf16[512,512]{1,0:T(8,128)(2...) custom-call(bf16[11,128,512]{2,1,0:T(8,128)(2,1)S(1)} %get-tuple-ele, ...), custom_call_target="tpu_custom_call" | custom-call | flops 1 | bytes 1 | tf_op jit(solution)/shard_map/pallas_call | solution.py:90
  43.9 1.3 shard_map.178
  45.3 4.7 %collective-permute-start.9 = (bf16[256,512]{1,0:T(8,128)(2,1)S(1)}, bf16[256,512]{1,0:T(8,128)(2,1)S(1)}, u32[]{:S(2)}, u32[]{:S(2)}) collective-permute-start(bf16[256,512]{1,0:T(8,128)(2,1)S(1)} %get-tuple-element.120.refs_19_.refs_14_), channel_id=1, source_target_pairs={{8,0},{9,1},{10,2},{11,3},{12,4},{13,5},{14,6},{15,7},{0,8},{1,9},... | collective-permute-start | bytes 786440 | tf_op jit(solution)/shard_map/ppermute | solution.py:22
  50.0 1.7 %collective-permute-start.7 = (bf16[128,512]{1,0:T(8,128)(2,1)S(1)}, bf16[128,512]{1,0:T(8,128)(2,1)S(1)}, u32[]{:S(2)}, u32[]{:S(2)}) collective-permute-start(bf16[128,512]{1,0:T(8,128)(2,1)S(1)} %get-tuple-element.118.refs_17_.refs_12_), channel_id=1, source_target_pairs={{4,0},{5,1},{6,2},{7,3},{8,4},{9,5},{10,6},{11,7},{12,8},{13,9},{1... | collective-permute-start | bytes 393224 | tf_op jit(solution)/shard_map/ppermute | solution.py:22
  51.7 0.4 collective-permute-start.8
  52.0 2.1 %shard_map.176 = (bf16[896,512]{1,0:T(8,128)(2,1)S(1)}, bf16[384,512]{1,0:T(8,128)(2,1)S(1)}, bf16[128,512]{1,0:T(8,128)(2,1)S(1)}, bf16[128,512]{1,0:T(8,128)(2...) custom-call(bf16[11,128,512]{2,1,0:T(8,128)(2,1)S(1)} %get-tuple-element.81.refs_0_.refs_1_, ...), custom_call_target="tpu_custom_call" | custom-call | flops 1 | bytes 1 | tf_op jit(solution)/shard_map/pallas_call | solution.py:90
  54.1 3.9 %shard_map.177 = (f32[4,256,512]{2,1,0:T(8,128)S(1)}, bf16[4,256,512]{2,1,0:T(8,128)(2,1)S(1)}, bf16[320,512]{1,0:T(8,128)(2,1)S(1)}) custom-call(bf16[11,128,512]{2,1,0:T(8,128)(2,1)S(1)} %get-tuple-element.82.refs_0_, bf16[320,1408]{1,0:T(8,128)(2,1)S(1)} %get-tuple-element.92.refs_2_.refs_4_.refs_1_, s32[1]{0:T(128)} %bitcast.refs_0_.refs_2_, ...), custom_call_target="tpu_custom_call" | custom-call | flops 1 | bytes 1 | tf_op jit(solution)/shard_map/pallas_call | solution.py:90
  58.1 2.1 %collective-permute-start.12 = (bf16[3,128,512]{2,1,0:T(8,128)(2,1)S(1)}, bf16[3,128,512]{2,1,0:T(8,128)(2,1)S(1)}, u32[]{:S(2)}, u32[]{:S(2)}) collective-permute-start(bf16[3,128,512]{2,1,0:T(8,128)(2,1)S(1)} %get-tuple-element.138), channel_id=1, source_target_pairs={{0,2},{1,3},{2,0},{3,1},{4,6},{5,7},{6,4},{7,5},{8,10},{9,11},{10,... | collective-permute-start | bytes 1179656 | tf_op jit(solution)/shard_map/ppermute | solution.py:493
  60.3 3.8 %collective-permute-done.8.refs_2_.refs_11_ = bf16[128,512]{1,0:T(8,128)(2,1)S(1)} collective-permute-done((bf16[128,512]{1,0:T(8,128)(2,1)S(1)}, bf16[128,512]{1,0:T(8,128)(2,1)S(1)}, u32[]{:S(2)}, u32[]{:S(2)}) %collective-permute-start.8) | collective-permute-done | bytes 131104 | tf_op jit(solution)/shard_map/ppermute | solution.py:22
  64.0 1.5 %collective-permute-done.9.refs_3_.refs_12_ = bf16[256,512]{1,0:T(8,128)(2,1)S(1)} collective-permute-done((bf16[256,512]{1,0:T(8,128)(2,1)S(1)}, bf16[256,512]{1,0:T(8,128)(2,1)S(1)}, u32[]{:S(2)}, u32[]{:S(2)}) %collective-permute-start.9) | collective-permute-done | bytes 262176 | tf_op jit(solution)/shard_map/ppermute | solution.py:22
  65.6 3.5 %shard_map.181 = (bf16[11,128,512]{2,1,0:T(8,128)(2,1)}, bf16[11,128,512]{2,1,0:T(8,128)(2,1)}) custom-call(bf16[11,128,512]{2,1,0:T(8,128)(2,1)S(1)} %get-tuple-element.82.refs_0_, bf16[11,128,512]{2,1,0:T(8,128)(2,1)S(1)} %get-tuple-element.81.refs_0_.refs_1_, bf16[1536,512]{1,0:T(8,128)(2,1)S(1)} %get-tuple-element.85.refs_4_.refs_6_.refs_2_.refs_3_, ...), custom_call_target="tpu_custom_call" | custom-call | flops 20000000000 | bytes 1 | tf_op jit(solution)/shard_map/pallas_call | solution.py:90
  69.1 0.3 collective-permute-done.12.refs_2_
  69.7 2.9 %collective-permute-start.13 = (bf16[4,128,512]{2,1,0:T(8,128)(2,1)S(1)}, bf16[4,128,512]{2,1,0:T(8,128)(2,1)S(1)}, u32[]{:S(2)}, u32[]{:S(2)}) collective-permute-start(bf16[4,128,512]{2,1,0:T(8,128)(2,1)S(1)} %get-tuple-element.141), channel_id=1, source_target_pairs={{0,2},{1,3},{2,0},{3,1},{4,6},{5,7},{6,4},{7,5},{8,10},{9,11},{10,... | collective-permute-start | bytes 1572872 | tf_op jit(solution)/shard_map/ppermute | solution.py:493
  72.6 3.0 %collective-permute-start.14 = (bf16[3,64,512]{2,1,0:T(8,128)(2,1)S(1)}, bf16[3,64,512]{2,1,0:T(8,128)(2,1)S(1)}, u32[]{:S(2)}, u32[]{:S(2)}) collective-permute-start(bf16[3,64,512]{2,1,0:T(8,128)(2,1)S(1)} %get-tuple-element.142), channel_id=1, source_target_pairs={{0,4},{1,5},{2,6},{3,7},{4,0},{5,1},{6,2},{7,3},{8,12},{9,13},{10,... | collective-permute-start | bytes 589832 | tf_op jit(solution)/shard_map/ppermute | solution.py:493
  75.6 5.3 %collective-permute-done.14.refs_2_ = bf16[3,64,512]{2,1,0:T(8,128)(2,1)S(1)} collective-permute-done((bf16[3,64,512]{2,1,0:T(8,128)(2,1)S(1)}, bf16[3,64,512]{2,1,0:T(8,128)(2,1)S(1)}, u32[]{:S(2)}, u32[]{:S(2)}) %collective-permute-start.14) | collective-permute-done | bytes 196640 | tf_op jit(solution)/shard_map/ppermute | solution.py:493
  80.9 4.3 %collective-permute-done.13.refs_2_ = bf16[4,128,512]{2,1,0:T(8,128)(2,1)S(1)} collective-permute-done((bf16[4,128,512]{2,1,0:T(8,128)(2,1)S(1)}, bf16[4,128,512]{2,1,0:T(8,128)(2,1)S(1)}, u32[]{:S(2)}, u32[]{:S(2)}) %collective-permute-start.13) | collective-permute-done | bytes 524320 | tf_op jit(solution)/shard_map/ppermute | solution.py:493
  85.3 3.0 %collective-permute-start.15 = (bf16[4,64,512]{2,1,0:T(8,128)(2,1)S(1)}, bf16[4,64,512]{2,1,0:T(8,128)(2,1)S(1)}, u32[]{:S(2)}, u32[]{:S(2)}) collective-permute-start(bf16[4,64,512]{2,1,0:T(8,128)(2,1)S(1)} %get-tuple-element.145), channel_id=1, source_target_pairs={{0,4},{1,5},{2,6},{3,7},{4,0},{5,1},{6,2},{7,3},{8,12},{9,13},{10,... | collective-permute-start | bytes 786440 | tf_op jit(solution)/shard_map/ppermute | solution.py:493
  88.3 7.8 %collective-permute-done.16.refs_2_ = bf16[3,32,512]{2,1,0:T(8,128)(2,1)S(1)} collective-permute-done((bf16[3,32,512]{2,1,0:T(8,128)(2,1)S(1)}, bf16[3,32,512]{2,1,0:T(8,128)(2,1)S(1)}, u32[]{:S(2)}, u32[]{:S(2)}) %collective-permute-start.16) | collective-permute-done | bytes 98336 | tf_op jit(solution)/shard_map/ppermute | solution.py:493
  96.1 3.5 %collective-permute-start.24 = (bf16[3,32,512]{2,1,0:T(8,128)(2,1)S(1)}, bf16[3,32,512]{2,1,0:T(8,128)(2,1)S(1)}, u32[]{:S(2)}, u32[]{:S(2)}) collective-permute-start(bf16[3,32,512]{2,1,0:T(8,128)(2,1)S(1)} %shard_map.186.refs_3_.refs_1_), channel_id=1, source_target_pairs={{0,8},{1,9},{2,10},{3,11},{4,12},{5,13},{6,14},{7,15},{8,0},{9,1},... | collective-permute-start | bytes 294920 | tf_op jit(solution)/shard_map/ppermute | solution.py:493
  99.8 7.4 %collective-permute-done.24.refs_2_ = bf16[3,32,512]{2,1,0:T(8,128)(2,1)S(1)} collective-permute-done((bf16[3,32,512]{2,1,0:T(8,128)(2,1)S(1)}, bf16[3,32,512]{2,1,0:T(8,128)(2,1)S(1)}, u32[]{:S(2)}, u32[]{:S(2)}) %collective-permute-start.24) | collective-permute-done | bytes 98336 | tf_op jit(solution)/shard_map/ppermute | solution.py:493
  107.4 2.8 %collective-permute-start.20 = (bf16[128,512]{1,0:T(8,128)(2,1)S(1)}, bf16[128,512]{1,0:T(8,128)(2,1)S(1)}, u32[]{:S(2)}, u32[]{:S(2)}) collective-permute-start(bf16[128,512]{1,0:T(8,128)(2,1)S(1)} %get-tuple-element.116.refs_15_.refs_10_), channel_id=1, source_target_pairs={{2,0},{3,1},{4,2},{5,3},{6,4},{7,5},{8,6},{9,7},{10,8},{11,9},{12,... | collective-permute-start | bytes 393224 | tf_op jit(solution)/shard_map/ppermute | solution.py:22
  110.5 2.5 %collective-permute-start.22 = (bf16[4,32,512]{2,1,0:T(8,128)(2,1)S(1)}, bf16[4,32,512]{2,1,0:T(8,128)(2,1)S(1)}, u32[]{:S(2)}, u32[]{:S(2)}) collective-permute-start(bf16[4,32,512]{2,1,0:T(8,128)(2,1)S(1)} %shard_map.188.refs_5_.refs_1_), channel_id=1, source_target_pairs={{0,8},{1,9},{2,10},{3,11},{4,12},{5,13},{6,14},{7,15},{8,0},{9,1},... | collective-permute-start | bytes 393224 | tf_op jit(solution)/shard_map/ppermute | solution.py:493
  112.9 0.5 shard_map.189.refs_1_
  113.5 1.8 %collective-permute-done.19.refs_7_ = bf16[128,512]{1,0:T(8,128)(2,1)S(1)} collective-permute-done((bf16[128,512]{1,0:T(8,128)(2,1)S(1)}, bf16[128,512]{1,0:T(8,128)(2,1)S(1)}, u32[]{:S(2)}, u32[]{:S(2)}) %collective-permute-start.19) | collective-permute-done | bytes 131104 | tf_op jit(solution)/shard_map/ppermute | solution.py:22
  115.2 3.4 %collective-permute-done.21.refs_9_ = bf16[128,512]{1,0:T(8,128)(2,1)S(1)} collective-permute-done((bf16[128,512]{1,0:T(8,128)(2,1)S(1)}, bf16[128,512]{1,0:T(8,128)(2,1)S(1)}, u32[]{:S(2)}, u32[]{:S(2)}) %collective-permute-start.21) | collective-permute-done | bytes 131104 | tf_op jit(solution)/shard_map/ppermute | solution.py:22
  118.6 1.6 %shard_map.190.refs_3_ = bf16[320,512]{1,0:T(8,128)(2,1)} custom-call(s32[1]{0:T(128)} %bitcast.refs_0_.refs_2_, f32[320,512]{1,0:T(8,128)S(1)} %shard_map.189.refs_1_, bf16[1536,512]{1,0:T(8,128)(2,1)S(1)} %get-tuple-element.85.refs_4_.refs_6_.refs_2_.refs_3_, s32[11,1,128]{2,1,0:T(1,128)S(1)} %get-tuple-element.84.refs_1_.refs_2_.refs_3_, ...), custom_call_target="tpu_custom_call" | custom-call | flops 1 | bytes 1 | tf_op jit(solution)/shard_map/pallas_call | solution.py:90
  120.6 3.6 %collective-permute-start.26 = (bf16[3,128,512]{2,1,0:T(8,128)(2,1)S(1)}, bf16[3,128,512]{2,1,0:T(8,128)(2,1)S(1)}, u32[]{:S(2)}, u32[]{:S(2)}) collective-permute-start(bf16[3,128,512]{2,1,0:T(8,128)(2,1)S(1)} %shard_map.193.refs_1_), channel_id=1, source_target_pairs={{0,2},{1,3},{2,0},{3,1},{4,6},{5,7},{6,4},{7,5},{8,10},{9,11},{10,... | collective-permute-start | bytes 1179656 | tf_op jit(solution)/shard_map/ppermute | solution.py:493
  124.2 8.4 %collective-permute-done.23.refs_2_ = bf16[4,64,512]{2,1,0:T(8,128)(2,1)S(1)} collective-permute-done((bf16[4,64,512]{2,1,0:T(8,128)(2,1)S(1)}, bf16[4,64,512]{2,1,0:T(8,128)(2,1)S(1)}, u32[]{:S(2)}, u32[]{:S(2)}) %collective-permute-start.23) | collective-permute-done | bytes 262176 | tf_op jit(solution)/shard_map/ppermute | solution.py:493
  132.6 1.3 collective-permute-done.26.refs_3_.refs_0_
  133.9 1.8 %collective-permute-start.27 = (bf16[4,128,512]{2,1,0:T(8,128)(2,1)S(1)}, bf16[4,128,512]{2,1,0:T(8,128)(2,1)S(1)}, u32[]{:S(2)}, u32[]{:S(2)}) collective-permute-start(bf16[4,128,512]{2,1,0:T(8,128)(2,1)S(1)} %shard_map.194.refs_1_), channel_id=1, source_target_pairs={{0,2},{1,3},{2,0},{3,1},{4,6},{5,7},{6,4},{7,5},{8,10},{9,11},{10,... | collective-permute-start | bytes 1572872 | tf_op jit(solution)/shard_map/ppermute | solution.py:493
  135.8 0.5 collective-permute-start.29
  136.3 1.2 collective-permute-done.28.refs_3_
  137.5 0.6 collective-permute-done.29.refs_4_
  138.1 1.3 shard_map.196
  139.3 8.3 %collective-permute-done.27.refs_0_ = bf16[4,128,512]{2,1,0:T(8,128)(2,1)S(1)} collective-permute-done((bf16[4,128,512]{2,1,0:T(8,128)(2,1)S(1)}, bf16[4,128,512]{2,1,0:T(8,128)(2,1)S(1)}, u32[]{:S(2)}, u32[]{:S(2)}) %collective-permute-start.27) | collective-permute-done | bytes 524320 | tf_op jit(solution)/shard_map/ppermute | solution.py:493
  147.7 1.9 %collective-permute-done.31.refs_4_ = bf16[4,128,512]{2,1,0:T(8,128)(2,1)S(1)} collective-permute-done((bf16[4,128,512]{2,1,0:T(8,128)(2,1)S(1)}, bf16[4,128,512]{2,1,0:T(8,128)(2,1)S(1)}, u32[]{:S(2)}, u32[]{:S(2)}) %collective-permute-start.31) | collective-permute-done | bytes 524320 | tf_op jit(solution)/shard_map/ppermute | solution.py:493
  149.6 1.5 shard_map.198
  (46 shorter events, 2.1 us)
Async XLA Ops:
  18.4 5.5 %collective-permute-start.1 = (bf16[128,512]{1,0:T(8,128)(2,1)S(1)}, bf16[128,512]{1,0:T(8,128)(2,1)S(1)}, u32[]{:S(2)}, u32[]{:S(2)}) collective-permute-start(bf16[128,512]{1,0:T(8,128)(2,1)S(1)} %get-tuple-element.94), channel_id=1, source_target_pairs={{1,0},{2,1},{3,2},{4,3},{5,4},{6,5},{7,6},{8,7},{9,8},{10,9},{11,1... | collective-permute-start | bytes 393224 | tf_op jit(solution)/shard_map/ppermute | solution.py:22
  18.6 9.1 %collective-permute-start.2 = (bf16[128,512]{1,0:T(8,128)(2,1)S(1)}, bf16[128,512]{1,0:T(8,128)(2,1)S(1)}, u32[]{:S(2)}, u32[]{:S(2)}) collective-permute-start(bf16[128,512]{1,0:T(8,128)(2,1)S(1)} %get-tuple-element.95), channel_id=1, source_target_pairs={{14,0},{15,1},{0,2},{1,3},{2,4},{3,5},{4,6},{5,7},{6,8},{7,9},{8,1... | collective-permute-start | bytes 393224 | tf_op jit(solution)/shard_map/ppermute | solution.py:22
  19.8 19.6 %collective-permute-start.6 = (bf16[256,512]{1,0:T(8,128)(2,1)S(1)}, bf16[256,512]{1,0:T(8,128)(2,1)S(1)}, u32[]{:S(2)}, u32[]{:S(2)}) collective-permute-start(bf16[256,512]{1,0:T(8,128)(2,1)S(1)} %get-tuple-element.103), channel_id=1, source_target_pairs={{8,0},{9,1},{10,2},{11,3},{12,4},{13,5},{14,6},{15,7},{0,8},{1,9},... | collective-permute-start | bytes 786440 | tf_op jit(solution)/shard_map/ppermute | solution.py:22
  20.6 11.6 %collective-permute-start.3 = (bf16[128,512]{1,0:T(8,128)(2,1)S(1)}, bf16[128,512]{1,0:T(8,128)(2,1)S(1)}, u32[]{:S(2)}, u32[]{:S(2)}) collective-permute-start(bf16[128,512]{1,0:T(8,128)(2,1)S(1)} %get-tuple-element.96), channel_id=1, source_target_pairs={{2,0},{3,1},{4,2},{5,3},{6,4},{7,5},{8,6},{9,7},{10,8},{11,9},{12,... | collective-permute-start | bytes 393224 | tf_op jit(solution)/shard_map/ppermute | solution.py:22
  23.9 11.1 %collective-permute-start = (bf16[128,512]{1,0:T(8,128)(2,1)S(1)}, bf16[128,512]{1,0:T(8,128)(2,1)S(1)}, u32[]{:S(2)}, u32[]{:S(2)}) collective-permute-start(bf16[128,512]{1,0:T(8,128)(2,1)S(1)} %get-tuple-element.88.refs_7_), channel_id=1, source_target_pairs={{15,0},{0,1},{1,2},{2,3},{3,4},{4,5},{5,6},{6,7},{7,8},{8,9},{9,10... | collective-permute-start | bytes 393224 | tf_op jit(solution)/shard_map/ppermute | solution.py:22
  23.9 12.7 %collective-permute-start.4 = (bf16[128,512]{1,0:T(8,128)(2,1)S(1)}, bf16[128,512]{1,0:T(8,128)(2,1)S(1)}, u32[]{:S(2)}, u32[]{:S(2)}) collective-permute-start(bf16[128,512]{1,0:T(8,128)(2,1)S(1)} %get-tuple-element.101), channel_id=1, source_target_pairs={{12,0},{13,1},{14,2},{15,3},{0,4},{1,5},{2,6},{3,7},{4,8},{5,9},{6... | collective-permute-start | bytes 393224 | tf_op jit(solution)/shard_map/ppermute | solution.py:22
  27.8 11.6 %collective-permute-start.5 = (bf16[128,512]{1,0:T(8,128)(2,1)S(1)}, bf16[128,512]{1,0:T(8,128)(2,1)S(1)}, u32[]{:S(2)}, u32[]{:S(2)}) collective-permute-start(bf16[128,512]{1,0:T(8,128)(2,1)S(1)} %get-tuple-element.102), channel_id=1, source_target_pairs={{4,0},{5,1},{6,2},{7,3},{8,4},{9,5},{10,6},{11,7},{12,8},{13,9},{1... | collective-permute-start | bytes 393224 | tf_op jit(solution)/shard_map/ppermute | solution.py:22
  45.2 12.8 %collective-permute-start.10 = (bf16[3,256,512]{2,1,0:T(8,128)(2,1)S(1)}, bf16[3,256,512]{2,1,0:T(8,128)(2,1)S(1)}, u32[]{:S(2)}, u32[]{:S(2)}) collective-permute-start(bf16[3,256,512]{2,1,0:T(8,128)(2,1)S(1)} %get-tuple-element.133), channel_id=1, source_target_pairs={{0,1},{1,0},{2,3},{3,2},{4,5},{5,4},{6,7},{7,6},{8,9},{9,8},{10,11... | collective-permute-start | bytes 2359304 | tf_op jit(solution)/shard_map/ppermute | solution.py:493
  45.3 20.3 %collective-permute-start.9 = (bf16[256,512]{1,0:T(8,128)(2,1)S(1)}, bf16[256,512]{1,0:T(8,128)(2,1)S(1)}, u32[]{:S(2)}, u32[]{:S(2)}) collective-permute-start(bf16[256,512]{1,0:T(8,128)(2,1)S(1)} %get-tuple-element.120.refs_19_.refs_14_), channel_id=1, source_target_pairs={{8,0},{9,1},{10,2},{11,3},{12,4},{13,5},{14,6},{15,7},{0,8},{1,9},... | collective-permute-start | bytes 786440 | tf_op jit(solution)/shard_map/ppermute | solution.py:22
  50.0 10.2 %collective-permute-start.7 = (bf16[128,512]{1,0:T(8,128)(2,1)S(1)}, bf16[128,512]{1,0:T(8,128)(2,1)S(1)}, u32[]{:S(2)}, u32[]{:S(2)}) collective-permute-start(bf16[128,512]{1,0:T(8,128)(2,1)S(1)} %get-tuple-element.118.refs_17_.refs_12_), channel_id=1, source_target_pairs={{4,0},{5,1},{6,2},{7,3},{8,4},{9,5},{10,6},{11,7},{12,8},{13,9},{1... | collective-permute-start | bytes 393224 | tf_op jit(solution)/shard_map/ppermute | solution.py:22
  51.7 12.4 %collective-permute-start.8 = (bf16[128,512]{1,0:T(8,128)(2,1)S(1)}, bf16[128,512]{1,0:T(8,128)(2,1)S(1)}, u32[]{:S(2)}, u32[]{:S(2)}) collective-permute-start(bf16[128,512]{1,0:T(8,128)(2,1)S(1)} %get-tuple-element.119.refs_18_.refs_13_), channel_id=1, source_target_pairs={{12,0},{13,1},{14,2},{15,3},{0,4},{1,5},{2,6},{3,7},{4,8},{5,9},{6... | collective-permute-start | bytes 393224 | tf_op jit(solution)/shard_map/ppermute | solution.py:22
  58.1 11.3 %collective-permute-start.12 = (bf16[3,128,512]{2,1,0:T(8,128)(2,1)S(1)}, bf16[3,128,512]{2,1,0:T(8,128)(2,1)S(1)}, u32[]{:S(2)}, u32[]{:S(2)}) collective-permute-start(bf16[3,128,512]{2,1,0:T(8,128)(2,1)S(1)} %get-tuple-element.138), channel_id=1, source_target_pairs={{0,2},{1,3},{2,0},{3,1},{4,6},{5,7},{6,4},{7,5},{8,10},{9,11},{10,... | collective-permute-start | bytes 1179656 | tf_op jit(solution)/shard_map/ppermute | solution.py:493
  65.6 3.9 %collective-permute-start.11 = (bf16[4,256,512]{2,1,0:T(8,128)(2,1)S(1)}, bf16[4,256,512]{2,1,0:T(8,128)(2,1)S(1)}, u32[]{:S(2)}, u32[]{:S(2)}) collective-permute-start(bf16[4,256,512]{2,1,0:T(8,128)(2,1)S(1)} %shard_map.180.refs_15_), channel_id=1, source_target_pairs={{0,1},{1,0},{2,3},{3,2},{4,5},{5,4},{6,7},{7,6},{8,9},{9,8},{10,11... | collective-permute-start | bytes 3145736 | tf_op jit(solution)/shard_map/ppermute | solution.py:493
  69.7 15.5 %collective-permute-start.13 = (bf16[4,128,512]{2,1,0:T(8,128)(2,1)S(1)}, bf16[4,128,512]{2,1,0:T(8,128)(2,1)S(1)}, u32[]{:S(2)}, u32[]{:S(2)}) collective-permute-start(bf16[4,128,512]{2,1,0:T(8,128)(2,1)S(1)} %get-tuple-element.141), channel_id=1, source_target_pairs={{0,2},{1,3},{2,0},{3,1},{4,6},{5,7},{6,4},{7,5},{8,10},{9,11},{10,... | collective-permute-start | bytes 1572872 | tf_op jit(solution)/shard_map/ppermute | solution.py:493
  72.6 8.3 %collective-permute-start.14 = (bf16[3,64,512]{2,1,0:T(8,128)(2,1)S(1)}, bf16[3,64,512]{2,1,0:T(8,128)(2,1)S(1)}, u32[]{:S(2)}, u32[]{:S(2)}) collective-permute-start(bf16[3,64,512]{2,1,0:T(8,128)(2,1)S(1)} %get-tuple-element.142), channel_id=1, source_target_pairs={{0,4},{1,5},{2,6},{3,7},{4,0},{5,1},{6,2},{7,3},{8,12},{9,13},{10,... | collective-permute-start | bytes 589832 | tf_op jit(solution)/shard_map/ppermute | solution.py:493
  85.3 14.3 %collective-permute-start.15 = (bf16[4,64,512]{2,1,0:T(8,128)(2,1)S(1)}, bf16[4,64,512]{2,1,0:T(8,128)(2,1)S(1)}, u32[]{:S(2)}, u32[]{:S(2)}) collective-permute-start(bf16[4,64,512]{2,1,0:T(8,128)(2,1)S(1)} %get-tuple-element.145), channel_id=1, source_target_pairs={{0,4},{1,5},{2,6},{3,7},{4,0},{5,1},{6,2},{7,3},{8,12},{9,13},{10,... | collective-permute-start | bytes 786440 | tf_op jit(solution)/shard_map/ppermute | solution.py:493
  88.3 7.8 %collective-permute-start.16 = (bf16[3,32,512]{2,1,0:T(8,128)(2,1)S(1)}, bf16[3,32,512]{2,1,0:T(8,128)(2,1)S(1)}, u32[]{:S(2)}, u32[]{:S(2)}) collective-permute-start(bf16[3,32,512]{2,1,0:T(8,128)(2,1)S(1)} %get-tuple-element.146), channel_id=1, source_target_pairs={{0,8},{1,9},{2,10},{3,11},{4,12},{5,13},{6,14},{7,15},{8,0},{9,1},... | collective-permute-start | bytes 294920 | tf_op jit(solution)/shard_map/ppermute | solution.py:493
  96.1 11.1 %collective-permute-start.24 = (bf16[3,32,512]{2,1,0:T(8,128)(2,1)S(1)}, bf16[3,32,512]{2,1,0:T(8,128)(2,1)S(1)}, u32[]{:S(2)}, u32[]{:S(2)}) collective-permute-start(bf16[3,32,512]{2,1,0:T(8,128)(2,1)S(1)} %shard_map.186.refs_3_.refs_1_), channel_id=1, source_target_pairs={{0,8},{1,9},{2,10},{3,11},{4,12},{5,13},{6,14},{7,15},{8,0},{9,1},... | collective-permute-start | bytes 294920 | tf_op jit(solution)/shard_map/ppermute | solution.py:493
  99.6 10.6 %collective-permute-start.17 = (bf16[4,32,512]{2,1,0:T(8,128)(2,1)S(1)}, bf16[4,32,512]{2,1,0:T(8,128)(2,1)S(1)}, u32[]{:S(2)}, u32[]{:S(2)}) collective-permute-start(bf16[4,32,512]{2,1,0:T(8,128)(2,1)S(1)} %get-tuple-element.148), channel_id=1, source_target_pairs={{0,8},{1,9},{2,10},{3,11},{4,12},{5,13},{6,14},{7,15},{8,0},{9,1},... | collective-permute-start | bytes 393224 | tf_op jit(solution)/shard_map/ppermute | solution.py:493
  99.7 10.7 %collective-permute-start.18 = (bf16[128,512]{1,0:T(8,128)(2,1)S(1)}, bf16[128,512]{1,0:T(8,128)(2,1)S(1)}, u32[]{:S(2)}, u32[]{:S(2)}) collective-permute-start(bf16[128,512]{1,0:T(8,128)(2,1)S(1)} %get-tuple-element.114.refs_13_.refs_8_), channel_id=1, source_target_pairs={{1,0},{2,1},{3,2},{4,3},{5,4},{6,5},{7,6},{8,7},{9,8},{10,9},{11,1... | collective-permute-start | bytes 393224 | tf_op jit(solution)/shard_map/ppermute | solution.py:22
  107.2 13.4 %collective-permute-start.25 = (bf16[3,64,512]{2,1,0:T(8,128)(2,1)S(1)}, bf16[3,64,512]{2,1,0:T(8,128)(2,1)S(1)}, u32[]{:S(2)}, u32[]{:S(2)}) collective-permute-start(bf16[3,64,512]{2,1,0:T(8,128)(2,1)S(1)} %shard_map.192.refs_1_), channel_id=1, source_target_pairs={{0,4},{1,5},{2,6},{3,7},{4,0},{5,1},{6,2},{7,3},{8,12},{9,13},{10,... | collective-permute-start | bytes 589832 | tf_op jit(solution)/shard_map/ppermute | solution.py:493
  107.4 7.8 %collective-permute-start.19 = (bf16[128,512]{1,0:T(8,128)(2,1)S(1)}, bf16[128,512]{1,0:T(8,128)(2,1)S(1)}, u32[]{:S(2)}, u32[]{:S(2)}) collective-permute-start(bf16[128,512]{1,0:T(8,128)(2,1)S(1)} %get-tuple-element.115.refs_14_.refs_9_), channel_id=1, source_target_pairs={{15,0},{0,1},{1,2},{2,3},{3,4},{4,5},{5,6},{6,7},{7,8},{8,9},{9,10... | collective-permute-start | bytes 393224 | tf_op jit(solution)/shard_map/ppermute | solution.py:22
  107.4 7.8 %collective-permute-start.20 = (bf16[128,512]{1,0:T(8,128)(2,1)S(1)}, bf16[128,512]{1,0:T(8,128)(2,1)S(1)}, u32[]{:S(2)}, u32[]{:S(2)}) collective-permute-start(bf16[128,512]{1,0:T(8,128)(2,1)S(1)} %get-tuple-element.116.refs_15_.refs_10_), channel_id=1, source_target_pairs={{2,0},{3,1},{4,2},{5,3},{6,4},{7,5},{8,6},{9,7},{10,8},{11,9},{12,... | collective-permute-start | bytes 393224 | tf_op jit(solution)/shard_map/ppermute | solution.py:22
  110.2 8.4 %collective-permute-start.21 = (bf16[128,512]{1,0:T(8,128)(2,1)S(1)}, bf16[128,512]{1,0:T(8,128)(2,1)S(1)}, u32[]{:S(2)}, u32[]{:S(2)}) collective-permute-start(bf16[128,512]{1,0:T(8,128)(2,1)S(1)} %get-tuple-element.117.refs_16_.refs_11_), channel_id=1, source_target_pairs={{14,0},{15,1},{0,2},{1,3},{2,4},{3,5},{4,6},{5,7},{6,8},{7,9},{8,1... | collective-permute-start | bytes 393224 | tf_op jit(solution)/shard_map/ppermute | solution.py:22
  110.5 10.1 %collective-permute-start.22 = (bf16[4,32,512]{2,1,0:T(8,128)(2,1)S(1)}, bf16[4,32,512]{2,1,0:T(8,128)(2,1)S(1)}, u32[]{:S(2)}, u32[]{:S(2)}) collective-permute-start(bf16[4,32,512]{2,1,0:T(8,128)(2,1)S(1)} %shard_map.188.refs_5_.refs_1_), channel_id=1, source_target_pairs={{0,8},{1,9},{2,10},{3,11},{4,12},{5,13},{6,14},{7,15},{8,0},{9,1},... | collective-permute-start | bytes 393224 | tf_op jit(solution)/shard_map/ppermute | solution.py:493
  120.6 13.3 %collective-permute-start.26 = (bf16[3,128,512]{2,1,0:T(8,128)(2,1)S(1)}, bf16[3,128,512]{2,1,0:T(8,128)(2,1)S(1)}, u32[]{:S(2)}, u32[]{:S(2)}) collective-permute-start(bf16[3,128,512]{2,1,0:T(8,128)(2,1)S(1)} %shard_map.193.refs_1_), channel_id=1, source_target_pairs={{0,2},{1,3},{2,0},{3,1},{4,6},{5,7},{6,4},{7,5},{8,10},{9,11},{10,... | collective-permute-start | bytes 1179656 | tf_op jit(solution)/shard_map/ppermute | solution.py:493
  124.2 8.4 %collective-permute-start.23 = (bf16[4,64,512]{2,1,0:T(8,128)(2,1)S(1)}, bf16[4,64,512]{2,1,0:T(8,128)(2,1)S(1)}, u32[]{:S(2)}, u32[]{:S(2)}) collective-permute-start(bf16[4,64,512]{2,1,0:T(8,128)(2,1)S(1)} %shard_map.191.refs_3_.refs_1_), channel_id=1, source_target_pairs={{0,4},{1,5},{2,6},{3,7},{4,0},{5,1},{6,2},{7,3},{8,12},{9,13},{10,... | collective-permute-start | bytes 786440 | tf_op jit(solution)/shard_map/ppermute | solution.py:493
  133.9 13.7 %collective-permute-start.27 = (bf16[4,128,512]{2,1,0:T(8,128)(2,1)S(1)}, bf16[4,128,512]{2,1,0:T(8,128)(2,1)S(1)}, u32[]{:S(2)}, u32[]{:S(2)}) collective-permute-start(bf16[4,128,512]{2,1,0:T(8,128)(2,1)S(1)} %shard_map.194.refs_1_), channel_id=1, source_target_pairs={{0,2},{1,3},{2,0},{3,1},{4,6},{5,7},{6,4},{7,5},{8,10},{9,11},{10,... | collective-permute-start | bytes 1572872 | tf_op jit(solution)/shard_map/ppermute | solution.py:493
  135.8 1.7 %collective-permute-start.28 = (bf16[3,128,512]{2,1,0:T(8,128)(2,1)S(1)}, bf16[3,128,512]{2,1,0:T(8,128)(2,1)S(1)}, u32[]{:S(2)}, u32[]{:S(2)}) collective-permute-start(bf16[3,128,512]{2,1,0:T(8,128)(2,1)S(1)} %shard_map.193.refs_1_), channel_id=1, source_target_pairs={{0,1},{1,0},{2,3},{3,2},{4,5},{5,4},{6,7},{7,6},{8,9},{9,8},{10,11... | collective-permute-start | bytes 1179656 | tf_op jit(solution)/shard_map/ppermute | solution.py:493
  135.8 2.3 %collective-permute-start.29 = (bf16[3,128,512]{2,1,0:T(8,128)(2,1)S(1)}, bf16[3,128,512]{2,1,0:T(8,128)(2,1)S(1)}, u32[]{:S(2)}, u32[]{:S(2)}) collective-permute-start(bf16[3,128,512]{2,1,0:T(8,128)(2,1)S(1)} %shard_map.195.refs_2_), channel_id=1, source_target_pairs={{0,1},{1,0},{2,3},{3,2},{4,5},{5,4},{6,7},{7,6},{8,9},{9,8},{10,11... | collective-permute-start | bytes 1179656 | tf_op jit(solution)/shard_map/ppermute | solution.py:493
  136.3 11.4 %collective-permute-start.30 = (bf16[4,128,512]{2,1,0:T(8,128)(2,1)S(1)}, bf16[4,128,512]{2,1,0:T(8,128)(2,1)S(1)}, u32[]{:S(2)}, u32[]{:S(2)}) collective-permute-start(bf16[4,128,512]{2,1,0:T(8,128)(2,1)S(1)} %shard_map.194.refs_1_), channel_id=1, source_target_pairs={{0,1},{1,0},{2,3},{3,2},{4,5},{5,4},{6,7},{7,6},{8,9},{9,8},{10,11... | collective-permute-start | bytes 1572872 | tf_op jit(solution)/shard_map/ppermute | solution.py:493
  147.7 1.9 %collective-permute-start.31 = (bf16[4,128,512]{2,1,0:T(8,128)(2,1)S(1)}, bf16[4,128,512]{2,1,0:T(8,128)(2,1)S(1)}, u32[]{:S(2)}, u32[]{:S(2)}) collective-permute-start(bf16[4,128,512]{2,1,0:T(8,128)(2,1)S(1)} %shard_map.197.refs_2_), channel_id=1, source_target_pairs={{0,1},{1,0},{2,3},{3,2},{4,5},{5,4},{6,7},{7,6},{8,9},{9,8},{10,11... | collective-permute-start | bytes 1572872 | tf_op jit(solution)/shard_map/ppermute | solution.py:493

commit v15 on v14

--- a/solution.py
+++ b/solution.py
@@ -811,6 +811,7 @@
             *back_near,
             *back_far,
             smem=(0,),
+            work=edge_work,
             last=(0,),
         )
         return grad_nodes
@@ -847,15 +848,17 @@
         keep_edge, came_edge = add_stage(me, keep_edge, came_edge, 2, [keep_node])
         keep_node, came_node = add_stage(me, keep_node, came_node, 8, [keep_edge])
         keep_edge, came_edge = add_stage(me, keep_edge, came_edge, 4, [keep_node])
+        keep_edge, came_edge = add_stage(me, keep_edge, came_edge, 8, [])
         piece_node, _ = add_stage(me, keep_node, came_node, 1, [keep_edge], 1, bf16)
-        keep_edge, came_edge = add_stage(me, keep_edge, came_edge, 8, [piece_node])
-        piece_node = gather_stage(me, piece_node, over(piece_node, 8), 8, [keep_edge])
         piece_edge, _ = add_stage(me, keep_edge, came_edge, 1, [], 1, bf16)
+        piece_node = gather_stage(me, piece_node, over(piece_node, 8), 8, [piece_edge])
+        piece_edge = gather_stage(me, piece_edge, over(piece_edge, 8), 8, [])
         grad_nodes = node_output([piece_edge])
-        piece_edge = gather_stage(me, piece_edge, over(piece_edge, 8), 8, [in_hbm(grad_nodes)])
         piece_node = gather_stage(me, piece_node, over(piece_node, 4), 4, [piece_edge])
         other_node = over(piece_node, 2)
-        piece_edge = gather_stage(me, piece_edge, over(piece_edge, 4), 4, [other_node])
+        piece_edge = gather_stage(
+            me, piece_edge, over(piece_edge, 4), 4, [other_node, in_hbm(grad_nodes)]
+        )
         other_node = held_until(other_node, [piece_edge])
         grad_n1, grad_n2 = join_stage(me, piece_node, other_node, first, node_blocks, node_shapes)
         other_edge = held_until(over(piece_edge, 2), [in_hbm(grad_n2)])

time: 151 us -> 149 us (0.987)
  starting transfers between devices: 38.6 us -> 35.3 us
    ppermute x18, starting transfers between devices: 23.3 us -> 18.6 us  [in_group(): return lax.ppermute(block, axis, route)]
    ppermute x18, waiting for transfers between devices: 47 us -> 49.8 us  [in_group(): return lax.ppermute(block, axis, route)]
  transfers between devices with their start and end apart: 32 -> 32, of which waited for: 19 -> 20; matrix products, arithmetic and copies ran while one was open for 0% -> 0% of each run, Pallas kernels for 13% -> 13%
where the time goes in v15:
time: 149 us
  waiting for transfers between devices  68.3 us (46%)
  starting transfers between devices  35.3 us (24%)
  Pallas kernels  31 us (21%)
  blocking collectives  13.7 us (9%)
    ppermute x18, waiting for transfers between devices, in_group(): return lax.ppermute(block, axis, route)  49.8 us
    pallas_call x25, Pallas kernels, call(): pl.pallas_call(kernel, out_shape=[(pltpu.HBM if i in last else pltpu.VMEM...  27.8 us
    ppermute x18, starting transfers between devices, in_group(): return lax.ppermute(block, axis, route)  18.6 us
    ppermute x14, waiting for transfers between devices, passed_along(): return lax.ppermute(block, axis, route)  18.5 us
    ppermute x14, starting transfers between devices, passed_along(): return lax.ppermute(block, axis, route)  16.8 us
    all_to_all x1, blocking collectives, local(): ids = lax.all_to_all(ids, 'band', 0, 0, tiled=True)  13.7 us
    pallas_call x1, Pallas kernels, loaded(): pl.pallas_call(functools.partial(load_kernel, count), out_shape=[pltpu.VM...  3.24 us
  transfers between devices with their start and end apart: 32, of which 20 were waited for; matrix products, arithmetic and copies ran while one was open for 0% of the time, Pallas kernels for 13%

profile of v15, /device:TPU:0, one launch (start us, length us, event | category | flops | bytes accessed | tf_op | source)
XLA Modules:
  0.0 149.2 jit_solution(14043414723288529134)
XLA Ops:
  0.6 3.2 %shard_map.170 = (bf16[320,512]{1,0:T(8,128)(2,1)S(1)}, s32[11,1,128]{2,1,0:T(1,128)S(1)}, s32[11,1,128]{2,1,0:T(1,128)S(1)}, bf16[11,128,512]{2,1,0:T(8,128)(2,...) custom-call(s32[1]{0:T(128)} %bitcast.refs_0_.refs_2_, ...), custom_call_target="tpu_custom_call" | custom-call | flops 1 | bytes 1 | tf_op jit(solution)/shard_map/pallas_call | solution.py:121
  3.9 13.7 %all_to_all.5.refs_2_.refs_4_ = s32[16,1,256]{2,1,0:T(1,128)S(1)} all-to-all(s32[16,1,256]{2,1,0:T(1,128)S(1)} %shard_map.171), channel_id=1, replica_groups=mesh['groups'=2,'band'=16] {'band'}, dimensions={0} | all-to-all | bytes 32768 | tf_op jit(solution)/shard_map/all_to_all | solution.py:638
  17.6 0.8 shard_map.172
  18.6 1.2 collective-permute-start.2
  19.8 0.8 collective-permute-start.6
  20.6 3.3 %collective-permute-start.3 = (bf16[128,512]{1,0:T(8,128)(2,1)S(1)}, bf16[128,512]{1,0:T(8,128)(2,1)S(1)}, u32[]{:S(2)}, u32[]{:S(2)}) collective-permute-start(bf16[128,512]{1,0:T(8,128)(2,1)S(1)} %get-tuple-element.96), channel_id=1, source_target_pairs={{2,0},{3,1},{4,2},{5,3},{6,4},{7,5},{8,6},{9,7},{10,8},{11,9},{12,... | collective-permute-start | bytes 393224 | tf_op jit(solution)/shard_map/ppermute | solution.py:22
  23.9 3.8 %collective-permute-done.2.refs_8_.refs_7_ = bf16[128,512]{1,0:T(8,128)(2,1)S(1)} collective-permute-done((bf16[128,512]{1,0:T(8,128)(2,1)S(1)}, bf16[128,512]{1,0:T(8,128)(2,1)S(1)}, u32[]{:S(2)}, u32[]{:S(2)}) %collective-permute-start.2) | collective-permute-done | bytes 131104 | tf_op jit(solution)/shard_map/ppermute | solution.py:22
  27.8 4.5 %shard_map.173 = (bf16[1408,320]{1,0:T(8,128)(2,1)S(1)}, bf16[320,1408]{1,0:T(8,128)(2,1)S(1)}, f32[1408,128]{1,0:T(8,128)S(1)}, f32[1024,512]{1,0:T(8,128)S(1)}...) custom-call(bf16[11,128,512]{2,1,0:T(8,128)(2,1)S(1)} %get-tuple-ele, ...), custom_call_target="tpu_custom_call" | custom-call | flops 1 | bytes 1 | tf_op jit(solution)/shard_map/pallas_call | solution.py:90
  32.3 2.7 %collective-permute-done.refs_6_.refs_5_ = bf16[128,512]{1,0:T(8,128)(2,1)S(1)} collective-permute-done((bf16[128,512]{1,0:T(8,128)(2,1)S(1)}, bf16[128,512]{1,0:T(8,128)(2,1)S(1)}, u32[]{:S(2)}, u32[]{:S(2)}) %collective-permute-start) | collective-permute-done | bytes 131104 | tf_op jit(solution)/shard_map/ppermute | solution.py:22
  35.0 1.6 %shard_map.174 = (bf16[512,512]{1,0:T(8,128)(2,1)S(1)}, f32[512,512]{1,0:T(8,128)S(1)}, f32[512,512]{1,0:T(8,128)S(1)}, f32[512,128]{1,0:T(8,128)S(1)}, f32[320,512]{1,0:T(8,128)S(1)}) custom-call(f32[1024,512]{1,0:T(8,128)S(1)} %get-tuple-element.89.refs_0_.refs_1_, f32[1408,128]{1,0:T(8,128)S(1)} %get-tuple-element.90.refs_1_.refs_2_.refs_3_, ...), custom_call_target="tpu_custom_call" | custom-call | flops 1 | bytes 1 | tf_op jit(solution)/shard_map/pallas_call | solution.py:90
  36.6 2.8 %collective-permute-done.5.refs_13_.refs_10_ = bf16[128,512]{1,0:T(8,128)(2,1)S(1)} collective-permute-done((bf16[128,512]{1,0:T(8,128)(2,1)S(1)}, bf16[128,512]{1,0:T(8,128)(2,1)S(1)}, u32[]{:S(2)}, u32[]{:S(2)}) %collective-permute-start.5) | collective-permute-done | bytes 131104 | tf_op jit(solution)/shard_map/ppermute | solution.py:22
  39.4 4.5 %shard_map.175 = (bf16[128,512]{1,0:T(8,128)(2,1)S(1)}, bf16[128,512]{1,0:T(8,128)(2,1)S(1)}, bf16[256,512]{1,0:T(8,128)(2,1)S(1)}, bf16[512,512]{1,0:T(8,128)(2...) custom-call(bf16[11,128,512]{2,1,0:T(8,128)(2,1)S(1)} %get-tuple-ele, ...), custom_call_target="tpu_custom_call" | custom-call | flops 1 | bytes 1 | tf_op jit(solution)/shard_map/pallas_call | solution.py:90
  43.9 1.3 shard_map.178
  45.3 4.7 %collective-permute-start.9 = (bf16[256,512]{1,0:T(8,128)(2,1)S(1)}, bf16[256,512]{1,0:T(8,128)(2,1)S(1)}, u32[]{:S(2)}, u32[]{:S(2)}) collective-permute-start(bf16[256,512]{1,0:T(8,128)(2,1)S(1)} %get-tuple-element.120.refs_19_.refs_14_), channel_id=1, source_target_pairs={{8,0},{9,1},{10,2},{11,3},{12,4},{13,5},{14,6},{15,7},{0,8},{1,9},... | collective-permute-start | bytes 786440 | tf_op jit(solution)/shard_map/ppermute | solution.py:22
  50.0 1.7 %collective-permute-start.7 = (bf16[128,512]{1,0:T(8,128)(2,1)S(1)}, bf16[128,512]{1,0:T(8,128)(2,1)S(1)}, u32[]{:S(2)}, u32[]{:S(2)}) collective-permute-start(bf16[128,512]{1,0:T(8,128)(2,1)S(1)} %get-tuple-element.118.refs_17_.refs_12_), channel_id=1, source_target_pairs={{4,0},{5,1},{6,2},{7,3},{8,4},{9,5},{10,6},{11,7},{12,8},{13,9},{1... | collective-permute-start | bytes 393224 | tf_op jit(solution)/shard_map/ppermute | solution.py:22
  52.0 2.1 %shard_map.176 = (bf16[896,512]{1,0:T(8,128)(2,1)S(1)}, bf16[384,512]{1,0:T(8,128)(2,1)S(1)}, bf16[128,512]{1,0:T(8,128)(2,1)S(1)}, bf16[128,512]{1,0:T(8,128)(2...) custom-call(bf16[11,128,512]{2,1,0:T(8,128)(2,1)S(1)} %get-tuple-element.81.refs_0_.refs_1_, ...), custom_call_target="tpu_custom_call" | custom-call | flops 1 | bytes 1 | tf_op jit(solution)/shard_map/pallas_call | solution.py:90
  54.1 3.9 %shard_map.177 = (f32[4,256,512]{2,1,0:T(8,128)S(1)}, bf16[4,256,512]{2,1,0:T(8,128)(2,1)S(1)}, bf16[320,512]{1,0:T(8,128)(2,1)S(1)}) custom-call(bf16[11,128,512]{2,1,0:T(8,128)(2,1)S(1)} %get-tuple-element.82.refs_0_, bf16[320,1408]{1,0:T(8,128)(2,1)S(1)} %get-tuple-element.92.refs_2_.refs_4_.refs_1_, s32[1]{0:T(128)} %bitcast.refs_0_.refs_2_, ...), custom_call_target="tpu_custom_call" | custom-call | flops 1 | bytes 1 | tf_op jit(solution)/shard_map/pallas_call | solution.py:90
  58.2 2.1 %collective-permute-start.12 = (bf16[3,128,512]{2,1,0:T(8,128)(2,1)S(1)}, bf16[3,128,512]{2,1,0:T(8,128)(2,1)S(1)}, u32[]{:S(2)}, u32[]{:S(2)}) collective-permute-start(bf16[3,128,512]{2,1,0:T(8,128)(2,1)S(1)} %get-tuple-element.138), channel_id=1, source_target_pairs={{0,2},{1,3},{2,0},{3,1},{4,6},{5,7},{6,4},{7,5},{8,10},{9,11},{10,... | collective-permute-start | bytes 1179656 | tf_op jit(solution)/shard_map/ppermute | solution.py:493
  60.3 3.8 %collective-permute-done.8.refs_2_.refs_11_ = bf16[128,512]{1,0:T(8,128)(2,1)S(1)} collective-permute-done((bf16[128,512]{1,0:T(8,128)(2,1)S(1)}, bf16[128,512]{1,0:T(8,128)(2,1)S(1)}, u32[]{:S(2)}, u32[]{:S(2)}) %collective-permute-start.8) | collective-permute-done | bytes 131104 | tf_op jit(solution)/shard_map/ppermute | solution.py:22
  64.0 1.5 %collective-permute-done.9.refs_3_.refs_12_ = bf16[256,512]{1,0:T(8,128)(2,1)S(1)} collective-permute-done((bf16[256,512]{1,0:T(8,128)(2,1)S(1)}, bf16[256,512]{1,0:T(8,128)(2,1)S(1)}, u32[]{:S(2)}, u32[]{:S(2)}) %collective-permute-start.9) | collective-permute-done | bytes 262176 | tf_op jit(solution)/shard_map/ppermute | solution.py:22
  65.6 3.5 %shard_map.181 = (bf16[11,128,512]{2,1,0:T(8,128)(2,1)}, bf16[11,128,512]{2,1,0:T(8,128)(2,1)}) custom-call(bf16[11,128,512]{2,1,0:T(8,128)(2,1)S(1)} %get-tuple-element.82.refs_0_, bf16[11,128,512]{2,1,0:T(8,128)(2,1)S(1)} %get-tuple-element.81.refs_0_.refs_1_, bf16[1536,512]{1,0:T(8,128)(2,1)S(1)} %get-tuple-element.85.refs_4_.refs_6_.refs_2_.refs_3_, ...), custom_call_target="tpu_custom_call" | custom-call | flops 20000000000 | bytes 1 | tf_op jit(solution)/shard_map/pallas_call | solution.py:90
  69.7 2.9 %collective-permute-start.13 = (bf16[4,128,512]{2,1,0:T(8,128)(2,1)S(1)}, bf16[4,128,512]{2,1,0:T(8,128)(2,1)S(1)}, u32[]{:S(2)}, u32[]{:S(2)}) collective-permute-start(bf16[4,128,512]{2,1,0:T(8,128)(2,1)S(1)} %get-tuple-element.141), channel_id=1, source_target_pairs={{0,2},{1,3},{2,0},{3,1},{4,6},{5,7},{6,4},{7,5},{8,10},{9,11},{10,... | collective-permute-start | bytes 1572872 | tf_op jit(solution)/shard_map/ppermute | solution.py:493
  72.6 3.0 %collective-permute-start.14 = (bf16[3,64,512]{2,1,0:T(8,128)(2,1)S(1)}, bf16[3,64,512]{2,1,0:T(8,128)(2,1)S(1)}, u32[]{:S(2)}, u32[]{:S(2)}) collective-permute-start(bf16[3,64,512]{2,1,0:T(8,128)(2,1)S(1)} %get-tuple-element.142), channel_id=1, source_target_pairs={{0,4},{1,5},{2,6},{3,7},{4,0},{5,1},{6,2},{7,3},{8,12},{9,13},{10,... | collective-permute-start | bytes 589832 | tf_op jit(solution)/shard_map/ppermute | solution.py:493
  75.6 5.3 %collective-permute-done.14.refs_2_ = bf16[3,64,512]{2,1,0:T(8,128)(2,1)S(1)} collective-permute-done((bf16[3,64,512]{2,1,0:T(8,128)(2,1)S(1)}, bf16[3,64,512]{2,1,0:T(8,128)(2,1)S(1)}, u32[]{:S(2)}, u32[]{:S(2)}) %collective-permute-start.14) | collective-permute-done | bytes 196640 | tf_op jit(solution)/shard_map/ppermute | solution.py:493
  80.9 4.3 %collective-permute-done.13.refs_2_ = bf16[4,128,512]{2,1,0:T(8,128)(2,1)S(1)} collective-permute-done((bf16[4,128,512]{2,1,0:T(8,128)(2,1)S(1)}, bf16[4,128,512]{2,1,0:T(8,128)(2,1)S(1)}, u32[]{:S(2)}, u32[]{:S(2)}) %collective-permute-start.13) | collective-permute-done | bytes 524320 | tf_op jit(solution)/shard_map/ppermute | solution.py:493
  85.3 3.0 %collective-permute-start.15 = (bf16[4,64,512]{2,1,0:T(8,128)(2,1)S(1)}, bf16[4,64,512]{2,1,0:T(8,128)(2,1)S(1)}, u32[]{:S(2)}, u32[]{:S(2)}) collective-permute-start(bf16[4,64,512]{2,1,0:T(8,128)(2,1)S(1)} %get-tuple-element.145), channel_id=1, source_target_pairs={{0,4},{1,5},{2,6},{3,7},{4,0},{5,1},{6,2},{7,3},{8,12},{9,13},{10,... | collective-permute-start | bytes 786440 | tf_op jit(solution)/shard_map/ppermute | solution.py:493
  88.3 8.5 %collective-permute-done.15.refs_2_ = bf16[4,64,512]{2,1,0:T(8,128)(2,1)S(1)} collective-permute-done((bf16[4,64,512]{2,1,0:T(8,128)(2,1)S(1)}, bf16[4,64,512]{2,1,0:T(8,128)(2,1)S(1)}, u32[]{:S(2)}, u32[]{:S(2)}) %collective-permute-start.15) | collective-permute-done | bytes 262176 | tf_op jit(solution)/shard_map/ppermute | solution.py:493
  97.3 2.7 %collective-permute-start.24 = (bf16[3,32,512]{2,1,0:T(8,128)(2,1)S(1)}, bf16[3,32,512]{2,1,0:T(8,128)(2,1)S(1)}, u32[]{:S(2)}, u32[]{:S(2)}) collective-permute-start(bf16[3,32,512]{2,1,0:T(8,128)(2,1)S(1)} %shard_map.191.refs_1_), channel_id=1, source_target_pairs={{0,8},{1,9},{2,10},{3,11},{4,12},{5,13},{6,14},{7,15},{8,0},{9,1},... | collective-permute-start | bytes 294920 | tf_op jit(solution)/shard_map/ppermute | solution.py:493
  99.9 7.3 %collective-permute-done.16.refs_2_ = bf16[4,32,512]{2,1,0:T(8,128)(2,1)S(1)} collective-permute-done((bf16[4,32,512]{2,1,0:T(8,128)(2,1)S(1)}, bf16[4,32,512]{2,1,0:T(8,128)(2,1)S(1)}, u32[]{:S(2)}, u32[]{:S(2)}) %collective-permute-start.16) | collective-permute-done | bytes 131104 | tf_op jit(solution)/shard_map/ppermute | solution.py:493
  107.3 1.3 collective-permute-done.24.refs_2_
  108.6 0.9 collective-permute-start.25
  109.6 1.3 collective-permute-start.18
  110.9 2.2 %collective-permute-start.20 = (bf16[128,512]{1,0:T(8,128)(2,1)S(1)}, bf16[128,512]{1,0:T(8,128)(2,1)S(1)}, u32[]{:S(2)}, u32[]{:S(2)}) collective-permute-start(bf16[128,512]{1,0:T(8,128)(2,1)S(1)} %get-tuple-element.116.refs_15_.refs_10_), channel_id=1, source_target_pairs={{2,0},{3,1},{4,2},{5,3},{6,4},{7,5},{8,6},{9,7},{10,8},{11,9},{12,... | collective-permute-start | bytes 393224 | tf_op jit(solution)/shard_map/ppermute | solution.py:22
  113.0 2.2 %collective-permute-done.17.refs_2_ = bf16[4,32,512]{2,1,0:T(8,128)(2,1)S(1)} collective-permute-done((bf16[4,32,512]{2,1,0:T(8,128)(2,1)S(1)}, bf16[4,32,512]{2,1,0:T(8,128)(2,1)S(1)}, u32[]{:S(2)}, u32[]{:S(2)}) %collective-permute-start.17) | collective-permute-done | bytes 131104 | tf_op jit(solution)/shard_map/ppermute | solution.py:493
  115.2 1.0 collective-permute-start.21
  116.8 2.2 %collective-permute-done.25.refs_2_ = bf16[3,64,512]{2,1,0:T(8,128)(2,1)S(1)} collective-permute-done((bf16[3,64,512]{2,1,0:T(8,128)(2,1)S(1)}, bf16[3,64,512]{2,1,0:T(8,128)(2,1)S(1)}, u32[]{:S(2)}, u32[]{:S(2)}) %collective-permute-start.25) | collective-permute-done | bytes 196640 | tf_op jit(solution)/shard_map/ppermute | solution.py:493
  119.0 1.4 collective-permute-start.26
  120.4 3.8 %collective-permute-done.21.refs_9_ = bf16[128,512]{1,0:T(8,128)(2,1)S(1)} collective-permute-done((bf16[128,512]{1,0:T(8,128)(2,1)S(1)}, bf16[128,512]{1,0:T(8,128)(2,1)S(1)}, u32[]{:S(2)}, u32[]{:S(2)}) %collective-permute-start.21) | collective-permute-done | bytes 131104 | tf_op jit(solution)/shard_map/ppermute | solution.py:22
  124.2 1.6 %shard_map.190.refs_4_ = bf16[320,512]{1,0:T(8,128)(2,1)} custom-call(s32[1]{0:T(128)} %bitcast.refs_0_.refs_2_, f32[320,512]{1,0:T(8,128)S(1)} %shard_map.189.refs_1_, bf16[1536,512]{1,0:T(8,128)(2,1)S(1)} %get-tuple-element.85.refs_4_.refs_6_.refs_2_.refs_3_, s32[11,1,128]{2,1,0:T(1,128)S(1)} %get-tuple-element.84.refs_1_.refs_2_.refs_3_, ...), custom_call_target="tpu_custom_call" | custom-call | flops 20000000000 | bytes 1 | tf_op jit(solution)/shard_map/pallas_call | solution.py:90
  125.9 1.5 %collective-permute-done.22.refs_2_ = bf16[4,64,512]{2,1,0:T(8,128)(2,1)S(1)} collective-permute-done((bf16[4,64,512]{2,1,0:T(8,128)(2,1)S(1)}, bf16[4,64,512]{2,1,0:T(8,128)(2,1)S(1)}, u32[]{:S(2)}, u32[]{:S(2)}) %collective-permute-start.22) | collective-permute-done | bytes 262176 | tf_op jit(solution)/shard_map/ppermute | solution.py:493
  127.4 4.2 %collective-permute-done.26.refs_3_.refs_0_ = bf16[3,128,512]{2,1,0:T(8,128)(2,1)S(1)} collective-permute-done((bf16[3,128,512]{2,1,0:T(8,128)(2,1)S(1)}, bf16[3,128,512]{2,1,0:T(8,128)(2,1)S(1)}, u32[]{:S(2)}, u32[]{:S(2)}) %collective-permute-start.26) | collective-permute-done | bytes 393248 | tf_op jit(solution)/shard_map/ppermute | solution.py:493
  131.7 1.0 collective-permute-start.27
  133.6 0.8 collective-permute-done.28.refs_3_
  134.5 0.6 collective-permute-done.29.refs_4_
  135.0 1.3 shard_map.196
  136.3 9.6 %collective-permute-done.27.refs_0_ = bf16[4,128,512]{2,1,0:T(8,128)(2,1)S(1)} collective-permute-done((bf16[4,128,512]{2,1,0:T(8,128)(2,1)S(1)}, bf16[4,128,512]{2,1,0:T(8,128)(2,1)S(1)}, u32[]{:S(2)}, u32[]{:S(2)}) %collective-permute-start.27) | collective-permute-done | bytes 524320 | tf_op jit(solution)/shard_map/ppermute | solution.py:493
  145.8 1.9 %collective-permute-done.31.refs_4_ = bf16[4,128,512]{2,1,0:T(8,128)(2,1)S(1)} collective-permute-done((bf16[4,128,512]{2,1,0:T(8,128)(2,1)S(1)}, bf16[4,128,512]{2,1,0:T(8,128)(2,1)S(1)}, u32[]{:S(2)}, u32[]{:S(2)}) %collective-permute-start.31) | collective-permute-done | bytes 524320 | tf_op jit(solution)/shard_map/ppermute | solution.py:493
  147.7 1.5 shard_map.198
  (46 shorter events, 3.8 us)
Async XLA Ops:
  18.4 5.5 %collective-permute-start.1 = (bf16[128,512]{1,0:T(8,128)(2,1)S(1)}, bf16[128,512]{1,0:T(8,128)(2,1)S(1)}, u32[]{:S(2)}, u32[]{:S(2)}) collective-permute-start(bf16[128,512]{1,0:T(8,128)(2,1)S(1)} %get-tuple-element.94), channel_id=1, source_target_pairs={{1,0},{2,1},{3,2},{4,3},{5,4},{6,5},{7,6},{8,7},{9,8},{10,9},{11,1... | collective-permute-start | bytes 393224 | tf_op jit(solution)/shard_map/ppermute | solution.py:22
  18.6 9.1 %collective-permute-start.2 = (bf16[128,512]{1,0:T(8,128)(2,1)S(1)}, bf16[128,512]{1,0:T(8,128)(2,1)S(1)}, u32[]{:S(2)}, u32[]{:S(2)}) collective-permute-start(bf16[128,512]{1,0:T(8,128)(2,1)S(1)} %get-tuple-element.95), channel_id=1, source_target_pairs={{14,0},{15,1},{0,2},{1,3},{2,4},{3,5},{4,6},{5,7},{6,8},{7,9},{8,1... | collective-permute-start | bytes 393224 | tf_op jit(solution)/shard_map/ppermute | solution.py:22
  19.8 19.6 %collective-permute-start.6 = (bf16[256,512]{1,0:T(8,128)(2,1)S(1)}, bf16[256,512]{1,0:T(8,128)(2,1)S(1)}, u32[]{:S(2)}, u32[]{:S(2)}) collective-permute-start(bf16[256,512]{1,0:T(8,128)(2,1)S(1)} %get-tuple-element.103), channel_id=1, source_target_pairs={{8,0},{9,1},{10,2},{11,3},{12,4},{13,5},{14,6},{15,7},{0,8},{1,9},... | collective-permute-start | bytes 786440 | tf_op jit(solution)/shard_map/ppermute | solution.py:22
  20.6 11.6 %collective-permute-start.3 = (bf16[128,512]{1,0:T(8,128)(2,1)S(1)}, bf16[128,512]{1,0:T(8,128)(2,1)S(1)}, u32[]{:S(2)}, u32[]{:S(2)}) collective-permute-start(bf16[128,512]{1,0:T(8,128)(2,1)S(1)} %get-tuple-element.96), channel_id=1, source_target_pairs={{2,0},{3,1},{4,2},{5,3},{6,4},{7,5},{8,6},{9,7},{10,8},{11,9},{12,... | collective-permute-start | bytes 393224 | tf_op jit(solution)/shard_map/ppermute | solution.py:22
  23.9 11.1 %collective-permute-start = (bf16[128,512]{1,0:T(8,128)(2,1)S(1)}, bf16[128,512]{1,0:T(8,128)(2,1)S(1)}, u32[]{:S(2)}, u32[]{:S(2)}) collective-permute-start(bf16[128,512]{1,0:T(8,128)(2,1)S(1)} %get-tuple-element.88.refs_7_), channel_id=1, source_target_pairs={{15,0},{0,1},{1,2},{2,3},{3,4},{4,5},{5,6},{6,7},{7,8},{8,9},{9,10... | collective-permute-start | bytes 393224 | tf_op jit(solution)/shard_map/ppermute | solution.py:22
  23.9 12.7 %collective-permute-start.4 = (bf16[128,512]{1,0:T(8,128)(2,1)S(1)}, bf16[128,512]{1,0:T(8,128)(2,1)S(1)}, u32[]{:S(2)}, u32[]{:S(2)}) collective-permute-start(bf16[128,512]{1,0:T(8,128)(2,1)S(1)} %get-tuple-element.101), channel_id=1, source_target_pairs={{12,0},{13,1},{14,2},{15,3},{0,4},{1,5},{2,6},{3,7},{4,8},{5,9},{6... | collective-permute-start | bytes 393224 | tf_op jit(solution)/shard_map/ppermute | solution.py:22
  27.8 11.6 %collective-permute-start.5 = (bf16[128,512]{1,0:T(8,128)(2,1)S(1)}, bf16[128,512]{1,0:T(8,128)(2,1)S(1)}, u32[]{:S(2)}, u32[]{:S(2)}) collective-permute-start(bf16[128,512]{1,0:T(8,128)(2,1)S(1)} %get-tuple-element.102), channel_id=1, source_target_pairs={{4,0},{5,1},{6,2},{7,3},{8,4},{9,5},{10,6},{11,7},{12,8},{13,9},{1... | collective-permute-start | bytes 393224 | tf_op jit(solution)/shard_map/ppermute | solution.py:22
  45.2 12.8 %collective-permute-start.10 = (bf16[3,256,512]{2,1,0:T(8,128)(2,1)S(1)}, bf16[3,256,512]{2,1,0:T(8,128)(2,1)S(1)}, u32[]{:S(2)}, u32[]{:S(2)}) collective-permute-start(bf16[3,256,512]{2,1,0:T(8,128)(2,1)S(1)} %get-tuple-element.133), channel_id=1, source_target_pairs={{0,1},{1,0},{2,3},{3,2},{4,5},{5,4},{6,7},{7,6},{8,9},{9,8},{10,11... | collective-permute-start | bytes 2359304 | tf_op jit(solution)/shard_map/ppermute | solution.py:493
  45.3 20.3 %collective-permute-start.9 = (bf16[256,512]{1,0:T(8,128)(2,1)S(1)}, bf16[256,512]{1,0:T(8,128)(2,1)S(1)}, u32[]{:S(2)}, u32[]{:S(2)}) collective-permute-start(bf16[256,512]{1,0:T(8,128)(2,1)S(1)} %get-tuple-element.120.refs_19_.refs_14_), channel_id=1, source_target_pairs={{8,0},{9,1},{10,2},{11,3},{12,4},{13,5},{14,6},{15,7},{0,8},{1,9},... | collective-permute-start | bytes 786440 | tf_op jit(solution)/shard_map/ppermute | solution.py:22
  50.0 10.3 %collective-permute-start.7 = (bf16[128,512]{1,0:T(8,128)(2,1)S(1)}, bf16[128,512]{1,0:T(8,128)(2,1)S(1)}, u32[]{:S(2)}, u32[]{:S(2)}) collective-permute-start(bf16[128,512]{1,0:T(8,128)(2,1)S(1)} %get-tuple-element.118.refs_17_.refs_12_), channel_id=1, source_target_pairs={{4,0},{5,1},{6,2},{7,3},{8,4},{9,5},{10,6},{11,7},{12,8},{13,9},{1... | collective-permute-start | bytes 393224 | tf_op jit(solution)/shard_map/ppermute | solution.py:22
  51.7 12.4 %collective-permute-start.8 = (bf16[128,512]{1,0:T(8,128)(2,1)S(1)}, bf16[128,512]{1,0:T(8,128)(2,1)S(1)}, u32[]{:S(2)}, u32[]{:S(2)}) collective-permute-start(bf16[128,512]{1,0:T(8,128)(2,1)S(1)} %get-tuple-element.119.refs_18_.refs_13_), channel_id=1, source_target_pairs={{12,0},{13,1},{14,2},{15,3},{0,4},{1,5},{2,6},{3,7},{4,8},{5,9},{6... | collective-permute-start | bytes 393224 | tf_op jit(solution)/shard_map/ppermute | solution.py:22
  58.2 11.3 %collective-permute-start.12 = (bf16[3,128,512]{2,1,0:T(8,128)(2,1)S(1)}, bf16[3,128,512]{2,1,0:T(8,128)(2,1)S(1)}, u32[]{:S(2)}, u32[]{:S(2)}) collective-permute-start(bf16[3,128,512]{2,1,0:T(8,128)(2,1)S(1)} %get-tuple-element.138), channel_id=1, source_target_pairs={{0,2},{1,3},{2,0},{3,1},{4,6},{5,7},{6,4},{7,5},{8,10},{9,11},{10,... | collective-permute-start | bytes 1179656 | tf_op jit(solution)/shard_map/ppermute | solution.py:493
  65.6 3.9 %collective-permute-start.11 = (bf16[4,256,512]{2,1,0:T(8,128)(2,1)S(1)}, bf16[4,256,512]{2,1,0:T(8,128)(2,1)S(1)}, u32[]{:S(2)}, u32[]{:S(2)}) collective-permute-start(bf16[4,256,512]{2,1,0:T(8,128)(2,1)S(1)} %shard_map.180.refs_15_), channel_id=1, source_target_pairs={{0,1},{1,0},{2,3},{3,2},{4,5},{5,4},{6,7},{7,6},{8,9},{9,8},{10,11... | collective-permute-start | bytes 3145736 | tf_op jit(solution)/shard_map/ppermute | solution.py:493
  69.7 15.5 %collective-permute-start.13 = (bf16[4,128,512]{2,1,0:T(8,128)(2,1)S(1)}, bf16[4,128,512]{2,1,0:T(8,128)(2,1)S(1)}, u32[]{:S(2)}, u32[]{:S(2)}) collective-permute-start(bf16[4,128,512]{2,1,0:T(8,128)(2,1)S(1)} %get-tuple-element.141), channel_id=1, source_target_pairs={{0,2},{1,3},{2,0},{3,1},{4,6},{5,7},{6,4},{7,5},{8,10},{9,11},{10,... | collective-permute-start | bytes 1572872 | tf_op jit(solution)/shard_map/ppermute | solution.py:493
  72.6 8.3 %collective-permute-start.14 = (bf16[3,64,512]{2,1,0:T(8,128)(2,1)S(1)}, bf16[3,64,512]{2,1,0:T(8,128)(2,1)S(1)}, u32[]{:S(2)}, u32[]{:S(2)}) collective-permute-start(bf16[3,64,512]{2,1,0:T(8,128)(2,1)S(1)} %get-tuple-element.142), channel_id=1, source_target_pairs={{0,4},{1,5},{2,6},{3,7},{4,0},{5,1},{6,2},{7,3},{8,12},{9,13},{10,... | collective-permute-start | bytes 589832 | tf_op jit(solution)/shard_map/ppermute | solution.py:493
  85.3 11.5 %collective-permute-start.15 = (bf16[4,64,512]{2,1,0:T(8,128)(2,1)S(1)}, bf16[4,64,512]{2,1,0:T(8,128)(2,1)S(1)}, u32[]{:S(2)}, u32[]{:S(2)}) collective-permute-start(bf16[4,64,512]{2,1,0:T(8,128)(2,1)S(1)} %get-tuple-element.145), channel_id=1, source_target_pairs={{0,4},{1,5},{2,6},{3,7},{4,0},{5,1},{6,2},{7,3},{8,12},{9,13},{10,... | collective-permute-start | bytes 786440 | tf_op jit(solution)/shard_map/ppermute | solution.py:493
  88.3 8.9 %collective-permute-start.23 = (bf16[3,32,512]{2,1,0:T(8,128)(2,1)S(1)}, bf16[3,32,512]{2,1,0:T(8,128)(2,1)S(1)}, u32[]{:S(2)}, u32[]{:S(2)}) collective-permute-start(bf16[3,32,512]{2,1,0:T(8,128)(2,1)S(1)} %get-tuple-element.149), channel_id=1, source_target_pairs={{0,8},{1,9},{2,10},{3,11},{4,12},{5,13},{6,14},{7,15},{8,0},{9,1},... | collective-permute-start | bytes 294920 | tf_op jit(solution)/shard_map/ppermute | solution.py:493
  96.9 10.3 %collective-permute-start.16 = (bf16[4,32,512]{2,1,0:T(8,128)(2,1)S(1)}, bf16[4,32,512]{2,1,0:T(8,128)(2,1)S(1)}, u32[]{:S(2)}, u32[]{:S(2)}) collective-permute-start(bf16[4,32,512]{2,1,0:T(8,128)(2,1)S(1)} %get-tuple-element.147), channel_id=1, source_target_pairs={{0,8},{1,9},{2,10},{3,11},{4,12},{5,13},{6,14},{7,15},{8,0},{9,1},... | collective-permute-start | bytes 393224 | tf_op jit(solution)/shard_map/ppermute | solution.py:493
  97.3 11.3 %collective-permute-start.24 = (bf16[3,32,512]{2,1,0:T(8,128)(2,1)S(1)}, bf16[3,32,512]{2,1,0:T(8,128)(2,1)S(1)}, u32[]{:S(2)}, u32[]{:S(2)}) collective-permute-start(bf16[3,32,512]{2,1,0:T(8,128)(2,1)S(1)} %shard_map.191.refs_1_), channel_id=1, source_target_pairs={{0,8},{1,9},{2,10},{3,11},{4,12},{5,13},{6,14},{7,15},{8,0},{9,1},... | collective-permute-start | bytes 294920 | tf_op jit(solution)/shard_map/ppermute | solution.py:493
  107.2 8.0 %collective-permute-start.17 = (bf16[4,32,512]{2,1,0:T(8,128)(2,1)S(1)}, bf16[4,32,512]{2,1,0:T(8,128)(2,1)S(1)}, u32[]{:S(2)}, u32[]{:S(2)}) collective-permute-start(bf16[4,32,512]{2,1,0:T(8,128)(2,1)S(1)} %shard_map.187.refs_1_.refs_3_), channel_id=1, source_target_pairs={{0,8},{1,9},{2,10},{3,11},{4,12},{5,13},{6,14},{7,15},{8,0},{9,1},... | collective-permute-start | bytes 393224 | tf_op jit(solution)/shard_map/ppermute | solution.py:493
  108.6 10.3 %collective-permute-start.25 = (bf16[3,64,512]{2,1,0:T(8,128)(2,1)S(1)}, bf16[3,64,512]{2,1,0:T(8,128)(2,1)S(1)}, u32[]{:S(2)}, u32[]{:S(2)}) collective-permute-start(bf16[3,64,512]{2,1,0:T(8,128)(2,1)S(1)} %shard_map.192.refs_1_), channel_id=1, source_target_pairs={{0,4},{1,5},{2,6},{3,7},{4,0},{5,1},{6,2},{7,3},{8,12},{9,13},{10,... | collective-permute-start | bytes 589832 | tf_op jit(solution)/shard_map/ppermute | solution.py:493
  109.6 9.4 %collective-permute-start.18 = (bf16[128,512]{1,0:T(8,128)(2,1)S(1)}, bf16[128,512]{1,0:T(8,128)(2,1)S(1)}, u32[]{:S(2)}, u32[]{:S(2)}) collective-permute-start(bf16[128,512]{1,0:T(8,128)(2,1)S(1)} %get-tuple-element.114.refs_13_.refs_8_), channel_id=1, source_target_pairs={{1,0},{2,1},{3,2},{4,3},{5,4},{6,5},{7,6},{8,7},{9,8},{10,9},{11,1... | collective-permute-start | bytes 393224 | tf_op jit(solution)/shard_map/ppermute | solution.py:22
  110.9 9.6 %collective-permute-start.19 = (bf16[128,512]{1,0:T(8,128)(2,1)S(1)}, bf16[128,512]{1,0:T(8,128)(2,1)S(1)}, u32[]{:S(2)}, u32[]{:S(2)}) collective-permute-start(bf16[128,512]{1,0:T(8,128)(2,1)S(1)} %get-tuple-element.115.refs_14_.refs_9_), channel_id=1, source_target_pairs={{15,0},{0,1},{1,2},{2,3},{3,4},{4,5},{5,6},{6,7},{7,8},{8,9},{9,10... | collective-permute-start | bytes 393224 | tf_op jit(solution)/shard_map/ppermute | solution.py:22
  110.9 9.6 %collective-permute-start.20 = (bf16[128,512]{1,0:T(8,128)(2,1)S(1)}, bf16[128,512]{1,0:T(8,128)(2,1)S(1)}, u32[]{:S(2)}, u32[]{:S(2)}) collective-permute-start(bf16[128,512]{1,0:T(8,128)(2,1)S(1)} %get-tuple-element.116.refs_15_.refs_10_), channel_id=1, source_target_pairs={{2,0},{3,1},{4,2},{5,3},{6,4},{7,5},{8,6},{9,7},{10,8},{11,9},{12,... | collective-permute-start | bytes 393224 | tf_op jit(solution)/shard_map/ppermute | solution.py:22
  115.2 9.0 %collective-permute-start.21 = (bf16[128,512]{1,0:T(8,128)(2,1)S(1)}, bf16[128,512]{1,0:T(8,128)(2,1)S(1)}, u32[]{:S(2)}, u32[]{:S(2)}) collective-permute-start(bf16[128,512]{1,0:T(8,128)(2,1)S(1)} %get-tuple-element.117.refs_16_.refs_11_), channel_id=1, source_target_pairs={{14,0},{15,1},{0,2},{1,3},{2,4},{3,5},{4,6},{5,7},{6,8},{7,9},{8,1... | collective-permute-start | bytes 393224 | tf_op jit(solution)/shard_map/ppermute | solution.py:22
  118.9 8.4 %collective-permute-start.22 = (bf16[4,64,512]{2,1,0:T(8,128)(2,1)S(1)}, bf16[4,64,512]{2,1,0:T(8,128)(2,1)S(1)}, u32[]{:S(2)}, u32[]{:S(2)}) collective-permute-start(bf16[4,64,512]{2,1,0:T(8,128)(2,1)S(1)} %shard_map.188.refs_5_.refs_3_.refs_1_), channel_id=1, source_target_pairs={{0,4},{1,5},{2,6},{3,7},{4,0},{5,1},{6,2},{7,3},{8,12},{9,13},{10,... | collective-permute-start | bytes 786440 | tf_op jit(solution)/shard_map/ppermute | solution.py:493
  119.0 12.6 %collective-permute-start.26 = (bf16[3,128,512]{2,1,0:T(8,128)(2,1)S(1)}, bf16[3,128,512]{2,1,0:T(8,128)(2,1)S(1)}, u32[]{:S(2)}, u32[]{:S(2)}) collective-permute-start(bf16[3,128,512]{2,1,0:T(8,128)(2,1)S(1)} %shard_map.193.refs_1_), channel_id=1, source_target_pairs={{0,2},{1,3},{2,0},{3,1},{4,6},{5,7},{6,4},{7,5},{8,10},{9,11},{10,... | collective-permute-start | bytes 1179656 | tf_op jit(solution)/shard_map/ppermute | solution.py:493
  131.7 14.2 %collective-permute-start.27 = (bf16[4,128,512]{2,1,0:T(8,128)(2,1)S(1)}, bf16[4,128,512]{2,1,0:T(8,128)(2,1)S(1)}, u32[]{:S(2)}, u32[]{:S(2)}) collective-permute-start(bf16[4,128,512]{2,1,0:T(8,128)(2,1)S(1)} %shard_map.194.refs_1_), channel_id=1, source_target_pairs={{0,2},{1,3},{2,0},{3,1},{4,6},{5,7},{6,4},{7,5},{8,10},{9,11},{10,... | collective-permute-start | bytes 1572872 | tf_op jit(solution)/shard_map/ppermute | solution.py:493
  132.7 1.8 %collective-permute-start.28 = (bf16[3,128,512]{2,1,0:T(8,128)(2,1)S(1)}, bf16[3,128,512]{2,1,0:T(8,128)(2,1)S(1)}, u32[]{:S(2)}, u32[]{:S(2)}) collective-permute-start(bf16[3,128,512]{2,1,0:T(8,128)(2,1)S(1)} %shard_map.193.refs_1_), channel_id=1, source_target_pairs={{0,1},{1,0},{2,3},{3,2},{4,5},{5,4},{6,7},{7,6},{8,9},{9,8},{10,11... | collective-permute-start | bytes 1179656 | tf_op jit(solution)/shard_map/ppermute | solution.py:493
  133.1 1.9 %collective-permute-start.29 = (bf16[3,128,512]{2,1,0:T(8,128)(2,1)S(1)}, bf16[3,128,512]{2,1,0:T(8,128)(2,1)S(1)}, u32[]{:S(2)}, u32[]{:S(2)}) collective-permute-start(bf16[3,128,512]{2,1,0:T(8,128)(2,1)S(1)} %shard_map.195.refs_2_), channel_id=1, source_target_pairs={{0,1},{1,0},{2,3},{3,2},{4,5},{5,4},{6,7},{7,6},{8,9},{9,8},{10,11... | collective-permute-start | bytes 1179656 | tf_op jit(solution)/shard_map/ppermute | solution.py:493
  133.2 12.6 %collective-permute-start.30 = (bf16[4,128,512]{2,1,0:T(8,128)(2,1)S(1)}, bf16[4,128,512]{2,1,0:T(8,128)(2,1)S(1)}, u32[]{:S(2)}, u32[]{:S(2)}) collective-permute-start(bf16[4,128,512]{2,1,0:T(8,128)(2,1)S(1)} %shard_map.194.refs_1_), channel_id=1, source_target_pairs={{0,1},{1,0},{2,3},{3,2},{4,5},{5,4},{6,7},{7,6},{8,9},{9,8},{10,11... | collective-permute-start | bytes 1572872 | tf_op jit(solution)/shard_map/ppermute | solution.py:493
  145.8 1.9 %collective-permute-start.31 = (bf16[4,128,512]{2,1,0:T(8,128)(2,1)S(1)}, bf16[4,128,512]{2,1,0:T(8,128)(2,1)S(1)}, u32[]{:S(2)}, u32[]{:S(2)}) collective-permute-start(bf16[4,128,512]{2,1,0:T(8,128)(2,1)S(1)} %shard_map.197.refs_2_), channel_id=1, source_target_pairs={{0,1},{1,0},{2,3},{3,2},{4,5},{5,4},{6,7},{7,6},{8,9},{9,8},{10,11... | collective-permute-start | bytes 1572872 | tf_op jit(solution)/shard_map/ppermute | solution.py:493

commit v16 on v15

--- a/solution.py
+++ b/solution.py
@@ -856,9 +856,7 @@
         grad_nodes = node_output([piece_edge])
         piece_node = gather_stage(me, piece_node, over(piece_node, 4), 4, [piece_edge])
         other_node = over(piece_node, 2)
-        piece_edge = gather_stage(
-            me, piece_edge, over(piece_edge, 4), 4, [other_node, in_hbm(grad_nodes)]
-        )
+        piece_edge = gather_stage(me, piece_edge, over(piece_edge, 4), 4, [in_hbm(grad_nodes)])
         other_node = held_until(other_node, [piece_edge])
         grad_n1, grad_n2 = join_stage(me, piece_node, other_node, first, node_blocks, node_shapes)
         other_edge = held_until(over(piece_edge, 2), [in_hbm(grad_n2)])

time: 149 us -> 146 us (0.980)
  waiting for transfers between devices: 68.3 us -> 63.6 us
  starting transfers between devices: 35.3 us -> 37.1 us
    ppermute x18, waiting for transfers between devices: 49.8 us -> 45.1 us  [in_group(): return lax.ppermute(block, axis, route)]
    ppermute x18, starting transfers between devices: 18.6 us -> 20.3 us  [in_group(): return lax.ppermute(block, axis, route)]
  transfers between devices with their start and end apart: 32 -> 32, of which waited for: 20 -> 19; matrix products, arithmetic and copies ran while one was open for 0% -> 0% of each run, Pallas kernels for 13% -> 13%
where the time goes in v16:
time: 146 us
  waiting for transfers between devices  63.6 us (44%)
  starting transfers between devices  37.1 us (25%)
  Pallas kernels  31 us (21%)
  blocking collectives  13.7 us (9%)
    ppermute x18, waiting for transfers between devices, in_group(): return lax.ppermute(block, axis, route)  45.1 us
    pallas_call x25, Pallas kernels, call(): pl.pallas_call(kernel, out_shape=[(pltpu.HBM if i in last else pltpu.VMEM...  27.8 us
    ppermute x18, starting transfers between devices, in_group(): return lax.ppermute(block, axis, route)  20.3 us
    ppermute x14, waiting for transfers between devices, passed_along(): return lax.ppermute(block, axis, route)  18.5 us
    ppermute x14, starting transfers between devices, passed_along(): return lax.ppermute(block, axis, route)  16.8 us
    all_to_all x1, blocking collectives, local(): ids = lax.all_to_all(ids, 'band', 0, 0, tiled=True)  13.7 us
    pallas_call x1, Pallas kernels, loaded(): pl.pallas_call(functools.partial(load_kernel, count), out_shape=[pltpu.VM...  3.24 us
  transfers between devices with their start and end apart: 32, of which 19 were waited for; matrix products, arithmetic and copies ran while one was open for 0% of the time, Pallas kernels for 13%

profile of v16, /device:TPU:0, one launch (start us, length us, event | category | flops | bytes accessed | tf_op | source)
XLA Modules:
  0.0 146.2 jit_solution(17769785169038418575)
XLA Ops:
  0.6 3.2 %shard_map.170 = (bf16[320,512]{1,0:T(8,128)(2,1)S(1)}, s32[11,1,128]{2,1,0:T(1,128)S(1)}, s32[11,1,128]{2,1,0:T(1,128)S(1)}, bf16[11,128,512]{2,1,0:T(8,128)(2,...) custom-call(s32[1]{0:T(128)} %bitcast.refs_0_.refs_2_, ...), custom_call_target="tpu_custom_call" | custom-call | flops 1 | bytes 1 | tf_op jit(solution)/shard_map/pallas_call | solution.py:121
  3.9 13.7 %all_to_all.5.refs_2_.refs_4_ = s32[16,1,256]{2,1,0:T(1,128)S(1)} all-to-all(s32[16,1,256]{2,1,0:T(1,128)S(1)} %shard_map.171), channel_id=1, replica_groups=mesh['groups'=2,'band'=16] {'band'}, dimensions={0} | all-to-all | bytes 32768 | tf_op jit(solution)/shard_map/all_to_all | solution.py:638
  17.6 0.8 shard_map.172
  18.6 1.2 collective-permute-start.2
  19.8 0.8 collective-permute-start.6
  20.6 3.3 %collective-permute-start.3 = (bf16[128,512]{1,0:T(8,128)(2,1)S(1)}, bf16[128,512]{1,0:T(8,128)(2,1)S(1)}, u32[]{:S(2)}, u32[]{:S(2)}) collective-permute-start(bf16[128,512]{1,0:T(8,128)(2,1)S(1)} %get-tuple-element.96), channel_id=1, source_target_pairs={{2,0},{3,1},{4,2},{5,3},{6,4},{7,5},{8,6},{9,7},{10,8},{11,9},{12,... | collective-permute-start | bytes 393224 | tf_op jit(solution)/shard_map/ppermute | solution.py:22
  23.9 3.8 %collective-permute-done.2.refs_8_.refs_7_ = bf16[128,512]{1,0:T(8,128)(2,1)S(1)} collective-permute-done((bf16[128,512]{1,0:T(8,128)(2,1)S(1)}, bf16[128,512]{1,0:T(8,128)(2,1)S(1)}, u32[]{:S(2)}, u32[]{:S(2)}) %collective-permute-start.2) | collective-permute-done | bytes 131104 | tf_op jit(solution)/shard_map/ppermute | solution.py:22
  27.8 4.5 %shard_map.173 = (bf16[1408,320]{1,0:T(8,128)(2,1)S(1)}, bf16[320,1408]{1,0:T(8,128)(2,1)S(1)}, f32[1408,128]{1,0:T(8,128)S(1)}, f32[1024,512]{1,0:T(8,128)S(1)}...) custom-call(bf16[11,128,512]{2,1,0:T(8,128)(2,1)S(1)} %get-tuple-ele, ...), custom_call_target="tpu_custom_call" | custom-call | flops 1 | bytes 1 | tf_op jit(solution)/shard_map/pallas_call | solution.py:90
  32.3 2.7 %collective-permute-done.refs_6_.refs_5_ = bf16[128,512]{1,0:T(8,128)(2,1)S(1)} collective-permute-done((bf16[128,512]{1,0:T(8,128)(2,1)S(1)}, bf16[128,512]{1,0:T(8,128)(2,1)S(1)}, u32[]{:S(2)}, u32[]{:S(2)}) %collective-permute-start) | collective-permute-done | bytes 131104 | tf_op jit(solution)/shard_map/ppermute | solution.py:22
  35.0 1.6 %shard_map.174 = (bf16[512,512]{1,0:T(8,128)(2,1)S(1)}, f32[512,512]{1,0:T(8,128)S(1)}, f32[512,512]{1,0:T(8,128)S(1)}, f32[512,128]{1,0:T(8,128)S(1)}, f32[320,512]{1,0:T(8,128)S(1)}) custom-call(f32[1024,512]{1,0:T(8,128)S(1)} %get-tuple-element.89.refs_0_.refs_1_, f32[1408,128]{1,0:T(8,128)S(1)} %get-tuple-element.90.refs_1_.refs_2_.refs_3_, ...), custom_call_target="tpu_custom_call" | custom-call | flops 1 | bytes 1 | tf_op jit(solution)/shard_map/pallas_call | solution.py:90
  36.6 2.8 %collective-permute-done.5.refs_13_.refs_10_ = bf16[128,512]{1,0:T(8,128)(2,1)S(1)} collective-permute-done((bf16[128,512]{1,0:T(8,128)(2,1)S(1)}, bf16[128,512]{1,0:T(8,128)(2,1)S(1)}, u32[]{:S(2)}, u32[]{:S(2)}) %collective-permute-start.5) | collective-permute-done | bytes 131104 | tf_op jit(solution)/shard_map/ppermute | solution.py:22
  39.4 4.5 %shard_map.175 = (bf16[128,512]{1,0:T(8,128)(2,1)S(1)}, bf16[128,512]{1,0:T(8,128)(2,1)S(1)}, bf16[256,512]{1,0:T(8,128)(2,1)S(1)}, bf16[512,512]{1,0:T(8,128)(2...) custom-call(bf16[11,128,512]{2,1,0:T(8,128)(2,1)S(1)} %get-tuple-ele, ...), custom_call_target="tpu_custom_call" | custom-call | flops 1 | bytes 1 | tf_op jit(solution)/shard_map/pallas_call | solution.py:90
  43.9 1.3 shard_map.178
  45.3 4.7 %collective-permute-start.9 = (bf16[256,512]{1,0:T(8,128)(2,1)S(1)}, bf16[256,512]{1,0:T(8,128)(2,1)S(1)}, u32[]{:S(2)}, u32[]{:S(2)}) collective-permute-start(bf16[256,512]{1,0:T(8,128)(2,1)S(1)} %get-tuple-element.120.refs_19_.refs_14_), channel_id=1, source_target_pairs={{8,0},{9,1},{10,2},{11,3},{12,4},{13,5},{14,6},{15,7},{0,8},{1,9},... | collective-permute-start | bytes 786440 | tf_op jit(solution)/shard_map/ppermute | solution.py:22
  50.0 1.7 %collective-permute-start.7 = (bf16[128,512]{1,0:T(8,128)(2,1)S(1)}, bf16[128,512]{1,0:T(8,128)(2,1)S(1)}, u32[]{:S(2)}, u32[]{:S(2)}) collective-permute-start(bf16[128,512]{1,0:T(8,128)(2,1)S(1)} %get-tuple-element.118.refs_17_.refs_12_), channel_id=1, source_target_pairs={{4,0},{5,1},{6,2},{7,3},{8,4},{9,5},{10,6},{11,7},{12,8},{13,9},{1... | collective-permute-start | bytes 393224 | tf_op jit(solution)/shard_map/ppermute | solution.py:22
  52.0 2.1 %shard_map.176 = (bf16[896,512]{1,0:T(8,128)(2,1)S(1)}, bf16[384,512]{1,0:T(8,128)(2,1)S(1)}, bf16[128,512]{1,0:T(8,128)(2,1)S(1)}, bf16[128,512]{1,0:T(8,128)(2...) custom-call(bf16[11,128,512]{2,1,0:T(8,128)(2,1)S(1)} %get-tuple-element.81.refs_0_.refs_1_, ...), custom_call_target="tpu_custom_call" | custom-call | flops 1 | bytes 1 | tf_op jit(solution)/shard_map/pallas_call | solution.py:90
  54.1 3.9 %shard_map.177 = (f32[4,256,512]{2,1,0:T(8,128)S(1)}, bf16[4,256,512]{2,1,0:T(8,128)(2,1)S(1)}, bf16[320,512]{1,0:T(8,128)(2,1)S(1)}) custom-call(bf16[11,128,512]{2,1,0:T(8,128)(2,1)S(1)} %get-tuple-element.82.refs_0_, bf16[320,1408]{1,0:T(8,128)(2,1)S(1)} %get-tuple-element.92.refs_2_.refs_4_.refs_1_, s32[1]{0:T(128)} %bitcast.refs_0_.refs_2_, ...), custom_call_target="tpu_custom_call" | custom-call | flops 1 | bytes 1 | tf_op jit(solution)/shard_map/pallas_call | solution.py:90
  58.2 2.1 %collective-permute-start.12 = (bf16[3,128,512]{2,1,0:T(8,128)(2,1)S(1)}, bf16[3,128,512]{2,1,0:T(8,128)(2,1)S(1)}, u32[]{:S(2)}, u32[]{:S(2)}) collective-permute-start(bf16[3,128,512]{2,1,0:T(8,128)(2,1)S(1)} %get-tuple-element.138), channel_id=1, source_target_pairs={{0,2},{1,3},{2,0},{3,1},{4,6},{5,7},{6,4},{7,5},{8,10},{9,11},{10,... | collective-permute-start | bytes 1179656 | tf_op jit(solution)/shard_map/ppermute | solution.py:493
  60.3 3.8 %collective-permute-done.8.refs_2_.refs_11_ = bf16[128,512]{1,0:T(8,128)(2,1)S(1)} collective-permute-done((bf16[128,512]{1,0:T(8,128)(2,1)S(1)}, bf16[128,512]{1,0:T(8,128)(2,1)S(1)}, u32[]{:S(2)}, u32[]{:S(2)}) %collective-permute-start.8) | collective-permute-done | bytes 131104 | tf_op jit(solution)/shard_map/ppermute | solution.py:22
  64.0 1.5 %collective-permute-done.9.refs_3_.refs_12_ = bf16[256,512]{1,0:T(8,128)(2,1)S(1)} collective-permute-done((bf16[256,512]{1,0:T(8,128)(2,1)S(1)}, bf16[256,512]{1,0:T(8,128)(2,1)S(1)}, u32[]{:S(2)}, u32[]{:S(2)}) %collective-permute-start.9) | collective-permute-done | bytes 262176 | tf_op jit(solution)/shard_map/ppermute | solution.py:22
  65.6 3.5 %shard_map.181 = (bf16[11,128,512]{2,1,0:T(8,128)(2,1)}, bf16[11,128,512]{2,1,0:T(8,128)(2,1)}) custom-call(bf16[11,128,512]{2,1,0:T(8,128)(2,1)S(1)} %get-tuple-element.82.refs_0_, bf16[11,128,512]{2,1,0:T(8,128)(2,1)S(1)} %get-tuple-element.81.refs_0_.refs_1_, bf16[1536,512]{1,0:T(8,128)(2,1)S(1)} %get-tuple-element.85.refs_4_.refs_6_.refs_2_.refs_3_, ...), custom_call_target="tpu_custom_call" | custom-call | flops 20000000000 | bytes 1 | tf_op jit(solution)/shard_map/pallas_call | solution.py:90
  69.7 2.9 %collective-permute-start.13 = (bf16[4,128,512]{2,1,0:T(8,128)(2,1)S(1)}, bf16[4,128,512]{2,1,0:T(8,128)(2,1)S(1)}, u32[]{:S(2)}, u32[]{:S(2)}) collective-permute-start(bf16[4,128,512]{2,1,0:T(8,128)(2,1)S(1)} %get-tuple-element.141), channel_id=1, source_target_pairs={{0,2},{1,3},{2,0},{3,1},{4,6},{5,7},{6,4},{7,5},{8,10},{9,11},{10,... | collective-permute-start | bytes 1572872 | tf_op jit(solution)/shard_map/ppermute | solution.py:493
  72.6 3.0 %collective-permute-start.14 = (bf16[3,64,512]{2,1,0:T(8,128)(2,1)S(1)}, bf16[3,64,512]{2,1,0:T(8,128)(2,1)S(1)}, u32[]{:S(2)}, u32[]{:S(2)}) collective-permute-start(bf16[3,64,512]{2,1,0:T(8,128)(2,1)S(1)} %get-tuple-element.142), channel_id=1, source_target_pairs={{0,4},{1,5},{2,6},{3,7},{4,0},{5,1},{6,2},{7,3},{8,12},{9,13},{10,... | collective-permute-start | bytes 589832 | tf_op jit(solution)/shard_map/ppermute | solution.py:493
  75.6 5.3 %collective-permute-done.14.refs_2_ = bf16[3,64,512]{2,1,0:T(8,128)(2,1)S(1)} collective-permute-done((bf16[3,64,512]{2,1,0:T(8,128)(2,1)S(1)}, bf16[3,64,512]{2,1,0:T(8,128)(2,1)S(1)}, u32[]{:S(2)}, u32[]{:S(2)}) %collective-permute-start.14) | collective-permute-done | bytes 196640 | tf_op jit(solution)/shard_map/ppermute | solution.py:493
  80.9 4.3 %collective-permute-done.13.refs_2_ = bf16[4,128,512]{2,1,0:T(8,128)(2,1)S(1)} collective-permute-done((bf16[4,128,512]{2,1,0:T(8,128)(2,1)S(1)}, bf16[4,128,512]{2,1,0:T(8,128)(2,1)S(1)}, u32[]{:S(2)}, u32[]{:S(2)}) %collective-permute-start.13) | collective-permute-done | bytes 524320 | tf_op jit(solution)/shard_map/ppermute | solution.py:493
  85.3 3.0 %collective-permute-start.15 = (bf16[4,64,512]{2,1,0:T(8,128)(2,1)S(1)}, bf16[4,64,512]{2,1,0:T(8,128)(2,1)S(1)}, u32[]{:S(2)}, u32[]{:S(2)}) collective-permute-start(bf16[4,64,512]{2,1,0:T(8,128)(2,1)S(1)} %get-tuple-element.145), channel_id=1, source_target_pairs={{0,4},{1,5},{2,6},{3,7},{4,0},{5,1},{6,2},{7,3},{8,12},{9,13},{10,... | collective-permute-start | bytes 786440 | tf_op jit(solution)/shard_map/ppermute | solution.py:493
  88.3 8.5 %collective-permute-done.15.refs_2_ = bf16[4,64,512]{2,1,0:T(8,128)(2,1)S(1)} collective-permute-done((bf16[4,64,512]{2,1,0:T(8,128)(2,1)S(1)}, bf16[4,64,512]{2,1,0:T(8,128)(2,1)S(1)}, u32[]{:S(2)}, u32[]{:S(2)}) %collective-permute-start.15) | collective-permute-done | bytes 262176 | tf_op jit(solution)/shard_map/ppermute | solution.py:493
  97.3 2.7 %collective-permute-start.25 = (bf16[3,32,512]{2,1,0:T(8,128)(2,1)S(1)}, bf16[3,32,512]{2,1,0:T(8,128)(2,1)S(1)}, u32[]{:S(2)}, u32[]{:S(2)}) collective-permute-start(bf16[3,32,512]{2,1,0:T(8,128)(2,1)S(1)} %shard_map.192.refs_1_), channel_id=1, source_target_pairs={{0,8},{1,9},{2,10},{3,11},{4,12},{5,13},{6,14},{7,15},{8,0},{9,1},... | collective-permute-start | bytes 294920 | tf_op jit(solution)/shard_map/ppermute | solution.py:493
  99.9 7.3 %collective-permute-done.16.refs_2_ = bf16[4,32,512]{2,1,0:T(8,128)(2,1)S(1)} collective-permute-done((bf16[4,32,512]{2,1,0:T(8,128)(2,1)S(1)}, bf16[4,32,512]{2,1,0:T(8,128)(2,1)S(1)}, u32[]{:S(2)}, u32[]{:S(2)}) %collective-permute-start.16) | collective-permute-done | bytes 131104 | tf_op jit(solution)/shard_map/ppermute | solution.py:493
  107.3 1.3 collective-permute-done.25.refs_2_
  108.6 0.9 collective-permute-start.26
  109.6 1.3 collective-permute-start.18
  110.9 2.2 %collective-permute-start.20 = (bf16[128,512]{1,0:T(8,128)(2,1)S(1)}, bf16[128,512]{1,0:T(8,128)(2,1)S(1)}, u32[]{:S(2)}, u32[]{:S(2)}) collective-permute-start(bf16[128,512]{1,0:T(8,128)(2,1)S(1)} %get-tuple-element.116.refs_15_.refs_10_), channel_id=1, source_target_pairs={{2,0},{3,1},{4,2},{5,3},{6,4},{7,5},{8,6},{9,7},{10,8},{11,9},{12,... | collective-permute-start | bytes 393224 | tf_op jit(solution)/shard_map/ppermute | solution.py:22
  113.0 2.2 %collective-permute-done.17.refs_2_ = bf16[4,32,512]{2,1,0:T(8,128)(2,1)S(1)} collective-permute-done((bf16[4,32,512]{2,1,0:T(8,128)(2,1)S(1)}, bf16[4,32,512]{2,1,0:T(8,128)(2,1)S(1)}, u32[]{:S(2)}, u32[]{:S(2)}) %collective-permute-start.17) | collective-permute-done | bytes 131104 | tf_op jit(solution)/shard_map/ppermute | solution.py:493
  115.2 1.0 collective-permute-start.21
  116.8 2.2 %collective-permute-done.26.refs_2_ = bf16[3,64,512]{2,1,0:T(8,128)(2,1)S(1)} collective-permute-done((bf16[3,64,512]{2,1,0:T(8,128)(2,1)S(1)}, bf16[3,64,512]{2,1,0:T(8,128)(2,1)S(1)}, u32[]{:S(2)}, u32[]{:S(2)}) %collective-permute-start.26) | collective-permute-done | bytes 196640 | tf_op jit(solution)/shard_map/ppermute | solution.py:493
  119.0 1.4 collective-permute-start.27
  120.4 3.8 %collective-permute-done.21.refs_9_ = bf16[128,512]{1,0:T(8,128)(2,1)S(1)} collective-permute-done((bf16[128,512]{1,0:T(8,128)(2,1)S(1)}, bf16[128,512]{1,0:T(8,128)(2,1)S(1)}, u32[]{:S(2)}, u32[]{:S(2)}) %collective-permute-start.21) | collective-permute-done | bytes 131104 | tf_op jit(solution)/shard_map/ppermute | solution.py:22
  124.2 1.6 %shard_map.190.refs_3_ = bf16[320,512]{1,0:T(8,128)(2,1)} custom-call(s32[1]{0:T(128)} %bitcast.refs_0_.refs_2_, f32[320,512]{1,0:T(8,128)S(1)} %shard_map.189.refs_1_, bf16[1536,512]{1,0:T(8,128)(2,1)S(1)} %get-tuple-element.85.refs_4_.refs_6_.refs_2_.refs_3_, s32[11,1,128]{2,1,0:T(1,128)S(1)} %get-tuple-element.84.refs_1_.refs_2_.refs_3_, ...), custom_call_target="tpu_custom_call" | custom-call | flops 20000000000 | bytes 1 | tf_op jit(solution)/shard_map/pallas_call | solution.py:90
  125.9 1.5 %collective-permute-done.22.refs_2_ = bf16[4,64,512]{2,1,0:T(8,128)(2,1)S(1)} collective-permute-done((bf16[4,64,512]{2,1,0:T(8,128)(2,1)S(1)}, bf16[4,64,512]{2,1,0:T(8,128)(2,1)S(1)}, u32[]{:S(2)}, u32[]{:S(2)}) %collective-permute-start.22) | collective-permute-done | bytes 262176 | tf_op jit(solution)/shard_map/ppermute | solution.py:493
  127.4 2.4 %collective-permute-start.23 = (bf16[4,128,512]{2,1,0:T(8,128)(2,1)S(1)}, bf16[4,128,512]{2,1,0:T(8,128)(2,1)S(1)}, u32[]{:S(2)}, u32[]{:S(2)}) collective-permute-start(bf16[4,128,512]{2,1,0:T(8,128)(2,1)S(1)} %shard_map.191.refs_1_), channel_id=1, source_target_pairs={{0,2},{1,3},{2,0},{3,1},{4,6},{5,7},{6,4},{7,5},{8,10},{9,11},{10,... | collective-permute-start | bytes 1572872 | tf_op jit(solution)/shard_map/ppermute | solution.py:493
  129.8 1.8 %collective-permute-done.27.refs_0_ = bf16[3,128,512]{2,1,0:T(8,128)(2,1)S(1)} collective-permute-done((bf16[3,128,512]{2,1,0:T(8,128)(2,1)S(1)}, bf16[3,128,512]{2,1,0:T(8,128)(2,1)S(1)}, u32[]{:S(2)}, u32[]{:S(2)}) %collective-permute-start.27) | collective-permute-done | bytes 393248 | tf_op jit(solution)/shard_map/ppermute | solution.py:493
  131.6 1.0 collective-permute-start.29
  132.6 1.3 collective-permute-done.29.refs_4_
  134.0 1.3 shard_map.196
  135.2 7.6 %collective-permute-done.23.refs_0_ = bf16[4,128,512]{2,1,0:T(8,128)(2,1)S(1)} collective-permute-done((bf16[4,128,512]{2,1,0:T(8,128)(2,1)S(1)}, bf16[4,128,512]{2,1,0:T(8,128)(2,1)S(1)}, u32[]{:S(2)}, u32[]{:S(2)}) %collective-permute-start.23) | collective-permute-done | bytes 524320 | tf_op jit(solution)/shard_map/ppermute | solution.py:493
  143.1 1.6 %collective-permute-done.31.refs_4_ = bf16[4,128,512]{2,1,0:T(8,128)(2,1)S(1)} collective-permute-done((bf16[4,128,512]{2,1,0:T(8,128)(2,1)S(1)}, bf16[4,128,512]{2,1,0:T(8,128)(2,1)S(1)}, u32[]{:S(2)}, u32[]{:S(2)}) %collective-permute-start.31) | collective-permute-done | bytes 524320 | tf_op jit(solution)/shard_map/ppermute | solution.py:493
  144.8 1.5 shard_map.198
  (46 shorter events, 3.2 us)
Async XLA Ops:
  18.4 5.5 %collective-permute-start.1 = (bf16[128,512]{1,0:T(8,128)(2,1)S(1)}, bf16[128,512]{1,0:T(8,128)(2,1)S(1)}, u32[]{:S(2)}, u32[]{:S(2)}) collective-permute-start(bf16[128,512]{1,0:T(8,128)(2,1)S(1)} %get-tuple-element.94), channel_id=1, source_target_pairs={{1,0},{2,1},{3,2},{4,3},{5,4},{6,5},{7,6},{8,7},{9,8},{10,9},{11,1... | collective-permute-start | bytes 393224 | tf_op jit(solution)/shard_map/ppermute | solution.py:22
  18.6 9.1 %collective-permute-start.2 = (bf16[128,512]{1,0:T(8,128)(2,1)S(1)}, bf16[128,512]{1,0:T(8,128)(2,1)S(1)}, u32[]{:S(2)}, u32[]{:S(2)}) collective-permute-start(bf16[128,512]{1,0:T(8,128)(2,1)S(1)} %get-tuple-element.95), channel_id=1, source_target_pairs={{14,0},{15,1},{0,2},{1,3},{2,4},{3,5},{4,6},{5,7},{6,8},{7,9},{8,1... | collective-permute-start | bytes 393224 | tf_op jit(solution)/shard_map/ppermute | solution.py:22
  19.8 19.6 %collective-permute-start.6 = (bf16[256,512]{1,0:T(8,128)(2,1)S(1)}, bf16[256,512]{1,0:T(8,128)(2,1)S(1)}, u32[]{:S(2)}, u32[]{:S(2)}) collective-permute-start(bf16[256,512]{1,0:T(8,128)(2,1)S(1)} %get-tuple-element.103), channel_id=1, source_target_pairs={{8,0},{9,1},{10,2},{11,3},{12,4},{13,5},{14,6},{15,7},{0,8},{1,9},... | collective-permute-start | bytes 786440 | tf_op jit(solution)/shard_map/ppermute | solution.py:22
  20.6 11.6 %collective-permute-start.3 = (bf16[128,512]{1,0:T(8,128)(2,1)S(1)}, bf16[128,512]{1,0:T(8,128)(2,1)S(1)}, u32[]{:S(2)}, u32[]{:S(2)}) collective-permute-start(bf16[128,512]{1,0:T(8,128)(2,1)S(1)} %get-tuple-element.96), channel_id=1, source_target_pairs={{2,0},{3,1},{4,2},{5,3},{6,4},{7,5},{8,6},{9,7},{10,8},{11,9},{12,... | collective-permute-start | bytes 393224 | tf_op jit(solution)/shard_map/ppermute | solution.py:22
  23.9 11.1 %collective-permute-start = (bf16[128,512]{1,0:T(8,128)(2,1)S(1)}, bf16[128,512]{1,0:T(8,128)(2,1)S(1)}, u32[]{:S(2)}, u32[]{:S(2)}) collective-permute-start(bf16[128,512]{1,0:T(8,128)(2,1)S(1)} %get-tuple-element.88.refs_7_), channel_id=1, source_target_pairs={{15,0},{0,1},{1,2},{2,3},{3,4},{4,5},{5,6},{6,7},{7,8},{8,9},{9,10... | collective-permute-start | bytes 393224 | tf_op jit(solution)/shard_map/ppermute | solution.py:22
  23.9 12.7 %collective-permute-start.4 = (bf16[128,512]{1,0:T(8,128)(2,1)S(1)}, bf16[128,512]{1,0:T(8,128)(2,1)S(1)}, u32[]{:S(2)}, u32[]{:S(2)}) collective-permute-start(bf16[128,512]{1,0:T(8,128)(2,1)S(1)} %get-tuple-element.101), channel_id=1, source_target_pairs={{12,0},{13,1},{14,2},{15,3},{0,4},{1,5},{2,6},{3,7},{4,8},{5,9},{6... | collective-permute-start | bytes 393224 | tf_op jit(solution)/shard_map/ppermute | solution.py:22
  27.8 11.6 %collective-permute-start.5 = (bf16[128,512]{1,0:T(8,128)(2,1)S(1)}, bf16[128,512]{1,0:T(8,128)(2,1)S(1)}, u32[]{:S(2)}, u32[]{:S(2)}) collective-permute-start(bf16[128,512]{1,0:T(8,128)(2,1)S(1)} %get-tuple-element.102), channel_id=1, source_target_pairs={{4,0},{5,1},{6,2},{7,3},{8,4},{9,5},{10,6},{11,7},{12,8},{13,9},{1... | collective-permute-start | bytes 393224 | tf_op jit(solution)/shard_map/ppermute | solution.py:22
  45.2 12.8 %collective-permute-start.10 = (bf16[3,256,512]{2,1,0:T(8,128)(2,1)S(1)}, bf16[3,256,512]{2,1,0:T(8,128)(2,1)S(1)}, u32[]{:S(2)}, u32[]{:S(2)}) collective-permute-start(bf16[3,256,512]{2,1,0:T(8,128)(2,1)S(1)} %get-tuple-element.133), channel_id=1, source_target_pairs={{0,1},{1,0},{2,3},{3,2},{4,5},{5,4},{6,7},{7,6},{8,9},{9,8},{10,11... | collective-permute-start | bytes 2359304 | tf_op jit(solution)/shard_map/ppermute | solution.py:493
  45.3 20.3 %collective-permute-start.9 = (bf16[256,512]{1,0:T(8,128)(2,1)S(1)}, bf16[256,512]{1,0:T(8,128)(2,1)S(1)}, u32[]{:S(2)}, u32[]{:S(2)}) collective-permute-start(bf16[256,512]{1,0:T(8,128)(2,1)S(1)} %get-tuple-element.120.refs_19_.refs_14_), channel_id=1, source_target_pairs={{8,0},{9,1},{10,2},{11,3},{12,4},{13,5},{14,6},{15,7},{0,8},{1,9},... | collective-permute-start | bytes 786440 | tf_op jit(solution)/shard_map/ppermute | solution.py:22
  50.0 10.3 %collective-permute-start.7 = (bf16[128,512]{1,0:T(8,128)(2,1)S(1)}, bf16[128,512]{1,0:T(8,128)(2,1)S(1)}, u32[]{:S(2)}, u32[]{:S(2)}) collective-permute-start(bf16[128,512]{1,0:T(8,128)(2,1)S(1)} %get-tuple-element.118.refs_17_.refs_12_), channel_id=1, source_target_pairs={{4,0},{5,1},{6,2},{7,3},{8,4},{9,5},{10,6},{11,7},{12,8},{13,9},{1... | collective-permute-start | bytes 393224 | tf_op jit(solution)/shard_map/ppermute | solution.py:22
  51.7 12.4 %collective-permute-start.8 = (bf16[128,512]{1,0:T(8,128)(2,1)S(1)}, bf16[128,512]{1,0:T(8,128)(2,1)S(1)}, u32[]{:S(2)}, u32[]{:S(2)}) collective-permute-start(bf16[128,512]{1,0:T(8,128)(2,1)S(1)} %get-tuple-element.119.refs_18_.refs_13_), channel_id=1, source_target_pairs={{12,0},{13,1},{14,2},{15,3},{0,4},{1,5},{2,6},{3,7},{4,8},{5,9},{6... | collective-permute-start | bytes 393224 | tf_op jit(solution)/shard_map/ppermute | solution.py:22
  58.2 11.3 %collective-permute-start.12 = (bf16[3,128,512]{2,1,0:T(8,128)(2,1)S(1)}, bf16[3,128,512]{2,1,0:T(8,128)(2,1)S(1)}, u32[]{:S(2)}, u32[]{:S(2)}) collective-permute-start(bf16[3,128,512]{2,1,0:T(8,128)(2,1)S(1)} %get-tuple-element.138), channel_id=1, source_target_pairs={{0,2},{1,3},{2,0},{3,1},{4,6},{5,7},{6,4},{7,5},{8,10},{9,11},{10,... | collective-permute-start | bytes 1179656 | tf_op jit(solution)/shard_map/ppermute | solution.py:493
  65.6 3.9 %collective-permute-start.11 = (bf16[4,256,512]{2,1,0:T(8,128)(2,1)S(1)}, bf16[4,256,512]{2,1,0:T(8,128)(2,1)S(1)}, u32[]{:S(2)}, u32[]{:S(2)}) collective-permute-start(bf16[4,256,512]{2,1,0:T(8,128)(2,1)S(1)} %shard_map.180.refs_15_), channel_id=1, source_target_pairs={{0,1},{1,0},{2,3},{3,2},{4,5},{5,4},{6,7},{7,6},{8,9},{9,8},{10,11... | collective-permute-start | bytes 3145736 | tf_op jit(solution)/shard_map/ppermute | solution.py:493
  69.7 15.5 %collective-permute-start.13 = (bf16[4,128,512]{2,1,0:T(8,128)(2,1)S(1)}, bf16[4,128,512]{2,1,0:T(8,128)(2,1)S(1)}, u32[]{:S(2)}, u32[]{:S(2)}) collective-permute-start(bf16[4,128,512]{2,1,0:T(8,128)(2,1)S(1)} %get-tuple-element.141), channel_id=1, source_target_pairs={{0,2},{1,3},{2,0},{3,1},{4,6},{5,7},{6,4},{7,5},{8,10},{9,11},{10,... | collective-permute-start | bytes 1572872 | tf_op jit(solution)/shard_map/ppermute | solution.py:493
  72.6 8.3 %collective-permute-start.14 = (bf16[3,64,512]{2,1,0:T(8,128)(2,1)S(1)}, bf16[3,64,512]{2,1,0:T(8,128)(2,1)S(1)}, u32[]{:S(2)}, u32[]{:S(2)}) collective-permute-start(bf16[3,64,512]{2,1,0:T(8,128)(2,1)S(1)} %get-tuple-element.142), channel_id=1, source_target_pairs={{0,4},{1,5},{2,6},{3,7},{4,0},{5,1},{6,2},{7,3},{8,12},{9,13},{10,... | collective-permute-start | bytes 589832 | tf_op jit(solution)/shard_map/ppermute | solution.py:493
  85.3 11.5 %collective-permute-start.15 = (bf16[4,64,512]{2,1,0:T(8,128)(2,1)S(1)}, bf16[4,64,512]{2,1,0:T(8,128)(2,1)S(1)}, u32[]{:S(2)}, u32[]{:S(2)}) collective-permute-start(bf16[4,64,512]{2,1,0:T(8,128)(2,1)S(1)} %get-tuple-element.145), channel_id=1, source_target_pairs={{0,4},{1,5},{2,6},{3,7},{4,0},{5,1},{6,2},{7,3},{8,12},{9,13},{10,... | collective-permute-start | bytes 786440 | tf_op jit(solution)/shard_map/ppermute | solution.py:493
  88.3 8.9 %collective-permute-start.24 = (bf16[3,32,512]{2,1,0:T(8,128)(2,1)S(1)}, bf16[3,32,512]{2,1,0:T(8,128)(2,1)S(1)}, u32[]{:S(2)}, u32[]{:S(2)}) collective-permute-start(bf16[3,32,512]{2,1,0:T(8,128)(2,1)S(1)} %get-tuple-element.149), channel_id=1, source_target_pairs={{0,8},{1,9},{2,10},{3,11},{4,12},{5,13},{6,14},{7,15},{8,0},{9,1},... | collective-permute-start | bytes 294920 | tf_op jit(solution)/shard_map/ppermute | solution.py:493
  96.9 10.3 %collective-permute-start.16 = (bf16[4,32,512]{2,1,0:T(8,128)(2,1)S(1)}, bf16[4,32,512]{2,1,0:T(8,128)(2,1)S(1)}, u32[]{:S(2)}, u32[]{:S(2)}) collective-permute-start(bf16[4,32,512]{2,1,0:T(8,128)(2,1)S(1)} %get-tuple-element.147), channel_id=1, source_target_pairs={{0,8},{1,9},{2,10},{3,11},{4,12},{5,13},{6,14},{7,15},{8,0},{9,1},... | collective-permute-start | bytes 393224 | tf_op jit(solution)/shard_map/ppermute | solution.py:493
  97.3 11.3 %collective-permute-start.25 = (bf16[3,32,512]{2,1,0:T(8,128)(2,1)S(1)}, bf16[3,32,512]{2,1,0:T(8,128)(2,1)S(1)}, u32[]{:S(2)}, u32[]{:S(2)}) collective-permute-start(bf16[3,32,512]{2,1,0:T(8,128)(2,1)S(1)} %shard_map.192.refs_1_), channel_id=1, source_target_pairs={{0,8},{1,9},{2,10},{3,11},{4,12},{5,13},{6,14},{7,15},{8,0},{9,1},... | collective-permute-start | bytes 294920 | tf_op jit(solution)/shard_map/ppermute | solution.py:493
  107.2 8.0 %collective-permute-start.17 = (bf16[4,32,512]{2,1,0:T(8,128)(2,1)S(1)}, bf16[4,32,512]{2,1,0:T(8,128)(2,1)S(1)}, u32[]{:S(2)}, u32[]{:S(2)}) collective-permute-start(bf16[4,32,512]{2,1,0:T(8,128)(2,1)S(1)} %shard_map.187.refs_1_.refs_3_), channel_id=1, source_target_pairs={{0,8},{1,9},{2,10},{3,11},{4,12},{5,13},{6,14},{7,15},{8,0},{9,1},... | collective-permute-start | bytes 393224 | tf_op jit(solution)/shard_map/ppermute | solution.py:493
  108.6 10.3 %collective-permute-start.26 = (bf16[3,64,512]{2,1,0:T(8,128)(2,1)S(1)}, bf16[3,64,512]{2,1,0:T(8,128)(2,1)S(1)}, u32[]{:S(2)}, u32[]{:S(2)}) collective-permute-start(bf16[3,64,512]{2,1,0:T(8,128)(2,1)S(1)} %shard_map.193.refs_1_), channel_id=1, source_target_pairs={{0,4},{1,5},{2,6},{3,7},{4,0},{5,1},{6,2},{7,3},{8,12},{9,13},{10,... | collective-permute-start | bytes 589832 | tf_op jit(solution)/shard_map/ppermute | solution.py:493
  109.6 9.4 %collective-permute-start.18 = (bf16[128,512]{1,0:T(8,128)(2,1)S(1)}, bf16[128,512]{1,0:T(8,128)(2,1)S(1)}, u32[]{:S(2)}, u32[]{:S(2)}) collective-permute-start(bf16[128,512]{1,0:T(8,128)(2,1)S(1)} %get-tuple-element.114.refs_13_.refs_8_), channel_id=1, source_target_pairs={{1,0},{2,1},{3,2},{4,3},{5,4},{6,5},{7,6},{8,7},{9,8},{10,9},{11,1... | collective-permute-start | bytes 393224 | tf_op jit(solution)/shard_map/ppermute | solution.py:22
  110.9 9.6 %collective-permute-start.19 = (bf16[128,512]{1,0:T(8,128)(2,1)S(1)}, bf16[128,512]{1,0:T(8,128)(2,1)S(1)}, u32[]{:S(2)}, u32[]{:S(2)}) collective-permute-start(bf16[128,512]{1,0:T(8,128)(2,1)S(1)} %get-tuple-element.115.refs_14_.refs_9_), channel_id=1, source_target_pairs={{15,0},{0,1},{1,2},{2,3},{3,4},{4,5},{5,6},{6,7},{7,8},{8,9},{9,10... | collective-permute-start | bytes 393224 | tf_op jit(solution)/shard_map/ppermute | solution.py:22
  110.9 9.6 %collective-permute-start.20 = (bf16[128,512]{1,0:T(8,128)(2,1)S(1)}, bf16[128,512]{1,0:T(8,128)(2,1)S(1)}, u32[]{:S(2)}, u32[]{:S(2)}) collective-permute-start(bf16[128,512]{1,0:T(8,128)(2,1)S(1)} %get-tuple-element.116.refs_15_.refs_10_), channel_id=1, source_target_pairs={{2,0},{3,1},{4,2},{5,3},{6,4},{7,5},{8,6},{9,7},{10,8},{11,9},{12,... | collective-permute-start | bytes 393224 | tf_op jit(solution)/shard_map/ppermute | solution.py:22
  115.2 9.0 %collective-permute-start.21 = (bf16[128,512]{1,0:T(8,128)(2,1)S(1)}, bf16[128,512]{1,0:T(8,128)(2,1)S(1)}, u32[]{:S(2)}, u32[]{:S(2)}) collective-permute-start(bf16[128,512]{1,0:T(8,128)(2,1)S(1)} %get-tuple-element.117.refs_16_.refs_11_), channel_id=1, source_target_pairs={{14,0},{15,1},{0,2},{1,3},{2,4},{3,5},{4,6},{5,7},{6,8},{7,9},{8,1... | collective-permute-start | bytes 393224 | tf_op jit(solution)/shard_map/ppermute | solution.py:22
  118.9 8.4 %collective-permute-start.22 = (bf16[4,64,512]{2,1,0:T(8,128)(2,1)S(1)}, bf16[4,64,512]{2,1,0:T(8,128)(2,1)S(1)}, u32[]{:S(2)}, u32[]{:S(2)}) collective-permute-start(bf16[4,64,512]{2,1,0:T(8,128)(2,1)S(1)} %shard_map.188.refs_5_.refs_1_.refs_3_), channel_id=1, source_target_pairs={{0,4},{1,5},{2,6},{3,7},{4,0},{5,1},{6,2},{7,3},{8,12},{9,13},{10,... | collective-permute-start | bytes 786440 | tf_op jit(solution)/shard_map/ppermute | solution.py:493
  119.0 12.6 %collective-permute-start.27 = (bf16[3,128,512]{2,1,0:T(8,128)(2,1)S(1)}, bf16[3,128,512]{2,1,0:T(8,128)(2,1)S(1)}, u32[]{:S(2)}, u32[]{:S(2)}) collective-permute-start(bf16[3,128,512]{2,1,0:T(8,128)(2,1)S(1)} %shard_map.194.refs_1_), channel_id=1, source_target_pairs={{0,2},{1,3},{2,0},{3,1},{4,6},{5,7},{6,4},{7,5},{8,10},{9,11},{10,... | collective-permute-start | bytes 1179656 | tf_op jit(solution)/shard_map/ppermute | solution.py:493
  127.4 15.4 %collective-permute-start.23 = (bf16[4,128,512]{2,1,0:T(8,128)(2,1)S(1)}, bf16[4,128,512]{2,1,0:T(8,128)(2,1)S(1)}, u32[]{:S(2)}, u32[]{:S(2)}) collective-permute-start(bf16[4,128,512]{2,1,0:T(8,128)(2,1)S(1)} %shard_map.191.refs_1_), channel_id=1, source_target_pairs={{0,2},{1,3},{2,0},{3,1},{4,6},{5,7},{6,4},{7,5},{8,10},{9,11},{10,... | collective-permute-start | bytes 1572872 | tf_op jit(solution)/shard_map/ppermute | solution.py:493
  129.8 2.8 %collective-permute-start.28 = (bf16[3,128,512]{2,1,0:T(8,128)(2,1)S(1)}, bf16[3,128,512]{2,1,0:T(8,128)(2,1)S(1)}, u32[]{:S(2)}, u32[]{:S(2)}) collective-permute-start(bf16[3,128,512]{2,1,0:T(8,128)(2,1)S(1)} %shard_map.194.refs_1_), channel_id=1, source_target_pairs={{0,1},{1,0},{2,3},{3,2},{4,5},{5,4},{6,7},{7,6},{8,9},{9,8},{10,11... | collective-permute-start | bytes 1179656 | tf_op jit(solution)/shard_map/ppermute | solution.py:493
  131.6 2.3 %collective-permute-start.29 = (bf16[3,128,512]{2,1,0:T(8,128)(2,1)S(1)}, bf16[3,128,512]{2,1,0:T(8,128)(2,1)S(1)}, u32[]{:S(2)}, u32[]{:S(2)}) collective-permute-start(bf16[3,128,512]{2,1,0:T(8,128)(2,1)S(1)} %shard_map.195.refs_2_), channel_id=1, source_target_pairs={{0,1},{1,0},{2,3},{3,2},{4,5},{5,4},{6,7},{7,6},{8,9},{9,8},{10,11... | collective-permute-start | bytes 1179656 | tf_op jit(solution)/shard_map/ppermute | solution.py:493
  132.6 10.5 %collective-permute-start.30 = (bf16[4,128,512]{2,1,0:T(8,128)(2,1)S(1)}, bf16[4,128,512]{2,1,0:T(8,128)(2,1)S(1)}, u32[]{:S(2)}, u32[]{:S(2)}) collective-permute-start(bf16[4,128,512]{2,1,0:T(8,128)(2,1)S(1)} %shard_map.191.refs_1_), channel_id=1, source_target_pairs={{0,1},{1,0},{2,3},{3,2},{4,5},{5,4},{6,7},{7,6},{8,9},{9,8},{10,11... | collective-permute-start | bytes 1572872 | tf_op jit(solution)/shard_map/ppermute | solution.py:493
  142.9 1.9 %collective-permute-start.31 = (bf16[4,128,512]{2,1,0:T(8,128)(2,1)S(1)}, bf16[4,128,512]{2,1,0:T(8,128)(2,1)S(1)}, u32[]{:S(2)}, u32[]{:S(2)}) collective-permute-start(bf16[4,128,512]{2,1,0:T(8,128)(2,1)S(1)} %shard_map.197.refs_2_), channel_id=1, source_target_pairs={{0,1},{1,0},{2,3},{3,2},{4,5},{5,4},{6,7},{7,6},{8,9},{9,8},{10,11... | collective-permute-start | bytes 1572872 | tf_op jit(solution)/shard_map/ppermute | solution.py:493

commit v17 on v16

--- a/solution.py
+++ b/solution.py
@@ -856,10 +856,10 @@
         grad_nodes = node_output([piece_edge])
         piece_node = gather_stage(me, piece_node, over(piece_node, 4), 4, [piece_edge])
         other_node = over(piece_node, 2)
-        piece_edge = gather_stage(me, piece_edge, over(piece_edge, 4), 4, [in_hbm(grad_nodes)])
+        piece_edge = gather_stage(me, piece_edge, over(piece_edge, 4), 4, [])
         other_node = held_until(other_node, [piece_edge])
         grad_n1, grad_n2 = join_stage(me, piece_node, other_node, first, node_blocks, node_shapes)
-        other_edge = held_until(over(piece_edge, 2), [in_hbm(grad_n2)])
+        other_edge = held_until(over(piece_edge, 2), [in_hbm(grad_n2), in_hbm(grad_nodes)])
         grad_e1, grad_e2 = join_stage(me, piece_edge, other_edge, first, edge_blocks, edge_shapes)
     else:
         whole = reduce_whole(*node_weights([]))

time: 146 us -> 152 us (1.041)
  waiting for transfers between devices: 63.6 us -> 67.9 us
    ppermute x18, waiting for transfers between devices: 45.1 us -> 52.9 us  [in_group(): return lax.ppermute(block, axis, route)]
    ppermute x14, waiting for transfers between devices: 18.5 us -> 15 us  [passed_along(): return lax.ppermute(block, axis, route)]
    ppermute x18, starting transfers between devices: 20.3 us -> 22.3 us  [in_group(): return lax.ppermute(block, axis, route)]
  transfers between devices with their start and end apart: 32 -> 32, of which waited for: 19 -> 18; matrix products, arithmetic and copies ran while one was open for 0% -> 0% of each run, Pallas kernels for 13% -> 13%
where the time goes in v17:
time: 152 us; the launch traced here: 151 us
  waiting for transfers between devices  67.9 us (45%)
  starting transfers between devices  37.9 us (25%)
  Pallas kernels  31.1 us (20%)
  blocking collectives  13.7 us (9%)
    ppermute x18, waiting for transfers between devices, in_group(): return lax.ppermute(block, axis, route)  52.9 us
    pallas_call x25, Pallas kernels, call(): pl.pallas_call(kernel, out_shape=[(pltpu.HBM if i in last else pltpu.VMEM...  27.8 us
    ppermute x18, starting transfers between devices, in_group(): return lax.ppermute(block, axis, route)  22.3 us
    ppermute x14, starting transfers between devices, passed_along(): return lax.ppermute(block, axis, route)  15.6 us
    ppermute x14, waiting for transfers between devices, passed_along(): return lax.ppermute(block, axis, route)  15 us
    all_to_all x1, blocking collectives, local(): ids = lax.all_to_all(ids, 'band', 0, 0, tiled=True)  13.7 us
    pallas_call x1, Pallas kernels, loaded(): pl.pallas_call(functools.partial(load_kernel, count), out_shape=[pltpu.VM...  3.24 us
  transfers between devices with their start and end apart: 32, of which 18 were waited for; matrix products, arithmetic and copies ran while one was open for 0% of the time, Pallas kernels for 13%

profile of v17, /device:TPU:0, one launch (start us, length us, event | category | flops | bytes accessed | tf_op | source)
XLA Modules:
  0.0 151.3 jit_solution(13769172044931204555)
XLA Ops:
  0.6 3.2 %shard_map.170 = (bf16[320,512]{1,0:T(8,128)(2,1)S(1)}, s32[11,1,128]{2,1,0:T(1,128)S(1)}, s32[11,1,128]{2,1,0:T(1,128)S(1)}, bf16[11,128,512]{2,1,0:T(8,128)(2,...) custom-call(s32[1]{0:T(128)} %bitcast.refs_0_.refs_2_, ...), custom_call_target="tpu_custom_call" | custom-call | flops 1 | bytes 1 | tf_op jit(solution)/shard_map/pallas_call | solution.py:121
  3.9 13.7 %all_to_all.5.refs_2_.refs_4_ = s32[16,1,256]{2,1,0:T(1,128)S(1)} all-to-all(s32[16,1,256]{2,1,0:T(1,128)S(1)} %shard_map.171), channel_id=1, replica_groups=mesh['groups'=2,'band'=16] {'band'}, dimensions={0} | all-to-all | bytes 32768 | tf_op jit(solution)/shard_map/all_to_all | solution.py:638
  17.6 0.8 shard_map.172
  18.6 1.2 collective-permute-start.2
  19.8 0.8 collective-permute-start.6
  20.6 3.3 %collective-permute-start.3 = (bf16[128,512]{1,0:T(8,128)(2,1)S(1)}, bf16[128,512]{1,0:T(8,128)(2,1)S(1)}, u32[]{:S(2)}, u32[]{:S(2)}) collective-permute-start(bf16[128,512]{1,0:T(8,128)(2,1)S(1)} %get-tuple-element.96), channel_id=1, source_target_pairs={{2,0},{3,1},{4,2},{5,3},{6,4},{7,5},{8,6},{9,7},{10,8},{11,9},{12,... | collective-permute-start | bytes 393224 | tf_op jit(solution)/shard_map/ppermute | solution.py:22
  23.9 3.8 %collective-permute-done.2.refs_8_.refs_7_ = bf16[128,512]{1,0:T(8,128)(2,1)S(1)} collective-permute-done((bf16[128,512]{1,0:T(8,128)(2,1)S(1)}, bf16[128,512]{1,0:T(8,128)(2,1)S(1)}, u32[]{:S(2)}, u32[]{:S(2)}) %collective-permute-start.2) | collective-permute-done | bytes 131104 | tf_op jit(solution)/shard_map/ppermute | solution.py:22
  27.8 4.5 %shard_map.173 = (bf16[1408,320]{1,0:T(8,128)(2,1)S(1)}, bf16[320,1408]{1,0:T(8,128)(2,1)S(1)}, f32[1408,128]{1,0:T(8,128)S(1)}, f32[1024,512]{1,0:T(8,128)S(1)}...) custom-call(bf16[11,128,512]{2,1,0:T(8,128)(2,1)S(1)} %get-tuple-ele, ...), custom_call_target="tpu_custom_call" | custom-call | flops 1 | bytes 1 | tf_op jit(solution)/shard_map/pallas_call | solution.py:90
  32.3 2.7 %collective-permute-done.refs_6_.refs_5_ = bf16[128,512]{1,0:T(8,128)(2,1)S(1)} collective-permute-done((bf16[128,512]{1,0:T(8,128)(2,1)S(1)}, bf16[128,512]{1,0:T(8,128)(2,1)S(1)}, u32[]{:S(2)}, u32[]{:S(2)}) %collective-permute-start) | collective-permute-done | bytes 131104 | tf_op jit(solution)/shard_map/ppermute | solution.py:22
  35.0 1.6 %shard_map.174 = (bf16[512,512]{1,0:T(8,128)(2,1)S(1)}, f32[512,512]{1,0:T(8,128)S(1)}, f32[512,512]{1,0:T(8,128)S(1)}, f32[512,128]{1,0:T(8,128)S(1)}, f32[320,512]{1,0:T(8,128)S(1)}) custom-call(f32[1024,512]{1,0:T(8,128)S(1)} %get-tuple-element.89.refs_0_.refs_1_, f32[1408,128]{1,0:T(8,128)S(1)} %get-tuple-element.90.refs_1_.refs_2_.refs_3_, ...), custom_call_target="tpu_custom_call" | custom-call | flops 1 | bytes 1 | tf_op jit(solution)/shard_map/pallas_call | solution.py:90
  36.6 2.8 %collective-permute-done.5.refs_13_.refs_10_ = bf16[128,512]{1,0:T(8,128)(2,1)S(1)} collective-permute-done((bf16[128,512]{1,0:T(8,128)(2,1)S(1)}, bf16[128,512]{1,0:T(8,128)(2,1)S(1)}, u32[]{:S(2)}, u32[]{:S(2)}) %collective-permute-start.5) | collective-permute-done | bytes 131104 | tf_op jit(solution)/shard_map/ppermute | solution.py:22
  39.4 4.5 %shard_map.175 = (bf16[128,512]{1,0:T(8,128)(2,1)S(1)}, bf16[128,512]{1,0:T(8,128)(2,1)S(1)}, bf16[256,512]{1,0:T(8,128)(2,1)S(1)}, bf16[512,512]{1,0:T(8,128)(2...) custom-call(bf16[11,128,512]{2,1,0:T(8,128)(2,1)S(1)} %get-tuple-ele, ...), custom_call_target="tpu_custom_call" | custom-call | flops 1 | bytes 1 | tf_op jit(solution)/shard_map/pallas_call | solution.py:90
  43.9 1.3 shard_map.178
  45.3 4.7 %collective-permute-start.9 = (bf16[256,512]{1,0:T(8,128)(2,1)S(1)}, bf16[256,512]{1,0:T(8,128)(2,1)S(1)}, u32[]{:S(2)}, u32[]{:S(2)}) collective-permute-start(bf16[256,512]{1,0:T(8,128)(2,1)S(1)} %get-tuple-element.120.refs_19_.refs_14_), channel_id=1, source_target_pairs={{8,0},{9,1},{10,2},{11,3},{12,4},{13,5},{14,6},{15,7},{0,8},{1,9},... | collective-permute-start | bytes 786440 | tf_op jit(solution)/shard_map/ppermute | solution.py:22
  50.0 1.7 %collective-permute-start.7 = (bf16[128,512]{1,0:T(8,128)(2,1)S(1)}, bf16[128,512]{1,0:T(8,128)(2,1)S(1)}, u32[]{:S(2)}, u32[]{:S(2)}) collective-permute-start(bf16[128,512]{1,0:T(8,128)(2,1)S(1)} %get-tuple-element.118.refs_17_.refs_12_), channel_id=1, source_target_pairs={{4,0},{5,1},{6,2},{7,3},{8,4},{9,5},{10,6},{11,7},{12,8},{13,9},{1... | collective-permute-start | bytes 393224 | tf_op jit(solution)/shard_map/ppermute | solution.py:22
  52.0 2.1 %shard_map.176 = (bf16[896,512]{1,0:T(8,128)(2,1)S(1)}, bf16[384,512]{1,0:T(8,128)(2,1)S(1)}, bf16[128,512]{1,0:T(8,128)(2,1)S(1)}, bf16[128,512]{1,0:T(8,128)(2...) custom-call(bf16[11,128,512]{2,1,0:T(8,128)(2,1)S(1)} %get-tuple-element.81.refs_0_.refs_1_, ...), custom_call_target="tpu_custom_call" | custom-call | flops 1 | bytes 1 | tf_op jit(solution)/shard_map/pallas_call | solution.py:90
  54.1 3.9 %shard_map.177 = (f32[4,256,512]{2,1,0:T(8,128)S(1)}, bf16[4,256,512]{2,1,0:T(8,128)(2,1)S(1)}, bf16[320,512]{1,0:T(8,128)(2,1)S(1)}) custom-call(bf16[11,128,512]{2,1,0:T(8,128)(2,1)S(1)} %get-tuple-element.82.refs_0_, bf16[320,1408]{1,0:T(8,128)(2,1)S(1)} %get-tuple-element.92.refs_2_.refs_4_.refs_1_, s32[1]{0:T(128)} %bitcast.refs_0_.refs_2_, ...), custom_call_target="tpu_custom_call" | custom-call | flops 1 | bytes 1 | tf_op jit(solution)/shard_map/pallas_call | solution.py:90
  58.2 2.1 %collective-permute-start.12 = (bf16[3,128,512]{2,1,0:T(8,128)(2,1)S(1)}, bf16[3,128,512]{2,1,0:T(8,128)(2,1)S(1)}, u32[]{:S(2)}, u32[]{:S(2)}) collective-permute-start(bf16[3,128,512]{2,1,0:T(8,128)(2,1)S(1)} %get-tuple-element.138), channel_id=1, source_target_pairs={{0,2},{1,3},{2,0},{3,1},{4,6},{5,7},{6,4},{7,5},{8,10},{9,11},{10,... | collective-permute-start | bytes 1179656 | tf_op jit(solution)/shard_map/ppermute | solution.py:493
  60.3 3.8 %collective-permute-done.8.refs_2_.refs_11_ = bf16[128,512]{1,0:T(8,128)(2,1)S(1)} collective-permute-done((bf16[128,512]{1,0:T(8,128)(2,1)S(1)}, bf16[128,512]{1,0:T(8,128)(2,1)S(1)}, u32[]{:S(2)}, u32[]{:S(2)}) %collective-permute-start.8) | collective-permute-done | bytes 131104 | tf_op jit(solution)/shard_map/ppermute | solution.py:22
  64.0 1.5 %collective-permute-done.9.refs_3_.refs_12_ = bf16[256,512]{1,0:T(8,128)(2,1)S(1)} collective-permute-done((bf16[256,512]{1,0:T(8,128)(2,1)S(1)}, bf16[256,512]{1,0:T(8,128)(2,1)S(1)}, u32[]{:S(2)}, u32[]{:S(2)}) %collective-permute-start.9) | collective-permute-done | bytes 262176 | tf_op jit(solution)/shard_map/ppermute | solution.py:22
  65.6 3.5 %shard_map.181 = (bf16[11,128,512]{2,1,0:T(8,128)(2,1)}, bf16[11,128,512]{2,1,0:T(8,128)(2,1)}) custom-call(bf16[11,128,512]{2,1,0:T(8,128)(2,1)S(1)} %get-tuple-element.82.refs_0_, bf16[11,128,512]{2,1,0:T(8,128)(2,1)S(1)} %get-tuple-element.81.refs_0_.refs_1_, bf16[1536,512]{1,0:T(8,128)(2,1)S(1)} %get-tuple-element.85.refs_4_.refs_6_.refs_2_.refs_3_, ...), custom_call_target="tpu_custom_call" | custom-call | flops 20000000000 | bytes 1 | tf_op jit(solution)/shard_map/pallas_call | solution.py:90
  69.7 2.9 %collective-permute-start.13 = (bf16[4,128,512]{2,1,0:T(8,128)(2,1)S(1)}, bf16[4,128,512]{2,1,0:T(8,128)(2,1)S(1)}, u32[]{:S(2)}, u32[]{:S(2)}) collective-permute-start(bf16[4,128,512]{2,1,0:T(8,128)(2,1)S(1)} %get-tuple-element.141), channel_id=1, source_target_pairs={{0,2},{1,3},{2,0},{3,1},{4,6},{5,7},{6,4},{7,5},{8,10},{9,11},{10,... | collective-permute-start | bytes 1572872 | tf_op jit(solution)/shard_map/ppermute | solution.py:493
  72.6 3.0 %collective-permute-start.14 = (bf16[3,64,512]{2,1,0:T(8,128)(2,1)S(1)}, bf16[3,64,512]{2,1,0:T(8,128)(2,1)S(1)}, u32[]{:S(2)}, u32[]{:S(2)}) collective-permute-start(bf16[3,64,512]{2,1,0:T(8,128)(2,1)S(1)} %get-tuple-element.142), channel_id=1, source_target_pairs={{0,4},{1,5},{2,6},{3,7},{4,0},{5,1},{6,2},{7,3},{8,12},{9,13},{10,... | collective-permute-start | bytes 589832 | tf_op jit(solution)/shard_map/ppermute | solution.py:493
  75.6 5.3 %collective-permute-done.14.refs_2_ = bf16[3,64,512]{2,1,0:T(8,128)(2,1)S(1)} collective-permute-done((bf16[3,64,512]{2,1,0:T(8,128)(2,1)S(1)}, bf16[3,64,512]{2,1,0:T(8,128)(2,1)S(1)}, u32[]{:S(2)}, u32[]{:S(2)}) %collective-permute-start.14) | collective-permute-done | bytes 196640 | tf_op jit(solution)/shard_map/ppermute | solution.py:493
  80.9 4.3 %collective-permute-done.13.refs_2_ = bf16[4,128,512]{2,1,0:T(8,128)(2,1)S(1)} collective-permute-done((bf16[4,128,512]{2,1,0:T(8,128)(2,1)S(1)}, bf16[4,128,512]{2,1,0:T(8,128)(2,1)S(1)}, u32[]{:S(2)}, u32[]{:S(2)}) %collective-permute-start.13) | collective-permute-done | bytes 524320 | tf_op jit(solution)/shard_map/ppermute | solution.py:493
  85.3 3.0 %collective-permute-start.15 = (bf16[4,64,512]{2,1,0:T(8,128)(2,1)S(1)}, bf16[4,64,512]{2,1,0:T(8,128)(2,1)S(1)}, u32[]{:S(2)}, u32[]{:S(2)}) collective-permute-start(bf16[4,64,512]{2,1,0:T(8,128)(2,1)S(1)} %get-tuple-element.145), channel_id=1, source_target_pairs={{0,4},{1,5},{2,6},{3,7},{4,0},{5,1},{6,2},{7,3},{8,12},{9,13},{10,... | collective-permute-start | bytes 786440 | tf_op jit(solution)/shard_map/ppermute | solution.py:493
  88.3 8.5 %collective-permute-done.15.refs_2_ = bf16[4,64,512]{2,1,0:T(8,128)(2,1)S(1)} collective-permute-done((bf16[4,64,512]{2,1,0:T(8,128)(2,1)S(1)}, bf16[4,64,512]{2,1,0:T(8,128)(2,1)S(1)}, u32[]{:S(2)}, u32[]{:S(2)}) %collective-permute-start.15) | collective-permute-done | bytes 262176 | tf_op jit(solution)/shard_map/ppermute | solution.py:493
  96.9 0.4 collective-permute-start.16
  97.3 2.7 %collective-permute-start.25 = (bf16[3,32,512]{2,1,0:T(8,128)(2,1)S(1)}, bf16[3,32,512]{2,1,0:T(8,128)(2,1)S(1)}, u32[]{:S(2)}, u32[]{:S(2)}) collective-permute-start(bf16[3,32,512]{2,1,0:T(8,128)(2,1)S(1)} %shard_map.192.refs_1_), channel_id=1, source_target_pairs={{0,8},{1,9},{2,10},{3,11},{4,12},{5,13},{6,14},{7,15},{8,0},{9,1},... | collective-permute-start | bytes 294920 | tf_op jit(solution)/shard_map/ppermute | solution.py:493
  99.9 7.3 %collective-permute-done.16.refs_2_ = bf16[4,32,512]{2,1,0:T(8,128)(2,1)S(1)} collective-permute-done((bf16[4,32,512]{2,1,0:T(8,128)(2,1)S(1)}, bf16[4,32,512]{2,1,0:T(8,128)(2,1)S(1)}, u32[]{:S(2)}, u32[]{:S(2)}) %collective-permute-start.16) | collective-permute-done | bytes 131104 | tf_op jit(solution)/shard_map/ppermute | solution.py:493
  107.2 1.4 collective-permute-done.25.refs_2_
  108.7 2.7 %collective-permute-start.17 = (bf16[4,32,512]{2,1,0:T(8,128)(2,1)S(1)}, bf16[4,32,512]{2,1,0:T(8,128)(2,1)S(1)}, u32[]{:S(2)}, u32[]{:S(2)}) collective-permute-start(bf16[4,32,512]{2,1,0:T(8,128)(2,1)S(1)} %shard_map.187.refs_1_.refs_3_), channel_id=1, source_target_pairs={{0,8},{1,9},{2,10},{3,11},{4,12},{5,13},{6,14},{7,15},{8,0},{9,1},... | collective-permute-start | bytes 393224 | tf_op jit(solution)/shard_map/ppermute | solution.py:493
  111.4 4.1 %collective-permute-done.17.refs_2_ = bf16[4,32,512]{2,1,0:T(8,128)(2,1)S(1)} collective-permute-done((bf16[4,32,512]{2,1,0:T(8,128)(2,1)S(1)}, bf16[4,32,512]{2,1,0:T(8,128)(2,1)S(1)}, u32[]{:S(2)}, u32[]{:S(2)}) %collective-permute-start.17) | collective-permute-done | bytes 131104 | tf_op jit(solution)/shard_map/ppermute | solution.py:493
  115.6 2.1 %collective-permute-done.26.refs_2_ = bf16[3,64,512]{2,1,0:T(8,128)(2,1)S(1)} collective-permute-done((bf16[3,64,512]{2,1,0:T(8,128)(2,1)S(1)}, bf16[3,64,512]{2,1,0:T(8,128)(2,1)S(1)}, u32[]{:S(2)}, u32[]{:S(2)}) %collective-permute-start.26) | collective-permute-done | bytes 196640 | tf_op jit(solution)/shard_map/ppermute | solution.py:493
  117.7 1.4 collective-permute-start.27
  119.1 1.3 collective-permute-start.22
  120.4 0.5 collective-permute-start.19
  120.9 1.7 %collective-permute-start.20 = (bf16[128,512]{1,0:T(8,128)(2,1)S(1)}, bf16[128,512]{1,0:T(8,128)(2,1)S(1)}, u32[]{:S(2)}, u32[]{:S(2)}) collective-permute-start(bf16[128,512]{1,0:T(8,128)(2,1)S(1)} %get-tuple-element.116.refs_15_.refs_10_), channel_id=1, source_target_pairs={{2,0},{3,1},{4,2},{5,3},{6,4},{7,5},{8,6},{9,7},{10,8},{11,9},{12,... | collective-permute-start | bytes 393224 | tf_op jit(solution)/shard_map/ppermute | solution.py:22
  122.6 4.5 %collective-permute-done.22.refs_2_ = bf16[4,64,512]{2,1,0:T(8,128)(2,1)S(1)} collective-permute-done((bf16[4,64,512]{2,1,0:T(8,128)(2,1)S(1)}, bf16[4,64,512]{2,1,0:T(8,128)(2,1)S(1)}, u32[]{:S(2)}, u32[]{:S(2)}) %collective-permute-start.22) | collective-permute-done | bytes 262176 | tf_op jit(solution)/shard_map/ppermute | solution.py:493
  127.1 1.1 collective-permute-start.21
  128.1 0.5 shard_map.189.refs_1_
  128.7 4.1 %collective-permute-done.27.refs_0_ = bf16[3,128,512]{2,1,0:T(8,128)(2,1)S(1)} collective-permute-done((bf16[3,128,512]{2,1,0:T(8,128)(2,1)S(1)}, bf16[3,128,512]{2,1,0:T(8,128)(2,1)S(1)}, u32[]{:S(2)}, u32[]{:S(2)}) %collective-permute-start.27) | collective-permute-done | bytes 393248 | tf_op jit(solution)/shard_map/ppermute | solution.py:493
  132.9 2.5 %collective-permute-start.23 = (bf16[4,128,512]{2,1,0:T(8,128)(2,1)S(1)}, bf16[4,128,512]{2,1,0:T(8,128)(2,1)S(1)}, u32[]{:S(2)}, u32[]{:S(2)}) collective-permute-start(bf16[4,128,512]{2,1,0:T(8,128)(2,1)S(1)} %shard_map.191.refs_1_), channel_id=1, source_target_pairs={{0,2},{1,3},{2,0},{3,1},{4,6},{5,7},{6,4},{7,5},{8,10},{9,11},{10,... | collective-permute-start | bytes 1572872 | tf_op jit(solution)/shard_map/ppermute | solution.py:493
  136.0 1.6 %shard_map.190.refs_2_ = bf16[320,512]{1,0:T(8,128)(2,1)} custom-call(s32[1]{0:T(128)} %bitcast.refs_0_.refs_2_, f32[320,512]{1,0:T(8,128)S(1)} %shard_map.189.refs_1_, bf16[1536,512]{1,0:T(8,128)(2,1)S(1)} %get-tuple-element.85.refs_4_.refs_6_.refs_2_.refs_3_, s32[11,1,128]{2,1,0:T(1,128)S(1)} %get-tuple-element.84.refs_1_.refs_2_.refs_3_, ...), custom_call_target="tpu_custom_call" | custom-call | flops 20000000000 | bytes 1 | tf_op jit(solution)/shard_map/pallas_call | solution.py:90
  137.6 1.3 shard_map.196
  138.9 9.1 %collective-permute-done.23.refs_0_ = bf16[4,128,512]{2,1,0:T(8,128)(2,1)S(1)} collective-permute-done((bf16[4,128,512]{2,1,0:T(8,128)(2,1)S(1)}, bf16[4,128,512]{2,1,0:T(8,128)(2,1)S(1)}, u32[]{:S(2)}, u32[]{:S(2)}) %collective-permute-start.23) | collective-permute-done | bytes 524320 | tf_op jit(solution)/shard_map/ppermute | solution.py:493
  148.0 1.9 %collective-permute-done.31.refs_4_ = bf16[4,128,512]{2,1,0:T(8,128)(2,1)S(1)} collective-permute-done((bf16[4,128,512]{2,1,0:T(8,128)(2,1)S(1)}, bf16[4,128,512]{2,1,0:T(8,128)(2,1)S(1)}, u32[]{:S(2)}, u32[]{:S(2)}) %collective-permute-start.31) | collective-permute-done | bytes 524320 | tf_op jit(solution)/shard_map/ppermute | solution.py:493
  149.9 1.5 shard_map.198
  (46 shorter events, 2.5 us)
Async XLA Ops:
  18.4 5.5 %collective-permute-start.1 = (bf16[128,512]{1,0:T(8,128)(2,1)S(1)}, bf16[128,512]{1,0:T(8,128)(2,1)S(1)}, u32[]{:S(2)}, u32[]{:S(2)}) collective-permute-start(bf16[128,512]{1,0:T(8,128)(2,1)S(1)} %get-tuple-element.94), channel_id=1, source_target_pairs={{1,0},{2,1},{3,2},{4,3},{5,4},{6,5},{7,6},{8,7},{9,8},{10,9},{11,1... | collective-permute-start | bytes 393224 | tf_op jit(solution)/shard_map/ppermute | solution.py:22
  18.6 9.1 %collective-permute-start.2 = (bf16[128,512]{1,0:T(8,128)(2,1)S(1)}, bf16[128,512]{1,0:T(8,128)(2,1)S(1)}, u32[]{:S(2)}, u32[]{:S(2)}) collective-permute-start(bf16[128,512]{1,0:T(8,128)(2,1)S(1)} %get-tuple-element.95), channel_id=1, source_target_pairs={{14,0},{15,1},{0,2},{1,3},{2,4},{3,5},{4,6},{5,7},{6,8},{7,9},{8,1... | collective-permute-start | bytes 393224 | tf_op jit(solution)/shard_map/ppermute | solution.py:22
  19.8 19.6 %collective-permute-start.6 = (bf16[256,512]{1,0:T(8,128)(2,1)S(1)}, bf16[256,512]{1,0:T(8,128)(2,1)S(1)}, u32[]{:S(2)}, u32[]{:S(2)}) collective-permute-start(bf16[256,512]{1,0:T(8,128)(2,1)S(1)} %get-tuple-element.103), channel_id=1, source_target_pairs={{8,0},{9,1},{10,2},{11,3},{12,4},{13,5},{14,6},{15,7},{0,8},{1,9},... | collective-permute-start | bytes 786440 | tf_op jit(solution)/shard_map/ppermute | solution.py:22
  20.6 11.6 %collective-permute-start.3 = (bf16[128,512]{1,0:T(8,128)(2,1)S(1)}, bf16[128,512]{1,0:T(8,128)(2,1)S(1)}, u32[]{:S(2)}, u32[]{:S(2)}) collective-permute-start(bf16[128,512]{1,0:T(8,128)(2,1)S(1)} %get-tuple-element.96), channel_id=1, source_target_pairs={{2,0},{3,1},{4,2},{5,3},{6,4},{7,5},{8,6},{9,7},{10,8},{11,9},{12,... | collective-permute-start | bytes 393224 | tf_op jit(solution)/shard_map/ppermute | solution.py:22
  23.9 11.1 %collective-permute-start = (bf16[128,512]{1,0:T(8,128)(2,1)S(1)}, bf16[128,512]{1,0:T(8,128)(2,1)S(1)}, u32[]{:S(2)}, u32[]{:S(2)}) collective-permute-start(bf16[128,512]{1,0:T(8,128)(2,1)S(1)} %get-tuple-element.88.refs_7_), channel_id=1, source_target_pairs={{15,0},{0,1},{1,2},{2,3},{3,4},{4,5},{5,6},{6,7},{7,8},{8,9},{9,10... | collective-permute-start | bytes 393224 | tf_op jit(solution)/shard_map/ppermute | solution.py:22
  23.9 12.7 %collective-permute-start.4 = (bf16[128,512]{1,0:T(8,128)(2,1)S(1)}, bf16[128,512]{1,0:T(8,128)(2,1)S(1)}, u32[]{:S(2)}, u32[]{:S(2)}) collective-permute-start(bf16[128,512]{1,0:T(8,128)(2,1)S(1)} %get-tuple-element.101), channel_id=1, source_target_pairs={{12,0},{13,1},{14,2},{15,3},{0,4},{1,5},{2,6},{3,7},{4,8},{5,9},{6... | collective-permute-start | bytes 393224 | tf_op jit(solution)/shard_map/ppermute | solution.py:22
  27.8 11.6 %collective-permute-start.5 = (bf16[128,512]{1,0:T(8,128)(2,1)S(1)}, bf16[128,512]{1,0:T(8,128)(2,1)S(1)}, u32[]{:S(2)}, u32[]{:S(2)}) collective-permute-start(bf16[128,512]{1,0:T(8,128)(2,1)S(1)} %get-tuple-element.102), channel_id=1, source_target_pairs={{4,0},{5,1},{6,2},{7,3},{8,4},{9,5},{10,6},{11,7},{12,8},{13,9},{1... | collective-permute-start | bytes 393224 | tf_op jit(solution)/shard_map/ppermute | solution.py:22
  45.2 12.8 %collective-permute-start.10 = (bf16[3,256,512]{2,1,0:T(8,128)(2,1)S(1)}, bf16[3,256,512]{2,1,0:T(8,128)(2,1)S(1)}, u32[]{:S(2)}, u32[]{:S(2)}) collective-permute-start(bf16[3,256,512]{2,1,0:T(8,128)(2,1)S(1)} %get-tuple-element.133), channel_id=1, source_target_pairs={{0,1},{1,0},{2,3},{3,2},{4,5},{5,4},{6,7},{7,6},{8,9},{9,8},{10,11... | collective-permute-start | bytes 2359304 | tf_op jit(solution)/shard_map/ppermute | solution.py:493
  45.3 20.3 %collective-permute-start.9 = (bf16[256,512]{1,0:T(8,128)(2,1)S(1)}, bf16[256,512]{1,0:T(8,128)(2,1)S(1)}, u32[]{:S(2)}, u32[]{:S(2)}) collective-permute-start(bf16[256,512]{1,0:T(8,128)(2,1)S(1)} %get-tuple-element.120.refs_19_.refs_14_), channel_id=1, source_target_pairs={{8,0},{9,1},{10,2},{11,3},{12,4},{13,5},{14,6},{15,7},{0,8},{1,9},... | collective-permute-start | bytes 786440 | tf_op jit(solution)/shard_map/ppermute | solution.py:22
  50.0 10.3 %collective-permute-start.7 = (bf16[128,512]{1,0:T(8,128)(2,1)S(1)}, bf16[128,512]{1,0:T(8,128)(2,1)S(1)}, u32[]{:S(2)}, u32[]{:S(2)}) collective-permute-start(bf16[128,512]{1,0:T(8,128)(2,1)S(1)} %get-tuple-element.118.refs_17_.refs_12_), channel_id=1, source_target_pairs={{4,0},{5,1},{6,2},{7,3},{8,4},{9,5},{10,6},{11,7},{12,8},{13,9},{1... | collective-permute-start | bytes 393224 | tf_op jit(solution)/shard_map/ppermute | solution.py:22
  51.7 12.4 %collective-permute-start.8 = (bf16[128,512]{1,0:T(8,128)(2,1)S(1)}, bf16[128,512]{1,0:T(8,128)(2,1)S(1)}, u32[]{:S(2)}, u32[]{:S(2)}) collective-permute-start(bf16[128,512]{1,0:T(8,128)(2,1)S(1)} %get-tuple-element.119.refs_18_.refs_13_), channel_id=1, source_target_pairs={{12,0},{13,1},{14,2},{15,3},{0,4},{1,5},{2,6},{3,7},{4,8},{5,9},{6... | collective-permute-start | bytes 393224 | tf_op jit(solution)/shard_map/ppermute | solution.py:22
  58.2 11.3 %collective-permute-start.12 = (bf16[3,128,512]{2,1,0:T(8,128)(2,1)S(1)}, bf16[3,128,512]{2,1,0:T(8,128)(2,1)S(1)}, u32[]{:S(2)}, u32[]{:S(2)}) collective-permute-start(bf16[3,128,512]{2,1,0:T(8,128)(2,1)S(1)} %get-tuple-element.138), channel_id=1, source_target_pairs={{0,2},{1,3},{2,0},{3,1},{4,6},{5,7},{6,4},{7,5},{8,10},{9,11},{10,... | collective-permute-start | bytes 1179656 | tf_op jit(solution)/shard_map/ppermute | solution.py:493
  65.6 3.9 %collective-permute-start.11 = (bf16[4,256,512]{2,1,0:T(8,128)(2,1)S(1)}, bf16[4,256,512]{2,1,0:T(8,128)(2,1)S(1)}, u32[]{:S(2)}, u32[]{:S(2)}) collective-permute-start(bf16[4,256,512]{2,1,0:T(8,128)(2,1)S(1)} %shard_map.180.refs_15_), channel_id=1, source_target_pairs={{0,1},{1,0},{2,3},{3,2},{4,5},{5,4},{6,7},{7,6},{8,9},{9,8},{10,11... | collective-permute-start | bytes 3145736 | tf_op jit(solution)/shard_map/ppermute | solution.py:493
  69.7 15.5 %collective-permute-start.13 = (bf16[4,128,512]{2,1,0:T(8,128)(2,1)S(1)}, bf16[4,128,512]{2,1,0:T(8,128)(2,1)S(1)}, u32[]{:S(2)}, u32[]{:S(2)}) collective-permute-start(bf16[4,128,512]{2,1,0:T(8,128)(2,1)S(1)} %get-tuple-element.141), channel_id=1, source_target_pairs={{0,2},{1,3},{2,0},{3,1},{4,6},{5,7},{6,4},{7,5},{8,10},{9,11},{10,... | collective-permute-start | bytes 1572872 | tf_op jit(solution)/shard_map/ppermute | solution.py:493
  72.6 8.3 %collective-permute-start.14 = (bf16[3,64,512]{2,1,0:T(8,128)(2,1)S(1)}, bf16[3,64,512]{2,1,0:T(8,128)(2,1)S(1)}, u32[]{:S(2)}, u32[]{:S(2)}) collective-permute-start(bf16[3,64,512]{2,1,0:T(8,128)(2,1)S(1)} %get-tuple-element.142), channel_id=1, source_target_pairs={{0,4},{1,5},{2,6},{3,7},{4,0},{5,1},{6,2},{7,3},{8,12},{9,13},{10,... | collective-permute-start | bytes 589832 | tf_op jit(solution)/shard_map/ppermute | solution.py:493
  85.3 11.5 %collective-permute-start.15 = (bf16[4,64,512]{2,1,0:T(8,128)(2,1)S(1)}, bf16[4,64,512]{2,1,0:T(8,128)(2,1)S(1)}, u32[]{:S(2)}, u32[]{:S(2)}) collective-permute-start(bf16[4,64,512]{2,1,0:T(8,128)(2,1)S(1)} %get-tuple-element.145), channel_id=1, source_target_pairs={{0,4},{1,5},{2,6},{3,7},{4,0},{5,1},{6,2},{7,3},{8,12},{9,13},{10,... | collective-permute-start | bytes 786440 | tf_op jit(solution)/shard_map/ppermute | solution.py:493
  88.3 8.9 %collective-permute-start.24 = (bf16[3,32,512]{2,1,0:T(8,128)(2,1)S(1)}, bf16[3,32,512]{2,1,0:T(8,128)(2,1)S(1)}, u32[]{:S(2)}, u32[]{:S(2)}) collective-permute-start(bf16[3,32,512]{2,1,0:T(8,128)(2,1)S(1)} %get-tuple-element.149), channel_id=1, source_target_pairs={{0,8},{1,9},{2,10},{3,11},{4,12},{5,13},{6,14},{7,15},{8,0},{9,1},... | collective-permute-start | bytes 294920 | tf_op jit(solution)/shard_map/ppermute | solution.py:493
  96.9 10.3 %collective-permute-start.16 = (bf16[4,32,512]{2,1,0:T(8,128)(2,1)S(1)}, bf16[4,32,512]{2,1,0:T(8,128)(2,1)S(1)}, u32[]{:S(2)}, u32[]{:S(2)}) collective-permute-start(bf16[4,32,512]{2,1,0:T(8,128)(2,1)S(1)} %get-tuple-element.147), channel_id=1, source_target_pairs={{0,8},{1,9},{2,10},{3,11},{4,12},{5,13},{6,14},{7,15},{8,0},{9,1},... | collective-permute-start | bytes 393224 | tf_op jit(solution)/shard_map/ppermute | solution.py:493
  97.3 11.3 %collective-permute-start.25 = (bf16[3,32,512]{2,1,0:T(8,128)(2,1)S(1)}, bf16[3,32,512]{2,1,0:T(8,128)(2,1)S(1)}, u32[]{:S(2)}, u32[]{:S(2)}) collective-permute-start(bf16[3,32,512]{2,1,0:T(8,128)(2,1)S(1)} %shard_map.192.refs_1_), channel_id=1, source_target_pairs={{0,8},{1,9},{2,10},{3,11},{4,12},{5,13},{6,14},{7,15},{8,0},{9,1},... | collective-permute-start | bytes 294920 | tf_op jit(solution)/shard_map/ppermute | solution.py:493
  108.6 9.1 %collective-permute-start.26 = (bf16[3,64,512]{2,1,0:T(8,128)(2,1)S(1)}, bf16[3,64,512]{2,1,0:T(8,128)(2,1)S(1)}, u32[]{:S(2)}, u32[]{:S(2)}) collective-permute-start(bf16[3,64,512]{2,1,0:T(8,128)(2,1)S(1)} %shard_map.193.refs_1_), channel_id=1, source_target_pairs={{0,4},{1,5},{2,6},{3,7},{4,0},{5,1},{6,2},{7,3},{8,12},{9,13},{10,... | collective-permute-start | bytes 589832 | tf_op jit(solution)/shard_map/ppermute | solution.py:493
  108.7 6.8 %collective-permute-start.17 = (bf16[4,32,512]{2,1,0:T(8,128)(2,1)S(1)}, bf16[4,32,512]{2,1,0:T(8,128)(2,1)S(1)}, u32[]{:S(2)}, u32[]{:S(2)}) collective-permute-start(bf16[4,32,512]{2,1,0:T(8,128)(2,1)S(1)} %shard_map.187.refs_1_.refs_3_), channel_id=1, source_target_pairs={{0,8},{1,9},{2,10},{3,11},{4,12},{5,13},{6,14},{7,15},{8,0},{9,1},... | collective-permute-start | bytes 393224 | tf_op jit(solution)/shard_map/ppermute | solution.py:493
  117.7 15.2 %collective-permute-start.27 = (bf16[3,128,512]{2,1,0:T(8,128)(2,1)S(1)}, bf16[3,128,512]{2,1,0:T(8,128)(2,1)S(1)}, u32[]{:S(2)}, u32[]{:S(2)}) collective-permute-start(bf16[3,128,512]{2,1,0:T(8,128)(2,1)S(1)} %shard_map.194.refs_1_), channel_id=1, source_target_pairs={{0,2},{1,3},{2,0},{3,1},{4,6},{5,7},{6,4},{7,5},{8,10},{9,11},{10,... | collective-permute-start | bytes 1179656 | tf_op jit(solution)/shard_map/ppermute | solution.py:493
  119.1 7.9 %collective-permute-start.22 = (bf16[4,64,512]{2,1,0:T(8,128)(2,1)S(1)}, bf16[4,64,512]{2,1,0:T(8,128)(2,1)S(1)}, u32[]{:S(2)}, u32[]{:S(2)}) collective-permute-start(bf16[4,64,512]{2,1,0:T(8,128)(2,1)S(1)} %shard_map.188.refs_5_.refs_1_.refs_3_), channel_id=1, source_target_pairs={{0,4},{1,5},{2,6},{3,7},{4,0},{5,1},{6,2},{7,3},{8,12},{9,13},{10,... | collective-permute-start | bytes 786440 | tf_op jit(solution)/shard_map/ppermute | solution.py:493
  120.4 12.5 %collective-permute-start.18 = (bf16[128,512]{1,0:T(8,128)(2,1)S(1)}, bf16[128,512]{1,0:T(8,128)(2,1)S(1)}, u32[]{:S(2)}, u32[]{:S(2)}) collective-permute-start(bf16[128,512]{1,0:T(8,128)(2,1)S(1)} %get-tuple-element.114.refs_13_.refs_8_), channel_id=1, source_target_pairs={{1,0},{2,1},{3,2},{4,3},{5,4},{6,5},{7,6},{8,7},{9,8},{10,9},{11,1... | collective-permute-start | bytes 393224 | tf_op jit(solution)/shard_map/ppermute | solution.py:22
  120.4 15.1 %collective-permute-start.19 = (bf16[128,512]{1,0:T(8,128)(2,1)S(1)}, bf16[128,512]{1,0:T(8,128)(2,1)S(1)}, u32[]{:S(2)}, u32[]{:S(2)}) collective-permute-start(bf16[128,512]{1,0:T(8,128)(2,1)S(1)} %get-tuple-element.115.refs_14_.refs_9_), channel_id=1, source_target_pairs={{15,0},{0,1},{1,2},{2,3},{3,4},{4,5},{5,6},{6,7},{7,8},{8,9},{9,10... | collective-permute-start | bytes 393224 | tf_op jit(solution)/shard_map/ppermute | solution.py:22
  120.9 15.1 %collective-permute-start.20 = (bf16[128,512]{1,0:T(8,128)(2,1)S(1)}, bf16[128,512]{1,0:T(8,128)(2,1)S(1)}, u32[]{:S(2)}, u32[]{:S(2)}) collective-permute-start(bf16[128,512]{1,0:T(8,128)(2,1)S(1)} %get-tuple-element.116.refs_15_.refs_10_), channel_id=1, source_target_pairs={{2,0},{3,1},{4,2},{5,3},{6,4},{7,5},{8,6},{9,7},{10,8},{11,9},{12,... | collective-permute-start | bytes 393224 | tf_op jit(solution)/shard_map/ppermute | solution.py:22
  127.1 8.9 %collective-permute-start.21 = (bf16[128,512]{1,0:T(8,128)(2,1)S(1)}, bf16[128,512]{1,0:T(8,128)(2,1)S(1)}, u32[]{:S(2)}, u32[]{:S(2)}) collective-permute-start(bf16[128,512]{1,0:T(8,128)(2,1)S(1)} %get-tuple-element.117.refs_16_.refs_11_), channel_id=1, source_target_pairs={{14,0},{15,1},{0,2},{1,3},{2,4},{3,5},{4,6},{5,7},{6,8},{7,9},{8,1... | collective-permute-start | bytes 393224 | tf_op jit(solution)/shard_map/ppermute | solution.py:22
  132.9 4.7 %collective-permute-start.28 = (bf16[3,128,512]{2,1,0:T(8,128)(2,1)S(1)}, bf16[3,128,512]{2,1,0:T(8,128)(2,1)S(1)}, u32[]{:S(2)}, u32[]{:S(2)}) collective-permute-start(bf16[3,128,512]{2,1,0:T(8,128)(2,1)S(1)} %shard_map.194.refs_1_), channel_id=1, source_target_pairs={{0,1},{1,0},{2,3},{3,2},{4,5},{5,4},{6,7},{7,6},{8,9},{9,8},{10,11... | collective-permute-start | bytes 1179656 | tf_op jit(solution)/shard_map/ppermute | solution.py:493
  132.9 15.1 %collective-permute-start.23 = (bf16[4,128,512]{2,1,0:T(8,128)(2,1)S(1)}, bf16[4,128,512]{2,1,0:T(8,128)(2,1)S(1)}, u32[]{:S(2)}, u32[]{:S(2)}) collective-permute-start(bf16[4,128,512]{2,1,0:T(8,128)(2,1)S(1)} %shard_map.191.refs_1_), channel_id=1, source_target_pairs={{0,2},{1,3},{2,0},{3,1},{4,6},{5,7},{6,4},{7,5},{8,10},{9,11},{10,... | collective-permute-start | bytes 1572872 | tf_op jit(solution)/shard_map/ppermute | solution.py:493
  135.4 2.2 %collective-permute-start.29 = (bf16[3,128,512]{2,1,0:T(8,128)(2,1)S(1)}, bf16[3,128,512]{2,1,0:T(8,128)(2,1)S(1)}, u32[]{:S(2)}, u32[]{:S(2)}) collective-permute-start(bf16[3,128,512]{2,1,0:T(8,128)(2,1)S(1)} %shard_map.195.refs_2_), channel_id=1, source_target_pairs={{0,1},{1,0},{2,3},{3,2},{4,5},{5,4},{6,7},{7,6},{8,9},{9,8},{10,11... | collective-permute-start | bytes 1179656 | tf_op jit(solution)/shard_map/ppermute | solution.py:493
  137.6 10.4 %collective-permute-start.30 = (bf16[4,128,512]{2,1,0:T(8,128)(2,1)S(1)}, bf16[4,128,512]{2,1,0:T(8,128)(2,1)S(1)}, u32[]{:S(2)}, u32[]{:S(2)}) collective-permute-start(bf16[4,128,512]{2,1,0:T(8,128)(2,1)S(1)} %shard_map.191.refs_1_), channel_id=1, source_target_pairs={{0,1},{1,0},{2,3},{3,2},{4,5},{5,4},{6,7},{7,6},{8,9},{9,8},{10,11... | collective-permute-start | bytes 1572872 | tf_op jit(solution)/shard_map/ppermute | solution.py:493
  148.0 1.9 %collective-permute-start.31 = (bf16[4,128,512]{2,1,0:T(8,128)(2,1)S(1)}, bf16[4,128,512]{2,1,0:T(8,128)(2,1)S(1)}, u32[]{:S(2)}, u32[]{:S(2)}) collective-permute-start(bf16[4,128,512]{2,1,0:T(8,128)(2,1)S(1)} %shard_map.197.refs_2_), channel_id=1, source_target_pairs={{0,1},{1,0},{2,3},{3,2},{4,5},{5,4},{6,7},{7,6},{8,9},{9,8},{10,11... | collective-permute-start | bytes 1572872 | tf_op jit(solution)/shard_map/ppermute | solution.py:493
